TPU v7x, 32 devices: a whole 2x2x4 slice. The times are simulated.
32 devices in a mesh: plane: 8 (over z, x), span: 4 (over y, core).
Axes of the slice: x: 2, y: 2, z: 4, core: 2. Of those that a mesh axis runs over, the one named last changes fastest.
Arguments:
- pressure_source: float32 [512, 32, 1024], P('span', 'plane'), may hold values from -24 to 24
- solid_mask: int32 [32, 1024], P('plane'), may hold values from 0 to 1, as said below
Outputs:
- pressure: float32 [512, 32, 1024], P('span', 'plane')
Inputs may be any that keep to these rules, and one draw needn't show every extreme that they name: `solid_mask`: 1 where a plane cell lies inside a tube of a staggered bank of tubes, else 0.
All inputs are finite; a program needn't handle non-finite values.
Results may differ from a plain program's by a relative error of at most 0.0001.
Values sent between devices are 32-bit elements; how exact they have to be, the bound alone decides.
No kernel may reach another device: no remote copies, remote signals or barrier semaphores. Data moves between devices by JAX's collectives and lax.ppermute only.
A program may use at most 64 MiB of HBM per device.

v0:
```python
import jax
import jax.numpy as jnp
from jax import lax
from jax.sharding import PartitionSpec as P

NS = 512


PENALTY = 12.0


def with_halo(block, sides, width):
    for axis, dim in sides:
        count = lax.axis_size(axis)
        forward = [(i, i + 1) for i in range(count - 1)]
        backward = [(target, source) for source, target in forward]
        low = lax.ppermute(
            lax.slice_in_dim(block, block.shape[dim] - width, None, axis=dim), axis, forward
        )
        high = lax.ppermute(lax.slice_in_dim(block, 0, width, axis=dim), axis, backward)
        block = jnp.concatenate([low, block, high], axis=dim)
    return block


def tables(length):
    nyquist = length // 2
    modes = jnp.arange(length, dtype=jnp.int32)
    wavenumber = jnp.where(modes <= nyquist, modes, modes - nyquist)
    points = jnp.arange(length, dtype=jnp.int32)
    phases = points[:, None] * wavenumber[None, :] % length
    angles = phases.astype(jnp.float32) * jnp.float32(2.0 * jnp.pi / length)
    cosine_mode = modes <= nyquist
    forward = jnp.where(cosine_mode[None, :], jnp.cos(angles), jnp.sin(angles))
    weight = jnp.where(
        cosine_mode & ((wavenumber == 0) | (wavenumber == nyquist)),
        jnp.float32(1.0),
        jnp.float32(2.0),
    ) / jnp.float32(length)
    inverse = (forward * weight[None, :]).T
    eigen_values = 2.0 - 2.0 * jnp.cos(
        wavenumber.astype(jnp.float32) * jnp.float32(2.0 * jnp.pi / length)
    )
    kept = jnp.where(3 * wavenumber <= length, jnp.float32(1.0), jnp.float32(0.0))
    return (forward * kept[None, :], inverse, eigen_values)


def neighbours(padded):
    return padded[:, :-2, 1:-1] + padded[:, 2:, 1:-1] + padded[:, 1:-1, :-2] + padded[:, 1:-1, 2:]


def local(pressure_source, solid_mask):
    span_count = lax.axis_size("span")
    forward, inverse, eigen_values = tables(NS)
    penalty = solid_mask.astype(jnp.float32) * PENALTY
    spectrum = jnp.einsum(
        "sm,src->mrc",
        forward,
        lax.all_to_all(pressure_source, "span", split_axis=2, concat_axis=0, tiled=True),
        precision=lax.Precision.HIGHEST,
    )
    spectrum_rows = lax.all_to_all(spectrum, "span", split_axis=0, concat_axis=2, tiled=True)
    mode_count = NS // span_count
    offset = lax.axis_index("span") * mode_count
    eigen_local = lax.dynamic_slice_in_dim(eigen_values, offset, mode_count)
    diagonal = 4.0 + eigen_local[:, None, None] + penalty[None]
    sweep_one = spectrum_rows / diagonal
    padded = with_halo(sweep_one, (("plane", 1),), 1)
    padded = jnp.pad(padded, ((0, 0), (0, 0), (1, 1)))
    sweep_two = (spectrum_rows + neighbours(padded)) / diagonal
    field_out = jnp.einsum(
        "ms,mrc->src",
        inverse,
        lax.all_to_all(sweep_two, "span", split_axis=2, concat_axis=0, tiled=True),
        precision=lax.Precision.HIGHEST,
    )
    return lax.all_to_all(field_out, "span", split_axis=0, concat_axis=2, tiled=True)


def solution(mesh):
    placed = (P("span", "plane", None), P("plane", None))
    return jax.shard_map(
        local, mesh=mesh, in_specs=placed, out_specs=P("span", "plane", None), check_vma=False
    )
```

profile of v0, /device:TPU:25, one launch (start us, length us, event | category | flops | bytes accessed | tf_op | source)
XLA Modules:
  0.0 183.8 jit_solution(13608760919947527885)
XLA Ops:
  0.0 3.9 %copy.31 = f32[128,4,1024]{0,1,2:T(4,128)} copy(f32[128,4,1024]{2,1,0:T(4,128)} %param.2) | data formatting | bytes 4194304 | tf_op args[0]
  3.9 4.3 %all-to-all-start = ((f32[128,4,1024]{0,1,2:T(4,128)}), f32[128,4,1024]{0,1,2:T(4,128)S(1)}, u32[]{:S(2)}, u32[]{:S(2)}) async-start(f32[128,4,1024]{0,1,2:T(4,128)} %copy.31), calls=%async_computation | async-start | bytes 4194304 | tf_op jit(solution)/shard_map/all_to_all | solution.py:58
  8.2 24.8 %all-to-all-done = f32[128,4,1024]{0,1,2:T(4,128)S(1)} async-done(((f32[128,4,1024]{0,1,2:T(4,128)}), f32[128,4,1024]{0,1,2:T(4,128)S(1)}, u32[]{:S(2)}, u32[]{:S(2)}) %all-to-all-start) | async-done | bytes 2097184 | tf_op jit(solution)/shard_map/all_to_all | solution.py:58
  33.0 1.8 copy.32
  34.8 9.2 %fusion.6 = f32[512,4,256]{2,0,1:T(8,128)S(1)} fusion(f32[512,4,256]{2,0,1:T(8,128)} %bitcast.32, f32[512]{0:T(512)S(1)} %fusion.17, s32[512]{0:T(512)S(1)} %add_select_fusion.1, pred[512]{0:T(512)(128)(4,1)S(1)} %iota_compare_fusion.2), kind=kOutput, calls=%fused_computation.19 | convolution fusion | flops 3225419776 | bytes 4198912 | tf_op jit(solution)/shard_map/sm,src->mrc/dot_general | solution.py:55
  44.0 2.7 %copy.34 = f32[512,4,256]{2,1,0:T(4,128)} copy(f32[512,4,256]{2,0,1:T(8,128)S(1)} %fusion.6) | data formatting | bytes 4194304 | tf_op jit(solution)/shard_map/sm,src->mrc/dot_general | solution.py:55
  46.7 4.6 %all-to-all-start.1 = ((f32[512,4,256]{2,1,0:T(4,128)}), f32[512,4,256]{2,1,0:T(4,128)S(1)}, u32[]{:S(2)}, u32[]{:S(2)}) async-start(f32[512,4,256]{2,1,0:T(4,128)} %copy.34), calls=%async_computation.1 | async-start | bytes 4194304 | tf_op jit(solution)/shard_map/all_to_all | solution.py:61
  51.4 24.7 %all-to-all-done.1 = f32[512,4,256]{2,1,0:T(4,128)S(1)} async-done(((f32[512,4,256]{2,1,0:T(4,128)}), f32[512,4,256]{2,1,0:T(4,128)S(1)}, u32[]{:S(2)}, u32[]{:S(2)}) %all-to-all-start.1) | async-done | bytes 2097184 | tf_op jit(solution)/shard_map/all_to_all | solution.py:61
  76.1 1.7 copy.35
  77.8 1.9 %copy.36 = f32[128,4,4,256]{0,3,2,1:T(8,128)S(1)} copy(f32[128,4,4,256]{3,0,2,1:T(8,128)} %bitcast.28) | data formatting | bytes 4194304 | tf_op jit(solution)/shard_map/all_to_all | solution.py:61
  80.7 3.1 %collective-permute-start = (f32[128,1,1024]{0,2,1:T(8,128)S(1)}, f32[128,1,1024]{0,2,1:T(8,128)S(1)}, u32[]{:S(2)}, u32[]{:S(2)}) collective-permute-start(f32[128,1,1024]{0,2,1:T(8,128)S(1)} %get-tuple-element.5), channel_id=1, source_target_pairs={{0,4},{4,8},{8,12},{12,16},{16,20},{20,24},{24,28},{1,5},{5,9},{9,... | collective-permute-start | bytes 1572872 | tf_op jit(solution)/shard_map/ppermute | solution.py:17
  83.8 3.2 %collective-permute-start.1 = (f32[128,1,1024]{0,2,1:T(8,128)S(1)}, f32[128,1,1024]{0,2,1:T(8,128)S(1)}, u32[]{:S(2)}, u32[]{:S(2)}) collective-permute-start(f32[128,1,1024]{0,2,1:T(8,128)S(1)} %get-tuple-element.6), channel_id=1, source_target_pairs={{4,0},{8,4},{12,8},{16,12},{20,16},{24,20},{28,24},{5,1},{9,5},{13... | collective-permute-start | bytes 1572872 | tf_op jit(solution)/shard_map/ppermute | solution.py:20
  87.1 9.0 %collective-permute-done = f32[128,1,1024]{0,2,1:T(8,128)S(1)} collective-permute-done((f32[128,1,1024]{0,2,1:T(8,128)S(1)}, f32[128,1,1024]{0,2,1:T(8,128)S(1)}, u32[]{:S(2)}, u32[]{:S(2)}) %collective-permute-start) | collective-permute-done | bytes 524320 | tf_op jit(solution)/shard_map/ppermute | solution.py:17
  96.1 12.5 %collective-permute-done.1 = f32[128,1,1024]{0,2,1:T(8,128)S(1)} collective-permute-done((f32[128,1,1024]{0,2,1:T(8,128)S(1)}, f32[128,1,1024]{0,2,1:T(8,128)S(1)}, u32[]{:S(2)}, u32[]{:S(2)}) %collective-permute-start.1) | collective-permute-done | bytes 524320 | tf_op jit(solution)/shard_map/ppermute | solution.py:20
  108.8 1.0 add_divide_fusion
  109.8 2.7 %copy.37 = f32[128,4,1024]{0,1,2:T(4,128)} copy(f32[128,4,1024]{0,2,1:T(8,128)S(1)} %add_divide_fusion) | data formatting | bytes 4194304 | tf_op jit(solution)/shard_map/div | solution.py:69
  112.5 4.1 %all-to-all-start.2 = ((f32[128,4,1024]{0,1,2:T(4,128)}), f32[128,4,1024]{0,1,2:T(4,128)S(1)}, u32[]{:S(2)}, u32[]{:S(2)}) async-start(f32[128,4,1024]{0,1,2:T(4,128)} %copy.37), calls=%async_computation.2 | async-start | bytes 4194304 | tf_op jit(solution)/shard_map/all_to_all | solution.py:73
  116.6 24.8 %all-to-all-done.2 = f32[128,4,1024]{0,1,2:T(4,128)S(1)} async-done(((f32[128,4,1024]{0,1,2:T(4,128)}), f32[128,4,1024]{0,1,2:T(4,128)S(1)}, u32[]{:S(2)}, u32[]{:S(2)}) %all-to-all-start.2) | async-done | bytes 2097184 | tf_op jit(solution)/shard_map/all_to_all | solution.py:73
  141.4 1.5 copy.38
  142.9 1.9 %copy.39 = f32[4,128,4,256]{3,1,0,2:T(8,128)S(1)} copy(f32[4,128,4,256]{1,3,0,2:T(8,128)} %bitcast.29) | data formatting | bytes 4194304 | tf_op jit(solution)/shard_map/all_to_all | solution.py:73
  144.8 7.7 %fusion.8 = f32[512,4,256]{2,0,1:T(8,128)S(1)} fusion(f32[512,4,256]{2,0,1:T(8,128)S(1)} %bitcast.31, f32[512]{0:T(512)S(1)} %select_multiply_fusion, s32[512]{0:T(512)S(1)} %add_select_fusion.1, pred[512]{0:T(512)(128)(4,1)S(1)} %iota_compare_fusion.2), kind=kOutput, calls=%fused_computation.21 | convolution fusion | flops 3225419776 | bytes 4198912 | tf_op jit(solution)/shard_map/ms,mrc->src/dot_general | solution.py:70
  152.5 1.4 copy.40
  153.8 28.0 %all_to_all.72 = f32[512,4,256]{2,1,0:T(4,128)S(1)} all-to-all(f32[512,4,256]{2,1,0:T(4,128)S(1)} %copy.40), channel_id=1, replica_groups=mesh['plane'=8,'span'=4] {'span'}, dimensions={0} | all-to-all | bytes 4194304 | tf_op jit(solution)/shard_map/all_to_all | solution.py:76
  181.8 2.0 %copy.44 = f32[4,128,1,4,256]{4,3,0,2,1:T(4,128)} copy(f32[4,128,1,4,256]{4,3,2,1,0:T(4,128)S(1)} %bitcast.30) | data formatting | bytes 4194304 | tf_op jit(solution)/shard_map/all_to_all | solution.py:76
  (12 shorter events, 1.3 us)
Async XLA Ops:
  3.9 29.1 %all-to-all-start = ((f32[128,4,1024]{0,1,2:T(4,128)}), f32[128,4,1024]{0,1,2:T(4,128)S(1)}, u32[]{:S(2)}, u32[]{:S(2)}) async-start(f32[128,4,1024]{0,1,2:T(4,128)} %copy.31), calls=%async_computation | async-start | bytes 4194304 | tf_op jit(solution)/shard_map/all_to_all | solution.py:58
  46.7 4.7 %copy-start = (s32[4,1024]{1,0:T(4,128)S(1)}, s32[4,1024]{1,0:T(4,128)}, u32[]{:S(2)}) copy-start(s32[4,1024]{1,0:T(4,128)} %param.3) | copy-start | bytes 49156
  46.7 29.4 %all-to-all-start.1 = ((f32[512,4,256]{2,1,0:T(4,128)}), f32[512,4,256]{2,1,0:T(4,128)S(1)}, u32[]{:S(2)}, u32[]{:S(2)}) async-start(f32[512,4,256]{2,1,0:T(4,128)} %copy.34), calls=%async_computation.1 | async-start | bytes 4194304 | tf_op jit(solution)/shard_map/all_to_all | solution.py:61
  80.7 15.4 %collective-permute-start = (f32[128,1,1024]{0,2,1:T(8,128)S(1)}, f32[128,1,1024]{0,2,1:T(8,128)S(1)}, u32[]{:S(2)}, u32[]{:S(2)}) collective-permute-start(f32[128,1,1024]{0,2,1:T(8,128)S(1)} %get-tuple-element.5), channel_id=1, source_target_pairs={{0,4},{4,8},{8,12},{12,16},{16,20},{20,24},{24,28},{1,5},{5,9},{9,... | collective-permute-start | bytes 1572872 | tf_op jit(solution)/shard_map/ppermute | solution.py:17
  83.8 24.7 %collective-permute-start.1 = (f32[128,1,1024]{0,2,1:T(8,128)S(1)}, f32[128,1,1024]{0,2,1:T(8,128)S(1)}, u32[]{:S(2)}, u32[]{:S(2)}) collective-permute-start(f32[128,1,1024]{0,2,1:T(8,128)S(1)} %get-tuple-element.6), channel_id=1, source_target_pairs={{4,0},{8,4},{12,8},{16,12},{20,16},{24,20},{28,24},{5,1},{9,5},{13... | collective-permute-start | bytes 1572872 | tf_op jit(solution)/shard_map/ppermute | solution.py:20
  112.5 28.9 %all-to-all-start.2 = ((f32[128,4,1024]{0,1,2:T(4,128)}), f32[128,4,1024]{0,1,2:T(4,128)S(1)}, u32[]{:S(2)}, u32[]{:S(2)}) async-start(f32[128,4,1024]{0,1,2:T(4,128)} %copy.37), calls=%async_computation.2 | async-start | bytes 4194304 | tf_op jit(solution)/shard_map/all_to_all | solution.py:73
where the time goes:
time: 185 us; the launch traced here: 184 us
  waiting for transfers between devices  95.8 us (52%)
  blocking collectives  28 us (15%)
  local copies, waits for them, and re-layouts  21.4 us (12%)
  starting transfers between devices  19.3 us (10%)
  matrix products  16.9 us (9%)
  other arithmetic  2.29 us (1%)
    all_to_all x1, blocking collectives, local(): lax.all_to_all(field_out, 'span', split_axis=0, concat_axis=2, tiled=True)  28 us
    all_to_all x1, waiting for transfers between devices, local(): lax.all_to_all(sweep_two, 'span', split_axis=2, concat_axis=0, tiled=True)  24.8 us
    all_to_all x1, waiting for transfers between devices, local(): lax.all_to_all(pressure_source, 'span', split_axis=2, concat_axis=0, tile...  24.8 us
    all_to_all x1, waiting for transfers between devices, local(): lax.all_to_all(spectrum, 'span', split_axis=0, concat_axis=2, tiled=True)  24.7 us
    ppermute x1, waiting for transfers between devices, with_halo(): lax.ppermute(lax.slice_in_dim(block, 0, width, axis=dim), axis, backward)  12.5 us
    dot_general x1, matrix products, local(): jnp.einsum('sm,src->mrc', forward, lax.all_to_all(pressure_source, 'span'...  9.22 us
    ppermute x1, waiting for transfers between devices, with_halo(): lax.ppermute(lax.slice_in_dim(block, block.shape[dim] - width, None, axis...  9.02 us
    dot_general x1, matrix products, local(): jnp.einsum('ms,mrc->src', inverse, lax.all_to_all(sweep_two, 'span', spli...  7.68 us
  transfers between devices with their start and end apart: 5, of which 5 were waited for; matrix products, arithmetic and copies ran while one was open for 0% of the time, Pallas kernels for 0%

commit v1 on v0

v1 whole, which is shorter than its diff:
```python
import functools

import jax
import jax.numpy as jnp
import ml_dtypes
import numpy as np
from jax import lax
from jax.experimental import pallas as pl
from jax.experimental.pallas import tpu as pltpu
from jax.sharding import PartitionSpec as P

PENALTY = 12.0
LANES = 128
VMEM = pl.BlockSpec(memory_space=pltpu.VMEM)
PARAMS = pltpu.CompilerParams(vmem_limit_bytes=32 * 1024 * 1024)


def split(values):
    high = values.astype(ml_dtypes.bfloat16)
    low = (values - high.astype(np.float64)).astype(ml_dtypes.bfloat16)
    return high, low


def tables(length, cells):
    half = length // 2
    points = np.arange(half)
    groups = []
    for parity in (0, 1):
        kept = [k for k in range(length // 2 + 1) if 3 * k <= length and k % 2 == parity]
        modes = [(k, False) for k in kept] + [(k, True) for k in kept if 0 < k < length // 2]
        groups.append(modes)
    padded = -(-max(len(modes) for modes in groups) // 16) * 16
    forward = np.zeros((2, padded, half))
    inverse = np.zeros((2, half, padded))
    fluid = np.zeros((2 * padded, 1))
    solid = np.zeros((2 * padded, 1))
    for parity, modes in enumerate(groups):
        for at, (k, sine) in enumerate(modes):
            angles = (points * k % length) * (2.0 * np.pi / length)
            wave = np.sin(angles) if sine else np.cos(angles)
            weight = 1.0 if k in (0, length // 2) else 2.0
            eigen = 2.0 - 2.0 * np.cos(2.0 * np.pi * k / length)
            forward[parity, at] = wave
            inverse[parity, :, at] = wave * weight / length
            fluid[parity * padded + at] = 1.0 / (4.0 + eigen)
            solid[parity * padded + at] = 1.0 / (4.0 + eigen + PENALTY)
    blocks = half // cells
    high, low = split(forward.reshape(2, padded, blocks, cells).transpose(0, 2, 1, 3))
    forward = np.concatenate([high, low, high], axis=3)
    high, low = split(inverse.reshape(2, blocks, cells, padded))
    inverse = np.concatenate([high, low, high], axis=3)
    return forward, inverse, fluid.astype(np.float32), solid.astype(np.float32)


def thirds(values, axis):
    high = values.astype(jnp.bfloat16)
    low = (values - high.astype(jnp.float32)).astype(jnp.bfloat16)
    return jnp.concatenate([high, high, low], axis=axis)


def pack_kernel(rows, row_count, count, cells, width, x_ref, *outs):
    me = lax.axis_index("span")
    tiles = width // LANES
    stride = count * tiles * row_count
    lane = lax.broadcasted_iota(jnp.int32, (cells, LANES), 1)
    sides = jnp.zeros((cells, LANES), jnp.float32)
    for d in range(count):
        target = jnp.bitwise_xor(me, d)
        for i, row in enumerate(rows):
            for tile in range(tiles):
                outs[d][i * cells : (i + 1) * cells, tile * LANES : (tile + 1) * LANES] = x_ref[
                    pl.ds((target * tiles + tile) * row_count + row, cells, stride=stride), :
                ]
            before = jnp.maximum(target * tiles - 1, 0)
            after = jnp.minimum((target + 1) * tiles, count * tiles - 1)
            for side, (tile, source) in enumerate(((before, LANES - 1), (after, 0))):
                at = d * 8 + i * 2 + side
                column = x_ref[pl.ds(tile * row_count + row, cells, stride=stride), :]
                column = pltpu.roll(column, (at - source) % LANES, 1)
                sides = jnp.where(lane == at, column, sides)
    if cells < LANES:
        sides = jnp.concatenate([sides, jnp.zeros((LANES - cells, LANES), jnp.float32)], axis=0)
    turned = sides.T
    for d in range(count):
        if width > LANES:
            outs[d][len(rows) * cells :, :] = jnp.zeros((8, width), jnp.float32)
        outs[d][len(rows) * cells :, :LANES] = turned[d * 8 : (d + 1) * 8]


def transform(rows, count, cells, blocks, forward_ref):
    me = lax.axis_index("span")
    half = count // 2
    spectra = []
    for i in range(rows + 1):
        parts = []
        for parity in (0, 1):
            total = None
            for d in range(half):
                table = forward_ref[parity, jnp.bitwise_and(jnp.bitwise_xor(me, d), half - 1)]
                if i < rows:
                    near = blocks[d][i * cells : (i + 1) * cells, :]
                    far = blocks[d + half][i * cells : (i + 1) * cells, :]
                else:
                    near = blocks[d][rows * cells :, :cells]
                    far = blocks[d + half][rows * cells :, :cells]
                value = near + far if parity == 0 else near - far
                if i < rows:
                    term = jnp.dot(table, thirds(value, 0), preferred_element_type=jnp.float32)
                else:
                    value = jnp.concatenate([value, jnp.zeros_like(value)], axis=0)
                    term = lax.dot_general(
                        table, thirds(value, 1), (((1,), (1,)), ((), ())), preferred_element_type=jnp.float32
                    )
                total = term if total is None else total + term
            parts.append(total)
        spectra.append(jnp.concatenate(parts, axis=0))
    return spectra[:-1], spectra[-1]


def inverse_rows(sweeps, count, cells, inverse_ref, outs):
    me = lax.axis_index("span")
    half = count // 2
    padded = sweeps[0].shape[0] // 2
    for i, sweep in enumerate(sweeps):
        even = thirds(sweep[:padded], 0)
        odd = thirds(sweep[padded:], 0)
        for d in range(half):
            place = jnp.bitwise_and(jnp.bitwise_xor(me, d), half - 1)
            first = jnp.dot(inverse_ref[0, place], even, preferred_element_type=jnp.float32)
            second = jnp.dot(inverse_ref[1, place], odd, preferred_element_type=jnp.float32)
            outs[d][i * cells : (i + 1) * cells, :] = first + second
            outs[d + half][i * cells : (i + 1) * cells, :] = first - second


def second_sweep(spectrum, one, above, below, sides, at, inverse_diagonal):
    width = one.shape[1]
    lane = lax.broadcasted_iota(jnp.int32, one.shape, 1)
    left = jnp.where(lane == 0, sides[:, at : at + 1], pltpu.roll(one, 1, 1))
    right = jnp.where(lane == width - 1, sides[:, at + 1 : at + 2], pltpu.roll(one, width - 1, 1))
    return (spectrum + above + below + left + right) * inverse_diagonal


def edge_kernel(count, cells, *refs):
    blocks, (forward_ref, fluid_ref, solid_ref, mask_ref, side_ref), outs = refs[:count], refs[count : count + 5], refs[count + 5 :]
    spectrum_ref, first_ref, last_ref, sides_ref = outs
    spectra, sides = transform(2, count, cells, blocks, forward_ref)
    fluid, solid = fluid_ref[...], solid_ref[...]
    for i, one_ref in enumerate((first_ref, last_ref)):
        spectrum_ref[i] = spectra[i]
        one_ref[...] = spectra[i] * jnp.where(mask_ref[i : i + 1, :] != 0, solid, fluid)
    sides_ref[...] = sides * side_factor(side_ref, fluid, solid)


def side_factor(side_ref, fluid, solid):
    kind = side_ref[0:1, :16]
    return jnp.where(kind == 0, fluid, jnp.where(kind == 1, solid, 0.0))


def inner_kernel(rows, count, cells, *refs):
    blocks, rest = refs[:count], refs[count:]
    forward_ref, inverse_ref, fluid_ref, solid_ref, mask_ref, side_ref, first_ref, last_ref = rest[:8]
    outs, ones_ref = rest[8 : 8 + count], rest[8 + count]
    spectra, sides = transform(rows, count, cells, blocks, forward_ref)
    fluid, solid = fluid_ref[...], solid_ref[...]
    sides = sides * side_factor(side_ref, fluid, solid)
    diagonals = [jnp.where(mask_ref[i : i + 1, :] != 0, solid, fluid) for i in range(rows)]
    ones = [spectra[i] * diagonals[i] for i in range(rows)]
    ones_ref[0] = ones[0]
    ones_ref[1] = ones[-1]
    around = [first_ref[...]] + ones + [last_ref[...]]
    sweeps = [
        second_sweep(spectra[i], ones[i], around[i], around[i + 2], sides, 2 * i, diagonals[i]) for i in range(rows)
    ]
    inverse_rows(sweeps, count, cells, inverse_ref, outs)


def rim_kernel(count, cells, *refs):
    spectrum_ref, first_ref, last_ref, sides_ref, ones_ref, low_ref, high_ref = refs[:7]
    inverse_ref, fluid_ref, solid_ref, mask_ref = refs[7:11]
    outs = refs[11:]
    fluid, solid = fluid_ref[...], solid_ref[...]
    sides = sides_ref[...]
    sweeps = []
    for i, (one, above, below) in enumerate(
        ((first_ref, low_ref, ones_ref.at[0]), (last_ref, ones_ref.at[1], high_ref))
    ):
        diagonal = jnp.where(mask_ref[i : i + 1, :] != 0, solid, fluid)
        sweeps.append(second_sweep(spectrum_ref[i], one[...], above[...], below[...], sides, 2 * i, diagonal))
    inverse_rows(sweeps, count, cells, inverse_ref, outs)


def unpack_kernel(row_groups, row_count, count, cells, width, *refs):
    me = lax.axis_index("span")
    tiles = width // LANES
    stride = count * tiles * row_count
    out_ref = refs[-1]
    for g, rows in enumerate(row_groups):
        for d in range(count):
            block = refs[g * count + d]
            source = jnp.bitwise_xor(me, d)
            for i, row in enumerate(rows):
                for tile in range(tiles):
                    out_ref[pl.ds((source * tiles + tile) * row_count + row, cells, stride=stride), :] = block[
                        i * cells : (i + 1) * cells, tile * LANES : (tile + 1) * LANES
                    ]


def call(kernel, outs, *args):
    shapes = [jax.ShapeDtypeStruct(shape, jnp.float32) for shape in outs]
    return pl.pallas_call(
        kernel,
        out_shape=shapes,
        in_specs=[VMEM] * len(args),
        out_specs=[VMEM] * len(outs),
        compiler_params=PARAMS,
    )(*args)


def exchange(blocks):
    count = len(blocks)
    return [blocks[0]] + [
        lax.ppermute(blocks[d], "span", [(i, i ^ d) for i in range(count)]) for d in range(1, count)
    ]


def local(pressure_source, solid_mask):
    count = lax.axis_size("span")
    plane_count = lax.axis_size("plane")
    cells, row_count, columns = pressure_source.shape
    width = columns // count
    tiles = columns // LANES
    inner = tuple(range(1, row_count - 1))
    edges = (0, row_count - 1)
    forward, inverse, fluid, solid = tables(cells * count, cells)
    modes = fluid.shape[0]
    forward, inverse, fluid, solid = map(jnp.asarray, (forward, inverse, fluid, solid))

    source = pressure_source.reshape(cells, row_count, tiles, LANES).transpose(0, 2, 1, 3).reshape(-1, LANES)

    me = lax.axis_index("span")
    mask = lax.dynamic_slice_in_dim(solid_mask, me * width, width, axis=1)
    outside = jnp.full((row_count, 1), 2, jnp.int32)
    framed = jnp.concatenate([outside, solid_mask, outside], axis=1)
    before = lax.dynamic_slice_in_dim(framed, me * width, 1, axis=1)
    after = lax.dynamic_slice_in_dim(framed, me * width + width + 1, 1, axis=1)
    beside = jnp.concatenate([before, after], axis=1)

    def picked(rows):
        kinds = jnp.concatenate([beside[row] for row in rows])
        kinds = jnp.pad(kinds, (0, LANES - kinds.shape[0]), constant_values=2)
        return jnp.stack([mask[row] for row in rows]), kinds[None, :]

    edge_mask, edge_sides = picked(edges)
    inner_mask, inner_sides = picked(inner)

    def pack(rows):
        return call(
            functools.partial(pack_kernel, rows, row_count, count, cells, width),
            [(len(rows) * cells + 8, width)] * count,
            source,
        )

    edge_blocks = exchange(pack(edges))
    inner_blocks = exchange(pack(inner))
    spectrum, first, last, sides = call(
        functools.partial(edge_kernel, count, cells),
        [(2, modes, width), (modes, width), (modes, width), (modes, 16)],
        *edge_blocks, forward, fluid, solid, edge_mask, edge_sides,
    )
    up = [(i, i + 1) for i in range(plane_count - 1)]
    down = [(i + 1, i) for i in range(plane_count - 1)]
    low = lax.ppermute(last, "plane", up)
    high = lax.ppermute(first, "plane", down)
    *inner_out, ones = call(
        functools.partial(inner_kernel, len(inner), count, cells),
        [(len(inner) * cells, width)] * count + [(2, modes, width)],
        *inner_blocks, forward, inverse, fluid, solid, inner_mask, inner_sides, first, last,
    )
    inner_got = exchange(inner_out)
    edge_out = call(
        functools.partial(rim_kernel, count, cells),
        [(2 * cells, width)] * count,
        spectrum, first, last, sides, ones, low, high, inverse, fluid, solid, edge_mask,
    )
    edge_got = exchange(edge_out)
    (result,) = call(
        functools.partial(unpack_kernel, (inner, edges), row_count, count, cells, width),
        [(cells * tiles * row_count, LANES)],
        *inner_got, *edge_got,
    )
    return result.reshape(cells, tiles, row_count, LANES).transpose(0, 2, 1, 3).reshape(cells, row_count, columns)


def solution(mesh):
    placed = (P("span", "plane", None), P("plane", None))
    return jax.shard_map(
        local, mesh=mesh, in_specs=placed, out_specs=P("span", "plane", None), check_vma=False
    )
```

time: 185 us -> 67 us (0.36)
  waiting for transfers between devices: 95.8 us -> 35.8 us
  blocking collectives: 28 us -> 0 us
  local copies, waits for them, and re-layouts: 21.4 us -> 2.66 us
  matrix products: 16.9 us -> 0 us
  Pallas kernels: 0 us -> 13.1 us
  starting transfers between devices: 19.3 us -> 14.8 us
  other arithmetic: 2.29 us -> 0.24 us
    all_to_all x3 -> x0, waiting for transfers between devices: 74.3 us -> none  [the longest x1 24.8 us: local(): lax.all_to_all(sweep_two, 'span', split_axis=2, concat_axis=0, tiled=True)]
    all_to_all x1 -> x0, blocking collectives: 28 us -> none  [local(): lax.all_to_all(field_out, 'span', split_axis=0, concat_axis=2, tiled=True)]
    dot_general x2 -> x0, matrix products: 16.9 us -> none  [the longest x1 9.22 us: local(): jnp.einsum('sm,src->mrc', forward, lax.all_to_all(pressure_source, 'span'...]
    ppermute x2 -> x14, waiting for transfers between devices: 21.5 us -> 35.8 us  [the longest x12 26.1 us: exchange(): lax.ppermute(blocks[d], 'span', [(i, i ^ d) for i in range(count)])]
    pallas_call x0 -> x6, Pallas kernels: none -> 13.1 us  [call(): pl.pallas_call(kernel, out_shape=shapes, in_specs=[VMEM] * len(args), out...]
    all_to_all x3 -> x0, starting transfers between devices: 12.9 us -> none  [the longest x1 4.58 us: local(): lax.all_to_all(spectrum, 'span', split_axis=0, concat_axis=2, tiled=True)]
    all_to_all x6 -> x0, local copies, waits for them, and re-layouts: 10.8 us -> none  [the longest x2 3.6 us: local(): lax.all_to_all(spectrum, 'span', split_axis=0, concat_axis=2, tiled=True)]
    ppermute x2 -> x14, starting transfers between devices: 6.36 us -> 14.8 us  [the longest x12 8.63 us: exchange(): lax.ppermute(blocks[d], 'span', [(i, i ^ d) for i in range(count)])]
  transfers between devices with their start and end apart: 5 -> 14, of which waited for: 5 -> 6; matrix products, arithmetic and copies ran while one was open for 0% -> 1% of each run, Pallas kernels for 0% -> 11%
where the time goes in v1:
time: 67 us; the launch traced here: 66.8 us
  waiting for transfers between devices  35.8 us (53%)
  starting transfers between devices  14.8 us (22%)
  Pallas kernels  13.1 us (20%)
  local copies, waits for them, and re-layouts  2.66 us (4%)
    ppermute x12, waiting for transfers between devices, exchange(): lax.ppermute(blocks[d], 'span', [(i, i ^ d) for i in range(count)])  26.1 us
    pallas_call x6, Pallas kernels, call(): pl.pallas_call(kernel, out_shape=shapes, in_specs=[VMEM] * len(args), out...  13.1 us
    ppermute x12, starting transfers between devices, exchange(): lax.ppermute(blocks[d], 'span', [(i, i ^ d) for i in range(count)])  8.63 us
    ppermute x1, waiting for transfers between devices, local(): high = lax.ppermute(first, 'plane', down)  7.69 us
    ppermute x1, starting transfers between devices, local(): low = lax.ppermute(last, 'plane', up)  3.12 us
    ppermute x1, starting transfers between devices, local(): high = lax.ppermute(first, 'plane', down)  3.06 us
    unnamed x14, local copies, waits for them, and re-layouts  2.31 us
    ppermute x1, waiting for transfers between devices, local(): low = lax.ppermute(last, 'plane', up)  2.07 us
  transfers between devices with their start and end apart: 14, of which 6 were waited for; matrix products, arithmetic and copies ran while one was open for 1% of the time, Pallas kernels for 11%

profile of v1, /device:TPU:25, one launch (start us, length us, event | category | flops | bytes accessed | tf_op | source)
XLA Modules:
  0.0 66.8 jit_solution(13518148581901875159)
XLA Ops:
  0.0 1.6 %copy-done = f32[128,4,1024]{2,1,0:T(4,128)S(1)} copy-done((f32[128,4,1024]{2,1,0:T(4,128)S(1)}, f32[128,4,1024]{2,1,0:T(4,128)}, u32[]{:S(2)}) %copy-start) | copy-done | bytes 2097176
  1.6 2.6 %shard_map.64 = (f32[264,256]{1,0:T(8,128)S(1)}, f32[264,256]{1,0:T(8,128)}, f32[264,256]{1,0:T(8,128)}, f32[264,256]{1,0:T(8,128)S(1)}) custom-call(f32[4096,128]{1,0:T(8,128)S(1)} %bitcast.22), custom_call_target="tpu_custom_call" | custom-call | tf_op jit(solution)/shard_map/pallas_call | solution.py:210
  4.2 0.7 %copy-done.5 = f32[264,256]{1,0:T(8,128)} copy-done((f32[264,256]{1,0:T(8,128)}, f32[264,256]{1,0:T(8,128)S(1)}, u32[]{:S(2)}) %copy-start.5) | copy-done | bytes 270360
  4.9 0.7 %collective-permute-start = (f32[264,256]{1,0:T(8,128)}, f32[264,256]{1,0:T(8,128)S(1)}, u32[]{:S(2)}, u32[]{:S(2)}) collective-permute-start(f32[264,256]{1,0:T(8,128)} %get-tuple-element.27), channel_id=1, source_target_pairs={{0,1},{1,0},{2,3},{3,2},{4,5},{5,4},{6,7},{7,6},{8,9},{9,8},{10,11... | collective-permute-start | bytes 811016 | tf_op jit(solution)/shard_map/ppermute | solution.py:222
  5.6 1.2 %collective-permute-start.1 = (f32[264,256]{1,0:T(8,128)}, f32[264,256]{1,0:T(8,128)S(1)}, u32[]{:S(2)}, u32[]{:S(2)}) collective-permute-start(f32[264,256]{1,0:T(8,128)} %get-tuple-element.28), channel_id=1, source_target_pairs={{0,2},{1,3},{2,0},{3,1},{4,6},{5,7},{6,4},{7,5},{8,10},{9,11},{10,... | collective-permute-start | bytes 811016 | tf_op jit(solution)/shard_map/ppermute | solution.py:222
  6.8 2.5 %shard_map.65 = (f32[264,256]{1,0:T(8,128)S(1)}, f32[264,256]{1,0:T(8,128)}, f32[264,256]{1,0:T(8,128)}, f32[264,256]{1,0:T(8,128)}) custom-call(f32[4096,128]{1,0:T(8,128)S(1)} %bitcast.23), custom_call_target="tpu_custom_call" | custom-call | tf_op jit(solution)/shard_map/pallas_call | solution.py:210
  9.8 1.6 %collective-permute-start.5 = (f32[264,256]{1,0:T(8,128)}, f32[264,256]{1,0:T(8,128)S(1)}, u32[]{:S(2)}, u32[]{:S(2)}) collective-permute-start(f32[264,256]{1,0:T(8,128)} %get-tuple-element.33), channel_id=1, source_target_pairs={{0,3},{1,2},{2,1},{3,0},{4,7},{5,6},{6,5},{7,4},{8,11},{9,10},{10,... | collective-permute-start | bytes 811016 | tf_op jit(solution)/shard_map/ppermute | solution.py:222
  12.2 7.5 %collective-permute-done.4.refs_2_ = f32[264,256]{1,0:T(8,128)S(1)} collective-permute-done((f32[264,256]{1,0:T(8,128)}, f32[264,256]{1,0:T(8,128)S(1)}, u32[]{:S(2)}, u32[]{:S(2)}) %collective-permute-start.4) | collective-permute-done | bytes 270368 | tf_op jit(solution)/shard_map/ppermute | solution.py:222
  19.7 6.7 %collective-permute-done.5.refs_3_ = f32[264,256]{1,0:T(8,128)S(1)} collective-permute-done((f32[264,256]{1,0:T(8,128)}, f32[264,256]{1,0:T(8,128)S(1)}, u32[]{:S(2)}, u32[]{:S(2)}) %collective-permute-start.5) | collective-permute-done | bytes 270368 | tf_op jit(solution)/shard_map/ppermute | solution.py:222
  26.4 0.8 %shard_map.66 = (f32[2,352,256]{2,1,0:T(8,128)S(1)}, f32[352,256]{1,0:T(8,128)S(1)}, f32[352,256]{1,0:T(8,128)S(1)}, f32[352,16]{1,0:T(8,128)S(1)}) custom-call(f32[264,256]{1,0:T(8,128)S(1)} %get-tuple-element.30.refs_0_, f32[264,256]{1,0:T(8,128)S(1)} %collective-permute-done.3.refs_1_, f32[264,256]{1,0:T(8,128)S(1)} %collective-permute-done.4.refs_2_, ...), custom_call_target="tpu_custom_call" | custom-call | tf_op jit(solution)/shard_map/pallas_call | solution.py:210
  27.1 3.1 %collective-permute-start.9 = (f32[352,256]{1,0:T(8,128)S(1)}, f32[352,256]{1,0:T(8,128)S(1)}, u32[]{:S(2)}, u32[]{:S(2)}) collective-permute-start(f32[352,256]{1,0:T(8,128)S(1)} %get-tuple-element.35.refs_11_.refs_2_), channel_id=1, source_target_pairs={{0,4},{4,8},{8,12},{12,16},{16,20},{20,24},{24,28},{1,5},{5,9},{9,... | collective-permute-start | bytes 1081352 | tf_op jit(solution)/shard_map/ppermute | solution.py:272
  30.3 3.1 %collective-permute-start.10 = (f32[352,256]{1,0:T(8,128)S(1)}, f32[352,256]{1,0:T(8,128)S(1)}, u32[]{:S(2)}, u32[]{:S(2)}) collective-permute-start(f32[352,256]{1,0:T(8,128)S(1)} %get-tuple-element.34.refs_10_.refs_1_), channel_id=1, source_target_pairs={{4,0},{8,4},{12,8},{16,12},{20,16},{24,20},{28,24},{5,1},{9,5},{13... | collective-permute-start | bytes 1081352 | tf_op jit(solution)/shard_map/ppermute | solution.py:273
  33.4 2.7 %shard_map.67 = (f32[256,256]{1,0:T(8,128)S(1)}, f32[256,256]{1,0:T(8,128)S(1)}, f32[256,256]{1,0:T(8,128)S(1)}, f32[256,256]{1,0:T(8,128)S(1)}, f32[2,352,256]{2,1,0:T(8,128)S(1)}) custom-call(f32[264,256]{1,0:T(8,128)S(1)} %get-tuple-element.26.refs_0_, f32[264,256]{1,0:T(8,128)S(1)} %collective-permute-done.refs_1_, ...), custom_call_target="tpu_custom_call" | custom-call | tf_op jit(solution)/shard_map/pallas_call | solution.py:210
  36.2 1.2 %collective-permute-start.7 = (f32[256,256]{1,0:T(8,128)S(1)}, f32[256,256]{1,0:T(8,128)S(1)}, u32[]{:S(2)}, u32[]{:S(2)}) collective-permute-start(f32[256,256]{1,0:T(8,128)S(1)} %get-tuple-element.38), channel_id=1, source_target_pairs={{0,2},{1,3},{2,0},{3,1},{4,6},{5,7},{6,4},{7,5},{8,10},{9,11},{10,... | collective-permute-start | bytes 786440 | tf_op jit(solution)/shard_map/ppermute | solution.py:222
  37.4 0.8 %collective-permute-start.8 = (f32[256,256]{1,0:T(8,128)S(1)}, f32[256,256]{1,0:T(8,128)S(1)}, u32[]{:S(2)}, u32[]{:S(2)}) collective-permute-start(f32[256,256]{1,0:T(8,128)S(1)} %get-tuple-element.39), channel_id=1, source_target_pairs={{0,3},{1,2},{2,1},{3,0},{4,7},{5,6},{6,5},{7,4},{8,11},{9,10},{10,... | collective-permute-start | bytes 786440 | tf_op jit(solution)/shard_map/ppermute | solution.py:222
  38.3 2.1 %collective-permute-done.9.refs_5_ = f32[352,256]{1,0:T(8,128)S(1)} collective-permute-done((f32[352,256]{1,0:T(8,128)S(1)}, f32[352,256]{1,0:T(8,128)S(1)}, u32[]{:S(2)}, u32[]{:S(2)}) %collective-permute-start.9) | collective-permute-done | bytes 360480 | tf_op jit(solution)/shard_map/ppermute | solution.py:272
  40.3 7.7 %collective-permute-done.10.refs_6_ = f32[352,256]{1,0:T(8,128)S(1)} collective-permute-done((f32[352,256]{1,0:T(8,128)S(1)}, f32[352,256]{1,0:T(8,128)S(1)}, u32[]{:S(2)}, u32[]{:S(2)}) %collective-permute-start.10) | collective-permute-done | bytes 360480 | tf_op jit(solution)/shard_map/ppermute | solution.py:273
  48.0 1.3 %shard_map.68 = (f32[256,256]{1,0:T(8,128)S(1)}, f32[256,256]{1,0:T(8,128)S(1)}, f32[256,256]{1,0:T(8,128)S(1)}, f32[256,256]{1,0:T(8,128)S(1)}) custom-call(f32[2,352,256]{2,1,0:T(8,128)S(1)} %get-tuple-element.40.refs_0_, f32[352,256]{1,0:T(8,128)S(1)} %get-tuple-element.34.refs_10_.refs_1_, f32[352,256]{1,0:T(8,128)S(1)} %get-tuple-element.35.refs_11_.refs_2_, ...), custom_call_target="tpu_custom_call" | custom-call | tf_op jit(solution)/shard_map/pallas_call | solution.py:210
  49.4 0.5 collective-permute-start.11
  49.8 1.3 %collective-permute-start.12 = (f32[256,256]{1,0:T(8,128)S(1)}, f32[256,256]{1,0:T(8,128)S(1)}, u32[]{:S(2)}, u32[]{:S(2)}) collective-permute-start(f32[256,256]{1,0:T(8,128)S(1)} %get-tuple-element.45), channel_id=1, source_target_pairs={{0,2},{1,3},{2,0},{3,1},{4,6},{5,7},{6,4},{7,5},{8,10},{9,11},{10,... | collective-permute-start | bytes 786440 | tf_op jit(solution)/shard_map/ppermute | solution.py:222
  51.1 0.5 collective-permute-start.13
  51.6 6.1 %collective-permute-done.12.refs_6_ = f32[256,256]{1,0:T(8,128)S(1)} collective-permute-done((f32[256,256]{1,0:T(8,128)S(1)}, f32[256,256]{1,0:T(8,128)S(1)}, u32[]{:S(2)}, u32[]{:S(2)}) %collective-permute-start.12) | collective-permute-done | bytes 262176 | tf_op jit(solution)/shard_map/ppermute | solution.py:222
  57.7 5.8 %collective-permute-done.13.refs_7_ = f32[256,256]{1,0:T(8,128)S(1)} collective-permute-done((f32[256,256]{1,0:T(8,128)S(1)}, f32[256,256]{1,0:T(8,128)S(1)}, u32[]{:S(2)}, u32[]{:S(2)}) %collective-permute-start.13) | collective-permute-done | bytes 262176 | tf_op jit(solution)/shard_map/ppermute | solution.py:222
  63.5 3.3 %shard_map.69 = f32[4096,128]{1,0:T(8,128)} custom-call(f32[256,256]{1,0:T(8,128)S(1)} %get-tuple-element.36.refs_0_, f32[256,256]{1,0:T(8,128)S(1)} %collective-permute-done.6.refs_1_, f32[256,256]{1,0:T(8,128)S(1)} %collective-permute-done.7.refs_2_, f32[256,256]{1,0:T(8,128)S(1)} %collective-permute-done.8.refs_3_, ...), custom_call_target="tpu_custom_call" | custom-call | tf_op jit(solution)/shard_map/pallas_call | solution.py:210
  (36 shorter events, 1.4 us)
Async XLA Ops:
  0.0 1.6 %copy-start = (f32[128,4,1024]{2,1,0:T(4,128)S(1)}, f32[128,4,1024]{2,1,0:T(4,128)}, u32[]{:S(2)}) copy-start(f32[128,4,1024]{2,1,0:T(4,128)} %param.6) | copy-start | bytes 6291460
  1.6 9.9 %copy-start.6 = (s32[4,1024]{1,0:T(4,128)S(1)}, s32[4,1024]{1,0:T(4,128)}, u32[]{:S(2)}) copy-start(s32[4,1024]{1,0:T(4,128)} %param.7) | copy-start | bytes 49156
  1.6 24.8 %copy-start.2 = (bf16[2,2,176,384]{3,2,1,0:T(8,128)(2,1)S(1)}, bf16[2,2,176,384]{3,2,1,0:T(8,128)(2,1)}, u32[]{:S(2)}) copy-start(bf16[2,2,176,384]{3,2,1,0:T(8,128)(2,1)} %constant.28.clone.refs_4_) | copy-start | bytes 1622020
  1.6 24.8 %copy-start.3 = (f32[352,1]{1,0:T(8,128)S(1)}, f32[352,1]{1,0:T(8,128)}, u32[]{:S(2)}) copy-start(f32[352,1]{1,0:T(8,128)} %constant.30.clone.refs_5_.refs_6_.refs_8_) | copy-start | bytes 4228
  1.6 24.8 %copy-start.4 = (f32[352,1]{1,0:T(8,128)S(1)}, f32[352,1]{1,0:T(8,128)}, u32[]{:S(2)}) copy-start(f32[352,1]{1,0:T(8,128)} %constant.31.clone.refs_6_.refs_7_.refs_9_) | copy-start | bytes 4228
  4.2 0.7 %copy-start.5 = (f32[264,256]{1,0:T(8,128)}, f32[264,256]{1,0:T(8,128)S(1)}, u32[]{:S(2)}) copy-start(f32[264,256]{1,0:T(8,128)S(1)} %get-tuple-element.29) | copy-start | bytes 811012
  4.9 28.5 %collective-permute-start = (f32[264,256]{1,0:T(8,128)}, f32[264,256]{1,0:T(8,128)S(1)}, u32[]{:S(2)}, u32[]{:S(2)}) collective-permute-start(f32[264,256]{1,0:T(8,128)} %get-tuple-element.27), channel_id=1, source_target_pairs={{0,1},{1,0},{2,3},{3,2},{4,5},{5,4},{6,7},{7,6},{8,9},{9,8},{10,11... | collective-permute-start | bytes 811016 | tf_op jit(solution)/shard_map/ppermute | solution.py:222
  5.6 27.8 %copy-start.1 = (bf16[2,2,128,528]{3,2,1,0:T(8,128)(2,1)S(1)}, bf16[2,2,128,528]{3,2,1,0:T(8,128)(2,1)}, u32[]{:S(2)}) copy-start(bf16[2,2,128,528]{3,2,1,0:T(8,128)(2,1)} %constant.29.clone.refs_5_.refs_7_) | copy-start | bytes 1622020
  5.6 27.8 %collective-permute-start.1 = (f32[264,256]{1,0:T(8,128)}, f32[264,256]{1,0:T(8,128)S(1)}, u32[]{:S(2)}, u32[]{:S(2)}) collective-permute-start(f32[264,256]{1,0:T(8,128)} %get-tuple-element.28), channel_id=1, source_target_pairs={{0,2},{1,3},{2,0},{3,1},{4,6},{5,7},{6,4},{7,5},{8,10},{9,11},{10,... | collective-permute-start | bytes 811016 | tf_op jit(solution)/shard_map/ppermute | solution.py:222
  9.3 2.6 %collective-permute-start.3 = (f32[264,256]{1,0:T(8,128)}, f32[264,256]{1,0:T(8,128)S(1)}, u32[]{:S(2)}, u32[]{:S(2)}) collective-permute-start(f32[264,256]{1,0:T(8,128)} %get-tuple-element.31), channel_id=1, source_target_pairs={{0,1},{1,0},{2,3},{3,2},{4,5},{5,4},{6,7},{7,6},{8,9},{9,8},{10,11... | collective-permute-start | bytes 811016 | tf_op jit(solution)/shard_map/ppermute | solution.py:222
  9.6 10.1 %collective-permute-start.4 = (f32[264,256]{1,0:T(8,128)}, f32[264,256]{1,0:T(8,128)S(1)}, u32[]{:S(2)}, u32[]{:S(2)}) collective-permute-start(f32[264,256]{1,0:T(8,128)} %get-tuple-element.32), channel_id=1, source_target_pairs={{0,2},{1,3},{2,0},{3,1},{4,6},{5,7},{6,4},{7,5},{8,10},{9,11},{10,... | collective-permute-start | bytes 811016 | tf_op jit(solution)/shard_map/ppermute | solution.py:222
  9.8 16.5 %collective-permute-start.5 = (f32[264,256]{1,0:T(8,128)}, f32[264,256]{1,0:T(8,128)S(1)}, u32[]{:S(2)}, u32[]{:S(2)}) collective-permute-start(f32[264,256]{1,0:T(8,128)} %get-tuple-element.33), channel_id=1, source_target_pairs={{0,3},{1,2},{2,1},{3,0},{4,7},{5,6},{6,5},{7,4},{8,11},{9,10},{10,... | collective-permute-start | bytes 811016 | tf_op jit(solution)/shard_map/ppermute | solution.py:222
  11.9 21.5 %collective-permute-start.2 = (f32[264,256]{1,0:T(8,128)}, f32[264,256]{1,0:T(8,128)}, u32[]{:S(2)}, u32[]{:S(2)}) collective-permute-start(f32[264,256]{1,0:T(8,128)} %copy-done.5), channel_id=1, source_target_pairs={{0,3},{1,2},{2,1},{3,0},{4,7},{5,6},{6,5},{7,4},{8,11},{9,10},{10,... | collective-permute-start | bytes 811016 | tf_op jit(solution)/shard_map/ppermute | solution.py:222
  27.1 13.2 %collective-permute-start.9 = (f32[352,256]{1,0:T(8,128)S(1)}, f32[352,256]{1,0:T(8,128)S(1)}, u32[]{:S(2)}, u32[]{:S(2)}) collective-permute-start(f32[352,256]{1,0:T(8,128)S(1)} %get-tuple-element.35.refs_11_.refs_2_), channel_id=1, source_target_pairs={{0,4},{4,8},{8,12},{12,16},{16,20},{20,24},{24,28},{1,5},{5,9},{9,... | collective-permute-start | bytes 1081352 | tf_op jit(solution)/shard_map/ppermute | solution.py:272
  30.3 17.8 %collective-permute-start.10 = (f32[352,256]{1,0:T(8,128)S(1)}, f32[352,256]{1,0:T(8,128)S(1)}, u32[]{:S(2)}, u32[]{:S(2)}) collective-permute-start(f32[352,256]{1,0:T(8,128)S(1)} %get-tuple-element.34.refs_10_.refs_1_), channel_id=1, source_target_pairs={{4,0},{8,4},{12,8},{16,12},{20,16},{24,20},{28,24},{5,1},{9,5},{13... | collective-permute-start | bytes 1081352 | tf_op jit(solution)/shard_map/ppermute | solution.py:273
  36.1 15.0 %collective-permute-start.6 = (f32[256,256]{1,0:T(8,128)S(1)}, f32[256,256]{1,0:T(8,128)S(1)}, u32[]{:S(2)}, u32[]{:S(2)}) collective-permute-start(f32[256,256]{1,0:T(8,128)S(1)} %get-tuple-element.37), channel_id=1, source_target_pairs={{0,1},{1,0},{2,3},{3,2},{4,5},{5,4},{6,7},{7,6},{8,9},{9,8},{10,11... | collective-permute-start | bytes 786440 | tf_op jit(solution)/shard_map/ppermute | solution.py:222
  36.2 15.4 %collective-permute-start.7 = (f32[256,256]{1,0:T(8,128)S(1)}, f32[256,256]{1,0:T(8,128)S(1)}, u32[]{:S(2)}, u32[]{:S(2)}) collective-permute-start(f32[256,256]{1,0:T(8,128)S(1)} %get-tuple-element.38), channel_id=1, source_target_pairs={{0,2},{1,3},{2,0},{3,1},{4,6},{5,7},{6,4},{7,5},{8,10},{9,11},{10,... | collective-permute-start | bytes 786440 | tf_op jit(solution)/shard_map/ppermute | solution.py:222
  37.4 14.1 %collective-permute-start.8 = (f32[256,256]{1,0:T(8,128)S(1)}, f32[256,256]{1,0:T(8,128)S(1)}, u32[]{:S(2)}, u32[]{:S(2)}) collective-permute-start(f32[256,256]{1,0:T(8,128)S(1)} %get-tuple-element.39), channel_id=1, source_target_pairs={{0,3},{1,2},{2,1},{3,0},{4,7},{5,6},{6,5},{7,4},{8,11},{9,10},{10,... | collective-permute-start | bytes 786440 | tf_op jit(solution)/shard_map/ppermute | solution.py:222
  49.4 2.2 %collective-permute-start.11 = (f32[256,256]{1,0:T(8,128)S(1)}, f32[256,256]{1,0:T(8,128)S(1)}, u32[]{:S(2)}, u32[]{:S(2)}) collective-permute-start(f32[256,256]{1,0:T(8,128)S(1)} %get-tuple-element.44), channel_id=1, source_target_pairs={{0,1},{1,0},{2,3},{3,2},{4,5},{5,4},{6,7},{7,6},{8,9},{9,8},{10,11... | collective-permute-start | bytes 786440 | tf_op jit(solution)/shard_map/ppermute | solution.py:222
  49.8 7.9 %collective-permute-start.12 = (f32[256,256]{1,0:T(8,128)S(1)}, f32[256,256]{1,0:T(8,128)S(1)}, u32[]{:S(2)}, u32[]{:S(2)}) collective-permute-start(f32[256,256]{1,0:T(8,128)S(1)} %get-tuple-element.45), channel_id=1, source_target_pairs={{0,2},{1,3},{2,0},{3,1},{4,6},{5,7},{6,4},{7,5},{8,10},{9,11},{10,... | collective-permute-start | bytes 786440 | tf_op jit(solution)/shard_map/ppermute | solution.py:222
  51.1 12.4 %collective-permute-start.13 = (f32[256,256]{1,0:T(8,128)S(1)}, f32[256,256]{1,0:T(8,128)S(1)}, u32[]{:S(2)}, u32[]{:S(2)}) collective-permute-start(f32[256,256]{1,0:T(8,128)S(1)} %get-tuple-element.46), channel_id=1, source_target_pairs={{0,3},{1,2},{2,1},{3,0},{4,7},{5,6},{6,5},{7,4},{8,11},{9,10},{10,... | collective-permute-start | bytes 786440 | tf_op jit(solution)/shard_map/ppermute | solution.py:222

commit v2 on v1

v2 whole, which is shorter than its diff:
```python
import functools

import jax
import jax.numpy as jnp
import ml_dtypes
import numpy as np
from jax import lax
from jax.experimental import pallas as pl
from jax.experimental.pallas import tpu as pltpu
from jax.sharding import PartitionSpec as P

PENALTY = 12.0
LANES = 128
VMEM = pl.BlockSpec(memory_space=pltpu.VMEM)
PARAMS = pltpu.CompilerParams(vmem_limit_bytes=32 * 1024 * 1024)


def split(values):
    high = values.astype(ml_dtypes.bfloat16)
    low = (values - high.astype(np.float64)).astype(ml_dtypes.bfloat16)
    return high, low


def tables(length, cells):
    half = length // 2
    points = np.arange(half)
    groups = []
    for parity in (0, 1):
        kept = [k for k in range(length // 2 + 1) if 3 * k <= length and k % 2 == parity]
        modes = [(k, False) for k in kept] + [(k, True) for k in kept if 0 < k < length // 2]
        groups.append(modes)
    padded = -(-max(len(modes) for modes in groups) // 16) * 16
    forward = np.zeros((2, padded, half))
    inverse = np.zeros((2, half, padded))
    fluid = np.zeros((2 * padded, 1))
    solid = np.zeros((2 * padded, 1))
    for parity, modes in enumerate(groups):
        for at, (k, sine) in enumerate(modes):
            angles = (points * k % length) * (2.0 * np.pi / length)
            wave = np.sin(angles) if sine else np.cos(angles)
            weight = 1.0 if k in (0, length // 2) else 2.0
            eigen = 2.0 - 2.0 * np.cos(2.0 * np.pi * k / length)
            forward[parity, at] = wave
            inverse[parity, :, at] = wave * weight / length
            fluid[parity * padded + at] = 1.0 / (4.0 + eigen)
            solid[parity * padded + at] = 1.0 / (4.0 + eigen + PENALTY)
    blocks = half // cells
    high, low = split(forward.reshape(2, padded, blocks, cells).transpose(0, 2, 1, 3))
    forward = np.concatenate([high, low, high], axis=3)
    high, low = split(inverse.reshape(2, blocks, cells, padded))
    inverse = np.concatenate([high, low, high], axis=3)
    return forward, inverse, fluid.astype(np.float32), solid.astype(np.float32)


def thirds(values, axis):
    high = values.astype(jnp.bfloat16)
    low = (values - high.astype(jnp.float32)).astype(jnp.bfloat16)
    return jnp.concatenate([high, high, low], axis=axis)


def pack_kernel(jobs, row_count, count, cells, width, tiles, split_at, x_ref, *refs):
    outs, (held, arrived) = refs[:-2], refs[-2:]
    me = lax.axis_index("span")
    lines = x_ref.shape[1]
    pitch = held.shape[0] // cells
    some = cells // split_at
    copies = [
        pltpu.make_async_copy(
            x_ref.at[pl.ds(part * some, some)],
            held.reshape(cells, pitch, LANES).at[pl.ds(part * some, some), pl.ds(0, lines)],
            arrived.at[part],
        )
        for part in range(split_at)
    ]
    for copy in copies:
        copy.start()
    lane = lax.broadcasted_iota(jnp.int32, (some, LANES), 1)
    sides = []
    for part, copy in enumerate(copies):
        copy.wait()
        beside = jnp.zeros((some, LANES), jnp.float32)

        def line(tile, row):
            return held[pl.ds(part * some * pitch + tile * row_count + row, some, stride=pitch), :]

        for job, (out, place, d, column) in enumerate(jobs):
            first = (column * count + jnp.bitwise_xor(me, d)) * tiles
            base = place * (row_count * cells + 8) + part * some
            for row in range(row_count):
                for tile in range(tiles):
                    outs[out][base + row * cells : base + row * cells + some, tile * LANES : (tile + 1) * LANES] = line(
                        first + tile, row
                    )
                before = jnp.maximum(first - 1, 0)
                after = jnp.minimum(first + tiles, lines // row_count - 1)
                for side, (tile, source) in enumerate(((before, LANES - 1), (after, 0))):
                    at = job * 8 + row * 2 + side
                    beside = jnp.where(lane == at, pltpu.roll(line(tile, row), (at - source) % LANES, 1), beside)
        sides.append(beside)
    if cells < LANES:
        sides.append(jnp.zeros((LANES - cells, LANES), jnp.float32))
    turned = jnp.concatenate(sides, axis=0).T
    for job, (out, place, _, _) in enumerate(jobs):
        base = place * (row_count * cells + 8) + row_count * cells
        outs[out][base : base + 8, :LANES] = turned[job * 8 : (job + 1) * 8]
        if width > LANES:
            outs[out][base : base + 8, LANES:] = jnp.zeros((8, width - LANES), jnp.float32)


def transform(rows, count, cells, blocks, forward_ref):
    me = lax.axis_index("span")
    half = count // 2
    spectra = []
    for i in range(rows + 1):
        parts = []
        for parity in (0, 1):
            total = None
            for d in range(half):
                table = forward_ref[parity, jnp.bitwise_and(jnp.bitwise_xor(me, d), half - 1)]
                if i < rows:
                    near = blocks[d][i * cells : (i + 1) * cells, :]
                    far = blocks[d + half][i * cells : (i + 1) * cells, :]
                else:
                    near = blocks[d][rows * cells :, :cells]
                    far = blocks[d + half][rows * cells :, :cells]
                value = near + far if parity == 0 else near - far
                if i < rows:
                    term = jnp.dot(table, thirds(value, 0), preferred_element_type=jnp.float32)
                else:
                    value = jnp.concatenate([value, jnp.zeros_like(value)], axis=0)
                    term = lax.dot_general(
                        table, thirds(value, 1), (((1,), (1,)), ((), ())), preferred_element_type=jnp.float32
                    )
                total = term if total is None else total + term
            parts.append(total)
        spectra.append(jnp.concatenate(parts, axis=0))
    return spectra[:-1], spectra[-1]


def inverse_rows(sweeps, count, cells, inverse_ref, outs):
    me = lax.axis_index("span")
    half = count // 2
    padded = sweeps[0].shape[0] // 2
    for i, sweep in enumerate(sweeps):
        even = thirds(sweep[:padded], 0)
        odd = thirds(sweep[padded:], 0)
        for d in range(half):
            place = jnp.bitwise_and(jnp.bitwise_xor(me, d), half - 1)
            first = jnp.dot(inverse_ref[0, place], even, preferred_element_type=jnp.float32)
            second = jnp.dot(inverse_ref[1, place], odd, preferred_element_type=jnp.float32)
            outs[d][i * cells : (i + 1) * cells, :] = first + second
            outs[d + half][i * cells : (i + 1) * cells, :] = first - second


def second_sweep(spectrum, one, above, below, sides, at, inverse_diagonal):
    width = one.shape[1]
    lane = lax.broadcasted_iota(jnp.int32, one.shape, 1)
    left = jnp.where(lane == 0, sides[:, at : at + 1], pltpu.roll(one, 1, 1))
    right = jnp.where(lane == width - 1, sides[:, at + 1 : at + 2], pltpu.roll(one, width - 1, 1))
    return (spectrum + above + below + left + right) * inverse_diagonal


def side_factor(side_ref, fluid, solid):
    kind = side_ref[0:1, :16]
    return jnp.where(kind == 0, fluid, jnp.where(kind == 1, solid, 0.0))


def forward_kernel(rows, count, cells, column, *refs):
    blocks, (forward_ref, fluid_ref, solid_ref, mask_ref, side_ref), outs = refs[:count], refs[count : count + 5], refs[count + 5 :]
    spectrum_ref, first_ref, last_ref, sides_ref = outs
    size = rows * cells + 8
    blocks = [ref.at[column * size : (column + 1) * size] if ref.shape[0] > size else ref for ref in blocks]
    spectra, sides = transform(rows, count, cells, blocks, forward_ref)
    fluid, solid = fluid_ref[...], solid_ref[...]
    for row in range(rows):
        spectrum_ref[row] = spectra[row]
    first_ref[...] = spectra[0] * jnp.where(mask_ref[0:1, :] != 0, solid, fluid)
    last_ref[...] = spectra[-1] * jnp.where(mask_ref[rows - 1 : rows, :] != 0, solid, fluid)
    sides_ref[...] = sides * side_factor(side_ref, fluid, solid)


def sweep_kernel(wanted, rows, count, cells, *refs):
    spectrum_ref, sides_ref, low_ref, high_ref, inverse_ref, fluid_ref, solid_ref, mask_ref = refs[:8]
    outs = refs[8:]
    fluid, solid = fluid_ref[...], solid_ref[...]
    sides = sides_ref[...]
    needed = sorted({at for row in wanted for at in (row - 1, row, row + 1) if 0 <= at < rows})
    diagonal = {at: jnp.where(mask_ref[at : at + 1, :] != 0, solid, fluid) for at in needed}
    one = {at: spectrum_ref[at] * diagonal[at] for at in needed}
    if 0 in wanted:
        one[-1] = low_ref[...]
    if rows - 1 in wanted:
        one[rows] = high_ref[...]
    sweeps = [
        second_sweep(spectrum_ref[row], one[row], one[row - 1], one[row + 1], sides, 2 * row, diagonal[row])
        for row in wanted
    ]
    inverse_rows(sweeps, count, cells, inverse_ref, outs)


def unpack_kernel(row_groups, row_count, count, cells, tiles, column, *refs):
    me = lax.axis_index("span")
    blocks = refs[: len(row_groups) * count]
    out_ref, held, done = refs[-3:]
    pitch = held.shape[0] // cells
    lines = count * tiles * row_count
    for g, rows in enumerate(row_groups):
        for d in range(count):
            source = jnp.bitwise_xor(me, d)
            for i, row in enumerate(rows):
                for tile in range(tiles):
                    held[pl.ds((source * tiles + tile) * row_count + row, cells, stride=pitch), :] = blocks[g * count + d][
                        i * cells : (i + 1) * cells, tile * LANES : (tile + 1) * LANES
                    ]
    copy = pltpu.make_async_copy(
        held.reshape(cells, pitch, LANES).at[:, pl.ds(0, lines)], out_ref.at[:, pl.ds(column * lines, lines)], done
    )
    copy.start()
    copy.wait()


def call(kernel, outs, *args):
    shapes = [jax.ShapeDtypeStruct(shape, jnp.float32) for shape in outs]
    return pl.pallas_call(
        kernel,
        out_shape=shapes,
        in_specs=[VMEM] * len(args),
        out_specs=[VMEM] * len(outs),
        compiler_params=PARAMS,
    )(*args)


def local(pressure_source, solid_mask):
    count = lax.axis_size("span")
    plane_count = lax.axis_size("plane")
    cells, rows, columns = pressure_source.shape
    half = count // 2
    parts = 2 if columns // count >= 2 * LANES else 1
    width = columns // count // parts
    tiles = width // LANES
    lines = columns // LANES * rows
    inner = tuple(range(1, rows - 1))
    edges = (0, rows - 1)
    forward, inverse, fluid, solid = tables(cells * count, cells)
    modes = fluid.shape[0]
    forward, inverse, fluid, solid = map(jnp.asarray, (forward, inverse, fluid, solid))

    source = pressure_source.reshape(cells, rows, columns // LANES, LANES).transpose(0, 2, 1, 3).reshape(cells, lines, LANES)
    me = lax.axis_index("span")
    outside = jnp.full((rows, 1), 2, jnp.int32)
    framed = jnp.concatenate([outside, solid_mask, outside], axis=1)

    def masks(part):
        start = (part * count + me) * width
        mask = lax.dynamic_slice_in_dim(solid_mask, start, width, axis=1)
        before = lax.dynamic_slice_in_dim(framed, start, 1, axis=1)
        after = lax.dynamic_slice_in_dim(framed, start + width + 1, 1, axis=1)
        kinds = jnp.concatenate([before, after], axis=1).reshape(1, 2 * rows)
        return mask, jnp.pad(kinds, ((0, 0), (0, LANES - 2 * rows)), constant_values=2)

    size = rows * cells + 8

    def pack(jobs, sizes, limit):
        return pl.pallas_call(
            functools.partial(pack_kernel, jobs, rows, count, cells, width, tiles, 4),
            out_shape=[jax.ShapeDtypeStruct((places * size, width), jnp.float32) for places in sizes],
            in_specs=[pl.BlockSpec(memory_space=pl.ANY)],
            out_specs=[VMEM] * len(sizes),
            scratch_shapes=[
                pltpu.VMEM((cells * (lines + 8), LANES), jnp.float32),
                pltpu.SemaphoreType.DMA((4,)),
            ],
            compiler_params=pltpu.CompilerParams(vmem_limit_bytes=limit * 1024 * 1024),
        )(source)

    def swap(block, d):
        return lax.ppermute(block, "span", [(i, i ^ d) for i in range(count)])

    far = range(half, count)
    packed = pack([(d - half, 0, d, 0) for d in far], [1] * half, 56)
    got = {(0, d): swap(block, d) for d, block in zip(far, packed)}
    source = lax.optimization_barrier((source, *packed))[0]
    jobs = [(at, part, d, part) for at, d in enumerate(range(half)) for part in range(parts)]
    sizes = [parts] * half
    for part in range(1, parts):
        for d in far:
            jobs.append((len(sizes), 0, d, part))
            sizes.append(1)
    packed = pack(jobs, sizes, 32)
    near = [packed[0]] + [swap(packed[d], d) for d in range(1, half)]
    at = half
    for part in range(1, parts):
        for d in far:
            got[part, d] = swap(packed[at], d)
            at += 1

    up = [(i, i + 1) for i in range(plane_count - 1)]
    down = [(i + 1, i) for i in range(plane_count - 1)]
    state, inner_got, edge_got = [], [], []

    def sweep(wanted, part, low, high):
        spectrum, sides, mask = state[part][0], state[part][1], state[part][2]
        blocks = call(
            functools.partial(sweep_kernel, wanted, rows, count, cells),
            [(len(wanted) * cells, width)] * count,
            spectrum, sides, low, high, inverse, fluid, solid, mask,
        )
        return [blocks[0]] + [swap(blocks[d], d) for d in range(1, count)]

    for part in range(parts):
        mask, kinds = masks(part)
        spectrum, first, last, sides = call(
            functools.partial(forward_kernel, rows, count, cells, part),
            [(rows, modes, width), (modes, width), (modes, width), (modes, 16)],
            *near, *[got[part, d] for d in far], forward, fluid, solid, mask, kinds,
        )
        low = lax.ppermute(last, "plane", up)
        high = lax.ppermute(first, "plane", down)
        state.append((spectrum, sides, mask, low, high))
        inner_got.append(sweep(inner, part, first, last))
    for part in range(parts):
        edge_got.append(sweep(edges, part, state[part][3], state[part][4]))

    result = None
    for part in range(parts):
        blocks = inner_got[part] + edge_got[part]
        held = count * tiles * rows + 8
        result = pl.pallas_call(
            functools.partial(unpack_kernel, (inner, edges), rows, count, cells, tiles, part),
            out_shape=jax.ShapeDtypeStruct((cells, lines, LANES), jnp.float32),
            in_specs=[VMEM] * len(blocks) + [pl.BlockSpec(memory_space=pl.ANY)] * (result is not None),
            out_specs=pl.BlockSpec(memory_space=pl.ANY),
            scratch_shapes=[pltpu.VMEM((cells * held, LANES), jnp.float32), pltpu.SemaphoreType.DMA],
            input_output_aliases={} if result is None else {len(blocks): 0},
            compiler_params=PARAMS,
        )(*blocks, *([] if result is None else [result]))
    return result.reshape(cells, columns // LANES, rows, LANES).transpose(0, 2, 1, 3).reshape(cells, rows, columns)


def solution(mesh):
    placed = (P("span", "plane", None), P("plane", None))
    return jax.shard_map(
        local, mesh=mesh, in_specs=placed, out_specs=P("span", "plane", None), check_vma=False
    )
```

time: 67 us -> 69.9 us (1.043)
  the two profiles are of different devices: /device:TPU:25 before, /device:TPU:0 now
where the time goes in v2:
time: 69.9 us; the launch traced here: 69.6 us
  starting transfers between devices  27.7 us (40%)
  waiting for transfers between devices  20.7 us (30%)
  Pallas kernels  17.2 us (25%)
  local copies, waits for them, and re-layouts  3.7 us (5%)
    ppermute x17, waiting for transfers between devices, swap(): return lax.ppermute(block, 'span', [(i, i ^ d) for i in range(count)])  20.7 us
    ppermute x17, starting transfers between devices, swap(): return lax.ppermute(block, 'span', [(i, i ^ d) for i in range(count)])  15.3 us
    ppermute x2, starting transfers between devices, local(): low = lax.ppermute(last, 'plane', up)  9.81 us
    pallas_call x6, Pallas kernels, call(): pl.pallas_call(kernel, out_shape=shapes, in_specs=[VMEM] * len(args), out...  9.74 us
    pallas_call x2, Pallas kernels, pack(): pl.pallas_call(functools.partial(pack_kernel, jobs, rows, count, cells, w...  5.03 us
    unnamed x20, local copies, waits for them, and re-layouts  3.33 us
    ppermute x2, starting transfers between devices, local(): high = lax.ppermute(first, 'plane', down)  2.57 us
    pallas_call x2, Pallas kernels, local(): pl.pallas_call(functools.partial(unpack_kernel, (inner, edges), rows, cou...  2.47 us
  transfers between devices with their start and end apart: 21, of which 10 were waited for; matrix products, arithmetic and copies ran while one was open for 1% of the time, Pallas kernels for 16%

profile of v2, /device:TPU:0, one launch (start us, length us, event | category | flops | bytes accessed | tf_op | source)
XLA Modules:
  0.0 69.6 jit_solution(10942444870568566300)
XLA Ops:
  0.0 2.7 %shard_map.64 = (f32[520,128]{1,0:T(8,128)}, f32[520,128]{1,0:T(8,128)}) custom-call(f32[128,32,128]{2,1,0:T(8,128)} %bitcast.10), custom_call_target="tpu_custom_call" | custom-call | tf_op jit(solution)/shard_map/pallas_call | solution.py:264
  2.7 2.4 %shard_map.65 = (f32[1040,128]{1,0:T(8,128)S(1)}, f32[1040,128]{1,0:T(8,128)S(1)}, f32[520,128]{1,0:T(8,128)}, f32[520,128]{1,0:T(8,128)}) custom-call(f32[128,32,128]{2,1,0:T(8,128)S(1)} %bitcast.11), custom_call_target="tpu_custom_call" | custom-call | tf_op jit(solution)/shard_map/pallas_call | solution.py:264
  5.6 2.6 %collective-permute-start.11 = (f32[520,128]{1,0:T(8,128)}, f32[520,128]{1,0:T(8,128)S(1)}, u32[]{:S(2)}, u32[]{:S(2)}) collective-permute-start(f32[520,128]{1,0:T(8,128)} %get-tuple-element.36), channel_id=1, source_target_pairs={{0,2},{1,3},{2,0},{3,1},{4,6},{5,7},{6,4},{7,5},{8,10},{9,11},{10,... | collective-permute-start | bytes 798728 | tf_op jit(solution)/shard_map/ppermute | solution.py:277
  8.3 1.7 %collective-permute-start.1 = (f32[520,128]{1,0:T(8,128)}, f32[520,128]{1,0:T(8,128)}, u32[]{:S(2)}, u32[]{:S(2)}) collective-permute-start(f32[520,128]{1,0:T(8,128)} %get-tuple-element.41), channel_id=1, source_target_pairs={{0,2},{1,3},{2,0},{3,1},{4,6},{5,7},{6,4},{7,5},{8,10},{9,11},{10,... | collective-permute-start | bytes 798728 | tf_op jit(solution)/shard_map/ppermute | solution.py:277
  10.4 5.3 %collective-permute-done.11.refs_2_ = f32[520,128]{1,0:T(8,128)S(1)} collective-permute-done((f32[520,128]{1,0:T(8,128)}, f32[520,128]{1,0:T(8,128)S(1)}, u32[]{:S(2)}, u32[]{:S(2)}) %collective-permute-start.11) | collective-permute-done | bytes 266272 | tf_op jit(solution)/shard_map/ppermute | solution.py:277
  16.4 4.6 %collective-permute-done.12.refs_3_ = f32[520,128]{1,0:T(8,128)S(1)} collective-permute-done((f32[520,128]{1,0:T(8,128)}, f32[520,128]{1,0:T(8,128)S(1)}, u32[]{:S(2)}, u32[]{:S(2)}) %collective-permute-start.12) | collective-permute-done | bytes 266272 | tf_op jit(solution)/shard_map/ppermute | solution.py:277
  23.6 1.7 %shard_map.69 = (f32[4,352,128]{2,1,0:T(8,128)S(1)}, f32[352,128]{1,0:T(8,128)}, f32[352,128]{1,0:T(8,128)}, f32[352,16]{1,0:T(8,128)S(1)}) custom-call(f32[1040,128]{1,0:T(8,128)S(1)} %get-tuple-element.39.refs_0_, f32[1040,128]{1,0:T(8,128)S(1)} %collective-permute-done.refs_1_, f32[520,128]{1,0:T(8,128)S(1)} %copy-done.6, f32[520,128]{1,0:T(8,128)S(1)} %copy-done.8, ...), custom_call_target="tpu_custom_call" | custom-call | tf_op jit(solution)/shard_map/pallas_call | solution.py:224
  25.3 1.3 %collective-permute-start.17 = (f32[352,128]{1,0:T(8,128)}, f32[352,128]{1,0:T(8,128)}, u32[]{:S(2)}, u32[]{:S(2)}) collective-permute-start(f32[352,128]{1,0:T(8,128)} %get-tuple-element.57.refs_2_), channel_id=1, source_target_pairs={{4,0},{8,4},{12,8},{16,12},{20,16},{24,20},{28,24},{5,1},{9,5},{13... | collective-permute-start | bytes 540680 | tf_op jit(solution)/shard_map/ppermute | solution.py:318
  26.6 5.2 %collective-permute-start.16 = (f32[352,128]{1,0:T(8,128)}, f32[352,128]{1,0:T(8,128)}, u32[]{:S(2)}, u32[]{:S(2)}) collective-permute-start(f32[352,128]{1,0:T(8,128)} %get-tuple-element.58.refs_3_), channel_id=1, source_target_pairs={{0,4},{4,8},{8,12},{12,16},{16,20},{20,24},{24,28},{1,5},{5,9},{9,... | collective-permute-start | bytes 540680 | tf_op jit(solution)/shard_map/ppermute | solution.py:317
  32.4 2.1 %shard_map.66 = (f32[4,352,128]{2,1,0:T(8,128)S(1)}, f32[352,128]{1,0:T(8,128)S(1)}, f32[352,128]{1,0:T(8,128)S(1)}, f32[352,16]{1,0:T(8,128)S(1)}) custom-call(f32[1040,128]{1,0:T(8,128)S(1)} %get-tuple-element.39.refs_0_, f32[1040,128]{1,0:T(8,128)S(1)} %collective-permute-done.refs_1_, f32[520,128]{1,0:T(8,128)} %collective-permute-done.1.refs_2_, ...), custom_call_target="tpu_custom_call" | custom-call | tf_op jit(solution)/shard_map/pallas_call | solution.py:224
  34.5 1.3 %collective-permute-start.7 = (f32[352,128]{1,0:T(8,128)S(1)}, f32[352,128]{1,0:T(8,128)S(1)}, u32[]{:S(2)}, u32[]{:S(2)}) collective-permute-start(f32[352,128]{1,0:T(8,128)S(1)} %get-tuple-element.45.refs_2_), channel_id=1, source_target_pairs={{4,0},{8,4},{12,8},{16,12},{20,16},{24,20},{28,24},{5,1},{9,5},{13... | collective-permute-start | bytes 540680 | tf_op jit(solution)/shard_map/ppermute | solution.py:318
  35.8 4.6 %collective-permute-start.6 = (f32[352,128]{1,0:T(8,128)S(1)}, f32[352,128]{1,0:T(8,128)S(1)}, u32[]{:S(2)}, u32[]{:S(2)}) collective-permute-start(f32[352,128]{1,0:T(8,128)S(1)} %get-tuple-element.46.refs_3_), channel_id=1, source_target_pairs={{0,4},{4,8},{8,12},{12,16},{16,20},{20,24},{24,28},{1,5},{5,9},{9,... | collective-permute-start | bytes 540680 | tf_op jit(solution)/shard_map/ppermute | solution.py:317
  40.4 2.0 %shard_map.70 = (f32[256,128]{1,0:T(8,128)S(1)}, f32[256,128]{1,0:T(8,128)S(1)}, f32[256,128]{1,0:T(8,128)S(1)}, f32[256,128]{1,0:T(8,128)S(1)}) custom-call(f32[4,352,128]{2,1,0:T(8,128)S(1)} %get-tuple-element.55.refs_0_, f32[352,16]{1,0:T(8,128)S(1)} %get-tuple-element.56.refs_1_, f32[352,128]{1,0:T(8,128)} %get-tuple-element.57.refs_2_, ...), custom_call_target="tpu_custom_call" | custom-call | tf_op jit(solution)/shard_map/pallas_call | solution.py:224
  42.5 1.6 %collective-permute-start.14 = (f32[256,128]{1,0:T(8,128)S(1)}, f32[256,128]{1,0:T(8,128)S(1)}, u32[]{:S(2)}, u32[]{:S(2)}) collective-permute-start(f32[256,128]{1,0:T(8,128)S(1)} %get-tuple-element.61), channel_id=1, source_target_pairs={{0,2},{1,3},{2,0},{3,1},{4,6},{5,7},{6,4},{7,5},{8,10},{9,11},{10,... | collective-permute-start | bytes 393224 | tf_op jit(solution)/shard_map/ppermute | solution.py:277
  45.4 2.0 %shard_map.71 = (f32[256,128]{1,0:T(8,128)S(1)}, f32[256,128]{1,0:T(8,128)S(1)}, f32[256,128]{1,0:T(8,128)S(1)}, f32[256,128]{1,0:T(8,128)S(1)}) custom-call(f32[4,352,128]{2,1,0:T(8,128)S(1)} %get-tuple-element.55.refs_0_, f32[352,16]{1,0:T(8,128)S(1)} %get-tuple-element.56.refs_1_, f32[352,128]{1,0:T(8,128)} %collective-permute-done.16.refs_2_, ...), custom_call_target="tpu_custom_call" | custom-call | tf_op jit(solution)/shard_map/pallas_call | solution.py:224
  48.6 1.8 %collective-permute-start.19 = (f32[256,128]{1,0:T(8,128)S(1)}, f32[256,128]{1,0:T(8,128)S(1)}, u32[]{:S(2)}, u32[]{:S(2)}) collective-permute-start(f32[256,128]{1,0:T(8,128)S(1)} %get-tuple-element.65), channel_id=1, source_target_pairs={{0,2},{1,3},{2,0},{3,1},{4,6},{5,7},{6,4},{7,5},{8,10},{9,11},{10,... | collective-permute-start | bytes 393224 | tf_op jit(solution)/shard_map/ppermute | solution.py:277
  51.6 1.8 %collective-permute-start.4 = (f32[256,128]{1,0:T(8,128)S(1)}, f32[256,128]{1,0:T(8,128)S(1)}, u32[]{:S(2)}, u32[]{:S(2)}) collective-permute-start(f32[256,128]{1,0:T(8,128)S(1)} %get-tuple-element.49), channel_id=1, source_target_pairs={{0,2},{1,3},{2,0},{3,1},{4,6},{5,7},{6,4},{7,5},{8,10},{9,11},{10,... | collective-permute-start | bytes 393224 | tf_op jit(solution)/shard_map/ppermute | solution.py:277
  54.9 1.8 %collective-permute-start.9 = (f32[256,128]{1,0:T(8,128)S(1)}, f32[256,128]{1,0:T(8,128)S(1)}, u32[]{:S(2)}, u32[]{:S(2)}) collective-permute-start(f32[256,128]{1,0:T(8,128)S(1)} %get-tuple-element.53), channel_id=1, source_target_pairs={{0,2},{1,3},{2,0},{3,1},{4,6},{5,7},{6,4},{7,5},{8,10},{9,11},{10,... | collective-permute-start | bytes 393224 | tf_op jit(solution)/shard_map/ppermute | solution.py:277
  57.1 1.8 %collective-permute-start.10 = (f32[256,128]{1,0:T(8,128)S(1)}, f32[256,128]{1,0:T(8,128)S(1)}, u32[]{:S(2)}, u32[]{:S(2)}) collective-permute-start(f32[256,128]{1,0:T(8,128)S(1)} %get-tuple-element.54), channel_id=1, source_target_pairs={{0,3},{1,2},{2,1},{3,0},{4,7},{5,6},{6,5},{7,4},{8,11},{9,10},{10,... | collective-permute-start | bytes 393224 | tf_op jit(solution)/shard_map/ppermute | solution.py:277
  59.0 1.2 %shard_map.72.refs_8_ = f32[128,32,128]{2,1,0:T(8,128)} custom-call(f32[256,128]{1,0:T(8,128)S(1)} %get-tuple-element.59.refs_0_, f32[256,128]{1,0:T(8,128)S(1)} %collective-permute-done.13.refs_1_, f32[256,128]{1,0:T(8,128)S(1)} %collective-permute-done.14.refs_2_, f32[256,128]{1,0:T(8,128)S(1)} %collective-permute-done.15.refs_3_, ...), custom_call_target="tpu_custom_call" | custom-call | tf_op jit(solution)/shard_map/pallas_call | solution.py:328
  60.5 2.2 %collective-permute-done.5.refs_3_ = f32[256,128]{1,0:T(8,128)S(1)} collective-permute-done((f32[256,128]{1,0:T(8,128)S(1)}, f32[256,128]{1,0:T(8,128)S(1)}, u32[]{:S(2)}, u32[]{:S(2)}) %collective-permute-start.5) | collective-permute-done | bytes 131104 | tf_op jit(solution)/shard_map/ppermute | solution.py:277
  62.7 3.4 %collective-permute-done.9.refs_6_ = f32[256,128]{1,0:T(8,128)S(1)} collective-permute-done((f32[256,128]{1,0:T(8,128)S(1)}, f32[256,128]{1,0:T(8,128)S(1)}, u32[]{:S(2)}, u32[]{:S(2)}) %collective-permute-start.9) | collective-permute-done | bytes 131104 | tf_op jit(solution)/shard_map/ppermute | solution.py:277
  66.1 2.2 %collective-permute-done.10.refs_7_ = f32[256,128]{1,0:T(8,128)S(1)} collective-permute-done((f32[256,128]{1,0:T(8,128)S(1)}, f32[256,128]{1,0:T(8,128)S(1)}, u32[]{:S(2)}, u32[]{:S(2)}) %collective-permute-start.10) | collective-permute-done | bytes 131104 | tf_op jit(solution)/shard_map/ppermute | solution.py:277
  68.4 1.2 %shard_map.73 = f32[128,32,128]{2,1,0:T(8,128)} custom-call(f32[256,128]{1,0:T(8,128)S(1)} %get-tuple-element.47.refs_0_, f32[256,128]{1,0:T(8,128)S(1)} %collective-permute-done.3.refs_1_, f32[256,128]{1,0:T(8,128)S(1)} %collective-permute-done.4.refs_2_, f32[256,128]{1,0:T(8,128)S(1)} %collective-permute-done.5.refs_3_, ...), custom_call_target="tpu_custom_call", output_to_operand_aliasing={{}: (8, {})} | custom-call | tf_op jit(solution)/shard_map/pallas_call | solution.py:328
  (57 shorter events, 10.8 us)
Async XLA Ops:
  0.0 21.7 %copy-start.2 = (f32[352,1]{1,0:T(8,128)S(1)}, f32[352,1]{1,0:T(8,128)}, u32[]{:S(2)}) copy-start(f32[352,1]{1,0:T(8,128)} %constant.35.clone.refs_6_) | copy-start | bytes 4228
  0.0 21.7 %copy-start.3 = (f32[352,1]{1,0:T(8,128)S(1)}, f32[352,1]{1,0:T(8,128)}, u32[]{:S(2)}) copy-start(f32[352,1]{1,0:T(8,128)} %constant.34.clone.refs_5_) | copy-start | bytes 4228
  0.0 21.7 %copy-start.4 = (bf16[2,2,176,384]{3,2,1,0:T(8,128)(2,1)S(1)}, bf16[2,2,176,384]{3,2,1,0:T(8,128)(2,1)}, u32[]{:S(2)}) copy-start(bf16[2,2,176,384]{3,2,1,0:T(8,128)(2,1)} %constant.32.clone.refs_4_) | copy-start | bytes 1622020
  5.1 16.6 %collective-permute-start = (f32[1040,128]{1,0:T(8,128)S(1)}, f32[1040,128]{1,0:T(8,128)S(1)}, u32[]{:S(2)}, u32[]{:S(2)}) collective-permute-start(f32[1040,128]{1,0:T(8,128)S(1)} %get-tuple-element.40), channel_id=1, source_target_pairs={{0,1},{1,0},{2,3},{3,2},{4,5},{5,4},{6,7},{7,6},{8,9},{9,8},{10,11... | collective-permute-start | bytes 1597448 | tf_op jit(solution)/shard_map/ppermute | solution.py:277
  5.6 10.0 %collective-permute-start.11 = (f32[520,128]{1,0:T(8,128)}, f32[520,128]{1,0:T(8,128)S(1)}, u32[]{:S(2)}, u32[]{:S(2)}) collective-permute-start(f32[520,128]{1,0:T(8,128)} %get-tuple-element.36), channel_id=1, source_target_pairs={{0,2},{1,3},{2,0},{3,1},{4,6},{5,7},{6,4},{7,5},{8,10},{9,11},{10,... | collective-permute-start | bytes 798728 | tf_op jit(solution)/shard_map/ppermute | solution.py:277
  8.2 12.7 %collective-permute-start.12 = (f32[520,128]{1,0:T(8,128)}, f32[520,128]{1,0:T(8,128)S(1)}, u32[]{:S(2)}, u32[]{:S(2)}) collective-permute-start(f32[520,128]{1,0:T(8,128)} %get-tuple-element.37), channel_id=1, source_target_pairs={{0,3},{1,2},{2,1},{3,0},{4,7},{5,6},{6,5},{7,4},{8,11},{9,10},{10,... | collective-permute-start | bytes 798728 | tf_op jit(solution)/shard_map/ppermute | solution.py:277
  8.3 23.6 %collective-permute-start.1 = (f32[520,128]{1,0:T(8,128)}, f32[520,128]{1,0:T(8,128)}, u32[]{:S(2)}, u32[]{:S(2)}) collective-permute-start(f32[520,128]{1,0:T(8,128)} %get-tuple-element.41), channel_id=1, source_target_pairs={{0,2},{1,3},{2,0},{3,1},{4,6},{5,7},{6,4},{7,5},{8,10},{9,11},{10,... | collective-permute-start | bytes 798728 | tf_op jit(solution)/shard_map/ppermute | solution.py:277
  10.1 22.3 %collective-permute-start.2 = (f32[520,128]{1,0:T(8,128)}, f32[520,128]{1,0:T(8,128)}, u32[]{:S(2)}, u32[]{:S(2)}) collective-permute-start(f32[520,128]{1,0:T(8,128)} %get-tuple-element.42), channel_id=1, source_target_pairs={{0,3},{1,2},{2,1},{3,0},{4,7},{5,6},{6,5},{7,4},{8,11},{9,10},{10,... | collective-permute-start | bytes 798728 | tf_op jit(solution)/shard_map/ppermute | solution.py:277
  25.3 17.2 %collective-permute-start.17 = (f32[352,128]{1,0:T(8,128)}, f32[352,128]{1,0:T(8,128)}, u32[]{:S(2)}, u32[]{:S(2)}) collective-permute-start(f32[352,128]{1,0:T(8,128)} %get-tuple-element.57.refs_2_), channel_id=1, source_target_pairs={{4,0},{8,4},{12,8},{16,12},{20,16},{24,20},{28,24},{5,1},{9,5},{13... | collective-permute-start | bytes 540680 | tf_op jit(solution)/shard_map/ppermute | solution.py:318
  26.6 18.5 %collective-permute-start.16 = (f32[352,128]{1,0:T(8,128)}, f32[352,128]{1,0:T(8,128)}, u32[]{:S(2)}, u32[]{:S(2)}) collective-permute-start(f32[352,128]{1,0:T(8,128)} %get-tuple-element.58.refs_3_), channel_id=1, source_target_pairs={{0,4},{4,8},{8,12},{12,16},{16,20},{20,24},{24,28},{1,5},{5,9},{9,... | collective-permute-start | bytes 540680 | tf_op jit(solution)/shard_map/ppermute | solution.py:317
  34.5 14.1 %collective-permute-start.7 = (f32[352,128]{1,0:T(8,128)S(1)}, f32[352,128]{1,0:T(8,128)S(1)}, u32[]{:S(2)}, u32[]{:S(2)}) collective-permute-start(f32[352,128]{1,0:T(8,128)S(1)} %get-tuple-element.45.refs_2_), channel_id=1, source_target_pairs={{4,0},{8,4},{12,8},{16,12},{20,16},{24,20},{28,24},{5,1},{9,5},{13... | collective-permute-start | bytes 540680 | tf_op jit(solution)/shard_map/ppermute | solution.py:318
  35.8 14.6 %collective-permute-start.6 = (f32[352,128]{1,0:T(8,128)S(1)}, f32[352,128]{1,0:T(8,128)S(1)}, u32[]{:S(2)}, u32[]{:S(2)}) collective-permute-start(f32[352,128]{1,0:T(8,128)S(1)} %get-tuple-element.46.refs_3_), channel_id=1, source_target_pairs={{0,4},{4,8},{8,12},{12,16},{16,20},{20,24},{24,28},{1,5},{5,9},{9,... | collective-permute-start | bytes 540680 | tf_op jit(solution)/shard_map/ppermute | solution.py:317
  42.4 5.0 %collective-permute-start.13 = (f32[256,128]{1,0:T(8,128)S(1)}, f32[256,128]{1,0:T(8,128)S(1)}, u32[]{:S(2)}, u32[]{:S(2)}) collective-permute-start(f32[256,128]{1,0:T(8,128)S(1)} %get-tuple-element.60), channel_id=1, source_target_pairs={{0,1},{1,0},{2,3},{3,2},{4,5},{5,4},{6,7},{7,6},{8,9},{9,8},{10,11... | collective-permute-start | bytes 393224 | tf_op jit(solution)/shard_map/ppermute | solution.py:277
  42.5 6.1 %collective-permute-start.14 = (f32[256,128]{1,0:T(8,128)S(1)}, f32[256,128]{1,0:T(8,128)S(1)}, u32[]{:S(2)}, u32[]{:S(2)}) collective-permute-start(f32[256,128]{1,0:T(8,128)S(1)} %get-tuple-element.61), channel_id=1, source_target_pairs={{0,2},{1,3},{2,0},{3,1},{4,6},{5,7},{6,4},{7,5},{8,10},{9,11},{10,... | collective-permute-start | bytes 393224 | tf_op jit(solution)/shard_map/ppermute | solution.py:277
  45.1 6.5 %collective-permute-start.15 = (f32[256,128]{1,0:T(8,128)S(1)}, f32[256,128]{1,0:T(8,128)S(1)}, u32[]{:S(2)}, u32[]{:S(2)}) collective-permute-start(f32[256,128]{1,0:T(8,128)S(1)} %get-tuple-element.62), channel_id=1, source_target_pairs={{0,3},{1,2},{2,1},{3,0},{4,7},{5,6},{6,5},{7,4},{8,11},{9,10},{10,... | collective-permute-start | bytes 393224 | tf_op jit(solution)/shard_map/ppermute | solution.py:277
  47.4 6.0 %collective-permute-start.3 = (f32[256,128]{1,0:T(8,128)S(1)}, f32[256,128]{1,0:T(8,128)S(1)}, u32[]{:S(2)}, u32[]{:S(2)}) collective-permute-start(f32[256,128]{1,0:T(8,128)S(1)} %get-tuple-element.48), channel_id=1, source_target_pairs={{0,1},{1,0},{2,3},{3,2},{4,5},{5,4},{6,7},{7,6},{8,9},{9,8},{10,11... | collective-permute-start | bytes 393224 | tf_op jit(solution)/shard_map/ppermute | solution.py:277
  48.6 4.8 %collective-permute-start.18 = (f32[256,128]{1,0:T(8,128)S(1)}, f32[256,128]{1,0:T(8,128)S(1)}, u32[]{:S(2)}, u32[]{:S(2)}) collective-permute-start(f32[256,128]{1,0:T(8,128)S(1)} %get-tuple-element.64), channel_id=1, source_target_pairs={{0,1},{1,0},{2,3},{3,2},{4,5},{5,4},{6,7},{7,6},{8,9},{9,8},{10,11... | collective-permute-start | bytes 393224 | tf_op jit(solution)/shard_map/ppermute | solution.py:277
  48.6 6.3 %collective-permute-start.19 = (f32[256,128]{1,0:T(8,128)S(1)}, f32[256,128]{1,0:T(8,128)S(1)}, u32[]{:S(2)}, u32[]{:S(2)}) collective-permute-start(f32[256,128]{1,0:T(8,128)S(1)} %get-tuple-element.65), channel_id=1, source_target_pairs={{0,2},{1,3},{2,0},{3,1},{4,6},{5,7},{6,4},{7,5},{8,10},{9,11},{10,... | collective-permute-start | bytes 393224 | tf_op jit(solution)/shard_map/ppermute | solution.py:277
  50.4 6.7 %collective-permute-start.20 = (f32[256,128]{1,0:T(8,128)S(1)}, f32[256,128]{1,0:T(8,128)S(1)}, u32[]{:S(2)}, u32[]{:S(2)}) collective-permute-start(f32[256,128]{1,0:T(8,128)S(1)} %get-tuple-element.66), channel_id=1, source_target_pairs={{0,3},{1,2},{2,1},{3,0},{4,7},{5,6},{6,5},{7,4},{8,11},{9,10},{10,... | collective-permute-start | bytes 393224 | tf_op jit(solution)/shard_map/ppermute | solution.py:277
  51.6 8.9 %collective-permute-start.4 = (f32[256,128]{1,0:T(8,128)S(1)}, f32[256,128]{1,0:T(8,128)S(1)}, u32[]{:S(2)}, u32[]{:S(2)}) collective-permute-start(f32[256,128]{1,0:T(8,128)S(1)} %get-tuple-element.49), channel_id=1, source_target_pairs={{0,2},{1,3},{2,0},{3,1},{4,6},{5,7},{6,4},{7,5},{8,10},{9,11},{10,... | collective-permute-start | bytes 393224 | tf_op jit(solution)/shard_map/ppermute | solution.py:277
  53.4 9.3 %collective-permute-start.5 = (f32[256,128]{1,0:T(8,128)S(1)}, f32[256,128]{1,0:T(8,128)S(1)}, u32[]{:S(2)}, u32[]{:S(2)}) collective-permute-start(f32[256,128]{1,0:T(8,128)S(1)} %get-tuple-element.50), channel_id=1, source_target_pairs={{0,3},{1,2},{2,1},{3,0},{4,7},{5,6},{6,5},{7,4},{8,11},{9,10},{10,... | collective-permute-start | bytes 393224 | tf_op jit(solution)/shard_map/ppermute | solution.py:277
  53.4 9.3 %collective-permute-start.8 = (f32[256,128]{1,0:T(8,128)S(1)}, f32[256,128]{1,0:T(8,128)S(1)}, u32[]{:S(2)}, u32[]{:S(2)}) collective-permute-start(f32[256,128]{1,0:T(8,128)S(1)} %get-tuple-element.52), channel_id=1, source_target_pairs={{0,1},{1,0},{2,3},{3,2},{4,5},{5,4},{6,7},{7,6},{8,9},{9,8},{10,11... | collective-permute-start | bytes 393224 | tf_op jit(solution)/shard_map/ppermute | solution.py:277
  54.9 11.2 %collective-permute-start.9 = (f32[256,128]{1,0:T(8,128)S(1)}, f32[256,128]{1,0:T(8,128)S(1)}, u32[]{:S(2)}, u32[]{:S(2)}) collective-permute-start(f32[256,128]{1,0:T(8,128)S(1)} %get-tuple-element.53), channel_id=1, source_target_pairs={{0,2},{1,3},{2,0},{3,1},{4,6},{5,7},{6,4},{7,5},{8,10},{9,11},{10,... | collective-permute-start | bytes 393224 | tf_op jit(solution)/shard_map/ppermute | solution.py:277
  57.1 11.2 %collective-permute-start.10 = (f32[256,128]{1,0:T(8,128)S(1)}, f32[256,128]{1,0:T(8,128)S(1)}, u32[]{:S(2)}, u32[]{:S(2)}) collective-permute-start(f32[256,128]{1,0:T(8,128)S(1)} %get-tuple-element.54), channel_id=1, source_target_pairs={{0,3},{1,2},{2,1},{3,0},{4,7},{5,6},{6,5},{7,4},{8,11},{9,10},{10,... | collective-permute-start | bytes 393224 | tf_op jit(solution)/shard_map/ppermute | solution.py:277
  (7 other events, 32.9 us)

commit v3 on v2

--- a/solution.py
+++ b/solution.py
@@ -12,7 +12,9 @@
 PENALTY = 12.0
 LANES = 128
 VMEM = pl.BlockSpec(memory_space=pltpu.VMEM)
-PARAMS = pltpu.CompilerParams(vmem_limit_bytes=32 * 1024 * 1024)
+ANY = pl.BlockSpec(memory_space=pl.ANY)
+PARAMS = pltpu.CompilerParams(vmem_limit_bytes=16 * 1024 * 1024)
+COST = pl.CostEstimate(flops=1024, bytes_accessed=1024, transcendentals=0)
 
 
 def split(values):
@@ -58,8 +60,8 @@
     return jnp.concatenate([high, high, low], axis=axis)
 
 
-def pack_kernel(jobs, row_count, count, cells, width, tiles, split_at, x_ref, *refs):
-    outs, (held, arrived) = refs[:-2], refs[-2:]
+def pack_kernel(jobs, earlier, row_count, count, cells, width, tiles, split_at, x_ref, *refs):
+    outs, (held, arrived) = refs[earlier:-2], refs[-2:]
     me = lax.axis_index("span")
     lines = x_ref.shape[1]
     pitch = held.shape[0] // cells
@@ -166,8 +168,8 @@
 
 
 def forward_kernel(rows, count, cells, column, *refs):
-    blocks, (forward_ref, fluid_ref, solid_ref, mask_ref, side_ref), outs = refs[:count], refs[count : count + 5], refs[count + 5 :]
-    spectrum_ref, first_ref, last_ref, sides_ref = outs
+    blocks, (forward_ref, fluid_ref, solid_ref, mask_ref, side_ref) = refs[:count], refs[count : count + 5]
+    spectrum_ref, first_ref, last_ref, sides_ref = refs[-4:]
     size = rows * cells + 8
     blocks = [ref.at[column * size : (column + 1) * size] if ref.shape[0] > size else ref for ref in blocks]
     spectra, sides = transform(rows, count, cells, blocks, forward_ref)
@@ -179,9 +181,8 @@
     sides_ref[...] = sides * side_factor(side_ref, fluid, solid)
 
 
-def sweep_kernel(wanted, rows, count, cells, *refs):
-    spectrum_ref, sides_ref, low_ref, high_ref, inverse_ref, fluid_ref, solid_ref, mask_ref = refs[:8]
-    outs = refs[8:]
+def sweep_rows(wanted, rows, refs):
+    spectrum_ref, sides_ref, low_ref, high_ref, fluid_ref, solid_ref, mask_ref = refs
     fluid, solid = fluid_ref[...], solid_ref[...]
     sides = sides_ref[...]
     needed = sorted({at for row in wanted for at in (row - 1, row, row + 1) if 0 <= at < rows})
@@ -191,27 +192,38 @@
         one[-1] = low_ref[...]
     if rows - 1 in wanted:
         one[rows] = high_ref[...]
-    sweeps = [
+    return [
         second_sweep(spectrum_ref[row], one[row], one[row - 1], one[row + 1], sides, 2 * row, diagonal[row])
         for row in wanted
     ]
-    inverse_rows(sweeps, count, cells, inverse_ref, outs)
+
+
+def inner_kernel(rows, count, cells, *refs):
+    sweeps = sweep_rows(range(1, rows - 1), rows, refs[:7])
+    inverse_rows(sweeps, count, cells, refs[7], refs[-count:])
+
+
+def edge_kernel(rows, count, cells, *refs):
+    half = count // 2
+    inner, outs = refs[8 : 8 + half], refs[-count:]
+    sweeps = sweep_rows((0, rows - 1), rows, refs[:7])
+    for d in range(half):
+        outs[d][2 * cells :, :] = inner[d][...]
+    inverse_rows(sweeps, count, cells, refs[7], outs)
 
 
 def unpack_kernel(row_groups, row_count, count, cells, tiles, column, *refs):
     me = lax.axis_index("span")
-    blocks = refs[: len(row_groups) * count]
     out_ref, held, done = refs[-3:]
     pitch = held.shape[0] // cells
     lines = count * tiles * row_count
-    for g, rows in enumerate(row_groups):
-        for d in range(count):
-            source = jnp.bitwise_xor(me, d)
-            for i, row in enumerate(rows):
-                for tile in range(tiles):
-                    held[pl.ds((source * tiles + tile) * row_count + row, cells, stride=pitch), :] = blocks[g * count + d][
-                        i * cells : (i + 1) * cells, tile * LANES : (tile + 1) * LANES
-                    ]
+    for at, (d, rows) in enumerate(row_groups):
+        source = jnp.bitwise_xor(me, d)
+        for i, row in enumerate(rows):
+            for tile in range(tiles):
+                held[pl.ds((source * tiles + tile) * row_count + row, cells, stride=pitch), :] = refs[at][
+                    i * cells : (i + 1) * cells, tile * LANES : (tile + 1) * LANES
+                ]
     copy = pltpu.make_async_copy(
         held.reshape(cells, pitch, LANES).at[:, pl.ds(0, lines)], out_ref.at[:, pl.ds(column * lines, lines)], done
     )
@@ -219,15 +231,16 @@
     copy.wait()
 
 
-def call(kernel, outs, *args):
+def call(kernel, outs, args, earlier=()):
     shapes = [jax.ShapeDtypeStruct(shape, jnp.float32) for shape in outs]
     return pl.pallas_call(
         kernel,
         out_shape=shapes,
-        in_specs=[VMEM] * len(args),
+        in_specs=[VMEM] * len(args) + [ANY] * len(earlier),
         out_specs=[VMEM] * len(outs),
         compiler_params=PARAMS,
-    )(*args)
+        cost_estimate=COST,
+    )(*args, *earlier)
 
 
 def local(pressure_source, solid_mask):
@@ -260,33 +273,33 @@
 
     size = rows * cells + 8
 
-    def pack(jobs, sizes, limit):
+    def pack(jobs, sizes, earlier):
         return pl.pallas_call(
-            functools.partial(pack_kernel, jobs, rows, count, cells, width, tiles, 4),
+            functools.partial(pack_kernel, jobs, len(earlier), rows, count, cells, width, tiles, 4),
             out_shape=[jax.ShapeDtypeStruct((places * size, width), jnp.float32) for places in sizes],
-            in_specs=[pl.BlockSpec(memory_space=pl.ANY)],
+            in_specs=[ANY] * (1 + len(earlier)),
             out_specs=[VMEM] * len(sizes),
             scratch_shapes=[
                 pltpu.VMEM((cells * (lines + 8), LANES), jnp.float32),
                 pltpu.SemaphoreType.DMA((4,)),
             ],
-            compiler_params=pltpu.CompilerParams(vmem_limit_bytes=limit * 1024 * 1024),
-        )(source)
+            compiler_params=PARAMS,
+            cost_estimate=COST,
+        )(source, *earlier)
 
     def swap(block, d):
         return lax.ppermute(block, "span", [(i, i ^ d) for i in range(count)])
 
     far = range(half, count)
-    packed = pack([(d - half, 0, d, 0) for d in far], [1] * half, 56)
-    got = {(0, d): swap(block, d) for d, block in zip(far, packed)}
-    source = lax.optimization_barrier((source, *packed))[0]
+    first_packed = pack([(d - half, 0, d, 0) for d in far], [1] * half, ())
+    got = {(0, d): swap(block, d) for d, block in zip(far, first_packed)}
     jobs = [(at, part, d, part) for at, d in enumerate(range(half)) for part in range(parts)]
     sizes = [parts] * half
     for part in range(1, parts):
         for d in far:
             jobs.append((len(sizes), 0, d, part))
             sizes.append(1)
-    packed = pack(jobs, sizes, 32)
+    packed = pack(jobs, sizes, (first_packed[-1],))
     near = [packed[0]] + [swap(packed[d], d) for d in range(1, half)]
     at = half
     for part in range(1, parts):
@@ -296,44 +309,55 @@
 
     up = [(i, i + 1) for i in range(plane_count - 1)]
     down = [(i + 1, i) for i in range(plane_count - 1)]
-    state, inner_got, edge_got = [], [], []
-
-    def sweep(wanted, part, low, high):
-        spectrum, sides, mask = state[part][0], state[part][1], state[part][2]
-        blocks = call(
-            functools.partial(sweep_kernel, wanted, rows, count, cells),
-            [(len(wanted) * cells, width)] * count,
-            spectrum, sides, low, high, inverse, fluid, solid, mask,
-        )
-        return [blocks[0]] + [swap(blocks[d], d) for d in range(1, count)]
-
+    state, blocks, groups, earlier = [], [], [], ()
     for part in range(parts):
         mask, kinds = masks(part)
         spectrum, first, last, sides = call(
             functools.partial(forward_kernel, rows, count, cells, part),
             [(rows, modes, width), (modes, width), (modes, width), (modes, 16)],
-            *near, *[got[part, d] for d in far], forward, fluid, solid, mask, kinds,
+            [*near, *[got[part, d] for d in far], forward, fluid, solid, mask, kinds],
+            earlier,
         )
         low = lax.ppermute(last, "plane", up)
         high = lax.ppermute(first, "plane", down)
-        state.append((spectrum, sides, mask, low, high))
-        inner_got.append(sweep(inner, part, first, last))
-    for part in range(parts):
-        edge_got.append(sweep(edges, part, state[part][3], state[part][4]))
-
+        state.append((spectrum, sides, low, high, fluid, solid, mask))
+        inner_out = call(
+            functools.partial(inner_kernel, rows, count, cells),
+            [(len(inner) * cells, width)] * count,
+            [spectrum, sides, first, last, fluid, solid, mask, inverse],
+        )
+        blocks.append(inner_out)
+        earlier = (inner_out[-1],)
+    sent = [[swap(block[d], d) for d in far] for block in blocks]
     result = None
     for part in range(parts):
-        blocks = inner_got[part] + edge_got[part]
-        held = count * tiles * rows + 8
+        edge_out = call(
+            functools.partial(edge_kernel, rows, count, cells),
+            [(rows * cells, width)] * half + [(2 * cells, width)] * half,
+            [*state[part], inverse, *blocks[part][:half]],
+            earlier,
+        )
+        earlier = (edge_out[-1],)
+        pieces = [(0, edges + inner, edge_out[0])]
+        pieces += [(d, inner, block) for d, block in zip(far, sent[part])]
+        pieces += [(d, edges, swap(edge_out[d], d)) for d in far]
+        pieces += [(d, edges + inner, swap(edge_out[d], d)) for d in range(1, half)]
+        previous = () if result is None else (result,)
         result = pl.pallas_call(
-            functools.partial(unpack_kernel, (inner, edges), rows, count, cells, tiles, part),
+            functools.partial(
+                unpack_kernel, [piece[:2] for piece in pieces], rows, count, cells, tiles, part
+            ),
             out_shape=jax.ShapeDtypeStruct((cells, lines, LANES), jnp.float32),
-            in_specs=[VMEM] * len(blocks) + [pl.BlockSpec(memory_space=pl.ANY)] * (result is not None),
-            out_specs=pl.BlockSpec(memory_space=pl.ANY),
-            scratch_shapes=[pltpu.VMEM((cells * held, LANES), jnp.float32), pltpu.SemaphoreType.DMA],
-            input_output_aliases={} if result is None else {len(blocks): 0},
+            in_specs=[VMEM] * len(pieces) + [ANY] * len(previous),
+            out_specs=ANY,
+            scratch_shapes=[
+                pltpu.VMEM((cells * (count * tiles * rows + 8), LANES), jnp.float32),
+                pltpu.SemaphoreType.DMA,
+            ],
+            input_output_aliases={len(pieces): 0} if previous else {},
             compiler_params=PARAMS,
-        )(*blocks, *([] if result is None else [result]))
+            cost_estimate=COST,
+        )(*[piece[2] for piece in pieces], *previous)
     return result.reshape(cells, columns // LANES, rows, LANES).transpose(0, 2, 1, 3).reshape(cells, rows, columns)
 
 

time: 69.9 us -> 73 us (1.044)
  the two profiles are of different devices: /device:TPU:0 before, /device:TPU:25 now
where the time goes in v3:
time: 73 us; the launch traced here: 72.6 us
  starting transfers between devices  27.7 us (38%)
  waiting for transfers between devices  23.8 us (33%)
  Pallas kernels  17.3 us (24%)
  local copies, waits for them, and re-layouts  3.65 us (5%)
    ppermute x15, waiting for transfers between devices, swap(): return lax.ppermute(block, 'span', [(i, i ^ d) for i in range(count)])  23.8 us
    ppermute x15, starting transfers between devices, swap(): return lax.ppermute(block, 'span', [(i, i ^ d) for i in range(count)])  15.5 us
    pallas_call x6, Pallas kernels, call(): pl.pallas_call(kernel, out_shape=shapes, in_specs=[VMEM] * len(args) + [A...  10.7 us
    ppermute x2, starting transfers between devices, local(): high = lax.ppermute(first, 'plane', down)  6.74 us
    ppermute x2, starting transfers between devices, local(): low = lax.ppermute(last, 'plane', up)  5.38 us
    pallas_call x2, Pallas kernels, pack(): pl.pallas_call(functools.partial(pack_kernel, jobs, len(earlier), rows, c...  4.1 us
    unnamed x16, local copies, waits for them, and re-layouts  3.28 us
    pallas_call x2, Pallas kernels, local(): pl.pallas_call(functools.partial(unpack_kernel, [piece[:2] for piece in p...  2.45 us
  transfers between devices with their start and end apart: 19, of which 8 were waited for; matrix products, arithmetic and copies ran while one was open for 1% of the time, Pallas kernels for 16%

profile of v3, /device:TPU:25, one launch (start us, length us, event | category | flops | bytes accessed | tf_op | source)
XLA Modules:
  0.0 72.6 jit_solution(4762376276043035653)
XLA Ops:
  0.0 1.6 %copy-done.1 = f32[128,4,1024]{2,1,0:T(4,128)S(1)} copy-done((f32[128,4,1024]{2,1,0:T(4,128)S(1)}, f32[128,4,1024]{2,1,0:T(4,128)}, u32[]{:S(2)}) %copy-start.1) | copy-done | bytes 2097176
  1.6 1.6 %shard_map.64 = (f32[520,128]{1,0:T(8,128)}, f32[520,128]{1,0:T(8,128)S(1)}) custom-call(f32[128,32,128]{2,1,0:T(8,128)S(1)} %bitcast.10), custom_call_target="tpu_custom_call" | custom-call | flops 1024 | bytes 1024 | tf_op jit(solution)/shard_map/pallas_call | solution.py:277
  3.2 2.5 %shard_map.65 = (f32[1040,128]{1,0:T(8,128)S(1)}, f32[1040,128]{1,0:T(8,128)}, f32[520,128]{1,0:T(8,128)}, f32[520,128]{1,0:T(8,128)}) custom-call(f32[128,32,128]{2,1,0:T(8,128)S(1)} %bitcast.11, f32[520,128]{1,0:T(8,128)S(1)} %get-tuple-element.35.refs_0_), custom_call_target="tpu_custom_call" | custom-call | flops 1024 | bytes 1024 | tf_op jit(solution)/shard_map/pallas_call | solution.py:277
  7.9 1.3 %collective-permute-start.1 = (f32[520,128]{1,0:T(8,128)}, f32[520,128]{1,0:T(8,128)}, u32[]{:S(2)}, u32[]{:S(2)}) collective-permute-start(f32[520,128]{1,0:T(8,128)} %get-tuple-element.38), channel_id=1, source_target_pairs={{0,2},{1,3},{2,0},{3,1},{4,6},{5,7},{6,4},{7,5},{8,10},{9,11},{10,... | collective-permute-start | bytes 798728 | tf_op jit(solution)/shard_map/ppermute | solution.py:291
  10.6 9.5 %collective-permute-done.3.refs_2_ = f32[520,128]{1,0:T(8,128)} collective-permute-done((f32[520,128]{1,0:T(8,128)}, f32[520,128]{1,0:T(8,128)}, u32[]{:S(2)}, u32[]{:S(2)}) %collective-permute-start.3) | collective-permute-done | bytes 266272 | tf_op jit(solution)/shard_map/ppermute | solution.py:291
  21.8 2.6 %shard_map.66 = (f32[4,352,128]{2,1,0:T(8,128)S(1)}, f32[352,128]{1,0:T(8,128)}, f32[352,128]{1,0:T(8,128)}, f32[352,16]{1,0:T(8,128)S(1)}) custom-call(f32[1040,128]{1,0:T(8,128)S(1)} %get-tuple-element.36.refs_0_, f32[1040,128]{1,0:T(8,128)S(1)} %collective-permute-done.refs_1_, f32[520,128]{1,0:T(8,128)} %collective-permute-done.3.refs_2_, ...), custom_call_target="tpu_custom_call" | custom-call | flops 1024 | bytes 1024 | tf_op jit(solution)/shard_map/pallas_call | solution.py:236
  24.4 3.0 %collective-permute-start.8 = (f32[352,128]{1,0:T(8,128)}, f32[352,128]{1,0:T(8,128)}, u32[]{:S(2)}, u32[]{:S(2)}) collective-permute-start(f32[352,128]{1,0:T(8,128)} %get-tuple-element.43.refs_2_), channel_id=1, source_target_pairs={{4,0},{8,4},{12,8},{16,12},{20,16},{24,20},{28,24},{5,1},{9,5},{13... | collective-permute-start | bytes 540680 | tf_op jit(solution)/shard_map/ppermute | solution.py:322
  27.4 3.0 %collective-permute-start.7 = (f32[352,128]{1,0:T(8,128)}, f32[352,128]{1,0:T(8,128)}, u32[]{:S(2)}, u32[]{:S(2)}) collective-permute-start(f32[352,128]{1,0:T(8,128)} %get-tuple-element.44.refs_3_), channel_id=1, source_target_pairs={{0,4},{4,8},{8,12},{12,16},{16,20},{20,24},{24,28},{1,5},{5,9},{9,... | collective-permute-start | bytes 540680 | tf_op jit(solution)/shard_map/ppermute | solution.py:321
  30.4 2.0 %shard_map.67 = (f32[256,128]{1,0:T(8,128)S(1)}, f32[256,128]{1,0:T(8,128)S(1)}, f32[256,128]{1,0:T(8,128)S(1)}, f32[256,128]{1,0:T(8,128)S(1)}) custom-call(f32[4,352,128]{2,1,0:T(8,128)S(1)} %get-tuple-element.41.refs_0_, f32[352,16]{1,0:T(8,128)S(1)} %get-tuple-element.42.refs_1_, f32[352,128]{1,0:T(8,128)} %get-tuple-element.43.refs_2_, ...), custom_call_target="tpu_custom_call" | custom-call | flops 1024 | bytes 1024 | tf_op jit(solution)/shard_map/pallas_call | solution.py:236
  32.4 2.1 %shard_map.68 = (f32[4,352,128]{2,1,0:T(8,128)S(1)}, f32[352,128]{1,0:T(8,128)S(1)}, f32[352,128]{1,0:T(8,128)S(1)}, f32[352,16]{1,0:T(8,128)S(1)}) custom-call(f32[1040,128]{1,0:T(8,128)S(1)} %get-tuple-element.36.refs_0_, f32[1040,128]{1,0:T(8,128)S(1)} %collective-permute-done.refs_1_, f32[520,128]{1,0:T(8,128)} %collective-permute-done.1.refs_2_, ...), custom_call_target="tpu_custom_call" | custom-call | flops 1024 | bytes 1024 | tf_op jit(solution)/shard_map/pallas_call | solution.py:236
  34.6 2.4 %collective-permute-start.5 = (f32[352,128]{1,0:T(8,128)S(1)}, f32[352,128]{1,0:T(8,128)S(1)}, u32[]{:S(2)}, u32[]{:S(2)}) collective-permute-start(f32[352,128]{1,0:T(8,128)S(1)} %get-tuple-element.48.refs_3_), channel_id=1, source_target_pairs={{0,4},{4,8},{8,12},{12,16},{16,20},{20,24},{24,28},{1,5},{5,9},{9,... | collective-permute-start | bytes 540680 | tf_op jit(solution)/shard_map/ppermute | solution.py:321
  37.0 3.8 %collective-permute-start.6 = (f32[352,128]{1,0:T(8,128)S(1)}, f32[352,128]{1,0:T(8,128)S(1)}, u32[]{:S(2)}, u32[]{:S(2)}) collective-permute-start(f32[352,128]{1,0:T(8,128)S(1)} %get-tuple-element.49.refs_2_), channel_id=1, source_target_pairs={{4,0},{8,4},{12,8},{16,12},{20,16},{24,20},{28,24},{5,1},{9,5},{13... | collective-permute-start | bytes 540680 | tf_op jit(solution)/shard_map/ppermute | solution.py:322
  41.8 2.0 %shard_map.70 = (f32[512,128]{1,0:T(8,128)S(1)}, f32[512,128]{1,0:T(8,128)S(1)}, f32[256,128]{1,0:T(8,128)S(1)}, f32[256,128]{1,0:T(8,128)S(1)}) custom-call(f32[4,352,128]{2,1,0:T(8,128)S(1)} %get-tuple-element.41.refs_0_, f32[352,16]{1,0:T(8,128)S(1)} %get-tuple-element.42.refs_1_, f32[352,128]{1,0:T(8,128)} %collective-permute-done.7.refs_2_, ...), custom_call_target="tpu_custom_call" | custom-call | flops 1024 | bytes 1024 | tf_op jit(solution)/shard_map/pallas_call | solution.py:236
  43.8 2.7 %collective-permute-start.18 = (f32[512,128]{1,0:T(8,128)S(1)}, f32[512,128]{1,0:T(8,128)S(1)}, u32[]{:S(2)}, u32[]{:S(2)}) collective-permute-start(f32[512,128]{1,0:T(8,128)S(1)} %get-tuple-element.64), channel_id=1, source_target_pairs={{0,1},{1,0},{2,3},{3,2},{4,5},{5,4},{6,7},{7,6},{8,9},{9,8},{10,11... | collective-permute-start | bytes 786440 | tf_op jit(solution)/shard_map/ppermute | solution.py:291
  46.5 1.3 %collective-permute-start.14 = (f32[256,128]{1,0:T(8,128)S(1)}, f32[256,128]{1,0:T(8,128)S(1)}, u32[]{:S(2)}, u32[]{:S(2)}) collective-permute-start(f32[256,128]{1,0:T(8,128)S(1)} %get-tuple-element.62), channel_id=1, source_target_pairs={{0,2},{1,3},{2,0},{3,1},{4,6},{5,7},{6,4},{7,5},{8,10},{9,11},{10,... | collective-permute-start | bytes 393224 | tf_op jit(solution)/shard_map/ppermute | solution.py:291
  48.2 1.3 %collective-permute-start.16 = (f32[256,128]{1,0:T(8,128)S(1)}, f32[256,128]{1,0:T(8,128)S(1)}, u32[]{:S(2)}, u32[]{:S(2)}) collective-permute-start(f32[256,128]{1,0:T(8,128)S(1)} %get-tuple-element.63), channel_id=1, source_target_pairs={{0,2},{1,3},{2,0},{3,1},{4,6},{5,7},{6,4},{7,5},{8,10},{9,11},{10,... | collective-permute-start | bytes 393224 | tf_op jit(solution)/shard_map/ppermute | solution.py:291
  51.6 1.3 %collective-permute-start.13 = (f32[512,128]{1,0:T(8,128)S(1)}, f32[512,128]{1,0:T(8,128)S(1)}, u32[]{:S(2)}, u32[]{:S(2)}) collective-permute-start(f32[512,128]{1,0:T(8,128)S(1)} %get-tuple-element.60), channel_id=1, source_target_pairs={{0,1},{1,0},{2,3},{3,2},{4,5},{5,4},{6,7},{7,6},{8,9},{9,8},{10,11... | collective-permute-start | bytes 786440 | tf_op jit(solution)/shard_map/ppermute | solution.py:291
  52.9 2.1 %collective-permute-done.15.refs_2_ = f32[256,128]{1,0:T(8,128)S(1)} collective-permute-done((f32[256,128]{1,0:T(8,128)S(1)}, f32[256,128]{1,0:T(8,128)S(1)}, u32[]{:S(2)}, u32[]{:S(2)}) %collective-permute-start.15) | collective-permute-done | bytes 131104 | tf_op jit(solution)/shard_map/ppermute | solution.py:291
  57.2 1.3 %collective-permute-start.9 = (f32[256,128]{1,0:T(8,128)S(1)}, f32[256,128]{1,0:T(8,128)S(1)}, u32[]{:S(2)}, u32[]{:S(2)}) collective-permute-start(f32[256,128]{1,0:T(8,128)S(1)} %get-tuple-element.57), channel_id=1, source_target_pairs={{0,2},{1,3},{2,0},{3,1},{4,6},{5,7},{6,4},{7,5},{8,10},{9,11},{10,... | collective-permute-start | bytes 393224 | tf_op jit(solution)/shard_map/ppermute | solution.py:291
  58.5 2.4 %collective-permute-done.17.refs_4_ = f32[256,128]{1,0:T(8,128)S(1)} collective-permute-done((f32[256,128]{1,0:T(8,128)S(1)}, f32[256,128]{1,0:T(8,128)S(1)}, u32[]{:S(2)}, u32[]{:S(2)}) %collective-permute-start.17) | collective-permute-done | bytes 131104 | tf_op jit(solution)/shard_map/ppermute | solution.py:291
  60.9 1.3 %collective-permute-start.11 = (f32[256,128]{1,0:T(8,128)S(1)}, f32[256,128]{1,0:T(8,128)S(1)}, u32[]{:S(2)}, u32[]{:S(2)}) collective-permute-start(f32[256,128]{1,0:T(8,128)S(1)} %get-tuple-element.58), channel_id=1, source_target_pairs={{0,2},{1,3},{2,0},{3,1},{4,6},{5,7},{6,4},{7,5},{8,10},{9,11},{10,... | collective-permute-start | bytes 393224 | tf_op jit(solution)/shard_map/ppermute | solution.py:291
  63.4 2.2 %collective-permute-done.9.refs_1_ = f32[256,128]{1,0:T(8,128)S(1)} collective-permute-done((f32[256,128]{1,0:T(8,128)S(1)}, f32[256,128]{1,0:T(8,128)S(1)}, u32[]{:S(2)}, u32[]{:S(2)}) %collective-permute-start.9) | collective-permute-done | bytes 131104 | tf_op jit(solution)/shard_map/ppermute | solution.py:291
  65.6 2.8 %collective-permute-done.11.refs_3_ = f32[256,128]{1,0:T(8,128)S(1)} collective-permute-done((f32[256,128]{1,0:T(8,128)S(1)}, f32[256,128]{1,0:T(8,128)S(1)}, u32[]{:S(2)}, u32[]{:S(2)}) %collective-permute-start.11) | collective-permute-done | bytes 131104 | tf_op jit(solution)/shard_map/ppermute | solution.py:291
  68.4 3.0 %collective-permute-done.12.refs_4_ = f32[256,128]{1,0:T(8,128)S(1)} collective-permute-done((f32[256,128]{1,0:T(8,128)S(1)}, f32[256,128]{1,0:T(8,128)S(1)}, u32[]{:S(2)}, u32[]{:S(2)}) %collective-permute-start.12) | collective-permute-done | bytes 131104 | tf_op jit(solution)/shard_map/ppermute | solution.py:291
  (49 shorter events, 13.5 us)
Async XLA Ops:
  1.6 8.6 %copy-start.7 = (s32[4,1024]{1,0:T(4,128)S(1)}, s32[4,1024]{1,0:T(4,128)}, u32[]{:S(2)}) copy-start(s32[4,1024]{1,0:T(4,128)} %param.7) | copy-start | bytes 49156
  1.6 19.2 %copy-start.2 = (f32[352,1]{1,0:T(8,128)S(1)}, f32[352,1]{1,0:T(8,128)}, u32[]{:S(2)}) copy-start(f32[352,1]{1,0:T(8,128)} %constant.35.clone.refs_6_.refs_5_) | copy-start | bytes 4228
  1.6 19.2 %copy-start.3 = (f32[352,1]{1,0:T(8,128)S(1)}, f32[352,1]{1,0:T(8,128)}, u32[]{:S(2)}) copy-start(f32[352,1]{1,0:T(8,128)} %constant.34.clone.refs_5_.refs_4_) | copy-start | bytes 4228
  1.6 19.2 %copy-start.4 = (bf16[2,2,176,384]{3,2,1,0:T(8,128)(2,1)S(1)}, bf16[2,2,176,384]{3,2,1,0:T(8,128)(2,1)}, u32[]{:S(2)}) copy-start(bf16[2,2,176,384]{3,2,1,0:T(8,128)(2,1)} %constant.32.clone.refs_4_) | copy-start | bytes 1622020
  3.2 27.2 %copy-start = (bf16[2,2,128,528]{3,2,1,0:T(8,128)(2,1)S(1)}, bf16[2,2,128,528]{3,2,1,0:T(8,128)(2,1)}, u32[]{:S(2)}) copy-start(bf16[2,2,128,528]{3,2,1,0:T(8,128)(2,1)} %constant.33.clone.refs_7_) | copy-start | bytes 1622020
  5.7 15.0 %collective-permute-start = (f32[1040,128]{1,0:T(8,128)}, f32[1040,128]{1,0:T(8,128)S(1)}, u32[]{:S(2)}, u32[]{:S(2)}) collective-permute-start(f32[1040,128]{1,0:T(8,128)} %get-tuple-element.37), channel_id=1, source_target_pairs={{0,1},{1,0},{2,3},{3,2},{4,5},{5,4},{6,7},{7,6},{8,9},{9,8},{10,11... | collective-permute-start | bytes 1597448 | tf_op jit(solution)/shard_map/ppermute | solution.py:291
  6.4 13.6 %collective-permute-start.4 = (f32[520,128]{1,0:T(8,128)S(1)}, f32[520,128]{1,0:T(8,128)S(1)}, u32[]{:S(2)}, u32[]{:S(2)}) collective-permute-start(f32[520,128]{1,0:T(8,128)S(1)} %get-tuple-element.35.refs_0_), channel_id=1, source_target_pairs={{0,3},{1,2},{2,1},{3,0},{4,7},{5,6},{6,5},{7,4},{8,11},{9,10},{10,... | collective-permute-start | bytes 798728 | tf_op jit(solution)/shard_map/ppermute | solution.py:291
  7.7 12.4 %collective-permute-start.3 = (f32[520,128]{1,0:T(8,128)}, f32[520,128]{1,0:T(8,128)}, u32[]{:S(2)}, u32[]{:S(2)}) collective-permute-start(f32[520,128]{1,0:T(8,128)} %get-tuple-element.40), channel_id=1, source_target_pairs={{0,2},{1,3},{2,0},{3,1},{4,6},{5,7},{6,4},{7,5},{8,10},{9,11},{10,... | collective-permute-start | bytes 798728 | tf_op jit(solution)/shard_map/ppermute | solution.py:291
  7.9 24.5 %collective-permute-start.1 = (f32[520,128]{1,0:T(8,128)}, f32[520,128]{1,0:T(8,128)}, u32[]{:S(2)}, u32[]{:S(2)}) collective-permute-start(f32[520,128]{1,0:T(8,128)} %get-tuple-element.38), channel_id=1, source_target_pairs={{0,2},{1,3},{2,0},{3,1},{4,6},{5,7},{6,4},{7,5},{8,10},{9,11},{10,... | collective-permute-start | bytes 798728 | tf_op jit(solution)/shard_map/ppermute | solution.py:291
  9.1 23.3 %collective-permute-start.2 = (f32[520,128]{1,0:T(8,128)}, f32[520,128]{1,0:T(8,128)}, u32[]{:S(2)}, u32[]{:S(2)}) collective-permute-start(f32[520,128]{1,0:T(8,128)} %get-tuple-element.39), channel_id=1, source_target_pairs={{0,3},{1,2},{2,1},{3,0},{4,7},{5,6},{6,5},{7,4},{8,11},{9,10},{10,... | collective-permute-start | bytes 798728 | tf_op jit(solution)/shard_map/ppermute | solution.py:291
  24.4 17.4 %collective-permute-start.8 = (f32[352,128]{1,0:T(8,128)}, f32[352,128]{1,0:T(8,128)}, u32[]{:S(2)}, u32[]{:S(2)}) collective-permute-start(f32[352,128]{1,0:T(8,128)} %get-tuple-element.43.refs_2_), channel_id=1, source_target_pairs={{4,0},{8,4},{12,8},{16,12},{20,16},{24,20},{28,24},{5,1},{9,5},{13... | collective-permute-start | bytes 540680 | tf_op jit(solution)/shard_map/ppermute | solution.py:322
  27.4 14.4 %collective-permute-start.7 = (f32[352,128]{1,0:T(8,128)}, f32[352,128]{1,0:T(8,128)}, u32[]{:S(2)}, u32[]{:S(2)}) collective-permute-start(f32[352,128]{1,0:T(8,128)} %get-tuple-element.44.refs_3_), channel_id=1, source_target_pairs={{0,4},{4,8},{8,12},{12,16},{16,20},{20,24},{24,28},{1,5},{5,9},{9,... | collective-permute-start | bytes 540680 | tf_op jit(solution)/shard_map/ppermute | solution.py:321
  34.6 13.6 %collective-permute-start.5 = (f32[352,128]{1,0:T(8,128)S(1)}, f32[352,128]{1,0:T(8,128)S(1)}, u32[]{:S(2)}, u32[]{:S(2)}) collective-permute-start(f32[352,128]{1,0:T(8,128)S(1)} %get-tuple-element.48.refs_3_), channel_id=1, source_target_pairs={{0,4},{4,8},{8,12},{12,16},{16,20},{20,24},{24,28},{1,5},{5,9},{9,... | collective-permute-start | bytes 540680 | tf_op jit(solution)/shard_map/ppermute | solution.py:321
  37.0 12.5 %collective-permute-start.6 = (f32[352,128]{1,0:T(8,128)S(1)}, f32[352,128]{1,0:T(8,128)S(1)}, u32[]{:S(2)}, u32[]{:S(2)}) collective-permute-start(f32[352,128]{1,0:T(8,128)S(1)} %get-tuple-element.49.refs_2_), channel_id=1, source_target_pairs={{4,0},{8,4},{12,8},{16,12},{20,16},{24,20},{28,24},{5,1},{9,5},{13... | collective-permute-start | bytes 540680 | tf_op jit(solution)/shard_map/ppermute | solution.py:322
  43.8 18.4 %collective-permute-start.18 = (f32[512,128]{1,0:T(8,128)S(1)}, f32[512,128]{1,0:T(8,128)S(1)}, u32[]{:S(2)}, u32[]{:S(2)}) collective-permute-start(f32[512,128]{1,0:T(8,128)S(1)} %get-tuple-element.64), channel_id=1, source_target_pairs={{0,1},{1,0},{2,3},{3,2},{4,5},{5,4},{6,7},{7,6},{8,9},{9,8},{10,11... | collective-permute-start | bytes 786440 | tf_op jit(solution)/shard_map/ppermute | solution.py:291
  46.5 5.1 %collective-permute-start.14 = (f32[256,128]{1,0:T(8,128)S(1)}, f32[256,128]{1,0:T(8,128)S(1)}, u32[]{:S(2)}, u32[]{:S(2)}) collective-permute-start(f32[256,128]{1,0:T(8,128)S(1)} %get-tuple-element.62), channel_id=1, source_target_pairs={{0,2},{1,3},{2,0},{3,1},{4,6},{5,7},{6,4},{7,5},{8,10},{9,11},{10,... | collective-permute-start | bytes 393224 | tf_op jit(solution)/shard_map/ppermute | solution.py:291
  47.8 7.2 %collective-permute-start.15 = (f32[256,128]{1,0:T(8,128)S(1)}, f32[256,128]{1,0:T(8,128)S(1)}, u32[]{:S(2)}, u32[]{:S(2)}) collective-permute-start(f32[256,128]{1,0:T(8,128)S(1)} %get-tuple-element.45.refs_9_), channel_id=1, source_target_pairs={{0,3},{1,2},{2,1},{3,0},{4,7},{5,6},{6,5},{7,4},{8,11},{9,10},{10,... | collective-permute-start | bytes 393224 | tf_op jit(solution)/shard_map/ppermute | solution.py:291
  48.2 9.0 %collective-permute-start.16 = (f32[256,128]{1,0:T(8,128)S(1)}, f32[256,128]{1,0:T(8,128)S(1)}, u32[]{:S(2)}, u32[]{:S(2)}) collective-permute-start(f32[256,128]{1,0:T(8,128)S(1)} %get-tuple-element.63), channel_id=1, source_target_pairs={{0,2},{1,3},{2,0},{3,1},{4,6},{5,7},{6,4},{7,5},{8,10},{9,11},{10,... | collective-permute-start | bytes 393224 | tf_op jit(solution)/shard_map/ppermute | solution.py:291
  49.5 11.4 %collective-permute-start.17 = (f32[256,128]{1,0:T(8,128)S(1)}, f32[256,128]{1,0:T(8,128)S(1)}, u32[]{:S(2)}, u32[]{:S(2)}) collective-permute-start(f32[256,128]{1,0:T(8,128)S(1)} %get-tuple-element.55.refs_10_), channel_id=1, source_target_pairs={{0,3},{1,2},{2,1},{3,0},{4,7},{5,6},{6,5},{7,4},{8,11},{9,10},{10,... | collective-permute-start | bytes 393224 | tf_op jit(solution)/shard_map/ppermute | solution.py:291
  51.6 19.8 %collective-permute-start.13 = (f32[512,128]{1,0:T(8,128)S(1)}, f32[512,128]{1,0:T(8,128)S(1)}, u32[]{:S(2)}, u32[]{:S(2)}) collective-permute-start(f32[512,128]{1,0:T(8,128)S(1)} %get-tuple-element.60), channel_id=1, source_target_pairs={{0,1},{1,0},{2,3},{3,2},{4,5},{5,4},{6,7},{7,6},{8,9},{9,8},{10,11... | collective-permute-start | bytes 786440 | tf_op jit(solution)/shard_map/ppermute | solution.py:291
  55.0 10.6 %collective-permute-start.10 = (f32[256,128]{1,0:T(8,128)S(1)}, f32[256,128]{1,0:T(8,128)S(1)}, u32[]{:S(2)}, u32[]{:S(2)}) collective-permute-start(f32[256,128]{1,0:T(8,128)S(1)} %get-tuple-element.54.refs_10_), channel_id=1, source_target_pairs={{0,3},{1,2},{2,1},{3,0},{4,7},{5,6},{6,5},{7,4},{8,11},{9,10},{10,... | collective-permute-start | bytes 393224 | tf_op jit(solution)/shard_map/ppermute | solution.py:291
  57.2 8.4 %collective-permute-start.9 = (f32[256,128]{1,0:T(8,128)S(1)}, f32[256,128]{1,0:T(8,128)S(1)}, u32[]{:S(2)}, u32[]{:S(2)}) collective-permute-start(f32[256,128]{1,0:T(8,128)S(1)} %get-tuple-element.57), channel_id=1, source_target_pairs={{0,2},{1,3},{2,0},{3,1},{4,6},{5,7},{6,4},{7,5},{8,10},{9,11},{10,... | collective-permute-start | bytes 393224 | tf_op jit(solution)/shard_map/ppermute | solution.py:291
  60.9 7.5 %collective-permute-start.11 = (f32[256,128]{1,0:T(8,128)S(1)}, f32[256,128]{1,0:T(8,128)S(1)}, u32[]{:S(2)}, u32[]{:S(2)}) collective-permute-start(f32[256,128]{1,0:T(8,128)S(1)} %get-tuple-element.58), channel_id=1, source_target_pairs={{0,2},{1,3},{2,0},{3,1},{4,6},{5,7},{6,4},{7,5},{8,10},{9,11},{10,... | collective-permute-start | bytes 393224 | tf_op jit(solution)/shard_map/ppermute | solution.py:291
  62.2 9.2 %collective-permute-start.12 = (f32[256,128]{1,0:T(8,128)S(1)}, f32[256,128]{1,0:T(8,128)S(1)}, u32[]{:S(2)}, u32[]{:S(2)}) collective-permute-start(f32[256,128]{1,0:T(8,128)S(1)} %get-tuple-element.59), channel_id=1, source_target_pairs={{0,3},{1,2},{2,1},{3,0},{4,7},{5,6},{6,5},{7,4},{8,11},{9,10},{10,... | collective-permute-start | bytes 393224 | tf_op jit(solution)/shard_map/ppermute | solution.py:291
  (3 other events, 3.3 us)

commit v4 on v3

--- a/solution.py
+++ b/solution.py
@@ -167,11 +167,11 @@
     return jnp.where(kind == 0, fluid, jnp.where(kind == 1, solid, 0.0))
 
 
-def forward_kernel(rows, count, cells, column, *refs):
-    blocks, (forward_ref, fluid_ref, solid_ref, mask_ref, side_ref) = refs[:count], refs[count : count + 5]
+def forward_kernel(rows, count, cells, bases, *refs):
+    size = rows * cells + 8
+    blocks = [ref.at[base : base + size] for ref, base in zip(refs, bases)]
+    forward_ref, fluid_ref, solid_ref, mask_ref, side_ref = refs[count : count + 5]
     spectrum_ref, first_ref, last_ref, sides_ref = refs[-4:]
-    size = rows * cells + 8
-    blocks = [ref.at[column * size : (column + 1) * size] if ref.shape[0] > size else ref for ref in blocks]
     spectra, sides = transform(rows, count, cells, blocks, forward_ref)
     fluid, solid = fluid_ref[...], solid_ref[...]
     for row in range(rows):
@@ -198,18 +198,26 @@
     ]
 
 
-def inner_kernel(rows, count, cells, *refs):
+def far_views(outs, half, size):
+    if len(outs) == half:
+        return list(outs)
+    return [outs[0].at[e * size : (e + 1) * size] for e in range(half)]
+
+
+def inner_kernel(rows, count, cells, outputs, *refs):
+    half = count // 2
+    outs = refs[-outputs:]
     sweeps = sweep_rows(range(1, rows - 1), rows, refs[:7])
-    inverse_rows(sweeps, count, cells, refs[7], refs[-count:])
-
-
-def edge_kernel(rows, count, cells, *refs):
-    half = count // 2
-    inner, outs = refs[8 : 8 + half], refs[-count:]
+    inverse_rows(sweeps, count, cells, refs[7], [*outs[:half], *far_views(outs[half:], half, (rows - 2) * cells)])
+
+
+def edge_kernel(rows, count, cells, outputs, *refs):
+    half = count // 2
+    inner, outs = refs[8 : 8 + half], refs[-outputs:]
     sweeps = sweep_rows((0, rows - 1), rows, refs[:7])
     for d in range(half):
         outs[d][2 * cells :, :] = inner[d][...]
-    inverse_rows(sweeps, count, cells, refs[7], outs)
+    inverse_rows(sweeps, count, cells, refs[7], [*outs[:half], *far_views(outs[half:], half, 2 * cells)])
 
 
 def unpack_kernel(row_groups, row_count, count, cells, tiles, column, *refs):
@@ -217,12 +225,12 @@
     out_ref, held, done = refs[-3:]
     pitch = held.shape[0] // cells
     lines = count * tiles * row_count
-    for at, (d, rows) in enumerate(row_groups):
+    for at, (d, base, rows) in enumerate(row_groups):
         source = jnp.bitwise_xor(me, d)
         for i, row in enumerate(rows):
             for tile in range(tiles):
                 held[pl.ds((source * tiles + tile) * row_count + row, cells, stride=pitch), :] = refs[at][
-                    i * cells : (i + 1) * cells, tile * LANES : (tile + 1) * LANES
+                    base + i * cells : base + (i + 1) * cells, tile * LANES : (tile + 1) * LANES
                 ]
     copy = pltpu.make_async_copy(
         held.reshape(cells, pitch, LANES).at[:, pl.ds(0, lines)], out_ref.at[:, pl.ds(column * lines, lines)], done
@@ -291,62 +299,73 @@
         return lax.ppermute(block, "span", [(i, i ^ d) for i in range(count)])
 
     far = range(half, count)
-    first_packed = pack([(d - half, 0, d, 0) for d in far], [1] * half, ())
-    got = {(0, d): swap(block, d) for d, block in zip(far, first_packed)}
-    jobs = [(at, part, d, part) for at, d in enumerate(range(half)) for part in range(parts)]
-    sizes = [parts] * half
+
+    def relay(block, size):
+        arrived = swap(block, half)
+        return [(arrived, 0)] + [(swap(arrived[e * size : (e + 1) * size], e), 0) for e in range(1, half)]
+
+    (first_packed,) = pack([(0, d - half, d, 0) for d in far], [half], ())
+    got = [relay(first_packed, size)]
+    jobs = [(part * half + d, 0, d, part) for part in range(parts) for d in range(half)]
+    sizes = [1] * (parts * half)
     for part in range(1, parts):
-        for d in far:
-            jobs.append((len(sizes), 0, d, part))
-            sizes.append(1)
-    packed = pack(jobs, sizes, (first_packed[-1],))
-    near = [packed[0]] + [swap(packed[d], d) for d in range(1, half)]
-    at = half
-    for part in range(1, parts):
-        for d in far:
-            got[part, d] = swap(packed[at], d)
-            at += 1
+        jobs += [(len(sizes), d - half, d, part) for d in far]
+        sizes.append(half)
+    packed = pack(jobs, sizes, (first_packed,))
+    near = [
+        [(packed[part * half], 0)] + [(swap(packed[part * half + d], d), 0) for d in range(1, half)]
+        for part in range(parts)
+    ]
+    got += [relay(block, size) for block in packed[parts * half :]]
 
     up = [(i, i + 1) for i in range(plane_count - 1)]
     down = [(i + 1, i) for i in range(plane_count - 1)]
-    state, blocks, groups, earlier = [], [], [], ()
+    result, earlier = None, ()
     for part in range(parts):
+        last_part = part == parts - 1
         mask, kinds = masks(part)
+        blocks = near[part] + got[part]
         spectrum, first, last, sides = call(
-            functools.partial(forward_kernel, rows, count, cells, part),
+            functools.partial(forward_kernel, rows, count, cells, [base for _, base in blocks]),
             [(rows, modes, width), (modes, width), (modes, width), (modes, 16)],
-            [*near, *[got[part, d] for d in far], forward, fluid, solid, mask, kinds],
+            [*[block for block, _ in blocks], forward, fluid, solid, mask, kinds],
             earlier,
         )
         low = lax.ppermute(last, "plane", up)
         high = lax.ppermute(first, "plane", down)
-        state.append((spectrum, sides, low, high, fluid, solid, mask))
+
+        def outputs(near_rows, far_rows):
+            far_shapes = [(far_rows * cells, width)] * half if last_part else [(half * far_rows * cells, width)]
+            return [(near_rows * cells, width)] * half + far_shapes
+
+        def send(blocks, size):
+            if last_part:
+                return [(swap(block, d), 0) for d, block in zip(far, blocks)]
+            return relay(blocks[0], size)
+
+        shapes = outputs(len(inner), len(inner))
         inner_out = call(
-            functools.partial(inner_kernel, rows, count, cells),
-            [(len(inner) * cells, width)] * count,
+            functools.partial(inner_kernel, rows, count, cells, len(shapes)),
+            shapes,
             [spectrum, sides, first, last, fluid, solid, mask, inverse],
         )
-        blocks.append(inner_out)
-        earlier = (inner_out[-1],)
-    sent = [[swap(block[d], d) for d in far] for block in blocks]
-    result = None
-    for part in range(parts):
+        inner_got = send(inner_out[half:], len(inner) * cells)
+        shapes = outputs(rows, 2)
         edge_out = call(
-            functools.partial(edge_kernel, rows, count, cells),
-            [(rows * cells, width)] * half + [(2 * cells, width)] * half,
-            [*state[part], inverse, *blocks[part][:half]],
-            earlier,
+            functools.partial(edge_kernel, rows, count, cells, len(shapes)),
+            shapes,
+            [spectrum, sides, low, high, fluid, solid, mask, inverse, *inner_out[:half]],
+            (inner_out[-1],) if result is None else (result,),
         )
         earlier = (edge_out[-1],)
-        pieces = [(0, edges + inner, edge_out[0])]
-        pieces += [(d, inner, block) for d, block in zip(far, sent[part])]
-        pieces += [(d, edges, swap(edge_out[d], d)) for d in far]
-        pieces += [(d, edges + inner, swap(edge_out[d], d)) for d in range(1, half)]
+        edge_got = send(edge_out[half:], 2 * cells)
+        pieces = [(0, 0, edges + inner, edge_out[0])]
+        pieces += [(d, base, inner, block) for d, (block, base) in zip(far, inner_got)]
+        pieces += [(d, base, edges, block) for d, (block, base) in zip(far, edge_got)]
+        pieces += [(d, 0, edges + inner, swap(edge_out[d], d)) for d in range(1, half)]
         previous = () if result is None else (result,)
         result = pl.pallas_call(
-            functools.partial(
-                unpack_kernel, [piece[:2] for piece in pieces], rows, count, cells, tiles, part
-            ),
+            functools.partial(unpack_kernel, [piece[:3] for piece in pieces], rows, count, cells, tiles, part),
             out_shape=jax.ShapeDtypeStruct((cells, lines, LANES), jnp.float32),
             in_specs=[VMEM] * len(pieces) + [ANY] * len(previous),
             out_specs=ANY,
@@ -357,7 +376,7 @@
             input_output_aliases={len(pieces): 0} if previous else {},
             compiler_params=PARAMS,
             cost_estimate=COST,
-        )(*[piece[2] for piece in pieces], *previous)
+        )(*[piece[3] for piece in pieces], *previous)
     return result.reshape(cells, columns // LANES, rows, LANES).transpose(0, 2, 1, 3).reshape(cells, rows, columns)
 
 

time: 73 us -> 74.8 us (1.025)
  local copies, waits for them, and re-layouts: 3.65 us -> 7.42 us
  starting transfers between devices: 27.7 us -> 26.8 us
  Pallas kernels: 17.3 us -> 16.5 us
    ppermute x15 -> x16, waiting for transfers between devices: 23.8 us -> 18.5 us  [swap(): return lax.ppermute(block, 'span', [(i, i ^ d) for i in range(count)])]
    ppermute x2, waiting for transfers between devices: 0.01 us -> 4.92 us  [local(): high = lax.ppermute(first, 'plane', down)]
    unnamed x16 -> x22, local copies, waits for them, and re-layouts: 3.28 us -> 5.58 us
    slice x0 -> x4, local copies, waits for them, and re-layouts: none -> 1.47 us  [relay(): arrived[e * size:(e + 1) * size]]
    ppermute x15 -> x16, starting transfers between devices: 15.5 us -> 14.5 us  [swap(): return lax.ppermute(block, 'span', [(i, i ^ d) for i in range(count)])]
    pallas_call x6, Pallas kernels: 10.7 us -> 9.74 us  [call(): pl.pallas_call(kernel, out_shape=shapes, in_specs=[VMEM] * len(args) + [A...]
    pallas_call x2, Pallas kernels: 2.45 us -> 3.39 us  [local(): pl.pallas_call(functools.partial(unpack_kernel, [piece[:3] for piece in p...]
  transfers between devices with their start and end apart: 19 -> 20, of which waited for: 8 -> 9; matrix products, arithmetic and copies ran while one was open for 1% -> 3% of each run, Pallas kernels for 16% -> 18%
where the time goes in v4:
time: 74.8 us; the launch traced here: 74.5 us
  starting transfers between devices  26.8 us (36%)
  waiting for transfers between devices  23.4 us (31%)
  Pallas kernels  16.5 us (22%)
  local copies, waits for them, and re-layouts  7.42 us (10%)
    ppermute x16, waiting for transfers between devices, swap(): return lax.ppermute(block, 'span', [(i, i ^ d) for i in range(count)])  18.5 us
    ppermute x16, starting transfers between devices, swap(): return lax.ppermute(block, 'span', [(i, i ^ d) for i in range(count)])  14.5 us
    pallas_call x6, Pallas kernels, call(): pl.pallas_call(kernel, out_shape=shapes, in_specs=[VMEM] * len(args) + [A...  9.74 us
    ppermute x2, starting transfers between devices, local(): high = lax.ppermute(first, 'plane', down)  7.32 us
    unnamed x22, local copies, waits for them, and re-layouts  5.58 us
    ppermute x2, starting transfers between devices, local(): low = lax.ppermute(last, 'plane', up)  5.04 us
    ppermute x2, waiting for transfers between devices, local(): high = lax.ppermute(first, 'plane', down)  4.92 us
    pallas_call x2, Pallas kernels, local(): pl.pallas_call(functools.partial(unpack_kernel, [piece[:3] for piece in p...  3.39 us
  transfers between devices with their start and end apart: 20, of which 9 were waited for; matrix products, arithmetic and copies ran while one was open for 3% of the time, Pallas kernels for 18%

profile of v4, /device:TPU:25, one launch (start us, length us, event | category | flops | bytes accessed | tf_op | source)
XLA Modules:
  0.0 74.5 jit_solution(1944532030939603409)
XLA Ops:
  0.0 1.6 %copy-done.2 = f32[128,4,1024]{2,1,0:T(4,128)S(1)} copy-done((f32[128,4,1024]{2,1,0:T(4,128)S(1)}, f32[128,4,1024]{2,1,0:T(4,128)}, u32[]{:S(2)}) %copy-start.2) | copy-done | bytes 2097176
  2.5 1.3 %collective-permute-start.4 = (f32[1040,128]{1,0:T(8,128)S(1)}, f32[1040,128]{1,0:T(8,128)S(1)}, u32[]{:S(2)}, u32[]{:S(2)}) collective-permute-start(f32[1040,128]{1,0:T(8,128)S(1)} %shard_map.64.refs_0_), channel_id=1, source_target_pairs={{0,2},{1,3},{2,0},{3,1},{4,6},{5,7},{6,4},{7,5},{8,10},{9,11},{10,... | collective-permute-start | bytes 1597448 | tf_op jit(solution)/shard_map/ppermute | solution.py:299
  3.8 2.5 %shard_map.65 = (f32[520,128]{1,0:T(8,128)S(1)}, f32[520,128]{1,0:T(8,128)}, f32[520,128]{1,0:T(8,128)S(1)}, f32[520,128]{1,0:T(8,128)}, f32[1040,128]{1,0:T(8,128)}) custom-call(f32[128,32,128]{2,1,0:T(8,128)S(1)} %bitcast.11, f32[1040,128]{1,0:T(8,128)S(1)} %shard_map.64.refs_0_), custom_call_target="tpu_custom_call" | custom-call | flops 1024 | bytes 1024 | tf_op jit(solution)/shard_map/pallas_call | solution.py:285
  8.6 6.9 %collective-permute-done.4.refs_2_ = f32[1040,128]{1,0:T(8,128)S(1)} collective-permute-done((f32[1040,128]{1,0:T(8,128)S(1)}, f32[1040,128]{1,0:T(8,128)S(1)}, u32[]{:S(2)}, u32[]{:S(2)}) %collective-permute-start.4) | collective-permute-done | bytes 532512 | tf_op jit(solution)/shard_map/ppermute | solution.py:299
  16.3 2.7 %collective-permute-start.5 = (f32[520,128]{1,0:T(8,128)}, f32[520,128]{1,0:T(8,128)S(1)}, u32[]{:S(2)}, u32[]{:S(2)}) collective-permute-start(f32[520,128]{1,0:T(8,128)} %slice.17), channel_id=1, source_target_pairs={{0,1},{1,0},{2,3},{3,2},{4,5},{5,4},{6,7},{7,6},{8,9},{9,8},{10,11... | collective-permute-start | bytes 798728 | tf_op jit(solution)/shard_map/ppermute | solution.py:299
  21.3 2.1 %shard_map.66 = (f32[4,352,128]{2,1,0:T(8,128)S(1)}, f32[352,128]{1,0:T(8,128)S(1)}, f32[352,128]{1,0:T(8,128)S(1)}, f32[352,16]{1,0:T(8,128)S(1)}) custom-call(f32[520,128]{1,0:T(8,128)S(1)} %copy-done.7, f32[520,128]{1,0:T(8,128)} %collective-permute-done.3.refs_1_, f32[1040,128]{1,0:T(8,128)S(1)} %collective-permute-done.4.refs_2_, ...), custom_call_target="tpu_custom_call" | custom-call | flops 1024 | bytes 1024 | tf_op jit(solution)/shard_map/pallas_call | solution.py:244
  23.3 3.1 %collective-permute-start.6 = (f32[352,128]{1,0:T(8,128)S(1)}, f32[352,128]{1,0:T(8,128)S(1)}, u32[]{:S(2)}, u32[]{:S(2)}) collective-permute-start(f32[352,128]{1,0:T(8,128)S(1)} %get-tuple-element.39.refs_3_), channel_id=1, source_target_pairs={{0,4},{4,8},{8,12},{12,16},{16,20},{20,24},{24,28},{1,5},{5,9},{9,... | collective-permute-start | bytes 540680 | tf_op jit(solution)/shard_map/ppermute | solution.py:334
  26.5 3.1 %collective-permute-start.7 = (f32[352,128]{1,0:T(8,128)S(1)}, f32[352,128]{1,0:T(8,128)S(1)}, u32[]{:S(2)}, u32[]{:S(2)}) collective-permute-start(f32[352,128]{1,0:T(8,128)S(1)} %get-tuple-element.40.refs_2_), channel_id=1, source_target_pairs={{4,0},{8,4},{12,8},{16,12},{20,16},{24,20},{28,24},{5,1},{9,5},{13... | collective-permute-start | bytes 540680 | tf_op jit(solution)/shard_map/ppermute | solution.py:335
  31.3 1.7 %shard_map.67 = (f32[256,128]{1,0:T(8,128)S(1)}, f32[256,128]{1,0:T(8,128)S(1)}, f32[512,128]{1,0:T(8,128)}) custom-call(f32[4,352,128]{2,1,0:T(8,128)S(1)} %get-tuple-element.37.refs_0_, f32[352,16]{1,0:T(8,128)S(1)} %get-tuple-element.38.refs_1_, f32[352,128]{1,0:T(8,128)S(1)} %get-tuple-element.40.refs_2_, f32[352,128]{1,0:T(8,128)S(1)} %get-tuple-element.39.refs_3_, ...), custom_call_target="tpu_custom_call" | custom-call | flops 1024 | bytes 1024 | tf_op jit(solution)/shard_map/pallas_call | solution.py:244
  33.0 1.2 %collective-permute-start.10 = (f32[512,128]{1,0:T(8,128)}, f32[512,128]{1,0:T(8,128)S(1)}, u32[]{:S(2)}, u32[]{:S(2)}) collective-permute-start(f32[512,128]{1,0:T(8,128)} %get-tuple-element.43.refs_10_), channel_id=1, source_target_pairs={{0,2},{1,3},{2,0},{3,1},{4,6},{5,7},{6,4},{7,5},{8,10},{9,11},{10,... | collective-permute-start | bytes 786440 | tf_op jit(solution)/shard_map/ppermute | solution.py:299
  34.3 2.2 %collective-permute-done.7.refs_3_ = f32[352,128]{1,0:T(8,128)S(1)} collective-permute-done((f32[352,128]{1,0:T(8,128)S(1)}, f32[352,128]{1,0:T(8,128)S(1)}, u32[]{:S(2)}, u32[]{:S(2)}) %collective-permute-start.7) | collective-permute-done | bytes 180256 | tf_op jit(solution)/shard_map/ppermute | solution.py:335
  36.5 1.8 %shard_map.68 = (f32[512,128]{1,0:T(8,128)S(1)}, f32[512,128]{1,0:T(8,128)}, f32[512,128]{1,0:T(8,128)}) custom-call(f32[4,352,128]{2,1,0:T(8,128)S(1)} %get-tuple-element.37.refs_0_, f32[352,16]{1,0:T(8,128)S(1)} %get-tuple-element.38.refs_1_, f32[352,128]{1,0:T(8,128)S(1)} %collective-permute-done.6.refs_2_, ...), custom_call_target="tpu_custom_call" | custom-call | flops 1024 | bytes 1024 | tf_op jit(solution)/shard_map/pallas_call | solution.py:244
  41.2 2.1 %shard_map.69 = (f32[4,352,128]{2,1,0:T(8,128)S(1)}, f32[352,128]{1,0:T(8,128)S(1)}, f32[352,128]{1,0:T(8,128)S(1)}, f32[352,16]{1,0:T(8,128)S(1)}) custom-call(f32[520,128]{1,0:T(8,128)S(1)} %get-tuple-element.32.refs_0_, f32[520,128]{1,0:T(8,128)S(1)} %collective-permute-done.refs_1_, f32[1040,128]{1,0:T(8,128)S(1)} %collective-permute-done.1.refs_2_, ...), custom_call_target="tpu_custom_call" | custom-call | flops 1024 | bytes 1024 | tf_op jit(solution)/shard_map/pallas_call | solution.py:244
  43.3 1.9 %collective-permute-start.8 = (f32[352,128]{1,0:T(8,128)S(1)}, f32[352,128]{1,0:T(8,128)S(1)}, u32[]{:S(2)}, u32[]{:S(2)}) collective-permute-start(f32[352,128]{1,0:T(8,128)S(1)} %get-tuple-element.47.refs_3_), channel_id=1, source_target_pairs={{0,4},{4,8},{8,12},{12,16},{16,20},{20,24},{24,28},{1,5},{5,9},{9,... | collective-permute-start | bytes 540680 | tf_op jit(solution)/shard_map/ppermute | solution.py:334
  45.2 4.3 %collective-permute-start.9 = (f32[352,128]{1,0:T(8,128)S(1)}, f32[352,128]{1,0:T(8,128)S(1)}, u32[]{:S(2)}, u32[]{:S(2)}) collective-permute-start(f32[352,128]{1,0:T(8,128)S(1)} %get-tuple-element.48.refs_2_), channel_id=1, source_target_pairs={{4,0},{8,4},{12,8},{16,12},{20,16},{24,20},{28,24},{5,1},{9,5},{13... | collective-permute-start | bytes 540680 | tf_op jit(solution)/shard_map/ppermute | solution.py:335
  51.6 2.2 %shard_map.71.refs_10_.refs_6_ = f32[128,32,128]{2,1,0:T(8,128)} custom-call(f32[512,128]{1,0:T(8,128)S(1)} %copy-done.9, f32[512,128]{1,0:T(8,128)S(1)} %collective-permute-done.10.refs_1_, f32[256,128]{1,0:T(8,128)S(1)} %collective-permute-done.11.refs_2_, f32[512,128]{1,0:T(8,128)S(1)} %collective-permute-done.12.refs_3_, ...), custom_call_target="tpu_custom_call" | custom-call | flops 1024 | bytes 1024 | tf_op jit(solution)/shard_map/pallas_call | solution.py:367
  53.7 2.7 %collective-permute-done.9.refs_3_ = f32[352,128]{1,0:T(8,128)S(1)} collective-permute-done((f32[352,128]{1,0:T(8,128)S(1)}, f32[352,128]{1,0:T(8,128)S(1)}, u32[]{:S(2)}, u32[]{:S(2)}) %collective-permute-start.9) | collective-permute-done | bytes 180256 | tf_op jit(solution)/shard_map/ppermute | solution.py:335
  56.5 1.6 %copy-done = f32[128,32,128]{2,1,0:T(8,128)S(1)} copy-done((f32[128,32,128]{2,1,0:T(8,128)S(1)}, f32[128,32,128]{2,1,0:T(8,128)}, u32[]{:S(2)}) %copy-start) | copy-done | bytes 2097176
  59.8 1.5 %collective-permute-start.16 = (f32[256,128]{1,0:T(8,128)S(1)}, f32[256,128]{1,0:T(8,128)S(1)}, u32[]{:S(2)}, u32[]{:S(2)}) collective-permute-start(f32[256,128]{1,0:T(8,128)S(1)} %get-tuple-element.55), channel_id=1, source_target_pairs={{0,3},{1,2},{2,1},{3,0},{4,7},{5,6},{6,5},{7,4},{8,11},{9,10},{10,... | collective-permute-start | bytes 393224 | tf_op jit(solution)/shard_map/ppermute | solution.py:299
  61.5 1.6 %collective-permute-start.18 = (f32[256,128]{1,0:T(8,128)S(1)}, f32[256,128]{1,0:T(8,128)S(1)}, u32[]{:S(2)}, u32[]{:S(2)}) collective-permute-start(f32[256,128]{1,0:T(8,128)S(1)} %get-tuple-element.57), channel_id=1, source_target_pairs={{0,3},{1,2},{2,1},{3,0},{4,7},{5,6},{6,5},{7,4},{8,11},{9,10},{10,... | collective-permute-start | bytes 393224 | tf_op jit(solution)/shard_map/ppermute | solution.py:299
  63.1 1.6 %collective-permute-done.15.refs_1_ = f32[256,128]{1,0:T(8,128)S(1)} collective-permute-done((f32[256,128]{1,0:T(8,128)S(1)}, f32[256,128]{1,0:T(8,128)S(1)}, u32[]{:S(2)}, u32[]{:S(2)}) %collective-permute-start.15) | collective-permute-done | bytes 131104 | tf_op jit(solution)/shard_map/ppermute | solution.py:299
  64.7 3.4 %collective-permute-done.16.refs_2_ = f32[256,128]{1,0:T(8,128)S(1)} collective-permute-done((f32[256,128]{1,0:T(8,128)S(1)}, f32[256,128]{1,0:T(8,128)S(1)}, u32[]{:S(2)}, u32[]{:S(2)}) %collective-permute-start.16) | collective-permute-done | bytes 131104 | tf_op jit(solution)/shard_map/ppermute | solution.py:299
  68.1 2.2 %collective-permute-done.17.refs_3_ = f32[256,128]{1,0:T(8,128)S(1)} collective-permute-done((f32[256,128]{1,0:T(8,128)S(1)}, f32[256,128]{1,0:T(8,128)S(1)}, u32[]{:S(2)}, u32[]{:S(2)}) %collective-permute-start.17) | collective-permute-done | bytes 131104 | tf_op jit(solution)/shard_map/ppermute | solution.py:299
  70.3 3.0 %collective-permute-done.18.refs_4_ = f32[256,128]{1,0:T(8,128)S(1)} collective-permute-done((f32[256,128]{1,0:T(8,128)S(1)}, f32[256,128]{1,0:T(8,128)S(1)}, u32[]{:S(2)}, u32[]{:S(2)}) %collective-permute-start.18) | collective-permute-done | bytes 131104 | tf_op jit(solution)/shard_map/ppermute | solution.py:299
  (61 shorter events, 16.0 us)
Async XLA Ops:
  2.5 17.9 %copy-start.3 = (f32[352,1]{1,0:T(8,128)S(1)}, f32[352,1]{1,0:T(8,128)}, u32[]{:S(2)}) copy-start(f32[352,1]{1,0:T(8,128)} %constant.35.clone.refs_6_.refs_5_) | copy-start | bytes 4228
  2.5 17.9 %copy-start.4 = (f32[352,1]{1,0:T(8,128)S(1)}, f32[352,1]{1,0:T(8,128)}, u32[]{:S(2)}) copy-start(f32[352,1]{1,0:T(8,128)} %constant.34.clone.refs_5_.refs_4_) | copy-start | bytes 4228
  2.5 17.9 %copy-start.5 = (bf16[2,2,176,384]{3,2,1,0:T(8,128)(2,1)S(1)}, bf16[2,2,176,384]{3,2,1,0:T(8,128)(2,1)}, u32[]{:S(2)}) copy-start(bf16[2,2,176,384]{3,2,1,0:T(8,128)(2,1)} %constant.32.clone.refs_4_) | copy-start | bytes 1622020
  2.5 13.0 %collective-permute-start.4 = (f32[1040,128]{1,0:T(8,128)S(1)}, f32[1040,128]{1,0:T(8,128)S(1)}, u32[]{:S(2)}, u32[]{:S(2)}) collective-permute-start(f32[1040,128]{1,0:T(8,128)S(1)} %shard_map.64.refs_0_), channel_id=1, source_target_pairs={{0,2},{1,3},{2,0},{3,1},{4,6},{5,7},{6,4},{7,5},{8,10},{9,11},{10,... | collective-permute-start | bytes 1597448 | tf_op jit(solution)/shard_map/ppermute | solution.py:299
  7.0 24.3 %copy-start.1 = (bf16[2,2,128,528]{3,2,1,0:T(8,128)(2,1)S(1)}, bf16[2,2,128,528]{3,2,1,0:T(8,128)(2,1)}, u32[]{:S(2)}) copy-start(bf16[2,2,128,528]{3,2,1,0:T(8,128)(2,1)} %constant.33.clone.refs_7_) | copy-start | bytes 1622020
  7.0 23.5 %collective-permute-start.1 = (f32[1040,128]{1,0:T(8,128)}, f32[1040,128]{1,0:T(8,128)S(1)}, u32[]{:S(2)}, u32[]{:S(2)}) collective-permute-start(f32[1040,128]{1,0:T(8,128)} %get-tuple-element.34), channel_id=1, source_target_pairs={{0,2},{1,3},{2,0},{3,1},{4,6},{5,7},{6,4},{7,5},{8,10},{9,11},{10,... | collective-permute-start | bytes 1597448 | tf_op jit(solution)/shard_map/ppermute | solution.py:299
  7.3 11.9 %collective-permute-start.3 = (f32[520,128]{1,0:T(8,128)}, f32[520,128]{1,0:T(8,128)}, u32[]{:S(2)}, u32[]{:S(2)}) collective-permute-start(f32[520,128]{1,0:T(8,128)} %get-tuple-element.36), channel_id=1, source_target_pairs={{0,1},{1,0},{2,3},{3,2},{4,5},{5,4},{6,7},{7,6},{8,9},{9,8},{10,11... | collective-permute-start | bytes 798728 | tf_op jit(solution)/shard_map/ppermute | solution.py:299
  16.3 4.1 %collective-permute-start.5 = (f32[520,128]{1,0:T(8,128)}, f32[520,128]{1,0:T(8,128)S(1)}, u32[]{:S(2)}, u32[]{:S(2)}) collective-permute-start(f32[520,128]{1,0:T(8,128)} %slice.17), channel_id=1, source_target_pairs={{0,1},{1,0},{2,3},{3,2},{4,5},{5,4},{6,7},{7,6},{8,9},{9,8},{10,11... | collective-permute-start | bytes 798728 | tf_op jit(solution)/shard_map/ppermute | solution.py:299
  23.3 10.9 %collective-permute-start.6 = (f32[352,128]{1,0:T(8,128)S(1)}, f32[352,128]{1,0:T(8,128)S(1)}, u32[]{:S(2)}, u32[]{:S(2)}) collective-permute-start(f32[352,128]{1,0:T(8,128)S(1)} %get-tuple-element.39.refs_3_), channel_id=1, source_target_pairs={{0,4},{4,8},{8,12},{12,16},{16,20},{20,24},{24,28},{1,5},{5,9},{9,... | collective-permute-start | bytes 540680 | tf_op jit(solution)/shard_map/ppermute | solution.py:334
  26.5 10.0 %collective-permute-start.7 = (f32[352,128]{1,0:T(8,128)S(1)}, f32[352,128]{1,0:T(8,128)S(1)}, u32[]{:S(2)}, u32[]{:S(2)}) collective-permute-start(f32[352,128]{1,0:T(8,128)S(1)} %get-tuple-element.40.refs_2_), channel_id=1, source_target_pairs={{4,0},{8,4},{12,8},{16,12},{20,16},{24,20},{28,24},{5,1},{9,5},{13... | collective-permute-start | bytes 540680 | tf_op jit(solution)/shard_map/ppermute | solution.py:335
  29.5 11.6 %collective-permute-start = (f32[520,128]{1,0:T(8,128)}, f32[520,128]{1,0:T(8,128)S(1)}, u32[]{:S(2)}, u32[]{:S(2)}) collective-permute-start(f32[520,128]{1,0:T(8,128)} %get-tuple-element.33), channel_id=1, source_target_pairs={{0,1},{1,0},{2,3},{3,2},{4,5},{5,4},{6,7},{7,6},{8,9},{9,8},{10,11... | collective-permute-start | bytes 798728 | tf_op jit(solution)/shard_map/ppermute | solution.py:299
  31.3 9.9 %collective-permute-start.2 = (f32[520,128]{1,0:T(8,128)}, f32[520,128]{1,0:T(8,128)}, u32[]{:S(2)}, u32[]{:S(2)}) collective-permute-start(f32[520,128]{1,0:T(8,128)} %slice.16), channel_id=1, source_target_pairs={{0,1},{1,0},{2,3},{3,2},{4,5},{5,4},{6,7},{7,6},{8,9},{9,8},{10,11... | collective-permute-start | bytes 798728 | tf_op jit(solution)/shard_map/ppermute | solution.py:299
  33.0 16.5 %collective-permute-start.10 = (f32[512,128]{1,0:T(8,128)}, f32[512,128]{1,0:T(8,128)S(1)}, u32[]{:S(2)}, u32[]{:S(2)}) collective-permute-start(f32[512,128]{1,0:T(8,128)} %get-tuple-element.43.refs_10_), channel_id=1, source_target_pairs={{0,2},{1,3},{2,0},{3,1},{4,6},{5,7},{6,4},{7,5},{8,10},{9,11},{10,... | collective-permute-start | bytes 786440 | tf_op jit(solution)/shard_map/ppermute | solution.py:299
  39.0 11.1 %collective-permute-start.12 = (f32[512,128]{1,0:T(8,128)}, f32[512,128]{1,0:T(8,128)S(1)}, u32[]{:S(2)}, u32[]{:S(2)}) collective-permute-start(f32[512,128]{1,0:T(8,128)} %get-tuple-element.44.refs_9_), channel_id=1, source_target_pairs={{0,2},{1,3},{2,0},{3,1},{4,6},{5,7},{6,4},{7,5},{8,10},{9,11},{10,... | collective-permute-start | bytes 786440 | tf_op jit(solution)/shard_map/ppermute | solution.py:299
  40.3 11.0 %collective-permute-start.14 = (f32[512,128]{1,0:T(8,128)}, f32[512,128]{1,0:T(8,128)}, u32[]{:S(2)}, u32[]{:S(2)}) collective-permute-start(f32[512,128]{1,0:T(8,128)} %get-tuple-element.52), channel_id=1, source_target_pairs={{0,1},{1,0},{2,3},{3,2},{4,5},{5,4},{6,7},{7,6},{8,9},{9,8},{10,11... | collective-permute-start | bytes 786440 | tf_op jit(solution)/shard_map/ppermute | solution.py:299
  43.3 10.5 %collective-permute-start.8 = (f32[352,128]{1,0:T(8,128)S(1)}, f32[352,128]{1,0:T(8,128)S(1)}, u32[]{:S(2)}, u32[]{:S(2)}) collective-permute-start(f32[352,128]{1,0:T(8,128)S(1)} %get-tuple-element.47.refs_3_), channel_id=1, source_target_pairs={{0,4},{4,8},{8,12},{12,16},{16,20},{20,24},{24,28},{1,5},{5,9},{9,... | collective-permute-start | bytes 540680 | tf_op jit(solution)/shard_map/ppermute | solution.py:334
  45.2 11.3 %collective-permute-start.9 = (f32[352,128]{1,0:T(8,128)S(1)}, f32[352,128]{1,0:T(8,128)S(1)}, u32[]{:S(2)}, u32[]{:S(2)}) collective-permute-start(f32[352,128]{1,0:T(8,128)S(1)} %get-tuple-element.48.refs_2_), channel_id=1, source_target_pairs={{4,0},{8,4},{12,8},{16,12},{20,16},{24,20},{28,24},{5,1},{9,5},{13... | collective-permute-start | bytes 540680 | tf_op jit(solution)/shard_map/ppermute | solution.py:335
  49.5 1.7 %collective-permute-start.11 = (f32[256,128]{1,0:T(8,128)S(1)}, f32[256,128]{1,0:T(8,128)S(1)}, u32[]{:S(2)}, u32[]{:S(2)}) collective-permute-start(f32[256,128]{1,0:T(8,128)S(1)} %slice.18), channel_id=1, source_target_pairs={{0,1},{1,0},{2,3},{3,2},{4,5},{5,4},{6,7},{7,6},{8,9},{9,8},{10,11... | collective-permute-start | bytes 393224 | tf_op jit(solution)/shard_map/ppermute | solution.py:299
  50.1 1.4 %collective-permute-start.13 = (f32[256,128]{1,0:T(8,128)S(1)}, f32[256,128]{1,0:T(8,128)S(1)}, u32[]{:S(2)}, u32[]{:S(2)}) collective-permute-start(f32[256,128]{1,0:T(8,128)S(1)} %slice.19), channel_id=1, source_target_pairs={{0,1},{1,0},{2,3},{3,2},{4,5},{5,4},{6,7},{7,6},{8,9},{9,8},{10,11... | collective-permute-start | bytes 393224 | tf_op jit(solution)/shard_map/ppermute | solution.py:299
  59.1 14.2 %collective-permute-start.19 = (f32[512,128]{1,0:T(8,128)S(1)}, f32[512,128]{1,0:T(8,128)S(1)}, u32[]{:S(2)}, u32[]{:S(2)}) collective-permute-start(f32[512,128]{1,0:T(8,128)S(1)} %get-tuple-element.58), channel_id=1, source_target_pairs={{0,1},{1,0},{2,3},{3,2},{4,5},{5,4},{6,7},{7,6},{8,9},{9,8},{10,11... | collective-permute-start | bytes 786440 | tf_op jit(solution)/shard_map/ppermute | solution.py:299
  59.6 5.1 %collective-permute-start.15 = (f32[256,128]{1,0:T(8,128)S(1)}, f32[256,128]{1,0:T(8,128)S(1)}, u32[]{:S(2)}, u32[]{:S(2)}) collective-permute-start(f32[256,128]{1,0:T(8,128)S(1)} %get-tuple-element.54), channel_id=1, source_target_pairs={{0,2},{1,3},{2,0},{3,1},{4,6},{5,7},{6,4},{7,5},{8,10},{9,11},{10,... | collective-permute-start | bytes 393224 | tf_op jit(solution)/shard_map/ppermute | solution.py:299
  59.8 8.3 %collective-permute-start.16 = (f32[256,128]{1,0:T(8,128)S(1)}, f32[256,128]{1,0:T(8,128)S(1)}, u32[]{:S(2)}, u32[]{:S(2)}) collective-permute-start(f32[256,128]{1,0:T(8,128)S(1)} %get-tuple-element.55), channel_id=1, source_target_pairs={{0,3},{1,2},{2,1},{3,0},{4,7},{5,6},{6,5},{7,4},{8,11},{9,10},{10,... | collective-permute-start | bytes 393224 | tf_op jit(solution)/shard_map/ppermute | solution.py:299
  61.3 9.0 %collective-permute-start.17 = (f32[256,128]{1,0:T(8,128)S(1)}, f32[256,128]{1,0:T(8,128)S(1)}, u32[]{:S(2)}, u32[]{:S(2)}) collective-permute-start(f32[256,128]{1,0:T(8,128)S(1)} %get-tuple-element.56), channel_id=1, source_target_pairs={{0,2},{1,3},{2,0},{3,1},{4,6},{5,7},{6,4},{7,5},{8,10},{9,11},{10,... | collective-permute-start | bytes 393224 | tf_op jit(solution)/shard_map/ppermute | solution.py:299
  61.5 11.7 %collective-permute-start.18 = (f32[256,128]{1,0:T(8,128)S(1)}, f32[256,128]{1,0:T(8,128)S(1)}, u32[]{:S(2)}, u32[]{:S(2)}) collective-permute-start(f32[256,128]{1,0:T(8,128)S(1)} %get-tuple-element.57), channel_id=1, source_target_pairs={{0,3},{1,2},{2,1},{3,0},{4,7},{5,6},{6,5},{7,4},{8,11},{9,10},{10,... | collective-permute-start | bytes 393224 | tf_op jit(solution)/shard_map/ppermute | solution.py:299
  (7 other events, 22.9 us)

commit v5 on v3

--- a/solution.py
+++ b/solution.py
@@ -62,6 +62,7 @@
 
 def pack_kernel(jobs, earlier, row_count, count, cells, width, tiles, split_at, x_ref, *refs):
     outs, (held, arrived) = refs[earlier:-2], refs[-2:]
+    outs[-1][...] = jnp.zeros((8, LANES), jnp.float32)
     me = lax.axis_index("span")
     lines = x_ref.shape[1]
     pitch = held.shape[0] // cells
@@ -89,7 +90,7 @@
             first = (column * count + jnp.bitwise_xor(me, d)) * tiles
             base = place * (row_count * cells + 8) + part * some
             for row in range(row_count):
-                for tile in range(tiles):
+                for tile in range(tiles if d else 0):
                     outs[out][base + row * cells : base + row * cells + some, tile * LANES : (tile + 1) * LANES] = line(
                         first + tile, row
                     )
@@ -102,8 +103,8 @@
     if cells < LANES:
         sides.append(jnp.zeros((LANES - cells, LANES), jnp.float32))
     turned = jnp.concatenate(sides, axis=0).T
-    for job, (out, place, _, _) in enumerate(jobs):
-        base = place * (row_count * cells + 8) + row_count * cells
+    for job, (out, place, d, _) in enumerate(jobs):
+        base = place * (row_count * cells + 8) + (row_count * cells if d else 0)
         outs[out][base : base + 8, :LANES] = turned[job * 8 : (job + 1) * 8]
         if width > LANES:
             outs[out][base : base + 8, LANES:] = jnp.zeros((8, width - LANES), jnp.float32)
@@ -168,17 +169,28 @@
 
 
 def forward_kernel(rows, count, cells, column, *refs):
-    blocks, (forward_ref, fluid_ref, solid_ref, mask_ref, side_ref) = refs[:count], refs[count : count + 5]
-    spectrum_ref, first_ref, last_ref, sides_ref = refs[-4:]
-    size = rows * cells + 8
-    blocks = [ref.at[column * size : (column + 1) * size] if ref.shape[0] > size else ref for ref in blocks]
-    spectra, sides = transform(rows, count, cells, blocks, forward_ref)
+    source_ref, beside_ref, blocks = refs[0], refs[1], list(refs[2 : count + 1])
+    forward_ref, fluid_ref, solid_ref, mask_ref, side_ref = refs[count + 1 : count + 6]
+    spectrum_ref, first_ref, last_ref, sides_ref, token_ref = refs[-5:]
+    width = mask_ref.shape[1]
+    tiles = width // LANES
+    first = (column * count + lax.axis_index("span")) * tiles
+    stride = source_ref.shape[0] // cells
+    own = [
+        jnp.concatenate(
+            [source_ref[pl.ds((first + tile) * rows + row, cells, stride=stride), :] for tile in range(tiles)], axis=1
+        )
+        for row in range(rows)
+    ]
+    own = jnp.concatenate([*own, beside_ref[...]], axis=0)
+    spectra, sides = transform(rows, count, cells, [own, *blocks], forward_ref)
     fluid, solid = fluid_ref[...], solid_ref[...]
     for row in range(rows):
         spectrum_ref[row] = spectra[row]
     first_ref[...] = spectra[0] * jnp.where(mask_ref[0:1, :] != 0, solid, fluid)
     last_ref[...] = spectra[-1] * jnp.where(mask_ref[rows - 1 : rows, :] != 0, solid, fluid)
     sides_ref[...] = sides * side_factor(side_ref, fluid, solid)
+    token_ref[...] = jnp.zeros((8, LANES), jnp.float32)
 
 
 def sweep_rows(wanted, rows, refs):
@@ -198,18 +210,19 @@
     ]
 
 
-def inner_kernel(rows, count, cells, *refs):
-    sweeps = sweep_rows(range(1, rows - 1), rows, refs[:7])
-    inverse_rows(sweeps, count, cells, refs[7], refs[-count:])
-
-
-def edge_kernel(rows, count, cells, *refs):
+def output_kernel(wanted, rows, count, cells, taken, outputs, *refs):
     half = count // 2
-    inner, outs = refs[8 : 8 + half], refs[-count:]
-    sweeps = sweep_rows((0, rows - 1), rows, refs[:7])
-    for d in range(half):
-        outs[d][2 * cells :, :] = inner[d][...]
-    inverse_rows(sweeps, count, cells, refs[7], outs)
+    outs, token_ref = refs[-outputs - 1 : -1], refs[-1]
+    sweeps = sweep_rows(wanted, rows, refs[:7])
+    size = len(wanted) * cells
+    if taken:
+        for d in range(half):
+            outs[d][size:, :] = refs[8 + d][...]
+    far = outs[half:]
+    if outputs < count:
+        far = [far[0].at[e * size : (e + 1) * size] for e in range(half)]
+    inverse_rows(sweeps, count, cells, refs[7], [*outs[:half], *far])
+    token_ref[...] = jnp.zeros((8, LANES), jnp.float32)
 
 
 def unpack_kernel(row_groups, row_count, count, cells, tiles, column, *refs):
@@ -232,12 +245,12 @@
 
 
 def call(kernel, outs, args, earlier=()):
-    shapes = [jax.ShapeDtypeStruct(shape, jnp.float32) for shape in outs]
+    shapes = [jax.ShapeDtypeStruct(shape, jnp.float32) for shape in (*outs, (8, LANES))]
     return pl.pallas_call(
         kernel,
         out_shape=shapes,
         in_specs=[VMEM] * len(args) + [ANY] * len(earlier),
-        out_specs=[VMEM] * len(outs),
+        out_specs=[VMEM] * len(shapes),
         compiler_params=PARAMS,
         cost_estimate=COST,
     )(*args, *earlier)
@@ -274,11 +287,12 @@
     size = rows * cells + 8
 
     def pack(jobs, sizes, earlier):
+        shapes = [*[(length, width) for length in sizes], (8, LANES)]
         return pl.pallas_call(
             functools.partial(pack_kernel, jobs, len(earlier), rows, count, cells, width, tiles, 4),
-            out_shape=[jax.ShapeDtypeStruct((places * size, width), jnp.float32) for places in sizes],
+            out_shape=[jax.ShapeDtypeStruct(shape, jnp.float32) for shape in shapes],
             in_specs=[ANY] * (1 + len(earlier)),
-            out_specs=[VMEM] * len(sizes),
+            out_specs=[VMEM] * len(shapes),
             scratch_shapes=[
                 pltpu.VMEM((cells * (lines + 8), LANES), jnp.float32),
                 pltpu.SemaphoreType.DMA((4,)),
@@ -290,74 +304,89 @@
     def swap(block, d):
         return lax.ppermute(block, "span", [(i, i ^ d) for i in range(count)])
 
-    far = range(half, count)
-    first_packed = pack([(d - half, 0, d, 0) for d in far], [1] * half, ())
-    got = {(0, d): swap(block, d) for d, block in zip(far, first_packed)}
-    jobs = [(at, part, d, part) for at, d in enumerate(range(half)) for part in range(parts)]
-    sizes = [parts] * half
-    for part in range(1, parts):
-        for d in far:
-            jobs.append((len(sizes), 0, d, part))
-            sizes.append(1)
-    packed = pack(jobs, sizes, (first_packed[-1],))
-    near = [packed[0]] + [swap(packed[d], d) for d in range(1, half)]
-    at = half
-    for part in range(1, parts):
-        for d in far:
-            got[part, d] = swap(packed[at], d)
-            at += 1
+    near, far = range(1, half), range(half, count)
+
+    def relay(block, size):
+        arrived = swap(block, half)
+        return [arrived] + [swap(arrived[e * size : (e + 1) * size], e) for e in near]
+
+    got, earlier = [], ()
+    for part in range(parts):
+        *packed, token = pack([(d, 0, d, part) for d in range(count)], [8] + [size] * (count - 1), earlier)
+        earlier = (token,)
+        got.append([packed[0]] + [swap(packed[d], d) for d in range(1, count)])
 
     up = [(i, i + 1) for i in range(plane_count - 1)]
     down = [(i + 1, i) for i in range(plane_count - 1)]
-    state, blocks, groups, earlier = [], [], [], ()
+    flat = source.reshape(cells * lines, LANES)
+    everywhere = tuple(range(rows))
+    states, inners, earlier = [], [], ()
     for part in range(parts):
         mask, kinds = masks(part)
-        spectrum, first, last, sides = call(
+        spectrum, first, last, sides, token = call(
             functools.partial(forward_kernel, rows, count, cells, part),
             [(rows, modes, width), (modes, width), (modes, width), (modes, 16)],
-            [*near, *[got[part, d] for d in far], forward, fluid, solid, mask, kinds],
+            [flat, *got[part], forward, fluid, solid, mask, kinds],
             earlier,
         )
+        earlier = (token,)
         low = lax.ppermute(last, "plane", up)
         high = lax.ppermute(first, "plane", down)
-        state.append((spectrum, sides, low, high, fluid, solid, mask))
-        inner_out = call(
-            functools.partial(inner_kernel, rows, count, cells),
-            [(len(inner) * cells, width)] * count,
-            [spectrum, sides, first, last, fluid, solid, mask, inverse],
-        )
-        blocks.append(inner_out)
-        earlier = (inner_out[-1],)
-    sent = [[swap(block[d], d) for d in far] for block in blocks]
+        states.append([spectrum, sides, low, high, fluid, solid, mask, inverse])
+        if part < parts - 1:
+            length = len(inner) * cells
+            *inner_out, token = call(
+                functools.partial(output_kernel, inner, rows, count, cells, False, half + 1),
+                [(length, width)] * half + [(half * length, width)],
+                [spectrum, sides, first, last, fluid, solid, mask, inverse],
+                earlier,
+            )
+            earlier = (token,)
+            inners.append((inner_out[:half], relay(inner_out[half], length)))
+
+    pieces = []
+    for part in range(parts - 1):
+        length = len(edges) * cells
+        *edge_out, token = call(
+            functools.partial(output_kernel, edges, rows, count, cells, True, half + 1),
+            [(rows * cells, width)] * half + [(half * length, width)],
+            [*states[part], *inners[part][0]],
+            earlier,
+        )
+        earlier = (token, inners[part][1][-1])
+        edge_got = relay(edge_out[half], length)
+        pieces.append(
+            [(0, edges + inner, edge_out[0])]
+            + [(d, inner, block) for d, block in zip(far, inners[part][1])]
+            + [(d, edges, block) for d, block in zip(far, edge_got)]
+            + [(d, edges + inner, swap(edge_out[d], d)) for d in near]
+        )
+    *last_out, token = call(
+        functools.partial(output_kernel, everywhere, rows, count, cells, False, count),
+        [(rows * cells, width)] * count,
+        states[-1],
+        earlier,
+    )
+    pieces.append(
+        [(0, everywhere, last_out[0])] + [(d, everywhere, swap(last_out[d], d)) for d in (*far, *near)]
+    )
+
     result = None
     for part in range(parts):
-        edge_out = call(
-            functools.partial(edge_kernel, rows, count, cells),
-            [(rows * cells, width)] * half + [(2 * cells, width)] * half,
-            [*state[part], inverse, *blocks[part][:half]],
-            earlier,
-        )
-        earlier = (edge_out[-1],)
-        pieces = [(0, edges + inner, edge_out[0])]
-        pieces += [(d, inner, block) for d, block in zip(far, sent[part])]
-        pieces += [(d, edges, swap(edge_out[d], d)) for d in far]
-        pieces += [(d, edges + inner, swap(edge_out[d], d)) for d in range(1, half)]
         previous = () if result is None else (result,)
         result = pl.pallas_call(
-            functools.partial(
-                unpack_kernel, [piece[:2] for piece in pieces], rows, count, cells, tiles, part
-            ),
+            functools.partial(unpack_kernel, [piece[:2] for piece in pieces[part]], rows, count, cells, tiles, part),
             out_shape=jax.ShapeDtypeStruct((cells, lines, LANES), jnp.float32),
-            in_specs=[VMEM] * len(pieces) + [ANY] * len(previous),
+            in_specs=[VMEM] * len(pieces[part]) + [ANY] * len(previous),
             out_specs=ANY,
             scratch_shapes=[
                 pltpu.VMEM((cells * (count * tiles * rows + 8), LANES), jnp.float32),
                 pltpu.SemaphoreType.DMA,
             ],
-            input_output_aliases={len(pieces): 0} if previous else {},
+            input_output_aliases={len(pieces[part]): 0} if previous else {},
             compiler_params=PARAMS,
             cost_estimate=COST,
-        )(*[piece[2] for piece in pieces], *previous)
+        )(*[piece[2] for piece in pieces[part]], *previous)
     return result.reshape(cells, columns // LANES, rows, LANES).transpose(0, 2, 1, 3).reshape(cells, rows, columns)
 
 

time: 73 us -> 75.2 us (1.030)
  local copies, waits for them, and re-layouts: 3.65 us -> 14.8 us
  waiting for transfers between devices: 23.8 us -> 17.8 us
  starting transfers between devices: 27.7 us -> 22.8 us
  Pallas kernels: 17.3 us -> 18.4 us
    ppermute x15 -> x14, waiting for transfers between devices: 23.8 us -> 14.8 us  [swap(): return lax.ppermute(block, 'span', [(i, i ^ d) for i in range(count)])]
    unnamed x16 -> x48, local copies, waits for them, and re-layouts: 3.28 us -> 12 us
    ppermute x15 -> x14, starting transfers between devices: 15.5 us -> 10.7 us  [swap(): return lax.ppermute(block, 'span', [(i, i ^ d) for i in range(count)])]
    ppermute x2, waiting for transfers between devices: 0.01 us -> 3.01 us  [local(): high = lax.ppermute(first, 'plane', down)]
    pallas_call x6 -> x5, Pallas kernels: 10.7 us -> 12 us  [call(): pl.pallas_call(kernel, out_shape=shapes, in_specs=[VMEM] * len(args) + [A...]
    reshape x2, local copies, waits for them, and re-layouts: 0.17 us -> 1.36 us  [masks(): kinds = jnp.concatenate([before, after], axis=1).reshape(1, 2 * rows)]
  transfers between devices with their start and end apart: 19 -> 18, of which waited for: 8 -> 6; matrix products, arithmetic and copies ran while one was open for 1% -> 5% of each run, Pallas kernels for 16% -> 20%
where the time goes in v5:
time: 75.2 us; the launch traced here: 74.6 us
  starting transfers between devices  22.8 us (30%)
  Pallas kernels  18.4 us (24%)
  waiting for transfers between devices  17.8 us (24%)
  local copies, waits for them, and re-layouts  14.8 us (20%)
    ppermute x14, waiting for transfers between devices, swap(): return lax.ppermute(block, 'span', [(i, i ^ d) for i in range(count)])  14.8 us
    pallas_call x5, Pallas kernels, call(): pl.pallas_call(kernel, out_shape=shapes, in_specs=[VMEM] * len(args) + [A...  12 us
    unnamed x48, local copies, waits for them, and re-layouts  12 us
    ppermute x14, starting transfers between devices, swap(): return lax.ppermute(block, 'span', [(i, i ^ d) for i in range(count)])  10.7 us
    ppermute x2, starting transfers between devices, local(): high = lax.ppermute(first, 'plane', down)  7.25 us
    ppermute x2, starting transfers between devices, local(): low = lax.ppermute(last, 'plane', up)  4.84 us
    pallas_call x2, Pallas kernels, pack(): pl.pallas_call(functools.partial(pack_kernel, jobs, len(earlier), rows, c...  3.97 us
    ppermute x2, waiting for transfers between devices, local(): high = lax.ppermute(first, 'plane', down)  3.01 us
  transfers between devices with their start and end apart: 18, of which 6 were waited for; matrix products, arithmetic and copies ran while one was open for 5% of the time, Pallas kernels for 20%

profile of v5, /device:TPU:25, one launch (start us, length us, event | category | flops | bytes accessed | tf_op | source)
XLA Modules:
  0.0 74.6 jit_solution(486833902690474110)
XLA Ops:
  0.0 1.6 %copy-done = f32[128,4,1024]{2,1,0:T(4,128)S(1)} copy-done((f32[128,4,1024]{2,1,0:T(4,128)S(1)}, f32[128,4,1024]{2,1,0:T(4,128)}, u32[]{:S(2)}) %copy-start) | copy-done | bytes 2097176
  1.6 2.0 %shard_map.64 = (f32[8,128]{1,0:T(8,128)S(1)}, f32[520,128]{1,0:T(8,128)}, f32[520,128]{1,0:T(8,128)}, f32[520,128]{1,0:T(8,128)}, f32[8,128]{1,0:T(8,128)S(1)}) custom-call(f32[128,32,128]{2,1,0:T(8,128)S(1)} %bitcast.12), custom_call_target="tpu_custom_call" | custom-call | flops 1024 | bytes 1024 | tf_op jit(solution)/shard_map/pallas_call | solution.py:291
  4.4 1.3 %collective-permute-start.4 = (f32[520,128]{1,0:T(8,128)}, f32[520,128]{1,0:T(8,128)}, u32[]{:S(2)}, u32[]{:S(2)}) collective-permute-start(f32[520,128]{1,0:T(8,128)} %get-tuple-element.43), channel_id=1, source_target_pairs={{0,2},{1,3},{2,0},{3,1},{4,6},{5,7},{6,4},{7,5},{8,10},{9,11},{10,... | collective-permute-start | bytes 798728 | tf_op jit(solution)/shard_map/ppermute | solution.py:305
  6.1 1.9 %shard_map.65 = (f32[8,128]{1,0:T(8,128)S(1)}, f32[520,128]{1,0:T(8,128)}, f32[520,128]{1,0:T(8,128)}, f32[520,128]{1,0:T(8,128)S(1)}, f32[8,128]{1,0:T(8,128)}) custom-call(f32[128,32,128]{2,1,0:T(8,128)S(1)} %bitcast.13, f32[8,128]{1,0:T(8,128)S(1)} %get-tuple-element.36.refs_0_), custom_call_target="tpu_custom_call" | custom-call | flops 1024 | bytes 1024 | tf_op jit(solution)/shard_map/pallas_call | solution.py:291
  9.5 1.3 %collective-permute-start.1 = (f32[520,128]{1,0:T(8,128)}, f32[520,128]{1,0:T(8,128)}, u32[]{:S(2)}, u32[]{:S(2)}) collective-permute-start(f32[520,128]{1,0:T(8,128)} %get-tuple-element.39), channel_id=1, source_target_pairs={{0,2},{1,3},{2,0},{3,1},{4,6},{5,7},{6,4},{7,5},{8,10},{9,11},{10,... | collective-permute-start | bytes 798728 | tf_op jit(solution)/shard_map/ppermute | solution.py:305
  13.7 5.3 %collective-permute-done.5.refs_4_ = f32[520,128]{1,0:T(8,128)} collective-permute-done((f32[520,128]{1,0:T(8,128)}, f32[520,128]{1,0:T(8,128)}, u32[]{:S(2)}, u32[]{:S(2)}) %collective-permute-start.5) | collective-permute-done | bytes 266272 | tf_op jit(solution)/shard_map/ppermute | solution.py:305
  21.0 2.8 %shard_map.66 = (f32[4,352,128]{2,1,0:T(8,128)S(1)}, f32[352,128]{1,0:T(8,128)}, f32[352,128]{1,0:T(8,128)}, f32[352,16]{1,0:T(8,128)S(1)}, f32[8,128]{1,0:T(8,128)S(1)}) custom-call(f32[4096,128]{1,0:T(8,128)S(1)} %bitcast.14, f32[8,128]{1,0:T(8,128)S(1)} %get-tuple-element.41.refs_1_, f32[520,128]{1,0:T(8,128)S(1)} %copy-done.10, ...), custom_call_target="tpu_custom_call" | custom-call | flops 1024 | bytes 1024 | tf_op jit(solution)/shard_map/pallas_call | solution.py:249
  23.8 2.7 %shard_map.67 = (f32[256,128]{1,0:T(8,128)S(1)}, f32[256,128]{1,0:T(8,128)S(1)}, f32[512,128]{1,0:T(8,128)}, f32[8,128]{1,0:T(8,128)S(1)}) custom-call(f32[4,352,128]{2,1,0:T(8,128)S(1)} %get-tuple-element.45.refs_0_, f32[352,16]{1,0:T(8,128)S(1)} %get-tuple-element.46.refs_1_, f32[352,128]{1,0:T(8,128)} %get-tuple-element.47.refs_2_, ...), custom_call_target="tpu_custom_call" | custom-call | flops 1024 | bytes 1024 | tf_op jit(solution)/shard_map/pallas_call | solution.py:249
  29.9 1.3 %collective-permute-start.10 = (f32[512,128]{1,0:T(8,128)}, f32[512,128]{1,0:T(8,128)S(1)}, u32[]{:S(2)}, u32[]{:S(2)}) collective-permute-start(f32[512,128]{1,0:T(8,128)} %get-tuple-element.59), channel_id=1, source_target_pairs={{0,2},{1,3},{2,0},{3,1},{4,6},{5,7},{6,4},{7,5},{8,10},{9,11},{10,... | collective-permute-start | bytes 786440 | tf_op jit(solution)/shard_map/ppermute | solution.py:305
  31.2 3.0 %collective-permute-start.9 = (f32[352,128]{1,0:T(8,128)}, f32[352,128]{1,0:T(8,128)}, u32[]{:S(2)}, u32[]{:S(2)}) collective-permute-start(f32[352,128]{1,0:T(8,128)} %get-tuple-element.47.refs_2_), channel_id=1, source_target_pairs={{4,0},{8,4},{12,8},{16,12},{20,16},{24,20},{28,24},{5,1},{9,5},{13... | collective-permute-start | bytes 540680 | tf_op jit(solution)/shard_map/ppermute | solution.py:334
  34.2 2.9 %collective-permute-start.8 = (f32[352,128]{1,0:T(8,128)}, f32[352,128]{1,0:T(8,128)}, u32[]{:S(2)}, u32[]{:S(2)}) collective-permute-start(f32[352,128]{1,0:T(8,128)} %get-tuple-element.48.refs_3_), channel_id=1, source_target_pairs={{0,4},{4,8},{8,12},{12,16},{16,20},{20,24},{24,28},{1,5},{5,9},{9,... | collective-permute-start | bytes 540680 | tf_op jit(solution)/shard_map/ppermute | solution.py:333
  37.1 1.3 %reshape.20 = s32[1,8]{1,0:T(1,128)} reshape(s32[4,2]{1,0:T(4,128)} %get-tuple-element.73) | data formatting | bytes 64 | tf_op jit(solution)/shard_map/reshape | solution.py:284
  42.1 2.4 %shard_map.68 = (f32[4,352,128]{2,1,0:T(8,128)S(1)}, f32[352,128]{1,0:T(8,128)S(1)}, f32[352,128]{1,0:T(8,128)S(1)}, f32[352,16]{1,0:T(8,128)S(1)}, f32[8,128]{1,0:T(8,128)S(1)}) custom-call(f32[4096,128]{1,0:T(8,128)S(1)} %bitcast.15, f32[8,128]{1,0:T(8,128)S(1)} %copy-done.19, f32[520,128]{1,0:T(8,128)} %collective-permute-done.refs_2_, ...), custom_call_target="tpu_custom_call" | custom-call | flops 1024 | bytes 1024 | tf_op jit(solution)/shard_map/pallas_call | solution.py:249
  44.5 1.9 %collective-permute-start.6 = (f32[352,128]{1,0:T(8,128)S(1)}, f32[352,128]{1,0:T(8,128)S(1)}, u32[]{:S(2)}, u32[]{:S(2)}) collective-permute-start(f32[352,128]{1,0:T(8,128)S(1)} %get-tuple-element.53), channel_id=1, source_target_pairs={{0,4},{4,8},{8,12},{12,16},{16,20},{20,24},{24,28},{1,5},{5,9},{9,... | collective-permute-start | bytes 540680 | tf_op jit(solution)/shard_map/ppermute | solution.py:333
  46.4 4.3 %collective-permute-start.7 = (f32[352,128]{1,0:T(8,128)S(1)}, f32[352,128]{1,0:T(8,128)S(1)}, u32[]{:S(2)}, u32[]{:S(2)}) collective-permute-start(f32[352,128]{1,0:T(8,128)S(1)} %get-tuple-element.54), channel_id=1, source_target_pairs={{4,0},{8,4},{12,8},{16,12},{20,16},{24,20},{28,24},{5,1},{9,5},{13... | collective-permute-start | bytes 540680 | tf_op jit(solution)/shard_map/ppermute | solution.py:334
  50.7 1.2 %collective-permute-start.11 = (f32[256,128]{1,0:T(8,128)S(1)}, f32[256,128]{1,0:T(8,128)S(1)}, u32[]{:S(2)}, u32[]{:S(2)}) collective-permute-start(f32[256,128]{1,0:T(8,128)S(1)} %slice.8), channel_id=1, source_target_pairs={{0,1},{1,0},{2,3},{3,2},{4,5},{5,4},{6,7},{7,6},{8,9},{9,8},{10,11... | collective-permute-start | bytes 393224 | tf_op jit(solution)/shard_map/ppermute | solution.py:305
  52.0 2.0 %shard_map.69 = (f32[512,128]{1,0:T(8,128)S(1)}, f32[512,128]{1,0:T(8,128)S(1)}, f32[512,128]{1,0:T(8,128)S(1)}, f32[8,128]{1,0:T(8,128)S(1)}) custom-call(f32[4,352,128]{2,1,0:T(8,128)S(1)} %copy-done.6, f32[352,16]{1,0:T(8,128)S(1)} %get-tuple-element.46.refs_1_, f32[352,128]{1,0:T(8,128)} %collective-permute-done.8.refs_2_, ...), custom_call_target="tpu_custom_call" | custom-call | flops 1024 | bytes 1024 | tf_op jit(solution)/shard_map/pallas_call | solution.py:249
  54.6 3.0 %collective-permute-done.7.refs_3_ = f32[352,128]{1,0:T(8,128)S(1)} collective-permute-done((f32[352,128]{1,0:T(8,128)S(1)}, f32[352,128]{1,0:T(8,128)S(1)}, u32[]{:S(2)}, u32[]{:S(2)}) %collective-permute-start.7) | collective-permute-done | bytes 180256 | tf_op jit(solution)/shard_map/ppermute | solution.py:334
  57.6 2.0 %shard_map.70 = (f32[512,128]{1,0:T(8,128)S(1)}, f32[512,128]{1,0:T(8,128)S(1)}, f32[512,128]{1,0:T(8,128)S(1)}, f32[512,128]{1,0:T(8,128)S(1)}, f32[8,128]{1,0:T(8,128)}) custom-call(f32[4,352,128]{2,1,0:T(8,128)S(1)} %get-tuple-element.51.refs_0_, f32[352,16]{1,0:T(8,128)S(1)} %get-tuple-element.52.refs_1_, f32[352,128]{1,0:T(8,128)S(1)} %collective-permute-done.6.refs_2_, ...), custom_call_target="tpu_custom_call" | custom-call | flops 1024 | bytes 1024 | tf_op jit(solution)/shard_map/pallas_call | solution.py:249
  59.9 2.0 %collective-permute-start.13 = (f32[512,128]{1,0:T(8,128)S(1)}, f32[512,128]{1,0:T(8,128)S(1)}, u32[]{:S(2)}, u32[]{:S(2)}) collective-permute-start(f32[512,128]{1,0:T(8,128)S(1)} %get-tuple-element.62), channel_id=1, source_target_pairs={{0,3},{1,2},{2,1},{3,0},{4,7},{5,6},{6,5},{7,4},{8,11},{9,10},{10,... | collective-permute-start | bytes 786440 | tf_op jit(solution)/shard_map/ppermute | solution.py:305
  63.9 1.2 %shard_map.71.refs_4_ = f32[128,32,128]{2,1,0:T(8,128)} custom-call(f32[512,128]{1,0:T(8,128)S(1)} %get-tuple-element.64.refs_0_, f32[512,128]{1,0:T(8,128)S(1)} %collective-permute-done.10.refs_1_, f32[256,128]{1,0:T(8,128)S(1)} %collective-permute-done.11.refs_9_.refs_2_, f32[512,128]{1,0:T(8,128)S(1)} %collective-permute-done.15.refs_3_, ...), custom_call_target="tpu_custom_call" | custom-call | flops 1024 | bytes 1024 | tf_op jit(solution)/shard_map/pallas_call | solution.py:377
  65.2 2.1 %collective-permute-done.12.refs_1_ = f32[512,128]{1,0:T(8,128)S(1)} collective-permute-done((f32[512,128]{1,0:T(8,128)S(1)}, f32[512,128]{1,0:T(8,128)S(1)}, u32[]{:S(2)}, u32[]{:S(2)}) %collective-permute-start.12) | collective-permute-done | bytes 262176 | tf_op jit(solution)/shard_map/ppermute | solution.py:305
  67.2 6.2 %collective-permute-done.13.refs_2_ = f32[512,128]{1,0:T(8,128)S(1)} collective-permute-done((f32[512,128]{1,0:T(8,128)S(1)}, f32[512,128]{1,0:T(8,128)S(1)}, u32[]{:S(2)}, u32[]{:S(2)}) %collective-permute-start.13) | collective-permute-done | bytes 262176 | tf_op jit(solution)/shard_map/ppermute | solution.py:305
  73.4 1.2 %shard_map.72 = f32[128,32,128]{2,1,0:T(8,128)} custom-call(f32[512,128]{1,0:T(8,128)S(1)} %get-tuple-element.60.refs_0_, f32[512,128]{1,0:T(8,128)S(1)} %collective-permute-done.12.refs_1_, f32[512,128]{1,0:T(8,128)S(1)} %collective-permute-done.13.refs_2_, f32[512,128]{1,0:T(8,128)S(1)} %collective-permute-done.14.refs_3_, ...), custom_call_target="tpu_custom_call", output_to_operand_aliasing={{}: (4, {})} | custom-call | flops 1024 | bytes 1024 | tf_op jit(solution)/shard_map/pallas_call | solution.py:377
  (80 shorter events, 17.5 us)
Async XLA Ops:
  1.6 17.4 %copy-start.1 = (f32[128,4,1024]{2,1,0:T(4,128)S(1)}, f32[128,4,1024]{2,1,0:T(4,128)}, u32[]{:S(2)}) copy-start(f32[128,4,1024]{2,1,0:T(4,128)} %param.6) | copy-start | bytes 6291460
  1.6 17.4 %copy-start.3 = (f32[352,1]{1,0:T(8,128)S(1)}, f32[352,1]{1,0:T(8,128)}, u32[]{:S(2)}) copy-start(f32[352,1]{1,0:T(8,128)} %constant.35.clone.refs_7_.refs_5_) | copy-start | bytes 4228
  1.6 17.4 %copy-start.4 = (f32[352,1]{1,0:T(8,128)S(1)}, f32[352,1]{1,0:T(8,128)}, u32[]{:S(2)}) copy-start(f32[352,1]{1,0:T(8,128)} %constant.34.clone.refs_6_.refs_4_) | copy-start | bytes 4228
  3.7 7.9 %collective-permute-start.3 = (f32[520,128]{1,0:T(8,128)}, f32[520,128]{1,0:T(8,128)S(1)}, u32[]{:S(2)}, u32[]{:S(2)}) collective-permute-start(f32[520,128]{1,0:T(8,128)} %get-tuple-element.42), channel_id=1, source_target_pairs={{0,1},{1,0},{2,3},{3,2},{4,5},{5,4},{6,7},{7,6},{8,9},{9,8},{10,11... | collective-permute-start | bytes 798728 | tf_op jit(solution)/shard_map/ppermute | solution.py:305
  4.4 9.3 %collective-permute-start.4 = (f32[520,128]{1,0:T(8,128)}, f32[520,128]{1,0:T(8,128)}, u32[]{:S(2)}, u32[]{:S(2)}) collective-permute-start(f32[520,128]{1,0:T(8,128)} %get-tuple-element.43), channel_id=1, source_target_pairs={{0,2},{1,3},{2,0},{3,1},{4,6},{5,7},{6,4},{7,5},{8,10},{9,11},{10,... | collective-permute-start | bytes 798728 | tf_op jit(solution)/shard_map/ppermute | solution.py:305
  5.6 13.3 %collective-permute-start.5 = (f32[520,128]{1,0:T(8,128)}, f32[520,128]{1,0:T(8,128)}, u32[]{:S(2)}, u32[]{:S(2)}) collective-permute-start(f32[520,128]{1,0:T(8,128)} %get-tuple-element.44), channel_id=1, source_target_pairs={{0,3},{1,2},{2,1},{3,0},{4,7},{5,6},{6,5},{7,4},{8,11},{9,10},{10,... | collective-permute-start | bytes 798728 | tf_op jit(solution)/shard_map/ppermute | solution.py:305
  9.3 14.5 %copy-start.2 = (bf16[2,2,128,528]{3,2,1,0:T(8,128)(2,1)S(1)}, bf16[2,2,128,528]{3,2,1,0:T(8,128)(2,1)}, u32[]{:S(2)}) copy-start(bf16[2,2,128,528]{3,2,1,0:T(8,128)(2,1)} %constant.33.clone.refs_7_) | copy-start | bytes 1622020
  9.3 24.8 %collective-permute-start = (f32[520,128]{1,0:T(8,128)}, f32[520,128]{1,0:T(8,128)}, u32[]{:S(2)}, u32[]{:S(2)}) collective-permute-start(f32[520,128]{1,0:T(8,128)} %get-tuple-element.38), channel_id=1, source_target_pairs={{0,1},{1,0},{2,3},{3,2},{4,5},{5,4},{6,7},{7,6},{8,9},{9,8},{10,11... | collective-permute-start | bytes 798728 | tf_op jit(solution)/shard_map/ppermute | solution.py:305
  9.5 29.6 %collective-permute-start.1 = (f32[520,128]{1,0:T(8,128)}, f32[520,128]{1,0:T(8,128)}, u32[]{:S(2)}, u32[]{:S(2)}) collective-permute-start(f32[520,128]{1,0:T(8,128)} %get-tuple-element.39), channel_id=1, source_target_pairs={{0,2},{1,3},{2,0},{3,1},{4,6},{5,7},{6,4},{7,5},{8,10},{9,11},{10,... | collective-permute-start | bytes 798728 | tf_op jit(solution)/shard_map/ppermute | solution.py:305
  12.2 26.8 %collective-permute-start.2 = (f32[520,128]{1,0:T(8,128)}, f32[520,128]{1,0:T(8,128)}, u32[]{:S(2)}, u32[]{:S(2)}) collective-permute-start(f32[520,128]{1,0:T(8,128)} %copy-done.22), channel_id=1, source_target_pairs={{0,3},{1,2},{2,1},{3,0},{4,7},{5,6},{6,5},{7,4},{8,11},{9,10},{10,... | collective-permute-start | bytes 798728 | tf_op jit(solution)/shard_map/ppermute | solution.py:305
  29.9 20.9 %collective-permute-start.10 = (f32[512,128]{1,0:T(8,128)}, f32[512,128]{1,0:T(8,128)S(1)}, u32[]{:S(2)}, u32[]{:S(2)}) collective-permute-start(f32[512,128]{1,0:T(8,128)} %get-tuple-element.59), channel_id=1, source_target_pairs={{0,2},{1,3},{2,0},{3,1},{4,6},{5,7},{6,4},{7,5},{8,10},{9,11},{10,... | collective-permute-start | bytes 786440 | tf_op jit(solution)/shard_map/ppermute | solution.py:305
  31.2 20.8 %collective-permute-start.9 = (f32[352,128]{1,0:T(8,128)}, f32[352,128]{1,0:T(8,128)}, u32[]{:S(2)}, u32[]{:S(2)}) collective-permute-start(f32[352,128]{1,0:T(8,128)} %get-tuple-element.47.refs_2_), channel_id=1, source_target_pairs={{4,0},{8,4},{12,8},{16,12},{20,16},{24,20},{28,24},{5,1},{9,5},{13... | collective-permute-start | bytes 540680 | tf_op jit(solution)/shard_map/ppermute | solution.py:334
  34.2 17.8 %collective-permute-start.8 = (f32[352,128]{1,0:T(8,128)}, f32[352,128]{1,0:T(8,128)}, u32[]{:S(2)}, u32[]{:S(2)}) collective-permute-start(f32[352,128]{1,0:T(8,128)} %get-tuple-element.48.refs_3_), channel_id=1, source_target_pairs={{0,4},{4,8},{8,12},{12,16},{16,20},{20,24},{24,28},{1,5},{5,9},{9,... | collective-permute-start | bytes 540680 | tf_op jit(solution)/shard_map/ppermute | solution.py:333
  38.4 13.6 %copy-start.6 = (f32[4,352,128]{2,1,0:T(8,128)S(1)}, f32[4,352,128]{2,1,0:T(8,128)}, u32[]{:S(2)}) copy-start(f32[4,352,128]{2,1,0:T(8,128)} %copy-done.5) | copy-start | bytes 2162692
  42.1 9.9 %copy-start.16 = (s32[4,128]{1,0:T(4,128)S(1)}, s32[4,128]{1,0:T(4,128)}, u32[]{:S(2)}) copy-start(s32[4,128]{1,0:T(4,128)} %copy-done.15) | copy-start | bytes 6148
  44.5 10.1 %collective-permute-start.6 = (f32[352,128]{1,0:T(8,128)S(1)}, f32[352,128]{1,0:T(8,128)S(1)}, u32[]{:S(2)}, u32[]{:S(2)}) collective-permute-start(f32[352,128]{1,0:T(8,128)S(1)} %get-tuple-element.53), channel_id=1, source_target_pairs={{0,4},{4,8},{8,12},{12,16},{16,20},{20,24},{24,28},{1,5},{5,9},{9,... | collective-permute-start | bytes 540680 | tf_op jit(solution)/shard_map/ppermute | solution.py:333
  46.4 11.2 %collective-permute-start.7 = (f32[352,128]{1,0:T(8,128)S(1)}, f32[352,128]{1,0:T(8,128)S(1)}, u32[]{:S(2)}, u32[]{:S(2)}) collective-permute-start(f32[352,128]{1,0:T(8,128)S(1)} %get-tuple-element.54), channel_id=1, source_target_pairs={{4,0},{8,4},{12,8},{16,12},{20,16},{24,20},{28,24},{5,1},{9,5},{13... | collective-permute-start | bytes 540680 | tf_op jit(solution)/shard_map/ppermute | solution.py:334
  50.7 6.9 %collective-permute-start.11 = (f32[256,128]{1,0:T(8,128)S(1)}, f32[256,128]{1,0:T(8,128)S(1)}, u32[]{:S(2)}, u32[]{:S(2)}) collective-permute-start(f32[256,128]{1,0:T(8,128)S(1)} %slice.8), channel_id=1, source_target_pairs={{0,1},{1,0},{2,3},{3,2},{4,5},{5,4},{6,7},{7,6},{8,9},{9,8},{10,11... | collective-permute-start | bytes 393224 | tf_op jit(solution)/shard_map/ppermute | solution.py:305
  54.1 8.0 %collective-permute-start.15 = (f32[512,128]{1,0:T(8,128)S(1)}, f32[512,128]{1,0:T(8,128)S(1)}, u32[]{:S(2)}, u32[]{:S(2)}) collective-permute-start(f32[512,128]{1,0:T(8,128)S(1)} %get-tuple-element.65), channel_id=1, source_target_pairs={{0,2},{1,3},{2,0},{3,1},{4,6},{5,7},{6,4},{7,5},{8,10},{9,11},{10,... | collective-permute-start | bytes 786440 | tf_op jit(solution)/shard_map/ppermute | solution.py:305
  54.3 8.6 %collective-permute-start.17 = (f32[512,128]{1,0:T(8,128)S(1)}, f32[512,128]{1,0:T(8,128)S(1)}, u32[]{:S(2)}, u32[]{:S(2)}) collective-permute-start(f32[512,128]{1,0:T(8,128)S(1)} %get-tuple-element.66), channel_id=1, source_target_pairs={{0,1},{1,0},{2,3},{3,2},{4,5},{5,4},{6,7},{7,6},{8,9},{9,8},{10,11... | collective-permute-start | bytes 786440 | tf_op jit(solution)/shard_map/ppermute | solution.py:305
  59.7 7.5 %collective-permute-start.12 = (f32[512,128]{1,0:T(8,128)S(1)}, f32[512,128]{1,0:T(8,128)S(1)}, u32[]{:S(2)}, u32[]{:S(2)}) collective-permute-start(f32[512,128]{1,0:T(8,128)S(1)} %get-tuple-element.61), channel_id=1, source_target_pairs={{0,2},{1,3},{2,0},{3,1},{4,6},{5,7},{6,4},{7,5},{8,10},{9,11},{10,... | collective-permute-start | bytes 786440 | tf_op jit(solution)/shard_map/ppermute | solution.py:305
  59.9 13.6 %collective-permute-start.13 = (f32[512,128]{1,0:T(8,128)S(1)}, f32[512,128]{1,0:T(8,128)S(1)}, u32[]{:S(2)}, u32[]{:S(2)}) collective-permute-start(f32[512,128]{1,0:T(8,128)S(1)} %get-tuple-element.62), channel_id=1, source_target_pairs={{0,3},{1,2},{2,1},{3,0},{4,7},{5,6},{6,5},{7,4},{8,11},{9,10},{10,... | collective-permute-start | bytes 786440 | tf_op jit(solution)/shard_map/ppermute | solution.py:305
  61.8 11.6 %collective-permute-start.14 = (f32[512,128]{1,0:T(8,128)S(1)}, f32[512,128]{1,0:T(8,128)S(1)}, u32[]{:S(2)}, u32[]{:S(2)}) collective-permute-start(f32[512,128]{1,0:T(8,128)S(1)} %get-tuple-element.63), channel_id=1, source_target_pairs={{0,1},{1,0},{2,3},{3,2},{4,5},{5,4},{6,7},{7,6},{8,9},{9,8},{10,11... | collective-permute-start | bytes 786440 | tf_op jit(solution)/shard_map/ppermute | solution.py:305
  62.1 1.9 %collective-permute-start.16 = (f32[256,128]{1,0:T(8,128)S(1)}, f32[256,128]{1,0:T(8,128)S(1)}, u32[]{:S(2)}, u32[]{:S(2)}) collective-permute-start(f32[256,128]{1,0:T(8,128)S(1)} %slice.9), channel_id=1, source_target_pairs={{0,1},{1,0},{2,3},{3,2},{4,5},{5,4},{6,7},{7,6},{8,9},{9,8},{10,11... | collective-permute-start | bytes 393224 | tf_op jit(solution)/shard_map/ppermute | solution.py:305
  (18 other events, 40.9 us)

commit v6 on v1

--- a/solution.py
+++ b/solution.py
@@ -12,7 +12,10 @@
 PENALTY = 12.0
 LANES = 128
 VMEM = pl.BlockSpec(memory_space=pltpu.VMEM)
-PARAMS = pltpu.CompilerParams(vmem_limit_bytes=32 * 1024 * 1024)
+ANY = pl.BlockSpec(memory_space=pl.ANY)
+PARAMS = pltpu.CompilerParams(vmem_limit_bytes=24 * 1024 * 1024)
+COST = pl.CostEstimate(flops=0, bytes_accessed=200_000_000, transcendentals=0)
+SPLIT = 4
 
 
 def split(values):
@@ -58,29 +61,47 @@
     return jnp.concatenate([high, high, low], axis=axis)
 
 
-def pack_kernel(rows, row_count, count, cells, width, x_ref, *outs):
+def pack_kernel(rows, row_count, count, cells, width, earlier, x_ref, *refs):
+    outs, (held, arrived) = refs[earlier:-2], refs[-2:]
     me = lax.axis_index("span")
     tiles = width // LANES
-    stride = count * tiles * row_count
-    lane = lax.broadcasted_iota(jnp.int32, (cells, LANES), 1)
-    sides = jnp.zeros((cells, LANES), jnp.float32)
-    for d in range(count):
-        target = jnp.bitwise_xor(me, d)
-        for i, row in enumerate(rows):
-            for tile in range(tiles):
-                outs[d][i * cells : (i + 1) * cells, tile * LANES : (tile + 1) * LANES] = x_ref[
-                    pl.ds((target * tiles + tile) * row_count + row, cells, stride=stride), :
-                ]
-            before = jnp.maximum(target * tiles - 1, 0)
-            after = jnp.minimum((target + 1) * tiles, count * tiles - 1)
-            for side, (tile, source) in enumerate(((before, LANES - 1), (after, 0))):
-                at = d * 8 + i * 2 + side
-                column = x_ref[pl.ds(tile * row_count + row, cells, stride=stride), :]
-                column = pltpu.roll(column, (at - source) % LANES, 1)
-                sides = jnp.where(lane == at, column, sides)
+    lines = x_ref.shape[1]
+    pitch = held.shape[0] // cells
+    some = cells // SPLIT
+    copies = [
+        pltpu.make_async_copy(
+            x_ref.at[pl.ds(part * some, some)],
+            held.reshape(cells, pitch, LANES).at[pl.ds(part * some, some), pl.ds(0, lines)],
+            arrived.at[part],
+        )
+        for part in range(SPLIT)
+    ]
+    for copy in copies:
+        copy.start()
+    lane = lax.broadcasted_iota(jnp.int32, (some, LANES), 1)
+    sides = []
+    for part, copy in enumerate(copies):
+        copy.wait()
+        beside = jnp.zeros((some, LANES), jnp.float32)
+
+        def line(tile, row):
+            return held[pl.ds(part * some * pitch + tile * row_count + row, some, stride=pitch), :]
+
+        for d in range(count):
+            first = jnp.bitwise_xor(me, d) * tiles
+            for i, row in enumerate(rows):
+                base = i * cells + part * some
+                for tile in range(tiles):
+                    outs[d][base : base + some, tile * LANES : (tile + 1) * LANES] = line(first + tile, row)
+                before = jnp.maximum(first - 1, 0)
+                after = jnp.minimum(first + tiles, count * tiles - 1)
+                for side, (tile, source) in enumerate(((before, LANES - 1), (after, 0))):
+                    at = d * 8 + i * 2 + side
+                    beside = jnp.where(lane == at, pltpu.roll(line(tile, row), (at - source) % LANES, 1), beside)
+        sides.append(beside)
     if cells < LANES:
-        sides = jnp.concatenate([sides, jnp.zeros((LANES - cells, LANES), jnp.float32)], axis=0)
-    turned = sides.T
+        sides.append(jnp.zeros((LANES - cells, LANES), jnp.float32))
+    turned = jnp.concatenate(sides, axis=0).T
     for d in range(count):
         if width > LANES:
             outs[d][len(rows) * cells :, :] = jnp.zeros((8, width), jnp.float32)
@@ -192,17 +213,32 @@
 def unpack_kernel(row_groups, row_count, count, cells, width, *refs):
     me = lax.axis_index("span")
     tiles = width // LANES
-    stride = count * tiles * row_count
-    out_ref = refs[-1]
-    for g, rows in enumerate(row_groups):
-        for d in range(count):
-            block = refs[g * count + d]
-            source = jnp.bitwise_xor(me, d)
-            for i, row in enumerate(rows):
-                for tile in range(tiles):
-                    out_ref[pl.ds((source * tiles + tile) * row_count + row, cells, stride=stride), :] = block[
-                        i * cells : (i + 1) * cells, tile * LANES : (tile + 1) * LANES
-                    ]
+    blocks, (out_ref, held, done) = refs[:-3], refs[-3:]
+    pitch = held.shape[0] // cells
+    lines = out_ref.shape[1]
+    some = cells // SPLIT
+    copies = []
+    for part in range(SPLIT):
+        for g, rows in enumerate(row_groups):
+            for d in range(count):
+                source = jnp.bitwise_xor(me, d)
+                for i, row in enumerate(rows):
+                    base = i * cells + part * some
+                    for tile in range(tiles):
+                        at = part * some * pitch + (source * tiles + tile) * row_count + row
+                        held[pl.ds(at, some, stride=pitch), :] = blocks[g * count + d][
+                            base : base + some, tile * LANES : (tile + 1) * LANES
+                        ]
+        copies.append(
+            pltpu.make_async_copy(
+                held.reshape(cells, pitch, LANES).at[pl.ds(part * some, some), pl.ds(0, lines)],
+                out_ref.at[pl.ds(part * some, some)],
+                done.at[part],
+            )
+        )
+        copies[-1].start()
+    for copy in copies:
+        copy.wait()
 
 
 def call(kernel, outs, *args):
@@ -213,6 +249,7 @@
         in_specs=[VMEM] * len(args),
         out_specs=[VMEM] * len(outs),
         compiler_params=PARAMS,
+        cost_estimate=COST,
     )(*args)
 
 
@@ -235,7 +272,8 @@
     modes = fluid.shape[0]
     forward, inverse, fluid, solid = map(jnp.asarray, (forward, inverse, fluid, solid))
 
-    source = pressure_source.reshape(cells, row_count, tiles, LANES).transpose(0, 2, 1, 3).reshape(-1, LANES)
+    source = pressure_source.reshape(cells, row_count, tiles, LANES).transpose(0, 2, 1, 3)
+    source = source.reshape(cells, tiles * row_count, LANES)
 
     me = lax.axis_index("span")
     mask = lax.dynamic_slice_in_dim(solid_mask, me * width, width, axis=1)
@@ -253,15 +291,22 @@
     edge_mask, edge_sides = picked(edges)
     inner_mask, inner_sides = picked(inner)
 
-    def pack(rows):
-        return call(
-            functools.partial(pack_kernel, rows, row_count, count, cells, width),
-            [(len(rows) * cells + 8, width)] * count,
-            source,
-        )
+    lines = tiles * row_count
+    scratch = [pltpu.VMEM((cells * (lines + 8), LANES), jnp.float32), pltpu.SemaphoreType.DMA((SPLIT,))]
+
+    def pack(rows, *earlier):
+        return pl.pallas_call(
+            functools.partial(pack_kernel, rows, row_count, count, cells, width, len(earlier)),
+            out_shape=[jax.ShapeDtypeStruct((len(rows) * cells + 8, width), jnp.float32)] * count,
+            in_specs=[ANY] * (1 + len(earlier)),
+            out_specs=[VMEM] * count,
+            scratch_shapes=scratch,
+            compiler_params=PARAMS,
+            cost_estimate=COST,
+        )(source, *earlier)
 
     edge_blocks = exchange(pack(edges))
-    inner_blocks = exchange(pack(inner))
+    inner_blocks = exchange(pack(inner, edge_blocks[1]))
     spectrum, first, last, sides = call(
         functools.partial(edge_kernel, count, cells),
         [(2, modes, width), (modes, width), (modes, width), (modes, 16)],
@@ -283,11 +328,16 @@
         spectrum, first, last, sides, ones, low, high, inverse, fluid, solid, edge_mask,
     )
     edge_got = exchange(edge_out)
-    (result,) = call(
+    blocks = [*inner_got, *edge_got]
+    result = pl.pallas_call(
         functools.partial(unpack_kernel, (inner, edges), row_count, count, cells, width),
-        [(cells * tiles * row_count, LANES)],
-        *inner_got, *edge_got,
-    )
+        out_shape=jax.ShapeDtypeStruct((cells, lines, LANES), jnp.float32),
+        in_specs=[VMEM] * len(blocks),
+        out_specs=ANY,
+        scratch_shapes=scratch,
+        compiler_params=PARAMS,
+        cost_estimate=COST,
+    )(*blocks)
     return result.reshape(cells, tiles, row_count, LANES).transpose(0, 2, 1, 3).reshape(cells, row_count, columns)
 
 

time: 67 us -> 61.5 us (0.918)
  waiting for transfers between devices: 35.8 us -> 27.4 us
  local copies, waits for them, and re-layouts: 2.66 us -> 8.31 us
  Pallas kernels: 13.1 us -> 9.97 us
    pallas_call x6 -> x3, Pallas kernels: 13.1 us -> 5 us  [call(): pl.pallas_call(kernel, out_shape=shapes, in_specs=[VMEM] * len(args), out...]
    ppermute x12, waiting for transfers between devices: 26.1 us -> 19 us  [exchange(): lax.ppermute(blocks[d], 'span', [(i, i ^ d) for i in range(count)])]
    pallas_call x0 -> x3, Pallas kernels: none -> 4.97 us  [the longest x2 3.55 us: pack(): pl.pallas_call(functools.partial(pack_kernel, rows, row_count, count, cel...]
    unnamed x14 -> x24, local copies, waits for them, and re-layouts: 2.31 us -> 5.81 us
    ppermute x1, waiting for transfers between devices: 2.07 us -> 0.54 us  [local(): low = lax.ppermute(last, 'plane', up)]
    slice x1, local copies, waits for them, and re-layouts: 0.07 us -> 0.84 us  [picked(): return (jnp.stack([mask[row] for row in rows]), kinds[None, :])]
    concatenate x1, local copies, waits for them, and re-layouts: 0.1 us -> 0.82 us  [local(): framed = jnp.concatenate([outside, solid_mask, outside], axis=1)]
    another operation x1, local copies, waits for them, and re-layouts: 0.07 us -> 0.76 us  [picked(): return (jnp.stack([mask[row] for row in rows]), kinds[None, :])]
  transfers between devices with their start and end apart: 14 -> 14, of which waited for: 6 -> 6; matrix products, arithmetic and copies ran while one was open for 1% -> 4% of each run, Pallas kernels for 11% -> 11%
where the time goes in v6:
time: 61.5 us; the launch traced here: 61.1 us
  waiting for transfers between devices  27.4 us (45%)
  starting transfers between devices  15.1 us (25%)
  Pallas kernels  9.97 us (16%)
  local copies, waits for them, and re-layouts  8.31 us (14%)
    ppermute x12, waiting for transfers between devices, exchange(): lax.ppermute(blocks[d], 'span', [(i, i ^ d) for i in range(count)])  19 us
    ppermute x12, starting transfers between devices, exchange(): lax.ppermute(blocks[d], 'span', [(i, i ^ d) for i in range(count)])  8.88 us
    ppermute x1, waiting for transfers between devices, local(): high = lax.ppermute(first, 'plane', down)  7.9 us
    unnamed x24, local copies, waits for them, and re-layouts  5.81 us
    pallas_call x3, Pallas kernels, call(): pl.pallas_call(kernel, out_shape=shapes, in_specs=[VMEM] * len(args), out...  5 us
    pallas_call x2, Pallas kernels, pack(): pl.pallas_call(functools.partial(pack_kernel, rows, row_count, count, cel...  3.55 us
    ppermute x1, starting transfers between devices, local(): low = lax.ppermute(last, 'plane', up)  3.12 us
    ppermute x1, starting transfers between devices, local(): high = lax.ppermute(first, 'plane', down)  3.06 us
  transfers between devices with their start and end apart: 14, of which 6 were waited for; matrix products, arithmetic and copies ran while one was open for 4% of the time, Pallas kernels for 11%

profile of v6, /device:TPU:25, one launch (start us, length us, event | category | flops | bytes accessed | tf_op | source)
XLA Modules:
  0.0 61.1 jit_solution(16596207882682140757)
XLA Ops:
  0.0 1.6 %copy-done = f32[128,4,1024]{2,1,0:T(4,128)S(1)} copy-done((f32[128,4,1024]{2,1,0:T(4,128)S(1)}, f32[128,4,1024]{2,1,0:T(4,128)}, u32[]{:S(2)}) %copy-start) | copy-done | bytes 2097176
  1.6 1.8 %shard_map.64 = (f32[264,256]{1,0:T(8,128)S(1)}, f32[264,256]{1,0:T(8,128)}, f32[264,256]{1,0:T(8,128)}, f32[264,256]{1,0:T(8,128)}) custom-call(f32[128,32,128]{2,1,0:T(8,128)S(1)} %bitcast.22), custom_call_target="tpu_custom_call" | custom-call | bytes 200000000 | tf_op jit(solution)/shard_map/pallas_call | solution.py:298
  4.8 1.2 %collective-permute-start.4 = (f32[264,256]{1,0:T(8,128)}, f32[264,256]{1,0:T(8,128)}, u32[]{:S(2)}, u32[]{:S(2)}) collective-permute-start(f32[264,256]{1,0:T(8,128)} %get-tuple-element.32), channel_id=1, source_target_pairs={{0,2},{1,3},{2,0},{3,1},{4,6},{5,7},{6,4},{7,5},{8,10},{9,11},{10,... | collective-permute-start | bytes 811016 | tf_op jit(solution)/shard_map/ppermute | solution.py:259
  6.4 0.8 %concatenate.12 = s32[4,1026]{1,0:T(4,128)S(1)} concatenate(s32[4,1]{1,0:T(4,128)S(1)} %broadcast.7, s32[4,1024]{1,0:T(4,128)} %param.7, s32[4,1]{1,0:T(4,128)S(1)} %broadcast.7), dimensions={1} | concatenate | bytes 32832 | tf_op jit(solution)/shard_map/concatenate | solution.py:281
  7.5 0.8 %constant_dynamic-slice_fusion = (s32[1,256]{1,0:T(1,128)S(1)}, s32[1,256]{1,0:T(1,128)S(1)}) fusion(s32[4,1024]{1,0:T(4,128)} %param.7, s32[]{:T(128)S(6)} %select_n.9, s32[]{:T(128)S(6)} %add.30), kind=kLoop, calls=%fused_computation.2 | loop fusion | bytes 4104 | tf_op jit(solution)/shard_map/slice | solution.py:289
  8.3 1.8 %shard_map.65 = (f32[264,256]{1,0:T(8,128)S(1)}, f32[264,256]{1,0:T(8,128)}, f32[264,256]{1,0:T(8,128)}, f32[264,256]{1,0:T(8,128)}) custom-call(f32[128,32,128]{2,1,0:T(8,128)S(1)} %bitcast.23, f32[264,256]{1,0:T(8,128)} %collective-permute-done.refs_0_.refs_1_), custom_call_target="tpu_custom_call" | custom-call | bytes 200000000 | tf_op jit(solution)/shard_map/pallas_call | solution.py:298
  11.0 1.2 %collective-permute-start.2 = (f32[264,256]{1,0:T(8,128)}, f32[264,256]{1,0:T(8,128)S(1)}, u32[]{:S(2)}, u32[]{:S(2)}) collective-permute-start(f32[264,256]{1,0:T(8,128)} %get-tuple-element.29), channel_id=1, source_target_pairs={{0,2},{1,3},{2,0},{3,1},{4,6},{5,7},{6,4},{7,5},{8,10},{9,11},{10,... | collective-permute-start | bytes 811016 | tf_op jit(solution)/shard_map/ppermute | solution.py:259
  13.8 5.7 %collective-permute-done.5.refs_3_ = f32[264,256]{1,0:T(8,128)} collective-permute-done((f32[264,256]{1,0:T(8,128)}, f32[264,256]{1,0:T(8,128)}, u32[]{:S(2)}, u32[]{:S(2)}) %collective-permute-start.5) | collective-permute-done | bytes 270368 | tf_op jit(solution)/shard_map/ppermute | solution.py:259
  19.5 0.9 %copy-done.5 = f32[352,1]{1,0:T(8,128)S(1)} copy-done((f32[352,1]{1,0:T(8,128)S(1)}, f32[352,1]{1,0:T(8,128)}, u32[]{:S(2)}) %copy-start.5) | copy-done | bytes 1432
  20.4 1.0 %copy-done.9 = f32[264,256]{1,0:T(8,128)S(1)} copy-done((f32[264,256]{1,0:T(8,128)S(1)}, f32[264,256]{1,0:T(8,128)}, u32[]{:S(2)}) %copy-start.9) | copy-done | bytes 270360
  21.3 1.9 %shard_map.66 = (f32[2,352,256]{2,1,0:T(8,128)S(1)}, f32[352,256]{1,0:T(8,128)S(1)}, f32[352,256]{1,0:T(8,128)S(1)}, f32[352,16]{1,0:T(8,128)S(1)}) custom-call(f32[264,256]{1,0:T(8,128)S(1)} %copy-done.9, f32[264,256]{1,0:T(8,128)} %collective-permute-done.refs_0_.refs_1_, f32[264,256]{1,0:T(8,128)} %collective-permute-done.4.refs_2_, ...), custom_call_target="tpu_custom_call" | custom-call | bytes 200000000 | tf_op jit(solution)/shard_map/pallas_call | solution.py:246
  23.3 3.1 %collective-permute-start.9 = (f32[352,256]{1,0:T(8,128)S(1)}, f32[352,256]{1,0:T(8,128)S(1)}, u32[]{:S(2)}, u32[]{:S(2)}) collective-permute-start(f32[352,256]{1,0:T(8,128)S(1)} %get-tuple-element.35.refs_11_.refs_2_), channel_id=1, source_target_pairs={{0,4},{4,8},{8,12},{12,16},{16,20},{20,24},{24,28},{1,5},{5,9},{9,... | collective-permute-start | bytes 1081352 | tf_op jit(solution)/shard_map/ppermute | solution.py:317
  26.4 3.1 %collective-permute-start.10 = (f32[352,256]{1,0:T(8,128)S(1)}, f32[352,256]{1,0:T(8,128)S(1)}, u32[]{:S(2)}, u32[]{:S(2)}) collective-permute-start(f32[352,256]{1,0:T(8,128)S(1)} %get-tuple-element.34.refs_10_.refs_1_), channel_id=1, source_target_pairs={{4,0},{8,4},{12,8},{16,12},{20,16},{24,20},{28,24},{5,1},{9,5},{13... | collective-permute-start | bytes 1081352 | tf_op jit(solution)/shard_map/ppermute | solution.py:318
  29.5 1.3 %collective-permute-done.3.refs_3_ = f32[264,256]{1,0:T(8,128)S(1)} collective-permute-done((f32[264,256]{1,0:T(8,128)}, f32[264,256]{1,0:T(8,128)S(1)}, u32[]{:S(2)}, u32[]{:S(2)}) %collective-permute-start.3) | collective-permute-done | bytes 270368 | tf_op jit(solution)/shard_map/ppermute | solution.py:259
  30.9 0.9 %copy-done.6 = f32[352,1]{1,0:T(8,128)S(1)} copy-done((f32[352,1]{1,0:T(8,128)S(1)}, f32[352,1]{1,0:T(8,128)}, u32[]{:S(2)}) %copy-start.6) | copy-done | bytes 1432
  31.8 1.7 %shard_map.67 = (f32[256,256]{1,0:T(8,128)S(1)}, f32[256,256]{1,0:T(8,128)S(1)}, f32[256,256]{1,0:T(8,128)S(1)}, f32[256,256]{1,0:T(8,128)S(1)}, f32[2,352,256]{2,1,0:T(8,128)S(1)}) custom-call(f32[264,256]{1,0:T(8,128)S(1)} %copy-done.11, f32[264,256]{1,0:T(8,128)S(1)} %collective-permute-done.1.refs_1_, f32[264,256]{1,0:T(8,128)S(1)} %collective-permute-done.2.refs_2_, ...), custom_call_target="tpu_custom_call" | custom-call | bytes 200000000 | tf_op jit(solution)/shard_map/pallas_call | solution.py:246
  33.6 1.3 %collective-permute-start.7 = (f32[256,256]{1,0:T(8,128)S(1)}, f32[256,256]{1,0:T(8,128)S(1)}, u32[]{:S(2)}, u32[]{:S(2)}) collective-permute-start(f32[256,256]{1,0:T(8,128)S(1)} %get-tuple-element.38), channel_id=1, source_target_pairs={{0,2},{1,3},{2,0},{3,1},{4,6},{5,7},{6,4},{7,5},{8,10},{9,11},{10,... | collective-permute-start | bytes 786440 | tf_op jit(solution)/shard_map/ppermute | solution.py:259
  34.9 0.8 %collective-permute-start.8 = (f32[256,256]{1,0:T(8,128)S(1)}, f32[256,256]{1,0:T(8,128)S(1)}, u32[]{:S(2)}, u32[]{:S(2)}) collective-permute-start(f32[256,256]{1,0:T(8,128)S(1)} %get-tuple-element.39), channel_id=1, source_target_pairs={{0,3},{1,2},{2,1},{3,0},{4,7},{5,6},{6,5},{7,4},{8,11},{9,10},{10,... | collective-permute-start | bytes 786440 | tf_op jit(solution)/shard_map/ppermute | solution.py:259
  36.3 7.9 %collective-permute-done.10.refs_6_ = f32[352,256]{1,0:T(8,128)S(1)} collective-permute-done((f32[352,256]{1,0:T(8,128)S(1)}, f32[352,256]{1,0:T(8,128)S(1)}, u32[]{:S(2)}, u32[]{:S(2)}) %collective-permute-start.10) | collective-permute-done | bytes 360480 | tf_op jit(solution)/shard_map/ppermute | solution.py:318
  44.2 1.3 %shard_map.68 = (f32[256,256]{1,0:T(8,128)S(1)}, f32[256,256]{1,0:T(8,128)S(1)}, f32[256,256]{1,0:T(8,128)S(1)}, f32[256,256]{1,0:T(8,128)S(1)}) custom-call(f32[2,352,256]{2,1,0:T(8,128)S(1)} %get-tuple-element.40.refs_0_, f32[352,256]{1,0:T(8,128)S(1)} %get-tuple-element.34.refs_10_.refs_1_, f32[352,256]{1,0:T(8,128)S(1)} %get-tuple-element.35.refs_11_.refs_2_, ...), custom_call_target="tpu_custom_call" | custom-call | bytes 200000000 | tf_op jit(solution)/shard_map/pallas_call | solution.py:246
  46.0 1.3 %collective-permute-start.12 = (f32[256,256]{1,0:T(8,128)S(1)}, f32[256,256]{1,0:T(8,128)S(1)}, u32[]{:S(2)}, u32[]{:S(2)}) collective-permute-start(f32[256,256]{1,0:T(8,128)S(1)} %get-tuple-element.45), channel_id=1, source_target_pairs={{0,2},{1,3},{2,0},{3,1},{4,6},{5,7},{6,4},{7,5},{8,10},{9,11},{10,... | collective-permute-start | bytes 786440 | tf_op jit(solution)/shard_map/ppermute | solution.py:259
  47.8 6.2 %collective-permute-done.12.refs_6_ = f32[256,256]{1,0:T(8,128)S(1)} collective-permute-done((f32[256,256]{1,0:T(8,128)S(1)}, f32[256,256]{1,0:T(8,128)S(1)}, u32[]{:S(2)}, u32[]{:S(2)}) %collective-permute-start.12) | collective-permute-done | bytes 262176 | tf_op jit(solution)/shard_map/ppermute | solution.py:259
  53.9 5.8 %collective-permute-done.13.refs_7_ = f32[256,256]{1,0:T(8,128)S(1)} collective-permute-done((f32[256,256]{1,0:T(8,128)S(1)}, f32[256,256]{1,0:T(8,128)S(1)}, u32[]{:S(2)}, u32[]{:S(2)}) %collective-permute-start.13) | collective-permute-done | bytes 262176 | tf_op jit(solution)/shard_map/ppermute | solution.py:259
  59.7 1.4 %shard_map.69 = f32[128,32,128]{2,1,0:T(8,128)} custom-call(f32[256,256]{1,0:T(8,128)S(1)} %get-tuple-element.36.refs_0_, f32[256,256]{1,0:T(8,128)S(1)} %collective-permute-done.6.refs_1_, f32[256,256]{1,0:T(8,128)S(1)} %collective-permute-done.7.refs_2_, f32[256,256]{1,0:T(8,128)S(1)} %collective-permute-done.8.refs_3_, ...), custom_call_target="tpu_custom_call" | custom-call | bytes 200000000 | tf_op jit(solution)/shard_map/pallas_call | solution.py:332
  (46 shorter events, 6.1 us)
Async XLA Ops:
  0.0 1.6 %copy-start = (f32[128,4,1024]{2,1,0:T(4,128)S(1)}, f32[128,4,1024]{2,1,0:T(4,128)}, u32[]{:S(2)}) copy-start(f32[128,4,1024]{2,1,0:T(4,128)} %param.6) | copy-start | bytes 6291460
  1.6 6.7 %copy-start.1 = (f32[128,4,1024]{2,1,0:T(4,128)S(1)}, f32[128,4,1024]{2,1,0:T(4,128)}, u32[]{:S(2)}) copy-start(f32[128,4,1024]{2,1,0:T(4,128)} %param.6) | copy-start | bytes 6291460
  1.6 17.9 %copy-start.3 = (bf16[2,2,176,384]{3,2,1,0:T(8,128)(2,1)S(1)}, bf16[2,2,176,384]{3,2,1,0:T(8,128)(2,1)}, u32[]{:S(2)}) copy-start(bf16[2,2,176,384]{3,2,1,0:T(8,128)(2,1)} %constant.28.clone.refs_4_) | copy-start | bytes 1622020
  1.6 17.9 %copy-start.4 = (f32[352,1]{1,0:T(8,128)S(1)}, f32[352,1]{1,0:T(8,128)}, u32[]{:S(2)}) copy-start(f32[352,1]{1,0:T(8,128)} %constant.30.clone.refs_5_.refs_6_.refs_8_) | copy-start | bytes 4228
  4.1 4.2 %collective-permute-start = (f32[264,256]{1,0:T(8,128)}, f32[264,256]{1,0:T(8,128)}, u32[]{:S(2)}, u32[]{:S(2)}) collective-permute-start(f32[264,256]{1,0:T(8,128)} %get-tuple-element.26), channel_id=1, source_target_pairs={{0,1},{1,0},{2,3},{3,2},{4,5},{5,4},{6,7},{7,6},{8,9},{9,8},{10,11... | collective-permute-start | bytes 811016 | tf_op jit(solution)/shard_map/ppermute | solution.py:259
  4.8 9.0 %collective-permute-start.4 = (f32[264,256]{1,0:T(8,128)}, f32[264,256]{1,0:T(8,128)}, u32[]{:S(2)}, u32[]{:S(2)}) collective-permute-start(f32[264,256]{1,0:T(8,128)} %get-tuple-element.32), channel_id=1, source_target_pairs={{0,2},{1,3},{2,0},{3,1},{4,6},{5,7},{6,4},{7,5},{8,10},{9,11},{10,... | collective-permute-start | bytes 811016 | tf_op jit(solution)/shard_map/ppermute | solution.py:259
  6.0 13.5 %collective-permute-start.5 = (f32[264,256]{1,0:T(8,128)}, f32[264,256]{1,0:T(8,128)}, u32[]{:S(2)}, u32[]{:S(2)}) collective-permute-start(f32[264,256]{1,0:T(8,128)} %get-tuple-element.33), channel_id=1, source_target_pairs={{0,3},{1,2},{2,1},{3,0},{4,7},{5,6},{6,5},{7,4},{8,11},{9,10},{10,... | collective-permute-start | bytes 811016 | tf_op jit(solution)/shard_map/ppermute | solution.py:259
  8.3 22.6 %copy-start.2 = (bf16[2,2,128,528]{3,2,1,0:T(8,128)(2,1)S(1)}, bf16[2,2,128,528]{3,2,1,0:T(8,128)(2,1)}, u32[]{:S(2)}) copy-start(bf16[2,2,128,528]{3,2,1,0:T(8,128)(2,1)} %constant.29.clone.refs_5_.refs_7_) | copy-start | bytes 1622020
  10.8 18.7 %collective-permute-start.1 = (f32[264,256]{1,0:T(8,128)}, f32[264,256]{1,0:T(8,128)S(1)}, u32[]{:S(2)}, u32[]{:S(2)}) collective-permute-start(f32[264,256]{1,0:T(8,128)} %get-tuple-element.28), channel_id=1, source_target_pairs={{0,1},{1,0},{2,3},{3,2},{4,5},{5,4},{6,7},{7,6},{8,9},{9,8},{10,11... | collective-permute-start | bytes 811016 | tf_op jit(solution)/shard_map/ppermute | solution.py:259
  11.0 18.5 %collective-permute-start.2 = (f32[264,256]{1,0:T(8,128)}, f32[264,256]{1,0:T(8,128)S(1)}, u32[]{:S(2)}, u32[]{:S(2)}) collective-permute-start(f32[264,256]{1,0:T(8,128)} %get-tuple-element.29), channel_id=1, source_target_pairs={{0,2},{1,3},{2,0},{3,1},{4,6},{5,7},{6,4},{7,5},{8,10},{9,11},{10,... | collective-permute-start | bytes 811016 | tf_op jit(solution)/shard_map/ppermute | solution.py:259
  12.3 18.6 %collective-permute-start.3 = (f32[264,256]{1,0:T(8,128)}, f32[264,256]{1,0:T(8,128)S(1)}, u32[]{:S(2)}, u32[]{:S(2)}) collective-permute-start(f32[264,256]{1,0:T(8,128)} %get-tuple-element.30), channel_id=1, source_target_pairs={{0,3},{1,2},{2,1},{3,0},{4,7},{5,6},{6,5},{7,4},{8,11},{9,10},{10,... | collective-permute-start | bytes 811016 | tf_op jit(solution)/shard_map/ppermute | solution.py:259
  19.5 0.9 %copy-start.5 = (f32[352,1]{1,0:T(8,128)S(1)}, f32[352,1]{1,0:T(8,128)}, u32[]{:S(2)}) copy-start(f32[352,1]{1,0:T(8,128)} %constant.31.clone.refs_6_.refs_7_.refs_9_) | copy-start | bytes 4228
  20.4 1.0 %copy-start.9 = (f32[264,256]{1,0:T(8,128)S(1)}, f32[264,256]{1,0:T(8,128)}, u32[]{:S(2)}) copy-start(f32[264,256]{1,0:T(8,128)} %copy-done.8) | copy-start | bytes 811012
  21.3 9.5 %copy-start.11 = (f32[264,256]{1,0:T(8,128)S(1)}, f32[264,256]{1,0:T(8,128)}, u32[]{:S(2)}) copy-start(f32[264,256]{1,0:T(8,128)} %copy-done.10) | copy-start | bytes 811012
  21.3 22.8 %copy-start.7 = (f32[352,1]{1,0:T(8,128)S(1)}, f32[352,1]{1,0:T(8,128)}, u32[]{:S(2)}) copy-start(f32[352,1]{1,0:T(8,128)} %constant.31.clone.refs_6_.refs_7_.refs_9_) | copy-start | bytes 4228
  23.3 13.0 %collective-permute-start.9 = (f32[352,256]{1,0:T(8,128)S(1)}, f32[352,256]{1,0:T(8,128)S(1)}, u32[]{:S(2)}, u32[]{:S(2)}) collective-permute-start(f32[352,256]{1,0:T(8,128)S(1)} %get-tuple-element.35.refs_11_.refs_2_), channel_id=1, source_target_pairs={{0,4},{4,8},{8,12},{12,16},{16,20},{20,24},{24,28},{1,5},{5,9},{9,... | collective-permute-start | bytes 1081352 | tf_op jit(solution)/shard_map/ppermute | solution.py:317
  26.4 17.8 %collective-permute-start.10 = (f32[352,256]{1,0:T(8,128)S(1)}, f32[352,256]{1,0:T(8,128)S(1)}, u32[]{:S(2)}, u32[]{:S(2)}) collective-permute-start(f32[352,256]{1,0:T(8,128)S(1)} %get-tuple-element.34.refs_10_.refs_1_), channel_id=1, source_target_pairs={{4,0},{8,4},{12,8},{16,12},{20,16},{24,20},{28,24},{5,1},{9,5},{13... | collective-permute-start | bytes 1081352 | tf_op jit(solution)/shard_map/ppermute | solution.py:318
  30.9 0.9 %copy-start.6 = (f32[352,1]{1,0:T(8,128)S(1)}, f32[352,1]{1,0:T(8,128)}, u32[]{:S(2)}) copy-start(f32[352,1]{1,0:T(8,128)} %constant.31.clone.refs_6_.refs_7_.refs_9_) | copy-start | bytes 4228
  33.5 13.8 %collective-permute-start.6 = (f32[256,256]{1,0:T(8,128)S(1)}, f32[256,256]{1,0:T(8,128)S(1)}, u32[]{:S(2)}, u32[]{:S(2)}) collective-permute-start(f32[256,256]{1,0:T(8,128)S(1)} %get-tuple-element.37), channel_id=1, source_target_pairs={{0,1},{1,0},{2,3},{3,2},{4,5},{5,4},{6,7},{7,6},{8,9},{9,8},{10,11... | collective-permute-start | bytes 786440 | tf_op jit(solution)/shard_map/ppermute | solution.py:259
  33.6 14.1 %collective-permute-start.7 = (f32[256,256]{1,0:T(8,128)S(1)}, f32[256,256]{1,0:T(8,128)S(1)}, u32[]{:S(2)}, u32[]{:S(2)}) collective-permute-start(f32[256,256]{1,0:T(8,128)S(1)} %get-tuple-element.38), channel_id=1, source_target_pairs={{0,2},{1,3},{2,0},{3,1},{4,6},{5,7},{6,4},{7,5},{8,10},{9,11},{10,... | collective-permute-start | bytes 786440 | tf_op jit(solution)/shard_map/ppermute | solution.py:259
  34.9 12.8 %collective-permute-start.8 = (f32[256,256]{1,0:T(8,128)S(1)}, f32[256,256]{1,0:T(8,128)S(1)}, u32[]{:S(2)}, u32[]{:S(2)}) collective-permute-start(f32[256,256]{1,0:T(8,128)S(1)} %get-tuple-element.39), channel_id=1, source_target_pairs={{0,3},{1,2},{2,1},{3,0},{4,7},{5,6},{6,5},{7,4},{8,11},{9,10},{10,... | collective-permute-start | bytes 786440 | tf_op jit(solution)/shard_map/ppermute | solution.py:259
  45.5 2.2 %collective-permute-start.11 = (f32[256,256]{1,0:T(8,128)S(1)}, f32[256,256]{1,0:T(8,128)S(1)}, u32[]{:S(2)}, u32[]{:S(2)}) collective-permute-start(f32[256,256]{1,0:T(8,128)S(1)} %get-tuple-element.44), channel_id=1, source_target_pairs={{0,1},{1,0},{2,3},{3,2},{4,5},{5,4},{6,7},{7,6},{8,9},{9,8},{10,11... | collective-permute-start | bytes 786440 | tf_op jit(solution)/shard_map/ppermute | solution.py:259
  46.0 7.9 %collective-permute-start.12 = (f32[256,256]{1,0:T(8,128)S(1)}, f32[256,256]{1,0:T(8,128)S(1)}, u32[]{:S(2)}, u32[]{:S(2)}) collective-permute-start(f32[256,256]{1,0:T(8,128)S(1)} %get-tuple-element.45), channel_id=1, source_target_pairs={{0,2},{1,3},{2,0},{3,1},{4,6},{5,7},{6,4},{7,5},{8,10},{9,11},{10,... | collective-permute-start | bytes 786440 | tf_op jit(solution)/shard_map/ppermute | solution.py:259
  47.3 12.4 %collective-permute-start.13 = (f32[256,256]{1,0:T(8,128)S(1)}, f32[256,256]{1,0:T(8,128)S(1)}, u32[]{:S(2)}, u32[]{:S(2)}) collective-permute-start(f32[256,256]{1,0:T(8,128)S(1)} %get-tuple-element.46), channel_id=1, source_target_pairs={{0,3},{1,2},{2,1},{3,0},{4,7},{5,6},{6,5},{7,4},{8,11},{9,10},{10,... | collective-permute-start | bytes 786440 | tf_op jit(solution)/shard_map/ppermute | solution.py:259
  (2 other events, 1.4 us)

commit v7 on v6

v7 whole, which is shorter than its diff:
```python
import functools

import jax
import jax.numpy as jnp
import ml_dtypes
import numpy as np
from jax import lax
from jax.experimental import pallas as pl
from jax.experimental.pallas import tpu as pltpu
from jax.sharding import PartitionSpec as P

PENALTY = 12.0
LANES = 128
VMEM = pl.BlockSpec(memory_space=pltpu.VMEM)
ANY = pl.BlockSpec(memory_space=pl.ANY)
PARAMS = pltpu.CompilerParams(vmem_limit_bytes=24 * 1024 * 1024)
LONG = pl.CostEstimate(flops=0, bytes_accessed=200_000_000, transcendentals=0)
SHORT = pl.CostEstimate(flops=0, bytes_accessed=1024, transcendentals=0)
SPLIT = 4
HEAD_LIMIT = 24


def split(values):
    high = values.astype(ml_dtypes.bfloat16)
    low = (values - high.astype(np.float64)).astype(ml_dtypes.bfloat16)
    return high, low


def tables(length, cells):
    half = length // 2
    points = np.arange(half)
    groups = []
    for parity in (0, 1):
        kept = [k for k in range(length // 2 + 1) if 3 * k <= length and k % 2 == parity]
        modes = [(k, False) for k in kept] + [(k, True) for k in kept if 0 < k < length // 2]
        groups.append(modes)
    padded = -(-max(len(modes) for modes in groups) // 16) * 16
    forward = np.zeros((2, padded, half))
    inverse = np.zeros((2, half, padded))
    fluid = np.zeros((2 * padded, 1))
    solid = np.zeros((2 * padded, 1))
    for parity, modes in enumerate(groups):
        for at, (k, sine) in enumerate(modes):
            angles = (points * k % length) * (2.0 * np.pi / length)
            wave = np.sin(angles) if sine else np.cos(angles)
            weight = 1.0 if k in (0, length // 2) else 2.0
            eigen = 2.0 - 2.0 * np.cos(2.0 * np.pi * k / length)
            forward[parity, at] = wave
            inverse[parity, :, at] = wave * weight / length
            fluid[parity * padded + at] = 1.0 / (4.0 + eigen)
            solid[parity * padded + at] = 1.0 / (4.0 + eigen + PENALTY)
    columns = np.zeros((8, -(-2 * padded // LANES) * LANES), np.float32)
    columns[0, : 2 * padded] = fluid[:, 0]
    columns[1, : 2 * padded] = solid[:, 0]
    blocks = half // cells
    high, low = split(forward.reshape(2, padded, blocks, cells).transpose(0, 2, 1, 3))
    forward = np.concatenate([high, low, high], axis=3)
    high, low = split(inverse.reshape(2, blocks, cells, padded))
    inverse = np.concatenate([high, low, high], axis=3)
    return forward, inverse, columns


def thirds(values, axis):
    high = values.astype(jnp.bfloat16)
    low = (values - high.astype(jnp.float32)).astype(jnp.bfloat16)
    return jnp.concatenate([high, high, low], axis=axis)


def pack_kernel(jobs, row_count, cells, earlier, x_ref, *refs):
    outs, (held, arrived) = refs[earlier:-2], refs[-2:]
    me = lax.axis_index("span")
    lines = x_ref.shape[1]
    all_tiles = lines // row_count
    own_tiles = all_tiles // lax.axis_size("span")
    pitch = held.shape[0] // cells
    some = cells // SPLIT
    copies = [
        pltpu.make_async_copy(
            x_ref.at[pl.ds(part * some, some)],
            held.reshape(cells, pitch, LANES).at[pl.ds(part * some, some), pl.ds(0, lines)],
            arrived.at[part],
        )
        for part in range(SPLIT)
    ]
    for copy in copies:
        copy.start()
    lane = lax.broadcasted_iota(jnp.int32, (some, LANES), 1)
    sides = []
    for part, copy in enumerate(copies):
        copy.wait()
        beside = jnp.zeros((some, LANES), jnp.float32)

        def line(tile, row):
            return held[pl.ds(part * some * pitch + tile * row_count + row, some, stride=pitch), :]

        for job, (out, base, d, rows, offset, tiles) in enumerate(jobs):
            first = jnp.bitwise_xor(me, d) * own_tiles + offset
            for i, row in enumerate(rows):
                at = base + i * cells + part * some
                for tile in range(tiles):
                    outs[out][at : at + some, tile * LANES : (tile + 1) * LANES] = line(first + tile, row)
                before = jnp.maximum(first - 1, 0)
                after = jnp.minimum(first + tiles, all_tiles - 1)
                for side, (tile, source) in enumerate(((before, LANES - 1), (after, 0))):
                    at = job * 8 + i * 2 + side
                    beside = jnp.where(lane == at, pltpu.roll(line(tile, row), (at - source) % LANES, 1), beside)
        sides.append(beside)
    if cells < LANES:
        sides.append(jnp.zeros((LANES - cells, LANES), jnp.float32))
    turned = jnp.concatenate(sides, axis=0).T
    for job, (out, base, _, rows, _, tiles) in enumerate(jobs):
        at = base + len(rows) * cells
        outs[out][at : at + 8, :LANES] = turned[job * 8 : (job + 1) * 8]
        if tiles > 1:
            outs[out][at : at + 8, LANES:] = jnp.zeros((8, (tiles - 1) * LANES), jnp.float32)


def transform(rows, count, cells, blocks, forward_ref):
    me = lax.axis_index("span")
    half = count // 2
    spectra = []
    for i in range(rows + 1):
        parts = []
        for parity in (0, 1):
            total = None
            for d in range(half):
                table = forward_ref[parity, jnp.bitwise_and(jnp.bitwise_xor(me, d), half - 1)]
                if i < rows:
                    near = blocks[d][i * cells : (i + 1) * cells, :]
                    far = blocks[d + half][i * cells : (i + 1) * cells, :]
                else:
                    near = blocks[d][rows * cells :, :cells]
                    far = blocks[d + half][rows * cells :, :cells]
                value = near + far if parity == 0 else near - far
                if i < rows:
                    term = jnp.dot(table, thirds(value, 0), preferred_element_type=jnp.float32)
                else:
                    value = jnp.concatenate([value, jnp.zeros_like(value)], axis=0)
                    term = lax.dot_general(
                        table, thirds(value, 1), (((1,), (1,)), ((), ())), preferred_element_type=jnp.float32
                    )
                total = term if total is None else total + term
            parts.append(total)
        spectra.append(jnp.concatenate(parts, axis=0))
    return spectra[:-1], spectra[-1]


def inverse_rows(sweeps, count, cells, inverse_ref, outs):
    me = lax.axis_index("span")
    half = count // 2
    padded = sweeps[0].shape[0] // 2
    for i, sweep in enumerate(sweeps):
        even = thirds(sweep[:padded], 0)
        odd = thirds(sweep[padded:], 0)
        for d in range(half):
            place = jnp.bitwise_and(jnp.bitwise_xor(me, d), half - 1)
            first = jnp.dot(inverse_ref[0, place], even, preferred_element_type=jnp.float32)
            second = jnp.dot(inverse_ref[1, place], odd, preferred_element_type=jnp.float32)
            outs[d][i * cells : (i + 1) * cells, :] = first + second
            outs[d + half][i * cells : (i + 1) * cells, :] = first - second


def second_sweep(spectrum, one, above, below, sides, at, inverse_diagonal):
    width = one.shape[1]
    lane = lax.broadcasted_iota(jnp.int32, one.shape, 1)
    left = jnp.where(lane == 0, sides[:, at : at + 1], pltpu.roll(one, 1, 1))
    right = jnp.where(lane == width - 1, sides[:, at + 1 : at + 2], pltpu.roll(one, width - 1, 1))
    return (spectrum + above + below + left + right) * inverse_diagonal


def reciprocals(mask_ref, columns_ref, modes, rows, offset, width):
    turned = columns_ref[...].T
    fluid, solid = turned[:modes, 0:1], turned[:modes, 1:2]
    own = mask_ref.shape[1] // lax.axis_size("span")
    start = pl.multiple_of(lax.axis_index("span") * own + offset, LANES)
    last = mask_ref.shape[1] - LANES
    before = mask_ref[:, pl.ds(pl.multiple_of(jnp.maximum(start - LANES, 0), LANES), LANES)][:, LANES - 1 :]
    after = mask_ref[:, pl.ds(pl.multiple_of(jnp.minimum(start + width, last), LANES), LANES)][:, :1]
    before = jnp.where(start == 0, 2, before)
    after = jnp.where(start + width == mask_ref.shape[1], 2, after)
    lane = lax.broadcasted_iota(jnp.int32, (1, 16), 1)
    kinds = jnp.full((1, 16), 2, jnp.int32)
    diagonals = []
    for i, row in enumerate(rows):
        kinds = jnp.where(lane == 2 * i, before[row : row + 1], kinds)
        kinds = jnp.where(lane == 2 * i + 1, after[row : row + 1], kinds)
        mask = mask_ref[row : row + 1, pl.ds(start, width)]
        diagonals.append(jnp.where(mask != 0, solid, fluid))
    return diagonals, jnp.where(kinds == 0, fluid, jnp.where(kinds == 1, solid, 0.0))


def views(refs, places, size):
    return [ref.at[base : base + size] for ref, base in zip(refs, places)]


def edge_kernel(rows, count, cells, *refs):
    blocks, (forward_ref, columns_ref, mask_ref) = refs[:count], refs[count : count + 3]
    spectrum_ref, first_ref, last_ref, sides_ref = refs[count + 3 :]
    spectra, sides = transform(len(rows), count, cells, blocks, forward_ref)
    modes, width = spectra[0].shape
    diagonals, beside = reciprocals(mask_ref, columns_ref, modes, rows, 0, width)
    for i, one_ref in enumerate((first_ref, last_ref)):
        spectrum_ref[i] = spectra[i]
        one_ref[...] = spectra[i] * diagonals[i]
    sides_ref[...] = sides * beside


def inner_kernel(rows, count, cells, offset, width, places, *refs):
    half = count // 2
    blocks = views(refs, places, len(rows) * cells + 8)
    forward_ref, inverse_ref, columns_ref, mask_ref, first_ref, last_ref = refs[count : count + 6]
    outs, far_ref, ones_ref = refs[-2 - half : -2], refs[-2], refs[-1]
    spectra, sides = transform(len(rows), count, cells, blocks, forward_ref)
    diagonals, beside = reciprocals(mask_ref, columns_ref, spectra[0].shape[0], rows, offset, width)
    sides = sides * beside
    ones = [spectrum * diagonal for spectrum, diagonal in zip(spectra, diagonals)]
    ones_ref[0] = ones[0]
    ones_ref[1] = ones[-1]
    around = [first_ref[:, offset : offset + width], *ones, last_ref[:, offset : offset + width]]
    sweeps = [
        second_sweep(spectra[i], ones[i], around[i], around[i + 2], sides, 2 * i, diagonals[i])
        for i in range(len(rows))
    ]
    size = len(rows) * cells
    inverse_rows(sweeps, count, cells, inverse_ref, [*outs, *views([far_ref] * half, range(0, half * size, size), size)])


def rim_kernel(rows, parts, count, cells, *refs):
    spectrum_ref, first_ref, last_ref, sides_ref, low_ref, high_ref, inverse_ref, columns_ref, mask_ref = refs[:9]
    ones, outs = refs[9 : 9 + parts], refs[-count:]
    modes, width = first_ref.shape
    diagonals, _ = reciprocals(mask_ref, columns_ref, modes, rows, 0, width)
    sides = sides_ref[...]
    inner = [jnp.concatenate([one[i] for one in ones], axis=1) for i in (0, 1)]
    sweeps = [
        second_sweep(spectrum_ref[0], first_ref[...], low_ref[...], inner[0], sides, 0, diagonals[0]),
        second_sweep(spectrum_ref[1], last_ref[...], inner[1], high_ref[...], sides, 2, diagonals[1]),
    ]
    inverse_rows(sweeps, count, cells, inverse_ref, outs)


def unpack_kernel(pieces, row_count, cells, *refs):
    me = lax.axis_index("span")
    blocks, (out_ref, held, done) = refs[:-3], refs[-3:]
    pitch = held.shape[0] // cells
    lines = out_ref.shape[1]
    own_tiles = lines // row_count // lax.axis_size("span")
    some = cells // SPLIT
    copies = []
    for part in range(SPLIT):
        for block, (d, base, rows, offset, tiles) in zip(blocks, pieces):
            first = jnp.bitwise_xor(me, d) * own_tiles + offset
            for i, row in enumerate(rows):
                line = base + i * cells + part * some
                for tile in range(tiles):
                    at = part * some * pitch + (first + tile) * row_count + row
                    held[pl.ds(at, some, stride=pitch), :] = block[line : line + some, tile * LANES : (tile + 1) * LANES]
        copies.append(
            pltpu.make_async_copy(
                held.reshape(cells, pitch, LANES).at[pl.ds(part * some, some), pl.ds(0, lines)],
                out_ref.at[pl.ds(part * some, some)],
                done.at[part],
            )
        )
        copies[-1].start()
    for copy in copies:
        copy.wait()


def call(kernel, outs, *args, cost=LONG, earlier=()):
    shapes = [jax.ShapeDtypeStruct(shape, jnp.float32) for shape in outs]
    return pl.pallas_call(
        kernel,
        out_shape=shapes,
        in_specs=[VMEM] * len(args) + [ANY] * len(earlier),
        out_specs=[VMEM] * len(outs),
        compiler_params=PARAMS,
        cost_estimate=cost,
    )(*args, *earlier)


def swap(block, d):
    return lax.ppermute(block, "span", [(i, i ^ d) for i in range(lax.axis_size("span"))])


def local(pressure_source, solid_mask):
    count = lax.axis_size("span")
    half = count // 2
    plane_count = lax.axis_size("plane")
    cells, row_count, columns = pressure_source.shape
    width = columns // count
    tiles = width // LANES
    parts = 2 if tiles % 2 == 0 else 1
    part_tiles, part_width = tiles // parts, width // parts
    inner = tuple(range(1, row_count - 1))
    edges = (0, row_count - 1)
    near, far = range(1, half), range(half, count)
    forward, inverse, one_over = map(jnp.asarray, tables(cells * count, cells))
    modes = 2 * forward.shape[2]

    lines = columns // LANES * row_count
    source = pressure_source.reshape(cells, row_count, columns // LANES, LANES).transpose(0, 2, 1, 3)
    source = source.reshape(cells, lines, LANES)
    scratch = [pltpu.VMEM((cells * (lines + 8), LANES), jnp.float32), pltpu.SemaphoreType.DMA((SPLIT,))]

    def pack(jobs, shapes, limit, *earlier):
        return pl.pallas_call(
            functools.partial(pack_kernel, jobs, row_count, cells, len(earlier)),
            out_shape=[jax.ShapeDtypeStruct(shape, jnp.float32) for shape in shapes],
            in_specs=[ANY] * (1 + len(earlier)),
            out_specs=[VMEM] * len(shapes),
            scratch_shapes=scratch,
            compiler_params=pltpu.CompilerParams(vmem_limit_bytes=limit * 1024 * 1024),
            cost_estimate=LONG,
        )(source, *earlier)

    edge_size, size = len(edges) * cells + 8, len(inner) * cells + 8
    jobs = [(d - 1, 0, d, edges, 0, tiles) for d in range(1, count)]
    packed = pack(jobs, [(edge_size, width)] * (count - 1), HEAD_LIMIT)
    edge_blocks = [swap(block, d) for d, block in enumerate(packed, 1)]
    jobs, shapes = [(0, 0, 0, edges, 0, tiles)], [(edge_size, width)]

    def add(d, wanted):
        jobs.extend(
            (len(shapes), at * size, d, inner, part * part_tiles, part_tiles) for at, part in enumerate(wanted)
        )
        shapes.append((len(wanted) * size, part_width))

    for d in range(half):
        add(d, range(parts))
    for part in range(parts):
        for d in far:
            add(d, [part])
    packed = pack(jobs, shapes, 24, *edge_blocks[: half - 1])
    edge_blocks = [packed[0], *edge_blocks]
    near_blocks = [packed[1]] + [swap(packed[1 + d], d) for d in near]
    far_blocks = []
    for part in range(parts):
        mine = packed[1 + half * (part + 1) : 1 + half * (part + 2)]
        message = [mine[0]] + [swap(mine[d], d) for d in near]
        far_blocks.append(swap(jnp.concatenate(message), half))

    spectrum, first, last, sides = call(
        functools.partial(edge_kernel, edges, count, cells),
        [(2, modes, width), (modes, width), (modes, width), (modes, 16)],
        *edge_blocks, forward, one_over, solid_mask,
    )
    up = [(i, i + 1) for i in range(plane_count - 1)]
    down = [(i + 1, i) for i in range(plane_count - 1)]
    low = lax.ppermute(last, "plane", up)
    high = lax.ppermute(first, "plane", down)

    ones, made, arrived, pieces, earlier = [], [], [], [], ()
    size = len(inner) * cells
    for part in range(parts):
        blocks = [(block, part * (size + 8)) for block in near_blocks]
        blocks += [(far_blocks[part], e * (size + 8)) for e in range(half)]
        offset = part * part_width
        *outs, one = call(
            functools.partial(
                inner_kernel, inner, count, cells, offset, part_width, [base for _, base in blocks]
            ),
            [(size, part_width)] * half + [(half * size, part_width), (2, modes, part_width)],
            *[block for block, _ in blocks], forward, inverse, one_over, solid_mask, first, last,
            cost=SHORT, earlier=earlier,
        )
        ones.append(one)
        earlier = (one,)
        made.append(outs[:half])
        arrived.append(swap(outs[half], half))

    def place(part):
        return inner, part * part_tiles, part_tiles

    def onward(part, d):
        return arrived[part][d * size : (d + 1) * size]

    earlier = list(arrived[:-1])
    for part in range(parts):
        pieces += [(made[part][0], 0, 0, *place(part)), (arrived[part], half, 0, *place(part))]
        for d in near:
            if part < parts - 1:
                message = swap(jnp.concatenate([onward(part, d), made[part][d]]), d)
                pieces += [(message, half + d, 0, *place(part)), (message, d, size, *place(part))]
            else:
                earlier.append(swap(made[part][d], d))
                pieces += [(earlier[-1], d, 0, *place(part))]
                pieces += [(swap(onward(part, d), d), half + d, 0, *place(part))]
    outs = call(
        functools.partial(rim_kernel, edges, parts, count, cells),
        [(len(edges) * cells, width)] * count,
        spectrum, first, last, sides, low, high, inverse, one_over, solid_mask, *ones, earlier=tuple(earlier),
    )
    pieces.append((outs[0], 0, 0, edges, 0, tiles))
    pieces += [(swap(outs[d], d), d, 0, edges, 0, tiles) for d in (*far, *near)]
    result = pl.pallas_call(
        functools.partial(unpack_kernel, [piece[1:] for piece in pieces], row_count, cells),
        out_shape=jax.ShapeDtypeStruct((cells, lines, LANES), jnp.float32),
        in_specs=[VMEM] * len(pieces),
        out_specs=ANY,
        scratch_shapes=scratch,
        compiler_params=PARAMS,
        cost_estimate=LONG,
    )(*[piece[0] for piece in pieces])
    result = result.reshape(cells, columns // LANES, row_count, LANES).transpose(0, 2, 1, 3)
    return result.reshape(cells, row_count, columns)


def solution(mesh):
    placed = (P("span", "plane", None), P("plane", None))
    return jax.shard_map(
        local, mesh=mesh, in_specs=placed, out_specs=P("span", "plane", None), check_vma=False
    )
```

time: 61.5 us -> 59.7 us (0.971)
  local copies, waits for them, and re-layouts: 8.31 us -> 1.64 us
  waiting for transfers between devices: 27.4 us -> 31 us
  starting transfers between devices: 15.1 us -> 17.7 us
  Pallas kernels: 9.97 us -> 8.93 us
    ppermute x12 -> x16, waiting for transfers between devices: 19 us -> 23.5 us  [swap(): lax.ppermute(block, 'span', [(i, i ^ d) for i in range(lax.axis_size('spa...]
    unnamed x24 -> x10, local copies, waits for them, and re-layouts: 5.81 us -> 1.62 us
    ppermute x12 -> x16, starting transfers between devices: 8.88 us -> 11.6 us  [swap(): lax.ppermute(block, 'span', [(i, i ^ d) for i in range(lax.axis_size('spa...]
    pallas_call x6 -> x7, Pallas kernels: 9.97 us -> 8.93 us  [the longest x4 5.35 us: call(): pl.pallas_call(kernel, out_shape=shapes, in_specs=[VMEM] * len(args) + [A...]
    slice x1 -> x2, local copies, waits for them, and re-layouts: 0.84 us -> 0.02 us  [onward(): return arrived[part][d * size:(d + 1) * size]]
    concatenate x1 -> x0, local copies, waits for them, and re-layouts: 0.82 us -> none  [local(): framed = jnp.concatenate([outside, solid_mask, outside], axis=1)]
    another operation x2 -> x0, local copies, waits for them, and re-layouts: 0.76 us -> none  [the longest x1 0.76 us: picked(): return (jnp.stack([mask[row] for row in rows]), kinds[None, :])]
  transfers between devices with their start and end apart: 14 -> 18, of which waited for: 6 -> 8; matrix products, arithmetic and copies ran while one was open for 4% -> 0% of each run, Pallas kernels for 11% -> 9%
where the time goes in v7:
time: 59.7 us; the launch traced here: 59.5 us
  waiting for transfers between devices  31 us (52%)
  starting transfers between devices  17.7 us (30%)
  Pallas kernels  8.93 us (15%)
  local copies, waits for them, and re-layouts  1.64 us (3%)
    ppermute x16, waiting for transfers between devices, swap(): lax.ppermute(block, 'span', [(i, i ^ d) for i in range(lax.axis_size('spa...  23.5 us
    ppermute x16, starting transfers between devices, swap(): lax.ppermute(block, 'span', [(i, i ^ d) for i in range(lax.axis_size('spa...  11.6 us
    ppermute x1, waiting for transfers between devices, local(): high = lax.ppermute(first, 'plane', down)  7.43 us
    pallas_call x4, Pallas kernels, call(): pl.pallas_call(kernel, out_shape=shapes, in_specs=[VMEM] * len(args) + [A...  5.35 us
    ppermute x1, starting transfers between devices, local(): low = lax.ppermute(last, 'plane', up)  3.12 us
    ppermute x1, starting transfers between devices, local(): high = lax.ppermute(first, 'plane', down)  3.06 us
    pallas_call x2, Pallas kernels, pack(): pl.pallas_call(functools.partial(pack_kernel, jobs, row_count, cells, len...  2.15 us
    unnamed x10, local copies, waits for them, and re-layouts  1.62 us
  transfers between devices with their start and end apart: 18, of which 8 were waited for; matrix products, arithmetic and copies ran while one was open for 0% of the time, Pallas kernels for 9%

profile of v7, /device:TPU:25, one launch (start us, length us, event | category | flops | bytes accessed | tf_op | source)
XLA Modules:
  0.0 59.5 jit_solution(9496136766357692102)
XLA Ops:
  0.0 1.6 %copy-done = f32[128,4,1024]{2,1,0:T(4,128)S(1)} copy-done((f32[128,4,1024]{2,1,0:T(4,128)S(1)}, f32[128,4,1024]{2,1,0:T(4,128)}, u32[]{:S(2)}) %copy-start) | copy-done | bytes 2097176
  1.6 0.8 %shard_map.55 = (f32[264,256]{1,0:T(8,128)S(1)}, f32[264,256]{1,0:T(8,128)S(1)}, f32[264,256]{1,0:T(8,128)S(1)}) custom-call(f32[128,32,128]{2,1,0:T(8,128)S(1)} %bitcast.10), custom_call_target="tpu_custom_call" | custom-call | bytes 200000000 | tf_op jit(solution)/shard_map/pallas_call | solution.py:307
  3.2 1.2 %collective-permute-done.refs_0_.refs_1_ = f32[264,256]{1,0:T(8,128)S(1)} collective-permute-done((f32[264,256]{1,0:T(8,128)S(1)}, f32[264,256]{1,0:T(8,128)S(1)}, u32[]{:S(2)}, u32[]{:S(2)}) %collective-permute-start) | collective-permute-done | bytes 270368 | tf_op jit(solution)/shard_map/ppermute | solution.py:283
  4.4 1.3 %shard_map.56 = (f32[264,256]{1,0:T(8,128)S(1)}, f32[528,128]{1,0:T(8,128)S(1)}, f32[528,128]{1,0:T(8,128)S(1)}, f32[264,128]{1,0:T(8,128)S(1)}, f32[264,128]{1,...) custom-call(f32[128,32,128]{2,1,0:T(8,128)S(1)} %bitcast.11, ...), custom_call_target="tpu_custom_call" | custom-call | bytes 200000000 | tf_op jit(solution)/shard_map/pallas_call | solution.py:307
  6.3 1.2 %collective-permute-start.4 = (f32[264,256]{1,0:T(8,128)S(1)}, f32[264,256]{1,0:T(8,128)S(1)}, u32[]{:S(2)}, u32[]{:S(2)}) collective-permute-start(f32[264,256]{1,0:T(8,128)S(1)} %get-tuple-element.37), channel_id=1, source_target_pairs={{0,2},{1,3},{2,0},{3,1},{4,6},{5,7},{6,4},{7,5},{8,10},{9,11},{10,... | collective-permute-start | bytes 811016 | tf_op jit(solution)/shard_map/ppermute | solution.py:283
  8.3 1.3 %collective-permute-start.3 = (f32[528,128]{1,0:T(8,128)S(1)}, f32[528,128]{1,0:T(8,128)S(1)}, u32[]{:S(2)}, u32[]{:S(2)}) collective-permute-start(f32[528,128]{1,0:T(8,128)S(1)} %pad_maximum_fusion), channel_id=1, source_target_pairs={{0,2},{1,3},{2,0},{3,1},{4,6},{5,7},{6,4},{7,5},{8,10},{9,11},{10,... | collective-permute-start | bytes 811016 | tf_op jit(solution)/shard_map/ppermute | solution.py:283
  10.0 4.0 %collective-permute-done.4.refs_2_ = f32[264,256]{1,0:T(8,128)S(1)} collective-permute-done((f32[264,256]{1,0:T(8,128)S(1)}, f32[264,256]{1,0:T(8,128)S(1)}, u32[]{:S(2)}, u32[]{:S(2)}) %collective-permute-start.4) | collective-permute-done | bytes 270368 | tf_op jit(solution)/shard_map/ppermute | solution.py:283
  14.0 7.1 %collective-permute-done.5.refs_3_ = f32[264,256]{1,0:T(8,128)S(1)} collective-permute-done((f32[264,256]{1,0:T(8,128)S(1)}, f32[264,256]{1,0:T(8,128)S(1)}, u32[]{:S(2)}, u32[]{:S(2)}) %collective-permute-start.5) | collective-permute-done | bytes 270368 | tf_op jit(solution)/shard_map/ppermute | solution.py:283
  21.1 0.8 %shard_map.57 = (f32[2,352,256]{2,1,0:T(8,128)S(1)}, f32[352,256]{1,0:T(8,128)S(1)}, f32[352,256]{1,0:T(8,128)S(1)}, f32[352,16]{1,0:T(8,128)S(1)}) custom-call(f32[264,256]{1,0:T(8,128)S(1)} %get-tuple-element.36.refs_0_, f32[264,256]{1,0:T(8,128)S(1)} %collective-permute-done.refs_0_.refs_1_, f32[264,256]{1,0:T(8,128)S(1)} %collective-permute-done.4.refs_2_, ...), custom_call_target="tpu_custom_call" | custom-call | bytes 200000000 | tf_op jit(solution)/shard_map/pallas_call | solution.py:272
  22.0 3.1 %collective-permute-start.13 = (f32[352,256]{1,0:T(8,128)S(1)}, f32[352,256]{1,0:T(8,128)S(1)}, u32[]{:S(2)}, u32[]{:S(2)}) collective-permute-start(f32[352,256]{1,0:T(8,128)S(1)} %get-tuple-element.40.refs_9_.refs_2_), channel_id=1, source_target_pairs={{0,4},{4,8},{8,12},{12,16},{16,20},{20,24},{24,28},{1,5},{5,9},{9,... | collective-permute-start | bytes 1081352 | tf_op jit(solution)/shard_map/ppermute | solution.py:350
  25.1 3.1 %collective-permute-start.14 = (f32[352,256]{1,0:T(8,128)S(1)}, f32[352,256]{1,0:T(8,128)S(1)}, u32[]{:S(2)}, u32[]{:S(2)}) collective-permute-start(f32[352,256]{1,0:T(8,128)S(1)} %get-tuple-element.39.refs_8_.refs_1_), channel_id=1, source_target_pairs={{4,0},{8,4},{12,8},{16,12},{20,16},{24,20},{28,24},{5,1},{9,5},{13... | collective-permute-start | bytes 1081352 | tf_op jit(solution)/shard_map/ppermute | solution.py:351
  28.2 1.5 %shard_map.58 = (f32[256,128]{1,0:T(8,128)S(1)}, f32[256,128]{1,0:T(8,128)S(1)}, f32[512,128]{1,0:T(8,128)S(1)}, f32[2,352,128]{2,1,0:T(8,128)S(1)}) custom-call(f32[528,128]{1,0:T(8,128)S(1)} %get-tuple-element.32.refs_0_, f32[528,128]{1,0:T(8,128)S(1)} %collective-permute-done.1.refs_1_, f32[528,128]{1,0:T(8,128)S(1)} %collective-permute-done.3.refs_2_.refs_3_, ...), custom_call_target="tpu_custom_call" | custom-call | bytes 1024 | tf_op jit(solution)/shard_map/pallas_call | solution.py:272
  29.7 1.3 %collective-permute-start.6 = (f32[512,128]{1,0:T(8,128)S(1)}, f32[512,128]{1,0:T(8,128)S(1)}, u32[]{:S(2)}, u32[]{:S(2)}) collective-permute-start(f32[512,128]{1,0:T(8,128)S(1)} %get-tuple-element.42), channel_id=1, source_target_pairs={{0,2},{1,3},{2,0},{3,1},{4,6},{5,7},{6,4},{7,5},{8,10},{9,11},{10,... | collective-permute-start | bytes 786440 | tf_op jit(solution)/shard_map/ppermute | solution.py:283
  31.4 1.5 %shard_map.59 = (f32[256,128]{1,0:T(8,128)S(1)}, f32[256,128]{1,0:T(8,128)S(1)}, f32[512,128]{1,0:T(8,128)S(1)}, f32[2,352,128]{2,1,0:T(8,128)S(1)}) custom-call(f32[528,128]{1,0:T(8,128)S(1)} %get-tuple-element.32.refs_0_, f32[528,128]{1,0:T(8,128)S(1)} %collective-permute-done.1.refs_1_, f32[528,128]{1,0:T(8,128)S(1)} %collective-permute-done.9.refs_2_.refs_3_, ...), custom_call_target="tpu_custom_call" | custom-call | bytes 1024 | tf_op jit(solution)/shard_map/pallas_call | solution.py:272
  32.9 1.3 %collective-permute-start.11 = (f32[256,128]{1,0:T(8,128)S(1)}, f32[256,128]{1,0:T(8,128)S(1)}, u32[]{:S(2)}, u32[]{:S(2)}) collective-permute-start(f32[256,128]{1,0:T(8,128)S(1)} %get-tuple-element.49), channel_id=1, source_target_pairs={{0,1},{1,0},{2,3},{3,2},{4,5},{5,4},{6,7},{7,6},{8,9},{9,8},{10,11... | collective-permute-start | bytes 393224 | tf_op jit(solution)/shard_map/ppermute | solution.py:283
  34.2 1.3 %collective-permute-start.10 = (f32[512,128]{1,0:T(8,128)S(1)}, f32[512,128]{1,0:T(8,128)S(1)}, u32[]{:S(2)}, u32[]{:S(2)}) collective-permute-start(f32[512,128]{1,0:T(8,128)S(1)} %get-tuple-element.48), channel_id=1, source_target_pairs={{0,2},{1,3},{2,0},{3,1},{4,6},{5,7},{6,4},{7,5},{8,10},{9,11},{10,... | collective-permute-start | bytes 786440 | tf_op jit(solution)/shard_map/ppermute | solution.py:283
  35.4 7.4 %collective-permute-done.14.refs_5_ = f32[352,256]{1,0:T(8,128)S(1)} collective-permute-done((f32[352,256]{1,0:T(8,128)S(1)}, f32[352,256]{1,0:T(8,128)S(1)}, u32[]{:S(2)}, u32[]{:S(2)}) %collective-permute-start.14) | collective-permute-done | bytes 360480 | tf_op jit(solution)/shard_map/ppermute | solution.py:351
  42.9 1.4 %shard_map.60 = (f32[256,256]{1,0:T(8,128)S(1)}, f32[256,256]{1,0:T(8,128)S(1)}, f32[256,256]{1,0:T(8,128)S(1)}, f32[256,256]{1,0:T(8,128)S(1)}) custom-call(f32[2,352,256]{2,1,0:T(8,128)S(1)} %get-tuple-element.50.refs_0_, f32[352,256]{1,0:T(8,128)S(1)} %get-tuple-element.39.refs_8_.refs_1_, f32[352,256]{1,0:T(8,128)S(1)} %get-tuple-element.40.refs_9_.refs_2_, ...), custom_call_target="tpu_custom_call" | custom-call | bytes 200000000 | tf_op jit(solution)/shard_map/pallas_call | solution.py:272
  44.3 0.9 %collective-permute-start.15 = (f32[256,256]{1,0:T(8,128)S(1)}, f32[256,256]{1,0:T(8,128)S(1)}, u32[]{:S(2)}, u32[]{:S(2)}) collective-permute-start(f32[256,256]{1,0:T(8,128)S(1)} %get-tuple-element.54), channel_id=1, source_target_pairs={{0,2},{1,3},{2,0},{3,1},{4,6},{5,7},{6,4},{7,5},{8,10},{9,11},{10,... | collective-permute-start | bytes 786440 | tf_op jit(solution)/shard_map/ppermute | solution.py:283
  45.2 1.3 %collective-permute-start.16 = (f32[256,256]{1,0:T(8,128)S(1)}, f32[256,256]{1,0:T(8,128)S(1)}, u32[]{:S(2)}, u32[]{:S(2)}) collective-permute-start(f32[256,256]{1,0:T(8,128)S(1)} %get-tuple-element.55), channel_id=1, source_target_pairs={{0,3},{1,2},{2,1},{3,0},{4,7},{5,6},{6,5},{7,4},{8,11},{9,10},{10,... | collective-permute-start | bytes 786440 | tf_op jit(solution)/shard_map/ppermute | solution.py:283
  47.2 1.4 %collective-permute-done.12.refs_7_ = f32[256,128]{1,0:T(8,128)S(1)} collective-permute-done((f32[256,128]{1,0:T(8,128)S(1)}, f32[256,128]{1,0:T(8,128)S(1)}, u32[]{:S(2)}, u32[]{:S(2)}) %collective-permute-start.12) | collective-permute-done | bytes 131104 | tf_op jit(solution)/shard_map/ppermute | solution.py:283
  48.6 3.3 %collective-permute-done.15.refs_9_ = f32[256,256]{1,0:T(8,128)S(1)} collective-permute-done((f32[256,256]{1,0:T(8,128)S(1)}, f32[256,256]{1,0:T(8,128)S(1)}, u32[]{:S(2)}, u32[]{:S(2)}) %collective-permute-start.15) | collective-permute-done | bytes 262176 | tf_op jit(solution)/shard_map/ppermute | solution.py:283
  51.8 6.2 %collective-permute-done.16.refs_10_ = f32[256,256]{1,0:T(8,128)S(1)} collective-permute-done((f32[256,256]{1,0:T(8,128)S(1)}, f32[256,256]{1,0:T(8,128)S(1)}, u32[]{:S(2)}, u32[]{:S(2)}) %collective-permute-start.16) | collective-permute-done | bytes 262176 | tf_op jit(solution)/shard_map/ppermute | solution.py:283
  58.0 1.4 %shard_map.61 = f32[128,32,128]{2,1,0:T(8,128)} custom-call(f32[256,128]{1,0:T(8,128)S(1)} %get-tuple-element.41.refs_0_, f32[512,128]{1,0:T(8,128)S(1)} %collective-permute-done.6.refs_11_.refs_1_, f32[512,128]{1,0:T(8,128)S(1)} %collective-permute-done.7.refs_2_.refs_3_, f32[512,128]{1,0:T(8,128)S(1)} %collective-permute-done.7.refs_2_.refs_3_, ...), custom_call_target="tpu_custom_call" | custom-call | bytes 200000000 | tf_op jit(solution)/shard_map/pallas_call | solution.py:396
  (34 shorter events, 3.5 us)
Async XLA Ops:
  0.0 1.6 %copy-start = (f32[128,4,1024]{2,1,0:T(4,128)S(1)}, f32[128,4,1024]{2,1,0:T(4,128)}, u32[]{:S(2)}) copy-start(f32[128,4,1024]{2,1,0:T(4,128)} %param.5) | copy-start | bytes 6291460
  2.4 18.7 %copy-start.2 = (bf16[2,2,176,384]{3,2,1,0:T(8,128)(2,1)S(1)}, bf16[2,2,176,384]{3,2,1,0:T(8,128)(2,1)}, u32[]{:S(2)}) copy-start(bf16[2,2,176,384]{3,2,1,0:T(8,128)(2,1)} %constant.6.clone.refs_4_) | copy-start | bytes 1622020
  2.4 18.7 %copy-start.3 = (s32[4,1024]{1,0:T(4,128)S(1)}, s32[4,1024]{1,0:T(4,128)}, u32[]{:S(2)}) copy-start(s32[4,1024]{1,0:T(4,128)} %refs_8_.1) | copy-start | bytes 49156
  2.4 18.7 %copy-start.4 = (f32[8,384]{1,0:T(8,128)S(1)}, f32[8,384]{1,0:T(8,128)}, u32[]{:S(2)}) copy-start(f32[8,384]{1,0:T(8,128)} %constant.8.clone.refs_5_.refs_6_.refs_7_) | copy-start | bytes 36868
  2.5 25.7 %copy-start.1 = (bf16[2,2,128,528]{3,2,1,0:T(8,128)(2,1)S(1)}, bf16[2,2,128,528]{3,2,1,0:T(8,128)(2,1)}, u32[]{:S(2)}) copy-start(bf16[2,2,128,528]{3,2,1,0:T(8,128)(2,1)} %constant.7.clone.refs_5_.refs_6_) | copy-start | bytes 1622020
  2.5 1.9 %collective-permute-start = (f32[264,256]{1,0:T(8,128)S(1)}, f32[264,256]{1,0:T(8,128)S(1)}, u32[]{:S(2)}, u32[]{:S(2)}) collective-permute-start(f32[264,256]{1,0:T(8,128)S(1)} %get-tuple-element.31), channel_id=1, source_target_pairs={{0,1},{1,0},{2,3},{3,2},{4,5},{5,4},{6,7},{7,6},{8,9},{9,8},{10,11... | collective-permute-start | bytes 811016 | tf_op jit(solution)/shard_map/ppermute | solution.py:283
  5.7 2.6 %collective-permute-start.2 = (f32[264,128]{1,0:T(8,128)S(1)}, f32[264,128]{1,0:T(8,128)S(1)}, u32[]{:S(2)}, u32[]{:S(2)}) collective-permute-start(f32[264,128]{1,0:T(8,128)S(1)} %get-tuple-element.35), channel_id=1, source_target_pairs={{0,1},{1,0},{2,3},{3,2},{4,5},{5,4},{6,7},{7,6},{8,9},{9,8},{10,11... | collective-permute-start | bytes 405512 | tf_op jit(solution)/shard_map/ppermute | solution.py:283
  6.2 3.5 %collective-permute-start.8 = (f32[264,128]{1,0:T(8,128)S(1)}, f32[264,128]{1,0:T(8,128)S(1)}, u32[]{:S(2)}, u32[]{:S(2)}) collective-permute-start(f32[264,128]{1,0:T(8,128)S(1)} %get-tuple-element.45), channel_id=1, source_target_pairs={{0,1},{1,0},{2,3},{3,2},{4,5},{5,4},{6,7},{7,6},{8,9},{9,8},{10,11... | collective-permute-start | bytes 405512 | tf_op jit(solution)/shard_map/ppermute | solution.py:283
  6.3 7.7 %collective-permute-start.4 = (f32[264,256]{1,0:T(8,128)S(1)}, f32[264,256]{1,0:T(8,128)S(1)}, u32[]{:S(2)}, u32[]{:S(2)}) collective-permute-start(f32[264,256]{1,0:T(8,128)S(1)} %get-tuple-element.37), channel_id=1, source_target_pairs={{0,2},{1,3},{2,0},{3,1},{4,6},{5,7},{6,4},{7,5},{8,10},{9,11},{10,... | collective-permute-start | bytes 811016 | tf_op jit(solution)/shard_map/ppermute | solution.py:283
  7.5 13.6 %collective-permute-start.5 = (f32[264,256]{1,0:T(8,128)S(1)}, f32[264,256]{1,0:T(8,128)S(1)}, u32[]{:S(2)}, u32[]{:S(2)}) collective-permute-start(f32[264,256]{1,0:T(8,128)S(1)} %get-tuple-element.38), channel_id=1, source_target_pairs={{0,3},{1,2},{2,1},{3,0},{4,7},{5,6},{6,5},{7,4},{8,11},{9,10},{10,... | collective-permute-start | bytes 811016 | tf_op jit(solution)/shard_map/ppermute | solution.py:283
  8.3 19.8 %collective-permute-start.1 = (f32[528,128]{1,0:T(8,128)S(1)}, f32[528,128]{1,0:T(8,128)S(1)}, u32[]{:S(2)}, u32[]{:S(2)}) collective-permute-start(f32[528,128]{1,0:T(8,128)S(1)} %get-tuple-element.33), channel_id=1, source_target_pairs={{0,1},{1,0},{2,3},{3,2},{4,5},{5,4},{6,7},{7,6},{8,9},{9,8},{10,11... | collective-permute-start | bytes 811016 | tf_op jit(solution)/shard_map/ppermute | solution.py:283
  8.3 19.8 %collective-permute-start.3 = (f32[528,128]{1,0:T(8,128)S(1)}, f32[528,128]{1,0:T(8,128)S(1)}, u32[]{:S(2)}, u32[]{:S(2)}) collective-permute-start(f32[528,128]{1,0:T(8,128)S(1)} %pad_maximum_fusion), channel_id=1, source_target_pairs={{0,2},{1,3},{2,0},{3,1},{4,6},{5,7},{6,4},{7,5},{8,10},{9,11},{10,... | collective-permute-start | bytes 811016 | tf_op jit(solution)/shard_map/ppermute | solution.py:283
  9.7 21.7 %collective-permute-start.9 = (f32[528,128]{1,0:T(8,128)S(1)}, f32[528,128]{1,0:T(8,128)S(1)}, u32[]{:S(2)}, u32[]{:S(2)}) collective-permute-start(f32[528,128]{1,0:T(8,128)S(1)} %pad_maximum_fusion.1), channel_id=1, source_target_pairs={{0,2},{1,3},{2,0},{3,1},{4,6},{5,7},{6,4},{7,5},{8,10},{9,11},{10,... | collective-permute-start | bytes 811016 | tf_op jit(solution)/shard_map/ppermute | solution.py:283
  22.0 13.5 %collective-permute-start.13 = (f32[352,256]{1,0:T(8,128)S(1)}, f32[352,256]{1,0:T(8,128)S(1)}, u32[]{:S(2)}, u32[]{:S(2)}) collective-permute-start(f32[352,256]{1,0:T(8,128)S(1)} %get-tuple-element.40.refs_9_.refs_2_), channel_id=1, source_target_pairs={{0,4},{4,8},{8,12},{12,16},{16,20},{20,24},{24,28},{1,5},{5,9},{9,... | collective-permute-start | bytes 1081352 | tf_op jit(solution)/shard_map/ppermute | solution.py:350
  25.1 17.8 %collective-permute-start.14 = (f32[352,256]{1,0:T(8,128)S(1)}, f32[352,256]{1,0:T(8,128)S(1)}, u32[]{:S(2)}, u32[]{:S(2)}) collective-permute-start(f32[352,256]{1,0:T(8,128)S(1)} %get-tuple-element.39.refs_8_.refs_1_), channel_id=1, source_target_pairs={{4,0},{8,4},{12,8},{16,12},{20,16},{24,20},{28,24},{5,1},{9,5},{13... | collective-permute-start | bytes 1081352 | tf_op jit(solution)/shard_map/ppermute | solution.py:351
  29.7 13.1 %collective-permute-start.6 = (f32[512,128]{1,0:T(8,128)S(1)}, f32[512,128]{1,0:T(8,128)S(1)}, u32[]{:S(2)}, u32[]{:S(2)}) collective-permute-start(f32[512,128]{1,0:T(8,128)S(1)} %get-tuple-element.42), channel_id=1, source_target_pairs={{0,2},{1,3},{2,0},{3,1},{4,6},{5,7},{6,4},{7,5},{8,10},{9,11},{10,... | collective-permute-start | bytes 786440 | tf_op jit(solution)/shard_map/ppermute | solution.py:283
  32.9 9.9 %collective-permute-start.11 = (f32[256,128]{1,0:T(8,128)S(1)}, f32[256,128]{1,0:T(8,128)S(1)}, u32[]{:S(2)}, u32[]{:S(2)}) collective-permute-start(f32[256,128]{1,0:T(8,128)S(1)} %get-tuple-element.49), channel_id=1, source_target_pairs={{0,1},{1,0},{2,3},{3,2},{4,5},{5,4},{6,7},{7,6},{8,9},{9,8},{10,11... | collective-permute-start | bytes 393224 | tf_op jit(solution)/shard_map/ppermute | solution.py:283
  34.2 12.9 %collective-permute-start.10 = (f32[512,128]{1,0:T(8,128)S(1)}, f32[512,128]{1,0:T(8,128)S(1)}, u32[]{:S(2)}, u32[]{:S(2)}) collective-permute-start(f32[512,128]{1,0:T(8,128)S(1)} %get-tuple-element.48), channel_id=1, source_target_pairs={{0,2},{1,3},{2,0},{3,1},{4,6},{5,7},{6,4},{7,5},{8,10},{9,11},{10,... | collective-permute-start | bytes 786440 | tf_op jit(solution)/shard_map/ppermute | solution.py:283
  44.3 7.5 %collective-permute-start.15 = (f32[256,256]{1,0:T(8,128)S(1)}, f32[256,256]{1,0:T(8,128)S(1)}, u32[]{:S(2)}, u32[]{:S(2)}) collective-permute-start(f32[256,256]{1,0:T(8,128)S(1)} %get-tuple-element.54), channel_id=1, source_target_pairs={{0,2},{1,3},{2,0},{3,1},{4,6},{5,7},{6,4},{7,5},{8,10},{9,11},{10,... | collective-permute-start | bytes 786440 | tf_op jit(solution)/shard_map/ppermute | solution.py:283
  45.2 12.9 %collective-permute-start.16 = (f32[256,256]{1,0:T(8,128)S(1)}, f32[256,256]{1,0:T(8,128)S(1)}, u32[]{:S(2)}, u32[]{:S(2)}) collective-permute-start(f32[256,256]{1,0:T(8,128)S(1)} %get-tuple-element.55), channel_id=1, source_target_pairs={{0,3},{1,2},{2,1},{3,0},{4,7},{5,6},{6,5},{7,4},{8,11},{9,10},{10,... | collective-permute-start | bytes 786440 | tf_op jit(solution)/shard_map/ppermute | solution.py:283
  46.5 11.6 %collective-permute-start.17 = (f32[256,256]{1,0:T(8,128)S(1)}, f32[256,256]{1,0:T(8,128)S(1)}, u32[]{:S(2)}, u32[]{:S(2)}) collective-permute-start(f32[256,256]{1,0:T(8,128)S(1)} %get-tuple-element.56), channel_id=1, source_target_pairs={{0,1},{1,0},{2,3},{3,2},{4,5},{5,4},{6,7},{7,6},{8,9},{9,8},{10,11... | collective-permute-start | bytes 786440 | tf_op jit(solution)/shard_map/ppermute | solution.py:283
  46.5 11.5 %collective-permute-start.7 = (f32[512,128]{1,0:T(8,128)S(1)}, f32[512,128]{1,0:T(8,128)S(1)}, u32[]{:S(2)}, u32[]{:S(2)}) collective-permute-start(f32[512,128]{1,0:T(8,128)S(1)} %pad_maximum_fusion.2), channel_id=1, source_target_pairs={{0,1},{1,0},{2,3},{3,2},{4,5},{5,4},{6,7},{7,6},{8,9},{9,8},{10,11... | collective-permute-start | bytes 786440 | tf_op jit(solution)/shard_map/ppermute | solution.py:283
  47.1 1.5 %collective-permute-start.12 = (f32[256,128]{1,0:T(8,128)S(1)}, f32[256,128]{1,0:T(8,128)S(1)}, u32[]{:S(2)}, u32[]{:S(2)}) collective-permute-start(f32[256,128]{1,0:T(8,128)S(1)} %slice.9), channel_id=1, source_target_pairs={{0,1},{1,0},{2,3},{3,2},{4,5},{5,4},{6,7},{7,6},{8,9},{9,8},{10,11... | collective-permute-start | bytes 393224 | tf_op jit(solution)/shard_map/ppermute | solution.py:283

commit v8 on v7

--- a/solution.py
+++ b/solution.py
@@ -17,7 +17,6 @@
 LONG = pl.CostEstimate(flops=0, bytes_accessed=200_000_000, transcendentals=0)
 SHORT = pl.CostEstimate(flops=0, bytes_accessed=1024, transcendentals=0)
 SPLIT = 4
-HEAD_LIMIT = 24
 
 
 def split(values):
@@ -66,8 +65,8 @@
     return jnp.concatenate([high, high, low], axis=axis)
 
 
-def pack_kernel(jobs, row_count, cells, earlier, x_ref, *refs):
-    outs, (held, arrived) = refs[earlier:-2], refs[-2:]
+def pack_kernel(jobs, row_count, cells, x_ref, *refs):
+    outs, (held, arrived) = refs[:-2], refs[-2:]
     me = lax.axis_index("span")
     lines = x_ref.shape[1]
     all_tiles = lines // row_count
@@ -239,6 +238,16 @@
     inverse_rows(sweeps, count, cells, inverse_ref, outs)
 
 
+def join_kernel(groups, *refs):
+    refs, outs = refs[:-groups], refs[-groups:]
+    size = len(refs) // groups
+    for group, out_ref in enumerate(outs):
+        at = 0
+        for ref in refs[group * size : (group + 1) * size]:
+            out_ref[at : at + ref.shape[0], :] = ref[...]
+            at += ref.shape[0]
+
+
 def unpack_kernel(pieces, row_count, cells, *refs):
     me = lax.axis_index("span")
     blocks, (out_ref, held, done) = refs[:-3], refs[-3:]
@@ -279,6 +288,12 @@
     )(*args, *earlier)
 
 
+def join(*groups):
+    shapes = [(sum(block.shape[0] for block in group), group[0].shape[1]) for group in groups]
+    blocks = [block for group in groups for block in group]
+    return call(functools.partial(join_kernel, len(groups)), shapes, *blocks, cost=SHORT)
+
+
 def swap(block, d):
     return lax.ppermute(block, "span", [(i, i ^ d) for i in range(lax.axis_size("span"))])
 
@@ -303,22 +318,9 @@
     source = source.reshape(cells, lines, LANES)
     scratch = [pltpu.VMEM((cells * (lines + 8), LANES), jnp.float32), pltpu.SemaphoreType.DMA((SPLIT,))]
 
-    def pack(jobs, shapes, limit, *earlier):
-        return pl.pallas_call(
-            functools.partial(pack_kernel, jobs, row_count, cells, len(earlier)),
-            out_shape=[jax.ShapeDtypeStruct(shape, jnp.float32) for shape in shapes],
-            in_specs=[ANY] * (1 + len(earlier)),
-            out_specs=[VMEM] * len(shapes),
-            scratch_shapes=scratch,
-            compiler_params=pltpu.CompilerParams(vmem_limit_bytes=limit * 1024 * 1024),
-            cost_estimate=LONG,
-        )(source, *earlier)
-
     edge_size, size = len(edges) * cells + 8, len(inner) * cells + 8
-    jobs = [(d - 1, 0, d, edges, 0, tiles) for d in range(1, count)]
-    packed = pack(jobs, [(edge_size, width)] * (count - 1), HEAD_LIMIT)
-    edge_blocks = [swap(block, d) for d, block in enumerate(packed, 1)]
-    jobs, shapes = [(0, 0, 0, edges, 0, tiles)], [(edge_size, width)]
+    jobs = [(d, 0, d, edges, 0, tiles) for d in range(count)]
+    shapes = [(edge_size, width)] * count
 
     def add(d, wanted):
         jobs.extend(
@@ -331,14 +333,22 @@
     for part in range(parts):
         for d in far:
             add(d, [part])
-    packed = pack(jobs, shapes, 24, *edge_blocks[: half - 1])
-    edge_blocks = [packed[0], *edge_blocks]
-    near_blocks = [packed[1]] + [swap(packed[1 + d], d) for d in near]
-    far_blocks = []
+    packed = pl.pallas_call(
+        functools.partial(pack_kernel, jobs, row_count, cells),
+        out_shape=[jax.ShapeDtypeStruct(shape, jnp.float32) for shape in shapes],
+        in_specs=[ANY],
+        out_specs=[VMEM] * len(shapes),
+        scratch_shapes=scratch,
+        compiler_params=PARAMS,
+        cost_estimate=LONG,
+    )(source)
+    edge_blocks = [packed[0]] + [swap(packed[d], d) for d in range(1, count)]
+    near_blocks = [packed[count]] + [swap(packed[count + d], d) for d in near]
+    messages = []
     for part in range(parts):
-        mine = packed[1 + half * (part + 1) : 1 + half * (part + 2)]
-        message = [mine[0]] + [swap(mine[d], d) for d in near]
-        far_blocks.append(swap(jnp.concatenate(message), half))
+        mine = packed[count + half * (part + 1) : count + half * (part + 2)]
+        messages.append([mine[0]] + [swap(mine[d], d) for d in near])
+    far_blocks = [swap(message, half) for message in join(*messages)]
 
     spectrum, first, last, sides = call(
         functools.partial(edge_kernel, edges, count, cells),
@@ -380,7 +390,7 @@
         pieces += [(made[part][0], 0, 0, *place(part)), (arrived[part], half, 0, *place(part))]
         for d in near:
             if part < parts - 1:
-                message = swap(jnp.concatenate([onward(part, d), made[part][d]]), d)
+                message = swap(join([onward(part, d), made[part][d]])[0], d)
                 pieces += [(message, half + d, 0, *place(part)), (message, d, size, *place(part))]
             else:
                 earlier.append(swap(made[part][d], d))

time: 59.7 us -> 57.6 us (0.965)
  waiting for transfers between devices: 31 us -> 30 us
    ppermute x16, waiting for transfers between devices: 23.5 us -> 22.9 us  [swap(): lax.ppermute(block, 'span', [(i, i ^ d) for i in range(lax.axis_size('spa...]
    pallas_call x2 -> x1, Pallas kernels: 2.15 us -> 1.7 us  [local(): pl.pallas_call(functools.partial(pack_kernel, jobs, row_count, cells), ou...]
    pallas_call x4 -> x6, Pallas kernels: 5.35 us -> 5.36 us  [call(): pl.pallas_call(kernel, out_shape=shapes, in_specs=[VMEM] * len(args) + [A...]
  transfers between devices with their start and end apart: 18 -> 18, of which waited for: 8 -> 7; matrix products, arithmetic and copies ran while one was open for 0% -> 0% of each run, Pallas kernels for 9% -> 9%
where the time goes in v8:
time: 57.6 us; the launch traced here: 57.4 us
  waiting for transfers between devices  30 us (52%)
  starting transfers between devices  17.2 us (30%)
  Pallas kernels  8.5 us (15%)
  local copies, waits for them, and re-layouts  1.68 us (3%)
    ppermute x16, waiting for transfers between devices, swap(): lax.ppermute(block, 'span', [(i, i ^ d) for i in range(lax.axis_size('spa...  22.9 us
    ppermute x16, starting transfers between devices, swap(): lax.ppermute(block, 'span', [(i, i ^ d) for i in range(lax.axis_size('spa...  11 us
    ppermute x1, waiting for transfers between devices, local(): high = lax.ppermute(first, 'plane', down)  7.06 us
    pallas_call x6, Pallas kernels, call(): pl.pallas_call(kernel, out_shape=shapes, in_specs=[VMEM] * len(args) + [A...  5.36 us
    ppermute x1, starting transfers between devices, local(): low = lax.ppermute(last, 'plane', up)  3.12 us
    ppermute x1, starting transfers between devices, local(): high = lax.ppermute(first, 'plane', down)  3.07 us
    pallas_call x1, Pallas kernels, local(): pl.pallas_call(functools.partial(pack_kernel, jobs, row_count, cells), ou...  1.7 us
    unnamed x10, local copies, waits for them, and re-layouts  1.66 us
  transfers between devices with their start and end apart: 18, of which 7 were waited for; matrix products, arithmetic and copies ran while one was open for 0% of the time, Pallas kernels for 9%

profile of v8, /device:TPU:25, one launch (start us, length us, event | category | flops | bytes accessed | tf_op | source)
XLA Modules:
  0.0 57.4 jit_solution(17135369544215372561)
XLA Ops:
  0.0 1.6 %copy-done.2 = f32[128,4,1024]{2,1,0:T(4,128)S(1)} copy-done((f32[128,4,1024]{2,1,0:T(4,128)S(1)}, f32[128,4,1024]{2,1,0:T(4,128)}, u32[]{:S(2)}) %copy-start.2) | copy-done | bytes 2097176
  1.7 1.7 %shard_map.55 = (f32[264,256]{1,0:T(8,128)S(1)}, f32[264,256]{1,0:T(8,128)S(1)}, f32[264,256]{1,0:T(8,128)S(1)}, f32[264,256]{1,0:T(8,128)S(1)}, f32[528,128]{1,...) custom-call(f32[128,32,128]{2,1,0:T(8,128)S(1)} %bitcast.10), custom_call_target="tpu_custom_call" | custom-call | bytes 200000000 | tf_op jit(solution)/shard_map/pallas_call | solution.py:336
  3.4 0.7 %collective-permute-start.4 = (f32[264,256]{1,0:T(8,128)S(1)}, f32[264,256]{1,0:T(8,128)S(1)}, u32[]{:S(2)}, u32[]{:S(2)}) collective-permute-start(f32[264,256]{1,0:T(8,128)S(1)} %get-tuple-element.41), channel_id=1, source_target_pairs={{0,1},{1,0},{2,3},{3,2},{4,5},{5,4},{6,7},{7,6},{8,9},{9,8},{10,11... | collective-permute-start | bytes 811016 | tf_op jit(solution)/shard_map/ppermute | solution.py:298
  4.6 1.3 %collective-permute-start.5 = (f32[264,256]{1,0:T(8,128)S(1)}, f32[264,256]{1,0:T(8,128)S(1)}, u32[]{:S(2)}, u32[]{:S(2)}) collective-permute-start(f32[264,256]{1,0:T(8,128)S(1)} %get-tuple-element.42), channel_id=1, source_target_pairs={{0,2},{1,3},{2,0},{3,1},{4,6},{5,7},{6,4},{7,5},{8,10},{9,11},{10,... | collective-permute-start | bytes 811016 | tf_op jit(solution)/shard_map/ppermute | solution.py:298
  6.5 1.3 %collective-permute-start.3 = (f32[528,128]{1,0:T(8,128)S(1)}, f32[528,128]{1,0:T(8,128)S(1)}, u32[]{:S(2)}, u32[]{:S(2)}) collective-permute-start(f32[528,128]{1,0:T(8,128)S(1)} %get-tuple-element.39), channel_id=1, source_target_pairs={{0,2},{1,3},{2,0},{3,1},{4,6},{5,7},{6,4},{7,5},{8,10},{9,11},{10,... | collective-permute-start | bytes 811016 | tf_op jit(solution)/shard_map/ppermute | solution.py:298
  8.1 4.6 %collective-permute-done.5.refs_2_ = f32[264,256]{1,0:T(8,128)S(1)} collective-permute-done((f32[264,256]{1,0:T(8,128)S(1)}, f32[264,256]{1,0:T(8,128)S(1)}, u32[]{:S(2)}, u32[]{:S(2)}) %collective-permute-start.5) | collective-permute-done | bytes 270368 | tf_op jit(solution)/shard_map/ppermute | solution.py:298
  12.7 6.4 %collective-permute-done.6.refs_3_ = f32[264,256]{1,0:T(8,128)S(1)} collective-permute-done((f32[264,256]{1,0:T(8,128)S(1)}, f32[264,256]{1,0:T(8,128)S(1)}, u32[]{:S(2)}, u32[]{:S(2)}) %collective-permute-start.6) | collective-permute-done | bytes 270368 | tf_op jit(solution)/shard_map/ppermute | solution.py:298
  19.1 0.8 %shard_map.57 = (f32[2,352,256]{2,1,0:T(8,128)S(1)}, f32[352,256]{1,0:T(8,128)S(1)}, f32[352,256]{1,0:T(8,128)S(1)}, f32[352,16]{1,0:T(8,128)S(1)}) custom-call(f32[264,256]{1,0:T(8,128)S(1)} %get-tuple-element.40.refs_0_, f32[264,256]{1,0:T(8,128)S(1)} %collective-permute-done.4.refs_1_, f32[264,256]{1,0:T(8,128)S(1)} %collective-permute-done.5.refs_2_, ...), custom_call_target="tpu_custom_call" | custom-call | bytes 200000000 | tf_op jit(solution)/shard_map/pallas_call | solution.py:281
  19.9 3.1 %collective-permute-start.13 = (f32[352,256]{1,0:T(8,128)S(1)}, f32[352,256]{1,0:T(8,128)S(1)}, u32[]{:S(2)}, u32[]{:S(2)}) collective-permute-start(f32[352,256]{1,0:T(8,128)S(1)} %get-tuple-element.45.refs_9_.refs_2_), channel_id=1, source_target_pairs={{0,4},{4,8},{8,12},{12,16},{16,20},{20,24},{24,28},{1,5},{5,9},{9,... | collective-permute-start | bytes 1081352 | tf_op jit(solution)/shard_map/ppermute | solution.py:360
  23.0 3.1 %collective-permute-start.14 = (f32[352,256]{1,0:T(8,128)S(1)}, f32[352,256]{1,0:T(8,128)S(1)}, u32[]{:S(2)}, u32[]{:S(2)}) collective-permute-start(f32[352,256]{1,0:T(8,128)S(1)} %get-tuple-element.44.refs_8_.refs_1_), channel_id=1, source_target_pairs={{4,0},{8,4},{12,8},{16,12},{20,16},{24,20},{28,24},{5,1},{9,5},{13... | collective-permute-start | bytes 1081352 | tf_op jit(solution)/shard_map/ppermute | solution.py:361
  26.2 1.5 %shard_map.58 = (f32[256,128]{1,0:T(8,128)S(1)}, f32[256,128]{1,0:T(8,128)S(1)}, f32[512,128]{1,0:T(8,128)S(1)}, f32[2,352,128]{2,1,0:T(8,128)S(1)}) custom-call(f32[528,128]{1,0:T(8,128)S(1)} %get-tuple-element.33.refs_0_, f32[528,128]{1,0:T(8,128)S(1)} %collective-permute-done.refs_1_, f32[528,128]{1,0:T(8,128)S(1)} %collective-permute-done.3.refs_2_.refs_3_, ...), custom_call_target="tpu_custom_call" | custom-call | bytes 1024 | tf_op jit(solution)/shard_map/pallas_call | solution.py:281
  27.7 1.3 %collective-permute-start.7 = (f32[512,128]{1,0:T(8,128)S(1)}, f32[512,128]{1,0:T(8,128)S(1)}, u32[]{:S(2)}, u32[]{:S(2)}) collective-permute-start(f32[512,128]{1,0:T(8,128)S(1)} %get-tuple-element.47), channel_id=1, source_target_pairs={{0,2},{1,3},{2,0},{3,1},{4,6},{5,7},{6,4},{7,5},{8,10},{9,11},{10,... | collective-permute-start | bytes 786440 | tf_op jit(solution)/shard_map/ppermute | solution.py:298
  29.0 1.1 %collective-permute-done.9.refs_2_.refs_3_ = f32[528,128]{1,0:T(8,128)S(1)} collective-permute-done((f32[528,128]{1,0:T(8,128)S(1)}, f32[528,128]{1,0:T(8,128)S(1)}, u32[]{:S(2)}, u32[]{:S(2)}) %collective-permute-start.9) | collective-permute-done | bytes 270368 | tf_op jit(solution)/shard_map/ppermute | solution.py:298
  30.1 1.5 %shard_map.60 = (f32[256,128]{1,0:T(8,128)S(1)}, f32[256,128]{1,0:T(8,128)S(1)}, f32[512,128]{1,0:T(8,128)S(1)}, f32[2,352,128]{2,1,0:T(8,128)S(1)}) custom-call(f32[528,128]{1,0:T(8,128)S(1)} %get-tuple-element.33.refs_0_, f32[528,128]{1,0:T(8,128)S(1)} %collective-permute-done.refs_1_, f32[528,128]{1,0:T(8,128)S(1)} %collective-permute-done.9.refs_2_.refs_3_, ...), custom_call_target="tpu_custom_call" | custom-call | bytes 1024 | tf_op jit(solution)/shard_map/pallas_call | solution.py:281
  31.6 0.9 %collective-permute-start.11 = (f32[256,128]{1,0:T(8,128)S(1)}, f32[256,128]{1,0:T(8,128)S(1)}, u32[]{:S(2)}, u32[]{:S(2)}) collective-permute-start(f32[256,128]{1,0:T(8,128)S(1)} %get-tuple-element.53), channel_id=1, source_target_pairs={{0,1},{1,0},{2,3},{3,2},{4,5},{5,4},{6,7},{7,6},{8,9},{9,8},{10,11... | collective-permute-start | bytes 393224 | tf_op jit(solution)/shard_map/ppermute | solution.py:298
  32.5 1.3 %collective-permute-start.10 = (f32[512,128]{1,0:T(8,128)S(1)}, f32[512,128]{1,0:T(8,128)S(1)}, u32[]{:S(2)}, u32[]{:S(2)}) collective-permute-start(f32[512,128]{1,0:T(8,128)S(1)} %get-tuple-element.52), channel_id=1, source_target_pairs={{0,2},{1,3},{2,0},{3,1},{4,6},{5,7},{6,4},{7,5},{8,10},{9,11},{10,... | collective-permute-start | bytes 786440 | tf_op jit(solution)/shard_map/ppermute | solution.py:298
  33.8 7.1 %collective-permute-done.14.refs_5_ = f32[352,256]{1,0:T(8,128)S(1)} collective-permute-done((f32[352,256]{1,0:T(8,128)S(1)}, f32[352,256]{1,0:T(8,128)S(1)}, u32[]{:S(2)}, u32[]{:S(2)}) %collective-permute-start.14) | collective-permute-done | bytes 360480 | tf_op jit(solution)/shard_map/ppermute | solution.py:361
  40.8 1.4 %shard_map.61 = (f32[256,256]{1,0:T(8,128)S(1)}, f32[256,256]{1,0:T(8,128)S(1)}, f32[256,256]{1,0:T(8,128)S(1)}, f32[256,256]{1,0:T(8,128)S(1)}) custom-call(f32[2,352,256]{2,1,0:T(8,128)S(1)} %get-tuple-element.54.refs_0_, f32[352,256]{1,0:T(8,128)S(1)} %get-tuple-element.44.refs_8_.refs_1_, f32[352,256]{1,0:T(8,128)S(1)} %get-tuple-element.45.refs_9_.refs_2_, ...), custom_call_target="tpu_custom_call" | custom-call | bytes 200000000 | tf_op jit(solution)/shard_map/pallas_call | solution.py:281
  42.3 1.3 %collective-permute-start.15 = (f32[256,256]{1,0:T(8,128)S(1)}, f32[256,256]{1,0:T(8,128)S(1)}, u32[]{:S(2)}, u32[]{:S(2)}) collective-permute-start(f32[256,256]{1,0:T(8,128)S(1)} %get-tuple-element.58), channel_id=1, source_target_pairs={{0,2},{1,3},{2,0},{3,1},{4,6},{5,7},{6,4},{7,5},{8,10},{9,11},{10,... | collective-permute-start | bytes 786440 | tf_op jit(solution)/shard_map/ppermute | solution.py:298
  43.6 0.8 %collective-permute-start.16 = (f32[256,256]{1,0:T(8,128)S(1)}, f32[256,256]{1,0:T(8,128)S(1)}, u32[]{:S(2)}, u32[]{:S(2)}) collective-permute-start(f32[256,256]{1,0:T(8,128)S(1)} %get-tuple-element.59), channel_id=1, source_target_pairs={{0,3},{1,2},{2,1},{3,0},{4,7},{5,6},{6,5},{7,4},{8,11},{9,10},{10,... | collective-permute-start | bytes 786440 | tf_op jit(solution)/shard_map/ppermute | solution.py:298
  45.1 1.4 %collective-permute-done.12.refs_7_ = f32[256,128]{1,0:T(8,128)S(1)} collective-permute-done((f32[256,128]{1,0:T(8,128)S(1)}, f32[256,128]{1,0:T(8,128)S(1)}, u32[]{:S(2)}, u32[]{:S(2)}) %collective-permute-start.12) | collective-permute-done | bytes 131104 | tf_op jit(solution)/shard_map/ppermute | solution.py:298
  46.5 3.3 %collective-permute-done.15.refs_9_ = f32[256,256]{1,0:T(8,128)S(1)} collective-permute-done((f32[256,256]{1,0:T(8,128)S(1)}, f32[256,256]{1,0:T(8,128)S(1)}, u32[]{:S(2)}, u32[]{:S(2)}) %collective-permute-start.15) | collective-permute-done | bytes 262176 | tf_op jit(solution)/shard_map/ppermute | solution.py:298
  49.8 6.2 %collective-permute-done.16.refs_10_ = f32[256,256]{1,0:T(8,128)S(1)} collective-permute-done((f32[256,256]{1,0:T(8,128)S(1)}, f32[256,256]{1,0:T(8,128)S(1)}, u32[]{:S(2)}, u32[]{:S(2)}) %collective-permute-start.16) | collective-permute-done | bytes 262176 | tf_op jit(solution)/shard_map/ppermute | solution.py:298
  56.0 1.4 %shard_map.62 = f32[128,32,128]{2,1,0:T(8,128)} custom-call(f32[256,128]{1,0:T(8,128)S(1)} %get-tuple-element.46.refs_0_, f32[512,128]{1,0:T(8,128)S(1)} %collective-permute-done.7.refs_11_.refs_1_, f32[512,128]{1,0:T(8,128)S(1)} %collective-permute-done.8.refs_2_.refs_3_, f32[512,128]{1,0:T(8,128)S(1)} %collective-permute-done.8.refs_2_.refs_3_, ...), custom_call_target="tpu_custom_call" | custom-call | bytes 200000000 | tf_op jit(solution)/shard_map/pallas_call | solution.py:406
  (32 shorter events, 2.2 us)
Async XLA Ops:
  0.0 19.1 %copy-start.1 = (bf16[2,2,176,384]{3,2,1,0:T(8,128)(2,1)S(1)}, bf16[2,2,176,384]{3,2,1,0:T(8,128)(2,1)}, u32[]{:S(2)}) copy-start(bf16[2,2,176,384]{3,2,1,0:T(8,128)(2,1)} %constant.6.clone.refs_4_) | copy-start | bytes 1622020
  0.0 1.7 %copy-start.2 = (f32[128,4,1024]{2,1,0:T(4,128)S(1)}, f32[128,4,1024]{2,1,0:T(4,128)}, u32[]{:S(2)}) copy-start(f32[128,4,1024]{2,1,0:T(4,128)} %param.5) | copy-start | bytes 6291460
  1.7 17.4 %copy-start.3 = (s32[4,1024]{1,0:T(4,128)S(1)}, s32[4,1024]{1,0:T(4,128)}, u32[]{:S(2)}) copy-start(s32[4,1024]{1,0:T(4,128)} %refs_8_.1) | copy-start | bytes 49156
  1.7 17.4 %copy-start.4 = (f32[8,384]{1,0:T(8,128)S(1)}, f32[8,384]{1,0:T(8,128)}, u32[]{:S(2)}) copy-start(f32[8,384]{1,0:T(8,128)} %constant.8.clone.refs_5_.refs_6_.refs_7_) | copy-start | bytes 36868
  1.7 24.5 %copy-start = (bf16[2,2,128,528]{3,2,1,0:T(8,128)(2,1)S(1)}, bf16[2,2,128,528]{3,2,1,0:T(8,128)(2,1)}, u32[]{:S(2)}) copy-start(bf16[2,2,128,528]{3,2,1,0:T(8,128)(2,1)} %constant.7.clone.refs_5_.refs_6_) | copy-start | bytes 1622020
  3.4 4.5 %collective-permute-start.4 = (f32[264,256]{1,0:T(8,128)S(1)}, f32[264,256]{1,0:T(8,128)S(1)}, u32[]{:S(2)}, u32[]{:S(2)}) collective-permute-start(f32[264,256]{1,0:T(8,128)S(1)} %get-tuple-element.41), channel_id=1, source_target_pairs={{0,1},{1,0},{2,3},{3,2},{4,5},{5,4},{6,7},{7,6},{8,9},{9,8},{10,11... | collective-permute-start | bytes 811016 | tf_op jit(solution)/shard_map/ppermute | solution.py:298
  4.1 2.2 %collective-permute-start.1 = (f32[264,128]{1,0:T(8,128)S(1)}, f32[264,128]{1,0:T(8,128)S(1)}, u32[]{:S(2)}, u32[]{:S(2)}) collective-permute-start(f32[264,128]{1,0:T(8,128)S(1)} %get-tuple-element.36), channel_id=1, source_target_pairs={{0,1},{1,0},{2,3},{3,2},{4,5},{5,4},{6,7},{7,6},{8,9},{9,8},{10,11... | collective-permute-start | bytes 405512 | tf_op jit(solution)/shard_map/ppermute | solution.py:298
  4.2 2.3 %collective-permute-start.2 = (f32[264,128]{1,0:T(8,128)S(1)}, f32[264,128]{1,0:T(8,128)S(1)}, u32[]{:S(2)}, u32[]{:S(2)}) collective-permute-start(f32[264,128]{1,0:T(8,128)S(1)} %get-tuple-element.38), channel_id=1, source_target_pairs={{0,1},{1,0},{2,3},{3,2},{4,5},{5,4},{6,7},{7,6},{8,9},{9,8},{10,11... | collective-permute-start | bytes 405512 | tf_op jit(solution)/shard_map/ppermute | solution.py:298
  4.6 8.1 %collective-permute-start.5 = (f32[264,256]{1,0:T(8,128)S(1)}, f32[264,256]{1,0:T(8,128)S(1)}, u32[]{:S(2)}, u32[]{:S(2)}) collective-permute-start(f32[264,256]{1,0:T(8,128)S(1)} %get-tuple-element.42), channel_id=1, source_target_pairs={{0,2},{1,3},{2,0},{3,1},{4,6},{5,7},{6,4},{7,5},{8,10},{9,11},{10,... | collective-permute-start | bytes 811016 | tf_op jit(solution)/shard_map/ppermute | solution.py:298
  5.9 13.2 %collective-permute-start.6 = (f32[264,256]{1,0:T(8,128)S(1)}, f32[264,256]{1,0:T(8,128)S(1)}, u32[]{:S(2)}, u32[]{:S(2)}) collective-permute-start(f32[264,256]{1,0:T(8,128)S(1)} %get-tuple-element.43), channel_id=1, source_target_pairs={{0,3},{1,2},{2,1},{3,0},{4,7},{5,6},{6,5},{7,4},{8,11},{9,10},{10,... | collective-permute-start | bytes 811016 | tf_op jit(solution)/shard_map/ppermute | solution.py:298
  6.3 19.8 %collective-permute-start = (f32[528,128]{1,0:T(8,128)S(1)}, f32[528,128]{1,0:T(8,128)S(1)}, u32[]{:S(2)}, u32[]{:S(2)}) collective-permute-start(f32[528,128]{1,0:T(8,128)S(1)} %get-tuple-element.34), channel_id=1, source_target_pairs={{0,1},{1,0},{2,3},{3,2},{4,5},{5,4},{6,7},{7,6},{8,9},{9,8},{10,11... | collective-permute-start | bytes 811016 | tf_op jit(solution)/shard_map/ppermute | solution.py:298
  6.5 19.6 %collective-permute-start.3 = (f32[528,128]{1,0:T(8,128)S(1)}, f32[528,128]{1,0:T(8,128)S(1)}, u32[]{:S(2)}, u32[]{:S(2)}) collective-permute-start(f32[528,128]{1,0:T(8,128)S(1)} %get-tuple-element.39), channel_id=1, source_target_pairs={{0,2},{1,3},{2,0},{3,1},{4,6},{5,7},{6,4},{7,5},{8,10},{9,11},{10,... | collective-permute-start | bytes 811016 | tf_op jit(solution)/shard_map/ppermute | solution.py:298
  7.8 22.2 %collective-permute-start.9 = (f32[528,128]{1,0:T(8,128)S(1)}, f32[528,128]{1,0:T(8,128)S(1)}, u32[]{:S(2)}, u32[]{:S(2)}) collective-permute-start(f32[528,128]{1,0:T(8,128)S(1)} %get-tuple-element.49), channel_id=1, source_target_pairs={{0,2},{1,3},{2,0},{3,1},{4,6},{5,7},{6,4},{7,5},{8,10},{9,11},{10,... | collective-permute-start | bytes 811016 | tf_op jit(solution)/shard_map/ppermute | solution.py:298
  19.9 13.8 %collective-permute-start.13 = (f32[352,256]{1,0:T(8,128)S(1)}, f32[352,256]{1,0:T(8,128)S(1)}, u32[]{:S(2)}, u32[]{:S(2)}) collective-permute-start(f32[352,256]{1,0:T(8,128)S(1)} %get-tuple-element.45.refs_9_.refs_2_), channel_id=1, source_target_pairs={{0,4},{4,8},{8,12},{12,16},{16,20},{20,24},{24,28},{1,5},{5,9},{9,... | collective-permute-start | bytes 1081352 | tf_op jit(solution)/shard_map/ppermute | solution.py:360
  23.0 17.8 %collective-permute-start.14 = (f32[352,256]{1,0:T(8,128)S(1)}, f32[352,256]{1,0:T(8,128)S(1)}, u32[]{:S(2)}, u32[]{:S(2)}) collective-permute-start(f32[352,256]{1,0:T(8,128)S(1)} %get-tuple-element.44.refs_8_.refs_1_), channel_id=1, source_target_pairs={{4,0},{8,4},{12,8},{16,12},{20,16},{24,20},{28,24},{5,1},{9,5},{13... | collective-permute-start | bytes 1081352 | tf_op jit(solution)/shard_map/ppermute | solution.py:361
  27.7 13.1 %collective-permute-start.7 = (f32[512,128]{1,0:T(8,128)S(1)}, f32[512,128]{1,0:T(8,128)S(1)}, u32[]{:S(2)}, u32[]{:S(2)}) collective-permute-start(f32[512,128]{1,0:T(8,128)S(1)} %get-tuple-element.47), channel_id=1, source_target_pairs={{0,2},{1,3},{2,0},{3,1},{4,6},{5,7},{6,4},{7,5},{8,10},{9,11},{10,... | collective-permute-start | bytes 786440 | tf_op jit(solution)/shard_map/ppermute | solution.py:298
  31.6 2.2 %collective-permute-start.11 = (f32[256,128]{1,0:T(8,128)S(1)}, f32[256,128]{1,0:T(8,128)S(1)}, u32[]{:S(2)}, u32[]{:S(2)}) collective-permute-start(f32[256,128]{1,0:T(8,128)S(1)} %get-tuple-element.53), channel_id=1, source_target_pairs={{0,1},{1,0},{2,3},{3,2},{4,5},{5,4},{6,7},{7,6},{8,9},{9,8},{10,11... | collective-permute-start | bytes 393224 | tf_op jit(solution)/shard_map/ppermute | solution.py:298
  32.5 12.5 %collective-permute-start.10 = (f32[512,128]{1,0:T(8,128)S(1)}, f32[512,128]{1,0:T(8,128)S(1)}, u32[]{:S(2)}, u32[]{:S(2)}) collective-permute-start(f32[512,128]{1,0:T(8,128)S(1)} %get-tuple-element.52), channel_id=1, source_target_pairs={{0,2},{1,3},{2,0},{3,1},{4,6},{5,7},{6,4},{7,5},{8,10},{9,11},{10,... | collective-permute-start | bytes 786440 | tf_op jit(solution)/shard_map/ppermute | solution.py:298
  42.3 7.5 %collective-permute-start.15 = (f32[256,256]{1,0:T(8,128)S(1)}, f32[256,256]{1,0:T(8,128)S(1)}, u32[]{:S(2)}, u32[]{:S(2)}) collective-permute-start(f32[256,256]{1,0:T(8,128)S(1)} %get-tuple-element.58), channel_id=1, source_target_pairs={{0,2},{1,3},{2,0},{3,1},{4,6},{5,7},{6,4},{7,5},{8,10},{9,11},{10,... | collective-permute-start | bytes 786440 | tf_op jit(solution)/shard_map/ppermute | solution.py:298
  43.6 12.4 %collective-permute-start.16 = (f32[256,256]{1,0:T(8,128)S(1)}, f32[256,256]{1,0:T(8,128)S(1)}, u32[]{:S(2)}, u32[]{:S(2)}) collective-permute-start(f32[256,256]{1,0:T(8,128)S(1)} %get-tuple-element.59), channel_id=1, source_target_pairs={{0,3},{1,2},{2,1},{3,0},{4,7},{5,6},{6,5},{7,4},{8,11},{9,10},{10,... | collective-permute-start | bytes 786440 | tf_op jit(solution)/shard_map/ppermute | solution.py:298
  44.4 11.6 %collective-permute-start.17 = (f32[256,256]{1,0:T(8,128)S(1)}, f32[256,256]{1,0:T(8,128)S(1)}, u32[]{:S(2)}, u32[]{:S(2)}) collective-permute-start(f32[256,256]{1,0:T(8,128)S(1)} %get-tuple-element.60), channel_id=1, source_target_pairs={{0,1},{1,0},{2,3},{3,2},{4,5},{5,4},{6,7},{7,6},{8,9},{9,8},{10,11... | collective-permute-start | bytes 786440 | tf_op jit(solution)/shard_map/ppermute | solution.py:298
  44.5 11.5 %collective-permute-start.8 = (f32[512,128]{1,0:T(8,128)S(1)}, f32[512,128]{1,0:T(8,128)S(1)}, u32[]{:S(2)}, u32[]{:S(2)}) collective-permute-start(f32[512,128]{1,0:T(8,128)S(1)} %shard_map.59), channel_id=1, source_target_pairs={{0,1},{1,0},{2,3},{3,2},{4,5},{5,4},{6,7},{7,6},{8,9},{9,8},{10,11... | collective-permute-start | bytes 786440 | tf_op jit(solution)/shard_map/ppermute | solution.py:298
  45.0 1.5 %collective-permute-start.12 = (f32[256,128]{1,0:T(8,128)S(1)}, f32[256,128]{1,0:T(8,128)S(1)}, u32[]{:S(2)}, u32[]{:S(2)}) collective-permute-start(f32[256,128]{1,0:T(8,128)S(1)} %slice.9), channel_id=1, source_target_pairs={{0,1},{1,0},{2,3},{3,2},{4,5},{5,4},{6,7},{7,6},{8,9},{9,8},{10,11... | collective-permute-start | bytes 393224 | tf_op jit(solution)/shard_map/ppermute | solution.py:298

commit v9 on v7

--- a/solution.py
+++ b/solution.py
@@ -17,7 +17,6 @@
 LONG = pl.CostEstimate(flops=0, bytes_accessed=200_000_000, transcendentals=0)
 SHORT = pl.CostEstimate(flops=0, bytes_accessed=1024, transcendentals=0)
 SPLIT = 4
-HEAD_LIMIT = 24
 
 
 def split(values):
@@ -239,6 +238,15 @@
     inverse_rows(sweeps, count, cells, inverse_ref, outs)
 
 
+def join_kernel(groups, size, *refs):
+    outs = refs[-groups:]
+    for group, out_ref in enumerate(outs):
+        at = 0
+        for ref in refs[group * size : (group + 1) * size]:
+            out_ref[at : at + ref.shape[0], :] = ref[...]
+            at += ref.shape[0]
+
+
 def unpack_kernel(pieces, row_count, cells, *refs):
     me = lax.axis_index("span")
     blocks, (out_ref, held, done) = refs[:-3], refs[-3:]
@@ -279,6 +287,12 @@
     )(*args, *earlier)
 
 
+def join(*groups, earlier=()):
+    shapes = [(sum(block.shape[0] for block in group), group[0].shape[1]) for group in groups]
+    blocks = [block for group in groups for block in group]
+    return call(functools.partial(join_kernel, len(groups), len(groups[0])), shapes, *blocks, cost=SHORT, earlier=earlier)
+
+
 def swap(block, d):
     return lax.ppermute(block, "span", [(i, i ^ d) for i in range(lax.axis_size("span"))])
 
@@ -303,21 +317,20 @@
     source = source.reshape(cells, lines, LANES)
     scratch = [pltpu.VMEM((cells * (lines + 8), LANES), jnp.float32), pltpu.SemaphoreType.DMA((SPLIT,))]
 
-    def pack(jobs, shapes, limit, *earlier):
+    def pack(jobs, shapes, *earlier):
         return pl.pallas_call(
             functools.partial(pack_kernel, jobs, row_count, cells, len(earlier)),
             out_shape=[jax.ShapeDtypeStruct(shape, jnp.float32) for shape in shapes],
             in_specs=[ANY] * (1 + len(earlier)),
             out_specs=[VMEM] * len(shapes),
             scratch_shapes=scratch,
-            compiler_params=pltpu.CompilerParams(vmem_limit_bytes=limit * 1024 * 1024),
+            compiler_params=PARAMS,
             cost_estimate=LONG,
         )(source, *earlier)
 
     edge_size, size = len(edges) * cells + 8, len(inner) * cells + 8
     jobs = [(d - 1, 0, d, edges, 0, tiles) for d in range(1, count)]
-    packed = pack(jobs, [(edge_size, width)] * (count - 1), HEAD_LIMIT)
-    edge_blocks = [swap(block, d) for d, block in enumerate(packed, 1)]
+    edge_blocks = [swap(block, d) for d, block in enumerate(pack(jobs, [(edge_size, width)] * (count - 1)), 1)]
     jobs, shapes = [(0, 0, 0, edges, 0, tiles)], [(edge_size, width)]
 
     def add(d, wanted):
@@ -331,14 +344,14 @@
     for part in range(parts):
         for d in far:
             add(d, [part])
-    packed = pack(jobs, shapes, 24, *edge_blocks[: half - 1])
+    packed = pack(jobs, shapes, *edge_blocks[: half - 1])
     edge_blocks = [packed[0], *edge_blocks]
     near_blocks = [packed[1]] + [swap(packed[1 + d], d) for d in near]
-    far_blocks = []
+    messages = []
     for part in range(parts):
         mine = packed[1 + half * (part + 1) : 1 + half * (part + 2)]
-        message = [mine[0]] + [swap(mine[d], d) for d in near]
-        far_blocks.append(swap(jnp.concatenate(message), half))
+        messages.append([mine[0]] + [swap(mine[d], d) for d in near])
+    far_blocks = [swap(message, half) for message in join(*messages, earlier=(edge_blocks[half],))]
 
     spectrum, first, last, sides = call(
         functools.partial(edge_kernel, edges, count, cells),
@@ -380,7 +393,7 @@
         pieces += [(made[part][0], 0, 0, *place(part)), (arrived[part], half, 0, *place(part))]
         for d in near:
             if part < parts - 1:
-                message = swap(jnp.concatenate([onward(part, d), made[part][d]]), d)
+                message = swap(join([onward(part, d), made[part][d]])[0], d)
                 pieces += [(message, half + d, 0, *place(part)), (message, d, size, *place(part))]
             else:
                 earlier.append(swap(made[part][d], d))

time: 59.7 us -> 56.2 us (0.941)
  waiting for transfers between devices: 31 us -> 27.2 us
    ppermute x16, waiting for transfers between devices: 23.5 us -> 20.1 us  [swap(): lax.ppermute(block, 'span', [(i, i ^ d) for i in range(lax.axis_size('spa...]
    pallas_call x4 -> x6, Pallas kernels: 5.35 us -> 5.39 us  [call(): pl.pallas_call(kernel, out_shape=shapes, in_specs=[VMEM] * len(args) + [A...]
  transfers between devices with their start and end apart: 18 -> 18, of which waited for: 8 -> 7; matrix products, arithmetic and copies ran while one was open for 0% -> 0% of each run, Pallas kernels for 9% -> 12%
where the time goes in v9:
time: 56.2 us; the launch traced here: 56.1 us
  waiting for transfers between devices  27.2 us (48%)
  starting transfers between devices  18.1 us (32%)
  Pallas kernels  8.97 us (16%)
  local copies, waits for them, and re-layouts  1.63 us (3%)
    ppermute x16, waiting for transfers between devices, swap(): lax.ppermute(block, 'span', [(i, i ^ d) for i in range(lax.axis_size('spa...  20.1 us
    ppermute x16, starting transfers between devices, swap(): lax.ppermute(block, 'span', [(i, i ^ d) for i in range(lax.axis_size('spa...  11.9 us
    ppermute x1, waiting for transfers between devices, local(): high = lax.ppermute(first, 'plane', down)  7.08 us
    pallas_call x6, Pallas kernels, call(): pl.pallas_call(kernel, out_shape=shapes, in_specs=[VMEM] * len(args) + [A...  5.39 us
    ppermute x1, starting transfers between devices, local(): low = lax.ppermute(last, 'plane', up)  3.12 us
    ppermute x1, starting transfers between devices, local(): high = lax.ppermute(first, 'plane', down)  3.06 us
    pallas_call x2, Pallas kernels, pack(): pl.pallas_call(functools.partial(pack_kernel, jobs, row_count, cells, len...  2.15 us
    unnamed x10, local copies, waits for them, and re-layouts  1.61 us
  transfers between devices with their start and end apart: 18, of which 7 were waited for; matrix products, arithmetic and copies ran while one was open for 0% of the time, Pallas kernels for 12%

profile of v9, /device:TPU:25, one launch (start us, length us, event | category | flops | bytes accessed | tf_op | source)
XLA Modules:
  0.0 56.1 jit_solution(2195191323074378810)
XLA Ops:
  0.0 1.6 %copy-done = f32[128,4,1024]{2,1,0:T(4,128)S(1)} copy-done((f32[128,4,1024]{2,1,0:T(4,128)S(1)}, f32[128,4,1024]{2,1,0:T(4,128)}, u32[]{:S(2)}) %copy-start) | copy-done | bytes 2097176
  3.2 1.3 %collective-permute-start.4 = (f32[264,256]{1,0:T(8,128)S(1)}, f32[264,256]{1,0:T(8,128)S(1)}, u32[]{:S(2)}, u32[]{:S(2)}) collective-permute-start(f32[264,256]{1,0:T(8,128)S(1)} %get-tuple-element.40), channel_id=1, source_target_pairs={{0,2},{1,3},{2,0},{3,1},{4,6},{5,7},{6,4},{7,5},{8,10},{9,11},{10,... | collective-permute-start | bytes 811016 | tf_op jit(solution)/shard_map/ppermute | solution.py:297
  4.5 1.3 %shard_map.56 = (f32[264,256]{1,0:T(8,128)S(1)}, f32[528,128]{1,0:T(8,128)S(1)}, f32[528,128]{1,0:T(8,128)S(1)}, f32[264,128]{1,0:T(8,128)S(1)}, f32[264,128]{1,...) custom-call(f32[128,32,128]{2,1,0:T(8,128)S(1)} %bitcast.11, ...), custom_call_target="tpu_custom_call" | custom-call | bytes 200000000 | tf_op jit(solution)/shard_map/pallas_call | solution.py:321
  6.4 1.4 %collective-permute-start.6 = (f32[264,256]{1,0:T(8,128)S(1)}, f32[264,256]{1,0:T(8,128)S(1)}, u32[]{:S(2)}, u32[]{:S(2)}) collective-permute-start(f32[264,256]{1,0:T(8,128)S(1)} %get-tuple-element.43), channel_id=1, source_target_pairs={{0,3},{1,2},{2,1},{3,0},{4,7},{5,6},{6,5},{7,4},{8,11},{9,10},{10,... | collective-permute-start | bytes 811016 | tf_op jit(solution)/shard_map/ppermute | solution.py:297
  7.9 3.3 %collective-permute-done.4.refs_4_.refs_2_ = f32[264,256]{1,0:T(8,128)S(1)} collective-permute-done((f32[264,256]{1,0:T(8,128)S(1)}, f32[264,256]{1,0:T(8,128)S(1)}, u32[]{:S(2)}, u32[]{:S(2)}) %collective-permute-start.4) | collective-permute-done | bytes 270368 | tf_op jit(solution)/shard_map/ppermute | solution.py:297
  11.3 1.3 %collective-permute-start.5 = (f32[528,128]{1,0:T(8,128)S(1)}, f32[528,128]{1,0:T(8,128)S(1)}, u32[]{:S(2)}, u32[]{:S(2)}) collective-permute-start(f32[528,128]{1,0:T(8,128)S(1)} %get-tuple-element.41), channel_id=1, source_target_pairs={{0,2},{1,3},{2,0},{3,1},{4,6},{5,7},{6,4},{7,5},{8,10},{9,11},{10,... | collective-permute-start | bytes 811016 | tf_op jit(solution)/shard_map/ppermute | solution.py:297
  12.8 4.9 %collective-permute-done.6.refs_3_ = f32[264,256]{1,0:T(8,128)S(1)} collective-permute-done((f32[264,256]{1,0:T(8,128)S(1)}, f32[264,256]{1,0:T(8,128)S(1)}, u32[]{:S(2)}, u32[]{:S(2)}) %collective-permute-start.6) | collective-permute-done | bytes 270368 | tf_op jit(solution)/shard_map/ppermute | solution.py:297
  17.7 0.8 %shard_map.58 = (f32[2,352,256]{2,1,0:T(8,128)S(1)}, f32[352,256]{1,0:T(8,128)S(1)}, f32[352,256]{1,0:T(8,128)S(1)}, f32[352,16]{1,0:T(8,128)S(1)}) custom-call(f32[264,256]{1,0:T(8,128)S(1)} %get-tuple-element.42.refs_0_, f32[264,256]{1,0:T(8,128)S(1)} %collective-permute-done.refs_0_.refs_1_, f32[264,256]{1,0:T(8,128)S(1)} %collective-permute-done.4.refs_4_.refs_2_, ...), custom_call_target="tpu_custom_call" | custom-call | bytes 200000000 | tf_op jit(solution)/shard_map/pallas_call | solution.py:280
  18.5 3.1 %collective-permute-start.13 = (f32[352,256]{1,0:T(8,128)S(1)}, f32[352,256]{1,0:T(8,128)S(1)}, u32[]{:S(2)}, u32[]{:S(2)}) collective-permute-start(f32[352,256]{1,0:T(8,128)S(1)} %get-tuple-element.45.refs_9_.refs_2_), channel_id=1, source_target_pairs={{0,4},{4,8},{8,12},{12,16},{16,20},{20,24},{24,28},{1,5},{5,9},{9,... | collective-permute-start | bytes 1081352 | tf_op jit(solution)/shard_map/ppermute | solution.py:363
  21.7 3.1 %collective-permute-start.14 = (f32[352,256]{1,0:T(8,128)S(1)}, f32[352,256]{1,0:T(8,128)S(1)}, u32[]{:S(2)}, u32[]{:S(2)}) collective-permute-start(f32[352,256]{1,0:T(8,128)S(1)} %get-tuple-element.44.refs_8_.refs_1_), channel_id=1, source_target_pairs={{4,0},{8,4},{12,8},{16,12},{20,16},{24,20},{28,24},{5,1},{9,5},{13... | collective-permute-start | bytes 1081352 | tf_op jit(solution)/shard_map/ppermute | solution.py:364
  24.8 1.5 %shard_map.59 = (f32[256,128]{1,0:T(8,128)S(1)}, f32[256,128]{1,0:T(8,128)S(1)}, f32[512,128]{1,0:T(8,128)S(1)}, f32[2,352,128]{2,1,0:T(8,128)S(1)}) custom-call(f32[528,128]{1,0:T(8,128)S(1)} %get-tuple-element.34.refs_0_, f32[528,128]{1,0:T(8,128)S(1)} %collective-permute-done.1.refs_1_, f32[528,128]{1,0:T(8,128)S(1)} %collective-permute-done.5.refs_2_.refs_3_, ...), custom_call_target="tpu_custom_call" | custom-call | bytes 1024 | tf_op jit(solution)/shard_map/pallas_call | solution.py:280
  26.3 1.3 %collective-permute-start.7 = (f32[512,128]{1,0:T(8,128)S(1)}, f32[512,128]{1,0:T(8,128)S(1)}, u32[]{:S(2)}, u32[]{:S(2)}) collective-permute-start(f32[512,128]{1,0:T(8,128)S(1)} %get-tuple-element.47), channel_id=1, source_target_pairs={{0,2},{1,3},{2,0},{3,1},{4,6},{5,7},{6,4},{7,5},{8,10},{9,11},{10,... | collective-permute-start | bytes 786440 | tf_op jit(solution)/shard_map/ppermute | solution.py:297
  27.6 1.0 %collective-permute-done.9.refs_2_.refs_3_ = f32[528,128]{1,0:T(8,128)S(1)} collective-permute-done((f32[528,128]{1,0:T(8,128)S(1)}, f32[528,128]{1,0:T(8,128)S(1)}, u32[]{:S(2)}, u32[]{:S(2)}) %collective-permute-start.9) | collective-permute-done | bytes 270368 | tf_op jit(solution)/shard_map/ppermute | solution.py:297
  28.6 1.5 %shard_map.61 = (f32[256,128]{1,0:T(8,128)S(1)}, f32[256,128]{1,0:T(8,128)S(1)}, f32[512,128]{1,0:T(8,128)S(1)}, f32[2,352,128]{2,1,0:T(8,128)S(1)}) custom-call(f32[528,128]{1,0:T(8,128)S(1)} %get-tuple-element.34.refs_0_, f32[528,128]{1,0:T(8,128)S(1)} %collective-permute-done.1.refs_1_, f32[528,128]{1,0:T(8,128)S(1)} %collective-permute-done.9.refs_2_.refs_3_, ...), custom_call_target="tpu_custom_call" | custom-call | bytes 1024 | tf_op jit(solution)/shard_map/pallas_call | solution.py:280
  30.2 0.9 %collective-permute-start.11 = (f32[256,128]{1,0:T(8,128)S(1)}, f32[256,128]{1,0:T(8,128)S(1)}, u32[]{:S(2)}, u32[]{:S(2)}) collective-permute-start(f32[256,128]{1,0:T(8,128)S(1)} %get-tuple-element.53), channel_id=1, source_target_pairs={{0,1},{1,0},{2,3},{3,2},{4,5},{5,4},{6,7},{7,6},{8,9},{9,8},{10,11... | collective-permute-start | bytes 393224 | tf_op jit(solution)/shard_map/ppermute | solution.py:297
  31.1 1.3 %collective-permute-start.10 = (f32[512,128]{1,0:T(8,128)S(1)}, f32[512,128]{1,0:T(8,128)S(1)}, u32[]{:S(2)}, u32[]{:S(2)}) collective-permute-start(f32[512,128]{1,0:T(8,128)S(1)} %get-tuple-element.52), channel_id=1, source_target_pairs={{0,2},{1,3},{2,0},{3,1},{4,6},{5,7},{6,4},{7,5},{8,10},{9,11},{10,... | collective-permute-start | bytes 786440 | tf_op jit(solution)/shard_map/ppermute | solution.py:297
  32.4 7.1 %collective-permute-done.14.refs_5_ = f32[352,256]{1,0:T(8,128)S(1)} collective-permute-done((f32[352,256]{1,0:T(8,128)S(1)}, f32[352,256]{1,0:T(8,128)S(1)}, u32[]{:S(2)}, u32[]{:S(2)}) %collective-permute-start.14) | collective-permute-done | bytes 360480 | tf_op jit(solution)/shard_map/ppermute | solution.py:364
  39.4 1.4 %shard_map.62 = (f32[256,256]{1,0:T(8,128)S(1)}, f32[256,256]{1,0:T(8,128)S(1)}, f32[256,256]{1,0:T(8,128)S(1)}, f32[256,256]{1,0:T(8,128)S(1)}) custom-call(f32[2,352,256]{2,1,0:T(8,128)S(1)} %get-tuple-element.54.refs_0_, f32[352,256]{1,0:T(8,128)S(1)} %get-tuple-element.44.refs_8_.refs_1_, f32[352,256]{1,0:T(8,128)S(1)} %get-tuple-element.45.refs_9_.refs_2_, ...), custom_call_target="tpu_custom_call" | custom-call | bytes 200000000 | tf_op jit(solution)/shard_map/pallas_call | solution.py:280
  40.9 1.3 %collective-permute-start.15 = (f32[256,256]{1,0:T(8,128)S(1)}, f32[256,256]{1,0:T(8,128)S(1)}, u32[]{:S(2)}, u32[]{:S(2)}) collective-permute-start(f32[256,256]{1,0:T(8,128)S(1)} %get-tuple-element.58), channel_id=1, source_target_pairs={{0,2},{1,3},{2,0},{3,1},{4,6},{5,7},{6,4},{7,5},{8,10},{9,11},{10,... | collective-permute-start | bytes 786440 | tf_op jit(solution)/shard_map/ppermute | solution.py:297
  42.2 0.8 %collective-permute-start.16 = (f32[256,256]{1,0:T(8,128)S(1)}, f32[256,256]{1,0:T(8,128)S(1)}, u32[]{:S(2)}, u32[]{:S(2)}) collective-permute-start(f32[256,256]{1,0:T(8,128)S(1)} %get-tuple-element.59), channel_id=1, source_target_pairs={{0,3},{1,2},{2,1},{3,0},{4,7},{5,6},{6,5},{7,4},{8,11},{9,10},{10,... | collective-permute-start | bytes 786440 | tf_op jit(solution)/shard_map/ppermute | solution.py:297
  43.8 1.4 %collective-permute-done.12.refs_7_ = f32[256,128]{1,0:T(8,128)S(1)} collective-permute-done((f32[256,128]{1,0:T(8,128)S(1)}, f32[256,128]{1,0:T(8,128)S(1)}, u32[]{:S(2)}, u32[]{:S(2)}) %collective-permute-start.12) | collective-permute-done | bytes 131104 | tf_op jit(solution)/shard_map/ppermute | solution.py:297
  45.1 3.3 %collective-permute-done.15.refs_9_ = f32[256,256]{1,0:T(8,128)S(1)} collective-permute-done((f32[256,256]{1,0:T(8,128)S(1)}, f32[256,256]{1,0:T(8,128)S(1)}, u32[]{:S(2)}, u32[]{:S(2)}) %collective-permute-start.15) | collective-permute-done | bytes 262176 | tf_op jit(solution)/shard_map/ppermute | solution.py:297
  48.4 6.2 %collective-permute-done.16.refs_10_ = f32[256,256]{1,0:T(8,128)S(1)} collective-permute-done((f32[256,256]{1,0:T(8,128)S(1)}, f32[256,256]{1,0:T(8,128)S(1)}, u32[]{:S(2)}, u32[]{:S(2)}) %collective-permute-start.16) | collective-permute-done | bytes 262176 | tf_op jit(solution)/shard_map/ppermute | solution.py:297
  54.6 1.4 %shard_map.63 = f32[128,32,128]{2,1,0:T(8,128)} custom-call(f32[256,128]{1,0:T(8,128)S(1)} %get-tuple-element.46.refs_0_, f32[512,128]{1,0:T(8,128)S(1)} %collective-permute-done.7.refs_11_.refs_1_, f32[512,128]{1,0:T(8,128)S(1)} %collective-permute-done.8.refs_2_.refs_3_, f32[512,128]{1,0:T(8,128)S(1)} %collective-permute-done.8.refs_2_.refs_3_, ...), custom_call_target="tpu_custom_call" | custom-call | bytes 200000000 | tf_op jit(solution)/shard_map/pallas_call | solution.py:409
  (33 shorter events, 3.3 us)
Async XLA Ops:
  0.0 1.6 %copy-start = (f32[128,4,1024]{2,1,0:T(4,128)S(1)}, f32[128,4,1024]{2,1,0:T(4,128)}, u32[]{:S(2)}) copy-start(f32[128,4,1024]{2,1,0:T(4,128)} %param.5) | copy-start | bytes 6291460
  2.4 15.3 %copy-start.2 = (bf16[2,2,176,384]{3,2,1,0:T(8,128)(2,1)S(1)}, bf16[2,2,176,384]{3,2,1,0:T(8,128)(2,1)}, u32[]{:S(2)}) copy-start(bf16[2,2,176,384]{3,2,1,0:T(8,128)(2,1)} %constant.6.clone.refs_4_) | copy-start | bytes 1622020
  2.4 15.3 %copy-start.3 = (s32[4,1024]{1,0:T(4,128)S(1)}, s32[4,1024]{1,0:T(4,128)}, u32[]{:S(2)}) copy-start(s32[4,1024]{1,0:T(4,128)} %refs_8_.1) | copy-start | bytes 49156
  2.4 15.2 %copy-start.4 = (f32[8,384]{1,0:T(8,128)S(1)}, f32[8,384]{1,0:T(8,128)}, u32[]{:S(2)}) copy-start(f32[8,384]{1,0:T(8,128)} %constant.8.clone.refs_5_.refs_6_.refs_7_) | copy-start | bytes 36868
  2.5 2.0 %collective-permute-start = (f32[264,256]{1,0:T(8,128)S(1)}, f32[264,256]{1,0:T(8,128)S(1)}, u32[]{:S(2)}, u32[]{:S(2)}) collective-permute-start(f32[264,256]{1,0:T(8,128)S(1)} %get-tuple-element.33), channel_id=1, source_target_pairs={{0,1},{1,0},{2,3},{3,2},{4,5},{5,4},{6,7},{7,6},{8,9},{9,8},{10,11... | collective-permute-start | bytes 811016 | tf_op jit(solution)/shard_map/ppermute | solution.py:297
  3.2 21.6 %copy-start.1 = (bf16[2,2,128,528]{3,2,1,0:T(8,128)(2,1)S(1)}, bf16[2,2,128,528]{3,2,1,0:T(8,128)(2,1)}, u32[]{:S(2)}) copy-start(bf16[2,2,128,528]{3,2,1,0:T(8,128)(2,1)} %constant.7.clone.refs_5_.refs_6_) | copy-start | bytes 1622020
  3.2 8.0 %collective-permute-start.4 = (f32[264,256]{1,0:T(8,128)S(1)}, f32[264,256]{1,0:T(8,128)S(1)}, u32[]{:S(2)}, u32[]{:S(2)}) collective-permute-start(f32[264,256]{1,0:T(8,128)S(1)} %get-tuple-element.40), channel_id=1, source_target_pairs={{0,2},{1,3},{2,0},{3,1},{4,6},{5,7},{6,4},{7,5},{8,10},{9,11},{10,... | collective-permute-start | bytes 811016 | tf_op jit(solution)/shard_map/ppermute | solution.py:297
  5.8 5.5 %collective-permute-start.2 = (f32[264,128]{1,0:T(8,128)S(1)}, f32[264,128]{1,0:T(8,128)S(1)}, u32[]{:S(2)}, u32[]{:S(2)}) collective-permute-start(f32[264,128]{1,0:T(8,128)S(1)} %get-tuple-element.37), channel_id=1, source_target_pairs={{0,1},{1,0},{2,3},{3,2},{4,5},{5,4},{6,7},{7,6},{8,9},{9,8},{10,11... | collective-permute-start | bytes 405512 | tf_op jit(solution)/shard_map/ppermute | solution.py:297
  6.2 5.0 %collective-permute-start.3 = (f32[264,128]{1,0:T(8,128)S(1)}, f32[264,128]{1,0:T(8,128)S(1)}, u32[]{:S(2)}, u32[]{:S(2)}) collective-permute-start(f32[264,128]{1,0:T(8,128)S(1)} %get-tuple-element.39), channel_id=1, source_target_pairs={{0,1},{1,0},{2,3},{3,2},{4,5},{5,4},{6,7},{7,6},{8,9},{9,8},{10,11... | collective-permute-start | bytes 405512 | tf_op jit(solution)/shard_map/ppermute | solution.py:297
  6.4 11.3 %collective-permute-start.6 = (f32[264,256]{1,0:T(8,128)S(1)}, f32[264,256]{1,0:T(8,128)S(1)}, u32[]{:S(2)}, u32[]{:S(2)}) collective-permute-start(f32[264,256]{1,0:T(8,128)S(1)} %get-tuple-element.43), channel_id=1, source_target_pairs={{0,3},{1,2},{2,1},{3,0},{4,7},{5,6},{6,5},{7,4},{8,11},{9,10},{10,... | collective-permute-start | bytes 811016 | tf_op jit(solution)/shard_map/ppermute | solution.py:297
  7.8 16.9 %collective-permute-start.1 = (f32[528,128]{1,0:T(8,128)S(1)}, f32[528,128]{1,0:T(8,128)S(1)}, u32[]{:S(2)}, u32[]{:S(2)}) collective-permute-start(f32[528,128]{1,0:T(8,128)S(1)} %get-tuple-element.35), channel_id=1, source_target_pairs={{0,1},{1,0},{2,3},{3,2},{4,5},{5,4},{6,7},{7,6},{8,9},{9,8},{10,11... | collective-permute-start | bytes 811016 | tf_op jit(solution)/shard_map/ppermute | solution.py:297
  11.3 13.4 %collective-permute-start.5 = (f32[528,128]{1,0:T(8,128)S(1)}, f32[528,128]{1,0:T(8,128)S(1)}, u32[]{:S(2)}, u32[]{:S(2)}) collective-permute-start(f32[528,128]{1,0:T(8,128)S(1)} %get-tuple-element.41), channel_id=1, source_target_pairs={{0,2},{1,3},{2,0},{3,1},{4,6},{5,7},{6,4},{7,5},{8,10},{9,11},{10,... | collective-permute-start | bytes 811016 | tf_op jit(solution)/shard_map/ppermute | solution.py:297
  12.6 16.0 %collective-permute-start.9 = (f32[528,128]{1,0:T(8,128)S(1)}, f32[528,128]{1,0:T(8,128)S(1)}, u32[]{:S(2)}, u32[]{:S(2)}) collective-permute-start(f32[528,128]{1,0:T(8,128)S(1)} %get-tuple-element.49), channel_id=1, source_target_pairs={{0,2},{1,3},{2,0},{3,1},{4,6},{5,7},{6,4},{7,5},{8,10},{9,11},{10,... | collective-permute-start | bytes 811016 | tf_op jit(solution)/shard_map/ppermute | solution.py:297
  18.5 13.8 %collective-permute-start.13 = (f32[352,256]{1,0:T(8,128)S(1)}, f32[352,256]{1,0:T(8,128)S(1)}, u32[]{:S(2)}, u32[]{:S(2)}) collective-permute-start(f32[352,256]{1,0:T(8,128)S(1)} %get-tuple-element.45.refs_9_.refs_2_), channel_id=1, source_target_pairs={{0,4},{4,8},{8,12},{12,16},{16,20},{20,24},{24,28},{1,5},{5,9},{9,... | collective-permute-start | bytes 1081352 | tf_op jit(solution)/shard_map/ppermute | solution.py:363
  21.7 17.8 %collective-permute-start.14 = (f32[352,256]{1,0:T(8,128)S(1)}, f32[352,256]{1,0:T(8,128)S(1)}, u32[]{:S(2)}, u32[]{:S(2)}) collective-permute-start(f32[352,256]{1,0:T(8,128)S(1)} %get-tuple-element.44.refs_8_.refs_1_), channel_id=1, source_target_pairs={{4,0},{8,4},{12,8},{16,12},{20,16},{24,20},{28,24},{5,1},{9,5},{13... | collective-permute-start | bytes 1081352 | tf_op jit(solution)/shard_map/ppermute | solution.py:364
  26.3 13.1 %collective-permute-start.7 = (f32[512,128]{1,0:T(8,128)S(1)}, f32[512,128]{1,0:T(8,128)S(1)}, u32[]{:S(2)}, u32[]{:S(2)}) collective-permute-start(f32[512,128]{1,0:T(8,128)S(1)} %get-tuple-element.47), channel_id=1, source_target_pairs={{0,2},{1,3},{2,0},{3,1},{4,6},{5,7},{6,4},{7,5},{8,10},{9,11},{10,... | collective-permute-start | bytes 786440 | tf_op jit(solution)/shard_map/ppermute | solution.py:297
  30.2 9.3 %collective-permute-start.11 = (f32[256,128]{1,0:T(8,128)S(1)}, f32[256,128]{1,0:T(8,128)S(1)}, u32[]{:S(2)}, u32[]{:S(2)}) collective-permute-start(f32[256,128]{1,0:T(8,128)S(1)} %get-tuple-element.53), channel_id=1, source_target_pairs={{0,1},{1,0},{2,3},{3,2},{4,5},{5,4},{6,7},{7,6},{8,9},{9,8},{10,11... | collective-permute-start | bytes 393224 | tf_op jit(solution)/shard_map/ppermute | solution.py:297
  31.1 12.5 %collective-permute-start.10 = (f32[512,128]{1,0:T(8,128)S(1)}, f32[512,128]{1,0:T(8,128)S(1)}, u32[]{:S(2)}, u32[]{:S(2)}) collective-permute-start(f32[512,128]{1,0:T(8,128)S(1)} %get-tuple-element.52), channel_id=1, source_target_pairs={{0,2},{1,3},{2,0},{3,1},{4,6},{5,7},{6,4},{7,5},{8,10},{9,11},{10,... | collective-permute-start | bytes 786440 | tf_op jit(solution)/shard_map/ppermute | solution.py:297
  40.9 7.5 %collective-permute-start.15 = (f32[256,256]{1,0:T(8,128)S(1)}, f32[256,256]{1,0:T(8,128)S(1)}, u32[]{:S(2)}, u32[]{:S(2)}) collective-permute-start(f32[256,256]{1,0:T(8,128)S(1)} %get-tuple-element.58), channel_id=1, source_target_pairs={{0,2},{1,3},{2,0},{3,1},{4,6},{5,7},{6,4},{7,5},{8,10},{9,11},{10,... | collective-permute-start | bytes 786440 | tf_op jit(solution)/shard_map/ppermute | solution.py:297
  42.2 12.4 %collective-permute-start.16 = (f32[256,256]{1,0:T(8,128)S(1)}, f32[256,256]{1,0:T(8,128)S(1)}, u32[]{:S(2)}, u32[]{:S(2)}) collective-permute-start(f32[256,256]{1,0:T(8,128)S(1)} %get-tuple-element.59), channel_id=1, source_target_pairs={{0,3},{1,2},{2,1},{3,0},{4,7},{5,6},{6,5},{7,4},{8,11},{9,10},{10,... | collective-permute-start | bytes 786440 | tf_op jit(solution)/shard_map/ppermute | solution.py:297
  43.0 11.6 %collective-permute-start.17 = (f32[256,256]{1,0:T(8,128)S(1)}, f32[256,256]{1,0:T(8,128)S(1)}, u32[]{:S(2)}, u32[]{:S(2)}) collective-permute-start(f32[256,256]{1,0:T(8,128)S(1)} %get-tuple-element.60), channel_id=1, source_target_pairs={{0,1},{1,0},{2,3},{3,2},{4,5},{5,4},{6,7},{7,6},{8,9},{9,8},{10,11... | collective-permute-start | bytes 786440 | tf_op jit(solution)/shard_map/ppermute | solution.py:297
  43.1 11.5 %collective-permute-start.8 = (f32[512,128]{1,0:T(8,128)S(1)}, f32[512,128]{1,0:T(8,128)S(1)}, u32[]{:S(2)}, u32[]{:S(2)}) collective-permute-start(f32[512,128]{1,0:T(8,128)S(1)} %shard_map.60), channel_id=1, source_target_pairs={{0,1},{1,0},{2,3},{3,2},{4,5},{5,4},{6,7},{7,6},{8,9},{9,8},{10,11... | collective-permute-start | bytes 786440 | tf_op jit(solution)/shard_map/ppermute | solution.py:297
  43.7 1.5 %collective-permute-start.12 = (f32[256,128]{1,0:T(8,128)S(1)}, f32[256,128]{1,0:T(8,128)S(1)}, u32[]{:S(2)}, u32[]{:S(2)}) collective-permute-start(f32[256,128]{1,0:T(8,128)S(1)} %slice.9), channel_id=1, source_target_pairs={{0,1},{1,0},{2,3},{3,2},{4,5},{5,4},{6,7},{7,6},{8,9},{9,8},{10,11... | collective-permute-start | bytes 393224 | tf_op jit(solution)/shard_map/ppermute | solution.py:297

commit v10 on v9

--- a/solution.py
+++ b/solution.py
@@ -247,30 +247,30 @@
             at += ref.shape[0]
 
 
-def unpack_kernel(pieces, row_count, cells, *refs):
+def unpack_kernel(pieces, devices, row_count, cells, *refs):
     me = lax.axis_index("span")
-    blocks, (out_ref, held, done) = refs[:-3], refs[-3:]
+    blocks, (out_ref, held, done) = refs[: len(pieces)], refs[-3:]
     pitch = held.shape[0] // cells
-    lines = out_ref.shape[1]
-    own_tiles = lines // row_count // lax.axis_size("span")
+    own_lines = out_ref.shape[1] // lax.axis_size("span")
     some = cells // SPLIT
     copies = []
     for part in range(SPLIT):
         for block, (d, base, rows, offset, tiles) in zip(blocks, pieces):
-            first = jnp.bitwise_xor(me, d) * own_tiles + offset
             for i, row in enumerate(rows):
                 line = base + i * cells + part * some
                 for tile in range(tiles):
-                    at = part * some * pitch + (first + tile) * row_count + row
+                    at = part * some * pitch + devices.index(d) * own_lines + (offset + tile) * row_count + row
                     held[pl.ds(at, some, stride=pitch), :] = block[line : line + some, tile * LANES : (tile + 1) * LANES]
-        copies.append(
-            pltpu.make_async_copy(
-                held.reshape(cells, pitch, LANES).at[pl.ds(part * some, some), pl.ds(0, lines)],
-                out_ref.at[pl.ds(part * some, some)],
-                done.at[part],
+        for at, d in enumerate(devices):
+            first = pl.multiple_of(jnp.bitwise_xor(me, d) * own_lines, own_lines)
+            copies.append(
+                pltpu.make_async_copy(
+                    held.reshape(cells, pitch, LANES).at[pl.ds(part * some, some), pl.ds(at * own_lines, own_lines)],
+                    out_ref.at[pl.ds(part * some, some), pl.ds(first, own_lines)],
+                    done.at[part, at],
+                )
             )
-        )
-        copies[-1].start()
+            copies[-1].start()
     for copy in copies:
         copy.wait()
 
@@ -406,15 +406,24 @@
     )
     pieces.append((outs[0], 0, 0, edges, 0, tiles))
     pieces += [(swap(outs[d], d), d, 0, edges, 0, tiles) for d in (*far, *near)]
-    result = pl.pallas_call(
-        functools.partial(unpack_kernel, [piece[1:] for piece in pieces], row_count, cells),
-        out_shape=jax.ShapeDtypeStruct((cells, lines, LANES), jnp.float32),
-        in_specs=[VMEM] * len(pieces),
-        out_specs=ANY,
-        scratch_shapes=scratch,
-        compiler_params=PARAMS,
-        cost_estimate=LONG,
-    )(*[piece[0] for piece in pieces])
+    result = None
+    own_lines = tiles * row_count
+    for devices in (range(count - 1), [count - 1]) if own_lines % 8 == 0 else (range(count),):
+        chosen = [piece for piece in pieces if piece[1] in devices]
+        previous = () if result is None else (result,)
+        result = pl.pallas_call(
+            functools.partial(unpack_kernel, [piece[1:] for piece in chosen], list(devices), row_count, cells),
+            out_shape=jax.ShapeDtypeStruct((cells, lines, LANES), jnp.float32),
+            in_specs=[VMEM] * len(chosen) + [ANY] * len(previous),
+            out_specs=ANY,
+            scratch_shapes=[
+                pltpu.VMEM((cells * (len(devices) * own_lines + 8), LANES), jnp.float32),
+                pltpu.SemaphoreType.DMA((SPLIT, len(devices))),
+            ],
+            input_output_aliases={len(chosen): 0} if previous else {},
+            compiler_params=PARAMS,
+            cost_estimate=SHORT if previous else LONG,
+        )(*[piece[0] for piece in chosen], *previous)
     result = result.reshape(cells, columns // LANES, row_count, LANES).transpose(0, 2, 1, 3)
     return result.reshape(cells, row_count, columns)
 

time: 56.2 us -> 55.7 us (level)
  waiting for transfers between devices: 27.2 us -> 24.8 us
  Pallas kernels: 8.97 us -> 10.8 us
    ppermute x16, waiting for transfers between devices: 20.1 us -> 17.7 us  [swap(): lax.ppermute(block, 'span', [(i, i ^ d) for i in range(lax.axis_size('spa...]
    pallas_call x1 -> x2, Pallas kernels: 1.44 us -> 3.25 us  [local(): pl.pallas_call(functools.partial(unpack_kernel, [piece[1:] for piece in c...]
  transfers between devices with their start and end apart: 18 -> 18, of which waited for: 7 -> 6; matrix products, arithmetic and copies ran while one was open for 0% -> 0% of each run, Pallas kernels for 12% -> 16%
where the time goes in v10:
time: 55.7 us; the launch traced here: 55.5 us
  waiting for transfers between devices  24.8 us (45%)
  starting transfers between devices  18.2 us (33%)
  Pallas kernels  10.8 us (19%)
  local copies, waits for them, and re-layouts  1.63 us (3%)
    ppermute x16, waiting for transfers between devices, swap(): lax.ppermute(block, 'span', [(i, i ^ d) for i in range(lax.axis_size('spa...  17.7 us
    ppermute x16, starting transfers between devices, swap(): lax.ppermute(block, 'span', [(i, i ^ d) for i in range(lax.axis_size('spa...  12 us
    ppermute x1, waiting for transfers between devices, local(): high = lax.ppermute(first, 'plane', down)  7.08 us
    pallas_call x6, Pallas kernels, call(): pl.pallas_call(kernel, out_shape=shapes, in_specs=[VMEM] * len(args) + [A...  5.39 us
    pallas_call x2, Pallas kernels, local(): pl.pallas_call(functools.partial(unpack_kernel, [piece[1:] for piece in c...  3.25 us
    ppermute x1, starting transfers between devices, local(): low = lax.ppermute(last, 'plane', up)  3.12 us
    ppermute x1, starting transfers between devices, local(): high = lax.ppermute(first, 'plane', down)  3.06 us
    pallas_call x2, Pallas kernels, pack(): pl.pallas_call(functools.partial(pack_kernel, jobs, row_count, cells, len...  2.15 us
  transfers between devices with their start and end apart: 18, of which 6 were waited for; matrix products, arithmetic and copies ran while one was open for 0% of the time, Pallas kernels for 16%

profile of v10, /device:TPU:25, one launch (start us, length us, event | category | flops | bytes accessed | tf_op | source)
XLA Modules:
  0.0 55.5 jit_solution(2694342725951694089)
XLA Ops:
  0.0 1.6 %copy-done = f32[128,4,1024]{2,1,0:T(4,128)S(1)} copy-done((f32[128,4,1024]{2,1,0:T(4,128)S(1)}, f32[128,4,1024]{2,1,0:T(4,128)}, u32[]{:S(2)}) %copy-start) | copy-done | bytes 2097176
  1.6 0.8 %shard_map.55 = (f32[264,256]{1,0:T(8,128)S(1)}, f32[264,256]{1,0:T(8,128)S(1)}, f32[264,256]{1,0:T(8,128)S(1)}) custom-call(f32[128,32,128]{2,1,0:T(8,128)S(1)} %bitcast.10), custom_call_target="tpu_custom_call" | custom-call | bytes 200000000 | tf_op jit(solution)/shard_map/pallas_call | solution.py:321
  3.2 1.3 %collective-permute-start.4 = (f32[264,256]{1,0:T(8,128)S(1)}, f32[264,256]{1,0:T(8,128)S(1)}, u32[]{:S(2)}, u32[]{:S(2)}) collective-permute-start(f32[264,256]{1,0:T(8,128)S(1)} %get-tuple-element.40), channel_id=1, source_target_pairs={{0,2},{1,3},{2,0},{3,1},{4,6},{5,7},{6,4},{7,5},{8,10},{9,11},{10,... | collective-permute-start | bytes 811016 | tf_op jit(solution)/shard_map/ppermute | solution.py:297
  4.5 1.3 %shard_map.56 = (f32[264,256]{1,0:T(8,128)S(1)}, f32[528,128]{1,0:T(8,128)S(1)}, f32[528,128]{1,0:T(8,128)S(1)}, f32[264,128]{1,0:T(8,128)S(1)}, f32[264,128]{1,...) custom-call(f32[128,32,128]{2,1,0:T(8,128)S(1)} %bitcast.11, ...), custom_call_target="tpu_custom_call" | custom-call | bytes 200000000 | tf_op jit(solution)/shard_map/pallas_call | solution.py:321
  6.4 1.4 %collective-permute-start.6 = (f32[264,256]{1,0:T(8,128)S(1)}, f32[264,256]{1,0:T(8,128)S(1)}, u32[]{:S(2)}, u32[]{:S(2)}) collective-permute-start(f32[264,256]{1,0:T(8,128)S(1)} %get-tuple-element.43), channel_id=1, source_target_pairs={{0,3},{1,2},{2,1},{3,0},{4,7},{5,6},{6,5},{7,4},{8,11},{9,10},{10,... | collective-permute-start | bytes 811016 | tf_op jit(solution)/shard_map/ppermute | solution.py:297
  7.9 3.3 %collective-permute-done.4.refs_4_.refs_2_ = f32[264,256]{1,0:T(8,128)S(1)} collective-permute-done((f32[264,256]{1,0:T(8,128)S(1)}, f32[264,256]{1,0:T(8,128)S(1)}, u32[]{:S(2)}, u32[]{:S(2)}) %collective-permute-start.4) | collective-permute-done | bytes 270368 | tf_op jit(solution)/shard_map/ppermute | solution.py:297
  11.3 1.3 %collective-permute-start.5 = (f32[528,128]{1,0:T(8,128)S(1)}, f32[528,128]{1,0:T(8,128)S(1)}, u32[]{:S(2)}, u32[]{:S(2)}) collective-permute-start(f32[528,128]{1,0:T(8,128)S(1)} %get-tuple-element.41), channel_id=1, source_target_pairs={{0,2},{1,3},{2,0},{3,1},{4,6},{5,7},{6,4},{7,5},{8,10},{9,11},{10,... | collective-permute-start | bytes 811016 | tf_op jit(solution)/shard_map/ppermute | solution.py:297
  12.8 4.9 %collective-permute-done.6.refs_3_ = f32[264,256]{1,0:T(8,128)S(1)} collective-permute-done((f32[264,256]{1,0:T(8,128)S(1)}, f32[264,256]{1,0:T(8,128)S(1)}, u32[]{:S(2)}, u32[]{:S(2)}) %collective-permute-start.6) | collective-permute-done | bytes 270368 | tf_op jit(solution)/shard_map/ppermute | solution.py:297
  17.7 0.8 %shard_map.58 = (f32[2,352,256]{2,1,0:T(8,128)S(1)}, f32[352,256]{1,0:T(8,128)S(1)}, f32[352,256]{1,0:T(8,128)S(1)}, f32[352,16]{1,0:T(8,128)S(1)}) custom-call(f32[264,256]{1,0:T(8,128)S(1)} %get-tuple-element.42.refs_0_, f32[264,256]{1,0:T(8,128)S(1)} %collective-permute-done.refs_0_.refs_1_, f32[264,256]{1,0:T(8,128)S(1)} %collective-permute-done.4.refs_4_.refs_2_, ...), custom_call_target="tpu_custom_call" | custom-call | bytes 200000000 | tf_op jit(solution)/shard_map/pallas_call | solution.py:280
  18.5 3.1 %collective-permute-start.12 = (f32[352,256]{1,0:T(8,128)S(1)}, f32[352,256]{1,0:T(8,128)S(1)}, u32[]{:S(2)}, u32[]{:S(2)}) collective-permute-start(f32[352,256]{1,0:T(8,128)S(1)} %get-tuple-element.45.refs_9_.refs_2_), channel_id=1, source_target_pairs={{0,4},{4,8},{8,12},{12,16},{16,20},{20,24},{24,28},{1,5},{5,9},{9,... | collective-permute-start | bytes 1081352 | tf_op jit(solution)/shard_map/ppermute | solution.py:363
  21.7 3.1 %collective-permute-start.13 = (f32[352,256]{1,0:T(8,128)S(1)}, f32[352,256]{1,0:T(8,128)S(1)}, u32[]{:S(2)}, u32[]{:S(2)}) collective-permute-start(f32[352,256]{1,0:T(8,128)S(1)} %get-tuple-element.44.refs_8_.refs_1_), channel_id=1, source_target_pairs={{4,0},{8,4},{12,8},{16,12},{20,16},{24,20},{28,24},{5,1},{9,5},{13... | collective-permute-start | bytes 1081352 | tf_op jit(solution)/shard_map/ppermute | solution.py:364
  24.8 1.5 %shard_map.59 = (f32[256,128]{1,0:T(8,128)S(1)}, f32[256,128]{1,0:T(8,128)S(1)}, f32[512,128]{1,0:T(8,128)S(1)}, f32[2,352,128]{2,1,0:T(8,128)S(1)}) custom-call(f32[528,128]{1,0:T(8,128)S(1)} %get-tuple-element.34.refs_0_, f32[528,128]{1,0:T(8,128)S(1)} %collective-permute-done.1.refs_1_, f32[528,128]{1,0:T(8,128)S(1)} %collective-permute-done.5.refs_2_.refs_3_, ...), custom_call_target="tpu_custom_call" | custom-call | bytes 1024 | tf_op jit(solution)/shard_map/pallas_call | solution.py:280
  26.3 1.3 %collective-permute-start.7 = (f32[512,128]{1,0:T(8,128)S(1)}, f32[512,128]{1,0:T(8,128)S(1)}, u32[]{:S(2)}, u32[]{:S(2)}) collective-permute-start(f32[512,128]{1,0:T(8,128)S(1)} %get-tuple-element.46), channel_id=1, source_target_pairs={{0,2},{1,3},{2,0},{3,1},{4,6},{5,7},{6,4},{7,5},{8,10},{9,11},{10,... | collective-permute-start | bytes 786440 | tf_op jit(solution)/shard_map/ppermute | solution.py:297
  27.6 1.0 %collective-permute-done.9.refs_2_.refs_3_ = f32[528,128]{1,0:T(8,128)S(1)} collective-permute-done((f32[528,128]{1,0:T(8,128)S(1)}, f32[528,128]{1,0:T(8,128)S(1)}, u32[]{:S(2)}, u32[]{:S(2)}) %collective-permute-start.9) | collective-permute-done | bytes 270368 | tf_op jit(solution)/shard_map/ppermute | solution.py:297
  28.6 1.5 %shard_map.61 = (f32[256,128]{1,0:T(8,128)S(1)}, f32[256,128]{1,0:T(8,128)S(1)}, f32[512,128]{1,0:T(8,128)S(1)}, f32[2,352,128]{2,1,0:T(8,128)S(1)}) custom-call(f32[528,128]{1,0:T(8,128)S(1)} %get-tuple-element.34.refs_0_, f32[528,128]{1,0:T(8,128)S(1)} %collective-permute-done.1.refs_1_, f32[528,128]{1,0:T(8,128)S(1)} %collective-permute-done.9.refs_2_.refs_3_, ...), custom_call_target="tpu_custom_call" | custom-call | bytes 1024 | tf_op jit(solution)/shard_map/pallas_call | solution.py:280
  30.2 0.9 %collective-permute-start.14 = (f32[256,128]{1,0:T(8,128)S(1)}, f32[256,128]{1,0:T(8,128)S(1)}, u32[]{:S(2)}, u32[]{:S(2)}) collective-permute-start(f32[256,128]{1,0:T(8,128)S(1)} %get-tuple-element.54), channel_id=1, source_target_pairs={{0,1},{1,0},{2,3},{3,2},{4,5},{5,4},{6,7},{7,6},{8,9},{9,8},{10,11... | collective-permute-start | bytes 393224 | tf_op jit(solution)/shard_map/ppermute | solution.py:297
  31.1 1.3 %collective-permute-start.10 = (f32[512,128]{1,0:T(8,128)S(1)}, f32[512,128]{1,0:T(8,128)S(1)}, u32[]{:S(2)}, u32[]{:S(2)}) collective-permute-start(f32[512,128]{1,0:T(8,128)S(1)} %get-tuple-element.50), channel_id=1, source_target_pairs={{0,2},{1,3},{2,0},{3,1},{4,6},{5,7},{6,4},{7,5},{8,10},{9,11},{10,... | collective-permute-start | bytes 786440 | tf_op jit(solution)/shard_map/ppermute | solution.py:297
  32.4 7.1 %collective-permute-done.13.refs_5_ = f32[352,256]{1,0:T(8,128)S(1)} collective-permute-done((f32[352,256]{1,0:T(8,128)S(1)}, f32[352,256]{1,0:T(8,128)S(1)}, u32[]{:S(2)}, u32[]{:S(2)}) %collective-permute-start.13) | collective-permute-done | bytes 360480 | tf_op jit(solution)/shard_map/ppermute | solution.py:364
  39.4 1.4 %shard_map.62 = (f32[256,256]{1,0:T(8,128)S(1)}, f32[256,256]{1,0:T(8,128)S(1)}, f32[256,256]{1,0:T(8,128)S(1)}, f32[256,256]{1,0:T(8,128)S(1)}) custom-call(f32[2,352,256]{2,1,0:T(8,128)S(1)} %get-tuple-element.51.refs_0_, f32[352,256]{1,0:T(8,128)S(1)} %get-tuple-element.44.refs_8_.refs_1_, f32[352,256]{1,0:T(8,128)S(1)} %get-tuple-element.45.refs_9_.refs_2_, ...), custom_call_target="tpu_custom_call" | custom-call | bytes 200000000 | tf_op jit(solution)/shard_map/pallas_call | solution.py:280
  40.9 1.3 %collective-permute-start.16 = (f32[256,256]{1,0:T(8,128)S(1)}, f32[256,256]{1,0:T(8,128)S(1)}, u32[]{:S(2)}, u32[]{:S(2)}) collective-permute-start(f32[256,256]{1,0:T(8,128)S(1)} %get-tuple-element.59), channel_id=1, source_target_pairs={{0,2},{1,3},{2,0},{3,1},{4,6},{5,7},{6,4},{7,5},{8,10},{9,11},{10,... | collective-permute-start | bytes 786440 | tf_op jit(solution)/shard_map/ppermute | solution.py:297
  43.8 4.6 %collective-permute-done.16.refs_7_ = f32[256,256]{1,0:T(8,128)S(1)} collective-permute-done((f32[256,256]{1,0:T(8,128)S(1)}, f32[256,256]{1,0:T(8,128)S(1)}, u32[]{:S(2)}, u32[]{:S(2)}) %collective-permute-start.16) | collective-permute-done | bytes 262176 | tf_op jit(solution)/shard_map/ppermute | solution.py:297
  48.4 2.3 %shard_map.63.refs_3_ = f32[128,32,128]{2,1,0:T(8,128)} custom-call(f32[256,128]{1,0:T(8,128)S(1)} %get-tuple-element.56.refs_0_, f32[512,128]{1,0:T(8,128)S(1)} %collective-permute-done.7.refs_11_.refs_1_, f32[512,128]{1,0:T(8,128)S(1)} %collective-permute-done.8.refs_2_.refs_0_, f32[256,128]{1,0:T(8,128)S(1)} %get-tuple-element.57.refs_3_, ...), custom_call_target="tpu_custom_call" | custom-call | bytes 200000000 | tf_op jit(solution)/shard_map/pallas_call | solution.py:414
  50.8 3.9 %collective-permute-done.15.refs_2_ = f32[256,256]{1,0:T(8,128)S(1)} collective-permute-done((f32[256,256]{1,0:T(8,128)S(1)}, f32[256,256]{1,0:T(8,128)S(1)}, u32[]{:S(2)}, u32[]{:S(2)}) %collective-permute-start.15) | collective-permute-done | bytes 262176 | tf_op jit(solution)/shard_map/ppermute | solution.py:297
  54.6 0.9 %shard_map.64 = f32[128,32,128]{2,1,0:T(8,128)} custom-call(f32[512,128]{1,0:T(8,128)S(1)} %collective-permute-done.8.refs_2_.refs_0_, f32[256,128]{1,0:T(8,128)S(1)} %collective-permute-done.11.refs_1_, f32[256,256]{1,0:T(8,128)S(1)} %collective-permute-done.15.refs_2_, f32[128,32,128]{2,1,0:T(8,128)} %shard_map.63.refs_3_), custom_call_target="tpu_custom_call", output_to_operand_aliasing={{}: (3, {})} | custom-call | bytes 1024 | tf_op jit(solution)/shard_map/pallas_call | solution.py:414
  (34 shorter events, 3.4 us)
Async XLA Ops:
  0.0 1.6 %copy-start = (f32[128,4,1024]{2,1,0:T(4,128)S(1)}, f32[128,4,1024]{2,1,0:T(4,128)}, u32[]{:S(2)}) copy-start(f32[128,4,1024]{2,1,0:T(4,128)} %param.5) | copy-start | bytes 6291460
  2.4 15.3 %copy-start.2 = (bf16[2,2,176,384]{3,2,1,0:T(8,128)(2,1)S(1)}, bf16[2,2,176,384]{3,2,1,0:T(8,128)(2,1)}, u32[]{:S(2)}) copy-start(bf16[2,2,176,384]{3,2,1,0:T(8,128)(2,1)} %constant.6.clone.refs_4_) | copy-start | bytes 1622020
  2.4 15.3 %copy-start.3 = (s32[4,1024]{1,0:T(4,128)S(1)}, s32[4,1024]{1,0:T(4,128)}, u32[]{:S(2)}) copy-start(s32[4,1024]{1,0:T(4,128)} %refs_8_.1) | copy-start | bytes 49156
  2.4 15.2 %copy-start.4 = (f32[8,384]{1,0:T(8,128)S(1)}, f32[8,384]{1,0:T(8,128)}, u32[]{:S(2)}) copy-start(f32[8,384]{1,0:T(8,128)} %constant.8.clone.refs_5_.refs_6_.refs_7_) | copy-start | bytes 36868
  2.5 2.0 %collective-permute-start = (f32[264,256]{1,0:T(8,128)S(1)}, f32[264,256]{1,0:T(8,128)S(1)}, u32[]{:S(2)}, u32[]{:S(2)}) collective-permute-start(f32[264,256]{1,0:T(8,128)S(1)} %get-tuple-element.33), channel_id=1, source_target_pairs={{0,1},{1,0},{2,3},{3,2},{4,5},{5,4},{6,7},{7,6},{8,9},{9,8},{10,11... | collective-permute-start | bytes 811016 | tf_op jit(solution)/shard_map/ppermute | solution.py:297
  3.2 21.5 %copy-start.1 = (bf16[2,2,128,528]{3,2,1,0:T(8,128)(2,1)S(1)}, bf16[2,2,128,528]{3,2,1,0:T(8,128)(2,1)}, u32[]{:S(2)}) copy-start(bf16[2,2,128,528]{3,2,1,0:T(8,128)(2,1)} %constant.7.clone.refs_5_.refs_6_) | copy-start | bytes 1622020
  3.2 8.0 %collective-permute-start.4 = (f32[264,256]{1,0:T(8,128)S(1)}, f32[264,256]{1,0:T(8,128)S(1)}, u32[]{:S(2)}, u32[]{:S(2)}) collective-permute-start(f32[264,256]{1,0:T(8,128)S(1)} %get-tuple-element.40), channel_id=1, source_target_pairs={{0,2},{1,3},{2,0},{3,1},{4,6},{5,7},{6,4},{7,5},{8,10},{9,11},{10,... | collective-permute-start | bytes 811016 | tf_op jit(solution)/shard_map/ppermute | solution.py:297
  5.8 5.5 %collective-permute-start.2 = (f32[264,128]{1,0:T(8,128)S(1)}, f32[264,128]{1,0:T(8,128)S(1)}, u32[]{:S(2)}, u32[]{:S(2)}) collective-permute-start(f32[264,128]{1,0:T(8,128)S(1)} %get-tuple-element.37), channel_id=1, source_target_pairs={{0,1},{1,0},{2,3},{3,2},{4,5},{5,4},{6,7},{7,6},{8,9},{9,8},{10,11... | collective-permute-start | bytes 405512 | tf_op jit(solution)/shard_map/ppermute | solution.py:297
  6.2 5.0 %collective-permute-start.3 = (f32[264,128]{1,0:T(8,128)S(1)}, f32[264,128]{1,0:T(8,128)S(1)}, u32[]{:S(2)}, u32[]{:S(2)}) collective-permute-start(f32[264,128]{1,0:T(8,128)S(1)} %get-tuple-element.39), channel_id=1, source_target_pairs={{0,1},{1,0},{2,3},{3,2},{4,5},{5,4},{6,7},{7,6},{8,9},{9,8},{10,11... | collective-permute-start | bytes 405512 | tf_op jit(solution)/shard_map/ppermute | solution.py:297
  6.4 11.3 %collective-permute-start.6 = (f32[264,256]{1,0:T(8,128)S(1)}, f32[264,256]{1,0:T(8,128)S(1)}, u32[]{:S(2)}, u32[]{:S(2)}) collective-permute-start(f32[264,256]{1,0:T(8,128)S(1)} %get-tuple-element.43), channel_id=1, source_target_pairs={{0,3},{1,2},{2,1},{3,0},{4,7},{5,6},{6,5},{7,4},{8,11},{9,10},{10,... | collective-permute-start | bytes 811016 | tf_op jit(solution)/shard_map/ppermute | solution.py:297
  7.8 16.9 %collective-permute-start.1 = (f32[528,128]{1,0:T(8,128)S(1)}, f32[528,128]{1,0:T(8,128)S(1)}, u32[]{:S(2)}, u32[]{:S(2)}) collective-permute-start(f32[528,128]{1,0:T(8,128)S(1)} %get-tuple-element.35), channel_id=1, source_target_pairs={{0,1},{1,0},{2,3},{3,2},{4,5},{5,4},{6,7},{7,6},{8,9},{9,8},{10,11... | collective-permute-start | bytes 811016 | tf_op jit(solution)/shard_map/ppermute | solution.py:297
  11.3 13.4 %collective-permute-start.5 = (f32[528,128]{1,0:T(8,128)S(1)}, f32[528,128]{1,0:T(8,128)S(1)}, u32[]{:S(2)}, u32[]{:S(2)}) collective-permute-start(f32[528,128]{1,0:T(8,128)S(1)} %get-tuple-element.41), channel_id=1, source_target_pairs={{0,2},{1,3},{2,0},{3,1},{4,6},{5,7},{6,4},{7,5},{8,10},{9,11},{10,... | collective-permute-start | bytes 811016 | tf_op jit(solution)/shard_map/ppermute | solution.py:297
  12.6 16.0 %collective-permute-start.9 = (f32[528,128]{1,0:T(8,128)S(1)}, f32[528,128]{1,0:T(8,128)S(1)}, u32[]{:S(2)}, u32[]{:S(2)}) collective-permute-start(f32[528,128]{1,0:T(8,128)S(1)} %get-tuple-element.48), channel_id=1, source_target_pairs={{0,2},{1,3},{2,0},{3,1},{4,6},{5,7},{6,4},{7,5},{8,10},{9,11},{10,... | collective-permute-start | bytes 811016 | tf_op jit(solution)/shard_map/ppermute | solution.py:297
  18.5 13.8 %collective-permute-start.12 = (f32[352,256]{1,0:T(8,128)S(1)}, f32[352,256]{1,0:T(8,128)S(1)}, u32[]{:S(2)}, u32[]{:S(2)}) collective-permute-start(f32[352,256]{1,0:T(8,128)S(1)} %get-tuple-element.45.refs_9_.refs_2_), channel_id=1, source_target_pairs={{0,4},{4,8},{8,12},{12,16},{16,20},{20,24},{24,28},{1,5},{5,9},{9,... | collective-permute-start | bytes 1081352 | tf_op jit(solution)/shard_map/ppermute | solution.py:363
  21.7 17.8 %collective-permute-start.13 = (f32[352,256]{1,0:T(8,128)S(1)}, f32[352,256]{1,0:T(8,128)S(1)}, u32[]{:S(2)}, u32[]{:S(2)}) collective-permute-start(f32[352,256]{1,0:T(8,128)S(1)} %get-tuple-element.44.refs_8_.refs_1_), channel_id=1, source_target_pairs={{4,0},{8,4},{12,8},{16,12},{20,16},{24,20},{28,24},{5,1},{9,5},{13... | collective-permute-start | bytes 1081352 | tf_op jit(solution)/shard_map/ppermute | solution.py:364
  26.3 13.1 %collective-permute-start.7 = (f32[512,128]{1,0:T(8,128)S(1)}, f32[512,128]{1,0:T(8,128)S(1)}, u32[]{:S(2)}, u32[]{:S(2)}) collective-permute-start(f32[512,128]{1,0:T(8,128)S(1)} %get-tuple-element.46), channel_id=1, source_target_pairs={{0,2},{1,3},{2,0},{3,1},{4,6},{5,7},{6,4},{7,5},{8,10},{9,11},{10,... | collective-permute-start | bytes 786440 | tf_op jit(solution)/shard_map/ppermute | solution.py:297
  30.2 9.3 %collective-permute-start.14 = (f32[256,128]{1,0:T(8,128)S(1)}, f32[256,128]{1,0:T(8,128)S(1)}, u32[]{:S(2)}, u32[]{:S(2)}) collective-permute-start(f32[256,128]{1,0:T(8,128)S(1)} %get-tuple-element.54), channel_id=1, source_target_pairs={{0,1},{1,0},{2,3},{3,2},{4,5},{5,4},{6,7},{7,6},{8,9},{9,8},{10,11... | collective-permute-start | bytes 393224 | tf_op jit(solution)/shard_map/ppermute | solution.py:297
  31.1 12.6 %collective-permute-start.10 = (f32[512,128]{1,0:T(8,128)S(1)}, f32[512,128]{1,0:T(8,128)S(1)}, u32[]{:S(2)}, u32[]{:S(2)}) collective-permute-start(f32[512,128]{1,0:T(8,128)S(1)} %get-tuple-element.50), channel_id=1, source_target_pairs={{0,2},{1,3},{2,0},{3,1},{4,6},{5,7},{6,4},{7,5},{8,10},{9,11},{10,... | collective-permute-start | bytes 786440 | tf_op jit(solution)/shard_map/ppermute | solution.py:297
  40.9 7.5 %collective-permute-start.16 = (f32[256,256]{1,0:T(8,128)S(1)}, f32[256,256]{1,0:T(8,128)S(1)}, u32[]{:S(2)}, u32[]{:S(2)}) collective-permute-start(f32[256,256]{1,0:T(8,128)S(1)} %get-tuple-element.59), channel_id=1, source_target_pairs={{0,2},{1,3},{2,0},{3,1},{4,6},{5,7},{6,4},{7,5},{8,10},{9,11},{10,... | collective-permute-start | bytes 786440 | tf_op jit(solution)/shard_map/ppermute | solution.py:297
  42.2 6.2 %collective-permute-start.17 = (f32[256,256]{1,0:T(8,128)S(1)}, f32[256,256]{1,0:T(8,128)S(1)}, u32[]{:S(2)}, u32[]{:S(2)}) collective-permute-start(f32[256,256]{1,0:T(8,128)S(1)} %get-tuple-element.60), channel_id=1, source_target_pairs={{0,1},{1,0},{2,3},{3,2},{4,5},{5,4},{6,7},{7,6},{8,9},{9,8},{10,11... | collective-permute-start | bytes 786440 | tf_op jit(solution)/shard_map/ppermute | solution.py:297
  43.0 5.4 %collective-permute-start.8 = (f32[512,128]{1,0:T(8,128)S(1)}, f32[512,128]{1,0:T(8,128)S(1)}, u32[]{:S(2)}, u32[]{:S(2)}) collective-permute-start(f32[512,128]{1,0:T(8,128)S(1)} %shard_map.60), channel_id=1, source_target_pairs={{0,1},{1,0},{2,3},{3,2},{4,5},{5,4},{6,7},{7,6},{8,9},{9,8},{10,11... | collective-permute-start | bytes 786440 | tf_op jit(solution)/shard_map/ppermute | solution.py:297
  43.0 11.6 %collective-permute-start.15 = (f32[256,256]{1,0:T(8,128)S(1)}, f32[256,256]{1,0:T(8,128)S(1)}, u32[]{:S(2)}, u32[]{:S(2)}) collective-permute-start(f32[256,256]{1,0:T(8,128)S(1)} %get-tuple-element.55), channel_id=1, source_target_pairs={{0,3},{1,2},{2,1},{3,0},{4,7},{5,6},{6,5},{7,4},{8,11},{9,10},{10,... | collective-permute-start | bytes 786440 | tf_op jit(solution)/shard_map/ppermute | solution.py:297
  43.7 7.1 %collective-permute-start.11 = (f32[256,128]{1,0:T(8,128)S(1)}, f32[256,128]{1,0:T(8,128)S(1)}, u32[]{:S(2)}, u32[]{:S(2)}) collective-permute-start(f32[256,128]{1,0:T(8,128)S(1)} %slice.9), channel_id=1, source_target_pairs={{0,1},{1,0},{2,3},{3,2},{4,5},{5,4},{6,7},{7,6},{8,9},{9,8},{10,11... | collective-permute-start | bytes 393224 | tf_op jit(solution)/shard_map/ppermute | solution.py:297

commit v11 on v10

--- a/solution.py
+++ b/solution.py
@@ -317,7 +317,7 @@
     source = source.reshape(cells, lines, LANES)
     scratch = [pltpu.VMEM((cells * (lines + 8), LANES), jnp.float32), pltpu.SemaphoreType.DMA((SPLIT,))]
 
-    def pack(jobs, shapes, *earlier):
+    def pack(source, jobs, shapes, *earlier):
         return pl.pallas_call(
             functools.partial(pack_kernel, jobs, row_count, cells, len(earlier)),
             out_shape=[jax.ShapeDtypeStruct(shape, jnp.float32) for shape in shapes],
@@ -330,7 +330,8 @@
 
     edge_size, size = len(edges) * cells + 8, len(inner) * cells + 8
     jobs = [(d - 1, 0, d, edges, 0, tiles) for d in range(1, count)]
-    edge_blocks = [swap(block, d) for d, block in enumerate(pack(jobs, [(edge_size, width)] * (count - 1)), 1)]
+    packed = pack(pltpu.with_memory_space_constraint(source, pltpu.HBM), jobs, [(edge_size, width)] * (count - 1))
+    edge_blocks = [swap(block, d) for d, block in enumerate(packed, 1)]
     jobs, shapes = [(0, 0, 0, edges, 0, tiles)], [(edge_size, width)]
 
     def add(d, wanted):
@@ -344,7 +345,7 @@
     for part in range(parts):
         for d in far:
             add(d, [part])
-    packed = pack(jobs, shapes, *edge_blocks[: half - 1])
+    packed = pack(source, jobs, shapes, packed[half - 1])
     edge_blocks = [packed[0], *edge_blocks]
     near_blocks = [packed[1]] + [swap(packed[1 + d], d) for d in near]
     messages = []

time: 55.7 us -> 55.1 us (0.989)
  local copies, waits for them, and re-layouts: 1.63 us -> 0.05 us
  Pallas kernels: 10.8 us -> 11.8 us
    unnamed x10, local copies, waits for them, and re-layouts: 1.61 us -> 0.03 us
    pallas_call x2, Pallas kernels: 2.15 us -> 3.22 us  [pack(): pl.pallas_call(functools.partial(pack_kernel, jobs, row_count, cells, len...]
    ppermute x1, waiting for transfers between devices: 7.08 us -> 7.77 us  [local(): high = lax.ppermute(first, 'plane', down)]
where the time goes in v11:
time: 55.1 us; the launch traced here: 55 us
  waiting for transfers between devices  25.2 us (46%)
  starting transfers between devices  17.8 us (32%)
  Pallas kernels  11.8 us (21%)
    ppermute x16, waiting for transfers between devices, swap(): lax.ppermute(block, 'span', [(i, i ^ d) for i in range(lax.axis_size('spa...  17.4 us
    ppermute x16, starting transfers between devices, swap(): lax.ppermute(block, 'span', [(i, i ^ d) for i in range(lax.axis_size('spa...  11.6 us
    ppermute x1, waiting for transfers between devices, local(): high = lax.ppermute(first, 'plane', down)  7.77 us
    pallas_call x6, Pallas kernels, call(): pl.pallas_call(kernel, out_shape=shapes, in_specs=[VMEM] * len(args) + [A...  5.33 us
    pallas_call x2, Pallas kernels, local(): pl.pallas_call(functools.partial(unpack_kernel, [piece[1:] for piece in c...  3.25 us
    pallas_call x2, Pallas kernels, pack(): pl.pallas_call(functools.partial(pack_kernel, jobs, row_count, cells, len...  3.22 us
    ppermute x1, starting transfers between devices, local(): low = lax.ppermute(last, 'plane', up)  3.12 us
    ppermute x1, starting transfers between devices, local(): high = lax.ppermute(first, 'plane', down)  3.06 us
  transfers between devices with their start and end apart: 18, of which 6 were waited for; matrix products, arithmetic and copies ran while one was open for 0% of the time, Pallas kernels for 16%

profile of v11, /device:TPU:25, one launch (start us, length us, event | category | flops | bytes accessed | tf_op | source)
XLA Modules:
  0.0 55.0 jit_solution(5182891866994067174)
XLA Ops:
  0.0 1.9 %shard_map.55 = (f32[264,256]{1,0:T(8,128)S(1)}, f32[264,256]{1,0:T(8,128)S(1)}, f32[264,256]{1,0:T(8,128)S(1)}) custom-call(f32[128,32,128]{2,1,0:T(8,128)} %bitcast.10), custom_call_target="tpu_custom_call" | custom-call | bytes 200000000 | tf_op jit(solution)/shard_map/pallas_call | solution.py:321
  2.0 1.3 %collective-permute-start.3 = (f32[264,256]{1,0:T(8,128)S(1)}, f32[264,256]{1,0:T(8,128)S(1)}, u32[]{:S(2)}, u32[]{:S(2)}) collective-permute-start(f32[264,256]{1,0:T(8,128)S(1)} %get-tuple-element.33.refs_0_), channel_id=1, source_target_pairs={{0,2},{1,3},{2,0},{3,1},{4,6},{5,7},{6,4},{7,5},{8,10},{9,11},{10,... | collective-permute-start | bytes 811016 | tf_op jit(solution)/shard_map/ppermute | solution.py:297
  3.3 1.3 %shard_map.56 = (f32[264,256]{1,0:T(8,128)S(1)}, f32[528,128]{1,0:T(8,128)S(1)}, f32[528,128]{1,0:T(8,128)S(1)}, f32[264,128]{1,0:T(8,128)S(1)}, f32[264,128]{1,...) custom-call(f32[128,32,128]{2,1,0:T(8,128)S(1)} %bitcast.11, f32[264,256]{1,0:T(8,128)S(1)} %get-tuple-element.33.refs_0_), custom_call_target="tpu_custom_call" | custom-call | bytes 200000000 | tf_op jit(solution)/shard_map/pallas_call | solution.py:321
  4.6 1.0 %collective-permute-start.1 = (f32[264,128]{1,0:T(8,128)S(1)}, f32[264,128]{1,0:T(8,128)S(1)}, u32[]{:S(2)}, u32[]{:S(2)}) collective-permute-start(f32[264,128]{1,0:T(8,128)S(1)} %get-tuple-element.37), channel_id=1, source_target_pairs={{0,1},{1,0},{2,3},{3,2},{4,5},{5,4},{6,7},{7,6},{8,9},{9,8},{10,11... | collective-permute-start | bytes 405512 | tf_op jit(solution)/shard_map/ppermute | solution.py:297
  7.0 2.4 %collective-permute-done.3.refs_4_.refs_2_ = f32[264,256]{1,0:T(8,128)S(1)} collective-permute-done((f32[264,256]{1,0:T(8,128)S(1)}, f32[264,256]{1,0:T(8,128)S(1)}, u32[]{:S(2)}, u32[]{:S(2)}) %collective-permute-start.3) | collective-permute-done | bytes 270368 | tf_op jit(solution)/shard_map/ppermute | solution.py:297
  9.4 1.3 %collective-permute-start.4 = (f32[528,128]{1,0:T(8,128)S(1)}, f32[528,128]{1,0:T(8,128)S(1)}, u32[]{:S(2)}, u32[]{:S(2)}) collective-permute-start(f32[528,128]{1,0:T(8,128)S(1)} %get-tuple-element.40), channel_id=1, source_target_pairs={{0,2},{1,3},{2,0},{3,1},{4,6},{5,7},{6,4},{7,5},{8,10},{9,11},{10,... | collective-permute-start | bytes 811016 | tf_op jit(solution)/shard_map/ppermute | solution.py:297
  10.9 6.2 %collective-permute-done.6.refs_3_ = f32[264,256]{1,0:T(8,128)S(1)} collective-permute-done((f32[264,256]{1,0:T(8,128)S(1)}, f32[264,256]{1,0:T(8,128)S(1)}, u32[]{:S(2)}, u32[]{:S(2)}) %collective-permute-start.6) | collective-permute-done | bytes 270368 | tf_op jit(solution)/shard_map/ppermute | solution.py:297
  17.2 0.8 %shard_map.58 = (f32[2,352,256]{2,1,0:T(8,128)S(1)}, f32[352,256]{1,0:T(8,128)S(1)}, f32[352,256]{1,0:T(8,128)S(1)}, f32[352,16]{1,0:T(8,128)S(1)}) custom-call(f32[264,256]{1,0:T(8,128)S(1)} %get-tuple-element.41.refs_0_, f32[264,256]{1,0:T(8,128)S(1)} %collective-permute-done.5.refs_1_, f32[264,256]{1,0:T(8,128)S(1)} %collective-permute-done.3.refs_4_.refs_2_, ...), custom_call_target="tpu_custom_call" | custom-call | bytes 200000000 | tf_op jit(solution)/shard_map/pallas_call | solution.py:280
  18.0 3.1 %collective-permute-start.12 = (f32[352,256]{1,0:T(8,128)S(1)}, f32[352,256]{1,0:T(8,128)S(1)}, u32[]{:S(2)}, u32[]{:S(2)}) collective-permute-start(f32[352,256]{1,0:T(8,128)S(1)} %get-tuple-element.45.refs_9_.refs_2_), channel_id=1, source_target_pairs={{0,4},{4,8},{8,12},{12,16},{16,20},{20,24},{24,28},{1,5},{5,9},{9,... | collective-permute-start | bytes 1081352 | tf_op jit(solution)/shard_map/ppermute | solution.py:364
  21.1 3.1 %collective-permute-start.13 = (f32[352,256]{1,0:T(8,128)S(1)}, f32[352,256]{1,0:T(8,128)S(1)}, u32[]{:S(2)}, u32[]{:S(2)}) collective-permute-start(f32[352,256]{1,0:T(8,128)S(1)} %get-tuple-element.44.refs_8_.refs_1_), channel_id=1, source_target_pairs={{4,0},{8,4},{12,8},{16,12},{20,16},{24,20},{28,24},{5,1},{9,5},{13... | collective-permute-start | bytes 1081352 | tf_op jit(solution)/shard_map/ppermute | solution.py:365
  24.2 1.5 %shard_map.59 = (f32[256,128]{1,0:T(8,128)S(1)}, f32[256,128]{1,0:T(8,128)S(1)}, f32[512,128]{1,0:T(8,128)S(1)}, f32[2,352,128]{2,1,0:T(8,128)S(1)}) custom-call(f32[528,128]{1,0:T(8,128)S(1)} %get-tuple-element.34.refs_0_, f32[528,128]{1,0:T(8,128)S(1)} %collective-permute-done.refs_1_, f32[528,128]{1,0:T(8,128)S(1)} %collective-permute-done.4.refs_2_.refs_3_, ...), custom_call_target="tpu_custom_call" | custom-call | bytes 1024 | tf_op jit(solution)/shard_map/pallas_call | solution.py:280
  25.8 1.3 %collective-permute-start.7 = (f32[512,128]{1,0:T(8,128)S(1)}, f32[512,128]{1,0:T(8,128)S(1)}, u32[]{:S(2)}, u32[]{:S(2)}) collective-permute-start(f32[512,128]{1,0:T(8,128)S(1)} %get-tuple-element.46), channel_id=1, source_target_pairs={{0,2},{1,3},{2,0},{3,1},{4,6},{5,7},{6,4},{7,5},{8,10},{9,11},{10,... | collective-permute-start | bytes 786440 | tf_op jit(solution)/shard_map/ppermute | solution.py:297
  27.1 1.5 %shard_map.61 = (f32[256,128]{1,0:T(8,128)S(1)}, f32[256,128]{1,0:T(8,128)S(1)}, f32[512,128]{1,0:T(8,128)S(1)}, f32[2,352,128]{2,1,0:T(8,128)S(1)}) custom-call(f32[528,128]{1,0:T(8,128)S(1)} %get-tuple-element.34.refs_0_, f32[528,128]{1,0:T(8,128)S(1)} %collective-permute-done.refs_1_, f32[528,128]{1,0:T(8,128)S(1)} %collective-permute-done.9.refs_2_.refs_3_, ...), custom_call_target="tpu_custom_call" | custom-call | bytes 1024 | tf_op jit(solution)/shard_map/pallas_call | solution.py:280
  28.6 1.3 %collective-permute-start.14 = (f32[256,128]{1,0:T(8,128)S(1)}, f32[256,128]{1,0:T(8,128)S(1)}, u32[]{:S(2)}, u32[]{:S(2)}) collective-permute-start(f32[256,128]{1,0:T(8,128)S(1)} %get-tuple-element.54), channel_id=1, source_target_pairs={{0,1},{1,0},{2,3},{3,2},{4,5},{5,4},{6,7},{7,6},{8,9},{9,8},{10,11... | collective-permute-start | bytes 393224 | tf_op jit(solution)/shard_map/ppermute | solution.py:297
  29.9 1.2 %collective-permute-start.10 = (f32[512,128]{1,0:T(8,128)S(1)}, f32[512,128]{1,0:T(8,128)S(1)}, u32[]{:S(2)}, u32[]{:S(2)}) collective-permute-start(f32[512,128]{1,0:T(8,128)S(1)} %get-tuple-element.50), channel_id=1, source_target_pairs={{0,2},{1,3},{2,0},{3,1},{4,6},{5,7},{6,4},{7,5},{8,10},{9,11},{10,... | collective-permute-start | bytes 786440 | tf_op jit(solution)/shard_map/ppermute | solution.py:297
  31.1 7.8 %collective-permute-done.13.refs_5_ = f32[352,256]{1,0:T(8,128)S(1)} collective-permute-done((f32[352,256]{1,0:T(8,128)S(1)}, f32[352,256]{1,0:T(8,128)S(1)}, u32[]{:S(2)}, u32[]{:S(2)}) %collective-permute-start.13) | collective-permute-done | bytes 360480 | tf_op jit(solution)/shard_map/ppermute | solution.py:365
  38.9 1.4 %shard_map.62 = (f32[256,256]{1,0:T(8,128)S(1)}, f32[256,256]{1,0:T(8,128)S(1)}, f32[256,256]{1,0:T(8,128)S(1)}, f32[256,256]{1,0:T(8,128)S(1)}) custom-call(f32[2,352,256]{2,1,0:T(8,128)S(1)} %get-tuple-element.51.refs_0_, f32[352,256]{1,0:T(8,128)S(1)} %get-tuple-element.44.refs_8_.refs_1_, f32[352,256]{1,0:T(8,128)S(1)} %get-tuple-element.45.refs_9_.refs_2_, ...), custom_call_target="tpu_custom_call" | custom-call | bytes 200000000 | tf_op jit(solution)/shard_map/pallas_call | solution.py:280
  40.3 0.5 collective-permute-start.16
  40.9 0.6 %collective-permute-start.17 = (f32[256,256]{1,0:T(8,128)S(1)}, f32[256,256]{1,0:T(8,128)S(1)}, u32[]{:S(2)}, u32[]{:S(2)}) collective-permute-start(f32[256,256]{1,0:T(8,128)S(1)} %get-tuple-element.60), channel_id=1, source_target_pairs={{0,1},{1,0},{2,3},{3,2},{4,5},{5,4},{6,7},{7,6},{8,9},{9,8},{10,11... | collective-permute-start | bytes 786440 | tf_op jit(solution)/shard_map/ppermute | solution.py:297
  41.6 1.5 %collective-permute-start.15 = (f32[256,256]{1,0:T(8,128)S(1)}, f32[256,256]{1,0:T(8,128)S(1)}, u32[]{:S(2)}, u32[]{:S(2)}) collective-permute-start(f32[256,256]{1,0:T(8,128)S(1)} %get-tuple-element.55), channel_id=1, source_target_pairs={{0,3},{1,2},{2,1},{3,0},{4,7},{5,6},{6,5},{7,4},{8,11},{9,10},{10,... | collective-permute-start | bytes 786440 | tf_op jit(solution)/shard_map/ppermute | solution.py:297
  43.3 4.6 %collective-permute-done.16.refs_7_ = f32[256,256]{1,0:T(8,128)S(1)} collective-permute-done((f32[256,256]{1,0:T(8,128)S(1)}, f32[256,256]{1,0:T(8,128)S(1)}, u32[]{:S(2)}, u32[]{:S(2)}) %collective-permute-start.16) | collective-permute-done | bytes 262176 | tf_op jit(solution)/shard_map/ppermute | solution.py:297
  47.9 2.3 %shard_map.63.refs_3_ = f32[128,32,128]{2,1,0:T(8,128)} custom-call(f32[256,128]{1,0:T(8,128)S(1)} %get-tuple-element.56.refs_0_, f32[512,128]{1,0:T(8,128)S(1)} %collective-permute-done.7.refs_11_.refs_1_, f32[512,128]{1,0:T(8,128)S(1)} %collective-permute-done.8.refs_2_.refs_0_, f32[256,128]{1,0:T(8,128)S(1)} %get-tuple-element.57.refs_3_, ...), custom_call_target="tpu_custom_call" | custom-call | bytes 200000000 | tf_op jit(solution)/shard_map/pallas_call | solution.py:415
  50.2 3.8 %collective-permute-done.15.refs_2_ = f32[256,256]{1,0:T(8,128)S(1)} collective-permute-done((f32[256,256]{1,0:T(8,128)S(1)}, f32[256,256]{1,0:T(8,128)S(1)}, u32[]{:S(2)}, u32[]{:S(2)}) %collective-permute-start.15) | collective-permute-done | bytes 262176 | tf_op jit(solution)/shard_map/ppermute | solution.py:297
  54.1 0.9 %shard_map.64 = f32[128,32,128]{2,1,0:T(8,128)} custom-call(f32[512,128]{1,0:T(8,128)S(1)} %collective-permute-done.8.refs_2_.refs_0_, f32[256,128]{1,0:T(8,128)S(1)} %collective-permute-done.11.refs_1_, f32[256,256]{1,0:T(8,128)S(1)} %collective-permute-done.15.refs_2_, f32[128,32,128]{2,1,0:T(8,128)} %shard_map.63.refs_3_), custom_call_target="tpu_custom_call", output_to_operand_aliasing={{}: (3, {})} | custom-call | bytes 1024 | tf_op jit(solution)/shard_map/pallas_call | solution.py:415
  (34 shorter events, 1.9 us)
Async XLA Ops:
  0.0 3.3 %copy-start = (f32[128,4,1024]{2,1,0:T(4,128)S(1)}, f32[128,4,1024]{2,1,0:T(4,128)}, u32[]{:S(2)}) copy-start(f32[128,4,1024]{2,1,0:T(4,128)} %param.5) | copy-start | bytes 6291460
  1.9 15.3 %copy-start.2 = (bf16[2,2,176,384]{3,2,1,0:T(8,128)(2,1)S(1)}, bf16[2,2,176,384]{3,2,1,0:T(8,128)(2,1)}, u32[]{:S(2)}) copy-start(bf16[2,2,176,384]{3,2,1,0:T(8,128)(2,1)} %constant.6.clone.refs_4_) | copy-start | bytes 1622020
  1.9 15.3 %copy-start.3 = (s32[4,1024]{1,0:T(4,128)S(1)}, s32[4,1024]{1,0:T(4,128)}, u32[]{:S(2)}) copy-start(s32[4,1024]{1,0:T(4,128)} %refs_8_.1) | copy-start | bytes 49156
  1.9 15.2 %copy-start.4 = (f32[8,384]{1,0:T(8,128)S(1)}, f32[8,384]{1,0:T(8,128)}, u32[]{:S(2)}) copy-start(f32[8,384]{1,0:T(8,128)} %constant.8.clone.refs_5_.refs_6_.refs_7_) | copy-start | bytes 36868
  1.9 22.3 %copy-start.1 = (bf16[2,2,128,528]{3,2,1,0:T(8,128)(2,1)S(1)}, bf16[2,2,128,528]{3,2,1,0:T(8,128)(2,1)}, u32[]{:S(2)}) copy-start(bf16[2,2,128,528]{3,2,1,0:T(8,128)(2,1)} %constant.7.clone.refs_5_.refs_6_) | copy-start | bytes 1622020
  2.0 7.4 %collective-permute-start.3 = (f32[264,256]{1,0:T(8,128)S(1)}, f32[264,256]{1,0:T(8,128)S(1)}, u32[]{:S(2)}, u32[]{:S(2)}) collective-permute-start(f32[264,256]{1,0:T(8,128)S(1)} %get-tuple-element.33.refs_0_), channel_id=1, source_target_pairs={{0,2},{1,3},{2,0},{3,1},{4,6},{5,7},{6,4},{7,5},{8,10},{9,11},{10,... | collective-permute-start | bytes 811016 | tf_op jit(solution)/shard_map/ppermute | solution.py:297
  4.6 2.0 %collective-permute-start.1 = (f32[264,128]{1,0:T(8,128)S(1)}, f32[264,128]{1,0:T(8,128)S(1)}, u32[]{:S(2)}, u32[]{:S(2)}) collective-permute-start(f32[264,128]{1,0:T(8,128)S(1)} %get-tuple-element.37), channel_id=1, source_target_pairs={{0,1},{1,0},{2,3},{3,2},{4,5},{5,4},{6,7},{7,6},{8,9},{9,8},{10,11... | collective-permute-start | bytes 405512 | tf_op jit(solution)/shard_map/ppermute | solution.py:297
  5.6 1.4 %collective-permute-start.2 = (f32[264,128]{1,0:T(8,128)S(1)}, f32[264,128]{1,0:T(8,128)S(1)}, u32[]{:S(2)}, u32[]{:S(2)}) collective-permute-start(f32[264,128]{1,0:T(8,128)S(1)} %get-tuple-element.39), channel_id=1, source_target_pairs={{0,1},{1,0},{2,3},{3,2},{4,5},{5,4},{6,7},{7,6},{8,9},{9,8},{10,11... | collective-permute-start | bytes 405512 | tf_op jit(solution)/shard_map/ppermute | solution.py:297
  5.7 5.2 %collective-permute-start.5 = (f32[264,256]{1,0:T(8,128)S(1)}, f32[264,256]{1,0:T(8,128)S(1)}, u32[]{:S(2)}, u32[]{:S(2)}) collective-permute-start(f32[264,256]{1,0:T(8,128)S(1)} %get-tuple-element.42), channel_id=1, source_target_pairs={{0,1},{1,0},{2,3},{3,2},{4,5},{5,4},{6,7},{7,6},{8,9},{9,8},{10,11... | collective-permute-start | bytes 811016 | tf_op jit(solution)/shard_map/ppermute | solution.py:297
  6.1 11.0 %collective-permute-start.6 = (f32[264,256]{1,0:T(8,128)S(1)}, f32[264,256]{1,0:T(8,128)S(1)}, u32[]{:S(2)}, u32[]{:S(2)}) collective-permute-start(f32[264,256]{1,0:T(8,128)S(1)} %get-tuple-element.43), channel_id=1, source_target_pairs={{0,3},{1,2},{2,1},{3,0},{4,7},{5,6},{6,5},{7,4},{8,11},{9,10},{10,... | collective-permute-start | bytes 811016 | tf_op jit(solution)/shard_map/ppermute | solution.py:297
  6.6 17.6 %collective-permute-start = (f32[528,128]{1,0:T(8,128)S(1)}, f32[528,128]{1,0:T(8,128)S(1)}, u32[]{:S(2)}, u32[]{:S(2)}) collective-permute-start(f32[528,128]{1,0:T(8,128)S(1)} %get-tuple-element.35), channel_id=1, source_target_pairs={{0,1},{1,0},{2,3},{3,2},{4,5},{5,4},{6,7},{7,6},{8,9},{9,8},{10,11... | collective-permute-start | bytes 811016 | tf_op jit(solution)/shard_map/ppermute | solution.py:297
  9.4 14.8 %collective-permute-start.4 = (f32[528,128]{1,0:T(8,128)S(1)}, f32[528,128]{1,0:T(8,128)S(1)}, u32[]{:S(2)}, u32[]{:S(2)}) collective-permute-start(f32[528,128]{1,0:T(8,128)S(1)} %get-tuple-element.40), channel_id=1, source_target_pairs={{0,2},{1,3},{2,0},{3,1},{4,6},{5,7},{6,4},{7,5},{8,10},{9,11},{10,... | collective-permute-start | bytes 811016 | tf_op jit(solution)/shard_map/ppermute | solution.py:297
  10.7 16.4 %collective-permute-start.9 = (f32[528,128]{1,0:T(8,128)S(1)}, f32[528,128]{1,0:T(8,128)S(1)}, u32[]{:S(2)}, u32[]{:S(2)}) collective-permute-start(f32[528,128]{1,0:T(8,128)S(1)} %get-tuple-element.48), channel_id=1, source_target_pairs={{0,2},{1,3},{2,0},{3,1},{4,6},{5,7},{6,4},{7,5},{8,10},{9,11},{10,... | collective-permute-start | bytes 811016 | tf_op jit(solution)/shard_map/ppermute | solution.py:297
  18.0 13.1 %collective-permute-start.12 = (f32[352,256]{1,0:T(8,128)S(1)}, f32[352,256]{1,0:T(8,128)S(1)}, u32[]{:S(2)}, u32[]{:S(2)}) collective-permute-start(f32[352,256]{1,0:T(8,128)S(1)} %get-tuple-element.45.refs_9_.refs_2_), channel_id=1, source_target_pairs={{0,4},{4,8},{8,12},{12,16},{16,20},{20,24},{24,28},{1,5},{5,9},{9,... | collective-permute-start | bytes 1081352 | tf_op jit(solution)/shard_map/ppermute | solution.py:364
  21.1 17.8 %collective-permute-start.13 = (f32[352,256]{1,0:T(8,128)S(1)}, f32[352,256]{1,0:T(8,128)S(1)}, u32[]{:S(2)}, u32[]{:S(2)}) collective-permute-start(f32[352,256]{1,0:T(8,128)S(1)} %get-tuple-element.44.refs_8_.refs_1_), channel_id=1, source_target_pairs={{4,0},{8,4},{12,8},{16,12},{20,16},{24,20},{28,24},{5,1},{9,5},{13... | collective-permute-start | bytes 1081352 | tf_op jit(solution)/shard_map/ppermute | solution.py:365
  25.8 13.2 %collective-permute-start.7 = (f32[512,128]{1,0:T(8,128)S(1)}, f32[512,128]{1,0:T(8,128)S(1)}, u32[]{:S(2)}, u32[]{:S(2)}) collective-permute-start(f32[512,128]{1,0:T(8,128)S(1)} %get-tuple-element.46), channel_id=1, source_target_pairs={{0,2},{1,3},{2,0},{3,1},{4,6},{5,7},{6,4},{7,5},{8,10},{9,11},{10,... | collective-permute-start | bytes 786440 | tf_op jit(solution)/shard_map/ppermute | solution.py:297
  28.6 10.3 %collective-permute-start.14 = (f32[256,128]{1,0:T(8,128)S(1)}, f32[256,128]{1,0:T(8,128)S(1)}, u32[]{:S(2)}, u32[]{:S(2)}) collective-permute-start(f32[256,128]{1,0:T(8,128)S(1)} %get-tuple-element.54), channel_id=1, source_target_pairs={{0,1},{1,0},{2,3},{3,2},{4,5},{5,4},{6,7},{7,6},{8,9},{9,8},{10,11... | collective-permute-start | bytes 393224 | tf_op jit(solution)/shard_map/ppermute | solution.py:297
  29.9 13.2 %collective-permute-start.10 = (f32[512,128]{1,0:T(8,128)S(1)}, f32[512,128]{1,0:T(8,128)S(1)}, u32[]{:S(2)}, u32[]{:S(2)}) collective-permute-start(f32[512,128]{1,0:T(8,128)S(1)} %get-tuple-element.50), channel_id=1, source_target_pairs={{0,2},{1,3},{2,0},{3,1},{4,6},{5,7},{6,4},{7,5},{8,10},{9,11},{10,... | collective-permute-start | bytes 786440 | tf_op jit(solution)/shard_map/ppermute | solution.py:297
  40.3 7.5 %collective-permute-start.16 = (f32[256,256]{1,0:T(8,128)S(1)}, f32[256,256]{1,0:T(8,128)S(1)}, u32[]{:S(2)}, u32[]{:S(2)}) collective-permute-start(f32[256,256]{1,0:T(8,128)S(1)} %get-tuple-element.59), channel_id=1, source_target_pairs={{0,2},{1,3},{2,0},{3,1},{4,6},{5,7},{6,4},{7,5},{8,10},{9,11},{10,... | collective-permute-start | bytes 786440 | tf_op jit(solution)/shard_map/ppermute | solution.py:297
  40.9 7.0 %collective-permute-start.17 = (f32[256,256]{1,0:T(8,128)S(1)}, f32[256,256]{1,0:T(8,128)S(1)}, u32[]{:S(2)}, u32[]{:S(2)}) collective-permute-start(f32[256,256]{1,0:T(8,128)S(1)} %get-tuple-element.60), channel_id=1, source_target_pairs={{0,1},{1,0},{2,3},{3,2},{4,5},{5,4},{6,7},{7,6},{8,9},{9,8},{10,11... | collective-permute-start | bytes 786440 | tf_op jit(solution)/shard_map/ppermute | solution.py:297
  41.5 6.3 %collective-permute-start.8 = (f32[512,128]{1,0:T(8,128)S(1)}, f32[512,128]{1,0:T(8,128)S(1)}, u32[]{:S(2)}, u32[]{:S(2)}) collective-permute-start(f32[512,128]{1,0:T(8,128)S(1)} %shard_map.60), channel_id=1, source_target_pairs={{0,1},{1,0},{2,3},{3,2},{4,5},{5,4},{6,7},{7,6},{8,9},{9,8},{10,11... | collective-permute-start | bytes 786440 | tf_op jit(solution)/shard_map/ppermute | solution.py:297
  41.6 12.4 %collective-permute-start.15 = (f32[256,256]{1,0:T(8,128)S(1)}, f32[256,256]{1,0:T(8,128)S(1)}, u32[]{:S(2)}, u32[]{:S(2)}) collective-permute-start(f32[256,256]{1,0:T(8,128)S(1)} %get-tuple-element.55), channel_id=1, source_target_pairs={{0,3},{1,2},{2,1},{3,0},{4,7},{5,6},{6,5},{7,4},{8,11},{9,10},{10,... | collective-permute-start | bytes 786440 | tf_op jit(solution)/shard_map/ppermute | solution.py:297
  43.1 7.1 %collective-permute-start.11 = (f32[256,128]{1,0:T(8,128)S(1)}, f32[256,128]{1,0:T(8,128)S(1)}, u32[]{:S(2)}, u32[]{:S(2)}) collective-permute-start(f32[256,128]{1,0:T(8,128)S(1)} %slice.9), channel_id=1, source_target_pairs={{0,1},{1,0},{2,3},{3,2},{4,5},{5,4},{6,7},{7,6},{8,9},{9,8},{10,11... | collective-permute-start | bytes 393224 | tf_op jit(solution)/shard_map/ppermute | solution.py:297

commit v12 on v11

--- a/solution.py
+++ b/solution.py
@@ -192,22 +192,30 @@
     return [ref.at[base : base + size] for ref, base in zip(refs, places)]
 
 
+def paired_edge():
+    return lax.rem(lax.axis_index("plane") + 1, 2)
+
+
 def edge_kernel(rows, count, cells, *refs):
     blocks, (forward_ref, columns_ref, mask_ref) = refs[:count], refs[count : count + 3]
-    spectrum_ref, first_ref, last_ref, sides_ref = refs[count + 3 :]
+    spectrum_ref, ones_ref, paired_ref, other_ref, sides_ref = refs[count + 3 :]
     spectra, sides = transform(len(rows), count, cells, blocks, forward_ref)
     modes, width = spectra[0].shape
     diagonals, beside = reciprocals(mask_ref, columns_ref, modes, rows, 0, width)
-    for i, one_ref in enumerate((first_ref, last_ref)):
+    ones = [spectrum * diagonal for spectrum, diagonal in zip(spectra, diagonals)]
+    for i in (0, 1):
         spectrum_ref[i] = spectra[i]
-        one_ref[...] = spectra[i] * diagonals[i]
+        ones_ref[i] = ones[i]
+    last = paired_edge() == 1
+    paired_ref[...] = jnp.where(last, ones[1], ones[0])
+    other_ref[...] = jnp.where(last, ones[0], ones[1])
     sides_ref[...] = sides * beside
 
 
 def inner_kernel(rows, count, cells, offset, width, places, *refs):
     half = count // 2
     blocks = views(refs, places, len(rows) * cells + 8)
-    forward_ref, inverse_ref, columns_ref, mask_ref, first_ref, last_ref = refs[count : count + 6]
+    forward_ref, inverse_ref, columns_ref, mask_ref, edges_ref = refs[count : count + 5]
     outs, far_ref, ones_ref = refs[-2 - half : -2], refs[-2], refs[-1]
     spectra, sides = transform(len(rows), count, cells, blocks, forward_ref)
     diagonals, beside = reciprocals(mask_ref, columns_ref, spectra[0].shape[0], rows, offset, width)
@@ -215,7 +223,7 @@
     ones = [spectrum * diagonal for spectrum, diagonal in zip(spectra, diagonals)]
     ones_ref[0] = ones[0]
     ones_ref[1] = ones[-1]
-    around = [first_ref[:, offset : offset + width], *ones, last_ref[:, offset : offset + width]]
+    around = [edges_ref[0, :, offset : offset + width], *ones, edges_ref[1, :, offset : offset + width]]
     sweeps = [
         second_sweep(spectra[i], ones[i], around[i], around[i + 2], sides, 2 * i, diagonals[i])
         for i in range(len(rows))
@@ -224,18 +232,17 @@
     inverse_rows(sweeps, count, cells, inverse_ref, [*outs, *views([far_ref] * half, range(0, half * size, size), size)])
 
 
-def rim_kernel(rows, parts, count, cells, *refs):
-    spectrum_ref, first_ref, last_ref, sides_ref, low_ref, high_ref, inverse_ref, columns_ref, mask_ref = refs[:9]
-    ones, outs = refs[9 : 9 + parts], refs[-count:]
-    modes, width = first_ref.shape
+def rim_kernel(rows, order, parts, count, cells, *refs):
+    spectrum_ref, edges_ref, sides_ref, halo_ref, inverse_ref, columns_ref, mask_ref = refs[:7]
+    ones, outs = refs[7 : 7 + parts], refs[-count:]
+    _, modes, width = edges_ref.shape
+    edge = paired_edge() if order == 0 else 1 - paired_edge()
     diagonals, _ = reciprocals(mask_ref, columns_ref, modes, rows, 0, width)
-    sides = sides_ref[...]
-    inner = [jnp.concatenate([one[i] for one in ones], axis=1) for i in (0, 1)]
-    sweeps = [
-        second_sweep(spectrum_ref[0], first_ref[...], low_ref[...], inner[0], sides, 0, diagonals[0]),
-        second_sweep(spectrum_ref[1], last_ref[...], inner[1], high_ref[...], sides, 2, diagonals[1]),
-    ]
-    inverse_rows(sweeps, count, cells, inverse_ref, outs)
+    sides = jnp.where(edge == 0, sides_ref[:, 0:2], sides_ref[:, 2:4])
+    beneath = jnp.concatenate([one[edge] for one in ones], axis=1)
+    diagonal = jnp.where(edge == 0, diagonals[0], diagonals[1])
+    sweep = second_sweep(spectrum_ref[edge], edges_ref[edge], halo_ref[...], beneath, sides, 0, diagonal)
+    inverse_rows([sweep], count, cells, inverse_ref, outs)
 
 
 def join_kernel(groups, size, *refs):
@@ -253,10 +260,13 @@
     pitch = held.shape[0] // cells
     own_lines = out_ref.shape[1] // lax.axis_size("span")
     some = cells // SPLIT
+    edge_rows = {"near": paired_edge() * (row_count - 1), "far": (1 - paired_edge()) * (row_count - 1)}
     copies = []
     for part in range(SPLIT):
         for block, (d, base, rows, offset, tiles) in zip(blocks, pieces):
             for i, row in enumerate(rows):
+                if row in edge_rows:
+                    row = edge_rows[row]
                 line = base + i * cells + part * some
                 for tile in range(tiles):
                     at = part * some * pitch + devices.index(d) * own_lines + (offset + tile) * row_count + row
@@ -354,15 +364,16 @@
         messages.append([mine[0]] + [swap(mine[d], d) for d in near])
     far_blocks = [swap(message, half) for message in join(*messages, earlier=(edge_blocks[half],))]
 
-    spectrum, first, last, sides = call(
+    spectrum, edge_ones, paired, other, sides = call(
         functools.partial(edge_kernel, edges, count, cells),
-        [(2, modes, width), (modes, width), (modes, width), (modes, 16)],
+        [(2, modes, width), (2, modes, width), (modes, width), (modes, width), (modes, 16)],
         *edge_blocks, forward, one_over, solid_mask,
     )
-    up = [(i, i + 1) for i in range(plane_count - 1)]
-    down = [(i + 1, i) for i in range(plane_count - 1)]
-    low = lax.ppermute(last, "plane", up)
-    high = lax.ppermute(first, "plane", down)
+    pairs = [[(i, i ^ 1) for i in range(plane_count)], [(i, ((i + 1) ^ 1) - 1) for i in range(plane_count)]]
+    halos = [
+        lax.ppermute(row, "plane", [(i, j) for i, j in pair if 0 <= j < plane_count])
+        for row, pair in zip((paired, other), pairs)
+    ]
 
     ones, made, arrived, pieces, earlier = [], [], [], [], ()
     size = len(inner) * cells
@@ -375,7 +386,7 @@
                 inner_kernel, inner, count, cells, offset, part_width, [base for _, base in blocks]
             ),
             [(size, part_width)] * half + [(half * size, part_width), (2, modes, part_width)],
-            *[block for block, _ in blocks], forward, inverse, one_over, solid_mask, first, last,
+            *[block for block, _ in blocks], forward, inverse, one_over, solid_mask, edge_ones,
             cost=SHORT, earlier=earlier,
         )
         ones.append(one)
@@ -400,13 +411,17 @@
                 earlier.append(swap(made[part][d], d))
                 pieces += [(earlier[-1], d, 0, *place(part))]
                 pieces += [(swap(onward(part, d), d), half + d, 0, *place(part))]
-    outs = call(
-        functools.partial(rim_kernel, edges, parts, count, cells),
-        [(len(edges) * cells, width)] * count,
-        spectrum, first, last, sides, low, high, inverse, one_over, solid_mask, *ones, earlier=tuple(earlier),
-    )
-    pieces.append((outs[0], 0, 0, edges, 0, tiles))
-    pieces += [(swap(outs[d], d), d, 0, edges, 0, tiles) for d in (*far, *near)]
+    before = ()
+    for order, name in enumerate(("near", "far")):
+        outs = call(
+            functools.partial(rim_kernel, edges, order, parts, count, cells),
+            [(cells, width)] * count,
+            spectrum, edge_ones, sides, halos[order], inverse, one_over, solid_mask, *ones,
+            cost=LONG if order else SHORT, earlier=(*before, *earlier) if order else (),
+        )
+        before = (outs[-1],)
+        pieces.append((outs[0], 0, 0, (name,), 0, tiles))
+        pieces += [(swap(outs[d], d), d, 0, (name,), 0, tiles) for d in (*far, *near)]
     result = None
     own_lines = tiles * row_count
     for devices in (range(count - 1), [count - 1]) if own_lines % 8 == 0 else (range(count),):

time: 55.1 us -> 52.7 us (0.956)
  the two profiles are of different devices: /device:TPU:25 before, /device:TPU:0 now
where the time goes in v12:
time: 52.7 us; the launch traced here: 52.5 us
  waiting for transfers between devices  22.4 us (43%)
  starting transfers between devices  17.2 us (33%)
  Pallas kernels  12.6 us (24%)
    ppermute x19, waiting for transfers between devices, swap(): lax.ppermute(block, 'span', [(i, i ^ d) for i in range(lax.axis_size('spa...  19.3 us
    ppermute x19, starting transfers between devices, swap(): lax.ppermute(block, 'span', [(i, i ^ d) for i in range(lax.axis_size('spa...  15 us
    pallas_call x7, Pallas kernels, call(): pl.pallas_call(kernel, out_shape=shapes, in_specs=[VMEM] * len(args) + [A...  6.16 us
    pallas_call x2, Pallas kernels, local(): pl.pallas_call(functools.partial(unpack_kernel, [piece[1:] for piece in c...  3.25 us
    pallas_call x2, Pallas kernels, pack(): pl.pallas_call(functools.partial(pack_kernel, jobs, row_count, cells, len...  3.22 us
    ppermute x2, waiting for transfers between devices, local(): lax.ppermute(row, 'plane', [(i, j) for i, j in pair if 0 <= j < plane_cou...  3.13 us
    ppermute x2, starting transfers between devices, local(): lax.ppermute(row, 'plane', [(i, j) for i, j in pair if 0 <= j < plane_cou...  2.23 us
  transfers between devices with their start and end apart: 21, of which 10 were waited for; matrix products, arithmetic and copies ran while one was open for 0% of the time, Pallas kernels for 19%

profile of v12, /device:TPU:0, one launch (start us, length us, event | category | flops | bytes accessed | tf_op | source)
XLA Modules:
  0.0 52.5 jit_solution(4827078817294622257)
XLA Ops:
  0.0 1.9 %shard_map.55 = (f32[264,256]{1,0:T(8,128)S(1)}, f32[264,256]{1,0:T(8,128)S(1)}, f32[264,256]{1,0:T(8,128)S(1)}) custom-call(f32[128,32,128]{2,1,0:T(8,128)} %bitcast.10), custom_call_target="tpu_custom_call" | custom-call | bytes 200000000 | tf_op jit(solution)/shard_map/pallas_call | solution.py:331
  2.0 3.0 %collective-permute-start.3 = (f32[264,256]{1,0:T(8,128)S(1)}, f32[264,256]{1,0:T(8,128)S(1)}, u32[]{:S(2)}, u32[]{:S(2)}) collective-permute-start(f32[264,256]{1,0:T(8,128)S(1)} %get-tuple-element.38.refs_0_), channel_id=1, source_target_pairs={{0,2},{1,3},{2,0},{3,1},{4,6},{5,7},{6,4},{7,5},{8,10},{9,11},{10,... | collective-permute-start | bytes 811016 | tf_op jit(solution)/shard_map/ppermute | solution.py:307
  5.0 1.3 %shard_map.56 = (f32[264,256]{1,0:T(8,128)S(1)}, f32[528,128]{1,0:T(8,128)S(1)}, f32[528,128]{1,0:T(8,128)S(1)}, f32[264,128]{1,0:T(8,128)S(1)}, f32[264,128]{1,...) custom-call(f32[128,32,128]{2,1,0:T(8,128)S(1)} %bitcast.11, f32[264,256]{1,0:T(8,128)S(1)} %get-tuple-element.38.refs_0_), custom_call_target="tpu_custom_call" | custom-call | bytes 200000000 | tf_op jit(solution)/shard_map/pallas_call | solution.py:331
  7.9 4.4 %collective-permute-done.3.refs_4_.refs_2_ = f32[264,256]{1,0:T(8,128)S(1)} collective-permute-done((f32[264,256]{1,0:T(8,128)S(1)}, f32[264,256]{1,0:T(8,128)S(1)}, u32[]{:S(2)}, u32[]{:S(2)}) %collective-permute-start.3) | collective-permute-done | bytes 270368 | tf_op jit(solution)/shard_map/ppermute | solution.py:307
  12.3 2.1 %collective-permute-start.4 = (f32[528,128]{1,0:T(8,128)S(1)}, f32[528,128]{1,0:T(8,128)S(1)}, u32[]{:S(2)}, u32[]{:S(2)}) collective-permute-start(f32[528,128]{1,0:T(8,128)S(1)} %get-tuple-element.45), channel_id=1, source_target_pairs={{0,2},{1,3},{2,0},{3,1},{4,6},{5,7},{6,4},{7,5},{8,10},{9,11},{10,... | collective-permute-start | bytes 811016 | tf_op jit(solution)/shard_map/ppermute | solution.py:307
  14.5 3.1 %collective-permute-done.6.refs_3_ = f32[264,256]{1,0:T(8,128)S(1)} collective-permute-done((f32[264,256]{1,0:T(8,128)S(1)}, f32[264,256]{1,0:T(8,128)S(1)}, u32[]{:S(2)}, u32[]{:S(2)}) %collective-permute-start.6) | collective-permute-done | bytes 270368 | tf_op jit(solution)/shard_map/ppermute | solution.py:307
  17.7 0.9 %shard_map.58 = (f32[2,352,256]{2,1,0:T(8,128)S(1)}, f32[2,352,256]{2,1,0:T(8,128)S(1)}, f32[352,256]{1,0:T(8,128)S(1)}, f32[352,256]{1,0:T(8,128)S(1)}, f32[352,16]{1,0:T(8,128)S(1)}) custom-call(f32[264,256]{1,0:T(8,128)S(1)} %get-tuple-element.46.refs_0_, f32[264,256]{1,0:T(8,128)S(1)} %collective-permute-done.5.refs_1_, ...), custom_call_target="tpu_custom_call" | custom-call | bytes 200000000 | tf_op jit(solution)/shard_map/pallas_call | solution.py:290
  18.6 1.6 %collective-permute-start.12 = (f32[352,256]{1,0:T(8,128)S(1)}, f32[352,256]{1,0:T(8,128)S(1)}, u32[]{:S(2)}, u32[]{:S(2)}) collective-permute-start(f32[352,256]{1,0:T(8,128)S(1)} %get-tuple-element.57), channel_id=1, source_target_pairs={{0,4},{4,0},{8,12},{12,8},{16,20},{20,16},{24,28},{28,24},{1,5},{5... | collective-permute-start | bytes 1081352 | tf_op jit(solution)/shard_map/ppermute | solution.py:374
  20.8 3.1 %collective-permute-done.4.refs_2_.refs_3_ = f32[528,128]{1,0:T(8,128)S(1)} collective-permute-done((f32[528,128]{1,0:T(8,128)S(1)}, f32[528,128]{1,0:T(8,128)S(1)}, u32[]{:S(2)}, u32[]{:S(2)}) %collective-permute-start.4) | collective-permute-done | bytes 270368 | tf_op jit(solution)/shard_map/ppermute | solution.py:307
  23.9 1.5 %shard_map.59 = (f32[256,128]{1,0:T(8,128)S(1)}, f32[256,128]{1,0:T(8,128)S(1)}, f32[512,128]{1,0:T(8,128)S(1)}, f32[2,352,128]{2,1,0:T(8,128)S(1)}) custom-call(f32[528,128]{1,0:T(8,128)S(1)} %get-tuple-element.39.refs_0_, f32[528,128]{1,0:T(8,128)S(1)} %collective-permute-done.refs_1_, f32[528,128]{1,0:T(8,128)S(1)} %collective-permute-done.4.refs_2_.refs_3_, ...), custom_call_target="tpu_custom_call" | custom-call | bytes 1024 | tf_op jit(solution)/shard_map/pallas_call | solution.py:290
  25.4 2.1 %collective-permute-start.7 = (f32[512,128]{1,0:T(8,128)S(1)}, f32[512,128]{1,0:T(8,128)S(1)}, u32[]{:S(2)}, u32[]{:S(2)}) collective-permute-start(f32[512,128]{1,0:T(8,128)S(1)} %get-tuple-element.50), channel_id=1, source_target_pairs={{0,2},{1,3},{2,0},{3,1},{4,6},{5,7},{6,4},{7,5},{8,10},{9,11},{10,... | collective-permute-start | bytes 786440 | tf_op jit(solution)/shard_map/ppermute | solution.py:307
  27.5 2.1 %collective-permute-done.9.refs_2_.refs_3_ = f32[528,128]{1,0:T(8,128)S(1)} collective-permute-done((f32[528,128]{1,0:T(8,128)S(1)}, f32[528,128]{1,0:T(8,128)S(1)}, u32[]{:S(2)}, u32[]{:S(2)}) %collective-permute-start.9) | collective-permute-done | bytes 270368 | tf_op jit(solution)/shard_map/ppermute | solution.py:307
  29.7 1.5 %shard_map.61 = (f32[256,128]{1,0:T(8,128)S(1)}, f32[256,128]{1,0:T(8,128)S(1)}, f32[512,128]{1,0:T(8,128)S(1)}, f32[2,352,128]{2,1,0:T(8,128)S(1)}) custom-call(f32[528,128]{1,0:T(8,128)S(1)} %get-tuple-element.39.refs_0_, f32[528,128]{1,0:T(8,128)S(1)} %collective-permute-done.refs_1_, f32[528,128]{1,0:T(8,128)S(1)} %collective-permute-done.9.refs_2_.refs_3_, ...), custom_call_target="tpu_custom_call" | custom-call | bytes 1024 | tf_op jit(solution)/shard_map/pallas_call | solution.py:290
  31.2 2.1 %collective-permute-start.10 = (f32[512,128]{1,0:T(8,128)S(1)}, f32[512,128]{1,0:T(8,128)S(1)}, u32[]{:S(2)}, u32[]{:S(2)}) collective-permute-start(f32[512,128]{1,0:T(8,128)S(1)} %get-tuple-element.54), channel_id=1, source_target_pairs={{0,2},{1,3},{2,0},{3,1},{4,6},{5,7},{6,4},{7,5},{8,10},{9,11},{10,... | collective-permute-start | bytes 786440 | tf_op jit(solution)/shard_map/ppermute | solution.py:307
  33.3 3.1 %collective-permute-done.12.refs_3_ = f32[352,256]{1,0:T(8,128)S(1)} collective-permute-done((f32[352,256]{1,0:T(8,128)S(1)}, f32[352,256]{1,0:T(8,128)S(1)}, u32[]{:S(2)}, u32[]{:S(2)}) %collective-permute-start.12) | collective-permute-done | bytes 360480 | tf_op jit(solution)/shard_map/ppermute | solution.py:374
  36.5 1.1 %shard_map.62 = (f32[128,256]{1,0:T(8,128)S(1)}, f32[128,256]{1,0:T(8,128)S(1)}, f32[128,256]{1,0:T(8,128)S(1)}, f32[128,256]{1,0:T(8,128)S(1)}) custom-call(f32[2,352,256]{2,1,0:T(8,128)S(1)} %get-tuple-element.55.refs_0_, f32[2,352,256]{2,1,0:T(8,128)S(1)} %get-tuple-element.49.refs_8_.refs_1_, f32[352,16]{1,0:T(8,128)S(1)} %get-tuple-element.56.refs_2_, ...), custom_call_target="tpu_custom_call" | custom-call | bytes 1024 | tf_op jit(solution)/shard_map/pallas_call | solution.py:290
  38.4 1.1 %shard_map.63 = (f32[128,256]{1,0:T(8,128)S(1)}, f32[128,256]{1,0:T(8,128)S(1)}, f32[128,256]{1,0:T(8,128)S(1)}, f32[128,256]{1,0:T(8,128)S(1)}) custom-call(f32[2,352,256]{2,1,0:T(8,128)S(1)} %get-tuple-element.55.refs_0_, f32[2,352,256]{2,1,0:T(8,128)S(1)} %get-tuple-element.49.refs_8_.refs_1_, f32[352,16]{1,0:T(8,128)S(1)} %get-tuple-element.56.refs_2_, ...), custom_call_target="tpu_custom_call" | custom-call | bytes 200000000 | tf_op jit(solution)/shard_map/pallas_call | solution.py:290
  39.4 2.0 %collective-permute-start.19 = (f32[128,256]{1,0:T(8,128)S(1)}, f32[128,256]{1,0:T(8,128)S(1)}, u32[]{:S(2)}, u32[]{:S(2)}) collective-permute-start(f32[128,256]{1,0:T(8,128)S(1)} %get-tuple-element.69), channel_id=1, source_target_pairs={{0,2},{1,3},{2,0},{3,1},{4,6},{5,7},{6,4},{7,5},{8,10},{9,11},{10,... | collective-permute-start | bytes 393224 | tf_op jit(solution)/shard_map/ppermute | solution.py:307
  41.5 1.9 %collective-permute-done.17.refs_7_ = f32[128,256]{1,0:T(8,128)S(1)} collective-permute-done((f32[128,256]{1,0:T(8,128)S(1)}, f32[128,256]{1,0:T(8,128)S(1)}, u32[]{:S(2)}, u32[]{:S(2)}) %collective-permute-start.17) | collective-permute-done | bytes 131104 | tf_op jit(solution)/shard_map/ppermute | solution.py:307
  43.6 1.4 %collective-permute-start.16 = (f32[128,256]{1,0:T(8,128)S(1)}, f32[128,256]{1,0:T(8,128)S(1)}, u32[]{:S(2)}, u32[]{:S(2)}) collective-permute-start(f32[128,256]{1,0:T(8,128)S(1)} %get-tuple-element.62), channel_id=1, source_target_pairs={{0,3},{1,2},{2,1},{3,0},{4,7},{5,6},{6,5},{7,4},{8,11},{9,10},{10,... | collective-permute-start | bytes 393224 | tf_op jit(solution)/shard_map/ppermute | solution.py:307
  45.1 0.7 %collective-permute-done.19.refs_10_ = f32[128,256]{1,0:T(8,128)S(1)} collective-permute-done((f32[128,256]{1,0:T(8,128)S(1)}, f32[128,256]{1,0:T(8,128)S(1)}, u32[]{:S(2)}, u32[]{:S(2)}) %collective-permute-start.19) | collective-permute-done | bytes 131104 | tf_op jit(solution)/shard_map/ppermute | solution.py:307
  45.8 2.3 %shard_map.64.refs_4_ = f32[128,32,128]{2,1,0:T(8,128)} custom-call(f32[256,128]{1,0:T(8,128)S(1)} %get-tuple-element.63.refs_0_, f32[512,128]{1,0:T(8,128)S(1)} %collective-permute-done.7.refs_10_.refs_1_, f32[512,128]{1,0:T(8,128)S(1)} %collective-permute-done.8.refs_2_.refs_0_, f32[256,128]{1,0:T(8,128)S(1)} %get-tuple-element.64.refs_3_, ...), custom_call_target="tpu_custom_call" | custom-call | bytes 200000000 | tf_op jit(solution)/shard_map/pallas_call | solution.py:430
  48.8 2.8 %collective-permute-done.16.refs_3_ = f32[128,256]{1,0:T(8,128)S(1)} collective-permute-done((f32[128,256]{1,0:T(8,128)S(1)}, f32[128,256]{1,0:T(8,128)S(1)}, u32[]{:S(2)}, u32[]{:S(2)}) %collective-permute-start.16) | collective-permute-done | bytes 131104 | tf_op jit(solution)/shard_map/ppermute | solution.py:307
  51.6 0.9 %shard_map.65 = f32[128,32,128]{2,1,0:T(8,128)} custom-call(f32[512,128]{1,0:T(8,128)S(1)} %collective-permute-done.8.refs_2_.refs_0_, f32[256,128]{1,0:T(8,128)S(1)} %collective-permute-done.11.refs_1_, f32[128,256]{1,0:T(8,128)S(1)} %collective-permute-done.13.refs_2_, ...), custom_call_target="tpu_custom_call", output_to_operand_aliasing={{}: (4, {})} | custom-call | bytes 1024 | tf_op jit(solution)/shard_map/pallas_call | solution.py:430
  (41 shorter events, 4.2 us)
Async XLA Ops:
  1.9 15.8 %copy-start.2 = (bf16[2,2,176,384]{3,2,1,0:T(8,128)(2,1)S(1)}, bf16[2,2,176,384]{3,2,1,0:T(8,128)(2,1)}, u32[]{:S(2)}) copy-start(bf16[2,2,176,384]{3,2,1,0:T(8,128)(2,1)} %constant.6.clone.refs_4_) | copy-start | bytes 1622020
  1.9 15.8 %copy-start.3 = (s32[4,1024]{1,0:T(4,128)S(1)}, s32[4,1024]{1,0:T(4,128)}, u32[]{:S(2)}) copy-start(s32[4,1024]{1,0:T(4,128)} %refs_6_.7) | copy-start | bytes 49156
  1.9 21.9 %copy-start = (bf16[2,2,128,528]{3,2,1,0:T(8,128)(2,1)S(1)}, bf16[2,2,128,528]{3,2,1,0:T(8,128)(2,1)}, u32[]{:S(2)}) copy-start(bf16[2,2,128,528]{3,2,1,0:T(8,128)(2,1)} %constant.7.clone.refs_5_.refs_4_) | copy-start | bytes 1622020
  2.0 10.3 %collective-permute-start.3 = (f32[264,256]{1,0:T(8,128)S(1)}, f32[264,256]{1,0:T(8,128)S(1)}, u32[]{:S(2)}, u32[]{:S(2)}) collective-permute-start(f32[264,256]{1,0:T(8,128)S(1)} %get-tuple-element.38.refs_0_), channel_id=1, source_target_pairs={{0,2},{1,3},{2,0},{3,1},{4,6},{5,7},{6,4},{7,5},{8,10},{9,11},{10,... | collective-permute-start | bytes 811016 | tf_op jit(solution)/shard_map/ppermute | solution.py:307
  6.3 1.4 %collective-permute-start.1 = (f32[264,128]{1,0:T(8,128)S(1)}, f32[264,128]{1,0:T(8,128)S(1)}, u32[]{:S(2)}, u32[]{:S(2)}) collective-permute-start(f32[264,128]{1,0:T(8,128)S(1)} %get-tuple-element.42), channel_id=1, source_target_pairs={{0,1},{1,0},{2,3},{3,2},{4,5},{5,4},{6,7},{7,6},{8,9},{9,8},{10,11... | collective-permute-start | bytes 405512 | tf_op jit(solution)/shard_map/ppermute | solution.py:307
  6.4 1.5 %collective-permute-start.2 = (f32[264,128]{1,0:T(8,128)S(1)}, f32[264,128]{1,0:T(8,128)S(1)}, u32[]{:S(2)}, u32[]{:S(2)}) collective-permute-start(f32[264,128]{1,0:T(8,128)S(1)} %get-tuple-element.44), channel_id=1, source_target_pairs={{0,1},{1,0},{2,3},{3,2},{4,5},{5,4},{6,7},{7,6},{8,9},{9,8},{10,11... | collective-permute-start | bytes 405512 | tf_op jit(solution)/shard_map/ppermute | solution.py:307
  6.9 7.6 %collective-permute-start.5 = (f32[264,256]{1,0:T(8,128)S(1)}, f32[264,256]{1,0:T(8,128)S(1)}, u32[]{:S(2)}, u32[]{:S(2)}) collective-permute-start(f32[264,256]{1,0:T(8,128)S(1)} %get-tuple-element.47), channel_id=1, source_target_pairs={{0,1},{1,0},{2,3},{3,2},{4,5},{5,4},{6,7},{7,6},{8,9},{9,8},{10,11... | collective-permute-start | bytes 811016 | tf_op jit(solution)/shard_map/ppermute | solution.py:307
  7.0 10.7 %collective-permute-start.6 = (f32[264,256]{1,0:T(8,128)S(1)}, f32[264,256]{1,0:T(8,128)S(1)}, u32[]{:S(2)}, u32[]{:S(2)}) collective-permute-start(f32[264,256]{1,0:T(8,128)S(1)} %get-tuple-element.48), channel_id=1, source_target_pairs={{0,3},{1,2},{2,1},{3,0},{4,7},{5,6},{6,5},{7,4},{8,11},{9,10},{10,... | collective-permute-start | bytes 811016 | tf_op jit(solution)/shard_map/ppermute | solution.py:307
  7.7 13.1 %collective-permute-start = (f32[528,128]{1,0:T(8,128)S(1)}, f32[528,128]{1,0:T(8,128)S(1)}, u32[]{:S(2)}, u32[]{:S(2)}) collective-permute-start(f32[528,128]{1,0:T(8,128)S(1)} %get-tuple-element.40), channel_id=1, source_target_pairs={{0,1},{1,0},{2,3},{3,2},{4,5},{5,4},{6,7},{7,6},{8,9},{9,8},{10,11... | collective-permute-start | bytes 811016 | tf_op jit(solution)/shard_map/ppermute | solution.py:307
  12.3 11.5 %collective-permute-start.4 = (f32[528,128]{1,0:T(8,128)S(1)}, f32[528,128]{1,0:T(8,128)S(1)}, u32[]{:S(2)}, u32[]{:S(2)}) collective-permute-start(f32[528,128]{1,0:T(8,128)S(1)} %get-tuple-element.45), channel_id=1, source_target_pairs={{0,2},{1,3},{2,0},{3,1},{4,6},{5,7},{6,4},{7,5},{8,10},{9,11},{10,... | collective-permute-start | bytes 811016 | tf_op jit(solution)/shard_map/ppermute | solution.py:307
  14.5 15.2 %collective-permute-start.9 = (f32[528,128]{1,0:T(8,128)S(1)}, f32[528,128]{1,0:T(8,128)S(1)}, u32[]{:S(2)}, u32[]{:S(2)}) collective-permute-start(f32[528,128]{1,0:T(8,128)S(1)} %get-tuple-element.52), channel_id=1, source_target_pairs={{0,2},{1,3},{2,0},{3,1},{4,6},{5,7},{6,4},{7,5},{8,10},{9,11},{10,... | collective-permute-start | bytes 811016 | tf_op jit(solution)/shard_map/ppermute | solution.py:307
  18.6 17.9 %collective-permute-start.12 = (f32[352,256]{1,0:T(8,128)S(1)}, f32[352,256]{1,0:T(8,128)S(1)}, u32[]{:S(2)}, u32[]{:S(2)}) collective-permute-start(f32[352,256]{1,0:T(8,128)S(1)} %get-tuple-element.57), channel_id=1, source_target_pairs={{0,4},{4,0},{8,12},{12,8},{16,20},{20,16},{24,28},{28,24},{1,5},{5... | collective-permute-start | bytes 1081352 | tf_op jit(solution)/shard_map/ppermute | solution.py:374
  20.1 18.1 %collective-permute-start.14 = (f32[352,256]{1,0:T(8,128)S(1)}, f32[352,256]{1,0:T(8,128)S(1)}, u32[]{:S(2)}, u32[]{:S(2)}) collective-permute-start(f32[352,256]{1,0:T(8,128)S(1)} %get-tuple-element.60), channel_id=1, source_target_pairs={{4,8},{8,4},{12,16},{16,12},{20,24},{24,20},{5,9},{9,5},{13,17},{1... | collective-permute-start | bytes 1081352 | tf_op jit(solution)/shard_map/ppermute | solution.py:374
  25.4 12.2 %collective-permute-start.7 = (f32[512,128]{1,0:T(8,128)S(1)}, f32[512,128]{1,0:T(8,128)S(1)}, u32[]{:S(2)}, u32[]{:S(2)}) collective-permute-start(f32[512,128]{1,0:T(8,128)S(1)} %get-tuple-element.50), channel_id=1, source_target_pairs={{0,2},{1,3},{2,0},{3,1},{4,6},{5,7},{6,4},{7,5},{8,10},{9,11},{10,... | collective-permute-start | bytes 786440 | tf_op jit(solution)/shard_map/ppermute | solution.py:307
  31.2 10.2 %collective-permute-start.10 = (f32[512,128]{1,0:T(8,128)S(1)}, f32[512,128]{1,0:T(8,128)S(1)}, u32[]{:S(2)}, u32[]{:S(2)}) collective-permute-start(f32[512,128]{1,0:T(8,128)S(1)} %get-tuple-element.54), channel_id=1, source_target_pairs={{0,2},{1,3},{2,0},{3,1},{4,6},{5,7},{6,4},{7,5},{8,10},{9,11},{10,... | collective-permute-start | bytes 786440 | tf_op jit(solution)/shard_map/ppermute | solution.py:307
  33.3 5.0 %collective-permute-start.15 = (f32[256,128]{1,0:T(8,128)S(1)}, f32[256,128]{1,0:T(8,128)S(1)}, u32[]{:S(2)}, u32[]{:S(2)}) collective-permute-start(f32[256,128]{1,0:T(8,128)S(1)} %get-tuple-element.61), channel_id=1, source_target_pairs={{0,1},{1,0},{2,3},{3,2},{4,5},{5,4},{6,7},{7,6},{8,9},{9,8},{10,11... | collective-permute-start | bytes 393224 | tf_op jit(solution)/shard_map/ppermute | solution.py:307
  37.6 5.8 %collective-permute-start.17 = (f32[128,256]{1,0:T(8,128)S(1)}, f32[128,256]{1,0:T(8,128)S(1)}, u32[]{:S(2)}, u32[]{:S(2)}) collective-permute-start(f32[128,256]{1,0:T(8,128)S(1)} %get-tuple-element.66), channel_id=1, source_target_pairs={{0,2},{1,3},{2,0},{3,1},{4,6},{5,7},{6,4},{7,5},{8,10},{9,11},{10,... | collective-permute-start | bytes 393224 | tf_op jit(solution)/shard_map/ppermute | solution.py:307
  37.7 8.1 %collective-permute-start.8 = (f32[512,128]{1,0:T(8,128)S(1)}, f32[512,128]{1,0:T(8,128)S(1)}, u32[]{:S(2)}, u32[]{:S(2)}) collective-permute-start(f32[512,128]{1,0:T(8,128)S(1)} %shard_map.60), channel_id=1, source_target_pairs={{0,1},{1,0},{2,3},{3,2},{4,5},{5,4},{6,7},{7,6},{8,9},{9,8},{10,11... | collective-permute-start | bytes 786440 | tf_op jit(solution)/shard_map/ppermute | solution.py:307
  38.3 5.4 %collective-permute-start.18 = (f32[128,256]{1,0:T(8,128)S(1)}, f32[128,256]{1,0:T(8,128)S(1)}, u32[]{:S(2)}, u32[]{:S(2)}) collective-permute-start(f32[128,256]{1,0:T(8,128)S(1)} %get-tuple-element.67), channel_id=1, source_target_pairs={{0,1},{1,0},{2,3},{3,2},{4,5},{5,4},{6,7},{7,6},{8,9},{9,8},{10,11... | collective-permute-start | bytes 393224 | tf_op jit(solution)/shard_map/ppermute | solution.py:307
  39.4 6.3 %collective-permute-start.19 = (f32[128,256]{1,0:T(8,128)S(1)}, f32[128,256]{1,0:T(8,128)S(1)}, u32[]{:S(2)}, u32[]{:S(2)}) collective-permute-start(f32[128,256]{1,0:T(8,128)S(1)} %get-tuple-element.69), channel_id=1, source_target_pairs={{0,2},{1,3},{2,0},{3,1},{4,6},{5,7},{6,4},{7,5},{8,10},{9,11},{10,... | collective-permute-start | bytes 393224 | tf_op jit(solution)/shard_map/ppermute | solution.py:307
  41.4 4.3 %collective-permute-start.20 = (f32[128,256]{1,0:T(8,128)S(1)}, f32[128,256]{1,0:T(8,128)S(1)}, u32[]{:S(2)}, u32[]{:S(2)}) collective-permute-start(f32[128,256]{1,0:T(8,128)S(1)} %get-tuple-element.70), channel_id=1, source_target_pairs={{0,1},{1,0},{2,3},{3,2},{4,5},{5,4},{6,7},{7,6},{8,9},{9,8},{10,11... | collective-permute-start | bytes 393224 | tf_op jit(solution)/shard_map/ppermute | solution.py:307
  43.3 5.5 %collective-permute-start.13 = (f32[128,256]{1,0:T(8,128)S(1)}, f32[128,256]{1,0:T(8,128)S(1)}, u32[]{:S(2)}, u32[]{:S(2)}) collective-permute-start(f32[128,256]{1,0:T(8,128)S(1)} %get-tuple-element.59.refs_9_), channel_id=1, source_target_pairs={{0,3},{1,2},{2,1},{3,0},{4,7},{5,6},{6,5},{7,4},{8,11},{9,10},{10,... | collective-permute-start | bytes 393224 | tf_op jit(solution)/shard_map/ppermute | solution.py:307
  43.6 8.0 %collective-permute-start.16 = (f32[128,256]{1,0:T(8,128)S(1)}, f32[128,256]{1,0:T(8,128)S(1)}, u32[]{:S(2)}, u32[]{:S(2)}) collective-permute-start(f32[128,256]{1,0:T(8,128)S(1)} %get-tuple-element.62), channel_id=1, source_target_pairs={{0,3},{1,2},{2,1},{3,0},{4,7},{5,6},{6,5},{7,4},{8,11},{9,10},{10,... | collective-permute-start | bytes 393224 | tf_op jit(solution)/shard_map/ppermute | solution.py:307
  45.8 5.8 %collective-permute-start.11 = (f32[256,128]{1,0:T(8,128)S(1)}, f32[256,128]{1,0:T(8,128)S(1)}, u32[]{:S(2)}, u32[]{:S(2)}) collective-permute-start(f32[256,128]{1,0:T(8,128)S(1)} %slice.9), channel_id=1, source_target_pairs={{0,1},{1,0},{2,3},{3,2},{4,5},{5,4},{6,7},{7,6},{8,9},{9,8},{10,11... | collective-permute-start | bytes 393224 | tf_op jit(solution)/shard_map/ppermute | solution.py:307
  (2 other events, 20.7 us)

commit v13 on v12

v13 whole, which is shorter than its diff:
```python
import functools

import jax
import jax.numpy as jnp
import ml_dtypes
import numpy as np
from jax import lax
from jax.experimental import pallas as pl
from jax.experimental.pallas import tpu as pltpu
from jax.sharding import PartitionSpec as P

PENALTY = 12.0
LANES = 128
VMEM = pl.BlockSpec(memory_space=pltpu.VMEM)
ANY = pl.BlockSpec(memory_space=pl.ANY)
PARAMS = pltpu.CompilerParams(vmem_limit_bytes=24 * 1024 * 1024)
LONG = pl.CostEstimate(flops=0, bytes_accessed=200_000_000, transcendentals=0)
SHORT = pl.CostEstimate(flops=0, bytes_accessed=1024, transcendentals=0)
SPLIT = 4


def split(values):
    high = values.astype(ml_dtypes.bfloat16)
    low = (values - high.astype(np.float64)).astype(ml_dtypes.bfloat16)
    return np.concatenate([high, low, high], axis=-1)


def table_modes(length, wanted):
    modes = [(k, False) for k in range(length // 2 + 1) if wanted(k)]
    return modes + [(k, True) for k in range(1, length // 2) if wanted(k)]


def wave(length, points, k, sine):
    angles = (points * k % length) * (2.0 * np.pi / length)
    return np.sin(angles) if sine else np.cos(angles)


def fill(length, modes, forward, inverse, fluid, solid):
    points = np.arange(length // 2)
    for at, (k, sine) in enumerate(modes):
        forward[at] = wave(length, points, k, sine)
        inverse[:, at] = forward[at] * (1.0 if k in (0, length // 2) else 2.0) / length
        eigen = 2.0 - 2.0 * np.cos(2.0 * np.pi * k / length)
        fluid[at] = 1.0 / (4.0 + eigen)
        solid[at] = 1.0 / (4.0 + eigen + PENALTY)


def up_to(number, step):
    return -(-number // step) * step


def tables(length, cells):
    half = length // 2
    blocks = half // cells
    kept = [table_modes(length, lambda k: 3 * k <= length and k % 2 == parity) for parity in (0, 1)]
    padded = up_to(max(len(modes) for modes in kept), 16)
    left = table_modes(length, lambda k: 3 * k > length)
    rest = up_to(len(left), 16)
    columns = np.zeros((8, up_to(max(2 * padded, rest), LANES)))
    forward, inverse = np.zeros((2, padded, half)), np.zeros((2, half, padded))
    for parity, modes in enumerate(kept):
        part = slice(parity * padded, (parity + 1) * padded)
        fill(length, modes, forward[parity], inverse[parity], columns[0, part], columns[1, part])
    powers = 8
    send, take = np.zeros((rest + 6 * powers, half)), np.zeros((half, up_to(rest + powers, 16)))
    fill(length, left, send[:rest], take[:, :rest], columns[2, :rest], columns[3, :rest])
    take[:, : len(left)] *= [-1.0 if k % 2 == 0 else 1.0 for k, _ in left]
    ends = (np.arange(half), half - 1.0 - np.arange(half))
    for side in (0, 1):
        x, y = ends[side], ends[1 - side] + 1.0
        first = rest + 4 * side
        for solid, diagonal in enumerate((6.0, 6.0 + PENALTY)):
            rho = diagonal / 2.0 - np.sqrt(diagonal * diagonal / 4.0 - 1.0)
            at = first + 2 * solid
            take[:, at], take[:, at + 1] = rho**x, x * rho**x
            single = rho / (1.0 - rho**2) * rho**y
            double = rho**2 / (1.0 - rho**2) ** 2
            send[at + powers * solid] = single
            send[at + powers * (2 + solid)] = (double * (1.0 + rho**2) / (1.0 - rho**2) + double * y) * rho**y
            send[at + 1 + powers * (2 + solid)] = double * rho**y
            send[at + powers * 4] = single / PENALTY * (1.0 if solid == 0 else -1.0)
    forward = split(forward.reshape(2, padded, blocks, cells).transpose(0, 2, 1, 3))
    inverse = split(inverse.reshape(2, blocks, cells, padded))
    send = split(send.reshape(-1, blocks, cells).transpose(1, 0, 2))
    take = split(take.reshape(blocks, cells, -1))
    return forward, inverse, send, take, columns.astype(np.float32), 2 * padded, rest


def thirds(values, axis):
    high = values.astype(jnp.bfloat16)
    low = (values - high.astype(jnp.float32)).astype(jnp.bfloat16)
    return jnp.concatenate([high, high, low], axis=axis)


def pack_kernel(jobs, row_count, cells, earlier, x_ref, *refs):
    outs, (held, arrived) = refs[earlier:-2], refs[-2:]
    me = lax.axis_index("span")
    lines = x_ref.shape[1]
    all_tiles = lines // row_count
    own_tiles = all_tiles // lax.axis_size("span")
    pitch = held.shape[0] // cells
    some = cells // SPLIT
    copies = [
        pltpu.make_async_copy(
            x_ref.at[pl.ds(part * some, some)],
            held.reshape(cells, pitch, LANES).at[pl.ds(part * some, some), pl.ds(0, lines)],
            arrived.at[part],
        )
        for part in range(SPLIT)
    ]
    for copy in copies:
        copy.start()
    lane = lax.broadcasted_iota(jnp.int32, (some, LANES), 1)
    sides = []
    for part, copy in enumerate(copies):
        copy.wait()
        beside = jnp.zeros((some, LANES), jnp.float32)

        def line(tile, row):
            return held[pl.ds(part * some * pitch + tile * row_count + row, some, stride=pitch), :]

        for job, (out, base, d, rows, offset, tiles) in enumerate(jobs):
            first = jnp.bitwise_xor(me, d) * own_tiles + offset
            for i, row in enumerate(rows):
                at = base + i * cells + part * some
                for tile in range(tiles):
                    outs[out][at : at + some, tile * LANES : (tile + 1) * LANES] = line(first + tile, row)
                before = jnp.maximum(first - 1, 0)
                after = jnp.minimum(first + tiles, all_tiles - 1)
                for side, (tile, source) in enumerate(((before, LANES - 1), (after, 0))):
                    at = job * 8 + i * 2 + side
                    beside = jnp.where(lane == at, pltpu.roll(line(tile, row), (at - source) % LANES, 1), beside)
        sides.append(beside)
    if cells < LANES:
        sides.append(jnp.zeros((LANES - cells, LANES), jnp.float32))
    turned = jnp.concatenate(sides, axis=0).T
    for job, (out, base, _, rows, _, tiles) in enumerate(jobs):
        at = base + len(rows) * cells
        outs[out][at : at + 8, :LANES] = turned[job * 8 : (job + 1) * 8]
        if tiles > 1:
            outs[out][at : at + 8, LANES:] = jnp.zeros((8, (tiles - 1) * LANES), jnp.float32)


def place(d):
    half = lax.axis_size("span") // 2
    return jnp.bitwise_and(jnp.bitwise_xor(lax.axis_index("span"), d), half - 1)


def row_product(table, value):
    return jnp.dot(table, thirds(value, 0), preferred_element_type=jnp.float32)


def side_product(table, value):
    value = thirds(jnp.concatenate([value, jnp.zeros_like(value)], axis=0), 1)
    return lax.dot_general(table, value, (((1,), (1,)), ((), ())), preferred_element_type=jnp.float32)


def transform(rows, cells, near, far, forward_ref):
    def spectrum(lines, lanes, product):
        halves = []
        for parity in (0, 1):
            total = 0.0
            for d, block in enumerate(near):
                value = block[lines, lanes]
                if far:
                    other = far[d][lines, lanes]
                    value = value + other if parity == 0 else value - other
                total = total + product(forward_ref[parity, place(d)], value)
            halves.append(total)
        return jnp.concatenate(halves, axis=0)

    spectra = [spectrum(slice(i * cells, (i + 1) * cells), slice(None), row_product) for i in range(rows)]
    return spectra, spectrum(slice(rows * cells, rows * cells + 8), slice(0, cells), side_product)


def inverse_rows(sweeps, cells, inverse_ref, near, far=()):
    padded = sweeps[0].shape[0] // 2
    for i, sweep in enumerate(sweeps):
        even = thirds(sweep[:padded], 0)
        odd = thirds(sweep[padded:], 0)
        for d, out in enumerate(near):
            first = jnp.dot(inverse_ref[0, place(d)], even, preferred_element_type=jnp.float32)
            second = jnp.dot(inverse_ref[1, place(d)], odd, preferred_element_type=jnp.float32)
            out[i * cells : (i + 1) * cells, :] = first + second
            if far:
                far[d][i * cells : (i + 1) * cells, :] = first - second


def second_sweep(spectrum, one, above, below, sides, at, inverse_diagonal):
    width = one.shape[1]
    lane = lax.broadcasted_iota(jnp.int32, one.shape, 1)
    left = jnp.where(lane == 0, sides[:, at : at + 1], pltpu.roll(one, 1, 1))
    right = jnp.where(lane == width - 1, sides[:, at + 1 : at + 2], pltpu.roll(one, width - 1, 1))
    return (spectrum + above + below + left + right) * inverse_diagonal


def masks(mask_ref, rows, d, width):
    start = pl.multiple_of(jnp.bitwise_xor(lax.axis_index("span"), d) * width, LANES)
    last = mask_ref.shape[1] - LANES
    before = mask_ref[:, pl.ds(pl.multiple_of(jnp.maximum(start - LANES, 0), LANES), LANES)][:, LANES - 1 :]
    after = mask_ref[:, pl.ds(pl.multiple_of(jnp.minimum(start + width, last), LANES), LANES)][:, :1]
    before = jnp.where(start == 0, 2, before)
    after = jnp.where(start + width == mask_ref.shape[1], 2, after)
    lane = lax.broadcasted_iota(jnp.int32, (1, 16), 1)
    kinds = jnp.full((1, 16), 2, jnp.int32)
    for i, row in enumerate(rows):
        kinds = jnp.where(lane == 2 * i, before[row : row + 1], kinds)
        kinds = jnp.where(lane == 2 * i + 1, after[row : row + 1], kinds)
    return [mask_ref[row : row + 1, pl.ds(start, width)] for row in range(mask_ref.shape[0])], kinds


def pick(kind, fluid, solid):
    return jnp.where(kind == 0, fluid, jnp.where(kind == 1, solid, 0.0))


def one_over(columns_ref, first, modes):
    turned = columns_ref[...].T
    return turned[:modes, first : first + 1], turned[:modes, first + 1 : first + 2]


def paired_edge():
    return lax.rem(lax.axis_index("plane") + 1, 2)


def edge_kernel(rows, count, cells, *refs):
    near, far = refs[: count // 2], refs[count // 2 : count]
    forward_ref, columns_ref, mask_ref = refs[count : count + 3]
    spectrum_ref, ones_ref, paired_ref, other_ref, sides_ref = refs[-5:]
    spectra, sides = transform(len(rows), cells, near, far, forward_ref)
    modes, width = spectra[0].shape
    mask, kinds = masks(mask_ref, rows, 0, width)
    fluid, solid = one_over(columns_ref, 0, modes)
    ones = [spectrum * pick(mask[row], fluid, solid) for spectrum, row in zip(spectra, rows)]
    for i in (0, 1):
        spectrum_ref[i] = spectra[i]
        ones_ref[i] = ones[i]
    last = paired_edge() == 1
    paired_ref[...] = jnp.where(last, ones[1], ones[0])
    other_ref[...] = jnp.where(last, ones[0], ones[1])
    sides_ref[...] = sides * pick(kinds, fluid, solid)


def inner_sweeps(spectra, sides, rows, mask, kinds, fluid, solid, edges):
    diagonals = [pick(mask[row], fluid, solid) for row in rows]
    ones = [spectrum * diagonal for spectrum, diagonal in zip(spectra, diagonals)]
    around = [edges[0], *ones, edges[1]]
    sides = sides * pick(kinds, fluid, solid)
    return ones, [
        second_sweep(spectra[i], ones[i], around[i], around[i + 2], sides, 2 * i, diagonals[i])
        for i in range(len(rows))
    ]


def inner_kernel(rows, count, cells, *refs):
    half = count // 2
    far_ref, forward_ref, inverse_ref, columns_ref, mask_ref, edges_ref = refs[half : half + 6]
    outs, ones_ref = refs[-1 - half : -1], refs[-1]
    size = len(rows) * cells + 8
    far = [far_ref.at[e * size : (e + 1) * size] for e in range(half)]
    spectra, sides = transform(len(rows), cells, refs[:half], far, forward_ref)
    modes, width = spectra[0].shape
    mask, kinds = masks(mask_ref, rows, 0, width)
    fluid, solid = one_over(columns_ref, 0, modes)
    ones, sweeps = inner_sweeps(spectra, sides, rows, mask, kinds, fluid, solid, (edges_ref[0], edges_ref[1]))
    ones_ref[0] = ones[0]
    ones_ref[1] = ones[-1]
    inverse_rows(sweeps, cells, inverse_ref, outs)


def local_kernel(rows, edge_rows, count, cells, *refs):
    half = count // 2
    message_ref, edges = refs[0], refs[1 : 1 + half]
    forward_ref, inverse_ref, columns_ref, mask_ref = refs[1 + half : 5 + half]
    out_ref = refs[-1]
    size = len(rows) * cells + 8
    near = [message_ref.at[d * size : (d + 1) * size] for d in range(half)]
    spectra, sides = transform(len(rows), cells, near, (), forward_ref)
    edge_spectra, _ = transform(len(edge_rows), cells, edges, (), forward_ref)
    modes, width = spectra[0].shape
    mask, kinds = masks(mask_ref, rows, half, width)
    fluid, solid = one_over(columns_ref, 0, modes)
    around = [spectrum * pick(mask[row], fluid, solid) for spectrum, row in zip(edge_spectra, edge_rows)]
    _, sweeps = inner_sweeps(spectra, sides, rows, mask, kinds, fluid, solid, around)
    size = len(rows) * cells
    inverse_rows(sweeps, cells, inverse_ref, [out_ref.at[d * size : (d + 1) * size] for d in range(half)])


def send_kernel(rows, edge_rows, rest, count, cells, *refs):
    half = count // 2
    inner, edges = refs[:half], refs[half : 2 * half]
    send_ref, columns_ref, mask_ref, out_ref = refs[2 * half :]

    def product(blocks, lines, lanes, kind):
        return sum(kind(send_ref[place(d)], block[lines, lanes]) for d, block in enumerate(blocks))

    def whole(blocks, i):
        return product(blocks, slice(i * cells, (i + 1) * cells), slice(None), row_product)

    spectra = [whole(inner, i) for i in range(len(rows))]
    around = [whole(edges, i) for i in range(len(edge_rows))]
    sides = product(inner, slice(len(rows) * cells, len(rows) * cells + 8), slice(0, cells), side_product)
    mask, kinds = masks(mask_ref, rows, 0, inner[0].shape[1])
    fluid, solid = one_over(columns_ref, 2, rest)
    outer = [values[:rest] * pick(mask[row], fluid, solid) for values, row in zip(around, edge_rows)]
    _, sweeps = inner_sweeps([v[:rest] for v in spectra], sides[:rest], rows, mask, kinds, fluid, solid, outer)

    def power(values, at):
        return values[rest + 8 * at : rest + 8 * at + 8]

    numbers = []
    for target in (0, 1):

        def beside(values, kind):
            same, cross = power(values, 2 + target), power(values, 4)
            return pick(kind, same, cross) if target == 0 else pick(kind, cross, same)

        own = [beside(values, mask[row]) for values, row in zip(spectra, rows)]
        edge = [beside(values, mask[row]) for values, row in zip(around, edge_rows)]
        column = [edge[0], *own, edge[1]]
        outside = beside(sides, kinds)
        numbers.append(
            [
                second_sweep(power(spectra[i], target), own[i], column[i], column[i + 2], outside, 2 * i, 1.0)
                for i in range(len(rows))
            ]
        )
    for i, row in enumerate(rows):
        base = i * (rest + 8)
        out_ref[base : base + rest, :] = sweeps[i]
        out_ref[base + rest : base + rest + 8, :] = jnp.where(mask[row] == 0, numbers[0][i], numbers[1][i])


def take_kernel(rows, count, cells, *refs):
    half = count // 2
    message_ref, local_ref, take_ref = refs[:3]
    outs = refs[-half:]
    lines = message_ref.shape[0] // len(rows)
    short = take_ref.shape[2] // 3 - lines
    for i in range(len(rows)):
        values = message_ref[i * lines : (i + 1) * lines, :]
        if short:
            values = jnp.concatenate([values, jnp.zeros((short, values.shape[1]), jnp.float32)], axis=0)
        values = thirds(values, 0)
        for d, out in enumerate(outs):
            base = (d * len(rows) + i) * cells
            out[i * cells : (i + 1) * cells, :] = local_ref[base : base + cells, :] + jnp.dot(
                take_ref[place(d)], values, preferred_element_type=jnp.float32
            )


def rim_kernel(rows, order, count, cells, *refs):
    spectrum_ref, edges_ref, sides_ref, halo_ref, ones_ref, inverse_ref, columns_ref, mask_ref = refs[:8]
    outs = refs[-count:]
    _, modes, width = edges_ref.shape
    edge = paired_edge() if order == 0 else 1 - paired_edge()
    mask, _ = masks(mask_ref, rows, 0, width)
    fluid, solid = one_over(columns_ref, 0, modes)
    sides = jnp.where(edge == 0, sides_ref[:, 0:2], sides_ref[:, 2:4])
    diagonal = pick(jnp.where(edge == 0, mask[rows[0]], mask[rows[1]]), fluid, solid)
    sweep = second_sweep(spectrum_ref[edge], edges_ref[edge], halo_ref[...], ones_ref[edge], sides, 0, diagonal)
    inverse_rows([sweep], cells, inverse_ref, outs[: count // 2], outs[count // 2 :])


def join_kernel(rows, cells, near, *refs):
    own_ref, blocks, out_ref = refs[0], refs[1 : 1 + rows * near], refs[-1]
    size = rows * cells + 8
    out_ref[:size, :] = own_ref[...]
    for d in range(near):
        base = (d + 1) * size
        out_ref[base + rows * cells : base + size, :] = jnp.zeros((8, out_ref.shape[1]), jnp.float32)
        for i in range(rows):
            block = blocks[d * rows + i]
            out_ref[base + i * cells : base + (i + 1) * cells, :] = block[:cells, :]
            at = base + rows * cells + 2 * i
            out_ref[at : at + 2, :] = block[cells : cells + 2, :]


def unpack_kernel(pieces, devices, row_count, cells, *refs):
    me = lax.axis_index("span")
    blocks, (out_ref, held, done) = refs[: len(pieces)], refs[-3:]
    pitch = held.shape[0] // cells
    own_lines = out_ref.shape[1] // lax.axis_size("span")
    some = cells // SPLIT
    edge_rows = {"near": paired_edge() * (row_count - 1), "far": (1 - paired_edge()) * (row_count - 1)}
    copies = []
    for part in range(SPLIT):
        for block, (d, base, rows, offset, tiles) in zip(blocks, pieces):
            for i, row in enumerate(rows):
                if row in edge_rows:
                    row = edge_rows[row]
                line = base + i * cells + part * some
                for tile in range(tiles):
                    at = part * some * pitch + devices.index(d) * own_lines + (offset + tile) * row_count + row
                    held[pl.ds(at, some, stride=pitch), :] = block[line : line + some, tile * LANES : (tile + 1) * LANES]
        for at, d in enumerate(devices):
            first = pl.multiple_of(jnp.bitwise_xor(me, d) * own_lines, own_lines)
            copies.append(
                pltpu.make_async_copy(
                    held.reshape(cells, pitch, LANES).at[pl.ds(part * some, some), pl.ds(at * own_lines, own_lines)],
                    out_ref.at[pl.ds(part * some, some), pl.ds(first, own_lines)],
                    done.at[part, at],
                )
            )
            copies[-1].start()
    for copy in copies:
        copy.wait()


def call(kernel, outs, *args, cost=LONG, earlier=()):
    shapes = [jax.ShapeDtypeStruct(shape, jnp.float32) for shape in outs]
    return pl.pallas_call(
        kernel,
        out_shape=shapes,
        in_specs=[VMEM] * len(args) + [ANY] * len(earlier),
        out_specs=[VMEM] * len(outs),
        compiler_params=PARAMS,
        cost_estimate=cost,
    )(*args, *earlier)


def swap(block, d):
    return lax.ppermute(block, "span", [(i, i ^ d) for i in range(lax.axis_size("span"))])


def local(pressure_source, solid_mask):
    count = lax.axis_size("span")
    half = count // 2
    plane_count = lax.axis_size("plane")
    cells, row_count, columns = pressure_source.shape
    width = columns // count
    tiles = width // LANES
    inner = tuple(range(1, row_count - 1))
    edges = (0, row_count - 1)
    near, far = range(1, half), range(half, count)
    *arrays, modes, rest = tables(cells * count, cells)
    forward, inverse, send, take, diagonals = map(jnp.asarray, arrays)

    lines = columns // LANES * row_count
    source = pressure_source.reshape(cells, row_count, columns // LANES, LANES).transpose(0, 2, 1, 3)
    source = source.reshape(cells, lines, LANES)
    scratch = [pltpu.VMEM((cells * (lines + 8), LANES), jnp.float32), pltpu.SemaphoreType.DMA((SPLIT,))]

    def pack(source, wanted, *earlier):
        jobs = [(at, 0, d, rows, 0, tiles) for at, (d, rows) in enumerate(wanted)]
        shapes = [(len(rows) * cells + 8, width) for _, rows in wanted]
        return pl.pallas_call(
            functools.partial(pack_kernel, jobs, row_count, cells, len(earlier)),
            out_shape=[jax.ShapeDtypeStruct(shape, jnp.float32) for shape in shapes],
            in_specs=[ANY] * (1 + len(earlier)),
            out_specs=[VMEM] * len(shapes),
            scratch_shapes=scratch,
            compiler_params=PARAMS,
            cost_estimate=LONG,
        )(source, *earlier)

    packed = pack(pltpu.with_memory_space_constraint(source, pltpu.HBM), [(d, edges) for d in range(1, count)])
    edge_blocks = [swap(block, d) for d, block in enumerate(packed, 1)]
    wanted = [(d, inner) for d in range(half + 1)] + [(0, edges)] + [(d, edges) for d in far]
    wanted += [(half + d, (row,)) for d in near for row in inner]
    packed = pack(source, wanted, packed[half - 1])
    edge_blocks = [packed[half + 1], *edge_blocks]
    inner_blocks = [packed[0]] + [swap(packed[d], d) for d in near]
    chip_edges = [packed[half + 2]] + [swap(packed[half + 2 + d], d) for d in near]
    relayed = packed[2 * half + 2 :]
    relayed = [swap(relayed[(d - 1) * len(inner) + i], d) for d in near for i in range(len(inner))]
    (message,) = call(
        functools.partial(join_kernel, len(inner), cells, half - 1),
        [(half * (len(inner) * cells + 8), width)],
        packed[half], *relayed, cost=SHORT, earlier=(edge_blocks[half],),
    )
    arrived = swap(message, half)

    length = len(inner) * cells
    (sent,) = call(
        functools.partial(send_kernel, inner, edges, rest, count, cells),
        [(len(inner) * (rest + 8), width)],
        *inner_blocks, *edge_blocks[:half], send, diagonals, solid_mask, cost=SHORT,
    )
    taken = swap(sent, half)
    (own,) = call(
        functools.partial(local_kernel, inner, edges, count, cells),
        [(half * length, width)],
        message, *chip_edges, forward, inverse, diagonals, solid_mask, cost=SHORT,
    )

    spectrum, edge_ones, paired, other, sides = call(
        functools.partial(edge_kernel, edges, count, cells),
        [(2, modes, width), (2, modes, width), (modes, width), (modes, width), (modes, 16)],
        *edge_blocks, forward, diagonals, solid_mask, earlier=(own,),
    )
    pairs = [[(i, i ^ 1) for i in range(plane_count)], [(i, ((i + 1) ^ 1) - 1) for i in range(plane_count)]]
    halos = [
        lax.ppermute(row, "plane", [(i, j) for i, j in pair if 0 <= j < plane_count])
        for row, pair in zip((paired, other), pairs)
    ]

    *made, ones = call(
        functools.partial(inner_kernel, inner, count, cells),
        [(length, width)] * half + [(2, modes, width)],
        *inner_blocks, arrived, forward, inverse, diagonals, solid_mask, edge_ones, cost=SHORT,
    )
    pieces = [(made[0], 0, 0, inner, 0, tiles)]
    pieces += [(swap(made[d], d), d, 0, inner, 0, tiles) for d in near]
    before = []
    for order, name in enumerate(("near", "far")):
        outs = call(
            functools.partial(rim_kernel, edges, order, count, cells),
            [(cells, width)] * count,
            spectrum, edge_ones, sides, halos[order], ones, inverse, diagonals, solid_mask,
            cost=LONG if order else SHORT, earlier=(*before, taken) if order else (),
        )
        before = (outs[-1],)
        pieces.append((outs[0], 0, 0, (name,), 0, tiles))
        pieces += [(swap(outs[d], d), d, 0, (name,), 0, tiles) for d in (*far, *near)]
        rim_got = pieces[-count + 1 :][0][0] if order == 0 else rim_got
    rebuilt = call(
        functools.partial(take_kernel, inner, count, cells), [(length, width)] * half, taken, own, take,
        cost=SHORT, earlier=(*before, rim_got),
    )
    pieces.append((rebuilt[0], half, 0, inner, 0, tiles))
    pieces += [(swap(rebuilt[d], d), half + d, 0, inner, 0, tiles) for d in near]

    result = None
    own_lines = tiles * row_count
    for devices in (range(count - 1), [count - 1]) if own_lines % 8 == 0 else (range(count),):
        chosen = [piece for piece in pieces if piece[1] in devices]
        previous = () if result is None else (result,)
        result = pl.pallas_call(
            functools.partial(unpack_kernel, [piece[1:] for piece in chosen], list(devices), row_count, cells),
            out_shape=jax.ShapeDtypeStruct((cells, lines, LANES), jnp.float32),
            in_specs=[VMEM] * len(chosen) + [ANY] * len(previous),
            out_specs=ANY,
            scratch_shapes=[
                pltpu.VMEM((cells * (len(devices) * own_lines + 8), LANES), jnp.float32),
                pltpu.SemaphoreType.DMA((SPLIT, len(devices))),
            ],
            input_output_aliases={len(chosen): 0} if previous else {},
            compiler_params=PARAMS,
            cost_estimate=SHORT if previous else LONG,
        )(*[piece[0] for piece in chosen], *previous)
    result = result.reshape(cells, columns // LANES, row_count, LANES).transpose(0, 2, 1, 3)
    return result.reshape(cells, row_count, columns)


def solution(mesh):
    placed = (P("span", "plane", None), P("plane", None))
    return jax.shard_map(
        local, mesh=mesh, in_specs=placed, out_specs=P("span", "plane", None), check_vma=False
    )
```

time: 52.7 us -> 53.4 us (1.013)
  the two profiles are of different devices: /device:TPU:0 before, /device:TPU:25 now
where the time goes in v13:
time: 53.4 us; the launch traced here: 53.1 us
  starting transfers between devices  19.3 us (36%)
  waiting for transfers between devices  19 us (36%)
  Pallas kernels  14.5 us (27%)
    ppermute x17, starting transfers between devices, swap(): lax.ppermute(block, 'span', [(i, i ^ d) for i in range(lax.axis_size('spa...  16 us
    ppermute x17, waiting for transfers between devices, swap(): lax.ppermute(block, 'span', [(i, i ^ d) for i in range(lax.axis_size('spa...  12 us
    pallas_call x8, Pallas kernels, call(): pl.pallas_call(kernel, out_shape=shapes, in_specs=[VMEM] * len(args) + [A...  8.04 us
    ppermute x2, waiting for transfers between devices, local(): lax.ppermute(row, 'plane', [(i, j) for i, j in pair if 0 <= j < plane_cou...  7.03 us
    ppermute x2, starting transfers between devices, local(): lax.ppermute(row, 'plane', [(i, j) for i, j in pair if 0 <= j < plane_cou...  3.32 us
    pallas_call x2, Pallas kernels, local(): pl.pallas_call(functools.partial(unpack_kernel, [piece[1:] for piece in c...  3.28 us
    pallas_call x2, Pallas kernels, pack(): pl.pallas_call(functools.partial(pack_kernel, jobs, row_count, cells, len...  3.16 us
  transfers between devices with their start and end apart: 19, of which 9 were waited for; matrix products, arithmetic and copies ran while one was open for 0% of the time, Pallas kernels for 22%

profile of v13, /device:TPU:25, one launch (start us, length us, event | category | flops | bytes accessed | tf_op | source)
XLA Modules:
  0.0 53.1 jit_solution(10867635134931752939)
XLA Ops:
  0.0 1.9 %shard_map.73 = (f32[264,256]{1,0:T(8,128)S(1)}, f32[264,256]{1,0:T(8,128)S(1)}, f32[264,256]{1,0:T(8,128)S(1)}) custom-call(f32[128,32,128]{2,1,0:T(8,128)} %bitcast.10), custom_call_target="tpu_custom_call" | custom-call | bytes 200000000 | tf_op jit(solution)/shard_map/pallas_call | solution.py:446
  2.0 1.3 %collective-permute-start.1 = (f32[264,256]{1,0:T(8,128)S(1)}, f32[264,256]{1,0:T(8,128)S(1)}, u32[]{:S(2)}, u32[]{:S(2)}) collective-permute-start(f32[264,256]{1,0:T(8,128)S(1)} %get-tuple-element.34.refs_0_), channel_id=1, source_target_pairs={{0,2},{1,3},{2,0},{3,1},{4,6},{5,7},{6,4},{7,5},{8,10},{9,11},{10,... | collective-permute-start | bytes 811016 | tf_op jit(solution)/shard_map/ppermute | solution.py:422
  3.3 1.3 %shard_map.74 = (f32[264,256]{1,0:T(8,128)S(1)}, f32[264,256]{1,0:T(8,128)S(1)}, f32[264,256]{1,0:T(8,128)S(1)}, f32[264,256]{1,0:T(8,128)S(1)}, f32[264,256]{1,...) custom-call(f32[128,32,128]{2,1,0:T(8,128)S(1)} %bitcast.11, ...), custom_call_target="tpu_custom_call" | custom-call | bytes 200000000 | tf_op jit(solution)/shard_map/pallas_call | solution.py:446
  4.5 1.0 %collective-permute-start.3 = (f32[136,256]{1,0:T(8,128)S(1)}, f32[136,256]{1,0:T(8,128)S(1)}, u32[]{:S(2)}, u32[]{:S(2)}) collective-permute-start(f32[136,256]{1,0:T(8,128)S(1)} %get-tuple-element.39), channel_id=1, source_target_pairs={{0,1},{1,0},{2,3},{3,2},{4,5},{5,4},{6,7},{7,6},{8,9},{9,8},{10,11... | collective-permute-start | bytes 417800 | tf_op jit(solution)/shard_map/ppermute | solution.py:422
  7.0 2.3 %collective-permute-done.1.refs_3_.refs_2_ = f32[264,256]{1,0:T(8,128)S(1)} collective-permute-done((f32[264,256]{1,0:T(8,128)S(1)}, f32[264,256]{1,0:T(8,128)S(1)}, u32[]{:S(2)}, u32[]{:S(2)}) %collective-permute-start.1) | collective-permute-done | bytes 270368 | tf_op jit(solution)/shard_map/ppermute | solution.py:422
  9.4 1.3 %collective-permute-start.8 = (f32[528,256]{1,0:T(8,128)S(1)}, f32[528,256]{1,0:T(8,128)S(1)}, u32[]{:S(2)}, u32[]{:S(2)}) collective-permute-start(f32[528,256]{1,0:T(8,128)S(1)} %shard_map.75.refs_0_), channel_id=1, source_target_pairs={{0,2},{1,3},{2,0},{3,1},{4,6},{5,7},{6,4},{7,5},{8,10},{9,11},{10,... | collective-permute-start | bytes 1622024 | tf_op jit(solution)/shard_map/ppermute | solution.py:422
  10.7 3.0 %collective-permute-start.7 = (f32[264,256]{1,0:T(8,128)S(1)}, f32[264,256]{1,0:T(8,128)S(1)}, u32[]{:S(2)}, u32[]{:S(2)}) collective-permute-start(f32[264,256]{1,0:T(8,128)S(1)} %get-tuple-element.48), channel_id=1, source_target_pairs={{0,1},{1,0},{2,3},{3,2},{4,5},{5,4},{6,7},{7,6},{8,9},{9,8},{10,11... | collective-permute-start | bytes 811016 | tf_op jit(solution)/shard_map/ppermute | solution.py:422
  13.7 1.9 %shard_map.76.refs_7_.refs_1_ = f32[512,256]{1,0:T(8,128)S(1)} custom-call(f32[528,256]{1,0:T(8,128)S(1)} %shard_map.75.refs_0_, f32[264,256]{1,0:T(8,128)S(1)} %get-tuple-element.41.refs_1_, f32[264,256]{1,0:T(8,128)S(1)} %collective-permute-done.5.refs_2_, bf16[2,2,176,384]{3,2,1,0:T(8,128)(2,1)S(1)} %copy-done.2, bf16[2,2,128,528]{3,2,1,0:T(8,128)(2,1)S(1)} %copy-done, ...), custom_call_target="tpu_custom_call" | custom-call | bytes 1024 | tf_op jit(solution)/shard_map/pallas_call | solution.py:411
  15.7 1.3 %collective-permute-done.2.refs_3_ = f32[264,256]{1,0:T(8,128)S(1)} collective-permute-done((f32[264,256]{1,0:T(8,128)S(1)}, f32[264,256]{1,0:T(8,128)S(1)}, u32[]{:S(2)}, u32[]{:S(2)}) %collective-permute-start.2) | collective-permute-done | bytes 270368 | tf_op jit(solution)/shard_map/ppermute | solution.py:422
  17.8 1.3 %collective-permute-start.6 = (f32[352,256]{1,0:T(8,128)S(1)}, f32[352,256]{1,0:T(8,128)S(1)}, u32[]{:S(2)}, u32[]{:S(2)}) collective-permute-start(f32[352,256]{1,0:T(8,128)S(1)} %get-tuple-element.46), channel_id=1, source_target_pairs={{0,4},{4,0},{8,12},{12,8},{16,20},{20,16},{24,28},{28,24},{1,5},{5... | collective-permute-start | bytes 1081352 | tf_op jit(solution)/shard_map/ppermute | solution.py:493
  19.1 0.9 %shard_map.80 = f32[368,256]{1,0:T(8,128)S(1)} custom-call(f32[264,256]{1,0:T(8,128)S(1)} %get-tuple-element.47.refs_0_, f32[264,256]{1,0:T(8,128)S(1)} %collective-permute-done.7.refs_1_, f32[264,256]{1,0:T(8,128)S(1)} %get-tuple-element.35.refs_0_.refs_2_, f32[264,256]{1,0:T(8,128)S(1)} %collective-permute-done.refs_1_.refs_3_, ...), custom_call_target="tpu_custom_call" | custom-call | bytes 1024 | tf_op jit(solution)/shard_map/pallas_call | solution.py:411
  20.1 1.5 %collective-permute-start.11 = (f32[368,256]{1,0:T(8,128)S(1)}, f32[368,256]{1,0:T(8,128)S(1)}, u32[]{:S(2)}, u32[]{:S(2)}) collective-permute-start(f32[368,256]{1,0:T(8,128)S(1)} %shard_map.80), channel_id=1, source_target_pairs={{0,2},{1,3},{2,0},{3,1},{4,6},{5,7},{6,4},{7,5},{8,10},{9,11},{10,... | collective-permute-start | bytes 1130504 | tf_op jit(solution)/shard_map/ppermute | solution.py:422
  21.6 2.0 %collective-permute-start.10 = (f32[352,256]{1,0:T(8,128)S(1)}, f32[352,256]{1,0:T(8,128)S(1)}, u32[]{:S(2)}, u32[]{:S(2)}) collective-permute-start(f32[352,256]{1,0:T(8,128)S(1)} %get-tuple-element.51), channel_id=1, source_target_pairs={{4,8},{8,4},{12,16},{16,12},{20,24},{24,20},{5,9},{9,5},{13,17},{1... | collective-permute-start | bytes 1081352 | tf_op jit(solution)/shard_map/ppermute | solution.py:493
  23.6 3.3 %collective-permute-done.8.refs_2_ = f32[528,256]{1,0:T(8,128)S(1)} collective-permute-done((f32[528,256]{1,0:T(8,128)S(1)}, f32[528,256]{1,0:T(8,128)S(1)}, u32[]{:S(2)}, u32[]{:S(2)}) %collective-permute-start.8) | collective-permute-done | bytes 540704 | tf_op jit(solution)/shard_map/ppermute | solution.py:422
  27.0 1.8 %shard_map.78 = (f32[256,256]{1,0:T(8,128)S(1)}, f32[256,256]{1,0:T(8,128)S(1)}, f32[2,352,256]{2,1,0:T(8,128)S(1)}) custom-call(f32[264,256]{1,0:T(8,128)S(1)} %get-tuple-element.47.refs_0_, f32[264,256]{1,0:T(8,128)S(1)} %collective-permute-done.7.refs_1_, f32[528,256]{1,0:T(8,128)S(1)} %collective-permute-done.8.refs_2_, ...), custom_call_target="tpu_custom_call" | custom-call | bytes 1024 | tf_op jit(solution)/shard_map/pallas_call | solution.py:411
  28.7 7.0 %collective-permute-done.6.refs_3_ = f32[352,256]{1,0:T(8,128)S(1)} collective-permute-done((f32[352,256]{1,0:T(8,128)S(1)}, f32[352,256]{1,0:T(8,128)S(1)}, u32[]{:S(2)}, u32[]{:S(2)}) %collective-permute-start.6) | collective-permute-done | bytes 360480 | tf_op jit(solution)/shard_map/ppermute | solution.py:493
  35.8 1.1 %shard_map.79 = (f32[128,256]{1,0:T(8,128)S(1)}, f32[128,256]{1,0:T(8,128)S(1)}, f32[128,256]{1,0:T(8,128)S(1)}, f32[128,256]{1,0:T(8,128)S(1)}) custom-call(f32[2,352,256]{2,1,0:T(8,128)S(1)} %get-tuple-element.43.refs_0_, f32[2,352,256]{2,1,0:T(8,128)S(1)} %get-tuple-element.44.refs_7_.refs_1_, f32[352,16]{1,0:T(8,128)S(1)} %get-tuple-element.45.refs_2_, ...), custom_call_target="tpu_custom_call" | custom-call | bytes 1024 | tf_op jit(solution)/shard_map/pallas_call | solution.py:411
  38.1 1.1 %shard_map.81 = (f32[128,256]{1,0:T(8,128)S(1)}, f32[128,256]{1,0:T(8,128)S(1)}, f32[128,256]{1,0:T(8,128)S(1)}, f32[128,256]{1,0:T(8,128)S(1)}) custom-call(f32[2,352,256]{2,1,0:T(8,128)S(1)} %get-tuple-element.43.refs_0_, f32[2,352,256]{2,1,0:T(8,128)S(1)} %get-tuple-element.44.refs_7_.refs_1_, f32[352,16]{1,0:T(8,128)S(1)} %get-tuple-element.45.refs_2_, ...), custom_call_target="tpu_custom_call" | custom-call | bytes 200000000 | tf_op jit(solution)/shard_map/pallas_call | solution.py:411
  39.2 1.3 %collective-permute-start.17 = (f32[128,256]{1,0:T(8,128)S(1)}, f32[128,256]{1,0:T(8,128)S(1)}, u32[]{:S(2)}, u32[]{:S(2)}) collective-permute-start(f32[128,256]{1,0:T(8,128)S(1)} %get-tuple-element.60), channel_id=1, source_target_pairs={{0,2},{1,3},{2,0},{3,1},{4,6},{5,7},{6,4},{7,5},{8,10},{9,11},{10,... | collective-permute-start | bytes 393224 | tf_op jit(solution)/shard_map/ppermute | solution.py:422
  41.6 2.1 %collective-permute-start.14 = (f32[256,256]{1,0:T(8,128)S(1)}, f32[256,256]{1,0:T(8,128)S(1)}, u32[]{:S(2)}, u32[]{:S(2)}) collective-permute-start(f32[256,256]{1,0:T(8,128)S(1)} %get-tuple-element.54), channel_id=1, source_target_pairs={{0,1},{1,0},{2,3},{3,2},{4,5},{5,4},{6,7},{7,6},{8,9},{9,8},{10,11... | collective-permute-start | bytes 786440 | tf_op jit(solution)/shard_map/ppermute | solution.py:422
  44.8 1.5 %collective-permute-start.12 = (f32[128,256]{1,0:T(8,128)S(1)}, f32[128,256]{1,0:T(8,128)S(1)}, u32[]{:S(2)}, u32[]{:S(2)}) collective-permute-start(f32[128,256]{1,0:T(8,128)S(1)} %get-tuple-element.52.refs_3_), channel_id=1, source_target_pairs={{0,3},{1,2},{2,1},{3,0},{4,7},{5,6},{6,5},{7,4},{8,11},{9,10},{10,... | collective-permute-start | bytes 393224 | tf_op jit(solution)/shard_map/ppermute | solution.py:422
  46.3 2.4 %shard_map.83.refs_3_ = f32[128,32,128]{2,1,0:T(8,128)} custom-call(f32[256,256]{1,0:T(8,128)S(1)} %get-tuple-element.55.refs_0_, f32[256,256]{1,0:T(8,128)S(1)} %collective-permute-done.15.refs_1_, f32[128,256]{1,0:T(8,128)S(1)} %get-tuple-element.57.refs_2_, f32[128,256]{1,0:T(8,128)S(1)} %collective-permute-done.13.refs_4_.refs_3_, ...), custom_call_target="tpu_custom_call" | custom-call | bytes 200000000 | tf_op jit(solution)/shard_map/pallas_call | solution.py:528
  48.7 1.2 %collective-permute-done.9.refs_0_ = f32[128,256]{1,0:T(8,128)S(1)} collective-permute-done((f32[128,256]{1,0:T(8,128)S(1)}, f32[128,256]{1,0:T(8,128)S(1)}, u32[]{:S(2)}, u32[]{:S(2)}) %collective-permute-start.9) | collective-permute-done | bytes 131104 | tf_op jit(solution)/shard_map/ppermute | solution.py:422
  49.9 2.3 %collective-permute-done.12.refs_1_ = f32[128,256]{1,0:T(8,128)S(1)} collective-permute-done((f32[128,256]{1,0:T(8,128)S(1)}, f32[128,256]{1,0:T(8,128)S(1)}, u32[]{:S(2)}, u32[]{:S(2)}) %collective-permute-start.12) | collective-permute-done | bytes 131104 | tf_op jit(solution)/shard_map/ppermute | solution.py:422
  (40 shorter events, 6.9 us)
Async XLA Ops:
  1.9 11.8 %copy-start = (bf16[2,2,128,528]{3,2,1,0:T(8,128)(2,1)S(1)}, bf16[2,2,128,528]{3,2,1,0:T(8,128)(2,1)}, u32[]{:S(2)}) copy-start(bf16[2,2,128,528]{3,2,1,0:T(8,128)(2,1)} %constant.11.clone.refs_4_.refs_5_) | copy-start | bytes 1622020
  1.9 11.8 %copy-start.2 = (bf16[2,2,176,384]{3,2,1,0:T(8,128)(2,1)S(1)}, bf16[2,2,176,384]{3,2,1,0:T(8,128)(2,1)}, u32[]{:S(2)}) copy-start(bf16[2,2,176,384]{3,2,1,0:T(8,128)(2,1)} %constant.10.clone.refs_3_.refs_4_) | copy-start | bytes 1622020
  1.9 11.8 %copy-start.3 = (s32[4,1024]{1,0:T(4,128)S(1)}, s32[4,1024]{1,0:T(4,128)}, u32[]{:S(2)}) copy-start(s32[4,1024]{1,0:T(4,128)} %refs_7_.3) | copy-start | bytes 49156
  1.9 11.8 %copy-start.4 = (f32[8,384]{1,0:T(8,128)S(1)}, f32[8,384]{1,0:T(8,128)}, u32[]{:S(2)}) copy-start(f32[8,384]{1,0:T(8,128)} %constant.14.clone.refs_5_.refs_6_) | copy-start | bytes 36868
  2.0 7.4 %collective-permute-start.1 = (f32[264,256]{1,0:T(8,128)S(1)}, f32[264,256]{1,0:T(8,128)S(1)}, u32[]{:S(2)}, u32[]{:S(2)}) collective-permute-start(f32[264,256]{1,0:T(8,128)S(1)} %get-tuple-element.34.refs_0_), channel_id=1, source_target_pairs={{0,2},{1,3},{2,0},{3,1},{4,6},{5,7},{6,4},{7,5},{8,10},{9,11},{10,... | collective-permute-start | bytes 811016 | tf_op jit(solution)/shard_map/ppermute | solution.py:422
  4.5 2.0 %collective-permute-start.3 = (f32[136,256]{1,0:T(8,128)S(1)}, f32[136,256]{1,0:T(8,128)S(1)}, u32[]{:S(2)}, u32[]{:S(2)}) collective-permute-start(f32[136,256]{1,0:T(8,128)S(1)} %get-tuple-element.39), channel_id=1, source_target_pairs={{0,1},{1,0},{2,3},{3,2},{4,5},{5,4},{6,7},{7,6},{8,9},{9,8},{10,11... | collective-permute-start | bytes 417800 | tf_op jit(solution)/shard_map/ppermute | solution.py:422
  5.6 1.5 %collective-permute-start.4 = (f32[136,256]{1,0:T(8,128)S(1)}, f32[136,256]{1,0:T(8,128)S(1)}, u32[]{:S(2)}, u32[]{:S(2)}) collective-permute-start(f32[136,256]{1,0:T(8,128)S(1)} %get-tuple-element.40), channel_id=1, source_target_pairs={{0,1},{1,0},{2,3},{3,2},{4,5},{5,4},{6,7},{7,6},{8,9},{9,8},{10,11... | collective-permute-start | bytes 417800 | tf_op jit(solution)/shard_map/ppermute | solution.py:422
  5.6 8.1 %collective-permute-start.5 = (f32[264,256]{1,0:T(8,128)S(1)}, f32[264,256]{1,0:T(8,128)S(1)}, u32[]{:S(2)}, u32[]{:S(2)}) collective-permute-start(f32[264,256]{1,0:T(8,128)S(1)} %get-tuple-element.42), channel_id=1, source_target_pairs={{0,1},{1,0},{2,3},{3,2},{4,5},{5,4},{6,7},{7,6},{8,9},{9,8},{10,11... | collective-permute-start | bytes 811016 | tf_op jit(solution)/shard_map/ppermute | solution.py:422
  6.1 9.6 %collective-permute-start = (f32[264,256]{1,0:T(8,128)S(1)}, f32[264,256]{1,0:T(8,128)S(1)}, u32[]{:S(2)}, u32[]{:S(2)}) collective-permute-start(f32[264,256]{1,0:T(8,128)S(1)} %get-tuple-element.36), channel_id=1, source_target_pairs={{0,1},{1,0},{2,3},{3,2},{4,5},{5,4},{6,7},{7,6},{8,9},{9,8},{10,11... | collective-permute-start | bytes 811016 | tf_op jit(solution)/shard_map/ppermute | solution.py:422
  6.6 10.4 %collective-permute-start.2 = (f32[264,256]{1,0:T(8,128)S(1)}, f32[264,256]{1,0:T(8,128)S(1)}, u32[]{:S(2)}, u32[]{:S(2)}) collective-permute-start(f32[264,256]{1,0:T(8,128)S(1)} %get-tuple-element.37), channel_id=1, source_target_pairs={{0,3},{1,2},{2,1},{3,0},{4,7},{5,6},{6,5},{7,4},{8,11},{9,10},{10,... | collective-permute-start | bytes 811016 | tf_op jit(solution)/shard_map/ppermute | solution.py:422
  9.4 17.5 %collective-permute-start.8 = (f32[528,256]{1,0:T(8,128)S(1)}, f32[528,256]{1,0:T(8,128)S(1)}, u32[]{:S(2)}, u32[]{:S(2)}) collective-permute-start(f32[528,256]{1,0:T(8,128)S(1)} %shard_map.75.refs_0_), channel_id=1, source_target_pairs={{0,2},{1,3},{2,0},{3,1},{4,6},{5,7},{6,4},{7,5},{8,10},{9,11},{10,... | collective-permute-start | bytes 1622024 | tf_op jit(solution)/shard_map/ppermute | solution.py:422
  10.7 8.4 %collective-permute-start.7 = (f32[264,256]{1,0:T(8,128)S(1)}, f32[264,256]{1,0:T(8,128)S(1)}, u32[]{:S(2)}, u32[]{:S(2)}) collective-permute-start(f32[264,256]{1,0:T(8,128)S(1)} %get-tuple-element.48), channel_id=1, source_target_pairs={{0,1},{1,0},{2,3},{3,2},{4,5},{5,4},{6,7},{7,6},{8,9},{9,8},{10,11... | collective-permute-start | bytes 811016 | tf_op jit(solution)/shard_map/ppermute | solution.py:422
  13.7 5.4 %copy-start.5 = (bf16[2,224,384]{2,1,0:T(8,128)(2,1)S(1)}, bf16[2,224,384]{2,1,0:T(8,128)(2,1)}, u32[]{:S(2)}) copy-start(bf16[2,224,384]{2,1,0:T(8,128)(2,1)} %constant.12.clone.refs_4_) | copy-start | bytes 1032196
  17.8 17.9 %collective-permute-start.6 = (f32[352,256]{1,0:T(8,128)S(1)}, f32[352,256]{1,0:T(8,128)S(1)}, u32[]{:S(2)}, u32[]{:S(2)}) collective-permute-start(f32[352,256]{1,0:T(8,128)S(1)} %get-tuple-element.46), channel_id=1, source_target_pairs={{0,4},{4,0},{8,12},{12,8},{16,20},{20,16},{24,28},{28,24},{1,5},{5... | collective-permute-start | bytes 1081352 | tf_op jit(solution)/shard_map/ppermute | solution.py:493
  20.1 18.1 %collective-permute-start.11 = (f32[368,256]{1,0:T(8,128)S(1)}, f32[368,256]{1,0:T(8,128)S(1)}, u32[]{:S(2)}, u32[]{:S(2)}) collective-permute-start(f32[368,256]{1,0:T(8,128)S(1)} %shard_map.80), channel_id=1, source_target_pairs={{0,2},{1,3},{2,0},{3,1},{4,6},{5,7},{6,4},{7,5},{8,10},{9,11},{10,... | collective-permute-start | bytes 1130504 | tf_op jit(solution)/shard_map/ppermute | solution.py:422
  21.6 16.6 %collective-permute-start.10 = (f32[352,256]{1,0:T(8,128)S(1)}, f32[352,256]{1,0:T(8,128)S(1)}, u32[]{:S(2)}, u32[]{:S(2)}) collective-permute-start(f32[352,256]{1,0:T(8,128)S(1)} %get-tuple-element.51), channel_id=1, source_target_pairs={{4,8},{8,4},{12,16},{16,12},{20,24},{24,20},{5,9},{9,5},{13,17},{1... | collective-permute-start | bytes 1081352 | tf_op jit(solution)/shard_map/ppermute | solution.py:493
  36.8 4.4 %collective-permute-start.13 = (f32[128,256]{1,0:T(8,128)S(1)}, f32[128,256]{1,0:T(8,128)S(1)}, u32[]{:S(2)}, u32[]{:S(2)}) collective-permute-start(f32[128,256]{1,0:T(8,128)S(1)} %get-tuple-element.53), channel_id=1, source_target_pairs={{0,2},{1,3},{2,0},{3,1},{4,6},{5,7},{6,4},{7,5},{8,10},{9,11},{10,... | collective-permute-start | bytes 393224 | tf_op jit(solution)/shard_map/ppermute | solution.py:422
  37.6 8.7 %collective-permute-start.15 = (f32[256,256]{1,0:T(8,128)S(1)}, f32[256,256]{1,0:T(8,128)S(1)}, u32[]{:S(2)}, u32[]{:S(2)}) collective-permute-start(f32[256,256]{1,0:T(8,128)S(1)} %get-tuple-element.56), channel_id=1, source_target_pairs={{0,1},{1,0},{2,3},{3,2},{4,5},{5,4},{6,7},{7,6},{8,9},{9,8},{10,11... | collective-permute-start | bytes 786440 | tf_op jit(solution)/shard_map/ppermute | solution.py:422
  37.7 6.1 %collective-permute-start.16 = (f32[128,256]{1,0:T(8,128)S(1)}, f32[128,256]{1,0:T(8,128)S(1)}, u32[]{:S(2)}, u32[]{:S(2)}) collective-permute-start(f32[128,256]{1,0:T(8,128)S(1)} %get-tuple-element.58), channel_id=1, source_target_pairs={{0,1},{1,0},{2,3},{3,2},{4,5},{5,4},{6,7},{7,6},{8,9},{9,8},{10,11... | collective-permute-start | bytes 393224 | tf_op jit(solution)/shard_map/ppermute | solution.py:422
  39.2 5.6 %collective-permute-start.17 = (f32[128,256]{1,0:T(8,128)S(1)}, f32[128,256]{1,0:T(8,128)S(1)}, u32[]{:S(2)}, u32[]{:S(2)}) collective-permute-start(f32[128,256]{1,0:T(8,128)S(1)} %get-tuple-element.60), channel_id=1, source_target_pairs={{0,2},{1,3},{2,0},{3,1},{4,6},{5,7},{6,4},{7,5},{8,10},{9,11},{10,... | collective-permute-start | bytes 393224 | tf_op jit(solution)/shard_map/ppermute | solution.py:422
  41.6 10.5 %collective-permute-start.14 = (f32[256,256]{1,0:T(8,128)S(1)}, f32[256,256]{1,0:T(8,128)S(1)}, u32[]{:S(2)}, u32[]{:S(2)}) collective-permute-start(f32[256,256]{1,0:T(8,128)S(1)} %get-tuple-element.54), channel_id=1, source_target_pairs={{0,1},{1,0},{2,3},{3,2},{4,5},{5,4},{6,7},{7,6},{8,9},{9,8},{10,11... | collective-permute-start | bytes 786440 | tf_op jit(solution)/shard_map/ppermute | solution.py:422
  43.7 2.6 %collective-permute-start.18 = (f32[128,256]{1,0:T(8,128)S(1)}, f32[128,256]{1,0:T(8,128)S(1)}, u32[]{:S(2)}, u32[]{:S(2)}) collective-permute-start(f32[128,256]{1,0:T(8,128)S(1)} %get-tuple-element.61), channel_id=1, source_target_pairs={{0,1},{1,0},{2,3},{3,2},{4,5},{5,4},{6,7},{7,6},{8,9},{9,8},{10,11... | collective-permute-start | bytes 393224 | tf_op jit(solution)/shard_map/ppermute | solution.py:422
  43.8 6.1 %collective-permute-start.9 = (f32[128,256]{1,0:T(8,128)S(1)}, f32[128,256]{1,0:T(8,128)S(1)}, u32[]{:S(2)}, u32[]{:S(2)}) collective-permute-start(f32[128,256]{1,0:T(8,128)S(1)} %get-tuple-element.50.refs_8_), channel_id=1, source_target_pairs={{0,3},{1,2},{2,1},{3,0},{4,7},{5,6},{6,5},{7,4},{8,11},{9,10},{10,... | collective-permute-start | bytes 393224 | tf_op jit(solution)/shard_map/ppermute | solution.py:422
  44.8 7.3 %collective-permute-start.12 = (f32[128,256]{1,0:T(8,128)S(1)}, f32[128,256]{1,0:T(8,128)S(1)}, u32[]{:S(2)}, u32[]{:S(2)}) collective-permute-start(f32[128,256]{1,0:T(8,128)S(1)} %get-tuple-element.52.refs_3_), channel_id=1, source_target_pairs={{0,3},{1,2},{2,1},{3,0},{4,7},{5,6},{6,5},{7,4},{8,11},{9,10},{10,... | collective-permute-start | bytes 393224 | tf_op jit(solution)/shard_map/ppermute | solution.py:422
  (2 other events, 7.7 us)

commit v14 on v13

--- a/solution.py
+++ b/solution.py
@@ -363,7 +363,7 @@
 
 def join_kernel(rows, cells, near, *refs):
     own_ref, blocks, out_ref = refs[0], refs[1 : 1 + rows * near], refs[-1]
-    size = rows * cells + 8
+    size = own_ref.shape[0]
     out_ref[:size, :] = own_ref[...]
     for d in range(near):
         base = (d + 1) * size
@@ -486,36 +486,39 @@
     spectrum, edge_ones, paired, other, sides = call(
         functools.partial(edge_kernel, edges, count, cells),
         [(2, modes, width), (2, modes, width), (modes, width), (modes, width), (modes, 16)],
-        *edge_blocks, forward, diagonals, solid_mask, earlier=(own,),
+        *edge_blocks, forward, diagonals, solid_mask,
     )
     pairs = [[(i, i ^ 1) for i in range(plane_count)], [(i, ((i + 1) ^ 1) - 1) for i in range(plane_count)]]
-    halos = [
-        lax.ppermute(row, "plane", [(i, j) for i, j in pair if 0 <= j < plane_count])
-        for row, pair in zip((paired, other), pairs)
-    ]
+    pairs = [[(i, j) for i, j in pair if 0 <= j < plane_count] for pair in pairs]
+    halos = [lax.ppermute(paired, "plane", pairs[0])]
+    (other,) = call(
+        functools.partial(join_kernel, 0, 0, 0), [(modes, width)], other, cost=SHORT, earlier=(own,)
+    )
+    halos.append(lax.ppermute(other, "plane", pairs[1]))
 
     *made, ones = call(
         functools.partial(inner_kernel, inner, count, cells),
         [(length, width)] * half + [(2, modes, width)],
-        *inner_blocks, arrived, forward, inverse, diagonals, solid_mask, edge_ones, cost=SHORT,
+        *inner_blocks, arrived, forward, inverse, diagonals, solid_mask, edge_ones, cost=SHORT, earlier=(own,),
     )
     pieces = [(made[0], 0, 0, inner, 0, tiles)]
-    pieces += [(swap(made[d], d), d, 0, inner, 0, tiles) for d in near]
-    before = []
+    made_got = [swap(made[d], d) for d in near]
+    pieces += [(block, d, 0, inner, 0, tiles) for d, block in zip(near, made_got)]
+    rim_got, earlier = [], []
     for order, name in enumerate(("near", "far")):
         outs = call(
             functools.partial(rim_kernel, edges, order, count, cells),
             [(cells, width)] * count,
             spectrum, edge_ones, sides, halos[order], ones, inverse, diagonals, solid_mask,
-            cost=LONG if order else SHORT, earlier=(*before, taken) if order else (),
+            cost=LONG if order else SHORT, earlier=earlier,
         )
-        before = (outs[-1],)
         pieces.append((outs[0], 0, 0, (name,), 0, tiles))
-        pieces += [(swap(outs[d], d), d, 0, (name,), 0, tiles) for d in (*far, *near)]
-        rim_got = pieces[-count + 1 :][0][0] if order == 0 else rim_got
+        rim_got.append([swap(outs[d], d) for d in (*far, *near)])
+        pieces += [(block, d, 0, (name,), 0, tiles) for d, block in zip((*far, *near), rim_got[order])]
+        earlier = [outs[-1], taken]
     rebuilt = call(
         functools.partial(take_kernel, inner, count, cells), [(length, width)] * half, taken, own, take,
-        cost=SHORT, earlier=(*before, rim_got),
+        cost=SHORT, earlier=[outs[-1], *rim_got[0][:half]],
     )
     pieces.append((rebuilt[0], half, 0, inner, 0, tiles))
     pieces += [(swap(rebuilt[d], d), half + d, 0, inner, 0, tiles) for d in near]

time: 53.4 us -> 55.6 us (1.041)
  the two profiles are of different devices: /device:TPU:25 before, /device:TPU:0 now
where the time goes in v14:
time: 55.6 us; the launch traced here: 55.5 us
  waiting for transfers between devices  25.9 us (47%)
  starting transfers between devices  14.8 us (27%)
  Pallas kernels  14.5 us (26%)
    ppermute x17, waiting for transfers between devices, swap(): lax.ppermute(block, 'span', [(i, i ^ d) for i in range(lax.axis_size('spa...  20.9 us
    ppermute x17, starting transfers between devices, swap(): lax.ppermute(block, 'span', [(i, i ^ d) for i in range(lax.axis_size('spa...  12.6 us
    pallas_call x9, Pallas kernels, call(): pl.pallas_call(kernel, out_shape=shapes, in_specs=[VMEM] * len(args) + [A...  8.09 us
    ppermute x1, waiting for transfers between devices, local(): halos = [lax.ppermute(paired, 'plane', pairs[0])]  4.99 us
    pallas_call x2, Pallas kernels, local(): pl.pallas_call(functools.partial(unpack_kernel, [piece[1:] for piece in c...  3.27 us
    pallas_call x2, Pallas kernels, pack(): pl.pallas_call(functools.partial(pack_kernel, jobs, row_count, cells, len...  3.16 us
    ppermute x1, starting transfers between devices, local(): halos = [lax.ppermute(paired, 'plane', pairs[0])]  1.56 us
  transfers between devices with their start and end apart: 19, of which 9 were waited for; matrix products, arithmetic and copies ran while one was open for 0% of the time, Pallas kernels for 21%

profile of v14, /device:TPU:0, one launch (start us, length us, event | category | flops | bytes accessed | tf_op | source)
XLA Modules:
  0.0 55.5 jit_solution(4324305140077066033)
XLA Ops:
  0.0 1.9 %shard_map.73 = (f32[264,256]{1,0:T(8,128)S(1)}, f32[264,256]{1,0:T(8,128)S(1)}, f32[264,256]{1,0:T(8,128)S(1)}) custom-call(f32[128,32,128]{2,1,0:T(8,128)} %bitcast.10), custom_call_target="tpu_custom_call" | custom-call | bytes 200000000 | tf_op jit(solution)/shard_map/pallas_call | solution.py:446
  1.9 3.0 %collective-permute-start.1 = (f32[264,256]{1,0:T(8,128)S(1)}, f32[264,256]{1,0:T(8,128)S(1)}, u32[]{:S(2)}, u32[]{:S(2)}) collective-permute-start(f32[264,256]{1,0:T(8,128)S(1)} %get-tuple-element.34.refs_0_), channel_id=1, source_target_pairs={{0,2},{1,3},{2,0},{3,1},{4,6},{5,7},{6,4},{7,5},{8,10},{9,11},{10,... | collective-permute-start | bytes 811016 | tf_op jit(solution)/shard_map/ppermute | solution.py:422
  5.0 1.3 %shard_map.74 = (f32[264,256]{1,0:T(8,128)S(1)}, f32[264,256]{1,0:T(8,128)S(1)}, f32[264,256]{1,0:T(8,128)S(1)}, f32[264,256]{1,0:T(8,128)S(1)}, f32[264,256]{1,...) custom-call(f32[128,32,128]{2,1,0:T(8,128)S(1)} %bitcast.11, ...), custom_call_target="tpu_custom_call" | custom-call | bytes 200000000 | tf_op jit(solution)/shard_map/pallas_call | solution.py:446
  7.9 4.4 %collective-permute-done.1.refs_2_.refs_3_ = f32[264,256]{1,0:T(8,128)S(1)} collective-permute-done((f32[264,256]{1,0:T(8,128)S(1)}, f32[264,256]{1,0:T(8,128)S(1)}, u32[]{:S(2)}, u32[]{:S(2)}) %collective-permute-start.1) | collective-permute-done | bytes 270368 | tf_op jit(solution)/shard_map/ppermute | solution.py:422
  12.3 2.1 %collective-permute-start.7 = (f32[528,256]{1,0:T(8,128)S(1)}, f32[528,256]{1,0:T(8,128)S(1)}, u32[]{:S(2)}, u32[]{:S(2)}) collective-permute-start(f32[528,256]{1,0:T(8,128)S(1)} %shard_map.76.refs_0_), channel_id=1, source_target_pairs={{0,2},{1,3},{2,0},{3,1},{4,6},{5,7},{6,4},{7,5},{8,10},{9,11},{10,... | collective-permute-start | bytes 1622024 | tf_op jit(solution)/shard_map/ppermute | solution.py:422
  15.0 2.7 %collective-permute-done.2.refs_3_ = f32[264,256]{1,0:T(8,128)S(1)} collective-permute-done((f32[264,256]{1,0:T(8,128)S(1)}, f32[264,256]{1,0:T(8,128)S(1)}, u32[]{:S(2)}, u32[]{:S(2)}) %collective-permute-start.2) | collective-permute-done | bytes 270368 | tf_op jit(solution)/shard_map/ppermute | solution.py:422
  17.7 0.9 %shard_map.75 = (f32[2,352,256]{2,1,0:T(8,128)S(1)}, f32[2,352,256]{2,1,0:T(8,128)S(1)}, f32[352,256]{1,0:T(8,128)S(1)}, f32[352,256]{1,0:T(8,128)S(1)}, f32[352,16]{1,0:T(8,128)S(1)}) custom-call(f32[264,256]{1,0:T(8,128)S(1)} %get-tuple-element.35.refs_0_.refs_2_, f32[264,256]{1,0:T(8,128)S(1)} %collective-permute-done.refs_1_.refs_3_, ...), custom_call_target="tpu_custom_call" | custom-call | bytes 200000000 | tf_op jit(solution)/shard_map/pallas_call | solution.py:411
  18.5 1.6 %collective-permute-start.3 = (f32[352,256]{1,0:T(8,128)S(1)}, f32[352,256]{1,0:T(8,128)S(1)}, u32[]{:S(2)}, u32[]{:S(2)}) collective-permute-start(f32[352,256]{1,0:T(8,128)S(1)} %get-tuple-element.41), channel_id=1, source_target_pairs={{0,4},{4,0},{8,12},{12,8},{16,20},{20,16},{24,28},{28,24},{1,5},{5... | collective-permute-start | bytes 1081352 | tf_op jit(solution)/shard_map/ppermute | solution.py:493
  20.1 0.9 %shard_map.81 = f32[368,256]{1,0:T(8,128)S(1)} custom-call(f32[264,256]{1,0:T(8,128)S(1)} %get-tuple-element.42.refs_0_, f32[264,256]{1,0:T(8,128)S(1)} %collective-permute-done.4.refs_1_, f32[264,256]{1,0:T(8,128)S(1)} %get-tuple-element.35.refs_0_.refs_2_, f32[264,256]{1,0:T(8,128)S(1)} %collective-permute-done.refs_1_.refs_3_, ...), custom_call_target="tpu_custom_call" | custom-call | bytes 1024 | tf_op jit(solution)/shard_map/pallas_call | solution.py:411
  21.6 2.0 %shard_map.77.refs_8_.refs_1_ = f32[512,256]{1,0:T(8,128)S(1)} custom-call(f32[528,256]{1,0:T(8,128)S(1)} %shard_map.76.refs_0_, f32[264,256]{1,0:T(8,128)S(1)} %get-tuple-element.47.refs_1_, f32[264,256]{1,0:T(8,128)S(1)} %collective-permute-done.8.refs_2_, bf16[2,2,176,384]{3,2,1,0:T(8,128)(2,1)S(1)} %copy-done.2, bf16[2,2,128,528]{3,2,1,0:T(8,128)(2,1)S(1)} %copy-done, ...), custom_call_target="tpu_custom_call" | custom-call | bytes 1024 | tf_op jit(solution)/shard_map/pallas_call | solution.py:411
  24.3 5.4 %collective-permute-done.7.refs_2_ = f32[528,256]{1,0:T(8,128)S(1)} collective-permute-done((f32[528,256]{1,0:T(8,128)S(1)}, f32[528,256]{1,0:T(8,128)S(1)}, u32[]{:S(2)}, u32[]{:S(2)}) %collective-permute-start.7) | collective-permute-done | bytes 540704 | tf_op jit(solution)/shard_map/ppermute | solution.py:422
  29.7 1.8 %shard_map.78 = (f32[256,256]{1,0:T(8,128)S(1)}, f32[256,256]{1,0:T(8,128)S(1)}, f32[2,352,256]{2,1,0:T(8,128)S(1)}) custom-call(f32[264,256]{1,0:T(8,128)S(1)} %get-tuple-element.42.refs_0_, f32[264,256]{1,0:T(8,128)S(1)} %collective-permute-done.4.refs_1_, f32[528,256]{1,0:T(8,128)S(1)} %collective-permute-done.7.refs_2_, ...), custom_call_target="tpu_custom_call" | custom-call | bytes 1024 | tf_op jit(solution)/shard_map/pallas_call | solution.py:411
  31.4 5.0 %collective-permute-done.3.refs_3_ = f32[352,256]{1,0:T(8,128)S(1)} collective-permute-done((f32[352,256]{1,0:T(8,128)S(1)}, f32[352,256]{1,0:T(8,128)S(1)}, u32[]{:S(2)}, u32[]{:S(2)}) %collective-permute-start.3) | collective-permute-done | bytes 360480 | tf_op jit(solution)/shard_map/ppermute | solution.py:493
  36.4 1.1 %shard_map.79 = (f32[128,256]{1,0:T(8,128)S(1)}, f32[128,256]{1,0:T(8,128)S(1)}, f32[128,256]{1,0:T(8,128)S(1)}, f32[128,256]{1,0:T(8,128)S(1)}) custom-call(f32[2,352,256]{2,1,0:T(8,128)S(1)} %get-tuple-element.38.refs_0_, f32[2,352,256]{2,1,0:T(8,128)S(1)} %get-tuple-element.39.refs_7_.refs_1_, f32[352,16]{1,0:T(8,128)S(1)} %get-tuple-element.40.refs_2_, ...), custom_call_target="tpu_custom_call" | custom-call | bytes 1024 | tf_op jit(solution)/shard_map/pallas_call | solution.py:411
  37.6 1.1 %collective-permute-start.9 = (f32[128,256]{1,0:T(8,128)S(1)}, f32[128,256]{1,0:T(8,128)S(1)}, u32[]{:S(2)}, u32[]{:S(2)}) collective-permute-start(f32[128,256]{1,0:T(8,128)S(1)} %get-tuple-element.50.refs_8_), channel_id=1, source_target_pairs={{0,3},{1,2},{2,1},{3,0},{4,7},{5,6},{6,5},{7,4},{8,11},{9,10},{10,... | collective-permute-start | bytes 393224 | tf_op jit(solution)/shard_map/ppermute | solution.py:422
  38.7 1.0 %collective-permute-start.15 = (f32[256,256]{1,0:T(8,128)S(1)}, f32[256,256]{1,0:T(8,128)S(1)}, u32[]{:S(2)}, u32[]{:S(2)}) collective-permute-start(f32[256,256]{1,0:T(8,128)S(1)} %get-tuple-element.56), channel_id=1, source_target_pairs={{0,1},{1,0},{2,3},{3,2},{4,5},{5,4},{6,7},{7,6},{8,9},{9,8},{10,11... | collective-permute-start | bytes 786440 | tf_op jit(solution)/shard_map/ppermute | solution.py:422
  39.7 1.1 %shard_map.82 = (f32[128,256]{1,0:T(8,128)S(1)}, f32[128,256]{1,0:T(8,128)S(1)}, f32[128,256]{1,0:T(8,128)S(1)}, f32[128,256]{1,0:T(8,128)S(1)}) custom-call(f32[2,352,256]{2,1,0:T(8,128)S(1)} %get-tuple-element.38.refs_0_, f32[2,352,256]{2,1,0:T(8,128)S(1)} %get-tuple-element.39.refs_7_.refs_1_, f32[352,16]{1,0:T(8,128)S(1)} %get-tuple-element.40.refs_2_, ...), custom_call_target="tpu_custom_call" | custom-call | bytes 200000000 | tf_op jit(solution)/shard_map/pallas_call | solution.py:411
  40.8 3.2 %collective-permute-done.13.refs_4_.refs_3_ = f32[128,256]{1,0:T(8,128)S(1)} collective-permute-done((f32[128,256]{1,0:T(8,128)S(1)}, f32[128,256]{1,0:T(8,128)S(1)}, u32[]{:S(2)}, u32[]{:S(2)}) %collective-permute-start.13) | collective-permute-done | bytes 131104 | tf_op jit(solution)/shard_map/ppermute | solution.py:422
  44.7 1.1 %collective-permute-start.14 = (f32[256,256]{1,0:T(8,128)S(1)}, f32[256,256]{1,0:T(8,128)S(1)}, u32[]{:S(2)}, u32[]{:S(2)}) collective-permute-start(f32[256,256]{1,0:T(8,128)S(1)} %get-tuple-element.54), channel_id=1, source_target_pairs={{0,1},{1,0},{2,3},{3,2},{4,5},{5,4},{6,7},{7,6},{8,9},{9,8},{10,11... | collective-permute-start | bytes 786440 | tf_op jit(solution)/shard_map/ppermute | solution.py:422
  45.8 1.2 %collective-permute-start.17 = (f32[128,256]{1,0:T(8,128)S(1)}, f32[128,256]{1,0:T(8,128)S(1)}, u32[]{:S(2)}, u32[]{:S(2)}) collective-permute-start(f32[128,256]{1,0:T(8,128)S(1)} %get-tuple-element.60), channel_id=1, source_target_pairs={{0,2},{1,3},{2,0},{3,1},{4,6},{5,7},{6,4},{7,5},{8,10},{9,11},{10,... | collective-permute-start | bytes 393224 | tf_op jit(solution)/shard_map/ppermute | solution.py:422
  47.1 0.9 %collective-permute-start.12 = (f32[128,256]{1,0:T(8,128)S(1)}, f32[128,256]{1,0:T(8,128)S(1)}, u32[]{:S(2)}, u32[]{:S(2)}) collective-permute-start(f32[128,256]{1,0:T(8,128)S(1)} %get-tuple-element.52.refs_3_), channel_id=1, source_target_pairs={{0,3},{1,2},{2,1},{3,0},{4,7},{5,6},{6,5},{7,4},{8,11},{9,10},{10,... | collective-permute-start | bytes 393224 | tf_op jit(solution)/shard_map/ppermute | solution.py:422
  48.0 4.2 %collective-permute-done.17.refs_6_ = f32[128,256]{1,0:T(8,128)S(1)} collective-permute-done((f32[128,256]{1,0:T(8,128)S(1)}, f32[128,256]{1,0:T(8,128)S(1)}, u32[]{:S(2)}, u32[]{:S(2)}) %collective-permute-start.17) | collective-permute-done | bytes 131104 | tf_op jit(solution)/shard_map/ppermute | solution.py:422
  52.2 2.3 %shard_map.84.refs_3_ = f32[128,32,128]{2,1,0:T(8,128)} custom-call(f32[256,256]{1,0:T(8,128)S(1)} %get-tuple-element.55.refs_0_, f32[256,256]{1,0:T(8,128)S(1)} %collective-permute-done.15.refs_1_, f32[128,256]{1,0:T(8,128)S(1)} %get-tuple-element.57.refs_2_, f32[128,256]{1,0:T(8,128)S(1)} %collective-permute-done.13.refs_4_.refs_3_, ...), custom_call_target="tpu_custom_call" | custom-call | bytes 200000000 | tf_op jit(solution)/shard_map/pallas_call | solution.py:531
  54.6 0.9 %shard_map.85 = f32[128,32,128]{2,1,0:T(8,128)} custom-call(f32[128,256]{1,0:T(8,128)S(1)} %collective-permute-done.9.refs_5_.refs_0_, f32[128,256]{1,0:T(8,128)S(1)} %collective-permute-done.12.refs_1_, f32[256,256]{1,0:T(8,128)S(1)} %collective-permute-done.14.refs_2_, f32[128,32,128]{2,1,0:T(8,128)} %shard_map.84.refs_3_), custom_call_target="tpu_custom_call", output_to_operand_aliasing={{}: (3, {})} | custom-call | bytes 1024 | tf_op jit(solution)/shard_map/pallas_call | solution.py:531
  (41 shorter events, 4.4 us)
Async XLA Ops:
  1.9 15.8 %copy-start.2 = (bf16[2,2,176,384]{3,2,1,0:T(8,128)(2,1)S(1)}, bf16[2,2,176,384]{3,2,1,0:T(8,128)(2,1)}, u32[]{:S(2)}) copy-start(bf16[2,2,176,384]{3,2,1,0:T(8,128)(2,1)} %constant.10.clone.refs_4_.refs_3_) | copy-start | bytes 1622020
  1.9 15.7 %copy-start.3 = (s32[4,1024]{1,0:T(4,128)S(1)}, s32[4,1024]{1,0:T(4,128)}, u32[]{:S(2)}) copy-start(s32[4,1024]{1,0:T(4,128)} %refs_7_.3) | copy-start | bytes 49156
  1.9 15.7 %copy-start.4 = (f32[8,384]{1,0:T(8,128)S(1)}, f32[8,384]{1,0:T(8,128)}, u32[]{:S(2)}) copy-start(f32[8,384]{1,0:T(8,128)} %constant.14.clone.refs_5_.refs_6_) | copy-start | bytes 36868
  1.9 10.3 %collective-permute-start.1 = (f32[264,256]{1,0:T(8,128)S(1)}, f32[264,256]{1,0:T(8,128)S(1)}, u32[]{:S(2)}, u32[]{:S(2)}) collective-permute-start(f32[264,256]{1,0:T(8,128)S(1)} %get-tuple-element.34.refs_0_), channel_id=1, source_target_pairs={{0,2},{1,3},{2,0},{3,1},{4,6},{5,7},{6,4},{7,5},{8,10},{9,11},{10,... | collective-permute-start | bytes 811016 | tf_op jit(solution)/shard_map/ppermute | solution.py:422
  6.3 13.8 %copy-start.5 = (bf16[2,224,384]{2,1,0:T(8,128)(2,1)S(1)}, bf16[2,224,384]{2,1,0:T(8,128)(2,1)}, u32[]{:S(2)}) copy-start(bf16[2,224,384]{2,1,0:T(8,128)(2,1)} %constant.12.clone.refs_4_) | copy-start | bytes 1032196
  6.3 1.4 %collective-permute-start.5 = (f32[136,256]{1,0:T(8,128)S(1)}, f32[136,256]{1,0:T(8,128)S(1)}, u32[]{:S(2)}, u32[]{:S(2)}) collective-permute-start(f32[136,256]{1,0:T(8,128)S(1)} %get-tuple-element.45), channel_id=1, source_target_pairs={{0,1},{1,0},{2,3},{3,2},{4,5},{5,4},{6,7},{7,6},{8,9},{9,8},{10,11... | collective-permute-start | bytes 417800 | tf_op jit(solution)/shard_map/ppermute | solution.py:422
  6.3 1.5 %collective-permute-start.6 = (f32[136,256]{1,0:T(8,128)S(1)}, f32[136,256]{1,0:T(8,128)S(1)}, u32[]{:S(2)}, u32[]{:S(2)}) collective-permute-start(f32[136,256]{1,0:T(8,128)S(1)} %get-tuple-element.46), channel_id=1, source_target_pairs={{0,1},{1,0},{2,3},{3,2},{4,5},{5,4},{6,7},{7,6},{8,9},{9,8},{10,11... | collective-permute-start | bytes 417800 | tf_op jit(solution)/shard_map/ppermute | solution.py:422
  6.8 8.1 %collective-permute-start = (f32[264,256]{1,0:T(8,128)S(1)}, f32[264,256]{1,0:T(8,128)S(1)}, u32[]{:S(2)}, u32[]{:S(2)}) collective-permute-start(f32[264,256]{1,0:T(8,128)S(1)} %get-tuple-element.36), channel_id=1, source_target_pairs={{0,1},{1,0},{2,3},{3,2},{4,5},{5,4},{6,7},{7,6},{8,9},{9,8},{10,11... | collective-permute-start | bytes 811016 | tf_op jit(solution)/shard_map/ppermute | solution.py:422
  6.9 10.7 %collective-permute-start.2 = (f32[264,256]{1,0:T(8,128)S(1)}, f32[264,256]{1,0:T(8,128)S(1)}, u32[]{:S(2)}, u32[]{:S(2)}) collective-permute-start(f32[264,256]{1,0:T(8,128)S(1)} %get-tuple-element.37), channel_id=1, source_target_pairs={{0,3},{1,2},{2,1},{3,0},{4,7},{5,6},{6,5},{7,4},{8,11},{9,10},{10,... | collective-permute-start | bytes 811016 | tf_op jit(solution)/shard_map/ppermute | solution.py:422
  12.3 9.3 %copy-start = (bf16[2,2,128,528]{3,2,1,0:T(8,128)(2,1)S(1)}, bf16[2,2,128,528]{3,2,1,0:T(8,128)(2,1)}, u32[]{:S(2)}) copy-start(bf16[2,2,128,528]{3,2,1,0:T(8,128)(2,1)} %constant.11.clone.refs_4_.refs_5_) | copy-start | bytes 1622020
  12.3 17.3 %collective-permute-start.7 = (f32[528,256]{1,0:T(8,128)S(1)}, f32[528,256]{1,0:T(8,128)S(1)}, u32[]{:S(2)}, u32[]{:S(2)}) collective-permute-start(f32[528,256]{1,0:T(8,128)S(1)} %shard_map.76.refs_0_), channel_id=1, source_target_pairs={{0,2},{1,3},{2,0},{3,1},{4,6},{5,7},{6,4},{7,5},{8,10},{9,11},{10,... | collective-permute-start | bytes 1622024 | tf_op jit(solution)/shard_map/ppermute | solution.py:422
  14.5 5.6 %collective-permute-start.4 = (f32[264,256]{1,0:T(8,128)S(1)}, f32[264,256]{1,0:T(8,128)S(1)}, u32[]{:S(2)}, u32[]{:S(2)}) collective-permute-start(f32[264,256]{1,0:T(8,128)S(1)} %get-tuple-element.43), channel_id=1, source_target_pairs={{0,1},{1,0},{2,3},{3,2},{4,5},{5,4},{6,7},{7,6},{8,9},{9,8},{10,11... | collective-permute-start | bytes 811016 | tf_op jit(solution)/shard_map/ppermute | solution.py:422
  14.5 7.2 %collective-permute-start.8 = (f32[264,256]{1,0:T(8,128)S(1)}, f32[264,256]{1,0:T(8,128)S(1)}, u32[]{:S(2)}, u32[]{:S(2)}) collective-permute-start(f32[264,256]{1,0:T(8,128)S(1)} %get-tuple-element.48), channel_id=1, source_target_pairs={{0,1},{1,0},{2,3},{3,2},{4,5},{5,4},{6,7},{7,6},{8,9},{9,8},{10,11... | collective-permute-start | bytes 811016 | tf_op jit(solution)/shard_map/ppermute | solution.py:422
  18.5 17.9 %collective-permute-start.3 = (f32[352,256]{1,0:T(8,128)S(1)}, f32[352,256]{1,0:T(8,128)S(1)}, u32[]{:S(2)}, u32[]{:S(2)}) collective-permute-start(f32[352,256]{1,0:T(8,128)S(1)} %get-tuple-element.41), channel_id=1, source_target_pairs={{0,4},{4,0},{8,12},{12,8},{16,20},{20,16},{24,28},{28,24},{1,5},{5... | collective-permute-start | bytes 1081352 | tf_op jit(solution)/shard_map/ppermute | solution.py:493
  21.0 18.7 %collective-permute-start.11 = (f32[368,256]{1,0:T(8,128)S(1)}, f32[368,256]{1,0:T(8,128)S(1)}, u32[]{:S(2)}, u32[]{:S(2)}) collective-permute-start(f32[368,256]{1,0:T(8,128)S(1)} %shard_map.81), channel_id=1, source_target_pairs={{0,2},{1,3},{2,0},{3,1},{4,6},{5,7},{6,4},{7,5},{8,10},{9,11},{10,... | collective-permute-start | bytes 1130504 | tf_op jit(solution)/shard_map/ppermute | solution.py:422
  23.6 16.1 %collective-permute-start.10 = (f32[352,256]{1,0:T(8,128)S(1)}, f32[352,256]{1,0:T(8,128)S(1)}, u32[]{:S(2)}, u32[]{:S(2)}) collective-permute-start(f32[352,256]{1,0:T(8,128)S(1)} %shard_map.80), channel_id=1, source_target_pairs={{4,8},{8,4},{12,16},{16,12},{20,24},{24,20},{5,9},{9,5},{13,17},{1... | collective-permute-start | bytes 1081352 | tf_op jit(solution)/shard_map/ppermute | solution.py:497
  37.5 6.5 %collective-permute-start.13 = (f32[128,256]{1,0:T(8,128)S(1)}, f32[128,256]{1,0:T(8,128)S(1)}, u32[]{:S(2)}, u32[]{:S(2)}) collective-permute-start(f32[128,256]{1,0:T(8,128)S(1)} %get-tuple-element.53), channel_id=1, source_target_pairs={{0,2},{1,3},{2,0},{3,1},{4,6},{5,7},{6,4},{7,5},{8,10},{9,11},{10,... | collective-permute-start | bytes 393224 | tf_op jit(solution)/shard_map/ppermute | solution.py:422
  37.6 6.8 %collective-permute-start.9 = (f32[128,256]{1,0:T(8,128)S(1)}, f32[128,256]{1,0:T(8,128)S(1)}, u32[]{:S(2)}, u32[]{:S(2)}) collective-permute-start(f32[128,256]{1,0:T(8,128)S(1)} %get-tuple-element.50.refs_8_), channel_id=1, source_target_pairs={{0,3},{1,2},{2,1},{3,0},{4,7},{5,6},{6,5},{7,4},{8,11},{9,10},{10,... | collective-permute-start | bytes 393224 | tf_op jit(solution)/shard_map/ppermute | solution.py:422
  38.7 13.5 %collective-permute-start.15 = (f32[256,256]{1,0:T(8,128)S(1)}, f32[256,256]{1,0:T(8,128)S(1)}, u32[]{:S(2)}, u32[]{:S(2)}) collective-permute-start(f32[256,256]{1,0:T(8,128)S(1)} %get-tuple-element.56), channel_id=1, source_target_pairs={{0,1},{1,0},{2,3},{3,2},{4,5},{5,4},{6,7},{7,6},{8,9},{9,8},{10,11... | collective-permute-start | bytes 786440 | tf_op jit(solution)/shard_map/ppermute | solution.py:422
  39.7 7.4 %collective-permute-start.16 = (f32[128,256]{1,0:T(8,128)S(1)}, f32[128,256]{1,0:T(8,128)S(1)}, u32[]{:S(2)}, u32[]{:S(2)}) collective-permute-start(f32[128,256]{1,0:T(8,128)S(1)} %get-tuple-element.58), channel_id=1, source_target_pairs={{0,1},{1,0},{2,3},{3,2},{4,5},{5,4},{6,7},{7,6},{8,9},{9,8},{10,11... | collective-permute-start | bytes 393224 | tf_op jit(solution)/shard_map/ppermute | solution.py:422
  44.7 9.8 %collective-permute-start.14 = (f32[256,256]{1,0:T(8,128)S(1)}, f32[256,256]{1,0:T(8,128)S(1)}, u32[]{:S(2)}, u32[]{:S(2)}) collective-permute-start(f32[256,256]{1,0:T(8,128)S(1)} %get-tuple-element.54), channel_id=1, source_target_pairs={{0,1},{1,0},{2,3},{3,2},{4,5},{5,4},{6,7},{7,6},{8,9},{9,8},{10,11... | collective-permute-start | bytes 786440 | tf_op jit(solution)/shard_map/ppermute | solution.py:422
  45.8 6.4 %collective-permute-start.17 = (f32[128,256]{1,0:T(8,128)S(1)}, f32[128,256]{1,0:T(8,128)S(1)}, u32[]{:S(2)}, u32[]{:S(2)}) collective-permute-start(f32[128,256]{1,0:T(8,128)S(1)} %get-tuple-element.60), channel_id=1, source_target_pairs={{0,2},{1,3},{2,0},{3,1},{4,6},{5,7},{6,4},{7,5},{8,10},{9,11},{10,... | collective-permute-start | bytes 393224 | tf_op jit(solution)/shard_map/ppermute | solution.py:422
  47.0 5.2 %collective-permute-start.18 = (f32[128,256]{1,0:T(8,128)S(1)}, f32[128,256]{1,0:T(8,128)S(1)}, u32[]{:S(2)}, u32[]{:S(2)}) collective-permute-start(f32[128,256]{1,0:T(8,128)S(1)} %get-tuple-element.61), channel_id=1, source_target_pairs={{0,1},{1,0},{2,3},{3,2},{4,5},{5,4},{6,7},{7,6},{8,9},{9,8},{10,11... | collective-permute-start | bytes 393224 | tf_op jit(solution)/shard_map/ppermute | solution.py:422
  47.1 7.4 %collective-permute-start.12 = (f32[128,256]{1,0:T(8,128)S(1)}, f32[128,256]{1,0:T(8,128)S(1)}, u32[]{:S(2)}, u32[]{:S(2)}) collective-permute-start(f32[128,256]{1,0:T(8,128)S(1)} %get-tuple-element.52.refs_3_), channel_id=1, source_target_pairs={{0,3},{1,2},{2,1},{3,0},{4,7},{5,6},{6,5},{7,4},{8,11},{9,10},{10,... | collective-permute-start | bytes 393224 | tf_op jit(solution)/shard_map/ppermute | solution.py:422
  (2 other events, 11.8 us)

commit v15 on v14

--- a/solution.py
+++ b/solution.py
@@ -333,7 +333,7 @@
 def take_kernel(rows, count, cells, *refs):
     half = count // 2
     message_ref, local_ref, take_ref = refs[:3]
-    outs = refs[-half:]
+    outs = refs[-1 - (half - 1) * len(rows) :]
     lines = message_ref.shape[0] // len(rows)
     short = take_ref.shape[2] // 3 - lines
     for i in range(len(rows)):
@@ -341,11 +341,15 @@
         if short:
             values = jnp.concatenate([values, jnp.zeros((short, values.shape[1]), jnp.float32)], axis=0)
         values = thirds(values, 0)
-        for d, out in enumerate(outs):
+        for d in range(half):
             base = (d * len(rows) + i) * cells
-            out[i * cells : (i + 1) * cells, :] = local_ref[base : base + cells, :] + jnp.dot(
+            value = local_ref[base : base + cells, :] + jnp.dot(
                 take_ref[place(d)], values, preferred_element_type=jnp.float32
             )
+            if d == 0:
+                outs[0][i * cells : (i + 1) * cells, :] = value
+            else:
+                outs[1 + (d - 1) * len(rows) + i][...] = value
 
 
 def rim_kernel(rows, order, count, cells, *refs):
@@ -359,6 +363,11 @@
     diagonal = pick(jnp.where(edge == 0, mask[rows[0]], mask[rows[1]]), fluid, solid)
     sweep = second_sweep(spectrum_ref[edge], edges_ref[edge], halo_ref[...], ones_ref[edge], sides, 0, diagonal)
     inverse_rows([sweep], cells, inverse_ref, outs[: count // 2], outs[count // 2 :])
+    if order == 1:
+        for d in range(1, count // 2):
+            outs[d][cells:, :] = refs[8 + d - 1][...]
+    for out in outs[count // 2 :]:
+        out[cells:, :] = jnp.zeros((out.shape[0] - cells, width), jnp.float32)
 
 
 def join_kernel(rows, cells, near, *refs):
@@ -491,37 +500,43 @@
     pairs = [[(i, i ^ 1) for i in range(plane_count)], [(i, ((i + 1) ^ 1) - 1) for i in range(plane_count)]]
     pairs = [[(i, j) for i, j in pair if 0 <= j < plane_count] for pair in pairs]
     halos = [lax.ppermute(paired, "plane", pairs[0])]
-    (other,) = call(
-        functools.partial(join_kernel, 0, 0, 0), [(modes, width)], other, cost=SHORT, earlier=(own,)
-    )
-    halos.append(lax.ppermute(other, "plane", pairs[1]))
-
     *made, ones = call(
         functools.partial(inner_kernel, inner, count, cells),
         [(length, width)] * half + [(2, modes, width)],
         *inner_blocks, arrived, forward, inverse, diagonals, solid_mask, edge_ones, cost=SHORT, earlier=(own,),
     )
+    (other,) = call(
+        functools.partial(join_kernel, 0, 0, 0), [(modes, width)], other, cost=SHORT, earlier=(halos[0], ones)
+    )
+    halos.append(lax.ppermute(other, "plane", pairs[1]))
+
     pieces = [(made[0], 0, 0, inner, 0, tiles)]
     made_got = [swap(made[d], d) for d in near]
     pieces += [(block, d, 0, inner, 0, tiles) for d, block in zip(near, made_got)]
-    rim_got, earlier = [], []
+    rim_got, near_rim, earlier = [], [], []
     for order, name in enumerate(("near", "far")):
         outs = call(
             functools.partial(rim_kernel, edges, order, count, cells),
-            [(cells, width)] * count,
-            spectrum, edge_ones, sides, halos[order], ones, inverse, diagonals, solid_mask,
+            [(cells, width)] + [((order + 1) * cells, width)] * (half - 1) + [(cells + 8, width)] * half,
+            spectrum, edge_ones, sides, halos[order], ones, inverse, diagonals, solid_mask, *near_rim,
             cost=LONG if order else SHORT, earlier=earlier,
         )
+        near_rim = outs[1:half]
         pieces.append((outs[0], 0, 0, (name,), 0, tiles))
-        rim_got.append([swap(outs[d], d) for d in (*far, *near)])
-        pieces += [(block, d, 0, (name,), 0, tiles) for d, block in zip((*far, *near), rim_got[order])]
+        rim_got.append([swap(outs[d], d) for d in far])
+        pieces += [(block, d, 0, (name,), 0, tiles) for d, block in zip(far, rim_got[order])]
         earlier = [outs[-1], taken]
+    pieces += [(swap(near_rim[d - 1], d), d, 0, ("far", "near"), 0, tiles) for d in near]
     rebuilt = call(
-        functools.partial(take_kernel, inner, count, cells), [(length, width)] * half, taken, own, take,
-        cost=SHORT, earlier=[outs[-1], *rim_got[0][:half]],
+        functools.partial(take_kernel, inner, count, cells),
+        [(length, width)] + [(cells, width)] * ((half - 1) * len(inner)),
+        taken, own, take,
+        cost=SHORT, earlier=[outs[-1], *rim_got[0], *made_got],
     )
     pieces.append((rebuilt[0], half, 0, inner, 0, tiles))
-    pieces += [(swap(rebuilt[d], d), half + d, 0, inner, 0, tiles) for d in near]
+    for d in near:
+        for i, row in enumerate(inner):
+            pieces.append((swap(rebuilt[1 + (d - 1) * len(inner) + i], d), half + d, 0, (row,), 0, tiles))
 
     result = None
     own_lines = tiles * row_count

time: 55.6 us -> 52.8 us (0.950)
  the two profiles are of different devices: /device:TPU:0 before, /device:TPU:25 now
where the time goes in v15:
time: 52.8 us; the launch traced here: 52.6 us
  starting transfers between devices  21.1 us (40%)
  waiting for transfers between devices  16.8 us (32%)
  Pallas kernels  14.5 us (27%)
    ppermute x17, starting transfers between devices, swap(): lax.ppermute(block, 'span', [(i, i ^ d) for i in range(lax.axis_size('spa...  16.9 us
    ppermute x17, waiting for transfers between devices, swap(): lax.ppermute(block, 'span', [(i, i ^ d) for i in range(lax.axis_size('spa...  15.6 us
    pallas_call x9, Pallas kernels, call(): pl.pallas_call(kernel, out_shape=shapes, in_specs=[VMEM] * len(args) + [A...  8.05 us
    pallas_call x2, Pallas kernels, local(): pl.pallas_call(functools.partial(unpack_kernel, [piece[1:] for piece in c...  3.26 us
    pallas_call x2, Pallas kernels, pack(): pl.pallas_call(functools.partial(pack_kernel, jobs, row_count, cells, len...  3.16 us
    ppermute x1, starting transfers between devices, local(): halos.append(lax.ppermute(other, 'plane', pairs[1]))  3 us
    ppermute x1, starting transfers between devices, local(): halos = [lax.ppermute(paired, 'plane', pairs[0])]  1.28 us
    ppermute x1, waiting for transfers between devices, local(): halos.append(lax.ppermute(other, 'plane', pairs[1]))  1.16 us
  transfers between devices with their start and end apart: 19, of which 9 were waited for; matrix products, arithmetic and copies ran while one was open for 0% of the time, Pallas kernels for 22%

profile of v15, /device:TPU:25, one launch (start us, length us, event | category | flops | bytes accessed | tf_op | source)
XLA Modules:
  0.0 52.6 jit_solution(17960712716771628882)
XLA Ops:
  0.0 1.9 %shard_map.73 = (f32[264,256]{1,0:T(8,128)S(1)}, f32[264,256]{1,0:T(8,128)S(1)}, f32[264,256]{1,0:T(8,128)S(1)}) custom-call(f32[128,32,128]{2,1,0:T(8,128)} %bitcast.10), custom_call_target="tpu_custom_call" | custom-call | bytes 200000000 | tf_op jit(solution)/shard_map/pallas_call | solution.py:455
  1.9 1.3 %collective-permute-start.1 = (f32[264,256]{1,0:T(8,128)S(1)}, f32[264,256]{1,0:T(8,128)S(1)}, u32[]{:S(2)}, u32[]{:S(2)}) collective-permute-start(f32[264,256]{1,0:T(8,128)S(1)} %get-tuple-element.35.refs_0_), channel_id=1, source_target_pairs={{0,2},{1,3},{2,0},{3,1},{4,6},{5,7},{6,4},{7,5},{8,10},{9,11},{10,... | collective-permute-start | bytes 811016 | tf_op jit(solution)/shard_map/ppermute | solution.py:431
  3.2 1.3 %shard_map.74 = (f32[264,256]{1,0:T(8,128)S(1)}, f32[264,256]{1,0:T(8,128)S(1)}, f32[264,256]{1,0:T(8,128)S(1)}, f32[264,256]{1,0:T(8,128)S(1)}, f32[264,256]{1,...) custom-call(f32[128,32,128]{2,1,0:T(8,128)S(1)} %bitcast.11, ...), custom_call_target="tpu_custom_call" | custom-call | bytes 200000000 | tf_op jit(solution)/shard_map/pallas_call | solution.py:455
  4.5 1.0 %collective-permute-start.5 = (f32[136,256]{1,0:T(8,128)S(1)}, f32[136,256]{1,0:T(8,128)S(1)}, u32[]{:S(2)}, u32[]{:S(2)}) collective-permute-start(f32[136,256]{1,0:T(8,128)S(1)} %get-tuple-element.46), channel_id=1, source_target_pairs={{0,1},{1,0},{2,3},{3,2},{4,5},{5,4},{6,7},{7,6},{8,9},{9,8},{10,11... | collective-permute-start | bytes 417800 | tf_op jit(solution)/shard_map/ppermute | solution.py:431
  6.9 2.4 %collective-permute-done.1.refs_2_.refs_3_ = f32[264,256]{1,0:T(8,128)S(1)} collective-permute-done((f32[264,256]{1,0:T(8,128)S(1)}, f32[264,256]{1,0:T(8,128)S(1)}, u32[]{:S(2)}, u32[]{:S(2)}) %collective-permute-start.1) | collective-permute-done | bytes 270368 | tf_op jit(solution)/shard_map/ppermute | solution.py:431
  9.4 1.3 %collective-permute-start.7 = (f32[528,256]{1,0:T(8,128)S(1)}, f32[528,256]{1,0:T(8,128)S(1)}, u32[]{:S(2)}, u32[]{:S(2)}) collective-permute-start(f32[528,256]{1,0:T(8,128)S(1)} %shard_map.76.refs_0_), channel_id=1, source_target_pairs={{0,2},{1,3},{2,0},{3,1},{4,6},{5,7},{6,4},{7,5},{8,10},{9,11},{10,... | collective-permute-start | bytes 1622024 | tf_op jit(solution)/shard_map/ppermute | solution.py:431
  10.7 6.4 %collective-permute-done.2.refs_3_ = f32[264,256]{1,0:T(8,128)S(1)} collective-permute-done((f32[264,256]{1,0:T(8,128)S(1)}, f32[264,256]{1,0:T(8,128)S(1)}, u32[]{:S(2)}, u32[]{:S(2)}) %collective-permute-start.2) | collective-permute-done | bytes 270368 | tf_op jit(solution)/shard_map/ppermute | solution.py:431
  18.0 1.3 %collective-permute-start.3 = (f32[352,256]{1,0:T(8,128)S(1)}, f32[352,256]{1,0:T(8,128)S(1)}, u32[]{:S(2)}, u32[]{:S(2)}) collective-permute-start(f32[352,256]{1,0:T(8,128)S(1)} %get-tuple-element.42), channel_id=1, source_target_pairs={{0,4},{4,0},{8,12},{12,8},{16,20},{20,16},{24,28},{28,24},{1,5},{5... | collective-permute-start | bytes 1081352 | tf_op jit(solution)/shard_map/ppermute | solution.py:502
  19.8 1.0 %collective-permute-done.4.refs_1_ = f32[264,256]{1,0:T(8,128)S(1)} collective-permute-done((f32[264,256]{1,0:T(8,128)S(1)}, f32[264,256]{1,0:T(8,128)S(1)}, u32[]{:S(2)}, u32[]{:S(2)}) %collective-permute-start.4) | collective-permute-done | bytes 270368 | tf_op jit(solution)/shard_map/ppermute | solution.py:431
  20.9 0.9 %shard_map.81 = f32[368,256]{1,0:T(8,128)S(1)} custom-call(f32[264,256]{1,0:T(8,128)S(1)} %get-tuple-element.43.refs_0_, f32[264,256]{1,0:T(8,128)S(1)} %collective-permute-done.4.refs_1_, f32[264,256]{1,0:T(8,128)S(1)} %get-tuple-element.36.refs_0_.refs_2_, f32[264,256]{1,0:T(8,128)S(1)} %collective-permute-done.refs_1_.refs_3_, ...), custom_call_target="tpu_custom_call" | custom-call | bytes 1024 | tf_op jit(solution)/shard_map/pallas_call | solution.py:420
  21.8 1.3 %collective-permute-start.11 = (f32[368,256]{1,0:T(8,128)S(1)}, f32[368,256]{1,0:T(8,128)S(1)}, u32[]{:S(2)}, u32[]{:S(2)}) collective-permute-start(f32[368,256]{1,0:T(8,128)S(1)} %shard_map.81), channel_id=1, source_target_pairs={{0,2},{1,3},{2,0},{3,1},{4,6},{5,7},{6,4},{7,5},{8,10},{9,11},{10,... | collective-permute-start | bytes 1130504 | tf_op jit(solution)/shard_map/ppermute | solution.py:431
  23.1 1.9 %shard_map.77.refs_8_.refs_1_ = f32[512,256]{1,0:T(8,128)S(1)} custom-call(f32[528,256]{1,0:T(8,128)S(1)} %shard_map.76.refs_0_, f32[264,256]{1,0:T(8,128)S(1)} %get-tuple-element.48.refs_1_, f32[264,256]{1,0:T(8,128)S(1)} %collective-permute-done.8.refs_2_, bf16[2,2,176,384]{3,2,1,0:T(8,128)(2,1)S(1)} %copy-done.2, bf16[2,2,128,528]{3,2,1,0:T(8,128)(2,1)S(1)} %copy-done, ...), custom_call_target="tpu_custom_call" | custom-call | bytes 1024 | tf_op jit(solution)/shard_map/pallas_call | solution.py:420
  25.1 1.7 %collective-permute-done.7.refs_2_ = f32[528,256]{1,0:T(8,128)S(1)} collective-permute-done((f32[528,256]{1,0:T(8,128)S(1)}, f32[528,256]{1,0:T(8,128)S(1)}, u32[]{:S(2)}, u32[]{:S(2)}) %collective-permute-start.7) | collective-permute-done | bytes 540704 | tf_op jit(solution)/shard_map/ppermute | solution.py:431
  26.7 1.8 %shard_map.78 = (f32[256,256]{1,0:T(8,128)S(1)}, f32[256,256]{1,0:T(8,128)S(1)}, f32[2,352,256]{2,1,0:T(8,128)S(1)}) custom-call(f32[264,256]{1,0:T(8,128)S(1)} %get-tuple-element.43.refs_0_, f32[264,256]{1,0:T(8,128)S(1)} %collective-permute-done.4.refs_1_, f32[528,256]{1,0:T(8,128)S(1)} %collective-permute-done.7.refs_2_, ...), custom_call_target="tpu_custom_call" | custom-call | bytes 1024 | tf_op jit(solution)/shard_map/pallas_call | solution.py:420
  28.6 3.0 %collective-permute-start.10 = (f32[352,256]{1,0:T(8,128)S(1)}, f32[352,256]{1,0:T(8,128)S(1)}, u32[]{:S(2)}, u32[]{:S(2)}) collective-permute-start(f32[352,256]{1,0:T(8,128)S(1)} %shard_map.80), channel_id=1, source_target_pairs={{4,8},{8,4},{12,16},{16,12},{20,24},{24,20},{5,9},{9,5},{13,17},{1... | collective-permute-start | bytes 1081352 | tf_op jit(solution)/shard_map/ppermute | solution.py:511
  31.6 3.0 %collective-permute-start.14 = (f32[256,256]{1,0:T(8,128)S(1)}, f32[256,256]{1,0:T(8,128)S(1)}, u32[]{:S(2)}, u32[]{:S(2)}) collective-permute-start(f32[256,256]{1,0:T(8,128)S(1)} %get-tuple-element.56), channel_id=1, source_target_pairs={{0,1},{1,0},{2,3},{3,2},{4,5},{5,4},{6,7},{7,6},{8,9},{9,8},{10,11... | collective-permute-start | bytes 786440 | tf_op jit(solution)/shard_map/ppermute | solution.py:431
  34.6 1.1 %shard_map.79 = (f32[128,256]{1,0:T(8,128)S(1)}, f32[128,256]{1,0:T(8,128)S(1)}, f32[136,256]{1,0:T(8,128)S(1)}, f32[136,256]{1,0:T(8,128)S(1)}) custom-call(f32[2,352,256]{2,1,0:T(8,128)S(1)} %get-tuple-element.39.refs_0_, f32[2,352,256]{2,1,0:T(8,128)S(1)} %get-tuple-element.40.refs_7_.refs_1_, f32[352,16]{1,0:T(8,128)S(1)} %get-tuple-element.41.refs_2_, ...), custom_call_target="tpu_custom_call" | custom-call | bytes 1024 | tf_op jit(solution)/shard_map/pallas_call | solution.py:420
  35.7 1.3 %collective-permute-start.13 = (f32[136,256]{1,0:T(8,128)S(1)}, f32[136,256]{1,0:T(8,128)S(1)}, u32[]{:S(2)}, u32[]{:S(2)}) collective-permute-start(f32[136,256]{1,0:T(8,128)S(1)} %get-tuple-element.55), channel_id=1, source_target_pairs={{0,2},{1,3},{2,0},{3,1},{4,6},{5,7},{6,4},{7,5},{8,10},{9,11},{10,... | collective-permute-start | bytes 417800 | tf_op jit(solution)/shard_map/ppermute | solution.py:431
  37.4 1.2 %collective-permute-done.10.refs_3_ = f32[352,256]{1,0:T(8,128)S(1)} collective-permute-done((f32[352,256]{1,0:T(8,128)S(1)}, f32[352,256]{1,0:T(8,128)S(1)}, u32[]{:S(2)}, u32[]{:S(2)}) %collective-permute-start.10) | collective-permute-done | bytes 360480 | tf_op jit(solution)/shard_map/ppermute | solution.py:511
  38.6 1.1 %shard_map.82 = (f32[128,256]{1,0:T(8,128)S(1)}, f32[256,256]{1,0:T(8,128)S(1)}, f32[136,256]{1,0:T(8,128)S(1)}, f32[136,256]{1,0:T(8,128)S(1)}) custom-call(f32[2,352,256]{2,1,0:T(8,128)S(1)} %get-tuple-element.39.refs_0_, f32[2,352,256]{2,1,0:T(8,128)S(1)} %get-tuple-element.40.refs_7_.refs_1_, f32[352,16]{1,0:T(8,128)S(1)} %get-tuple-element.41.refs_2_, ...), custom_call_target="tpu_custom_call" | custom-call | bytes 200000000 | tf_op jit(solution)/shard_map/pallas_call | solution.py:420
  39.6 3.7 %collective-permute-start.18 = (f32[256,256]{1,0:T(8,128)S(1)}, f32[256,256]{1,0:T(8,128)S(1)}, u32[]{:S(2)}, u32[]{:S(2)}) collective-permute-start(f32[256,256]{1,0:T(8,128)S(1)} %get-tuple-element.63), channel_id=1, source_target_pairs={{0,1},{1,0},{2,3},{3,2},{4,5},{5,4},{6,7},{7,6},{8,9},{9,8},{10,11... | collective-permute-start | bytes 786440 | tf_op jit(solution)/shard_map/ppermute | solution.py:431
  43.3 1.2 %collective-permute-start.17 = (f32[136,256]{1,0:T(8,128)S(1)}, f32[136,256]{1,0:T(8,128)S(1)}, u32[]{:S(2)}, u32[]{:S(2)}) collective-permute-start(f32[136,256]{1,0:T(8,128)S(1)} %get-tuple-element.62), channel_id=1, source_target_pairs={{0,2},{1,3},{2,0},{3,1},{4,6},{5,7},{6,4},{7,5},{8,10},{9,11},{10,... | collective-permute-start | bytes 417800 | tf_op jit(solution)/shard_map/ppermute | solution.py:431
  46.0 2.6 %collective-permute-done.17.refs_5_ = f32[136,256]{1,0:T(8,128)S(1)} collective-permute-done((f32[136,256]{1,0:T(8,128)S(1)}, f32[136,256]{1,0:T(8,128)S(1)}, u32[]{:S(2)}, u32[]{:S(2)}) %collective-permute-start.17) | collective-permute-done | bytes 139296 | tf_op jit(solution)/shard_map/ppermute | solution.py:431
  48.6 2.3 %shard_map.84.refs_4_ = f32[128,32,128]{2,1,0:T(8,128)} custom-call(f32[256,256]{1,0:T(8,128)S(1)} %get-tuple-element.59.refs_0_, f32[256,256]{1,0:T(8,128)S(1)} %collective-permute-done.14.refs_6_.refs_1_, f32[128,256]{1,0:T(8,128)S(1)} %get-tuple-element.60.refs_2_, f32[136,256]{1,0:T(8,128)S(1)} %collective-permute-done.13.refs_4_.refs_3_, ...), custom_call_target="tpu_custom_call" | custom-call | bytes 200000000 | tf_op jit(solution)/shard_map/pallas_call | solution.py:546
  (41 shorter events, 6.4 us)
Async XLA Ops:
  1.9 15.3 %copy-start.2 = (bf16[2,2,176,384]{3,2,1,0:T(8,128)(2,1)S(1)}, bf16[2,2,176,384]{3,2,1,0:T(8,128)(2,1)}, u32[]{:S(2)}) copy-start(bf16[2,2,176,384]{3,2,1,0:T(8,128)(2,1)} %constant.10.clone.refs_4_.refs_3_) | copy-start | bytes 1622020
  1.9 15.2 %copy-start.3 = (s32[4,1024]{1,0:T(4,128)S(1)}, s32[4,1024]{1,0:T(4,128)}, u32[]{:S(2)}) copy-start(s32[4,1024]{1,0:T(4,128)} %refs_7_.3) | copy-start | bytes 49156
  1.9 15.2 %copy-start.4 = (f32[8,384]{1,0:T(8,128)S(1)}, f32[8,384]{1,0:T(8,128)}, u32[]{:S(2)}) copy-start(f32[8,384]{1,0:T(8,128)} %constant.14.clone.refs_5_.refs_6_) | copy-start | bytes 36868
  1.9 7.4 %collective-permute-start.1 = (f32[264,256]{1,0:T(8,128)S(1)}, f32[264,256]{1,0:T(8,128)S(1)}, u32[]{:S(2)}, u32[]{:S(2)}) collective-permute-start(f32[264,256]{1,0:T(8,128)S(1)} %get-tuple-element.35.refs_0_), channel_id=1, source_target_pairs={{0,2},{1,3},{2,0},{3,1},{4,6},{5,7},{6,4},{7,5},{8,10},{9,11},{10,... | collective-permute-start | bytes 811016 | tf_op jit(solution)/shard_map/ppermute | solution.py:431
  4.5 16.4 %copy-start.5 = (bf16[2,224,384]{2,1,0:T(8,128)(2,1)S(1)}, bf16[2,224,384]{2,1,0:T(8,128)(2,1)}, u32[]{:S(2)}) copy-start(bf16[2,224,384]{2,1,0:T(8,128)(2,1)} %constant.12.clone.refs_4_) | copy-start | bytes 1032196
  4.5 2.0 %collective-permute-start.5 = (f32[136,256]{1,0:T(8,128)S(1)}, f32[136,256]{1,0:T(8,128)S(1)}, u32[]{:S(2)}, u32[]{:S(2)}) collective-permute-start(f32[136,256]{1,0:T(8,128)S(1)} %get-tuple-element.46), channel_id=1, source_target_pairs={{0,1},{1,0},{2,3},{3,2},{4,5},{5,4},{6,7},{7,6},{8,9},{9,8},{10,11... | collective-permute-start | bytes 417800 | tf_op jit(solution)/shard_map/ppermute | solution.py:431
  5.6 1.4 %collective-permute-start.6 = (f32[136,256]{1,0:T(8,128)S(1)}, f32[136,256]{1,0:T(8,128)S(1)}, u32[]{:S(2)}, u32[]{:S(2)}) collective-permute-start(f32[136,256]{1,0:T(8,128)S(1)} %get-tuple-element.47), channel_id=1, source_target_pairs={{0,1},{1,0},{2,3},{3,2},{4,5},{5,4},{6,7},{7,6},{8,9},{9,8},{10,11... | collective-permute-start | bytes 417800 | tf_op jit(solution)/shard_map/ppermute | solution.py:431
  5.6 5.1 %collective-permute-start = (f32[264,256]{1,0:T(8,128)S(1)}, f32[264,256]{1,0:T(8,128)S(1)}, u32[]{:S(2)}, u32[]{:S(2)}) collective-permute-start(f32[264,256]{1,0:T(8,128)S(1)} %get-tuple-element.37), channel_id=1, source_target_pairs={{0,1},{1,0},{2,3},{3,2},{4,5},{5,4},{6,7},{7,6},{8,9},{9,8},{10,11... | collective-permute-start | bytes 811016 | tf_op jit(solution)/shard_map/ppermute | solution.py:431
  6.1 11.1 %collective-permute-start.2 = (f32[264,256]{1,0:T(8,128)S(1)}, f32[264,256]{1,0:T(8,128)S(1)}, u32[]{:S(2)}, u32[]{:S(2)}) collective-permute-start(f32[264,256]{1,0:T(8,128)S(1)} %get-tuple-element.38), channel_id=1, source_target_pairs={{0,3},{1,2},{2,1},{3,0},{4,7},{5,6},{6,5},{7,4},{8,11},{9,10},{10,... | collective-permute-start | bytes 811016 | tf_op jit(solution)/shard_map/ppermute | solution.py:431
  9.4 13.8 %copy-start = (bf16[2,2,128,528]{3,2,1,0:T(8,128)(2,1)S(1)}, bf16[2,2,128,528]{3,2,1,0:T(8,128)(2,1)}, u32[]{:S(2)}) copy-start(bf16[2,2,128,528]{3,2,1,0:T(8,128)(2,1)} %constant.11.clone.refs_4_.refs_5_) | copy-start | bytes 1622020
  9.4 17.3 %collective-permute-start.7 = (f32[528,256]{1,0:T(8,128)S(1)}, f32[528,256]{1,0:T(8,128)S(1)}, u32[]{:S(2)}, u32[]{:S(2)}) collective-permute-start(f32[528,256]{1,0:T(8,128)S(1)} %shard_map.76.refs_0_), channel_id=1, source_target_pairs={{0,2},{1,3},{2,0},{3,1},{4,6},{5,7},{6,4},{7,5},{8,10},{9,11},{10,... | collective-permute-start | bytes 1622024 | tf_op jit(solution)/shard_map/ppermute | solution.py:431
  18.0 10.5 %collective-permute-start.3 = (f32[352,256]{1,0:T(8,128)S(1)}, f32[352,256]{1,0:T(8,128)S(1)}, u32[]{:S(2)}, u32[]{:S(2)}) collective-permute-start(f32[352,256]{1,0:T(8,128)S(1)} %get-tuple-element.42), channel_id=1, source_target_pairs={{0,4},{4,0},{8,12},{12,8},{16,20},{20,16},{24,28},{28,24},{1,5},{5... | collective-permute-start | bytes 1081352 | tf_op jit(solution)/shard_map/ppermute | solution.py:502
  19.3 1.5 %collective-permute-start.4 = (f32[264,256]{1,0:T(8,128)S(1)}, f32[264,256]{1,0:T(8,128)S(1)}, u32[]{:S(2)}, u32[]{:S(2)}) collective-permute-start(f32[264,256]{1,0:T(8,128)S(1)} %get-tuple-element.44), channel_id=1, source_target_pairs={{0,1},{1,0},{2,3},{3,2},{4,5},{5,4},{6,7},{7,6},{8,9},{9,8},{10,11... | collective-permute-start | bytes 811016 | tf_op jit(solution)/shard_map/ppermute | solution.py:431
  19.3 3.8 %collective-permute-start.8 = (f32[264,256]{1,0:T(8,128)S(1)}, f32[264,256]{1,0:T(8,128)S(1)}, u32[]{:S(2)}, u32[]{:S(2)}) collective-permute-start(f32[264,256]{1,0:T(8,128)S(1)} %get-tuple-element.49), channel_id=1, source_target_pairs={{0,1},{1,0},{2,3},{3,2},{4,5},{5,4},{6,7},{7,6},{8,9},{9,8},{10,11... | collective-permute-start | bytes 811016 | tf_op jit(solution)/shard_map/ppermute | solution.py:431
  21.8 15.6 %collective-permute-start.11 = (f32[368,256]{1,0:T(8,128)S(1)}, f32[368,256]{1,0:T(8,128)S(1)}, u32[]{:S(2)}, u32[]{:S(2)}) collective-permute-start(f32[368,256]{1,0:T(8,128)S(1)} %shard_map.81), channel_id=1, source_target_pairs={{0,2},{1,3},{2,0},{3,1},{4,6},{5,7},{6,4},{7,5},{8,10},{9,11},{10,... | collective-permute-start | bytes 1130504 | tf_op jit(solution)/shard_map/ppermute | solution.py:431
  28.6 10.0 %collective-permute-start.10 = (f32[352,256]{1,0:T(8,128)S(1)}, f32[352,256]{1,0:T(8,128)S(1)}, u32[]{:S(2)}, u32[]{:S(2)}) collective-permute-start(f32[352,256]{1,0:T(8,128)S(1)} %shard_map.80), channel_id=1, source_target_pairs={{4,8},{8,4},{12,16},{16,12},{20,24},{24,20},{5,9},{9,5},{13,17},{1... | collective-permute-start | bytes 1081352 | tf_op jit(solution)/shard_map/ppermute | solution.py:511
  31.6 13.5 %collective-permute-start.14 = (f32[256,256]{1,0:T(8,128)S(1)}, f32[256,256]{1,0:T(8,128)S(1)}, u32[]{:S(2)}, u32[]{:S(2)}) collective-permute-start(f32[256,256]{1,0:T(8,128)S(1)} %get-tuple-element.56), channel_id=1, source_target_pairs={{0,1},{1,0},{2,3},{3,2},{4,5},{5,4},{6,7},{7,6},{8,9},{9,8},{10,11... | collective-permute-start | bytes 786440 | tf_op jit(solution)/shard_map/ppermute | solution.py:431
  35.7 8.9 %collective-permute-start.13 = (f32[136,256]{1,0:T(8,128)S(1)}, f32[136,256]{1,0:T(8,128)S(1)}, u32[]{:S(2)}, u32[]{:S(2)}) collective-permute-start(f32[136,256]{1,0:T(8,128)S(1)} %get-tuple-element.55), channel_id=1, source_target_pairs={{0,2},{1,3},{2,0},{3,1},{4,6},{5,7},{6,4},{7,5},{8,10},{9,11},{10,... | collective-permute-start | bytes 417800 | tf_op jit(solution)/shard_map/ppermute | solution.py:431
  37.0 8.0 %collective-permute-start.9 = (f32[136,256]{1,0:T(8,128)S(1)}, f32[136,256]{1,0:T(8,128)S(1)}, u32[]{:S(2)}, u32[]{:S(2)}) collective-permute-start(f32[136,256]{1,0:T(8,128)S(1)} %get-tuple-element.51.refs_9_), channel_id=1, source_target_pairs={{0,3},{1,2},{2,1},{3,0},{4,7},{5,6},{6,5},{7,4},{8,11},{9,10},{10,... | collective-permute-start | bytes 417800 | tf_op jit(solution)/shard_map/ppermute | solution.py:431
  39.6 8.9 %collective-permute-start.18 = (f32[256,256]{1,0:T(8,128)S(1)}, f32[256,256]{1,0:T(8,128)S(1)}, u32[]{:S(2)}, u32[]{:S(2)}) collective-permute-start(f32[256,256]{1,0:T(8,128)S(1)} %get-tuple-element.63), channel_id=1, source_target_pairs={{0,1},{1,0},{2,3},{3,2},{4,5},{5,4},{6,7},{7,6},{8,9},{9,8},{10,11... | collective-permute-start | bytes 786440 | tf_op jit(solution)/shard_map/ppermute | solution.py:431
  43.3 5.3 %collective-permute-start.17 = (f32[136,256]{1,0:T(8,128)S(1)}, f32[136,256]{1,0:T(8,128)S(1)}, u32[]{:S(2)}, u32[]{:S(2)}) collective-permute-start(f32[136,256]{1,0:T(8,128)S(1)} %get-tuple-element.62), channel_id=1, source_target_pairs={{0,2},{1,3},{2,0},{3,1},{4,6},{5,7},{6,4},{7,5},{8,10},{9,11},{10,... | collective-permute-start | bytes 417800 | tf_op jit(solution)/shard_map/ppermute | solution.py:431
  44.6 7.1 %collective-permute-start.12 = (f32[136,256]{1,0:T(8,128)S(1)}, f32[136,256]{1,0:T(8,128)S(1)}, u32[]{:S(2)}, u32[]{:S(2)}) collective-permute-start(f32[136,256]{1,0:T(8,128)S(1)} %get-tuple-element.54.refs_3_), channel_id=1, source_target_pairs={{0,3},{1,2},{2,1},{3,0},{4,7},{5,6},{6,5},{7,4},{8,11},{9,10},{10,... | collective-permute-start | bytes 417800 | tf_op jit(solution)/shard_map/ppermute | solution.py:431
  45.4 5.5 %collective-permute-start.15 = (f32[128,256]{1,0:T(8,128)S(1)}, f32[128,256]{1,0:T(8,128)S(1)}, u32[]{:S(2)}, u32[]{:S(2)}) collective-permute-start(f32[128,256]{1,0:T(8,128)S(1)} %get-tuple-element.57), channel_id=1, source_target_pairs={{0,1},{1,0},{2,3},{3,2},{4,5},{5,4},{6,7},{7,6},{8,9},{9,8},{10,11... | collective-permute-start | bytes 393224 | tf_op jit(solution)/shard_map/ppermute | solution.py:431
  45.6 5.3 %collective-permute-start.16 = (f32[128,256]{1,0:T(8,128)S(1)}, f32[128,256]{1,0:T(8,128)S(1)}, u32[]{:S(2)}, u32[]{:S(2)}) collective-permute-start(f32[128,256]{1,0:T(8,128)S(1)} %get-tuple-element.58), channel_id=1, source_target_pairs={{0,1},{1,0},{2,3},{3,2},{4,5},{5,4},{6,7},{7,6},{8,9},{9,8},{10,11... | collective-permute-start | bytes 393224 | tf_op jit(solution)/shard_map/ppermute | solution.py:431
  (2 other events, 12.6 us)

commit v16 on v15

--- a/solution.py
+++ b/solution.py
@@ -265,6 +265,8 @@
     ones_ref[0] = ones[0]
     ones_ref[1] = ones[-1]
     inverse_rows(sweeps, cells, inverse_ref, outs)
+    for out in outs[1:]:
+        out[len(rows) * cells :, :] = jnp.zeros((out.shape[0] - len(rows) * cells, width), jnp.float32)
 
 
 def local_kernel(rows, edge_rows, count, cells, *refs):
@@ -288,7 +290,8 @@
 def send_kernel(rows, edge_rows, rest, count, cells, *refs):
     half = count // 2
     inner, edges = refs[:half], refs[half : 2 * half]
-    send_ref, columns_ref, mask_ref, out_ref = refs[2 * half :]
+    send_ref, columns_ref, mask_ref = refs[2 * half : 2 * half + 3]
+    out_ref = refs[-1]
 
     def product(blocks, lines, lanes, kind):
         return sum(kind(send_ref[place(d)], block[lines, lanes]) for d, block in enumerate(blocks))
@@ -480,17 +483,18 @@
     arrived = swap(message, half)
 
     length = len(inner) * cells
-    (sent,) = call(
-        functools.partial(send_kernel, inner, edges, rest, count, cells),
-        [(len(inner) * (rest + 8), width)],
-        *inner_blocks, *edge_blocks[:half], send, diagonals, solid_mask, cost=SHORT,
-    )
-    taken = swap(sent, half)
     (own,) = call(
         functools.partial(local_kernel, inner, edges, count, cells),
         [(half * length, width)],
         message, *chip_edges, forward, inverse, diagonals, solid_mask, cost=SHORT,
     )
+
+    (sent,) = call(
+        functools.partial(send_kernel, inner, edges, rest, count, cells),
+        [(len(inner) * (rest + 8), width)],
+        *inner_blocks, *edge_blocks[:half], send, diagonals, solid_mask, cost=SHORT, earlier=(own,),
+    )
+    taken = swap(sent, half)
 
     spectrum, edge_ones, paired, other, sides = call(
         functools.partial(edge_kernel, edges, count, cells),
@@ -502,11 +506,11 @@
     halos = [lax.ppermute(paired, "plane", pairs[0])]
     *made, ones = call(
         functools.partial(inner_kernel, inner, count, cells),
-        [(length, width)] * half + [(2, modes, width)],
+        [(length, width)] + [(length + cells, width)] * (half - 1) + [(2, modes, width)],
         *inner_blocks, arrived, forward, inverse, diagonals, solid_mask, edge_ones, cost=SHORT, earlier=(own,),
     )
     (other,) = call(
-        functools.partial(join_kernel, 0, 0, 0), [(modes, width)], other, cost=SHORT, earlier=(halos[0], ones)
+        functools.partial(join_kernel, 0, 0, 0), [(modes, width)], other, cost=SHORT, earlier=(halos[0],)
     )
     halos.append(lax.ppermute(other, "plane", pairs[1]))
 

time: 52.8 us -> 52.6 us (level)
  starting transfers between devices: 21.1 us -> 16.9 us
  waiting for transfers between devices: 16.8 us -> 20.9 us
    ppermute x17, starting transfers between devices: 16.9 us -> 12.6 us  [swap(): lax.ppermute(block, 'span', [(i, i ^ d) for i in range(lax.axis_size('spa...]
    ppermute x1, waiting for transfers between devices: 0.01 us -> 3.25 us  [local(): halos = [lax.ppermute(paired, 'plane', pairs[0])]]
    ppermute x1, waiting for transfers between devices: 1.16 us -> 3.63 us  [local(): halos.append(lax.ppermute(other, 'plane', pairs[1]))]
    ppermute x17, waiting for transfers between devices: 15.6 us -> 14 us  [swap(): lax.ppermute(block, 'span', [(i, i ^ d) for i in range(lax.axis_size('spa...]
where the time goes in v16:
time: 52.6 us; the launch traced here: 52.5 us
  waiting for transfers between devices  20.9 us (40%)
  starting transfers between devices  16.9 us (32%)
  Pallas kernels  14.5 us (28%)
    ppermute x17, waiting for transfers between devices, swap(): lax.ppermute(block, 'span', [(i, i ^ d) for i in range(lax.axis_size('spa...  14 us
    ppermute x17, starting transfers between devices, swap(): lax.ppermute(block, 'span', [(i, i ^ d) for i in range(lax.axis_size('spa...  12.6 us
    pallas_call x9, Pallas kernels, call(): pl.pallas_call(kernel, out_shape=shapes, in_specs=[VMEM] * len(args) + [A...  8.06 us
    ppermute x1, waiting for transfers between devices, local(): halos.append(lax.ppermute(other, 'plane', pairs[1]))  3.63 us
    pallas_call x2, Pallas kernels, local(): pl.pallas_call(functools.partial(unpack_kernel, [piece[1:] for piece in c...  3.26 us
    ppermute x1, waiting for transfers between devices, local(): halos = [lax.ppermute(paired, 'plane', pairs[0])]  3.25 us
    pallas_call x2, Pallas kernels, pack(): pl.pallas_call(functools.partial(pack_kernel, jobs, row_count, cells, len...  3.16 us
    ppermute x1, starting transfers between devices, local(): halos.append(lax.ppermute(other, 'plane', pairs[1]))  3.03 us
  transfers between devices with their start and end apart: 19, of which 9 were waited for; matrix products, arithmetic and copies ran while one was open for 0% of the time, Pallas kernels for 22%

profile of v16, /device:TPU:25, one launch (start us, length us, event | category | flops | bytes accessed | tf_op | source)
XLA Modules:
  0.0 52.5 jit_solution(6178390424259503416)
XLA Ops:
  0.0 1.9 %shard_map.73 = (f32[264,256]{1,0:T(8,128)S(1)}, f32[264,256]{1,0:T(8,128)S(1)}, f32[264,256]{1,0:T(8,128)S(1)}) custom-call(f32[128,32,128]{2,1,0:T(8,128)} %bitcast.10), custom_call_target="tpu_custom_call" | custom-call | bytes 200000000 | tf_op jit(solution)/shard_map/pallas_call | solution.py:458
  1.9 1.3 %collective-permute-start.1 = (f32[264,256]{1,0:T(8,128)S(1)}, f32[264,256]{1,0:T(8,128)S(1)}, u32[]{:S(2)}, u32[]{:S(2)}) collective-permute-start(f32[264,256]{1,0:T(8,128)S(1)} %get-tuple-element.35.refs_0_), channel_id=1, source_target_pairs={{0,2},{1,3},{2,0},{3,1},{4,6},{5,7},{6,4},{7,5},{8,10},{9,11},{10,... | collective-permute-start | bytes 811016 | tf_op jit(solution)/shard_map/ppermute | solution.py:434
  3.2 1.0 %collective-permute-start = (f32[264,256]{1,0:T(8,128)S(1)}, f32[264,256]{1,0:T(8,128)S(1)}, u32[]{:S(2)}, u32[]{:S(2)}) collective-permute-start(f32[264,256]{1,0:T(8,128)S(1)} %get-tuple-element.37), channel_id=1, source_target_pairs={{0,1},{1,0},{2,3},{3,2},{4,5},{5,4},{6,7},{7,6},{8,9},{9,8},{10,11... | collective-permute-start | bytes 811016 | tf_op jit(solution)/shard_map/ppermute | solution.py:434
  4.3 1.3 %shard_map.74 = (f32[264,256]{1,0:T(8,128)S(1)}, f32[264,256]{1,0:T(8,128)S(1)}, f32[264,256]{1,0:T(8,128)S(1)}, f32[264,256]{1,0:T(8,128)S(1)}, f32[264,256]{1,...) custom-call(f32[128,32,128]{2,1,0:T(8,128)S(1)} %bitcast.11, ...), custom_call_target="tpu_custom_call" | custom-call | bytes 200000000 | tf_op jit(solution)/shard_map/pallas_call | solution.py:458
  7.5 1.8 %collective-permute-done.1.refs_2_.refs_3_ = f32[264,256]{1,0:T(8,128)S(1)} collective-permute-done((f32[264,256]{1,0:T(8,128)S(1)}, f32[264,256]{1,0:T(8,128)S(1)}, u32[]{:S(2)}, u32[]{:S(2)}) %collective-permute-start.1) | collective-permute-done | bytes 270368 | tf_op jit(solution)/shard_map/ppermute | solution.py:434
  9.4 1.3 %collective-permute-start.7 = (f32[528,256]{1,0:T(8,128)S(1)}, f32[528,256]{1,0:T(8,128)S(1)}, u32[]{:S(2)}, u32[]{:S(2)}) collective-permute-start(f32[528,256]{1,0:T(8,128)S(1)} %shard_map.76.refs_0_), channel_id=1, source_target_pairs={{0,2},{1,3},{2,0},{3,1},{4,6},{5,7},{6,4},{7,5},{8,10},{9,11},{10,... | collective-permute-start | bytes 1622024 | tf_op jit(solution)/shard_map/ppermute | solution.py:434
  10.7 6.4 %collective-permute-done.2.refs_3_ = f32[264,256]{1,0:T(8,128)S(1)} collective-permute-done((f32[264,256]{1,0:T(8,128)S(1)}, f32[264,256]{1,0:T(8,128)S(1)}, u32[]{:S(2)}, u32[]{:S(2)}) %collective-permute-start.2) | collective-permute-done | bytes 270368 | tf_op jit(solution)/shard_map/ppermute | solution.py:434
  18.1 1.3 %collective-permute-start.3 = (f32[352,256]{1,0:T(8,128)S(1)}, f32[352,256]{1,0:T(8,128)S(1)}, u32[]{:S(2)}, u32[]{:S(2)}) collective-permute-start(f32[352,256]{1,0:T(8,128)S(1)} %get-tuple-element.42), channel_id=1, source_target_pairs={{0,4},{4,0},{8,12},{12,8},{16,20},{20,16},{24,28},{28,24},{1,5},{5... | collective-permute-start | bytes 1081352 | tf_op jit(solution)/shard_map/ppermute | solution.py:506
  19.9 1.0 %collective-permute-done.8.refs_2_ = f32[264,256]{1,0:T(8,128)S(1)} collective-permute-done((f32[264,256]{1,0:T(8,128)S(1)}, f32[264,256]{1,0:T(8,128)S(1)}, u32[]{:S(2)}, u32[]{:S(2)}) %collective-permute-start.8) | collective-permute-done | bytes 270368 | tf_op jit(solution)/shard_map/ppermute | solution.py:434
  20.9 1.9 %shard_map.77.refs_8_.refs_7_.refs_1_ = f32[512,256]{1,0:T(8,128)S(1)} custom-call(f32[528,256]{1,0:T(8,128)S(1)} %shard_map.76.refs_0_, f32[264,256]{1,0:T(8,128)S(1)} %get-tuple-element.48.refs_1_, f32[264,256]{1,0:T(8,128)S(1)} %collective-permute-done.8.refs_2_, bf16[2,2,176,384]{3,2,1,0:T(8,128)(2,1)S(1)} %copy-done.2, ...), custom_call_target="tpu_custom_call" | custom-call | bytes 1024 | tf_op jit(solution)/shard_map/pallas_call | solution.py:423
  22.9 0.9 %shard_map.81 = f32[368,256]{1,0:T(8,128)S(1)} custom-call(f32[264,256]{1,0:T(8,128)S(1)} %get-tuple-element.43.refs_0_, f32[264,256]{1,0:T(8,128)S(1)} %collective-permute-done.4.refs_1_, f32[264,256]{1,0:T(8,128)S(1)} %get-tuple-element.36.refs_0_.refs_2_, f32[264,256]{1,0:T(8,128)S(1)} %collective-permute-done.refs_1_.refs_3_, ...), custom_call_target="tpu_custom_call" | custom-call | bytes 1024 | tf_op jit(solution)/shard_map/pallas_call | solution.py:423
  23.8 1.3 %collective-permute-start.11 = (f32[368,256]{1,0:T(8,128)S(1)}, f32[368,256]{1,0:T(8,128)S(1)}, u32[]{:S(2)}, u32[]{:S(2)}) collective-permute-start(f32[368,256]{1,0:T(8,128)S(1)} %shard_map.81), channel_id=1, source_target_pairs={{0,2},{1,3},{2,0},{3,1},{4,6},{5,7},{6,4},{7,5},{8,10},{9,11},{10,... | collective-permute-start | bytes 1130504 | tf_op jit(solution)/shard_map/ppermute | solution.py:434
  25.1 3.3 %collective-permute-done.3.refs_3_.refs_1_ = f32[352,256]{1,0:T(8,128)S(1)} collective-permute-done((f32[352,256]{1,0:T(8,128)S(1)}, f32[352,256]{1,0:T(8,128)S(1)}, u32[]{:S(2)}, u32[]{:S(2)}) %collective-permute-start.3) | collective-permute-done | bytes 360480 | tf_op jit(solution)/shard_map/ppermute | solution.py:506
  28.4 3.0 %collective-permute-start.10 = (f32[352,256]{1,0:T(8,128)S(1)}, f32[352,256]{1,0:T(8,128)S(1)}, u32[]{:S(2)}, u32[]{:S(2)}) collective-permute-start(f32[352,256]{1,0:T(8,128)S(1)} %shard_map.80), channel_id=1, source_target_pairs={{4,8},{8,4},{12,16},{16,12},{20,24},{24,20},{5,9},{9,5},{13,17},{1... | collective-permute-start | bytes 1081352 | tf_op jit(solution)/shard_map/ppermute | solution.py:515
  31.4 1.8 %shard_map.78 = (f32[256,256]{1,0:T(8,128)S(1)}, f32[384,256]{1,0:T(8,128)S(1)}, f32[2,352,256]{2,1,0:T(8,128)S(1)}) custom-call(f32[264,256]{1,0:T(8,128)S(1)} %get-tuple-element.43.refs_0_, f32[264,256]{1,0:T(8,128)S(1)} %collective-permute-done.4.refs_1_, f32[528,256]{1,0:T(8,128)S(1)} %collective-permute-done.7.refs_2_, ...), custom_call_target="tpu_custom_call" | custom-call | bytes 1024 | tf_op jit(solution)/shard_map/pallas_call | solution.py:423
  33.2 0.9 %collective-permute-start.14 = (f32[384,256]{1,0:T(8,128)S(1)}, f32[384,256]{1,0:T(8,128)S(1)}, u32[]{:S(2)}, u32[]{:S(2)}) collective-permute-start(f32[384,256]{1,0:T(8,128)S(1)} %get-tuple-element.56), channel_id=1, source_target_pairs={{0,1},{1,0},{2,3},{3,2},{4,5},{5,4},{6,7},{7,6},{8,9},{9,8},{10,11... | collective-permute-start | bytes 1179656 | tf_op jit(solution)/shard_map/ppermute | solution.py:434
  34.1 1.1 %shard_map.79 = (f32[128,256]{1,0:T(8,128)S(1)}, f32[128,256]{1,0:T(8,128)S(1)}, f32[136,256]{1,0:T(8,128)S(1)}, f32[136,256]{1,0:T(8,128)S(1)}) custom-call(f32[2,352,256]{2,1,0:T(8,128)S(1)} %get-tuple-element.39.refs_0_, f32[2,352,256]{2,1,0:T(8,128)S(1)} %get-tuple-element.40.refs_7_.refs_1_, f32[352,16]{1,0:T(8,128)S(1)} %get-tuple-element.41.refs_2_, ...), custom_call_target="tpu_custom_call" | custom-call | bytes 1024 | tf_op jit(solution)/shard_map/pallas_call | solution.py:423
  35.3 1.6 %collective-permute-start.9 = (f32[136,256]{1,0:T(8,128)S(1)}, f32[136,256]{1,0:T(8,128)S(1)}, u32[]{:S(2)}, u32[]{:S(2)}) collective-permute-start(f32[136,256]{1,0:T(8,128)S(1)} %get-tuple-element.51.refs_9_), channel_id=1, source_target_pairs={{0,3},{1,2},{2,1},{3,0},{4,7},{5,6},{6,5},{7,4},{8,11},{9,10},{10,... | collective-permute-start | bytes 417800 | tf_op jit(solution)/shard_map/ppermute | solution.py:434
  36.9 3.6 %collective-permute-done.10.refs_3_ = f32[352,256]{1,0:T(8,128)S(1)} collective-permute-done((f32[352,256]{1,0:T(8,128)S(1)}, f32[352,256]{1,0:T(8,128)S(1)}, u32[]{:S(2)}, u32[]{:S(2)}) %collective-permute-start.10) | collective-permute-done | bytes 360480 | tf_op jit(solution)/shard_map/ppermute | solution.py:515
  40.6 1.1 %shard_map.82 = (f32[128,256]{1,0:T(8,128)S(1)}, f32[256,256]{1,0:T(8,128)S(1)}, f32[136,256]{1,0:T(8,128)S(1)}, f32[136,256]{1,0:T(8,128)S(1)}) custom-call(f32[2,352,256]{2,1,0:T(8,128)S(1)} %get-tuple-element.39.refs_0_, f32[2,352,256]{2,1,0:T(8,128)S(1)} %get-tuple-element.40.refs_7_.refs_1_, f32[352,16]{1,0:T(8,128)S(1)} %get-tuple-element.41.refs_2_, ...), custom_call_target="tpu_custom_call" | custom-call | bytes 200000000 | tf_op jit(solution)/shard_map/pallas_call | solution.py:423
  41.6 1.5 %collective-permute-start.18 = (f32[256,256]{1,0:T(8,128)S(1)}, f32[256,256]{1,0:T(8,128)S(1)}, u32[]{:S(2)}, u32[]{:S(2)}) collective-permute-start(f32[256,256]{1,0:T(8,128)S(1)} %get-tuple-element.63), channel_id=1, source_target_pairs={{0,1},{1,0},{2,3},{3,2},{4,5},{5,4},{6,7},{7,6},{8,9},{9,8},{10,11... | collective-permute-start | bytes 786440 | tf_op jit(solution)/shard_map/ppermute | solution.py:434
  43.8 1.1 %collective-permute-start.12 = (f32[136,256]{1,0:T(8,128)S(1)}, f32[136,256]{1,0:T(8,128)S(1)}, u32[]{:S(2)}, u32[]{:S(2)}) collective-permute-start(f32[136,256]{1,0:T(8,128)S(1)} %get-tuple-element.54.refs_3_), channel_id=1, source_target_pairs={{0,3},{1,2},{2,1},{3,0},{4,7},{5,6},{6,5},{7,4},{8,11},{9,10},{10,... | collective-permute-start | bytes 417800 | tf_op jit(solution)/shard_map/ppermute | solution.py:434
  45.8 2.6 %collective-permute-done.17.refs_5_ = f32[136,256]{1,0:T(8,128)S(1)} collective-permute-done((f32[136,256]{1,0:T(8,128)S(1)}, f32[136,256]{1,0:T(8,128)S(1)}, u32[]{:S(2)}, u32[]{:S(2)}) %collective-permute-start.17) | collective-permute-done | bytes 139296 | tf_op jit(solution)/shard_map/ppermute | solution.py:434
  48.4 2.3 %shard_map.84.refs_4_ = f32[128,32,128]{2,1,0:T(8,128)} custom-call(f32[256,256]{1,0:T(8,128)S(1)} %get-tuple-element.59.refs_0_, f32[384,256]{1,0:T(8,128)S(1)} %collective-permute-done.14.refs_6_.refs_1_, f32[128,256]{1,0:T(8,128)S(1)} %get-tuple-element.60.refs_2_, f32[136,256]{1,0:T(8,128)S(1)} %collective-permute-done.13.refs_4_.refs_3_, ...), custom_call_target="tpu_custom_call" | custom-call | bytes 200000000 | tf_op jit(solution)/shard_map/pallas_call | solution.py:550
  (41 shorter events, 6.9 us)
Async XLA Ops:
  1.9 15.3 %copy-start.2 = (bf16[2,2,176,384]{3,2,1,0:T(8,128)(2,1)S(1)}, bf16[2,2,176,384]{3,2,1,0:T(8,128)(2,1)}, u32[]{:S(2)}) copy-start(bf16[2,2,176,384]{3,2,1,0:T(8,128)(2,1)} %constant.10.clone.refs_4_.refs_3_) | copy-start | bytes 1622020
  1.9 15.2 %copy-start.3 = (s32[4,1024]{1,0:T(4,128)S(1)}, s32[4,1024]{1,0:T(4,128)}, u32[]{:S(2)}) copy-start(s32[4,1024]{1,0:T(4,128)} %refs_7_.3) | copy-start | bytes 49156
  1.9 15.2 %copy-start.4 = (f32[8,384]{1,0:T(8,128)S(1)}, f32[8,384]{1,0:T(8,128)}, u32[]{:S(2)}) copy-start(f32[8,384]{1,0:T(8,128)} %constant.14.clone.refs_5_.refs_6_) | copy-start | bytes 36868
  1.9 7.4 %collective-permute-start.1 = (f32[264,256]{1,0:T(8,128)S(1)}, f32[264,256]{1,0:T(8,128)S(1)}, u32[]{:S(2)}, u32[]{:S(2)}) collective-permute-start(f32[264,256]{1,0:T(8,128)S(1)} %get-tuple-element.35.refs_0_), channel_id=1, source_target_pairs={{0,2},{1,3},{2,0},{3,1},{4,6},{5,7},{6,4},{7,5},{8,10},{9,11},{10,... | collective-permute-start | bytes 811016 | tf_op jit(solution)/shard_map/ppermute | solution.py:434
  3.2 7.5 %collective-permute-start = (f32[264,256]{1,0:T(8,128)S(1)}, f32[264,256]{1,0:T(8,128)S(1)}, u32[]{:S(2)}, u32[]{:S(2)}) collective-permute-start(f32[264,256]{1,0:T(8,128)S(1)} %get-tuple-element.37), channel_id=1, source_target_pairs={{0,1},{1,0},{2,3},{3,2},{4,5},{5,4},{6,7},{7,6},{8,9},{9,8},{10,11... | collective-permute-start | bytes 811016 | tf_op jit(solution)/shard_map/ppermute | solution.py:434
  4.2 13.0 %collective-permute-start.2 = (f32[264,256]{1,0:T(8,128)S(1)}, f32[264,256]{1,0:T(8,128)S(1)}, u32[]{:S(2)}, u32[]{:S(2)}) collective-permute-start(f32[264,256]{1,0:T(8,128)S(1)} %get-tuple-element.38), channel_id=1, source_target_pairs={{0,3},{1,2},{2,1},{3,0},{4,7},{5,6},{6,5},{7,4},{8,11},{9,10},{10,... | collective-permute-start | bytes 811016 | tf_op jit(solution)/shard_map/ppermute | solution.py:434
  5.6 15.3 %copy-start = (bf16[2,2,128,528]{3,2,1,0:T(8,128)(2,1)S(1)}, bf16[2,2,128,528]{3,2,1,0:T(8,128)(2,1)}, u32[]{:S(2)}) copy-start(bf16[2,2,128,528]{3,2,1,0:T(8,128)(2,1)} %constant.11.clone.refs_4_.refs_5_) | copy-start | bytes 1622020
  5.6 1.6 %collective-permute-start.5 = (f32[136,256]{1,0:T(8,128)S(1)}, f32[136,256]{1,0:T(8,128)S(1)}, u32[]{:S(2)}, u32[]{:S(2)}) collective-permute-start(f32[136,256]{1,0:T(8,128)S(1)} %get-tuple-element.46), channel_id=1, source_target_pairs={{0,1},{1,0},{2,3},{3,2},{4,5},{5,4},{6,7},{7,6},{8,9},{9,8},{10,11... | collective-permute-start | bytes 417800 | tf_op jit(solution)/shard_map/ppermute | solution.py:434
  6.2 1.4 %collective-permute-start.6 = (f32[136,256]{1,0:T(8,128)S(1)}, f32[136,256]{1,0:T(8,128)S(1)}, u32[]{:S(2)}, u32[]{:S(2)}) collective-permute-start(f32[136,256]{1,0:T(8,128)S(1)} %get-tuple-element.47), channel_id=1, source_target_pairs={{0,1},{1,0},{2,3},{3,2},{4,5},{5,4},{6,7},{7,6},{8,9},{9,8},{10,11... | collective-permute-start | bytes 417800 | tf_op jit(solution)/shard_map/ppermute | solution.py:434
  9.4 22.0 %collective-permute-start.7 = (f32[528,256]{1,0:T(8,128)S(1)}, f32[528,256]{1,0:T(8,128)S(1)}, u32[]{:S(2)}, u32[]{:S(2)}) collective-permute-start(f32[528,256]{1,0:T(8,128)S(1)} %shard_map.76.refs_0_), channel_id=1, source_target_pairs={{0,2},{1,3},{2,0},{3,1},{4,6},{5,7},{6,4},{7,5},{8,10},{9,11},{10,... | collective-permute-start | bytes 1622024 | tf_op jit(solution)/shard_map/ppermute | solution.py:434
  18.1 10.3 %collective-permute-start.3 = (f32[352,256]{1,0:T(8,128)S(1)}, f32[352,256]{1,0:T(8,128)S(1)}, u32[]{:S(2)}, u32[]{:S(2)}) collective-permute-start(f32[352,256]{1,0:T(8,128)S(1)} %get-tuple-element.42), channel_id=1, source_target_pairs={{0,4},{4,0},{8,12},{12,8},{16,20},{20,16},{24,28},{28,24},{1,5},{5... | collective-permute-start | bytes 1081352 | tf_op jit(solution)/shard_map/ppermute | solution.py:506
  19.3 1.5 %collective-permute-start.8 = (f32[264,256]{1,0:T(8,128)S(1)}, f32[264,256]{1,0:T(8,128)S(1)}, u32[]{:S(2)}, u32[]{:S(2)}) collective-permute-start(f32[264,256]{1,0:T(8,128)S(1)} %get-tuple-element.49), channel_id=1, source_target_pairs={{0,1},{1,0},{2,3},{3,2},{4,5},{5,4},{6,7},{7,6},{8,9},{9,8},{10,11... | collective-permute-start | bytes 811016 | tf_op jit(solution)/shard_map/ppermute | solution.py:434
  19.4 3.5 %collective-permute-start.4 = (f32[264,256]{1,0:T(8,128)S(1)}, f32[264,256]{1,0:T(8,128)S(1)}, u32[]{:S(2)}, u32[]{:S(2)}) collective-permute-start(f32[264,256]{1,0:T(8,128)S(1)} %get-tuple-element.44), channel_id=1, source_target_pairs={{0,1},{1,0},{2,3},{3,2},{4,5},{5,4},{6,7},{7,6},{8,9},{9,8},{10,11... | collective-permute-start | bytes 811016 | tf_op jit(solution)/shard_map/ppermute | solution.py:434
  23.8 13.1 %collective-permute-start.11 = (f32[368,256]{1,0:T(8,128)S(1)}, f32[368,256]{1,0:T(8,128)S(1)}, u32[]{:S(2)}, u32[]{:S(2)}) collective-permute-start(f32[368,256]{1,0:T(8,128)S(1)} %shard_map.81), channel_id=1, source_target_pairs={{0,2},{1,3},{2,0},{3,1},{4,6},{5,7},{6,4},{7,5},{8,10},{9,11},{10,... | collective-permute-start | bytes 1130504 | tf_op jit(solution)/shard_map/ppermute | solution.py:434
  28.4 12.2 %collective-permute-start.10 = (f32[352,256]{1,0:T(8,128)S(1)}, f32[352,256]{1,0:T(8,128)S(1)}, u32[]{:S(2)}, u32[]{:S(2)}) collective-permute-start(f32[352,256]{1,0:T(8,128)S(1)} %shard_map.80), channel_id=1, source_target_pairs={{4,8},{8,4},{12,16},{16,12},{20,24},{24,20},{5,9},{9,5},{13,17},{1... | collective-permute-start | bytes 1081352 | tf_op jit(solution)/shard_map/ppermute | solution.py:515
  33.2 11.7 %collective-permute-start.14 = (f32[384,256]{1,0:T(8,128)S(1)}, f32[384,256]{1,0:T(8,128)S(1)}, u32[]{:S(2)}, u32[]{:S(2)}) collective-permute-start(f32[384,256]{1,0:T(8,128)S(1)} %get-tuple-element.56), channel_id=1, source_target_pairs={{0,1},{1,0},{2,3},{3,2},{4,5},{5,4},{6,7},{7,6},{8,9},{9,8},{10,11... | collective-permute-start | bytes 1179656 | tf_op jit(solution)/shard_map/ppermute | solution.py:434
  35.2 9.7 %copy-start.6 = (bf16[2,128,576]{2,1,0:T(8,128)(2,1)S(1)}, bf16[2,128,576]{2,1,0:T(8,128)(2,1)}, u32[]{:S(2)}) copy-start(bf16[2,128,576]{2,1,0:T(8,128)(2,1)} %constant.13.clone.refs_2_) | copy-start | bytes 884740
  35.2 8.5 %collective-permute-start.13 = (f32[136,256]{1,0:T(8,128)S(1)}, f32[136,256]{1,0:T(8,128)S(1)}, u32[]{:S(2)}, u32[]{:S(2)}) collective-permute-start(f32[136,256]{1,0:T(8,128)S(1)} %get-tuple-element.55), channel_id=1, source_target_pairs={{0,2},{1,3},{2,0},{3,1},{4,6},{5,7},{6,4},{7,5},{8,10},{9,11},{10,... | collective-permute-start | bytes 417800 | tf_op jit(solution)/shard_map/ppermute | solution.py:434
  35.3 9.6 %collective-permute-start.9 = (f32[136,256]{1,0:T(8,128)S(1)}, f32[136,256]{1,0:T(8,128)S(1)}, u32[]{:S(2)}, u32[]{:S(2)}) collective-permute-start(f32[136,256]{1,0:T(8,128)S(1)} %get-tuple-element.51.refs_9_), channel_id=1, source_target_pairs={{0,3},{1,2},{2,1},{3,0},{4,7},{5,6},{6,5},{7,4},{8,11},{9,10},{10,... | collective-permute-start | bytes 417800 | tf_op jit(solution)/shard_map/ppermute | solution.py:434
  41.6 6.8 %collective-permute-start.18 = (f32[256,256]{1,0:T(8,128)S(1)}, f32[256,256]{1,0:T(8,128)S(1)}, u32[]{:S(2)}, u32[]{:S(2)}) collective-permute-start(f32[256,256]{1,0:T(8,128)S(1)} %get-tuple-element.63), channel_id=1, source_target_pairs={{0,1},{1,0},{2,3},{3,2},{4,5},{5,4},{6,7},{7,6},{8,9},{9,8},{10,11... | collective-permute-start | bytes 786440 | tf_op jit(solution)/shard_map/ppermute | solution.py:434
  43.1 5.3 %collective-permute-start.17 = (f32[136,256]{1,0:T(8,128)S(1)}, f32[136,256]{1,0:T(8,128)S(1)}, u32[]{:S(2)}, u32[]{:S(2)}) collective-permute-start(f32[136,256]{1,0:T(8,128)S(1)} %get-tuple-element.62), channel_id=1, source_target_pairs={{0,2},{1,3},{2,0},{3,1},{4,6},{5,7},{6,4},{7,5},{8,10},{9,11},{10,... | collective-permute-start | bytes 417800 | tf_op jit(solution)/shard_map/ppermute | solution.py:434
  43.8 7.8 %collective-permute-start.12 = (f32[136,256]{1,0:T(8,128)S(1)}, f32[136,256]{1,0:T(8,128)S(1)}, u32[]{:S(2)}, u32[]{:S(2)}) collective-permute-start(f32[136,256]{1,0:T(8,128)S(1)} %get-tuple-element.54.refs_3_), channel_id=1, source_target_pairs={{0,3},{1,2},{2,1},{3,0},{4,7},{5,6},{6,5},{7,4},{8,11},{9,10},{10,... | collective-permute-start | bytes 417800 | tf_op jit(solution)/shard_map/ppermute | solution.py:434
  45.2 6.3 %collective-permute-start.15 = (f32[128,256]{1,0:T(8,128)S(1)}, f32[128,256]{1,0:T(8,128)S(1)}, u32[]{:S(2)}, u32[]{:S(2)}) collective-permute-start(f32[128,256]{1,0:T(8,128)S(1)} %get-tuple-element.57), channel_id=1, source_target_pairs={{0,1},{1,0},{2,3},{3,2},{4,5},{5,4},{6,7},{7,6},{8,9},{9,8},{10,11... | collective-permute-start | bytes 393224 | tf_op jit(solution)/shard_map/ppermute | solution.py:434
  45.5 6.1 %collective-permute-start.16 = (f32[128,256]{1,0:T(8,128)S(1)}, f32[128,256]{1,0:T(8,128)S(1)}, u32[]{:S(2)}, u32[]{:S(2)}) collective-permute-start(f32[128,256]{1,0:T(8,128)S(1)} %get-tuple-element.58), channel_id=1, source_target_pairs={{0,1},{1,0},{2,3},{3,2},{4,5},{5,4},{6,7},{7,6},{8,9},{9,8},{10,11... | collective-permute-start | bytes 393224 | tf_op jit(solution)/shard_map/ppermute | solution.py:434
  (2 other events, 10.0 us)

commit v17 on v16

--- a/solution.py
+++ b/solution.py
@@ -235,7 +235,8 @@
         spectrum_ref[i] = spectra[i]
         ones_ref[i] = ones[i]
     last = paired_edge() == 1
-    paired_ref[...] = jnp.where(last, ones[1], ones[0])
+    paired_ref[:modes, :] = jnp.where(last, ones[1], ones[0])
+    paired_ref[modes:, :] = jnp.zeros((paired_ref.shape[0] - modes, width), jnp.float32)
     other_ref[...] = jnp.where(last, ones[0], ones[1])
     sides_ref[...] = sides * pick(kinds, fluid, solid)
 
@@ -265,8 +266,6 @@
     ones_ref[0] = ones[0]
     ones_ref[1] = ones[-1]
     inverse_rows(sweeps, cells, inverse_ref, outs)
-    for out in outs[1:]:
-        out[len(rows) * cells :, :] = jnp.zeros((out.shape[0] - len(rows) * cells, width), jnp.float32)
 
 
 def local_kernel(rows, edge_rows, count, cells, *refs):
@@ -359,12 +358,12 @@
     spectrum_ref, edges_ref, sides_ref, halo_ref, ones_ref, inverse_ref, columns_ref, mask_ref = refs[:8]
     outs = refs[-count:]
     _, modes, width = edges_ref.shape
-    edge = paired_edge() if order == 0 else 1 - paired_edge()
+    edge = 1 - paired_edge() if order == 0 else paired_edge()
     mask, _ = masks(mask_ref, rows, 0, width)
     fluid, solid = one_over(columns_ref, 0, modes)
     sides = jnp.where(edge == 0, sides_ref[:, 0:2], sides_ref[:, 2:4])
     diagonal = pick(jnp.where(edge == 0, mask[rows[0]], mask[rows[1]]), fluid, solid)
-    sweep = second_sweep(spectrum_ref[edge], edges_ref[edge], halo_ref[...], ones_ref[edge], sides, 0, diagonal)
+    sweep = second_sweep(spectrum_ref[edge], edges_ref[edge], halo_ref[:modes, :], ones_ref[edge], sides, 0, diagonal)
     inverse_rows([sweep], cells, inverse_ref, outs[: count // 2], outs[count // 2 :])
     if order == 1:
         for d in range(1, count // 2):
@@ -375,7 +374,7 @@
 
 def join_kernel(rows, cells, near, *refs):
     own_ref, blocks, out_ref = refs[0], refs[1 : 1 + rows * near], refs[-1]
-    size = own_ref.shape[0]
+    size = rows * cells + 8
     out_ref[:size, :] = own_ref[...]
     for d in range(near):
         base = (d + 1) * size
@@ -385,6 +384,11 @@
             out_ref[base + i * cells : base + (i + 1) * cells, :] = block[:cells, :]
             at = base + rows * cells + 2 * i
             out_ref[at : at + 2, :] = block[cells : cells + 2, :]
+
+
+def copy_kernel(number, *refs):
+    for ref, out in zip(refs[:number], refs[-number:]):
+        out[...] = ref[...]
 
 
 def unpack_kernel(pieces, devices, row_count, cells, *refs):
@@ -471,16 +475,29 @@
     wanted += [(half + d, (row,)) for d in near for row in inner]
     packed = pack(source, wanted, packed[half - 1])
     edge_blocks = [packed[half + 1], *edge_blocks]
-    inner_blocks = [packed[0]] + [swap(packed[d], d) for d in near]
-    chip_edges = [packed[half + 2]] + [swap(packed[half + 2 + d], d) for d in near]
     relayed = packed[2 * half + 2 :]
     relayed = [swap(relayed[(d - 1) * len(inner) + i], d) for d in near for i in range(len(inner))]
+    size = len(inner) * cells + 8
     (message,) = call(
         functools.partial(join_kernel, len(inner), cells, half - 1),
-        [(half * (len(inner) * cells + 8), width)],
+        [(half * size, width)],
         packed[half], *relayed, cost=SHORT, earlier=(edge_blocks[half],),
     )
     arrived = swap(message, half)
+
+    spectrum, edge_ones, paired, other, sides = call(
+        functools.partial(edge_kernel, edges, count, cells),
+        [(2, modes, width), (2, modes, width), (modes + 16, width), (modes, width), (modes, 16)],
+        *edge_blocks, forward, diagonals, solid_mask,
+    )
+    later = [packed[d] for d in near] + [packed[half + 2 + d] for d in near]
+    if later:
+        later = call(
+            functools.partial(copy_kernel, len(later)), [block.shape for block in later], *later,
+            cost=SHORT, earlier=(sides,),
+        )
+    inner_blocks = [packed[0]] + [swap(later[d - 1], d) for d in near]
+    chip_edges = [packed[half + 2]] + [swap(later[half + d - 2], d) for d in near]
 
     length = len(inner) * cells
     (own,) = call(
@@ -496,41 +513,31 @@
     )
     taken = swap(sent, half)
 
-    spectrum, edge_ones, paired, other, sides = call(
-        functools.partial(edge_kernel, edges, count, cells),
-        [(2, modes, width), (2, modes, width), (modes, width), (modes, width), (modes, 16)],
-        *edge_blocks, forward, diagonals, solid_mask,
-    )
     pairs = [[(i, i ^ 1) for i in range(plane_count)], [(i, ((i + 1) ^ 1) - 1) for i in range(plane_count)]]
     pairs = [[(i, j) for i, j in pair if 0 <= j < plane_count] for pair in pairs]
-    halos = [lax.ppermute(paired, "plane", pairs[0])]
+    halos = [lax.ppermute(row, "plane", pair) for row, pair in zip((paired, other), pairs)]
     *made, ones = call(
         functools.partial(inner_kernel, inner, count, cells),
-        [(length, width)] + [(length + cells, width)] * (half - 1) + [(2, modes, width)],
+        [(length, width)] * half + [(2, modes, width)],
         *inner_blocks, arrived, forward, inverse, diagonals, solid_mask, edge_ones, cost=SHORT, earlier=(own,),
     )
-    (other,) = call(
-        functools.partial(join_kernel, 0, 0, 0), [(modes, width)], other, cost=SHORT, earlier=(halos[0],)
-    )
-    halos.append(lax.ppermute(other, "plane", pairs[1]))
-
     pieces = [(made[0], 0, 0, inner, 0, tiles)]
     made_got = [swap(made[d], d) for d in near]
     pieces += [(block, d, 0, inner, 0, tiles) for d, block in zip(near, made_got)]
     rim_got, near_rim, earlier = [], [], []
-    for order, name in enumerate(("near", "far")):
+    for order, name in enumerate(("far", "near")):
         outs = call(
             functools.partial(rim_kernel, edges, order, count, cells),
             [(cells, width)] + [((order + 1) * cells, width)] * (half - 1) + [(cells + 8, width)] * half,
-            spectrum, edge_ones, sides, halos[order], ones, inverse, diagonals, solid_mask, *near_rim,
+            spectrum, edge_ones, sides, halos[1 - order], ones, inverse, diagonals, solid_mask, *near_rim,
             cost=LONG if order else SHORT, earlier=earlier,
         )
         near_rim = outs[1:half]
         pieces.append((outs[0], 0, 0, (name,), 0, tiles))
         rim_got.append([swap(outs[d], d) for d in far])
         pieces += [(block, d, 0, (name,), 0, tiles) for d, block in zip(far, rim_got[order])]
-        earlier = [outs[-1], taken]
-    pieces += [(swap(near_rim[d - 1], d), d, 0, ("far", "near"), 0, tiles) for d in near]
+        earlier = [outs[-1]]
+    pieces += [(swap(near_rim[d - 1], d), d, 0, ("near", "far"), 0, tiles) for d in near]
     rebuilt = call(
         functools.partial(take_kernel, inner, count, cells),
         [(length, width)] + [(cells, width)] * ((half - 1) * len(inner)),

time: 52.6 us -> 50.2 us (0.954)
  the two profiles are of different devices: /device:TPU:25 before, /device:TPU:0 now
where the time goes in v17:
time: 50.2 us; the launch traced here: 50 us
  waiting for transfers between devices  19.6 us (39%)
  starting transfers between devices  15.5 us (31%)
  Pallas kernels  14.6 us (29%)
    ppermute x17, waiting for transfers between devices, swap(): lax.ppermute(block, 'span', [(i, i ^ d) for i in range(lax.axis_size('spa...  17.1 us
    ppermute x17, starting transfers between devices, swap(): lax.ppermute(block, 'span', [(i, i ^ d) for i in range(lax.axis_size('spa...  13 us
    pallas_call x9, Pallas kernels, call(): pl.pallas_call(kernel, out_shape=shapes, in_specs=[VMEM] * len(args) + [A...  8.12 us
    pallas_call x2, Pallas kernels, local(): pl.pallas_call(functools.partial(unpack_kernel, [piece[1:] for piece in c...  3.27 us
    pallas_call x2, Pallas kernels, pack(): pl.pallas_call(functools.partial(pack_kernel, jobs, row_count, cells, len...  3.16 us
    ppermute x2, starting transfers between devices, local(): lax.ppermute(row, 'plane', pair)  2.51 us
    ppermute x2, waiting for transfers between devices, local(): lax.ppermute(row, 'plane', pair)  2.47 us
  transfers between devices with their start and end apart: 19, of which 9 were waited for; matrix products, arithmetic and copies ran while one was open for 0% of the time, Pallas kernels for 23%

profile of v17, /device:TPU:0, one launch (start us, length us, event | category | flops | bytes accessed | tf_op | source)
XLA Modules:
  0.0 50.0 jit_solution(10935691954334561265)
XLA Ops:
  0.0 1.9 %shard_map.73 = (f32[264,256]{1,0:T(8,128)S(1)}, f32[264,256]{1,0:T(8,128)S(1)}, f32[264,256]{1,0:T(8,128)S(1)}) custom-call(f32[128,32,128]{2,1,0:T(8,128)} %bitcast.10), custom_call_target="tpu_custom_call" | custom-call | bytes 200000000 | tf_op jit(solution)/shard_map/pallas_call | solution.py:462
  1.9 3.0 %collective-permute-start.1 = (f32[264,256]{1,0:T(8,128)S(1)}, f32[264,256]{1,0:T(8,128)S(1)}, u32[]{:S(2)}, u32[]{:S(2)}) collective-permute-start(f32[264,256]{1,0:T(8,128)S(1)} %get-tuple-element.37.refs_0_), channel_id=1, source_target_pairs={{0,2},{1,3},{2,0},{3,1},{4,6},{5,7},{6,4},{7,5},{8,10},{9,11},{10,... | collective-permute-start | bytes 811016 | tf_op jit(solution)/shard_map/ppermute | solution.py:438
  5.0 1.3 %shard_map.74 = (f32[264,256]{1,0:T(8,128)S(1)}, f32[264,256]{1,0:T(8,128)S(1)}, f32[264,256]{1,0:T(8,128)S(1)}, f32[264,256]{1,0:T(8,128)S(1)}, f32[264,256]{1,...) custom-call(f32[128,32,128]{2,1,0:T(8,128)S(1)} %bitcast.11, ...), custom_call_target="tpu_custom_call" | custom-call | bytes 200000000 | tf_op jit(solution)/shard_map/pallas_call | solution.py:462
  7.9 4.4 %collective-permute-done.1.refs_2_.refs_3_ = f32[264,256]{1,0:T(8,128)S(1)} collective-permute-done((f32[264,256]{1,0:T(8,128)S(1)}, f32[264,256]{1,0:T(8,128)S(1)}, u32[]{:S(2)}, u32[]{:S(2)}) %collective-permute-start.1) | collective-permute-done | bytes 270368 | tf_op jit(solution)/shard_map/ppermute | solution.py:438
  12.3 2.1 %collective-permute-start.7 = (f32[528,256]{1,0:T(8,128)S(1)}, f32[528,256]{1,0:T(8,128)S(1)}, u32[]{:S(2)}, u32[]{:S(2)}) collective-permute-start(f32[528,256]{1,0:T(8,128)S(1)} %shard_map.77.refs_0_), channel_id=1, source_target_pairs={{0,2},{1,3},{2,0},{3,1},{4,6},{5,7},{6,4},{7,5},{8,10},{9,11},{10,... | collective-permute-start | bytes 1622024 | tf_op jit(solution)/shard_map/ppermute | solution.py:438
  14.5 3.2 %collective-permute-done.2.refs_3_ = f32[264,256]{1,0:T(8,128)S(1)} collective-permute-done((f32[264,256]{1,0:T(8,128)S(1)}, f32[264,256]{1,0:T(8,128)S(1)}, u32[]{:S(2)}, u32[]{:S(2)}) %collective-permute-start.2) | collective-permute-done | bytes 270368 | tf_op jit(solution)/shard_map/ppermute | solution.py:438
  17.7 0.9 %shard_map.75 = (f32[2,352,256]{2,1,0:T(8,128)S(1)}, f32[2,352,256]{2,1,0:T(8,128)S(1)}, f32[368,256]{1,0:T(8,128)S(1)}, f32[352,256]{1,0:T(8,128)S(1)}, f32[352,16]{1,0:T(8,128)S(1)}) custom-call(f32[264,256]{1,0:T(8,128)S(1)} %get-tuple-element.38.refs_0_.refs_2_, f32[264,256]{1,0:T(8,128)S(1)} %collective-permute-done.refs_1_.refs_3_, ...), custom_call_target="tpu_custom_call" | custom-call | bytes 200000000 | tf_op jit(solution)/shard_map/pallas_call | solution.py:427
  19.2 1.8 %collective-permute-start.10 = (f32[368,256]{1,0:T(8,128)S(1)}, f32[368,256]{1,0:T(8,128)S(1)}, u32[]{:S(2)}, u32[]{:S(2)}) collective-permute-start(f32[368,256]{1,0:T(8,128)S(1)} %get-tuple-element.56), channel_id=1, source_target_pairs={{0,4},{4,0},{8,12},{12,8},{16,20},{20,16},{24,28},{28,24},{1,5},{5... | collective-permute-start | bytes 1130504 | tf_op jit(solution)/shard_map/ppermute | solution.py:518
  21.0 0.7 %collective-permute-start.3 = (f32[352,256]{1,0:T(8,128)S(1)}, f32[352,256]{1,0:T(8,128)S(1)}, u32[]{:S(2)}, u32[]{:S(2)}) collective-permute-start(f32[352,256]{1,0:T(8,128)S(1)} %get-tuple-element.44), channel_id=1, source_target_pairs={{4,8},{8,4},{12,16},{16,12},{20,24},{24,20},{5,9},{9,5},{13,17},{1... | collective-permute-start | bytes 1081352 | tf_op jit(solution)/shard_map/ppermute | solution.py:518
  21.7 2.0 %shard_map.78.refs_8_.refs_7_.refs_1_ = f32[512,256]{1,0:T(8,128)S(1)} custom-call(f32[528,256]{1,0:T(8,128)S(1)} %shard_map.77.refs_0_, f32[264,256]{1,0:T(8,128)S(1)} %get-tuple-element.52.refs_1_, f32[264,256]{1,0:T(8,128)S(1)} %collective-permute-done.8.refs_2_, bf16[2,2,176,384]{3,2,1,0:T(8,128)(2,1)S(1)} %copy-done.2, ...), custom_call_target="tpu_custom_call" | custom-call | bytes 1024 | tf_op jit(solution)/shard_map/pallas_call | solution.py:427
  23.7 0.9 %shard_map.82 = f32[368,256]{1,0:T(8,128)S(1)} custom-call(f32[264,256]{1,0:T(8,128)S(1)} %get-tuple-element.45.refs_0_, f32[264,256]{1,0:T(8,128)S(1)} %collective-permute-done.4.refs_1_, f32[264,256]{1,0:T(8,128)S(1)} %get-tuple-element.38.refs_0_.refs_2_, f32[264,256]{1,0:T(8,128)S(1)} %collective-permute-done.refs_1_.refs_3_, ...), custom_call_target="tpu_custom_call" | custom-call | bytes 1024 | tf_op jit(solution)/shard_map/pallas_call | solution.py:427
  24.7 1.6 %collective-permute-start.12 = (f32[368,256]{1,0:T(8,128)S(1)}, f32[368,256]{1,0:T(8,128)S(1)}, u32[]{:S(2)}, u32[]{:S(2)}) collective-permute-start(f32[368,256]{1,0:T(8,128)S(1)} %shard_map.82), channel_id=1, source_target_pairs={{0,2},{1,3},{2,0},{3,1},{4,6},{5,7},{6,4},{7,5},{8,10},{9,11},{10,... | collective-permute-start | bytes 1130504 | tf_op jit(solution)/shard_map/ppermute | solution.py:438
  26.2 3.4 %collective-permute-done.7.refs_2_ = f32[528,256]{1,0:T(8,128)S(1)} collective-permute-done((f32[528,256]{1,0:T(8,128)S(1)}, f32[528,256]{1,0:T(8,128)S(1)}, u32[]{:S(2)}, u32[]{:S(2)}) %collective-permute-start.7) | collective-permute-done | bytes 540704 | tf_op jit(solution)/shard_map/ppermute | solution.py:438
  29.7 1.8 %shard_map.79 = (f32[256,256]{1,0:T(8,128)S(1)}, f32[256,256]{1,0:T(8,128)S(1)}, f32[2,352,256]{2,1,0:T(8,128)S(1)}) custom-call(f32[264,256]{1,0:T(8,128)S(1)} %get-tuple-element.45.refs_0_, f32[264,256]{1,0:T(8,128)S(1)} %collective-permute-done.4.refs_1_, f32[528,256]{1,0:T(8,128)S(1)} %collective-permute-done.7.refs_2_, ...), custom_call_target="tpu_custom_call" | custom-call | bytes 1024 | tf_op jit(solution)/shard_map/pallas_call | solution.py:427
  31.5 1.1 %shard_map.80 = (f32[128,256]{1,0:T(8,128)S(1)}, f32[128,256]{1,0:T(8,128)S(1)}, f32[136,256]{1,0:T(8,128)S(1)}, f32[136,256]{1,0:T(8,128)S(1)}) custom-call(f32[2,352,256]{2,1,0:T(8,128)S(1)} %get-tuple-element.41.refs_0_, f32[2,352,256]{2,1,0:T(8,128)S(1)} %get-tuple-element.42.refs_7_.refs_1_, f32[352,16]{1,0:T(8,128)S(1)} %get-tuple-element.43.refs_2_, ...), custom_call_target="tpu_custom_call" | custom-call | bytes 1024 | tf_op jit(solution)/shard_map/pallas_call | solution.py:427
  32.6 2.1 %collective-permute-start.13 = (f32[136,256]{1,0:T(8,128)S(1)}, f32[136,256]{1,0:T(8,128)S(1)}, u32[]{:S(2)}, u32[]{:S(2)}) collective-permute-start(f32[136,256]{1,0:T(8,128)S(1)} %get-tuple-element.59), channel_id=1, source_target_pairs={{0,2},{1,3},{2,0},{3,1},{4,6},{5,7},{6,4},{7,5},{8,10},{9,11},{10,... | collective-permute-start | bytes 417800 | tf_op jit(solution)/shard_map/ppermute | solution.py:438
  34.9 2.5 %collective-permute-done.10.refs_3_ = f32[368,256]{1,0:T(8,128)S(1)} collective-permute-done((f32[368,256]{1,0:T(8,128)S(1)}, f32[368,256]{1,0:T(8,128)S(1)}, u32[]{:S(2)}, u32[]{:S(2)}) %collective-permute-start.10) | collective-permute-done | bytes 376864 | tf_op jit(solution)/shard_map/ppermute | solution.py:518
  37.4 1.1 %shard_map.81 = (f32[128,256]{1,0:T(8,128)S(1)}, f32[256,256]{1,0:T(8,128)S(1)}, f32[136,256]{1,0:T(8,128)S(1)}, f32[136,256]{1,0:T(8,128)S(1)}) custom-call(f32[2,352,256]{2,1,0:T(8,128)S(1)} %get-tuple-element.41.refs_0_, f32[2,352,256]{2,1,0:T(8,128)S(1)} %get-tuple-element.42.refs_7_.refs_1_, f32[352,16]{1,0:T(8,128)S(1)} %get-tuple-element.43.refs_2_, ...), custom_call_target="tpu_custom_call" | custom-call | bytes 200000000 | tf_op jit(solution)/shard_map/pallas_call | solution.py:427
  38.5 1.6 %collective-permute-start.17 = (f32[136,256]{1,0:T(8,128)S(1)}, f32[136,256]{1,0:T(8,128)S(1)}, u32[]{:S(2)}, u32[]{:S(2)}) collective-permute-start(f32[136,256]{1,0:T(8,128)S(1)} %get-tuple-element.66), channel_id=1, source_target_pairs={{0,2},{1,3},{2,0},{3,1},{4,6},{5,7},{6,4},{7,5},{8,10},{9,11},{10,... | collective-permute-start | bytes 417800 | tf_op jit(solution)/shard_map/ppermute | solution.py:438
  40.7 2.2 %collective-permute-done.9.refs_5_.refs_0_ = f32[136,256]{1,0:T(8,128)S(1)} collective-permute-done((f32[136,256]{1,0:T(8,128)S(1)}, f32[136,256]{1,0:T(8,128)S(1)}, u32[]{:S(2)}, u32[]{:S(2)}) %collective-permute-start.9) | collective-permute-done | bytes 139296 | tf_op jit(solution)/shard_map/ppermute | solution.py:438
  43.3 0.7 %collective-permute-start.15 = (f32[128,256]{1,0:T(8,128)S(1)}, f32[128,256]{1,0:T(8,128)S(1)}, u32[]{:S(2)}, u32[]{:S(2)}) collective-permute-start(f32[128,256]{1,0:T(8,128)S(1)} %get-tuple-element.61), channel_id=1, source_target_pairs={{0,1},{1,0},{2,3},{3,2},{4,5},{5,4},{6,7},{7,6},{8,9},{9,8},{10,11... | collective-permute-start | bytes 393224 | tf_op jit(solution)/shard_map/ppermute | solution.py:438
  44.1 2.6 %collective-permute-done.17.refs_5_ = f32[136,256]{1,0:T(8,128)S(1)} collective-permute-done((f32[136,256]{1,0:T(8,128)S(1)}, f32[136,256]{1,0:T(8,128)S(1)}, u32[]{:S(2)}, u32[]{:S(2)}) %collective-permute-start.17) | collective-permute-done | bytes 139296 | tf_op jit(solution)/shard_map/ppermute | solution.py:438
  46.7 2.3 %shard_map.84.refs_4_ = f32[128,32,128]{2,1,0:T(8,128)} custom-call(f32[256,256]{1,0:T(8,128)S(1)} %get-tuple-element.63.refs_0_, f32[256,256]{1,0:T(8,128)S(1)} %collective-permute-done.14.refs_6_.refs_1_, f32[128,256]{1,0:T(8,128)S(1)} %get-tuple-element.64.refs_2_, f32[136,256]{1,0:T(8,128)S(1)} %collective-permute-done.13.refs_4_.refs_3_, ...), custom_call_target="tpu_custom_call" | custom-call | bytes 200000000 | tf_op jit(solution)/shard_map/pallas_call | solution.py:557
  49.1 0.9 %shard_map.85 = f32[128,32,128]{2,1,0:T(8,128)} custom-call(f32[136,256]{1,0:T(8,128)S(1)} %collective-permute-done.9.refs_5_.refs_0_, f32[136,256]{1,0:T(8,128)S(1)} %collective-permute-done.11.refs_1_, f32[128,256]{1,0:T(8,128)S(1)} %collective-permute-done.15.refs_2_, ...), custom_call_target="tpu_custom_call", output_to_operand_aliasing={{}: (4, {})} | custom-call | bytes 1024 | tf_op jit(solution)/shard_map/pallas_call | solution.py:557
  (41 shorter events, 3.7 us)
Async XLA Ops:
  1.9 15.8 %copy-start.2 = (bf16[2,2,176,384]{3,2,1,0:T(8,128)(2,1)S(1)}, bf16[2,2,176,384]{3,2,1,0:T(8,128)(2,1)}, u32[]{:S(2)}) copy-start(bf16[2,2,176,384]{3,2,1,0:T(8,128)(2,1)} %constant.10.clone.refs_4_.refs_3_) | copy-start | bytes 1622020
  1.9 15.7 %copy-start.3 = (s32[4,1024]{1,0:T(4,128)S(1)}, s32[4,1024]{1,0:T(4,128)}, u32[]{:S(2)}) copy-start(s32[4,1024]{1,0:T(4,128)} %refs_6_.9) | copy-start | bytes 49156
  1.9 15.7 %copy-start.4 = (f32[8,384]{1,0:T(8,128)S(1)}, f32[8,384]{1,0:T(8,128)}, u32[]{:S(2)}) copy-start(f32[8,384]{1,0:T(8,128)} %constant.14.clone.refs_5_.refs_6_) | copy-start | bytes 36868
  1.9 10.3 %collective-permute-start.1 = (f32[264,256]{1,0:T(8,128)S(1)}, f32[264,256]{1,0:T(8,128)S(1)}, u32[]{:S(2)}, u32[]{:S(2)}) collective-permute-start(f32[264,256]{1,0:T(8,128)S(1)} %get-tuple-element.37.refs_0_), channel_id=1, source_target_pairs={{0,2},{1,3},{2,0},{3,1},{4,6},{5,7},{6,4},{7,5},{8,10},{9,11},{10,... | collective-permute-start | bytes 811016 | tf_op jit(solution)/shard_map/ppermute | solution.py:438
  6.3 15.5 %copy-start = (bf16[2,2,128,528]{3,2,1,0:T(8,128)(2,1)S(1)}, bf16[2,2,128,528]{3,2,1,0:T(8,128)(2,1)}, u32[]{:S(2)}) copy-start(bf16[2,2,128,528]{3,2,1,0:T(8,128)(2,1)} %constant.11.clone.refs_4_.refs_5_) | copy-start | bytes 1622020
  6.3 1.4 %collective-permute-start.5 = (f32[136,256]{1,0:T(8,128)S(1)}, f32[136,256]{1,0:T(8,128)S(1)}, u32[]{:S(2)}, u32[]{:S(2)}) collective-permute-start(f32[136,256]{1,0:T(8,128)S(1)} %get-tuple-element.50), channel_id=1, source_target_pairs={{0,1},{1,0},{2,3},{3,2},{4,5},{5,4},{6,7},{7,6},{8,9},{9,8},{10,11... | collective-permute-start | bytes 417800 | tf_op jit(solution)/shard_map/ppermute | solution.py:438
  6.3 1.5 %collective-permute-start.6 = (f32[136,256]{1,0:T(8,128)S(1)}, f32[136,256]{1,0:T(8,128)S(1)}, u32[]{:S(2)}, u32[]{:S(2)}) collective-permute-start(f32[136,256]{1,0:T(8,128)S(1)} %get-tuple-element.51), channel_id=1, source_target_pairs={{0,1},{1,0},{2,3},{3,2},{4,5},{5,4},{6,7},{7,6},{8,9},{9,8},{10,11... | collective-permute-start | bytes 417800 | tf_op jit(solution)/shard_map/ppermute | solution.py:438
  6.8 7.6 %collective-permute-start = (f32[264,256]{1,0:T(8,128)S(1)}, f32[264,256]{1,0:T(8,128)S(1)}, u32[]{:S(2)}, u32[]{:S(2)}) collective-permute-start(f32[264,256]{1,0:T(8,128)S(1)} %get-tuple-element.39), channel_id=1, source_target_pairs={{0,1},{1,0},{2,3},{3,2},{4,5},{5,4},{6,7},{7,6},{8,9},{9,8},{10,11... | collective-permute-start | bytes 811016 | tf_op jit(solution)/shard_map/ppermute | solution.py:438
  6.9 10.7 %collective-permute-start.2 = (f32[264,256]{1,0:T(8,128)S(1)}, f32[264,256]{1,0:T(8,128)S(1)}, u32[]{:S(2)}, u32[]{:S(2)}) collective-permute-start(f32[264,256]{1,0:T(8,128)S(1)} %get-tuple-element.40), channel_id=1, source_target_pairs={{0,3},{1,2},{2,1},{3,0},{4,7},{5,6},{6,5},{7,4},{8,11},{9,10},{10,... | collective-permute-start | bytes 811016 | tf_op jit(solution)/shard_map/ppermute | solution.py:438
  12.3 17.3 %collective-permute-start.7 = (f32[528,256]{1,0:T(8,128)S(1)}, f32[528,256]{1,0:T(8,128)S(1)}, u32[]{:S(2)}, u32[]{:S(2)}) collective-permute-start(f32[528,256]{1,0:T(8,128)S(1)} %shard_map.77.refs_0_), channel_id=1, source_target_pairs={{0,2},{1,3},{2,0},{3,1},{4,6},{5,7},{6,4},{7,5},{8,10},{9,11},{10,... | collective-permute-start | bytes 1622024 | tf_op jit(solution)/shard_map/ppermute | solution.py:438
  18.6 3.1 %collective-permute-start.8 = (f32[264,256]{1,0:T(8,128)S(1)}, f32[264,256]{1,0:T(8,128)S(1)}, u32[]{:S(2)}, u32[]{:S(2)}) collective-permute-start(f32[264,256]{1,0:T(8,128)S(1)} %get-tuple-element.53), channel_id=1, source_target_pairs={{0,1},{1,0},{2,3},{3,2},{4,5},{5,4},{6,7},{7,6},{8,9},{9,8},{10,11... | collective-permute-start | bytes 811016 | tf_op jit(solution)/shard_map/ppermute | solution.py:438
  18.9 4.8 %collective-permute-start.4 = (f32[264,256]{1,0:T(8,128)S(1)}, f32[264,256]{1,0:T(8,128)S(1)}, u32[]{:S(2)}, u32[]{:S(2)}) collective-permute-start(f32[264,256]{1,0:T(8,128)S(1)} %get-tuple-element.48), channel_id=1, source_target_pairs={{0,1},{1,0},{2,3},{3,2},{4,5},{5,4},{6,7},{7,6},{8,9},{9,8},{10,11... | collective-permute-start | bytes 811016 | tf_op jit(solution)/shard_map/ppermute | solution.py:438
  19.2 18.2 %collective-permute-start.10 = (f32[368,256]{1,0:T(8,128)S(1)}, f32[368,256]{1,0:T(8,128)S(1)}, u32[]{:S(2)}, u32[]{:S(2)}) collective-permute-start(f32[368,256]{1,0:T(8,128)S(1)} %get-tuple-element.56), channel_id=1, source_target_pairs={{0,4},{4,0},{8,12},{12,8},{16,20},{20,16},{24,28},{28,24},{1,5},{5... | collective-permute-start | bytes 1130504 | tf_op jit(solution)/shard_map/ppermute | solution.py:518
  21.0 10.5 %collective-permute-start.3 = (f32[352,256]{1,0:T(8,128)S(1)}, f32[352,256]{1,0:T(8,128)S(1)}, u32[]{:S(2)}, u32[]{:S(2)}) collective-permute-start(f32[352,256]{1,0:T(8,128)S(1)} %get-tuple-element.44), channel_id=1, source_target_pairs={{4,8},{8,4},{12,16},{16,12},{20,24},{24,20},{5,9},{9,5},{13,17},{1... | collective-permute-start | bytes 1081352 | tf_op jit(solution)/shard_map/ppermute | solution.py:518
  24.7 13.9 %collective-permute-start.12 = (f32[368,256]{1,0:T(8,128)S(1)}, f32[368,256]{1,0:T(8,128)S(1)}, u32[]{:S(2)}, u32[]{:S(2)}) collective-permute-start(f32[368,256]{1,0:T(8,128)S(1)} %shard_map.82), channel_id=1, source_target_pairs={{0,2},{1,3},{2,0},{3,1},{4,6},{5,7},{6,4},{7,5},{8,10},{9,11},{10,... | collective-permute-start | bytes 1130504 | tf_op jit(solution)/shard_map/ppermute | solution.py:438
  31.4 11.4 %collective-permute-start.14 = (f32[256,256]{1,0:T(8,128)S(1)}, f32[256,256]{1,0:T(8,128)S(1)}, u32[]{:S(2)}, u32[]{:S(2)}) collective-permute-start(f32[256,256]{1,0:T(8,128)S(1)} %get-tuple-element.60), channel_id=1, source_target_pairs={{0,1},{1,0},{2,3},{3,2},{4,5},{5,4},{6,7},{7,6},{8,9},{9,8},{10,11... | collective-permute-start | bytes 786440 | tf_op jit(solution)/shard_map/ppermute | solution.py:438
  32.6 10.3 %copy-start.6 = (bf16[2,128,576]{2,1,0:T(8,128)(2,1)S(1)}, bf16[2,128,576]{2,1,0:T(8,128)(2,1)}, u32[]{:S(2)}) copy-start(bf16[2,128,576]{2,1,0:T(8,128)(2,1)} %constant.13.clone.refs_2_) | copy-start | bytes 884740
  32.6 8.1 %collective-permute-start.13 = (f32[136,256]{1,0:T(8,128)S(1)}, f32[136,256]{1,0:T(8,128)S(1)}, u32[]{:S(2)}, u32[]{:S(2)}) collective-permute-start(f32[136,256]{1,0:T(8,128)S(1)} %get-tuple-element.59), channel_id=1, source_target_pairs={{0,2},{1,3},{2,0},{3,1},{4,6},{5,7},{6,4},{7,5},{8,10},{9,11},{10,... | collective-permute-start | bytes 417800 | tf_op jit(solution)/shard_map/ppermute | solution.py:438
  34.7 8.1 %collective-permute-start.9 = (f32[136,256]{1,0:T(8,128)S(1)}, f32[136,256]{1,0:T(8,128)S(1)}, u32[]{:S(2)}, u32[]{:S(2)}) collective-permute-start(f32[136,256]{1,0:T(8,128)S(1)} %get-tuple-element.55.refs_9_), channel_id=1, source_target_pairs={{0,3},{1,2},{2,1},{3,0},{4,7},{5,6},{6,5},{7,4},{8,11},{9,10},{10,... | collective-permute-start | bytes 417800 | tf_op jit(solution)/shard_map/ppermute | solution.py:438
  38.4 8.3 %collective-permute-start.18 = (f32[256,256]{1,0:T(8,128)S(1)}, f32[256,256]{1,0:T(8,128)S(1)}, u32[]{:S(2)}, u32[]{:S(2)}) collective-permute-start(f32[256,256]{1,0:T(8,128)S(1)} %get-tuple-element.67), channel_id=1, source_target_pairs={{0,1},{1,0},{2,3},{3,2},{4,5},{5,4},{6,7},{7,6},{8,9},{9,8},{10,11... | collective-permute-start | bytes 786440 | tf_op jit(solution)/shard_map/ppermute | solution.py:438
  38.5 8.2 %collective-permute-start.17 = (f32[136,256]{1,0:T(8,128)S(1)}, f32[136,256]{1,0:T(8,128)S(1)}, u32[]{:S(2)}, u32[]{:S(2)}) collective-permute-start(f32[136,256]{1,0:T(8,128)S(1)} %get-tuple-element.66), channel_id=1, source_target_pairs={{0,2},{1,3},{2,0},{3,1},{4,6},{5,7},{6,4},{7,5},{8,10},{9,11},{10,... | collective-permute-start | bytes 417800 | tf_op jit(solution)/shard_map/ppermute | solution.py:438
  40.7 8.3 %collective-permute-start.11 = (f32[136,256]{1,0:T(8,128)S(1)}, f32[136,256]{1,0:T(8,128)S(1)}, u32[]{:S(2)}, u32[]{:S(2)}) collective-permute-start(f32[136,256]{1,0:T(8,128)S(1)} %get-tuple-element.58.refs_3_), channel_id=1, source_target_pairs={{0,3},{1,2},{2,1},{3,0},{4,7},{5,6},{6,5},{7,4},{8,11},{9,10},{10,... | collective-permute-start | bytes 417800 | tf_op jit(solution)/shard_map/ppermute | solution.py:438
  43.3 5.8 %collective-permute-start.15 = (f32[128,256]{1,0:T(8,128)S(1)}, f32[128,256]{1,0:T(8,128)S(1)}, u32[]{:S(2)}, u32[]{:S(2)}) collective-permute-start(f32[128,256]{1,0:T(8,128)S(1)} %get-tuple-element.61), channel_id=1, source_target_pairs={{0,1},{1,0},{2,3},{3,2},{4,5},{5,4},{6,7},{7,6},{8,9},{9,8},{10,11... | collective-permute-start | bytes 393224 | tf_op jit(solution)/shard_map/ppermute | solution.py:438
  44.0 5.1 %collective-permute-start.16 = (f32[128,256]{1,0:T(8,128)S(1)}, f32[128,256]{1,0:T(8,128)S(1)}, u32[]{:S(2)}, u32[]{:S(2)}) collective-permute-start(f32[128,256]{1,0:T(8,128)S(1)} %get-tuple-element.62), channel_id=1, source_target_pairs={{0,1},{1,0},{2,3},{3,2},{4,5},{5,4},{6,7},{7,6},{8,9},{9,8},{10,11... | collective-permute-start | bytes 393224 | tf_op jit(solution)/shard_map/ppermute | solution.py:438
  (2 other events, 10.1 us)

commit v18 on v17

--- a/solution.py
+++ b/solution.py
@@ -119,14 +119,15 @@
         def line(tile, row):
             return held[pl.ds(part * some * pitch + tile * row_count + row, some, stride=pitch), :]
 
-        for job, (out, base, d, rows, offset, tiles) in enumerate(jobs):
+        for job, (out, base, d, rows, offset, tiles, more) in enumerate(jobs):
             first = jnp.bitwise_xor(me, d) * own_tiles + offset
             for i, row in enumerate(rows):
                 at = base + i * cells + part * some
                 for tile in range(tiles):
                     outs[out][at : at + some, tile * LANES : (tile + 1) * LANES] = line(first + tile, row)
-                before = jnp.maximum(first - 1, 0)
-                after = jnp.minimum(first + tiles, all_tiles - 1)
+            before = jnp.maximum(first - 1, 0)
+            after = jnp.minimum(first + tiles, all_tiles - 1)
+            for i, row in enumerate(rows + more if more else ()):
                 for side, (tile, source) in enumerate(((before, LANES - 1), (after, 0))):
                     at = job * 8 + i * 2 + side
                     beside = jnp.where(lane == at, pltpu.roll(line(tile, row), (at - source) % LANES, 1), beside)
@@ -134,7 +135,9 @@
     if cells < LANES:
         sides.append(jnp.zeros((LANES - cells, LANES), jnp.float32))
     turned = jnp.concatenate(sides, axis=0).T
-    for job, (out, base, _, rows, _, tiles) in enumerate(jobs):
+    for job, (out, base, _, rows, _, tiles, more) in enumerate(jobs):
+        if not more:
+            continue
         at = base + len(rows) * cells
         outs[out][at : at + 8, :LANES] = turned[job * 8 : (job + 1) * 8]
         if tiles > 1:
@@ -155,7 +158,7 @@
     return lax.dot_general(table, value, (((1,), (1,)), ((), ())), preferred_element_type=jnp.float32)
 
 
-def transform(rows, cells, near, far, forward_ref):
+def transform(rows, cells, near, far, forward_ref, beside=False):
     def spectrum(lines, lanes, product):
         halves = []
         for parity in (0, 1):
@@ -169,8 +172,9 @@
             halves.append(total)
         return jnp.concatenate(halves, axis=0)
 
-    spectra = [spectrum(slice(i * cells, (i + 1) * cells), slice(None), row_product) for i in range(rows)]
-    return spectra, spectrum(slice(rows * cells, rows * cells + 8), slice(0, cells), side_product)
+    if beside:
+        return spectrum(slice(rows * cells, rows * cells + 8), slice(0, cells), side_product)
+    return [spectrum(slice(i * cells, (i + 1) * cells), slice(None), row_product) for i in range(rows)]
 
 
 def inverse_rows(sweeps, cells, inverse_ref, near, far=()):
@@ -194,7 +198,8 @@
     return (spectrum + above + below + left + right) * inverse_diagonal
 
 
-def masks(mask_ref, rows, d, width):
+def masks(mask_ref, d, width):
+    count = mask_ref.shape[0]
     start = pl.multiple_of(jnp.bitwise_xor(lax.axis_index("span"), d) * width, LANES)
     last = mask_ref.shape[1] - LANES
     before = mask_ref[:, pl.ds(pl.multiple_of(jnp.maximum(start - LANES, 0), LANES), LANES)][:, LANES - 1 :]
@@ -203,7 +208,7 @@
     after = jnp.where(start + width == mask_ref.shape[1], 2, after)
     lane = lax.broadcasted_iota(jnp.int32, (1, 16), 1)
     kinds = jnp.full((1, 16), 2, jnp.int32)
-    for i, row in enumerate(rows):
+    for i, row in enumerate((0, count - 1, *range(1, count - 1))):
         kinds = jnp.where(lane == 2 * i, before[row : row + 1], kinds)
         kinds = jnp.where(lane == 2 * i + 1, after[row : row + 1], kinds)
     return [mask_ref[row : row + 1, pl.ds(start, width)] for row in range(mask_ref.shape[0])], kinds
@@ -226,9 +231,10 @@
     near, far = refs[: count // 2], refs[count // 2 : count]
     forward_ref, columns_ref, mask_ref = refs[count : count + 3]
     spectrum_ref, ones_ref, paired_ref, other_ref, sides_ref = refs[-5:]
-    spectra, sides = transform(len(rows), cells, near, far, forward_ref)
+    spectra = transform(len(rows), cells, near, far, forward_ref)
+    sides = transform(len(rows), cells, near, far, forward_ref, beside=True)
     modes, width = spectra[0].shape
-    mask, kinds = masks(mask_ref, rows, 0, width)
+    mask, kinds = masks(mask_ref, 0, width)
     fluid, solid = one_over(columns_ref, 0, modes)
     ones = [spectrum * pick(mask[row], fluid, solid) for spectrum, row in zip(spectra, rows)]
     for i in (0, 1):
@@ -241,28 +247,27 @@
     sides_ref[...] = sides * pick(kinds, fluid, solid)
 
 
-def inner_sweeps(spectra, sides, rows, mask, kinds, fluid, solid, edges):
+def inner_sweeps(spectra, sides, rows, mask, fluid, solid, edges):
     diagonals = [pick(mask[row], fluid, solid) for row in rows]
     ones = [spectrum * diagonal for spectrum, diagonal in zip(spectra, diagonals)]
     around = [edges[0], *ones, edges[1]]
-    sides = sides * pick(kinds, fluid, solid)
     return ones, [
-        second_sweep(spectra[i], ones[i], around[i], around[i + 2], sides, 2 * i, diagonals[i])
+        second_sweep(spectra[i], ones[i], around[i], around[i + 2], sides, 4 + 2 * i, diagonals[i])
         for i in range(len(rows))
     ]
 
 
 def inner_kernel(rows, count, cells, *refs):
     half = count // 2
-    far_ref, forward_ref, inverse_ref, columns_ref, mask_ref, edges_ref = refs[half : half + 6]
+    far_ref, forward_ref, inverse_ref, columns_ref, mask_ref, edges_ref, sides_ref = refs[half : half + 7]
     outs, ones_ref = refs[-1 - half : -1], refs[-1]
-    size = len(rows) * cells + 8
+    size = len(rows) * cells
     far = [far_ref.at[e * size : (e + 1) * size] for e in range(half)]
-    spectra, sides = transform(len(rows), cells, refs[:half], far, forward_ref)
+    spectra = transform(len(rows), cells, refs[:half], far, forward_ref)
     modes, width = spectra[0].shape
-    mask, kinds = masks(mask_ref, rows, 0, width)
+    mask, _ = masks(mask_ref, 0, width)
     fluid, solid = one_over(columns_ref, 0, modes)
-    ones, sweeps = inner_sweeps(spectra, sides, rows, mask, kinds, fluid, solid, (edges_ref[0], edges_ref[1]))
+    ones, sweeps = inner_sweeps(spectra, sides_ref[...], rows, mask, fluid, solid, (edges_ref[0], edges_ref[1]))
     ones_ref[0] = ones[0]
     ones_ref[1] = ones[-1]
     inverse_rows(sweeps, cells, inverse_ref, outs)
@@ -273,16 +278,17 @@
     message_ref, edges = refs[0], refs[1 : 1 + half]
     forward_ref, inverse_ref, columns_ref, mask_ref = refs[1 + half : 5 + half]
     out_ref = refs[-1]
-    size = len(rows) * cells + 8
+    size = len(rows) * cells
     near = [message_ref.at[d * size : (d + 1) * size] for d in range(half)]
-    spectra, sides = transform(len(rows), cells, near, (), forward_ref)
-    edge_spectra, _ = transform(len(edge_rows), cells, edges, (), forward_ref)
+    spectra = transform(len(rows), cells, near, (), forward_ref)
+    edge_spectra = transform(len(edge_rows), cells, edges, (), forward_ref)
+    sides = transform(len(edge_rows), cells, edges, (), forward_ref, beside=True)
     modes, width = spectra[0].shape
-    mask, kinds = masks(mask_ref, rows, half, width)
+    mask, kinds = masks(mask_ref, half, width)
     fluid, solid = one_over(columns_ref, 0, modes)
     around = [spectrum * pick(mask[row], fluid, solid) for spectrum, row in zip(edge_spectra, edge_rows)]
-    _, sweeps = inner_sweeps(spectra, sides, rows, mask, kinds, fluid, solid, around)
-    size = len(rows) * cells
+    sides = sides * pick(kinds, fluid, solid)
+    _, sweeps = inner_sweeps(spectra, sides, rows, mask, fluid, solid, around)
     inverse_rows(sweeps, cells, inverse_ref, [out_ref.at[d * size : (d + 1) * size] for d in range(half)])
 
 
@@ -300,11 +306,13 @@
 
     spectra = [whole(inner, i) for i in range(len(rows))]
     around = [whole(edges, i) for i in range(len(edge_rows))]
-    sides = product(inner, slice(len(rows) * cells, len(rows) * cells + 8), slice(0, cells), side_product)
-    mask, kinds = masks(mask_ref, rows, 0, inner[0].shape[1])
+    lines = len(edge_rows) * cells
+    sides = product(edges, slice(lines, lines + 8), slice(0, cells), side_product)
+    mask, kinds = masks(mask_ref, 0, inner[0].shape[1])
     fluid, solid = one_over(columns_ref, 2, rest)
     outer = [values[:rest] * pick(mask[row], fluid, solid) for values, row in zip(around, edge_rows)]
-    _, sweeps = inner_sweeps([v[:rest] for v in spectra], sides[:rest], rows, mask, kinds, fluid, solid, outer)
+    outside = sides[:rest] * pick(kinds, fluid, solid)
+    _, sweeps = inner_sweeps([v[:rest] for v in spectra], outside, rows, mask, fluid, solid, outer)
 
     def power(values, at):
         return values[rest + 8 * at : rest + 8 * at + 8]
@@ -322,7 +330,7 @@
         outside = beside(sides, kinds)
         numbers.append(
             [
-                second_sweep(power(spectra[i], target), own[i], column[i], column[i + 2], outside, 2 * i, 1.0)
+                second_sweep(power(spectra[i], target), own[i], column[i], column[i + 2], outside, 4 + 2 * i, 1.0)
                 for i in range(len(rows))
             ]
         )
@@ -359,7 +367,7 @@
     outs = refs[-count:]
     _, modes, width = edges_ref.shape
     edge = 1 - paired_edge() if order == 0 else paired_edge()
-    mask, _ = masks(mask_ref, rows, 0, width)
+    mask, _ = masks(mask_ref, 0, width)
     fluid, solid = one_over(columns_ref, 0, modes)
     sides = jnp.where(edge == 0, sides_ref[:, 0:2], sides_ref[:, 2:4])
     diagonal = pick(jnp.where(edge == 0, mask[rows[0]], mask[rows[1]]), fluid, solid)
@@ -369,21 +377,15 @@
         for d in range(1, count // 2):
             outs[d][cells:, :] = refs[8 + d - 1][...]
     for out in outs[count // 2 :]:
-        out[cells:, :] = jnp.zeros((out.shape[0] - cells, width), jnp.float32)
-
-
-def join_kernel(rows, cells, near, *refs):
-    own_ref, blocks, out_ref = refs[0], refs[1 : 1 + rows * near], refs[-1]
-    size = rows * cells + 8
-    out_ref[:size, :] = own_ref[...]
-    for d in range(near):
-        base = (d + 1) * size
-        out_ref[base + rows * cells : base + size, :] = jnp.zeros((8, out_ref.shape[1]), jnp.float32)
-        for i in range(rows):
-            block = blocks[d * rows + i]
-            out_ref[base + i * cells : base + (i + 1) * cells, :] = block[:cells, :]
-            at = base + rows * cells + 2 * i
-            out_ref[at : at + 2, :] = block[cells : cells + 2, :]
+        if out.shape[0] > cells:
+            out[cells:, :] = jnp.zeros((out.shape[0] - cells, width), jnp.float32)
+
+
+def join_kernel(number, *refs):
+    at = 0
+    for ref in refs[:number]:
+        refs[-1][at : at + ref.shape[0], :] = ref[...]
+        at += ref.shape[0]
 
 
 def copy_kernel(number, *refs):
@@ -395,9 +397,15 @@
     me = lax.axis_index("span")
     blocks, (out_ref, held, done) = refs[: len(pieces)], refs[-3:]
     pitch = held.shape[0] // cells
-    own_lines = out_ref.shape[1] // lax.axis_size("span")
+    lines = out_ref.shape[1]
+    own_lines = lines // lax.axis_size("span")
+    whole = len(devices) > 1
     some = cells // SPLIT
     edge_rows = {"near": paired_edge() * (row_count - 1), "far": (1 - paired_edge()) * (row_count - 1)}
+
+    def first_line(d):
+        return pl.multiple_of(jnp.bitwise_xor(me, d) * own_lines, own_lines)
+
     copies = []
     for part in range(SPLIT):
         for block, (d, base, rows, offset, tiles) in zip(blocks, pieces):
@@ -406,18 +414,22 @@
                     row = edge_rows[row]
                 line = base + i * cells + part * some
                 for tile in range(tiles):
-                    at = part * some * pitch + devices.index(d) * own_lines + (offset + tile) * row_count + row
+                    at = part * some * pitch + (first_line(d) if whole else 0) + (offset + tile) * row_count + row
                     held[pl.ds(at, some, stride=pitch), :] = block[line : line + some, tile * LANES : (tile + 1) * LANES]
-        for at, d in enumerate(devices):
-            first = pl.multiple_of(jnp.bitwise_xor(me, d) * own_lines, own_lines)
-            copies.append(
-                pltpu.make_async_copy(
-                    held.reshape(cells, pitch, LANES).at[pl.ds(part * some, some), pl.ds(at * own_lines, own_lines)],
-                    out_ref.at[pl.ds(part * some, some), pl.ds(first, own_lines)],
-                    done.at[part, at],
-                )
+        if whole:
+            for d in set(range(lax.axis_size("span"))) - set(devices):
+                for line in range(own_lines):
+                    at = part * some * pitch + first_line(d) + line
+                    held[pl.ds(at, some, stride=pitch), :] = jnp.zeros((some, LANES), jnp.float32)
+        wanted = pl.ds(0, lines) if whole else pl.ds(first_line(devices[0]), own_lines)
+        copies.append(
+            pltpu.make_async_copy(
+                held.reshape(cells, pitch, LANES).at[pl.ds(part * some, some), pl.ds(0, lines if whole else own_lines)],
+                out_ref.at[pl.ds(part * some, some), wanted],
+                done.at[part],
             )
-            copies[-1].start()
+        )
+        copies[-1].start()
     for copy in copies:
         copy.wait()
 
@@ -457,8 +469,8 @@
     scratch = [pltpu.VMEM((cells * (lines + 8), LANES), jnp.float32), pltpu.SemaphoreType.DMA((SPLIT,))]
 
     def pack(source, wanted, *earlier):
-        jobs = [(at, 0, d, rows, 0, tiles) for at, (d, rows) in enumerate(wanted)]
-        shapes = [(len(rows) * cells + 8, width) for _, rows in wanted]
+        jobs = [(at, 0, d, rows, 0, tiles, inner if rows == edges else ()) for at, (d, rows) in enumerate(wanted)]
+        shapes = [(len(rows) * cells + (8 if rows == edges else 0), width) for _, rows in wanted]
         return pl.pallas_call(
             functools.partial(pack_kernel, jobs, row_count, cells, len(earlier)),
             out_shape=[jax.ShapeDtypeStruct(shape, jnp.float32) for shape in shapes],
@@ -477,10 +489,9 @@
     edge_blocks = [packed[half + 1], *edge_blocks]
     relayed = packed[2 * half + 2 :]
     relayed = [swap(relayed[(d - 1) * len(inner) + i], d) for d in near for i in range(len(inner))]
-    size = len(inner) * cells + 8
     (message,) = call(
-        functools.partial(join_kernel, len(inner), cells, half - 1),
-        [(half * size, width)],
+        functools.partial(join_kernel, 1 + len(relayed)),
+        [(half * len(inner) * cells, width)],
         packed[half], *relayed, cost=SHORT, earlier=(edge_blocks[half],),
     )
     arrived = swap(message, half)
@@ -519,7 +530,8 @@
     *made, ones = call(
         functools.partial(inner_kernel, inner, count, cells),
         [(length, width)] * half + [(2, modes, width)],
-        *inner_blocks, arrived, forward, inverse, diagonals, solid_mask, edge_ones, cost=SHORT, earlier=(own,),
+        *inner_blocks, arrived, forward, inverse, diagonals, solid_mask, edge_ones, sides,
+        cost=SHORT, earlier=(own,),
     )
     pieces = [(made[0], 0, 0, inner, 0, tiles)]
     made_got = [swap(made[d], d) for d in near]
@@ -528,7 +540,7 @@
     for order, name in enumerate(("far", "near")):
         outs = call(
             functools.partial(rim_kernel, edges, order, count, cells),
-            [(cells, width)] + [((order + 1) * cells, width)] * (half - 1) + [(cells + 8, width)] * half,
+            [(cells, width)] + [((order + 1) * cells, width)] * (half - 1) + [(cells + 8 * (1 - order), width)] * half,
             spectrum, edge_ones, sides, halos[1 - order], ones, inverse, diagonals, solid_mask, *near_rim,
             cost=LONG if order else SHORT, earlier=earlier,
         )
@@ -560,8 +572,8 @@
             in_specs=[VMEM] * len(chosen) + [ANY] * len(previous),
             out_specs=ANY,
             scratch_shapes=[
-                pltpu.VMEM((cells * (len(devices) * own_lines + 8), LANES), jnp.float32),
-                pltpu.SemaphoreType.DMA((SPLIT, len(devices))),
+                pltpu.VMEM((cells * ((lines if len(devices) > 1 else own_lines) + 8), LANES), jnp.float32),
+                pltpu.SemaphoreType.DMA((SPLIT,)),
             ],
             input_output_aliases={len(chosen): 0} if previous else {},
             compiler_params=PARAMS,

time: 50.2 us -> 49.6 us (0.988)
  the two profiles are of different devices: /device:TPU:0 before, /device:TPU:25 now
where the time goes in v18:
time: 49.6 us; the launch traced here: 48.8 us
  starting transfers between devices  19.2 us (39%)
  waiting for transfers between devices  15.7 us (32%)
  Pallas kernels  13.7 us (28%)
    ppermute x17, starting transfers between devices, swap(): lax.ppermute(block, 'span', [(i, i ^ d) for i in range(lax.axis_size('spa...  15.9 us
    ppermute x17, waiting for transfers between devices, swap(): lax.ppermute(block, 'span', [(i, i ^ d) for i in range(lax.axis_size('spa...  12.6 us
    pallas_call x9, Pallas kernels, call(): pl.pallas_call(kernel, out_shape=shapes, in_specs=[VMEM] * len(args) + [A...  8.11 us
    pallas_call x2, Pallas kernels, pack(): pl.pallas_call(functools.partial(pack_kernel, jobs, row_count, cells, len...  3.27 us
    ppermute x2, starting transfers between devices, local(): lax.ppermute(row, 'plane', pair)  3.26 us
    ppermute x2, waiting for transfers between devices, local(): lax.ppermute(row, 'plane', pair)  3.09 us
    pallas_call x2, Pallas kernels, local(): pl.pallas_call(functools.partial(unpack_kernel, [piece[1:] for piece in c...  2.35 us
  transfers between devices with their start and end apart: 19, of which 9 were waited for; matrix products, arithmetic and copies ran while one was open for 0% of the time, Pallas kernels for 22%

profile of v18, /device:TPU:25, one launch (start us, length us, event | category | flops | bytes accessed | tf_op | source)
XLA Modules:
  0.0 48.8 jit_solution(15946740594857749265)
XLA Ops:
  0.0 2.1 %shard_map.73 = (f32[264,256]{1,0:T(8,128)S(1)}, f32[264,256]{1,0:T(8,128)S(1)}, f32[264,256]{1,0:T(8,128)S(1)}) custom-call(f32[128,32,128]{2,1,0:T(8,128)} %bitcast.10), custom_call_target="tpu_custom_call" | custom-call | bytes 200000000 | tf_op jit(solution)/shard_map/pallas_call | solution.py:474
  2.1 1.3 %collective-permute-start.1 = (f32[264,256]{1,0:T(8,128)S(1)}, f32[264,256]{1,0:T(8,128)S(1)}, u32[]{:S(2)}, u32[]{:S(2)}) collective-permute-start(f32[264,256]{1,0:T(8,128)S(1)} %get-tuple-element.37.refs_0_), channel_id=1, source_target_pairs={{0,2},{1,3},{2,0},{3,1},{4,6},{5,7},{6,4},{7,5},{8,10},{9,11},{10,... | collective-permute-start | bytes 811016 | tf_op jit(solution)/shard_map/ppermute | solution.py:450
  3.4 1.0 %collective-permute-start = (f32[264,256]{1,0:T(8,128)S(1)}, f32[264,256]{1,0:T(8,128)S(1)}, u32[]{:S(2)}, u32[]{:S(2)}) collective-permute-start(f32[264,256]{1,0:T(8,128)S(1)} %get-tuple-element.39), channel_id=1, source_target_pairs={{0,1},{1,0},{2,3},{3,2},{4,5},{5,4},{6,7},{7,6},{8,9},{9,8},{10,11... | collective-permute-start | bytes 811016 | tf_op jit(solution)/shard_map/ppermute | solution.py:450
  4.5 1.2 %shard_map.74 = (f32[256,256]{1,0:T(8,128)S(1)}, f32[256,256]{1,0:T(8,128)S(1)}, f32[256,256]{1,0:T(8,128)S(1)}, f32[264,256]{1,0:T(8,128)S(1)}, f32[264,256]{1,...) custom-call(f32[128,32,128]{2,1,0:T(8,128)S(1)} %bitcast.11, ...), custom_call_target="tpu_custom_call" | custom-call | bytes 200000000 | tf_op jit(solution)/shard_map/pallas_call | solution.py:474
  7.6 1.9 %collective-permute-done.1.refs_2_.refs_3_ = f32[264,256]{1,0:T(8,128)S(1)} collective-permute-done((f32[264,256]{1,0:T(8,128)S(1)}, f32[264,256]{1,0:T(8,128)S(1)}, u32[]{:S(2)}, u32[]{:S(2)}) %collective-permute-start.1) | collective-permute-done | bytes 270368 | tf_op jit(solution)/shard_map/ppermute | solution.py:450
  9.6 1.3 %collective-permute-start.7 = (f32[512,256]{1,0:T(8,128)S(1)}, f32[512,256]{1,0:T(8,128)S(1)}, u32[]{:S(2)}, u32[]{:S(2)}) collective-permute-start(f32[512,256]{1,0:T(8,128)S(1)} %shard_map.77.refs_0_), channel_id=1, source_target_pairs={{0,2},{1,3},{2,0},{3,1},{4,6},{5,7},{6,4},{7,5},{8,10},{9,11},{10,... | collective-permute-start | bytes 1572872 | tf_op jit(solution)/shard_map/ppermute | solution.py:450
  10.9 6.5 %collective-permute-done.2.refs_3_ = f32[264,256]{1,0:T(8,128)S(1)} collective-permute-done((f32[264,256]{1,0:T(8,128)S(1)}, f32[264,256]{1,0:T(8,128)S(1)}, u32[]{:S(2)}, u32[]{:S(2)}) %collective-permute-start.2) | collective-permute-done | bytes 270368 | tf_op jit(solution)/shard_map/ppermute | solution.py:450
  18.9 1.2 %collective-permute-start.10 = (f32[368,256]{1,0:T(8,128)S(1)}, f32[368,256]{1,0:T(8,128)S(1)}, u32[]{:S(2)}, u32[]{:S(2)}) collective-permute-start(f32[368,256]{1,0:T(8,128)S(1)} %get-tuple-element.56), channel_id=1, source_target_pairs={{0,4},{4,0},{8,12},{12,8},{16,20},{20,16},{24,28},{28,24},{1,5},{5... | collective-permute-start | bytes 1130504 | tf_op jit(solution)/shard_map/ppermute | solution.py:529
  20.1 2.0 %collective-permute-start.3 = (f32[352,256]{1,0:T(8,128)S(1)}, f32[352,256]{1,0:T(8,128)S(1)}, u32[]{:S(2)}, u32[]{:S(2)}) collective-permute-start(f32[352,256]{1,0:T(8,128)S(1)} %get-tuple-element.44), channel_id=1, source_target_pairs={{4,8},{8,4},{12,16},{16,12},{20,24},{24,20},{5,9},{9,5},{13,17},{1... | collective-permute-start | bytes 1081352 | tf_op jit(solution)/shard_map/ppermute | solution.py:529
  22.1 2.1 %shard_map.78.refs_9_.refs_7_.refs_1_ = f32[512,256]{1,0:T(8,128)S(1)} custom-call(f32[512,256]{1,0:T(8,128)S(1)} %shard_map.77.refs_0_, f32[264,256]{1,0:T(8,128)S(1)} %get-tuple-element.52.refs_1_, f32[264,256]{1,0:T(8,128)S(1)} %collective-permute-done.8.refs_2_, bf16[2,2,176,384]{3,2,1,0:T(8,128)(2,1)S(1)} %copy-done.2, ...), custom_call_target="tpu_custom_call" | custom-call | bytes 1024 | tf_op jit(solution)/shard_map/pallas_call | solution.py:439
  24.3 1.0 %shard_map.82 = f32[368,256]{1,0:T(8,128)S(1)} custom-call(f32[256,256]{1,0:T(8,128)S(1)} %get-tuple-element.45.refs_0_, f32[256,256]{1,0:T(8,128)S(1)} %collective-permute-done.4.refs_1_, f32[264,256]{1,0:T(8,128)S(1)} %get-tuple-element.38.refs_0_.refs_2_, f32[264,256]{1,0:T(8,128)S(1)} %collective-permute-done.refs_1_.refs_3_, ...), custom_call_target="tpu_custom_call" | custom-call | bytes 1024 | tf_op jit(solution)/shard_map/pallas_call | solution.py:439
  25.2 1.3 %collective-permute-start.12 = (f32[368,256]{1,0:T(8,128)S(1)}, f32[368,256]{1,0:T(8,128)S(1)}, u32[]{:S(2)}, u32[]{:S(2)}) collective-permute-start(f32[368,256]{1,0:T(8,128)S(1)} %shard_map.82), channel_id=1, source_target_pairs={{0,2},{1,3},{2,0},{3,1},{4,6},{5,7},{6,4},{7,5},{8,10},{9,11},{10,... | collective-permute-start | bytes 1130504 | tf_op jit(solution)/shard_map/ppermute | solution.py:450
  26.6 1.6 %shard_map.79 = (f32[256,256]{1,0:T(8,128)S(1)}, f32[256,256]{1,0:T(8,128)S(1)}, f32[2,352,256]{2,1,0:T(8,128)S(1)}) custom-call(f32[256,256]{1,0:T(8,128)S(1)} %get-tuple-element.45.refs_0_, f32[256,256]{1,0:T(8,128)S(1)} %collective-permute-done.4.refs_1_, f32[512,256]{1,0:T(8,128)S(1)} %collective-permute-done.7.refs_2_, ...), custom_call_target="tpu_custom_call" | custom-call | bytes 1024 | tf_op jit(solution)/shard_map/pallas_call | solution.py:439
  28.2 1.6 %collective-permute-start.14 = (f32[256,256]{1,0:T(8,128)S(1)}, f32[256,256]{1,0:T(8,128)S(1)}, u32[]{:S(2)}, u32[]{:S(2)}) collective-permute-start(f32[256,256]{1,0:T(8,128)S(1)} %get-tuple-element.60), channel_id=1, source_target_pairs={{0,1},{1,0},{2,3},{3,2},{4,5},{5,4},{6,7},{7,6},{8,9},{9,8},{10,11... | collective-permute-start | bytes 786440 | tf_op jit(solution)/shard_map/ppermute | solution.py:450
  29.8 2.7 %collective-permute-done.3.refs_3_ = f32[352,256]{1,0:T(8,128)S(1)} collective-permute-done((f32[352,256]{1,0:T(8,128)S(1)}, f32[352,256]{1,0:T(8,128)S(1)}, u32[]{:S(2)}, u32[]{:S(2)}) %collective-permute-start.3) | collective-permute-done | bytes 360480 | tf_op jit(solution)/shard_map/ppermute | solution.py:529
  32.6 1.1 %shard_map.80 = (f32[128,256]{1,0:T(8,128)S(1)}, f32[128,256]{1,0:T(8,128)S(1)}, f32[136,256]{1,0:T(8,128)S(1)}, f32[136,256]{1,0:T(8,128)S(1)}) custom-call(f32[2,352,256]{2,1,0:T(8,128)S(1)} %get-tuple-element.41.refs_0_, f32[2,352,256]{2,1,0:T(8,128)S(1)} %get-tuple-element.42.refs_7_.refs_1_, f32[352,16]{1,0:T(8,128)S(1)} %get-tuple-element.43.refs_2_.refs_8_, ...), custom_call_target="tpu_custom_call" | custom-call | bytes 1024 | tf_op jit(solution)/shard_map/pallas_call | solution.py:439
  33.6 1.3 %collective-permute-start.13 = (f32[136,256]{1,0:T(8,128)S(1)}, f32[136,256]{1,0:T(8,128)S(1)}, u32[]{:S(2)}, u32[]{:S(2)}) collective-permute-start(f32[136,256]{1,0:T(8,128)S(1)} %get-tuple-element.59), channel_id=1, source_target_pairs={{0,2},{1,3},{2,0},{3,1},{4,6},{5,7},{6,4},{7,5},{8,10},{9,11},{10,... | collective-permute-start | bytes 417800 | tf_op jit(solution)/shard_map/ppermute | solution.py:450
  34.9 1.6 %collective-permute-start.9 = (f32[136,256]{1,0:T(8,128)S(1)}, f32[136,256]{1,0:T(8,128)S(1)}, u32[]{:S(2)}, u32[]{:S(2)}) collective-permute-start(f32[136,256]{1,0:T(8,128)S(1)} %get-tuple-element.55.refs_9_), channel_id=1, source_target_pairs={{0,3},{1,2},{2,1},{3,0},{4,7},{5,6},{6,5},{7,4},{8,11},{9,10},{10,... | collective-permute-start | bytes 417800 | tf_op jit(solution)/shard_map/ppermute | solution.py:450
  36.9 1.1 %shard_map.81 = (f32[128,256]{1,0:T(8,128)S(1)}, f32[256,256]{1,0:T(8,128)S(1)}, f32[128,256]{1,0:T(8,128)S(1)}, f32[128,256]{1,0:T(8,128)S(1)}) custom-call(f32[2,352,256]{2,1,0:T(8,128)S(1)} %get-tuple-element.41.refs_0_, f32[2,352,256]{2,1,0:T(8,128)S(1)} %get-tuple-element.42.refs_7_.refs_1_, f32[352,16]{1,0:T(8,128)S(1)} %get-tuple-element.43.refs_2_.refs_8_, ...), custom_call_target="tpu_custom_call" | custom-call | bytes 200000000 | tf_op jit(solution)/shard_map/pallas_call | solution.py:439
  38.9 1.2 %collective-permute-start.17 = (f32[128,256]{1,0:T(8,128)S(1)}, f32[128,256]{1,0:T(8,128)S(1)}, u32[]{:S(2)}, u32[]{:S(2)}) collective-permute-start(f32[128,256]{1,0:T(8,128)S(1)} %get-tuple-element.66), channel_id=1, source_target_pairs={{0,2},{1,3},{2,0},{3,1},{4,6},{5,7},{6,4},{7,5},{8,10},{9,11},{10,... | collective-permute-start | bytes 393224 | tf_op jit(solution)/shard_map/ppermute | solution.py:450
  40.2 2.4 %collective-permute-start.11 = (f32[128,256]{1,0:T(8,128)S(1)}, f32[128,256]{1,0:T(8,128)S(1)}, u32[]{:S(2)}, u32[]{:S(2)}) collective-permute-start(f32[128,256]{1,0:T(8,128)S(1)} %get-tuple-element.58.refs_3_), channel_id=1, source_target_pairs={{0,3},{1,2},{2,1},{3,0},{4,7},{5,6},{6,5},{7,4},{8,11},{9,10},{10,... | collective-permute-start | bytes 393224 | tf_op jit(solution)/shard_map/ppermute | solution.py:450
  43.8 1.0 %collective-permute-done.17.refs_5_ = f32[128,256]{1,0:T(8,128)S(1)} collective-permute-done((f32[128,256]{1,0:T(8,128)S(1)}, f32[128,256]{1,0:T(8,128)S(1)}, u32[]{:S(2)}, u32[]{:S(2)}) %collective-permute-start.17) | collective-permute-done | bytes 131104 | tf_op jit(solution)/shard_map/ppermute | solution.py:450
  44.8 1.4 %shard_map.84.refs_4_ = f32[128,32,128]{2,1,0:T(8,128)} custom-call(f32[256,256]{1,0:T(8,128)S(1)} %get-tuple-element.63.refs_0_, f32[256,256]{1,0:T(8,128)S(1)} %collective-permute-done.14.refs_6_.refs_1_, f32[128,256]{1,0:T(8,128)S(1)} %get-tuple-element.64.refs_2_, f32[136,256]{1,0:T(8,128)S(1)} %collective-permute-done.13.refs_4_.refs_3_, ...), custom_call_target="tpu_custom_call" | custom-call | bytes 200000000 | tf_op jit(solution)/shard_map/pallas_call | solution.py:569
  46.3 1.6 %collective-permute-done.11.refs_1_ = f32[128,256]{1,0:T(8,128)S(1)} collective-permute-done((f32[128,256]{1,0:T(8,128)S(1)}, f32[128,256]{1,0:T(8,128)S(1)}, u32[]{:S(2)}, u32[]{:S(2)}) %collective-permute-start.11) | collective-permute-done | bytes 131104 | tf_op jit(solution)/shard_map/ppermute | solution.py:450
  (41 shorter events, 7.0 us)
Async XLA Ops:
  2.1 15.3 %copy-start.2 = (bf16[2,2,176,384]{3,2,1,0:T(8,128)(2,1)S(1)}, bf16[2,2,176,384]{3,2,1,0:T(8,128)(2,1)}, u32[]{:S(2)}) copy-start(bf16[2,2,176,384]{3,2,1,0:T(8,128)(2,1)} %constant.10.clone.refs_4_.refs_3_) | copy-start | bytes 1622020
  2.1 15.2 %copy-start.3 = (s32[4,1024]{1,0:T(4,128)S(1)}, s32[4,1024]{1,0:T(4,128)}, u32[]{:S(2)}) copy-start(s32[4,1024]{1,0:T(4,128)} %refs_6_.9) | copy-start | bytes 49156
  2.1 15.2 %copy-start.4 = (f32[8,384]{1,0:T(8,128)S(1)}, f32[8,384]{1,0:T(8,128)}, u32[]{:S(2)}) copy-start(f32[8,384]{1,0:T(8,128)} %constant.14.clone.refs_5_.refs_6_) | copy-start | bytes 36868
  2.1 7.4 %collective-permute-start.1 = (f32[264,256]{1,0:T(8,128)S(1)}, f32[264,256]{1,0:T(8,128)S(1)}, u32[]{:S(2)}, u32[]{:S(2)}) collective-permute-start(f32[264,256]{1,0:T(8,128)S(1)} %get-tuple-element.37.refs_0_), channel_id=1, source_target_pairs={{0,2},{1,3},{2,0},{3,1},{4,6},{5,7},{6,4},{7,5},{8,10},{9,11},{10,... | collective-permute-start | bytes 811016 | tf_op jit(solution)/shard_map/ppermute | solution.py:450
  3.4 7.5 %collective-permute-start = (f32[264,256]{1,0:T(8,128)S(1)}, f32[264,256]{1,0:T(8,128)S(1)}, u32[]{:S(2)}, u32[]{:S(2)}) collective-permute-start(f32[264,256]{1,0:T(8,128)S(1)} %get-tuple-element.39), channel_id=1, source_target_pairs={{0,1},{1,0},{2,3},{3,2},{4,5},{5,4},{6,7},{7,6},{8,9},{9,8},{10,11... | collective-permute-start | bytes 811016 | tf_op jit(solution)/shard_map/ppermute | solution.py:450
  4.4 13.0 %collective-permute-start.2 = (f32[264,256]{1,0:T(8,128)S(1)}, f32[264,256]{1,0:T(8,128)S(1)}, u32[]{:S(2)}, u32[]{:S(2)}) collective-permute-start(f32[264,256]{1,0:T(8,128)S(1)} %get-tuple-element.40), channel_id=1, source_target_pairs={{0,3},{1,2},{2,1},{3,0},{4,7},{5,6},{6,5},{7,4},{8,11},{9,10},{10,... | collective-permute-start | bytes 811016 | tf_op jit(solution)/shard_map/ppermute | solution.py:450
  5.7 16.4 %copy-start = (bf16[2,2,128,528]{3,2,1,0:T(8,128)(2,1)S(1)}, bf16[2,2,128,528]{3,2,1,0:T(8,128)(2,1)}, u32[]{:S(2)}) copy-start(bf16[2,2,128,528]{3,2,1,0:T(8,128)(2,1)} %constant.11.clone.refs_4_.refs_5_) | copy-start | bytes 1622020
  5.7 1.6 %collective-permute-start.5 = (f32[128,256]{1,0:T(8,128)S(1)}, f32[128,256]{1,0:T(8,128)S(1)}, u32[]{:S(2)}, u32[]{:S(2)}) collective-permute-start(f32[128,256]{1,0:T(8,128)S(1)} %get-tuple-element.50), channel_id=1, source_target_pairs={{0,1},{1,0},{2,3},{3,2},{4,5},{5,4},{6,7},{7,6},{8,9},{9,8},{10,11... | collective-permute-start | bytes 393224 | tf_op jit(solution)/shard_map/ppermute | solution.py:450
  6.3 1.3 %collective-permute-start.6 = (f32[128,256]{1,0:T(8,128)S(1)}, f32[128,256]{1,0:T(8,128)S(1)}, u32[]{:S(2)}, u32[]{:S(2)}) collective-permute-start(f32[128,256]{1,0:T(8,128)S(1)} %get-tuple-element.51), channel_id=1, source_target_pairs={{0,1},{1,0},{2,3},{3,2},{4,5},{5,4},{6,7},{7,6},{8,9},{9,8},{10,11... | collective-permute-start | bytes 393224 | tf_op jit(solution)/shard_map/ppermute | solution.py:450
  9.6 17.0 %collective-permute-start.7 = (f32[512,256]{1,0:T(8,128)S(1)}, f32[512,256]{1,0:T(8,128)S(1)}, u32[]{:S(2)}, u32[]{:S(2)}) collective-permute-start(f32[512,256]{1,0:T(8,128)S(1)} %shard_map.77.refs_0_), channel_id=1, source_target_pairs={{0,2},{1,3},{2,0},{3,1},{4,6},{5,7},{6,4},{7,5},{8,10},{9,11},{10,... | collective-permute-start | bytes 1572872 | tf_op jit(solution)/shard_map/ppermute | solution.py:450
  18.3 3.8 %collective-permute-start.8 = (f32[264,256]{1,0:T(8,128)S(1)}, f32[264,256]{1,0:T(8,128)S(1)}, u32[]{:S(2)}, u32[]{:S(2)}) collective-permute-start(f32[264,256]{1,0:T(8,128)S(1)} %get-tuple-element.53), channel_id=1, source_target_pairs={{0,1},{1,0},{2,3},{3,2},{4,5},{5,4},{6,7},{7,6},{8,9},{9,8},{10,11... | collective-permute-start | bytes 811016 | tf_op jit(solution)/shard_map/ppermute | solution.py:450
  18.4 5.9 %collective-permute-start.4 = (f32[256,256]{1,0:T(8,128)S(1)}, f32[256,256]{1,0:T(8,128)S(1)}, u32[]{:S(2)}, u32[]{:S(2)}) collective-permute-start(f32[256,256]{1,0:T(8,128)S(1)} %get-tuple-element.48), channel_id=1, source_target_pairs={{0,1},{1,0},{2,3},{3,2},{4,5},{5,4},{6,7},{7,6},{8,9},{9,8},{10,11... | collective-permute-start | bytes 786440 | tf_op jit(solution)/shard_map/ppermute | solution.py:450
  18.9 18.1 %collective-permute-start.10 = (f32[368,256]{1,0:T(8,128)S(1)}, f32[368,256]{1,0:T(8,128)S(1)}, u32[]{:S(2)}, u32[]{:S(2)}) collective-permute-start(f32[368,256]{1,0:T(8,128)S(1)} %get-tuple-element.56), channel_id=1, source_target_pairs={{0,4},{4,0},{8,12},{12,8},{16,20},{20,16},{24,28},{28,24},{1,5},{5... | collective-permute-start | bytes 1130504 | tf_op jit(solution)/shard_map/ppermute | solution.py:529
  20.1 12.5 %collective-permute-start.3 = (f32[352,256]{1,0:T(8,128)S(1)}, f32[352,256]{1,0:T(8,128)S(1)}, u32[]{:S(2)}, u32[]{:S(2)}) collective-permute-start(f32[352,256]{1,0:T(8,128)S(1)} %get-tuple-element.44), channel_id=1, source_target_pairs={{4,8},{8,4},{12,16},{16,12},{20,24},{24,20},{5,9},{9,5},{13,17},{1... | collective-permute-start | bytes 1081352 | tf_op jit(solution)/shard_map/ppermute | solution.py:529
  25.2 13.7 %collective-permute-start.12 = (f32[368,256]{1,0:T(8,128)S(1)}, f32[368,256]{1,0:T(8,128)S(1)}, u32[]{:S(2)}, u32[]{:S(2)}) collective-permute-start(f32[368,256]{1,0:T(8,128)S(1)} %shard_map.82), channel_id=1, source_target_pairs={{0,2},{1,3},{2,0},{3,1},{4,6},{5,7},{6,4},{7,5},{8,10},{9,11},{10,... | collective-permute-start | bytes 1130504 | tf_op jit(solution)/shard_map/ppermute | solution.py:450
  28.2 14.7 %collective-permute-start.14 = (f32[256,256]{1,0:T(8,128)S(1)}, f32[256,256]{1,0:T(8,128)S(1)}, u32[]{:S(2)}, u32[]{:S(2)}) collective-permute-start(f32[256,256]{1,0:T(8,128)S(1)} %get-tuple-element.60), channel_id=1, source_target_pairs={{0,1},{1,0},{2,3},{3,2},{4,5},{5,4},{6,7},{7,6},{8,9},{9,8},{10,11... | collective-permute-start | bytes 786440 | tf_op jit(solution)/shard_map/ppermute | solution.py:450
  33.6 9.2 %copy-start.6 = (bf16[2,128,576]{2,1,0:T(8,128)(2,1)S(1)}, bf16[2,128,576]{2,1,0:T(8,128)(2,1)}, u32[]{:S(2)}) copy-start(bf16[2,128,576]{2,1,0:T(8,128)(2,1)} %constant.13.clone.refs_2_) | copy-start | bytes 884740
  33.6 6.5 %collective-permute-start.13 = (f32[136,256]{1,0:T(8,128)S(1)}, f32[136,256]{1,0:T(8,128)S(1)}, u32[]{:S(2)}, u32[]{:S(2)}) collective-permute-start(f32[136,256]{1,0:T(8,128)S(1)} %get-tuple-element.59), channel_id=1, source_target_pairs={{0,2},{1,3},{2,0},{3,1},{4,6},{5,7},{6,4},{7,5},{8,10},{9,11},{10,... | collective-permute-start | bytes 417800 | tf_op jit(solution)/shard_map/ppermute | solution.py:450
  34.9 7.9 %collective-permute-start.9 = (f32[136,256]{1,0:T(8,128)S(1)}, f32[136,256]{1,0:T(8,128)S(1)}, u32[]{:S(2)}, u32[]{:S(2)}) collective-permute-start(f32[136,256]{1,0:T(8,128)S(1)} %get-tuple-element.55.refs_9_), channel_id=1, source_target_pairs={{0,3},{1,2},{2,1},{3,0},{4,7},{5,6},{6,5},{7,4},{8,11},{9,10},{10,... | collective-permute-start | bytes 417800 | tf_op jit(solution)/shard_map/ppermute | solution.py:450
  38.0 6.8 %collective-permute-start.18 = (f32[256,256]{1,0:T(8,128)S(1)}, f32[256,256]{1,0:T(8,128)S(1)}, u32[]{:S(2)}, u32[]{:S(2)}) collective-permute-start(f32[256,256]{1,0:T(8,128)S(1)} %get-tuple-element.67), channel_id=1, source_target_pairs={{0,1},{1,0},{2,3},{3,2},{4,5},{5,4},{6,7},{7,6},{8,9},{9,8},{10,11... | collective-permute-start | bytes 786440 | tf_op jit(solution)/shard_map/ppermute | solution.py:450
  38.9 5.9 %collective-permute-start.17 = (f32[128,256]{1,0:T(8,128)S(1)}, f32[128,256]{1,0:T(8,128)S(1)}, u32[]{:S(2)}, u32[]{:S(2)}) collective-permute-start(f32[128,256]{1,0:T(8,128)S(1)} %get-tuple-element.66), channel_id=1, source_target_pairs={{0,2},{1,3},{2,0},{3,1},{4,6},{5,7},{6,4},{7,5},{8,10},{9,11},{10,... | collective-permute-start | bytes 393224 | tf_op jit(solution)/shard_map/ppermute | solution.py:450
  40.2 7.7 %collective-permute-start.11 = (f32[128,256]{1,0:T(8,128)S(1)}, f32[128,256]{1,0:T(8,128)S(1)}, u32[]{:S(2)}, u32[]{:S(2)}) collective-permute-start(f32[128,256]{1,0:T(8,128)S(1)} %get-tuple-element.58.refs_3_), channel_id=1, source_target_pairs={{0,3},{1,2},{2,1},{3,0},{4,7},{5,6},{6,5},{7,4},{8,11},{9,10},{10,... | collective-permute-start | bytes 393224 | tf_op jit(solution)/shard_map/ppermute | solution.py:450
  43.2 4.7 %collective-permute-start.15 = (f32[128,256]{1,0:T(8,128)S(1)}, f32[128,256]{1,0:T(8,128)S(1)}, u32[]{:S(2)}, u32[]{:S(2)}) collective-permute-start(f32[128,256]{1,0:T(8,128)S(1)} %get-tuple-element.61), channel_id=1, source_target_pairs={{0,1},{1,0},{2,3},{3,2},{4,5},{5,4},{6,7},{7,6},{8,9},{9,8},{10,11... | collective-permute-start | bytes 393224 | tf_op jit(solution)/shard_map/ppermute | solution.py:450
  43.3 4.6 %collective-permute-start.16 = (f32[128,256]{1,0:T(8,128)S(1)}, f32[128,256]{1,0:T(8,128)S(1)}, u32[]{:S(2)}, u32[]{:S(2)}) collective-permute-start(f32[128,256]{1,0:T(8,128)S(1)} %get-tuple-element.62), channel_id=1, source_target_pairs={{0,1},{1,0},{2,3},{3,2},{4,5},{5,4},{6,7},{7,6},{8,9},{9,8},{10,11... | collective-permute-start | bytes 393224 | tf_op jit(solution)/shard_map/ppermute | solution.py:450
  (2 other events, 10.5 us)

commit v19 on v18

--- a/solution.py
+++ b/solution.py
@@ -393,19 +393,17 @@
         out[...] = ref[...]
 
 
-def unpack_kernel(pieces, devices, row_count, cells, *refs):
+def unpack_kernel(pieces, row_count, cells, *refs):
     me = lax.axis_index("span")
     blocks, (out_ref, held, done) = refs[: len(pieces)], refs[-3:]
     pitch = held.shape[0] // cells
-    lines = out_ref.shape[1]
-    own_lines = lines // lax.axis_size("span")
-    whole = len(devices) > 1
+    count = lax.axis_size("span")
+    own_lines = out_ref.shape[1] // count
+    lines = own_lines * count // 2
     some = cells // SPLIT
     edge_rows = {"near": paired_edge() * (row_count - 1), "far": (1 - paired_edge()) * (row_count - 1)}
-
-    def first_line(d):
-        return pl.multiple_of(jnp.bitwise_xor(me, d) * own_lines, own_lines)
-
+    chip = jnp.bitwise_xor(me, pieces[0][0]) // (count // 2)
+    first = pl.multiple_of(chip * lines, lines)
     copies = []
     for part in range(SPLIT):
         for block, (d, base, rows, offset, tiles) in zip(blocks, pieces):
@@ -414,18 +412,12 @@
                     row = edge_rows[row]
                 line = base + i * cells + part * some
                 for tile in range(tiles):
-                    at = part * some * pitch + (first_line(d) if whole else 0) + (offset + tile) * row_count + row
+                    at = part * some * pitch + place(d) * own_lines + (offset + tile) * row_count + row
                     held[pl.ds(at, some, stride=pitch), :] = block[line : line + some, tile * LANES : (tile + 1) * LANES]
-        if whole:
-            for d in set(range(lax.axis_size("span"))) - set(devices):
-                for line in range(own_lines):
-                    at = part * some * pitch + first_line(d) + line
-                    held[pl.ds(at, some, stride=pitch), :] = jnp.zeros((some, LANES), jnp.float32)
-        wanted = pl.ds(0, lines) if whole else pl.ds(first_line(devices[0]), own_lines)
         copies.append(
             pltpu.make_async_copy(
-                held.reshape(cells, pitch, LANES).at[pl.ds(part * some, some), pl.ds(0, lines if whole else own_lines)],
-                out_ref.at[pl.ds(part * some, some), wanted],
+                held.reshape(cells, pitch, LANES).at[pl.ds(part * some, some), pl.ds(0, lines)],
+                out_ref.at[pl.ds(part * some, some), pl.ds(first, lines)],
                 done.at[part],
             )
         )
@@ -562,17 +554,16 @@
             pieces.append((swap(rebuilt[1 + (d - 1) * len(inner) + i], d), half + d, 0, (row,), 0, tiles))
 
     result = None
-    own_lines = tiles * row_count
-    for devices in (range(count - 1), [count - 1]) if own_lines % 8 == 0 else (range(count),):
+    for devices in (range(half), far):
         chosen = [piece for piece in pieces if piece[1] in devices]
         previous = () if result is None else (result,)
         result = pl.pallas_call(
-            functools.partial(unpack_kernel, [piece[1:] for piece in chosen], list(devices), row_count, cells),
+            functools.partial(unpack_kernel, [piece[1:] for piece in chosen], row_count, cells),
             out_shape=jax.ShapeDtypeStruct((cells, lines, LANES), jnp.float32),
             in_specs=[VMEM] * len(chosen) + [ANY] * len(previous),
             out_specs=ANY,
             scratch_shapes=[
-                pltpu.VMEM((cells * ((lines if len(devices) > 1 else own_lines) + 8), LANES), jnp.float32),
+                pltpu.VMEM((cells * (lines // 2 + 8), LANES), jnp.float32),
                 pltpu.SemaphoreType.DMA((SPLIT,)),
             ],
             input_output_aliases={len(chosen): 0} if previous else {},

time: 49.6 us -> 49.7 us (level)
  transfers between devices with their start and end apart: 19 -> 19, of which waited for: 9 -> 8; matrix products, arithmetic and copies ran while one was open for 0% -> 0% of each run, Pallas kernels for 22% -> 21%
where the time goes in v19:
time: 49.7 us; the launch traced here: 49 us
  starting transfers between devices  19.2 us (39%)
  waiting for transfers between devices  16.1 us (32%)
  Pallas kernels  13.5 us (27%)
    ppermute x17, starting transfers between devices, swap(): lax.ppermute(block, 'span', [(i, i ^ d) for i in range(lax.axis_size('spa...  15.9 us
    ppermute x17, waiting for transfers between devices, swap(): lax.ppermute(block, 'span', [(i, i ^ d) for i in range(lax.axis_size('spa...  13 us
    pallas_call x9, Pallas kernels, call(): pl.pallas_call(kernel, out_shape=shapes, in_specs=[VMEM] * len(args) + [A...  8.11 us
    pallas_call x2, Pallas kernels, pack(): pl.pallas_call(functools.partial(pack_kernel, jobs, row_count, cells, len...  3.27 us
    ppermute x2, starting transfers between devices, local(): lax.ppermute(row, 'plane', pair)  3.26 us
    ppermute x2, waiting for transfers between devices, local(): lax.ppermute(row, 'plane', pair)  3.09 us
    pallas_call x2, Pallas kernels, local(): pl.pallas_call(functools.partial(unpack_kernel, [piece[1:] for piece in c...  2.11 us
  transfers between devices with their start and end apart: 19, of which 8 were waited for; matrix products, arithmetic and copies ran while one was open for 0% of the time, Pallas kernels for 21%

profile of v19, /device:TPU:25, one launch (start us, length us, event | category | flops | bytes accessed | tf_op | source)
XLA Modules:
  0.0 49.0 jit_solution(13835812251161764445)
XLA Ops:
  0.0 2.1 %shard_map.73 = (f32[264,256]{1,0:T(8,128)S(1)}, f32[264,256]{1,0:T(8,128)S(1)}, f32[264,256]{1,0:T(8,128)S(1)}) custom-call(f32[128,32,128]{2,1,0:T(8,128)} %bitcast.10), custom_call_target="tpu_custom_call" | custom-call | bytes 200000000 | tf_op jit(solution)/shard_map/pallas_call | solution.py:466
  2.1 1.3 %collective-permute-start.1 = (f32[264,256]{1,0:T(8,128)S(1)}, f32[264,256]{1,0:T(8,128)S(1)}, u32[]{:S(2)}, u32[]{:S(2)}) collective-permute-start(f32[264,256]{1,0:T(8,128)S(1)} %get-tuple-element.37.refs_0_), channel_id=1, source_target_pairs={{0,2},{1,3},{2,0},{3,1},{4,6},{5,7},{6,4},{7,5},{8,10},{9,11},{10,... | collective-permute-start | bytes 811016 | tf_op jit(solution)/shard_map/ppermute | solution.py:442
  3.4 1.0 %collective-permute-start = (f32[264,256]{1,0:T(8,128)S(1)}, f32[264,256]{1,0:T(8,128)S(1)}, u32[]{:S(2)}, u32[]{:S(2)}) collective-permute-start(f32[264,256]{1,0:T(8,128)S(1)} %get-tuple-element.39), channel_id=1, source_target_pairs={{0,1},{1,0},{2,3},{3,2},{4,5},{5,4},{6,7},{7,6},{8,9},{9,8},{10,11... | collective-permute-start | bytes 811016 | tf_op jit(solution)/shard_map/ppermute | solution.py:442
  4.5 1.2 %shard_map.74 = (f32[256,256]{1,0:T(8,128)S(1)}, f32[256,256]{1,0:T(8,128)S(1)}, f32[256,256]{1,0:T(8,128)S(1)}, f32[264,256]{1,0:T(8,128)S(1)}, f32[264,256]{1,...) custom-call(f32[128,32,128]{2,1,0:T(8,128)S(1)} %bitcast.11, ...), custom_call_target="tpu_custom_call" | custom-call | bytes 200000000 | tf_op jit(solution)/shard_map/pallas_call | solution.py:466
  7.6 1.9 %collective-permute-done.1.refs_2_.refs_3_ = f32[264,256]{1,0:T(8,128)S(1)} collective-permute-done((f32[264,256]{1,0:T(8,128)S(1)}, f32[264,256]{1,0:T(8,128)S(1)}, u32[]{:S(2)}, u32[]{:S(2)}) %collective-permute-start.1) | collective-permute-done | bytes 270368 | tf_op jit(solution)/shard_map/ppermute | solution.py:442
  9.6 1.3 %collective-permute-start.7 = (f32[512,256]{1,0:T(8,128)S(1)}, f32[512,256]{1,0:T(8,128)S(1)}, u32[]{:S(2)}, u32[]{:S(2)}) collective-permute-start(f32[512,256]{1,0:T(8,128)S(1)} %shard_map.77.refs_0_), channel_id=1, source_target_pairs={{0,2},{1,3},{2,0},{3,1},{4,6},{5,7},{6,4},{7,5},{8,10},{9,11},{10,... | collective-permute-start | bytes 1572872 | tf_op jit(solution)/shard_map/ppermute | solution.py:442
  10.9 6.5 %collective-permute-done.2.refs_3_ = f32[264,256]{1,0:T(8,128)S(1)} collective-permute-done((f32[264,256]{1,0:T(8,128)S(1)}, f32[264,256]{1,0:T(8,128)S(1)}, u32[]{:S(2)}, u32[]{:S(2)}) %collective-permute-start.2) | collective-permute-done | bytes 270368 | tf_op jit(solution)/shard_map/ppermute | solution.py:442
  18.9 1.2 %collective-permute-start.11 = (f32[368,256]{1,0:T(8,128)S(1)}, f32[368,256]{1,0:T(8,128)S(1)}, u32[]{:S(2)}, u32[]{:S(2)}) collective-permute-start(f32[368,256]{1,0:T(8,128)S(1)} %get-tuple-element.57), channel_id=1, source_target_pairs={{0,4},{4,0},{8,12},{12,8},{16,20},{20,16},{24,28},{28,24},{1,5},{5... | collective-permute-start | bytes 1130504 | tf_op jit(solution)/shard_map/ppermute | solution.py:521
  20.1 2.0 %collective-permute-start.3 = (f32[352,256]{1,0:T(8,128)S(1)}, f32[352,256]{1,0:T(8,128)S(1)}, u32[]{:S(2)}, u32[]{:S(2)}) collective-permute-start(f32[352,256]{1,0:T(8,128)S(1)} %get-tuple-element.44), channel_id=1, source_target_pairs={{4,8},{8,4},{12,16},{16,12},{20,24},{24,20},{5,9},{9,5},{13,17},{1... | collective-permute-start | bytes 1081352 | tf_op jit(solution)/shard_map/ppermute | solution.py:521
  22.1 2.1 %shard_map.78.refs_9_.refs_7_.refs_1_ = f32[512,256]{1,0:T(8,128)S(1)} custom-call(f32[512,256]{1,0:T(8,128)S(1)} %shard_map.77.refs_0_, f32[264,256]{1,0:T(8,128)S(1)} %get-tuple-element.52.refs_1_, f32[264,256]{1,0:T(8,128)S(1)} %collective-permute-done.8.refs_2_, bf16[2,2,176,384]{3,2,1,0:T(8,128)(2,1)S(1)} %copy-done.2, ...), custom_call_target="tpu_custom_call" | custom-call | bytes 1024 | tf_op jit(solution)/shard_map/pallas_call | solution.py:431
  24.3 1.0 %shard_map.82 = f32[368,256]{1,0:T(8,128)S(1)} custom-call(f32[256,256]{1,0:T(8,128)S(1)} %get-tuple-element.45.refs_0_, f32[256,256]{1,0:T(8,128)S(1)} %collective-permute-done.4.refs_1_, f32[264,256]{1,0:T(8,128)S(1)} %get-tuple-element.38.refs_0_.refs_2_, f32[264,256]{1,0:T(8,128)S(1)} %collective-permute-done.refs_1_.refs_3_, ...), custom_call_target="tpu_custom_call" | custom-call | bytes 1024 | tf_op jit(solution)/shard_map/pallas_call | solution.py:431
  25.2 1.3 %collective-permute-start.14 = (f32[368,256]{1,0:T(8,128)S(1)}, f32[368,256]{1,0:T(8,128)S(1)}, u32[]{:S(2)}, u32[]{:S(2)}) collective-permute-start(f32[368,256]{1,0:T(8,128)S(1)} %shard_map.82), channel_id=1, source_target_pairs={{0,2},{1,3},{2,0},{3,1},{4,6},{5,7},{6,4},{7,5},{8,10},{9,11},{10,... | collective-permute-start | bytes 1130504 | tf_op jit(solution)/shard_map/ppermute | solution.py:442
  26.6 1.6 %shard_map.79 = (f32[256,256]{1,0:T(8,128)S(1)}, f32[256,256]{1,0:T(8,128)S(1)}, f32[2,352,256]{2,1,0:T(8,128)S(1)}) custom-call(f32[256,256]{1,0:T(8,128)S(1)} %get-tuple-element.45.refs_0_, f32[256,256]{1,0:T(8,128)S(1)} %collective-permute-done.4.refs_1_, f32[512,256]{1,0:T(8,128)S(1)} %collective-permute-done.7.refs_2_, ...), custom_call_target="tpu_custom_call" | custom-call | bytes 1024 | tf_op jit(solution)/shard_map/pallas_call | solution.py:431
  28.2 1.6 %collective-permute-start.15 = (f32[256,256]{1,0:T(8,128)S(1)}, f32[256,256]{1,0:T(8,128)S(1)}, u32[]{:S(2)}, u32[]{:S(2)}) collective-permute-start(f32[256,256]{1,0:T(8,128)S(1)} %get-tuple-element.61), channel_id=1, source_target_pairs={{0,1},{1,0},{2,3},{3,2},{4,5},{5,4},{6,7},{7,6},{8,9},{9,8},{10,11... | collective-permute-start | bytes 786440 | tf_op jit(solution)/shard_map/ppermute | solution.py:442
  29.8 2.7 %collective-permute-done.3.refs_3_ = f32[352,256]{1,0:T(8,128)S(1)} collective-permute-done((f32[352,256]{1,0:T(8,128)S(1)}, f32[352,256]{1,0:T(8,128)S(1)}, u32[]{:S(2)}, u32[]{:S(2)}) %collective-permute-start.3) | collective-permute-done | bytes 360480 | tf_op jit(solution)/shard_map/ppermute | solution.py:521
  32.6 1.1 %shard_map.80 = (f32[128,256]{1,0:T(8,128)S(1)}, f32[128,256]{1,0:T(8,128)S(1)}, f32[136,256]{1,0:T(8,128)S(1)}, f32[136,256]{1,0:T(8,128)S(1)}) custom-call(f32[2,352,256]{2,1,0:T(8,128)S(1)} %get-tuple-element.41.refs_0_, f32[2,352,256]{2,1,0:T(8,128)S(1)} %get-tuple-element.42.refs_7_.refs_1_, f32[352,16]{1,0:T(8,128)S(1)} %get-tuple-element.43.refs_2_.refs_8_, ...), custom_call_target="tpu_custom_call" | custom-call | bytes 1024 | tf_op jit(solution)/shard_map/pallas_call | solution.py:431
  33.6 1.3 %collective-permute-start.9 = (f32[136,256]{1,0:T(8,128)S(1)}, f32[136,256]{1,0:T(8,128)S(1)}, u32[]{:S(2)}, u32[]{:S(2)}) collective-permute-start(f32[136,256]{1,0:T(8,128)S(1)} %get-tuple-element.55), channel_id=1, source_target_pairs={{0,2},{1,3},{2,0},{3,1},{4,6},{5,7},{6,4},{7,5},{8,10},{9,11},{10,... | collective-permute-start | bytes 417800 | tf_op jit(solution)/shard_map/ppermute | solution.py:442
  34.9 1.6 %collective-permute-start.10 = (f32[136,256]{1,0:T(8,128)S(1)}, f32[136,256]{1,0:T(8,128)S(1)}, u32[]{:S(2)}, u32[]{:S(2)}) collective-permute-start(f32[136,256]{1,0:T(8,128)S(1)} %get-tuple-element.56.refs_9_), channel_id=1, source_target_pairs={{0,3},{1,2},{2,1},{3,0},{4,7},{5,6},{6,5},{7,4},{8,11},{9,10},{10,... | collective-permute-start | bytes 417800 | tf_op jit(solution)/shard_map/ppermute | solution.py:442
  36.9 1.1 %shard_map.81 = (f32[128,256]{1,0:T(8,128)S(1)}, f32[256,256]{1,0:T(8,128)S(1)}, f32[128,256]{1,0:T(8,128)S(1)}, f32[128,256]{1,0:T(8,128)S(1)}) custom-call(f32[2,352,256]{2,1,0:T(8,128)S(1)} %get-tuple-element.41.refs_0_, f32[2,352,256]{2,1,0:T(8,128)S(1)} %get-tuple-element.42.refs_7_.refs_1_, f32[352,16]{1,0:T(8,128)S(1)} %get-tuple-element.43.refs_2_.refs_8_, ...), custom_call_target="tpu_custom_call" | custom-call | bytes 200000000 | tf_op jit(solution)/shard_map/pallas_call | solution.py:431
  38.9 1.2 %collective-permute-start.12 = (f32[128,256]{1,0:T(8,128)S(1)}, f32[128,256]{1,0:T(8,128)S(1)}, u32[]{:S(2)}, u32[]{:S(2)}) collective-permute-start(f32[128,256]{1,0:T(8,128)S(1)} %get-tuple-element.59), channel_id=1, source_target_pairs={{0,2},{1,3},{2,0},{3,1},{4,6},{5,7},{6,4},{7,5},{8,10},{9,11},{10,... | collective-permute-start | bytes 393224 | tf_op jit(solution)/shard_map/ppermute | solution.py:442
  40.2 2.4 %collective-permute-start.13 = (f32[128,256]{1,0:T(8,128)S(1)}, f32[128,256]{1,0:T(8,128)S(1)}, u32[]{:S(2)}, u32[]{:S(2)}) collective-permute-start(f32[128,256]{1,0:T(8,128)S(1)} %get-tuple-element.60.refs_3_), channel_id=1, source_target_pairs={{0,3},{1,2},{2,1},{3,0},{4,7},{5,6},{6,5},{7,4},{8,11},{9,10},{10,... | collective-permute-start | bytes 393224 | tf_op jit(solution)/shard_map/ppermute | solution.py:442
  43.8 1.1 %shard_map.84.refs_7_ = f32[128,32,128]{2,1,0:T(8,128)} custom-call(f32[256,256]{1,0:T(8,128)S(1)} %get-tuple-element.65.refs_0_, f32[256,256]{1,0:T(8,128)S(1)} %collective-permute-done.15.refs_6_.refs_1_, f32[128,256]{1,0:T(8,128)S(1)} %get-tuple-element.66.refs_2_, f32[128,256]{1,0:T(8,128)S(1)} %get-tuple-element.67.refs_3_, ...), custom_call_target="tpu_custom_call" | custom-call | bytes 200000000 | tf_op jit(solution)/shard_map/pallas_call | solution.py:560
  44.9 3.0 %collective-permute-done.13.refs_3_ = f32[128,256]{1,0:T(8,128)S(1)} collective-permute-done((f32[128,256]{1,0:T(8,128)S(1)}, f32[128,256]{1,0:T(8,128)S(1)}, u32[]{:S(2)}, u32[]{:S(2)}) %collective-permute-start.13) | collective-permute-done | bytes 131104 | tf_op jit(solution)/shard_map/ppermute | solution.py:442
  47.9 1.1 %shard_map.85 = f32[128,32,128]{2,1,0:T(8,128)} custom-call(f32[136,256]{1,0:T(8,128)S(1)} %collective-permute-done.9.refs_4_.refs_0_, f32[136,256]{1,0:T(8,128)S(1)} %collective-permute-done.10.refs_5_.refs_1_, f32[128,256]{1,0:T(8,128)S(1)} %collective-permute-done.12.refs_2_, ...), custom_call_target="tpu_custom_call", output_to_operand_aliasing={{}: (7, {})} | custom-call | bytes 1024 | tf_op jit(solution)/shard_map/pallas_call | solution.py:560
  (41 shorter events, 6.1 us)
Async XLA Ops:
  2.1 15.3 %copy-start.2 = (bf16[2,2,176,384]{3,2,1,0:T(8,128)(2,1)S(1)}, bf16[2,2,176,384]{3,2,1,0:T(8,128)(2,1)}, u32[]{:S(2)}) copy-start(bf16[2,2,176,384]{3,2,1,0:T(8,128)(2,1)} %constant.10.clone.refs_4_.refs_3_) | copy-start | bytes 1622020
  2.1 15.2 %copy-start.3 = (s32[4,1024]{1,0:T(4,128)S(1)}, s32[4,1024]{1,0:T(4,128)}, u32[]{:S(2)}) copy-start(s32[4,1024]{1,0:T(4,128)} %refs_6_.9) | copy-start | bytes 49156
  2.1 15.2 %copy-start.4 = (f32[8,384]{1,0:T(8,128)S(1)}, f32[8,384]{1,0:T(8,128)}, u32[]{:S(2)}) copy-start(f32[8,384]{1,0:T(8,128)} %constant.14.clone.refs_5_.refs_6_) | copy-start | bytes 36868
  2.1 7.4 %collective-permute-start.1 = (f32[264,256]{1,0:T(8,128)S(1)}, f32[264,256]{1,0:T(8,128)S(1)}, u32[]{:S(2)}, u32[]{:S(2)}) collective-permute-start(f32[264,256]{1,0:T(8,128)S(1)} %get-tuple-element.37.refs_0_), channel_id=1, source_target_pairs={{0,2},{1,3},{2,0},{3,1},{4,6},{5,7},{6,4},{7,5},{8,10},{9,11},{10,... | collective-permute-start | bytes 811016 | tf_op jit(solution)/shard_map/ppermute | solution.py:442
  3.4 7.5 %collective-permute-start = (f32[264,256]{1,0:T(8,128)S(1)}, f32[264,256]{1,0:T(8,128)S(1)}, u32[]{:S(2)}, u32[]{:S(2)}) collective-permute-start(f32[264,256]{1,0:T(8,128)S(1)} %get-tuple-element.39), channel_id=1, source_target_pairs={{0,1},{1,0},{2,3},{3,2},{4,5},{5,4},{6,7},{7,6},{8,9},{9,8},{10,11... | collective-permute-start | bytes 811016 | tf_op jit(solution)/shard_map/ppermute | solution.py:442
  4.4 13.0 %collective-permute-start.2 = (f32[264,256]{1,0:T(8,128)S(1)}, f32[264,256]{1,0:T(8,128)S(1)}, u32[]{:S(2)}, u32[]{:S(2)}) collective-permute-start(f32[264,256]{1,0:T(8,128)S(1)} %get-tuple-element.40), channel_id=1, source_target_pairs={{0,3},{1,2},{2,1},{3,0},{4,7},{5,6},{6,5},{7,4},{8,11},{9,10},{10,... | collective-permute-start | bytes 811016 | tf_op jit(solution)/shard_map/ppermute | solution.py:442
  5.7 16.4 %copy-start = (bf16[2,2,128,528]{3,2,1,0:T(8,128)(2,1)S(1)}, bf16[2,2,128,528]{3,2,1,0:T(8,128)(2,1)}, u32[]{:S(2)}) copy-start(bf16[2,2,128,528]{3,2,1,0:T(8,128)(2,1)} %constant.11.clone.refs_4_.refs_5_) | copy-start | bytes 1622020
  5.7 1.6 %collective-permute-start.5 = (f32[128,256]{1,0:T(8,128)S(1)}, f32[128,256]{1,0:T(8,128)S(1)}, u32[]{:S(2)}, u32[]{:S(2)}) collective-permute-start(f32[128,256]{1,0:T(8,128)S(1)} %get-tuple-element.50), channel_id=1, source_target_pairs={{0,1},{1,0},{2,3},{3,2},{4,5},{5,4},{6,7},{7,6},{8,9},{9,8},{10,11... | collective-permute-start | bytes 393224 | tf_op jit(solution)/shard_map/ppermute | solution.py:442
  6.3 1.3 %collective-permute-start.6 = (f32[128,256]{1,0:T(8,128)S(1)}, f32[128,256]{1,0:T(8,128)S(1)}, u32[]{:S(2)}, u32[]{:S(2)}) collective-permute-start(f32[128,256]{1,0:T(8,128)S(1)} %get-tuple-element.51), channel_id=1, source_target_pairs={{0,1},{1,0},{2,3},{3,2},{4,5},{5,4},{6,7},{7,6},{8,9},{9,8},{10,11... | collective-permute-start | bytes 393224 | tf_op jit(solution)/shard_map/ppermute | solution.py:442
  9.6 17.0 %collective-permute-start.7 = (f32[512,256]{1,0:T(8,128)S(1)}, f32[512,256]{1,0:T(8,128)S(1)}, u32[]{:S(2)}, u32[]{:S(2)}) collective-permute-start(f32[512,256]{1,0:T(8,128)S(1)} %shard_map.77.refs_0_), channel_id=1, source_target_pairs={{0,2},{1,3},{2,0},{3,1},{4,6},{5,7},{6,4},{7,5},{8,10},{9,11},{10,... | collective-permute-start | bytes 1572872 | tf_op jit(solution)/shard_map/ppermute | solution.py:442
  18.3 3.8 %collective-permute-start.8 = (f32[264,256]{1,0:T(8,128)S(1)}, f32[264,256]{1,0:T(8,128)S(1)}, u32[]{:S(2)}, u32[]{:S(2)}) collective-permute-start(f32[264,256]{1,0:T(8,128)S(1)} %get-tuple-element.53), channel_id=1, source_target_pairs={{0,1},{1,0},{2,3},{3,2},{4,5},{5,4},{6,7},{7,6},{8,9},{9,8},{10,11... | collective-permute-start | bytes 811016 | tf_op jit(solution)/shard_map/ppermute | solution.py:442
  18.4 5.9 %collective-permute-start.4 = (f32[256,256]{1,0:T(8,128)S(1)}, f32[256,256]{1,0:T(8,128)S(1)}, u32[]{:S(2)}, u32[]{:S(2)}) collective-permute-start(f32[256,256]{1,0:T(8,128)S(1)} %get-tuple-element.48), channel_id=1, source_target_pairs={{0,1},{1,0},{2,3},{3,2},{4,5},{5,4},{6,7},{7,6},{8,9},{9,8},{10,11... | collective-permute-start | bytes 786440 | tf_op jit(solution)/shard_map/ppermute | solution.py:442
  18.9 18.1 %collective-permute-start.11 = (f32[368,256]{1,0:T(8,128)S(1)}, f32[368,256]{1,0:T(8,128)S(1)}, u32[]{:S(2)}, u32[]{:S(2)}) collective-permute-start(f32[368,256]{1,0:T(8,128)S(1)} %get-tuple-element.57), channel_id=1, source_target_pairs={{0,4},{4,0},{8,12},{12,8},{16,20},{20,16},{24,28},{28,24},{1,5},{5... | collective-permute-start | bytes 1130504 | tf_op jit(solution)/shard_map/ppermute | solution.py:521
  20.1 12.5 %collective-permute-start.3 = (f32[352,256]{1,0:T(8,128)S(1)}, f32[352,256]{1,0:T(8,128)S(1)}, u32[]{:S(2)}, u32[]{:S(2)}) collective-permute-start(f32[352,256]{1,0:T(8,128)S(1)} %get-tuple-element.44), channel_id=1, source_target_pairs={{4,8},{8,4},{12,16},{16,12},{20,24},{24,20},{5,9},{9,5},{13,17},{1... | collective-permute-start | bytes 1081352 | tf_op jit(solution)/shard_map/ppermute | solution.py:521
  25.2 13.7 %collective-permute-start.14 = (f32[368,256]{1,0:T(8,128)S(1)}, f32[368,256]{1,0:T(8,128)S(1)}, u32[]{:S(2)}, u32[]{:S(2)}) collective-permute-start(f32[368,256]{1,0:T(8,128)S(1)} %shard_map.82), channel_id=1, source_target_pairs={{0,2},{1,3},{2,0},{3,1},{4,6},{5,7},{6,4},{7,5},{8,10},{9,11},{10,... | collective-permute-start | bytes 1130504 | tf_op jit(solution)/shard_map/ppermute | solution.py:442
  28.2 14.7 %collective-permute-start.15 = (f32[256,256]{1,0:T(8,128)S(1)}, f32[256,256]{1,0:T(8,128)S(1)}, u32[]{:S(2)}, u32[]{:S(2)}) collective-permute-start(f32[256,256]{1,0:T(8,128)S(1)} %get-tuple-element.61), channel_id=1, source_target_pairs={{0,1},{1,0},{2,3},{3,2},{4,5},{5,4},{6,7},{7,6},{8,9},{9,8},{10,11... | collective-permute-start | bytes 786440 | tf_op jit(solution)/shard_map/ppermute | solution.py:442
  33.6 9.2 %copy-start.6 = (bf16[2,128,576]{2,1,0:T(8,128)(2,1)S(1)}, bf16[2,128,576]{2,1,0:T(8,128)(2,1)}, u32[]{:S(2)}) copy-start(bf16[2,128,576]{2,1,0:T(8,128)(2,1)} %constant.13.clone.refs_2_) | copy-start | bytes 884740
  33.6 6.5 %collective-permute-start.9 = (f32[136,256]{1,0:T(8,128)S(1)}, f32[136,256]{1,0:T(8,128)S(1)}, u32[]{:S(2)}, u32[]{:S(2)}) collective-permute-start(f32[136,256]{1,0:T(8,128)S(1)} %get-tuple-element.55), channel_id=1, source_target_pairs={{0,2},{1,3},{2,0},{3,1},{4,6},{5,7},{6,4},{7,5},{8,10},{9,11},{10,... | collective-permute-start | bytes 417800 | tf_op jit(solution)/shard_map/ppermute | solution.py:442
  34.9 7.9 %collective-permute-start.10 = (f32[136,256]{1,0:T(8,128)S(1)}, f32[136,256]{1,0:T(8,128)S(1)}, u32[]{:S(2)}, u32[]{:S(2)}) collective-permute-start(f32[136,256]{1,0:T(8,128)S(1)} %get-tuple-element.56.refs_9_), channel_id=1, source_target_pairs={{0,3},{1,2},{2,1},{3,0},{4,7},{5,6},{6,5},{7,4},{8,11},{9,10},{10,... | collective-permute-start | bytes 417800 | tf_op jit(solution)/shard_map/ppermute | solution.py:442
  38.0 5.8 %collective-permute-start.18 = (f32[256,256]{1,0:T(8,128)S(1)}, f32[256,256]{1,0:T(8,128)S(1)}, u32[]{:S(2)}, u32[]{:S(2)}) collective-permute-start(f32[256,256]{1,0:T(8,128)S(1)} %get-tuple-element.68), channel_id=1, source_target_pairs={{0,1},{1,0},{2,3},{3,2},{4,5},{5,4},{6,7},{7,6},{8,9},{9,8},{10,11... | collective-permute-start | bytes 786440 | tf_op jit(solution)/shard_map/ppermute | solution.py:442
  38.9 6.0 %collective-permute-start.12 = (f32[128,256]{1,0:T(8,128)S(1)}, f32[128,256]{1,0:T(8,128)S(1)}, u32[]{:S(2)}, u32[]{:S(2)}) collective-permute-start(f32[128,256]{1,0:T(8,128)S(1)} %get-tuple-element.59), channel_id=1, source_target_pairs={{0,2},{1,3},{2,0},{3,1},{4,6},{5,7},{6,4},{7,5},{8,10},{9,11},{10,... | collective-permute-start | bytes 393224 | tf_op jit(solution)/shard_map/ppermute | solution.py:442
  40.2 7.7 %collective-permute-start.13 = (f32[128,256]{1,0:T(8,128)S(1)}, f32[128,256]{1,0:T(8,128)S(1)}, u32[]{:S(2)}, u32[]{:S(2)}) collective-permute-start(f32[128,256]{1,0:T(8,128)S(1)} %get-tuple-element.60.refs_3_), channel_id=1, source_target_pairs={{0,3},{1,2},{2,1},{3,0},{4,7},{5,6},{6,5},{7,4},{8,11},{9,10},{10,... | collective-permute-start | bytes 393224 | tf_op jit(solution)/shard_map/ppermute | solution.py:442
  43.2 4.7 %collective-permute-start.16 = (f32[128,256]{1,0:T(8,128)S(1)}, f32[128,256]{1,0:T(8,128)S(1)}, u32[]{:S(2)}, u32[]{:S(2)}) collective-permute-start(f32[128,256]{1,0:T(8,128)S(1)} %get-tuple-element.63), channel_id=1, source_target_pairs={{0,1},{1,0},{2,3},{3,2},{4,5},{5,4},{6,7},{7,6},{8,9},{9,8},{10,11... | collective-permute-start | bytes 393224 | tf_op jit(solution)/shard_map/ppermute | solution.py:442
  43.3 4.6 %collective-permute-start.17 = (f32[128,256]{1,0:T(8,128)S(1)}, f32[128,256]{1,0:T(8,128)S(1)}, u32[]{:S(2)}, u32[]{:S(2)}) collective-permute-start(f32[128,256]{1,0:T(8,128)S(1)} %get-tuple-element.64), channel_id=1, source_target_pairs={{0,1},{1,0},{2,3},{3,2},{4,5},{5,4},{6,7},{7,6},{8,9},{9,8},{10,11... | collective-permute-start | bytes 393224 | tf_op jit(solution)/shard_map/ppermute | solution.py:442
  (2 other events, 10.5 us)

commit v20 on v19

--- a/solution.py
+++ b/solution.py
@@ -460,7 +460,7 @@
     source = source.reshape(cells, lines, LANES)
     scratch = [pltpu.VMEM((cells * (lines + 8), LANES), jnp.float32), pltpu.SemaphoreType.DMA((SPLIT,))]
 
-    def pack(source, wanted, *earlier):
+    def pack(wanted, *earlier):
         jobs = [(at, 0, d, rows, 0, tiles, inner if rows == edges else ()) for at, (d, rows) in enumerate(wanted)]
         shapes = [(len(rows) * cells + (8 if rows == edges else 0), width) for _, rows in wanted]
         return pl.pallas_call(
@@ -471,13 +471,13 @@
             scratch_shapes=scratch,
             compiler_params=PARAMS,
             cost_estimate=LONG,
-        )(source, *earlier)
-
-    packed = pack(pltpu.with_memory_space_constraint(source, pltpu.HBM), [(d, edges) for d in range(1, count)])
+        )(pltpu.with_memory_space_constraint(source, pltpu.HBM), *earlier)
+
+    packed = pack([(d, edges) for d in range(1, count)])
     edge_blocks = [swap(block, d) for d, block in enumerate(packed, 1)]
     wanted = [(d, inner) for d in range(half + 1)] + [(0, edges)] + [(d, edges) for d in far]
     wanted += [(half + d, (row,)) for d in near for row in inner]
-    packed = pack(source, wanted, packed[half - 1])
+    packed = pack(wanted, packed[half - 1])
     edge_blocks = [packed[half + 1], *edge_blocks]
     relayed = packed[2 * half + 2 :]
     relayed = [swap(relayed[(d - 1) * len(inner) + i], d) for d in near for i in range(len(inner))]

time: 49.7 us -> 49.6 us (level)
  waiting for transfers between devices: 16.1 us -> 15.2 us
  Pallas kernels: 13.5 us -> 14.2 us
    ppermute x17, waiting for transfers between devices: 13 us -> 12.1 us  [swap(): lax.ppermute(block, 'span', [(i, i ^ d) for i in range(lax.axis_size('spa...]
    pallas_call x2, Pallas kernels: 3.27 us -> 4.01 us  [pack(): pl.pallas_call(functools.partial(pack_kernel, jobs, row_count, cells, len...]
  transfers between devices with their start and end apart: 19 -> 19, of which waited for: 8 -> 8; matrix products, arithmetic and copies ran while one was open for 0% -> 0% of each run, Pallas kernels for 21% -> 23%
where the time goes in v20:
time: 49.6 us; the launch traced here: 48.8 us
  starting transfers between devices  19.2 us (39%)
  waiting for transfers between devices  15.2 us (31%)
  Pallas kernels  14.2 us (29%)
    ppermute x17, starting transfers between devices, swap(): lax.ppermute(block, 'span', [(i, i ^ d) for i in range(lax.axis_size('spa...  15.9 us
    ppermute x17, waiting for transfers between devices, swap(): lax.ppermute(block, 'span', [(i, i ^ d) for i in range(lax.axis_size('spa...  12.1 us
    pallas_call x9, Pallas kernels, call(): pl.pallas_call(kernel, out_shape=shapes, in_specs=[VMEM] * len(args) + [A...  8.08 us
    pallas_call x2, Pallas kernels, pack(): pl.pallas_call(functools.partial(pack_kernel, jobs, row_count, cells, len...  4.01 us
    ppermute x2, starting transfers between devices, local(): lax.ppermute(row, 'plane', pair)  3.26 us
    ppermute x2, waiting for transfers between devices, local(): lax.ppermute(row, 'plane', pair)  3.1 us
    pallas_call x2, Pallas kernels, local(): pl.pallas_call(functools.partial(unpack_kernel, [piece[1:] for piece in c...  2.11 us
  transfers between devices with their start and end apart: 19, of which 8 were waited for; matrix products, arithmetic and copies ran while one was open for 0% of the time, Pallas kernels for 23%

profile of v20, /device:TPU:25, one launch (start us, length us, event | category | flops | bytes accessed | tf_op | source)
XLA Modules:
  0.0 48.8 jit_solution(16685572378187419119)
XLA Ops:
  0.0 1.9 %shard_map.73 = (f32[264,256]{1,0:T(8,128)S(1)}, f32[264,256]{1,0:T(8,128)S(1)}, f32[264,256]{1,0:T(8,128)S(1)}) custom-call(f32[128,32,128]{2,1,0:T(8,128)} %bitcast.10), custom_call_target="tpu_custom_call" | custom-call | bytes 200000000 | tf_op jit(solution)/shard_map/pallas_call | solution.py:466
  2.0 1.3 %collective-permute-start.1 = (f32[264,256]{1,0:T(8,128)S(1)}, f32[264,256]{1,0:T(8,128)S(1)}, u32[]{:S(2)}, u32[]{:S(2)}) collective-permute-start(f32[264,256]{1,0:T(8,128)S(1)} %get-tuple-element.37.refs_0_), channel_id=1, source_target_pairs={{0,2},{1,3},{2,0},{3,1},{4,6},{5,7},{6,4},{7,5},{8,10},{9,11},{10,... | collective-permute-start | bytes 811016 | tf_op jit(solution)/shard_map/ppermute | solution.py:442
  3.3 1.0 %collective-permute-start = (f32[264,256]{1,0:T(8,128)S(1)}, f32[264,256]{1,0:T(8,128)S(1)}, u32[]{:S(2)}, u32[]{:S(2)}) collective-permute-start(f32[264,256]{1,0:T(8,128)S(1)} %get-tuple-element.39), channel_id=1, source_target_pairs={{0,1},{1,0},{2,3},{3,2},{4,5},{5,4},{6,7},{7,6},{8,9},{9,8},{10,11... | collective-permute-start | bytes 811016 | tf_op jit(solution)/shard_map/ppermute | solution.py:442
  4.3 2.1 %shard_map.74 = (f32[256,256]{1,0:T(8,128)S(1)}, f32[256,256]{1,0:T(8,128)S(1)}, f32[256,256]{1,0:T(8,128)S(1)}, f32[264,256]{1,0:T(8,128)S(1)}, f32[264,256]{1,...) custom-call(f32[128,32,128]{2,1,0:T(8,128)} %bitcast.11, ...), custom_call_target="tpu_custom_call" | custom-call | bytes 200000000 | tf_op jit(solution)/shard_map/pallas_call | solution.py:466
  8.4 1.0 %collective-permute-done.1.refs_2_.refs_3_ = f32[264,256]{1,0:T(8,128)S(1)} collective-permute-done((f32[264,256]{1,0:T(8,128)S(1)}, f32[264,256]{1,0:T(8,128)S(1)}, u32[]{:S(2)}, u32[]{:S(2)}) %collective-permute-start.1) | collective-permute-done | bytes 270368 | tf_op jit(solution)/shard_map/ppermute | solution.py:442
  9.4 1.3 %collective-permute-start.7 = (f32[512,256]{1,0:T(8,128)S(1)}, f32[512,256]{1,0:T(8,128)S(1)}, u32[]{:S(2)}, u32[]{:S(2)}) collective-permute-start(f32[512,256]{1,0:T(8,128)S(1)} %shard_map.77.refs_0_), channel_id=1, source_target_pairs={{0,2},{1,3},{2,0},{3,1},{4,6},{5,7},{6,4},{7,5},{8,10},{9,11},{10,... | collective-permute-start | bytes 1572872 | tf_op jit(solution)/shard_map/ppermute | solution.py:442
  10.7 6.5 %collective-permute-done.2.refs_3_ = f32[264,256]{1,0:T(8,128)S(1)} collective-permute-done((f32[264,256]{1,0:T(8,128)S(1)}, f32[264,256]{1,0:T(8,128)S(1)}, u32[]{:S(2)}, u32[]{:S(2)}) %collective-permute-start.2) | collective-permute-done | bytes 270368 | tf_op jit(solution)/shard_map/ppermute | solution.py:442
  18.7 1.2 %collective-permute-start.11 = (f32[368,256]{1,0:T(8,128)S(1)}, f32[368,256]{1,0:T(8,128)S(1)}, u32[]{:S(2)}, u32[]{:S(2)}) collective-permute-start(f32[368,256]{1,0:T(8,128)S(1)} %get-tuple-element.57), channel_id=1, source_target_pairs={{0,4},{4,0},{8,12},{12,8},{16,20},{20,16},{24,28},{28,24},{1,5},{5... | collective-permute-start | bytes 1130504 | tf_op jit(solution)/shard_map/ppermute | solution.py:521
  19.9 2.0 %collective-permute-start.3 = (f32[352,256]{1,0:T(8,128)S(1)}, f32[352,256]{1,0:T(8,128)S(1)}, u32[]{:S(2)}, u32[]{:S(2)}) collective-permute-start(f32[352,256]{1,0:T(8,128)S(1)} %get-tuple-element.44), channel_id=1, source_target_pairs={{4,8},{8,4},{12,16},{16,12},{20,24},{24,20},{5,9},{9,5},{13,17},{1... | collective-permute-start | bytes 1081352 | tf_op jit(solution)/shard_map/ppermute | solution.py:521
  22.0 2.1 %shard_map.78.refs_9_.refs_7_.refs_1_ = f32[512,256]{1,0:T(8,128)S(1)} custom-call(f32[512,256]{1,0:T(8,128)S(1)} %shard_map.77.refs_0_, f32[264,256]{1,0:T(8,128)S(1)} %get-tuple-element.52.refs_1_, f32[264,256]{1,0:T(8,128)S(1)} %collective-permute-done.8.refs_2_, bf16[2,2,176,384]{3,2,1,0:T(8,128)(2,1)S(1)} %copy-done.1, ...), custom_call_target="tpu_custom_call" | custom-call | bytes 1024 | tf_op jit(solution)/shard_map/pallas_call | solution.py:431
  24.1 1.0 %shard_map.82 = f32[368,256]{1,0:T(8,128)S(1)} custom-call(f32[256,256]{1,0:T(8,128)S(1)} %get-tuple-element.45.refs_0_, f32[256,256]{1,0:T(8,128)S(1)} %collective-permute-done.4.refs_1_, f32[264,256]{1,0:T(8,128)S(1)} %get-tuple-element.38.refs_0_.refs_2_, f32[264,256]{1,0:T(8,128)S(1)} %collective-permute-done.refs_1_.refs_3_, ...), custom_call_target="tpu_custom_call" | custom-call | bytes 1024 | tf_op jit(solution)/shard_map/pallas_call | solution.py:431
  25.1 1.3 %collective-permute-start.14 = (f32[368,256]{1,0:T(8,128)S(1)}, f32[368,256]{1,0:T(8,128)S(1)}, u32[]{:S(2)}, u32[]{:S(2)}) collective-permute-start(f32[368,256]{1,0:T(8,128)S(1)} %shard_map.82), channel_id=1, source_target_pairs={{0,2},{1,3},{2,0},{3,1},{4,6},{5,7},{6,4},{7,5},{8,10},{9,11},{10,... | collective-permute-start | bytes 1130504 | tf_op jit(solution)/shard_map/ppermute | solution.py:442
  26.4 1.6 %shard_map.79 = (f32[256,256]{1,0:T(8,128)S(1)}, f32[256,256]{1,0:T(8,128)S(1)}, f32[2,352,256]{2,1,0:T(8,128)S(1)}) custom-call(f32[256,256]{1,0:T(8,128)S(1)} %get-tuple-element.45.refs_0_, f32[256,256]{1,0:T(8,128)S(1)} %collective-permute-done.4.refs_1_, f32[512,256]{1,0:T(8,128)S(1)} %collective-permute-done.7.refs_2_, ...), custom_call_target="tpu_custom_call" | custom-call | bytes 1024 | tf_op jit(solution)/shard_map/pallas_call | solution.py:431
  28.0 1.6 %collective-permute-start.15 = (f32[256,256]{1,0:T(8,128)S(1)}, f32[256,256]{1,0:T(8,128)S(1)}, u32[]{:S(2)}, u32[]{:S(2)}) collective-permute-start(f32[256,256]{1,0:T(8,128)S(1)} %get-tuple-element.61), channel_id=1, source_target_pairs={{0,1},{1,0},{2,3},{3,2},{4,5},{5,4},{6,7},{7,6},{8,9},{9,8},{10,11... | collective-permute-start | bytes 786440 | tf_op jit(solution)/shard_map/ppermute | solution.py:442
  29.7 2.7 %collective-permute-done.3.refs_3_ = f32[352,256]{1,0:T(8,128)S(1)} collective-permute-done((f32[352,256]{1,0:T(8,128)S(1)}, f32[352,256]{1,0:T(8,128)S(1)}, u32[]{:S(2)}, u32[]{:S(2)}) %collective-permute-start.3) | collective-permute-done | bytes 360480 | tf_op jit(solution)/shard_map/ppermute | solution.py:521
  32.4 1.1 %shard_map.80 = (f32[128,256]{1,0:T(8,128)S(1)}, f32[128,256]{1,0:T(8,128)S(1)}, f32[136,256]{1,0:T(8,128)S(1)}, f32[136,256]{1,0:T(8,128)S(1)}) custom-call(f32[2,352,256]{2,1,0:T(8,128)S(1)} %get-tuple-element.41.refs_0_, f32[2,352,256]{2,1,0:T(8,128)S(1)} %get-tuple-element.42.refs_7_.refs_1_, f32[352,16]{1,0:T(8,128)S(1)} %get-tuple-element.43.refs_2_.refs_8_, ...), custom_call_target="tpu_custom_call" | custom-call | bytes 1024 | tf_op jit(solution)/shard_map/pallas_call | solution.py:431
  33.5 1.3 %collective-permute-start.9 = (f32[136,256]{1,0:T(8,128)S(1)}, f32[136,256]{1,0:T(8,128)S(1)}, u32[]{:S(2)}, u32[]{:S(2)}) collective-permute-start(f32[136,256]{1,0:T(8,128)S(1)} %get-tuple-element.55), channel_id=1, source_target_pairs={{0,2},{1,3},{2,0},{3,1},{4,6},{5,7},{6,4},{7,5},{8,10},{9,11},{10,... | collective-permute-start | bytes 417800 | tf_op jit(solution)/shard_map/ppermute | solution.py:442
  34.8 1.6 %collective-permute-start.10 = (f32[136,256]{1,0:T(8,128)S(1)}, f32[136,256]{1,0:T(8,128)S(1)}, u32[]{:S(2)}, u32[]{:S(2)}) collective-permute-start(f32[136,256]{1,0:T(8,128)S(1)} %get-tuple-element.56.refs_9_), channel_id=1, source_target_pairs={{0,3},{1,2},{2,1},{3,0},{4,7},{5,6},{6,5},{7,4},{8,11},{9,10},{10,... | collective-permute-start | bytes 417800 | tf_op jit(solution)/shard_map/ppermute | solution.py:442
  36.8 1.1 %shard_map.81 = (f32[128,256]{1,0:T(8,128)S(1)}, f32[256,256]{1,0:T(8,128)S(1)}, f32[128,256]{1,0:T(8,128)S(1)}, f32[128,256]{1,0:T(8,128)S(1)}) custom-call(f32[2,352,256]{2,1,0:T(8,128)S(1)} %get-tuple-element.41.refs_0_, f32[2,352,256]{2,1,0:T(8,128)S(1)} %get-tuple-element.42.refs_7_.refs_1_, f32[352,16]{1,0:T(8,128)S(1)} %get-tuple-element.43.refs_2_.refs_8_, ...), custom_call_target="tpu_custom_call" | custom-call | bytes 200000000 | tf_op jit(solution)/shard_map/pallas_call | solution.py:431
  38.7 1.2 %collective-permute-start.12 = (f32[128,256]{1,0:T(8,128)S(1)}, f32[128,256]{1,0:T(8,128)S(1)}, u32[]{:S(2)}, u32[]{:S(2)}) collective-permute-start(f32[128,256]{1,0:T(8,128)S(1)} %get-tuple-element.59), channel_id=1, source_target_pairs={{0,2},{1,3},{2,0},{3,1},{4,6},{5,7},{6,4},{7,5},{8,10},{9,11},{10,... | collective-permute-start | bytes 393224 | tf_op jit(solution)/shard_map/ppermute | solution.py:442
  40.0 2.4 %collective-permute-start.13 = (f32[128,256]{1,0:T(8,128)S(1)}, f32[128,256]{1,0:T(8,128)S(1)}, u32[]{:S(2)}, u32[]{:S(2)}) collective-permute-start(f32[128,256]{1,0:T(8,128)S(1)} %get-tuple-element.60.refs_3_), channel_id=1, source_target_pairs={{0,3},{1,2},{2,1},{3,0},{4,7},{5,6},{6,5},{7,4},{8,11},{9,10},{10,... | collective-permute-start | bytes 393224 | tf_op jit(solution)/shard_map/ppermute | solution.py:442
  43.6 1.1 %shard_map.84.refs_7_ = f32[128,32,128]{2,1,0:T(8,128)} custom-call(f32[256,256]{1,0:T(8,128)S(1)} %get-tuple-element.65.refs_0_, f32[256,256]{1,0:T(8,128)S(1)} %collective-permute-done.15.refs_6_.refs_1_, f32[128,256]{1,0:T(8,128)S(1)} %get-tuple-element.66.refs_2_, f32[128,256]{1,0:T(8,128)S(1)} %get-tuple-element.67.refs_3_, ...), custom_call_target="tpu_custom_call" | custom-call | bytes 200000000 | tf_op jit(solution)/shard_map/pallas_call | solution.py:560
  44.7 3.0 %collective-permute-done.13.refs_3_ = f32[128,256]{1,0:T(8,128)S(1)} collective-permute-done((f32[128,256]{1,0:T(8,128)S(1)}, f32[128,256]{1,0:T(8,128)S(1)}, u32[]{:S(2)}, u32[]{:S(2)}) %collective-permute-start.13) | collective-permute-done | bytes 131104 | tf_op jit(solution)/shard_map/ppermute | solution.py:442
  47.8 1.1 %shard_map.85 = f32[128,32,128]{2,1,0:T(8,128)} custom-call(f32[136,256]{1,0:T(8,128)S(1)} %collective-permute-done.9.refs_4_.refs_0_, f32[136,256]{1,0:T(8,128)S(1)} %collective-permute-done.10.refs_5_.refs_1_, f32[128,256]{1,0:T(8,128)S(1)} %collective-permute-done.12.refs_2_, ...), custom_call_target="tpu_custom_call", output_to_operand_aliasing={{}: (7, {})} | custom-call | bytes 1024 | tf_op jit(solution)/shard_map/pallas_call | solution.py:560
  (39 shorter events, 6.1 us)
Async XLA Ops:
  1.9 15.3 %copy-start.1 = (bf16[2,2,176,384]{3,2,1,0:T(8,128)(2,1)S(1)}, bf16[2,2,176,384]{3,2,1,0:T(8,128)(2,1)}, u32[]{:S(2)}) copy-start(bf16[2,2,176,384]{3,2,1,0:T(8,128)(2,1)} %constant.10.clone.refs_4_.refs_3_) | copy-start | bytes 1622020
  1.9 15.2 %copy-start.2 = (s32[4,1024]{1,0:T(4,128)S(1)}, s32[4,1024]{1,0:T(4,128)}, u32[]{:S(2)}) copy-start(s32[4,1024]{1,0:T(4,128)} %refs_6_.9) | copy-start | bytes 49156
  2.0 15.2 %copy-start.3 = (f32[8,384]{1,0:T(8,128)S(1)}, f32[8,384]{1,0:T(8,128)}, u32[]{:S(2)}) copy-start(f32[8,384]{1,0:T(8,128)} %constant.14.clone.refs_5_.refs_6_) | copy-start | bytes 36868
  2.0 7.4 %collective-permute-start.1 = (f32[264,256]{1,0:T(8,128)S(1)}, f32[264,256]{1,0:T(8,128)S(1)}, u32[]{:S(2)}, u32[]{:S(2)}) collective-permute-start(f32[264,256]{1,0:T(8,128)S(1)} %get-tuple-element.37.refs_0_), channel_id=1, source_target_pairs={{0,2},{1,3},{2,0},{3,1},{4,6},{5,7},{6,4},{7,5},{8,10},{9,11},{10,... | collective-permute-start | bytes 811016 | tf_op jit(solution)/shard_map/ppermute | solution.py:442
  3.3 7.5 %collective-permute-start = (f32[264,256]{1,0:T(8,128)S(1)}, f32[264,256]{1,0:T(8,128)S(1)}, u32[]{:S(2)}, u32[]{:S(2)}) collective-permute-start(f32[264,256]{1,0:T(8,128)S(1)} %get-tuple-element.39), channel_id=1, source_target_pairs={{0,1},{1,0},{2,3},{3,2},{4,5},{5,4},{6,7},{7,6},{8,9},{9,8},{10,11... | collective-permute-start | bytes 811016 | tf_op jit(solution)/shard_map/ppermute | solution.py:442
  4.2 13.0 %collective-permute-start.2 = (f32[264,256]{1,0:T(8,128)S(1)}, f32[264,256]{1,0:T(8,128)S(1)}, u32[]{:S(2)}, u32[]{:S(2)}) collective-permute-start(f32[264,256]{1,0:T(8,128)S(1)} %get-tuple-element.40), channel_id=1, source_target_pairs={{0,3},{1,2},{2,1},{3,0},{4,7},{5,6},{6,5},{7,4},{8,11},{9,10},{10,... | collective-permute-start | bytes 811016 | tf_op jit(solution)/shard_map/ppermute | solution.py:442
  6.4 15.5 %copy-start = (bf16[2,2,128,528]{3,2,1,0:T(8,128)(2,1)S(1)}, bf16[2,2,128,528]{3,2,1,0:T(8,128)(2,1)}, u32[]{:S(2)}) copy-start(bf16[2,2,128,528]{3,2,1,0:T(8,128)(2,1)} %constant.11.clone.refs_4_.refs_5_) | copy-start | bytes 1622020
  6.5 1.6 %collective-permute-start.5 = (f32[128,256]{1,0:T(8,128)S(1)}, f32[128,256]{1,0:T(8,128)S(1)}, u32[]{:S(2)}, u32[]{:S(2)}) collective-permute-start(f32[128,256]{1,0:T(8,128)S(1)} %get-tuple-element.50), channel_id=1, source_target_pairs={{0,1},{1,0},{2,3},{3,2},{4,5},{5,4},{6,7},{7,6},{8,9},{9,8},{10,11... | collective-permute-start | bytes 393224 | tf_op jit(solution)/shard_map/ppermute | solution.py:442
  7.0 1.3 %collective-permute-start.6 = (f32[128,256]{1,0:T(8,128)S(1)}, f32[128,256]{1,0:T(8,128)S(1)}, u32[]{:S(2)}, u32[]{:S(2)}) collective-permute-start(f32[128,256]{1,0:T(8,128)S(1)} %get-tuple-element.51), channel_id=1, source_target_pairs={{0,1},{1,0},{2,3},{3,2},{4,5},{5,4},{6,7},{7,6},{8,9},{9,8},{10,11... | collective-permute-start | bytes 393224 | tf_op jit(solution)/shard_map/ppermute | solution.py:442
  9.4 17.0 %collective-permute-start.7 = (f32[512,256]{1,0:T(8,128)S(1)}, f32[512,256]{1,0:T(8,128)S(1)}, u32[]{:S(2)}, u32[]{:S(2)}) collective-permute-start(f32[512,256]{1,0:T(8,128)S(1)} %shard_map.77.refs_0_), channel_id=1, source_target_pairs={{0,2},{1,3},{2,0},{3,1},{4,6},{5,7},{6,4},{7,5},{8,10},{9,11},{10,... | collective-permute-start | bytes 1572872 | tf_op jit(solution)/shard_map/ppermute | solution.py:442
  18.1 3.8 %collective-permute-start.8 = (f32[264,256]{1,0:T(8,128)S(1)}, f32[264,256]{1,0:T(8,128)S(1)}, u32[]{:S(2)}, u32[]{:S(2)}) collective-permute-start(f32[264,256]{1,0:T(8,128)S(1)} %get-tuple-element.53), channel_id=1, source_target_pairs={{0,1},{1,0},{2,3},{3,2},{4,5},{5,4},{6,7},{7,6},{8,9},{9,8},{10,11... | collective-permute-start | bytes 811016 | tf_op jit(solution)/shard_map/ppermute | solution.py:442
  18.2 5.9 %collective-permute-start.4 = (f32[256,256]{1,0:T(8,128)S(1)}, f32[256,256]{1,0:T(8,128)S(1)}, u32[]{:S(2)}, u32[]{:S(2)}) collective-permute-start(f32[256,256]{1,0:T(8,128)S(1)} %get-tuple-element.48), channel_id=1, source_target_pairs={{0,1},{1,0},{2,3},{3,2},{4,5},{5,4},{6,7},{7,6},{8,9},{9,8},{10,11... | collective-permute-start | bytes 786440 | tf_op jit(solution)/shard_map/ppermute | solution.py:442
  18.7 18.1 %collective-permute-start.11 = (f32[368,256]{1,0:T(8,128)S(1)}, f32[368,256]{1,0:T(8,128)S(1)}, u32[]{:S(2)}, u32[]{:S(2)}) collective-permute-start(f32[368,256]{1,0:T(8,128)S(1)} %get-tuple-element.57), channel_id=1, source_target_pairs={{0,4},{4,0},{8,12},{12,8},{16,20},{20,16},{24,28},{28,24},{1,5},{5... | collective-permute-start | bytes 1130504 | tf_op jit(solution)/shard_map/ppermute | solution.py:521
  19.9 12.5 %collective-permute-start.3 = (f32[352,256]{1,0:T(8,128)S(1)}, f32[352,256]{1,0:T(8,128)S(1)}, u32[]{:S(2)}, u32[]{:S(2)}) collective-permute-start(f32[352,256]{1,0:T(8,128)S(1)} %get-tuple-element.44), channel_id=1, source_target_pairs={{4,8},{8,4},{12,16},{16,12},{20,24},{24,20},{5,9},{9,5},{13,17},{1... | collective-permute-start | bytes 1081352 | tf_op jit(solution)/shard_map/ppermute | solution.py:521
  25.1 13.7 %collective-permute-start.14 = (f32[368,256]{1,0:T(8,128)S(1)}, f32[368,256]{1,0:T(8,128)S(1)}, u32[]{:S(2)}, u32[]{:S(2)}) collective-permute-start(f32[368,256]{1,0:T(8,128)S(1)} %shard_map.82), channel_id=1, source_target_pairs={{0,2},{1,3},{2,0},{3,1},{4,6},{5,7},{6,4},{7,5},{8,10},{9,11},{10,... | collective-permute-start | bytes 1130504 | tf_op jit(solution)/shard_map/ppermute | solution.py:442
  28.0 14.7 %collective-permute-start.15 = (f32[256,256]{1,0:T(8,128)S(1)}, f32[256,256]{1,0:T(8,128)S(1)}, u32[]{:S(2)}, u32[]{:S(2)}) collective-permute-start(f32[256,256]{1,0:T(8,128)S(1)} %get-tuple-element.61), channel_id=1, source_target_pairs={{0,1},{1,0},{2,3},{3,2},{4,5},{5,4},{6,7},{7,6},{8,9},{9,8},{10,11... | collective-permute-start | bytes 786440 | tf_op jit(solution)/shard_map/ppermute | solution.py:442
  33.5 9.2 %copy-start.5 = (bf16[2,128,576]{2,1,0:T(8,128)(2,1)S(1)}, bf16[2,128,576]{2,1,0:T(8,128)(2,1)}, u32[]{:S(2)}) copy-start(bf16[2,128,576]{2,1,0:T(8,128)(2,1)} %constant.13.clone.refs_2_) | copy-start | bytes 884740
  33.5 6.5 %collective-permute-start.9 = (f32[136,256]{1,0:T(8,128)S(1)}, f32[136,256]{1,0:T(8,128)S(1)}, u32[]{:S(2)}, u32[]{:S(2)}) collective-permute-start(f32[136,256]{1,0:T(8,128)S(1)} %get-tuple-element.55), channel_id=1, source_target_pairs={{0,2},{1,3},{2,0},{3,1},{4,6},{5,7},{6,4},{7,5},{8,10},{9,11},{10,... | collective-permute-start | bytes 417800 | tf_op jit(solution)/shard_map/ppermute | solution.py:442
  34.8 7.9 %collective-permute-start.10 = (f32[136,256]{1,0:T(8,128)S(1)}, f32[136,256]{1,0:T(8,128)S(1)}, u32[]{:S(2)}, u32[]{:S(2)}) collective-permute-start(f32[136,256]{1,0:T(8,128)S(1)} %get-tuple-element.56.refs_9_), channel_id=1, source_target_pairs={{0,3},{1,2},{2,1},{3,0},{4,7},{5,6},{6,5},{7,4},{8,11},{9,10},{10,... | collective-permute-start | bytes 417800 | tf_op jit(solution)/shard_map/ppermute | solution.py:442
  37.8 5.8 %collective-permute-start.18 = (f32[256,256]{1,0:T(8,128)S(1)}, f32[256,256]{1,0:T(8,128)S(1)}, u32[]{:S(2)}, u32[]{:S(2)}) collective-permute-start(f32[256,256]{1,0:T(8,128)S(1)} %get-tuple-element.68), channel_id=1, source_target_pairs={{0,1},{1,0},{2,3},{3,2},{4,5},{5,4},{6,7},{7,6},{8,9},{9,8},{10,11... | collective-permute-start | bytes 786440 | tf_op jit(solution)/shard_map/ppermute | solution.py:442
  38.7 6.0 %collective-permute-start.12 = (f32[128,256]{1,0:T(8,128)S(1)}, f32[128,256]{1,0:T(8,128)S(1)}, u32[]{:S(2)}, u32[]{:S(2)}) collective-permute-start(f32[128,256]{1,0:T(8,128)S(1)} %get-tuple-element.59), channel_id=1, source_target_pairs={{0,2},{1,3},{2,0},{3,1},{4,6},{5,7},{6,4},{7,5},{8,10},{9,11},{10,... | collective-permute-start | bytes 393224 | tf_op jit(solution)/shard_map/ppermute | solution.py:442
  40.0 7.7 %collective-permute-start.13 = (f32[128,256]{1,0:T(8,128)S(1)}, f32[128,256]{1,0:T(8,128)S(1)}, u32[]{:S(2)}, u32[]{:S(2)}) collective-permute-start(f32[128,256]{1,0:T(8,128)S(1)} %get-tuple-element.60.refs_3_), channel_id=1, source_target_pairs={{0,3},{1,2},{2,1},{3,0},{4,7},{5,6},{6,5},{7,4},{8,11},{9,10},{10,... | collective-permute-start | bytes 393224 | tf_op jit(solution)/shard_map/ppermute | solution.py:442
  43.1 4.7 %collective-permute-start.16 = (f32[128,256]{1,0:T(8,128)S(1)}, f32[128,256]{1,0:T(8,128)S(1)}, u32[]{:S(2)}, u32[]{:S(2)}) collective-permute-start(f32[128,256]{1,0:T(8,128)S(1)} %get-tuple-element.63), channel_id=1, source_target_pairs={{0,1},{1,0},{2,3},{3,2},{4,5},{5,4},{6,7},{7,6},{8,9},{9,8},{10,11... | collective-permute-start | bytes 393224 | tf_op jit(solution)/shard_map/ppermute | solution.py:442
  43.1 4.6 %collective-permute-start.17 = (f32[128,256]{1,0:T(8,128)S(1)}, f32[128,256]{1,0:T(8,128)S(1)}, u32[]{:S(2)}, u32[]{:S(2)}) collective-permute-start(f32[128,256]{1,0:T(8,128)S(1)} %get-tuple-element.64), channel_id=1, source_target_pairs={{0,1},{1,0},{2,3},{3,2},{4,5},{5,4},{6,7},{7,6},{8,9},{9,8},{10,11... | collective-permute-start | bytes 393224 | tf_op jit(solution)/shard_map/ppermute | solution.py:442
  (1 other events, 6.0 us)

commit v21 on v20

--- a/solution.py
+++ b/solution.py
@@ -512,7 +512,7 @@
     (sent,) = call(
         functools.partial(send_kernel, inner, edges, rest, count, cells),
         [(len(inner) * (rest + 8), width)],
-        *inner_blocks, *edge_blocks[:half], send, diagonals, solid_mask, cost=SHORT, earlier=(own,),
+        *inner_blocks, *edge_blocks[:half], send, diagonals, solid_mask, cost=SHORT,
     )
     taken = swap(sent, half)
 

time: 49.6 us -> 48.8 us (0.984); the launches traced: 48.8 us -> 48.6 us
  waiting for transfers between devices: 15.2 us -> 14 us
  starting transfers between devices: 19.2 us -> 20.2 us
    ppermute x2, waiting for transfers between devices: 3.1 us -> 1.95 us  [local(): lax.ppermute(row, 'plane', pair)]
    ppermute x17, starting transfers between devices: 15.9 us -> 16.9 us  [swap(): lax.ppermute(block, 'span', [(i, i ^ d) for i in range(lax.axis_size('spa...]
  transfers between devices with their start and end apart: 19 -> 19, of which waited for: 8 -> 9; matrix products, arithmetic and copies ran while one was open for 0% -> 0% of each run, Pallas kernels for 23% -> 23%
where the time goes in v21:
time: 48.8 us; the launch traced here: 48.6 us
  starting transfers between devices  20.2 us (41%)
  Pallas kernels  14.2 us (29%)
  waiting for transfers between devices  14 us (29%)
    ppermute x17, starting transfers between devices, swap(): lax.ppermute(block, 'span', [(i, i ^ d) for i in range(lax.axis_size('spa...  16.9 us
    ppermute x17, waiting for transfers between devices, swap(): lax.ppermute(block, 'span', [(i, i ^ d) for i in range(lax.axis_size('spa...  12 us
    pallas_call x9, Pallas kernels, call(): pl.pallas_call(kernel, out_shape=shapes, in_specs=[VMEM] * len(args) + [A...  8.08 us
    pallas_call x2, Pallas kernels, pack(): pl.pallas_call(functools.partial(pack_kernel, jobs, row_count, cells, len...  4.01 us
    ppermute x2, starting transfers between devices, local(): lax.ppermute(row, 'plane', pair)  3.26 us
    pallas_call x2, Pallas kernels, local(): pl.pallas_call(functools.partial(unpack_kernel, [piece[1:] for piece in c...  2.11 us
    ppermute x2, waiting for transfers between devices, local(): lax.ppermute(row, 'plane', pair)  1.95 us
  transfers between devices with their start and end apart: 19, of which 9 were waited for; matrix products, arithmetic and copies ran while one was open for 0% of the time, Pallas kernels for 23%

profile of v21, /device:TPU:25, one launch (start us, length us, event | category | flops | bytes accessed | tf_op | source)
XLA Modules:
  0.0 48.6 jit_solution(10280221612407742929)
XLA Ops:
  0.0 1.9 %shard_map.73 = (f32[264,256]{1,0:T(8,128)S(1)}, f32[264,256]{1,0:T(8,128)S(1)}, f32[264,256]{1,0:T(8,128)S(1)}) custom-call(f32[128,32,128]{2,1,0:T(8,128)} %bitcast.10), custom_call_target="tpu_custom_call" | custom-call | bytes 200000000 | tf_op jit(solution)/shard_map/pallas_call | solution.py:466
  2.0 1.3 %collective-permute-start.1 = (f32[264,256]{1,0:T(8,128)S(1)}, f32[264,256]{1,0:T(8,128)S(1)}, u32[]{:S(2)}, u32[]{:S(2)}) collective-permute-start(f32[264,256]{1,0:T(8,128)S(1)} %get-tuple-element.37.refs_0_), channel_id=1, source_target_pairs={{0,2},{1,3},{2,0},{3,1},{4,6},{5,7},{6,4},{7,5},{8,10},{9,11},{10,... | collective-permute-start | bytes 811016 | tf_op jit(solution)/shard_map/ppermute | solution.py:442
  3.3 2.1 %shard_map.74 = (f32[256,256]{1,0:T(8,128)S(1)}, f32[256,256]{1,0:T(8,128)S(1)}, f32[256,256]{1,0:T(8,128)S(1)}, f32[264,256]{1,0:T(8,128)S(1)}, f32[264,256]{1,...) custom-call(f32[128,32,128]{2,1,0:T(8,128)} %bitcast.11, ...), custom_call_target="tpu_custom_call" | custom-call | bytes 200000000 | tf_op jit(solution)/shard_map/pallas_call | solution.py:466
  5.4 1.0 %collective-permute-start.5 = (f32[128,256]{1,0:T(8,128)S(1)}, f32[128,256]{1,0:T(8,128)S(1)}, u32[]{:S(2)}, u32[]{:S(2)}) collective-permute-start(f32[128,256]{1,0:T(8,128)S(1)} %get-tuple-element.50), channel_id=1, source_target_pairs={{0,1},{1,0},{2,3},{3,2},{4,5},{5,4},{6,7},{7,6},{8,9},{9,8},{10,11... | collective-permute-start | bytes 393224 | tf_op jit(solution)/shard_map/ppermute | solution.py:442
  7.8 1.6 %collective-permute-done.1.refs_2_.refs_3_ = f32[264,256]{1,0:T(8,128)S(1)} collective-permute-done((f32[264,256]{1,0:T(8,128)S(1)}, f32[264,256]{1,0:T(8,128)S(1)}, u32[]{:S(2)}, u32[]{:S(2)}) %collective-permute-start.1) | collective-permute-done | bytes 270368 | tf_op jit(solution)/shard_map/ppermute | solution.py:442
  9.4 1.3 %collective-permute-start.7 = (f32[512,256]{1,0:T(8,128)S(1)}, f32[512,256]{1,0:T(8,128)S(1)}, u32[]{:S(2)}, u32[]{:S(2)}) collective-permute-start(f32[512,256]{1,0:T(8,128)S(1)} %shard_map.77.refs_0_), channel_id=1, source_target_pairs={{0,2},{1,3},{2,0},{3,1},{4,6},{5,7},{6,4},{7,5},{8,10},{9,11},{10,... | collective-permute-start | bytes 1572872 | tf_op jit(solution)/shard_map/ppermute | solution.py:442
  10.7 6.2 %collective-permute-done.2.refs_3_ = f32[264,256]{1,0:T(8,128)S(1)} collective-permute-done((f32[264,256]{1,0:T(8,128)S(1)}, f32[264,256]{1,0:T(8,128)S(1)}, u32[]{:S(2)}, u32[]{:S(2)}) %collective-permute-start.2) | collective-permute-done | bytes 270368 | tf_op jit(solution)/shard_map/ppermute | solution.py:442
  18.4 1.2 %collective-permute-start.11 = (f32[368,256]{1,0:T(8,128)S(1)}, f32[368,256]{1,0:T(8,128)S(1)}, u32[]{:S(2)}, u32[]{:S(2)}) collective-permute-start(f32[368,256]{1,0:T(8,128)S(1)} %get-tuple-element.57), channel_id=1, source_target_pairs={{0,4},{4,0},{8,12},{12,8},{16,20},{20,16},{24,28},{28,24},{1,5},{5... | collective-permute-start | bytes 1130504 | tf_op jit(solution)/shard_map/ppermute | solution.py:521
  19.6 2.0 %collective-permute-start.3 = (f32[352,256]{1,0:T(8,128)S(1)}, f32[352,256]{1,0:T(8,128)S(1)}, u32[]{:S(2)}, u32[]{:S(2)}) collective-permute-start(f32[352,256]{1,0:T(8,128)S(1)} %get-tuple-element.44), channel_id=1, source_target_pairs={{4,8},{8,4},{12,16},{16,12},{20,24},{24,20},{5,9},{9,5},{13,17},{1... | collective-permute-start | bytes 1081352 | tf_op jit(solution)/shard_map/ppermute | solution.py:521
  21.7 0.9 %shard_map.82 = f32[368,256]{1,0:T(8,128)S(1)} custom-call(f32[256,256]{1,0:T(8,128)S(1)} %get-tuple-element.45.refs_0_, f32[256,256]{1,0:T(8,128)S(1)} %collective-permute-done.4.refs_1_, f32[264,256]{1,0:T(8,128)S(1)} %get-tuple-element.38.refs_0_.refs_2_, f32[264,256]{1,0:T(8,128)S(1)} %collective-permute-done.refs_1_.refs_3_, ...), custom_call_target="tpu_custom_call" | custom-call | bytes 1024 | tf_op jit(solution)/shard_map/pallas_call | solution.py:431
  22.7 1.6 %collective-permute-start.14 = (f32[368,256]{1,0:T(8,128)S(1)}, f32[368,256]{1,0:T(8,128)S(1)}, u32[]{:S(2)}, u32[]{:S(2)}) collective-permute-start(f32[368,256]{1,0:T(8,128)S(1)} %shard_map.82), channel_id=1, source_target_pairs={{0,2},{1,3},{2,0},{3,1},{4,6},{5,7},{6,4},{7,5},{8,10},{9,11},{10,... | collective-permute-start | bytes 1130504 | tf_op jit(solution)/shard_map/ppermute | solution.py:442
  24.2 2.1 %shard_map.78.refs_9_.refs_1_ = f32[512,256]{1,0:T(8,128)S(1)} custom-call(f32[512,256]{1,0:T(8,128)S(1)} %shard_map.77.refs_0_, f32[264,256]{1,0:T(8,128)S(1)} %get-tuple-element.52.refs_1_, f32[264,256]{1,0:T(8,128)S(1)} %collective-permute-done.8.refs_2_, bf16[2,2,176,384]{3,2,1,0:T(8,128)(2,1)S(1)} %copy-done.1, bf16[2,2,128,528]{3,2,1,0:T(8,128)(2,1)S(1)} %copy-done, ...), custom_call_target="tpu_custom_call" | custom-call | bytes 1024 | tf_op jit(solution)/shard_map/pallas_call | solution.py:431
  26.7 1.6 %shard_map.79 = (f32[256,256]{1,0:T(8,128)S(1)}, f32[256,256]{1,0:T(8,128)S(1)}, f32[2,352,256]{2,1,0:T(8,128)S(1)}) custom-call(f32[256,256]{1,0:T(8,128)S(1)} %get-tuple-element.45.refs_0_, f32[256,256]{1,0:T(8,128)S(1)} %collective-permute-done.4.refs_1_, f32[512,256]{1,0:T(8,128)S(1)} %collective-permute-done.7.refs_2_, ...), custom_call_target="tpu_custom_call" | custom-call | bytes 1024 | tf_op jit(solution)/shard_map/pallas_call | solution.py:431
  28.3 2.2 %collective-permute-start.15 = (f32[256,256]{1,0:T(8,128)S(1)}, f32[256,256]{1,0:T(8,128)S(1)}, u32[]{:S(2)}, u32[]{:S(2)}) collective-permute-start(f32[256,256]{1,0:T(8,128)S(1)} %get-tuple-element.61), channel_id=1, source_target_pairs={{0,1},{1,0},{2,3},{3,2},{4,5},{5,4},{6,7},{7,6},{8,9},{9,8},{10,11... | collective-permute-start | bytes 786440 | tf_op jit(solution)/shard_map/ppermute | solution.py:442
  30.5 1.6 %collective-permute-done.3.refs_3_ = f32[352,256]{1,0:T(8,128)S(1)} collective-permute-done((f32[352,256]{1,0:T(8,128)S(1)}, f32[352,256]{1,0:T(8,128)S(1)}, u32[]{:S(2)}, u32[]{:S(2)}) %collective-permute-start.3) | collective-permute-done | bytes 360480 | tf_op jit(solution)/shard_map/ppermute | solution.py:521
  32.1 1.1 %shard_map.80 = (f32[128,256]{1,0:T(8,128)S(1)}, f32[128,256]{1,0:T(8,128)S(1)}, f32[136,256]{1,0:T(8,128)S(1)}, f32[136,256]{1,0:T(8,128)S(1)}) custom-call(f32[2,352,256]{2,1,0:T(8,128)S(1)} %get-tuple-element.41.refs_0_, f32[2,352,256]{2,1,0:T(8,128)S(1)} %get-tuple-element.42.refs_7_.refs_1_, f32[352,16]{1,0:T(8,128)S(1)} %get-tuple-element.43.refs_2_.refs_8_, ...), custom_call_target="tpu_custom_call" | custom-call | bytes 1024 | tf_op jit(solution)/shard_map/pallas_call | solution.py:431
  33.2 1.6 %collective-permute-start.9 = (f32[136,256]{1,0:T(8,128)S(1)}, f32[136,256]{1,0:T(8,128)S(1)}, u32[]{:S(2)}, u32[]{:S(2)}) collective-permute-start(f32[136,256]{1,0:T(8,128)S(1)} %get-tuple-element.55), channel_id=1, source_target_pairs={{0,2},{1,3},{2,0},{3,1},{4,6},{5,7},{6,4},{7,5},{8,10},{9,11},{10,... | collective-permute-start | bytes 417800 | tf_op jit(solution)/shard_map/ppermute | solution.py:442
  34.8 1.3 %collective-permute-start.10 = (f32[136,256]{1,0:T(8,128)S(1)}, f32[136,256]{1,0:T(8,128)S(1)}, u32[]{:S(2)}, u32[]{:S(2)}) collective-permute-start(f32[136,256]{1,0:T(8,128)S(1)} %get-tuple-element.56.refs_9_), channel_id=1, source_target_pairs={{0,3},{1,2},{2,1},{3,0},{4,7},{5,6},{6,5},{7,4},{8,11},{9,10},{10,... | collective-permute-start | bytes 417800 | tf_op jit(solution)/shard_map/ppermute | solution.py:442
  36.5 1.1 %shard_map.81 = (f32[128,256]{1,0:T(8,128)S(1)}, f32[256,256]{1,0:T(8,128)S(1)}, f32[128,256]{1,0:T(8,128)S(1)}, f32[128,256]{1,0:T(8,128)S(1)}) custom-call(f32[2,352,256]{2,1,0:T(8,128)S(1)} %get-tuple-element.41.refs_0_, f32[2,352,256]{2,1,0:T(8,128)S(1)} %get-tuple-element.42.refs_7_.refs_1_, f32[352,16]{1,0:T(8,128)S(1)} %get-tuple-element.43.refs_2_.refs_8_, ...), custom_call_target="tpu_custom_call" | custom-call | bytes 200000000 | tf_op jit(solution)/shard_map/pallas_call | solution.py:431
  38.5 1.5 %collective-permute-start.12 = (f32[128,256]{1,0:T(8,128)S(1)}, f32[128,256]{1,0:T(8,128)S(1)}, u32[]{:S(2)}, u32[]{:S(2)}) collective-permute-start(f32[128,256]{1,0:T(8,128)S(1)} %get-tuple-element.59), channel_id=1, source_target_pairs={{0,2},{1,3},{2,0},{3,1},{4,6},{5,7},{6,4},{7,5},{8,10},{9,11},{10,... | collective-permute-start | bytes 393224 | tf_op jit(solution)/shard_map/ppermute | solution.py:442
  40.0 2.2 %collective-permute-start.13 = (f32[128,256]{1,0:T(8,128)S(1)}, f32[128,256]{1,0:T(8,128)S(1)}, u32[]{:S(2)}, u32[]{:S(2)}) collective-permute-start(f32[128,256]{1,0:T(8,128)S(1)} %get-tuple-element.60.refs_3_), channel_id=1, source_target_pairs={{0,3},{1,2},{2,1},{3,0},{4,7},{5,6},{6,5},{7,4},{8,11},{9,10},{10,... | collective-permute-start | bytes 393224 | tf_op jit(solution)/shard_map/ppermute | solution.py:442
  43.2 1.1 %shard_map.84.refs_7_ = f32[128,32,128]{2,1,0:T(8,128)} custom-call(f32[256,256]{1,0:T(8,128)S(1)} %get-tuple-element.65.refs_0_, f32[256,256]{1,0:T(8,128)S(1)} %collective-permute-done.15.refs_6_.refs_1_, f32[128,256]{1,0:T(8,128)S(1)} %get-tuple-element.66.refs_2_, f32[128,256]{1,0:T(8,128)S(1)} %get-tuple-element.67.refs_3_, ...), custom_call_target="tpu_custom_call" | custom-call | bytes 200000000 | tf_op jit(solution)/shard_map/pallas_call | solution.py:560
  44.7 2.8 %collective-permute-done.13.refs_3_ = f32[128,256]{1,0:T(8,128)S(1)} collective-permute-done((f32[128,256]{1,0:T(8,128)S(1)}, f32[128,256]{1,0:T(8,128)S(1)}, u32[]{:S(2)}, u32[]{:S(2)}) %collective-permute-start.13) | collective-permute-done | bytes 131104 | tf_op jit(solution)/shard_map/ppermute | solution.py:442
  47.5 1.1 %shard_map.85 = f32[128,32,128]{2,1,0:T(8,128)} custom-call(f32[136,256]{1,0:T(8,128)S(1)} %collective-permute-done.9.refs_4_.refs_0_, f32[136,256]{1,0:T(8,128)S(1)} %collective-permute-done.10.refs_5_.refs_1_, f32[128,256]{1,0:T(8,128)S(1)} %collective-permute-done.12.refs_2_, ...), custom_call_target="tpu_custom_call", output_to_operand_aliasing={{}: (7, {})} | custom-call | bytes 1024 | tf_op jit(solution)/shard_map/pallas_call | solution.py:560
  (39 shorter events, 5.9 us)
Async XLA Ops:
  1.9 15.0 %copy-start.1 = (bf16[2,2,176,384]{3,2,1,0:T(8,128)(2,1)S(1)}, bf16[2,2,176,384]{3,2,1,0:T(8,128)(2,1)}, u32[]{:S(2)}) copy-start(bf16[2,2,176,384]{3,2,1,0:T(8,128)(2,1)} %constant.10.clone.refs_4_.refs_3_) | copy-start | bytes 1622020
  1.9 15.0 %copy-start.2 = (s32[4,1024]{1,0:T(4,128)S(1)}, s32[4,1024]{1,0:T(4,128)}, u32[]{:S(2)}) copy-start(s32[4,1024]{1,0:T(4,128)} %refs_6_.9) | copy-start | bytes 49156
  2.0 15.0 %copy-start.3 = (f32[8,384]{1,0:T(8,128)S(1)}, f32[8,384]{1,0:T(8,128)}, u32[]{:S(2)}) copy-start(f32[8,384]{1,0:T(8,128)} %constant.14.clone.refs_5_.refs_6_) | copy-start | bytes 36868
  2.0 7.4 %collective-permute-start.1 = (f32[264,256]{1,0:T(8,128)S(1)}, f32[264,256]{1,0:T(8,128)S(1)}, u32[]{:S(2)}, u32[]{:S(2)}) collective-permute-start(f32[264,256]{1,0:T(8,128)S(1)} %get-tuple-element.37.refs_0_), channel_id=1, source_target_pairs={{0,2},{1,3},{2,0},{3,1},{4,6},{5,7},{6,4},{7,5},{8,10},{9,11},{10,... | collective-permute-start | bytes 811016 | tf_op jit(solution)/shard_map/ppermute | solution.py:442
  5.4 16.3 %copy-start.4 = (bf16[2,224,384]{2,1,0:T(8,128)(2,1)S(1)}, bf16[2,224,384]{2,1,0:T(8,128)(2,1)}, u32[]{:S(2)}) copy-start(bf16[2,224,384]{2,1,0:T(8,128)(2,1)} %constant.12.clone.refs_4_) | copy-start | bytes 1032196
  5.4 2.0 %collective-permute-start.5 = (f32[128,256]{1,0:T(8,128)S(1)}, f32[128,256]{1,0:T(8,128)S(1)}, u32[]{:S(2)}, u32[]{:S(2)}) collective-permute-start(f32[128,256]{1,0:T(8,128)S(1)} %get-tuple-element.50), channel_id=1, source_target_pairs={{0,1},{1,0},{2,3},{3,2},{4,5},{5,4},{6,7},{7,6},{8,9},{9,8},{10,11... | collective-permute-start | bytes 393224 | tf_op jit(solution)/shard_map/ppermute | solution.py:442
  6.4 1.3 %collective-permute-start.6 = (f32[128,256]{1,0:T(8,128)S(1)}, f32[128,256]{1,0:T(8,128)S(1)}, u32[]{:S(2)}, u32[]{:S(2)}) collective-permute-start(f32[128,256]{1,0:T(8,128)S(1)} %get-tuple-element.51), channel_id=1, source_target_pairs={{0,1},{1,0},{2,3},{3,2},{4,5},{5,4},{6,7},{7,6},{8,9},{9,8},{10,11... | collective-permute-start | bytes 393224 | tf_op jit(solution)/shard_map/ppermute | solution.py:442
  6.5 4.2 %collective-permute-start = (f32[264,256]{1,0:T(8,128)S(1)}, f32[264,256]{1,0:T(8,128)S(1)}, u32[]{:S(2)}, u32[]{:S(2)}) collective-permute-start(f32[264,256]{1,0:T(8,128)S(1)} %get-tuple-element.39), channel_id=1, source_target_pairs={{0,1},{1,0},{2,3},{3,2},{4,5},{5,4},{6,7},{7,6},{8,9},{9,8},{10,11... | collective-permute-start | bytes 811016 | tf_op jit(solution)/shard_map/ppermute | solution.py:442
  6.9 10.0 %collective-permute-start.2 = (f32[264,256]{1,0:T(8,128)S(1)}, f32[264,256]{1,0:T(8,128)S(1)}, u32[]{:S(2)}, u32[]{:S(2)}) collective-permute-start(f32[264,256]{1,0:T(8,128)S(1)} %get-tuple-element.40), channel_id=1, source_target_pairs={{0,3},{1,2},{2,1},{3,0},{4,7},{5,6},{6,5},{7,4},{8,11},{9,10},{10,... | collective-permute-start | bytes 811016 | tf_op jit(solution)/shard_map/ppermute | solution.py:442
  9.4 17.3 %collective-permute-start.7 = (f32[512,256]{1,0:T(8,128)S(1)}, f32[512,256]{1,0:T(8,128)S(1)}, u32[]{:S(2)}, u32[]{:S(2)}) collective-permute-start(f32[512,256]{1,0:T(8,128)S(1)} %shard_map.77.refs_0_), channel_id=1, source_target_pairs={{0,2},{1,3},{2,0},{3,1},{4,6},{5,7},{6,4},{7,5},{8,10},{9,11},{10,... | collective-permute-start | bytes 1572872 | tf_op jit(solution)/shard_map/ppermute | solution.py:442
  17.8 3.8 %collective-permute-start.4 = (f32[256,256]{1,0:T(8,128)S(1)}, f32[256,256]{1,0:T(8,128)S(1)}, u32[]{:S(2)}, u32[]{:S(2)}) collective-permute-start(f32[256,256]{1,0:T(8,128)S(1)} %get-tuple-element.48), channel_id=1, source_target_pairs={{0,1},{1,0},{2,3},{3,2},{4,5},{5,4},{6,7},{7,6},{8,9},{9,8},{10,11... | collective-permute-start | bytes 786440 | tf_op jit(solution)/shard_map/ppermute | solution.py:442
  17.9 6.3 %collective-permute-start.8 = (f32[264,256]{1,0:T(8,128)S(1)}, f32[264,256]{1,0:T(8,128)S(1)}, u32[]{:S(2)}, u32[]{:S(2)}) collective-permute-start(f32[264,256]{1,0:T(8,128)S(1)} %get-tuple-element.53), channel_id=1, source_target_pairs={{0,1},{1,0},{2,3},{3,2},{4,5},{5,4},{6,7},{7,6},{8,9},{9,8},{10,11... | collective-permute-start | bytes 811016 | tf_op jit(solution)/shard_map/ppermute | solution.py:442
  18.4 18.1 %collective-permute-start.11 = (f32[368,256]{1,0:T(8,128)S(1)}, f32[368,256]{1,0:T(8,128)S(1)}, u32[]{:S(2)}, u32[]{:S(2)}) collective-permute-start(f32[368,256]{1,0:T(8,128)S(1)} %get-tuple-element.57), channel_id=1, source_target_pairs={{0,4},{4,0},{8,12},{12,8},{16,20},{20,16},{24,28},{28,24},{1,5},{5... | collective-permute-start | bytes 1130504 | tf_op jit(solution)/shard_map/ppermute | solution.py:521
  19.6 12.5 %collective-permute-start.3 = (f32[352,256]{1,0:T(8,128)S(1)}, f32[352,256]{1,0:T(8,128)S(1)}, u32[]{:S(2)}, u32[]{:S(2)}) collective-permute-start(f32[352,256]{1,0:T(8,128)S(1)} %get-tuple-element.44), channel_id=1, source_target_pairs={{4,8},{8,4},{12,16},{16,12},{20,24},{24,20},{5,9},{9,5},{13,17},{1... | collective-permute-start | bytes 1081352 | tf_op jit(solution)/shard_map/ppermute | solution.py:521
  22.7 15.8 %collective-permute-start.14 = (f32[368,256]{1,0:T(8,128)S(1)}, f32[368,256]{1,0:T(8,128)S(1)}, u32[]{:S(2)}, u32[]{:S(2)}) collective-permute-start(f32[368,256]{1,0:T(8,128)S(1)} %shard_map.82), channel_id=1, source_target_pairs={{0,2},{1,3},{2,0},{3,1},{4,6},{5,7},{6,4},{7,5},{8,10},{9,11},{10,... | collective-permute-start | bytes 1130504 | tf_op jit(solution)/shard_map/ppermute | solution.py:442
  28.3 14.0 %collective-permute-start.15 = (f32[256,256]{1,0:T(8,128)S(1)}, f32[256,256]{1,0:T(8,128)S(1)}, u32[]{:S(2)}, u32[]{:S(2)}) collective-permute-start(f32[256,256]{1,0:T(8,128)S(1)} %get-tuple-element.61), channel_id=1, source_target_pairs={{0,1},{1,0},{2,3},{3,2},{4,5},{5,4},{6,7},{7,6},{8,9},{9,8},{10,11... | collective-permute-start | bytes 786440 | tf_op jit(solution)/shard_map/ppermute | solution.py:442
  33.2 9.1 %copy-start.5 = (bf16[2,128,576]{2,1,0:T(8,128)(2,1)S(1)}, bf16[2,128,576]{2,1,0:T(8,128)(2,1)}, u32[]{:S(2)}) copy-start(bf16[2,128,576]{2,1,0:T(8,128)(2,1)} %constant.13.clone.refs_2_) | copy-start | bytes 884740
  33.2 6.8 %collective-permute-start.9 = (f32[136,256]{1,0:T(8,128)S(1)}, f32[136,256]{1,0:T(8,128)S(1)}, u32[]{:S(2)}, u32[]{:S(2)}) collective-permute-start(f32[136,256]{1,0:T(8,128)S(1)} %get-tuple-element.55), channel_id=1, source_target_pairs={{0,2},{1,3},{2,0},{3,1},{4,6},{5,7},{6,4},{7,5},{8,10},{9,11},{10,... | collective-permute-start | bytes 417800 | tf_op jit(solution)/shard_map/ppermute | solution.py:442
  34.8 7.5 %collective-permute-start.10 = (f32[136,256]{1,0:T(8,128)S(1)}, f32[136,256]{1,0:T(8,128)S(1)}, u32[]{:S(2)}, u32[]{:S(2)}) collective-permute-start(f32[136,256]{1,0:T(8,128)S(1)} %get-tuple-element.56.refs_9_), channel_id=1, source_target_pairs={{0,3},{1,2},{2,1},{3,0},{4,7},{5,6},{6,5},{7,4},{8,11},{9,10},{10,... | collective-permute-start | bytes 417800 | tf_op jit(solution)/shard_map/ppermute | solution.py:442
  37.6 5.7 %collective-permute-start.18 = (f32[256,256]{1,0:T(8,128)S(1)}, f32[256,256]{1,0:T(8,128)S(1)}, u32[]{:S(2)}, u32[]{:S(2)}) collective-permute-start(f32[256,256]{1,0:T(8,128)S(1)} %get-tuple-element.68), channel_id=1, source_target_pairs={{0,1},{1,0},{2,3},{3,2},{4,5},{5,4},{6,7},{7,6},{8,9},{9,8},{10,11... | collective-permute-start | bytes 786440 | tf_op jit(solution)/shard_map/ppermute | solution.py:442
  38.5 6.2 %collective-permute-start.12 = (f32[128,256]{1,0:T(8,128)S(1)}, f32[128,256]{1,0:T(8,128)S(1)}, u32[]{:S(2)}, u32[]{:S(2)}) collective-permute-start(f32[128,256]{1,0:T(8,128)S(1)} %get-tuple-element.59), channel_id=1, source_target_pairs={{0,2},{1,3},{2,0},{3,1},{4,6},{5,7},{6,4},{7,5},{8,10},{9,11},{10,... | collective-permute-start | bytes 393224 | tf_op jit(solution)/shard_map/ppermute | solution.py:442
  40.0 7.5 %collective-permute-start.13 = (f32[128,256]{1,0:T(8,128)S(1)}, f32[128,256]{1,0:T(8,128)S(1)}, u32[]{:S(2)}, u32[]{:S(2)}) collective-permute-start(f32[128,256]{1,0:T(8,128)S(1)} %get-tuple-element.60.refs_3_), channel_id=1, source_target_pairs={{0,3},{1,2},{2,1},{3,0},{4,7},{5,6},{6,5},{7,4},{8,11},{9,10},{10,... | collective-permute-start | bytes 393224 | tf_op jit(solution)/shard_map/ppermute | solution.py:442
  42.6 4.9 %collective-permute-start.16 = (f32[128,256]{1,0:T(8,128)S(1)}, f32[128,256]{1,0:T(8,128)S(1)}, u32[]{:S(2)}, u32[]{:S(2)}) collective-permute-start(f32[128,256]{1,0:T(8,128)S(1)} %get-tuple-element.63), channel_id=1, source_target_pairs={{0,1},{1,0},{2,3},{3,2},{4,5},{5,4},{6,7},{7,6},{8,9},{9,8},{10,11... | collective-permute-start | bytes 393224 | tf_op jit(solution)/shard_map/ppermute | solution.py:442
  42.8 4.7 %collective-permute-start.17 = (f32[128,256]{1,0:T(8,128)S(1)}, f32[128,256]{1,0:T(8,128)S(1)}, u32[]{:S(2)}, u32[]{:S(2)}) collective-permute-start(f32[128,256]{1,0:T(8,128)S(1)} %get-tuple-element.64), channel_id=1, source_target_pairs={{0,1},{1,0},{2,3},{3,2},{4,5},{5,4},{6,7},{7,6},{8,9},{9,8},{10,11... | collective-permute-start | bytes 393224 | tf_op jit(solution)/shard_map/ppermute | solution.py:442
  (1 other events, 7.3 us)

commit v22 on v21

--- a/solution.py
+++ b/solution.py
@@ -16,7 +16,7 @@
 PARAMS = pltpu.CompilerParams(vmem_limit_bytes=24 * 1024 * 1024)
 LONG = pl.CostEstimate(flops=0, bytes_accessed=200_000_000, transcendentals=0)
 SHORT = pl.CostEstimate(flops=0, bytes_accessed=1024, transcendentals=0)
-SPLIT = 4
+SPLIT = 8
 
 
 def split(values):
@@ -532,7 +532,7 @@
     for order, name in enumerate(("far", "near")):
         outs = call(
             functools.partial(rim_kernel, edges, order, count, cells),
-            [(cells, width)] + [((order + 1) * cells, width)] * (half - 1) + [(cells + 8 * (1 - order), width)] * half,
+            [(cells, width)] + [((order + 1) * cells, width)] * (half - 1) + [(cells, width)] * (half - 1) + [(cells + 8 * (1 - order), width)],
             spectrum, edge_ones, sides, halos[1 - order], ones, inverse, diagonals, solid_mask, *near_rim,
             cost=LONG if order else SHORT, earlier=earlier,
         )

time: 48.8 us -> 49.4 us (1.012)
  waiting for transfers between devices: 14 us -> 13.3 us
  Pallas kernels: 14.2 us -> 14.7 us
    pallas_call x2, Pallas kernels: 4.01 us -> 4.53 us  [pack(): pl.pallas_call(functools.partial(pack_kernel, jobs, row_count, cells, len...]
    ppermute x2, waiting for transfers between devices: 1.95 us -> 1.44 us  [local(): lax.ppermute(row, 'plane', pair)]
  transfers between devices with their start and end apart: 19 -> 19, of which waited for: 9 -> 8; matrix products, arithmetic and copies ran while one was open for 0% -> 0% of each run, Pallas kernels for 23% -> 24%
where the time goes in v22:
time: 49.4 us; the launch traced here: 48.8 us
  starting transfers between devices  20.6 us (42%)
  Pallas kernels  14.7 us (30%)
  waiting for transfers between devices  13.3 us (27%)
    ppermute x17, starting transfers between devices, swap(): lax.ppermute(block, 'span', [(i, i ^ d) for i in range(lax.axis_size('spa...  17.4 us
    ppermute x17, waiting for transfers between devices, swap(): lax.ppermute(block, 'span', [(i, i ^ d) for i in range(lax.axis_size('spa...  11.8 us
    pallas_call x9, Pallas kernels, call(): pl.pallas_call(kernel, out_shape=shapes, in_specs=[VMEM] * len(args) + [A...  8.08 us
    pallas_call x2, Pallas kernels, pack(): pl.pallas_call(functools.partial(pack_kernel, jobs, row_count, cells, len...  4.53 us
    ppermute x2, starting transfers between devices, local(): lax.ppermute(row, 'plane', pair)  3.25 us
    pallas_call x2, Pallas kernels, local(): pl.pallas_call(functools.partial(unpack_kernel, [piece[1:] for piece in c...  2.12 us
    ppermute x2, waiting for transfers between devices, local(): lax.ppermute(row, 'plane', pair)  1.44 us
  transfers between devices with their start and end apart: 19, of which 8 were waited for; matrix products, arithmetic and copies ran while one was open for 0% of the time, Pallas kernels for 24%

profile of v22, /device:TPU:25, one launch (start us, length us, event | category | flops | bytes accessed | tf_op | source)
XLA Modules:
  0.0 48.8 jit_solution(7836296342393043677)
XLA Ops:
  0.0 2.2 %shard_map.73 = (f32[264,256]{1,0:T(8,128)S(1)}, f32[264,256]{1,0:T(8,128)S(1)}, f32[264,256]{1,0:T(8,128)S(1)}) custom-call(f32[128,32,128]{2,1,0:T(8,128)} %bitcast.10), custom_call_target="tpu_custom_call" | custom-call | bytes 200000000 | tf_op jit(solution)/shard_map/pallas_call | solution.py:466
  2.2 1.3 %collective-permute-start.1 = (f32[264,256]{1,0:T(8,128)S(1)}, f32[264,256]{1,0:T(8,128)S(1)}, u32[]{:S(2)}, u32[]{:S(2)}) collective-permute-start(f32[264,256]{1,0:T(8,128)S(1)} %get-tuple-element.37.refs_0_), channel_id=1, source_target_pairs={{0,2},{1,3},{2,0},{3,1},{4,6},{5,7},{6,4},{7,5},{8,10},{9,11},{10,... | collective-permute-start | bytes 811016 | tf_op jit(solution)/shard_map/ppermute | solution.py:442
  3.5 2.4 %shard_map.74 = (f32[256,256]{1,0:T(8,128)S(1)}, f32[256,256]{1,0:T(8,128)S(1)}, f32[256,256]{1,0:T(8,128)S(1)}, f32[264,256]{1,0:T(8,128)S(1)}, f32[264,256]{1,...) custom-call(f32[128,32,128]{2,1,0:T(8,128)} %bitcast.11, ...), custom_call_target="tpu_custom_call" | custom-call | bytes 200000000 | tf_op jit(solution)/shard_map/pallas_call | solution.py:466
  8.3 1.4 %collective-permute-done.1.refs_2_.refs_3_ = f32[264,256]{1,0:T(8,128)S(1)} collective-permute-done((f32[264,256]{1,0:T(8,128)S(1)}, f32[264,256]{1,0:T(8,128)S(1)}, u32[]{:S(2)}, u32[]{:S(2)}) %collective-permute-start.1) | collective-permute-done | bytes 270368 | tf_op jit(solution)/shard_map/ppermute | solution.py:442
  9.7 1.3 %collective-permute-start.7 = (f32[512,256]{1,0:T(8,128)S(1)}, f32[512,256]{1,0:T(8,128)S(1)}, u32[]{:S(2)}, u32[]{:S(2)}) collective-permute-start(f32[512,256]{1,0:T(8,128)S(1)} %shard_map.77.refs_0_), channel_id=1, source_target_pairs={{0,2},{1,3},{2,0},{3,1},{4,6},{5,7},{6,4},{7,5},{8,10},{9,11},{10,... | collective-permute-start | bytes 1572872 | tf_op jit(solution)/shard_map/ppermute | solution.py:442
  11.0 5.9 %collective-permute-done.2.refs_3_ = f32[264,256]{1,0:T(8,128)S(1)} collective-permute-done((f32[264,256]{1,0:T(8,128)S(1)}, f32[264,256]{1,0:T(8,128)S(1)}, u32[]{:S(2)}, u32[]{:S(2)}) %collective-permute-start.2) | collective-permute-done | bytes 270368 | tf_op jit(solution)/shard_map/ppermute | solution.py:442
  18.4 1.2 %collective-permute-start.11 = (f32[368,256]{1,0:T(8,128)S(1)}, f32[368,256]{1,0:T(8,128)S(1)}, u32[]{:S(2)}, u32[]{:S(2)}) collective-permute-start(f32[368,256]{1,0:T(8,128)S(1)} %get-tuple-element.57), channel_id=1, source_target_pairs={{0,4},{4,0},{8,12},{12,8},{16,20},{20,16},{24,28},{28,24},{1,5},{5... | collective-permute-start | bytes 1130504 | tf_op jit(solution)/shard_map/ppermute | solution.py:521
  19.6 2.0 %collective-permute-start.3 = (f32[352,256]{1,0:T(8,128)S(1)}, f32[352,256]{1,0:T(8,128)S(1)}, u32[]{:S(2)}, u32[]{:S(2)}) collective-permute-start(f32[352,256]{1,0:T(8,128)S(1)} %get-tuple-element.44), channel_id=1, source_target_pairs={{4,8},{8,4},{12,16},{16,12},{20,24},{24,20},{5,9},{9,5},{13,17},{1... | collective-permute-start | bytes 1081352 | tf_op jit(solution)/shard_map/ppermute | solution.py:521
  22.6 1.9 %collective-permute-start.14 = (f32[368,256]{1,0:T(8,128)S(1)}, f32[368,256]{1,0:T(8,128)S(1)}, u32[]{:S(2)}, u32[]{:S(2)}) collective-permute-start(f32[368,256]{1,0:T(8,128)S(1)} %shard_map.82), channel_id=1, source_target_pairs={{0,2},{1,3},{2,0},{3,1},{4,6},{5,7},{6,4},{7,5},{8,10},{9,11},{10,... | collective-permute-start | bytes 1130504 | tf_op jit(solution)/shard_map/ppermute | solution.py:442
  24.5 2.1 %shard_map.78.refs_9_.refs_1_ = f32[512,256]{1,0:T(8,128)S(1)} custom-call(f32[512,256]{1,0:T(8,128)S(1)} %shard_map.77.refs_0_, f32[264,256]{1,0:T(8,128)S(1)} %get-tuple-element.52.refs_1_, f32[264,256]{1,0:T(8,128)S(1)} %collective-permute-done.8.refs_2_, bf16[2,2,176,384]{3,2,1,0:T(8,128)(2,1)S(1)} %copy-done.1, bf16[2,2,128,528]{3,2,1,0:T(8,128)(2,1)S(1)} %copy-done, ...), custom_call_target="tpu_custom_call" | custom-call | bytes 1024 | tf_op jit(solution)/shard_map/pallas_call | solution.py:431
  27.2 1.6 %shard_map.79 = (f32[256,256]{1,0:T(8,128)S(1)}, f32[256,256]{1,0:T(8,128)S(1)}, f32[2,352,256]{2,1,0:T(8,128)S(1)}) custom-call(f32[256,256]{1,0:T(8,128)S(1)} %get-tuple-element.45.refs_0_, f32[256,256]{1,0:T(8,128)S(1)} %collective-permute-done.4.refs_1_, f32[512,256]{1,0:T(8,128)S(1)} %collective-permute-done.7.refs_2_, ...), custom_call_target="tpu_custom_call" | custom-call | bytes 1024 | tf_op jit(solution)/shard_map/pallas_call | solution.py:431
  28.8 1.7 %collective-permute-start.15 = (f32[256,256]{1,0:T(8,128)S(1)}, f32[256,256]{1,0:T(8,128)S(1)}, u32[]{:S(2)}, u32[]{:S(2)}) collective-permute-start(f32[256,256]{1,0:T(8,128)S(1)} %get-tuple-element.61), channel_id=1, source_target_pairs={{0,1},{1,0},{2,3},{3,2},{4,5},{5,4},{6,7},{7,6},{8,9},{9,8},{10,11... | collective-permute-start | bytes 786440 | tf_op jit(solution)/shard_map/ppermute | solution.py:442
  30.5 1.4 %collective-permute-done.3.refs_3_ = f32[352,256]{1,0:T(8,128)S(1)} collective-permute-done((f32[352,256]{1,0:T(8,128)S(1)}, f32[352,256]{1,0:T(8,128)S(1)}, u32[]{:S(2)}, u32[]{:S(2)}) %collective-permute-start.3) | collective-permute-done | bytes 360480 | tf_op jit(solution)/shard_map/ppermute | solution.py:521
  31.9 1.1 %shard_map.80 = (f32[128,256]{1,0:T(8,128)S(1)}, f32[128,256]{1,0:T(8,128)S(1)}, f32[128,256]{1,0:T(8,128)S(1)}, f32[136,256]{1,0:T(8,128)S(1)}) custom-call(f32[2,352,256]{2,1,0:T(8,128)S(1)} %get-tuple-element.41.refs_0_, f32[2,352,256]{2,1,0:T(8,128)S(1)} %get-tuple-element.42.refs_7_.refs_1_, f32[352,16]{1,0:T(8,128)S(1)} %get-tuple-element.43.refs_2_.refs_8_, ...), custom_call_target="tpu_custom_call" | custom-call | bytes 1024 | tf_op jit(solution)/shard_map/pallas_call | solution.py:431
  33.0 3.2 %collective-permute-start.10 = (f32[136,256]{1,0:T(8,128)S(1)}, f32[136,256]{1,0:T(8,128)S(1)}, u32[]{:S(2)}, u32[]{:S(2)}) collective-permute-start(f32[136,256]{1,0:T(8,128)S(1)} %get-tuple-element.56.refs_9_), channel_id=1, source_target_pairs={{0,3},{1,2},{2,1},{3,0},{4,7},{5,6},{6,5},{7,4},{8,11},{9,10},{10,... | collective-permute-start | bytes 417800 | tf_op jit(solution)/shard_map/ppermute | solution.py:442
  36.2 1.1 %shard_map.81 = (f32[128,256]{1,0:T(8,128)S(1)}, f32[256,256]{1,0:T(8,128)S(1)}, f32[128,256]{1,0:T(8,128)S(1)}, f32[128,256]{1,0:T(8,128)S(1)}) custom-call(f32[2,352,256]{2,1,0:T(8,128)S(1)} %get-tuple-element.41.refs_0_, f32[2,352,256]{2,1,0:T(8,128)S(1)} %get-tuple-element.42.refs_7_.refs_1_, f32[352,16]{1,0:T(8,128)S(1)} %get-tuple-element.43.refs_2_.refs_8_, ...), custom_call_target="tpu_custom_call" | custom-call | bytes 200000000 | tf_op jit(solution)/shard_map/pallas_call | solution.py:431
  37.3 1.2 %collective-permute-start.18 = (f32[256,256]{1,0:T(8,128)S(1)}, f32[256,256]{1,0:T(8,128)S(1)}, u32[]{:S(2)}, u32[]{:S(2)}) collective-permute-start(f32[256,256]{1,0:T(8,128)S(1)} %get-tuple-element.68), channel_id=1, source_target_pairs={{0,1},{1,0},{2,3},{3,2},{4,5},{5,4},{6,7},{7,6},{8,9},{9,8},{10,11... | collective-permute-start | bytes 786440 | tf_op jit(solution)/shard_map/ppermute | solution.py:442
  38.4 1.8 %collective-permute-start.12 = (f32[128,256]{1,0:T(8,128)S(1)}, f32[128,256]{1,0:T(8,128)S(1)}, u32[]{:S(2)}, u32[]{:S(2)}) collective-permute-start(f32[128,256]{1,0:T(8,128)S(1)} %get-tuple-element.59), channel_id=1, source_target_pairs={{0,2},{1,3},{2,0},{3,1},{4,6},{5,7},{6,4},{7,5},{8,10},{9,11},{10,... | collective-permute-start | bytes 393224 | tf_op jit(solution)/shard_map/ppermute | solution.py:442
  40.2 2.1 %collective-permute-done.9.refs_4_.refs_0_ = f32[128,256]{1,0:T(8,128)S(1)} collective-permute-done((f32[128,256]{1,0:T(8,128)S(1)}, f32[128,256]{1,0:T(8,128)S(1)}, u32[]{:S(2)}, u32[]{:S(2)}) %collective-permute-start.9) | collective-permute-done | bytes 131104 | tf_op jit(solution)/shard_map/ppermute | solution.py:442
  42.4 1.5 %collective-permute-start.13 = (f32[128,256]{1,0:T(8,128)S(1)}, f32[128,256]{1,0:T(8,128)S(1)}, u32[]{:S(2)}, u32[]{:S(2)}) collective-permute-start(f32[128,256]{1,0:T(8,128)S(1)} %get-tuple-element.60.refs_3_), channel_id=1, source_target_pairs={{0,3},{1,2},{2,1},{3,0},{4,7},{5,6},{6,5},{7,4},{8,11},{9,10},{10,... | collective-permute-start | bytes 393224 | tf_op jit(solution)/shard_map/ppermute | solution.py:442
  44.3 1.2 %collective-permute-start.16 = (f32[128,256]{1,0:T(8,128)S(1)}, f32[128,256]{1,0:T(8,128)S(1)}, u32[]{:S(2)}, u32[]{:S(2)}) collective-permute-start(f32[128,256]{1,0:T(8,128)S(1)} %get-tuple-element.63), channel_id=1, source_target_pairs={{0,1},{1,0},{2,3},{3,2},{4,5},{5,4},{6,7},{7,6},{8,9},{9,8},{10,11... | collective-permute-start | bytes 393224 | tf_op jit(solution)/shard_map/ppermute | solution.py:442
  45.5 1.1 %shard_map.84.refs_7_ = f32[128,32,128]{2,1,0:T(8,128)} custom-call(f32[256,256]{1,0:T(8,128)S(1)} %get-tuple-element.65.refs_0_, f32[256,256]{1,0:T(8,128)S(1)} %collective-permute-done.15.refs_6_.refs_1_, f32[128,256]{1,0:T(8,128)S(1)} %get-tuple-element.66.refs_2_, f32[128,256]{1,0:T(8,128)S(1)} %get-tuple-element.67.refs_3_, ...), custom_call_target="tpu_custom_call" | custom-call | bytes 200000000 | tf_op jit(solution)/shard_map/pallas_call | solution.py:560
  46.6 1.2 %collective-permute-done.13.refs_3_ = f32[128,256]{1,0:T(8,128)S(1)} collective-permute-done((f32[128,256]{1,0:T(8,128)S(1)}, f32[128,256]{1,0:T(8,128)S(1)}, u32[]{:S(2)}, u32[]{:S(2)}) %collective-permute-start.13) | collective-permute-done | bytes 131104 | tf_op jit(solution)/shard_map/ppermute | solution.py:442
  47.8 1.1 %shard_map.85 = f32[128,32,128]{2,1,0:T(8,128)} custom-call(f32[128,256]{1,0:T(8,128)S(1)} %collective-permute-done.9.refs_4_.refs_0_, f32[136,256]{1,0:T(8,128)S(1)} %collective-permute-done.10.refs_5_.refs_1_, f32[128,256]{1,0:T(8,128)S(1)} %collective-permute-done.12.refs_2_, ...), custom_call_target="tpu_custom_call", output_to_operand_aliasing={{}: (7, {})} | custom-call | bytes 1024 | tf_op jit(solution)/shard_map/pallas_call | solution.py:560
  (39 shorter events, 6.0 us)
Async XLA Ops:
  2.2 14.7 %copy-start.1 = (bf16[2,2,176,384]{3,2,1,0:T(8,128)(2,1)S(1)}, bf16[2,2,176,384]{3,2,1,0:T(8,128)(2,1)}, u32[]{:S(2)}) copy-start(bf16[2,2,176,384]{3,2,1,0:T(8,128)(2,1)} %constant.10.clone.refs_4_.refs_3_) | copy-start | bytes 1622020
  2.2 14.7 %copy-start.2 = (s32[4,1024]{1,0:T(4,128)S(1)}, s32[4,1024]{1,0:T(4,128)}, u32[]{:S(2)}) copy-start(s32[4,1024]{1,0:T(4,128)} %refs_6_.9) | copy-start | bytes 49156
  2.2 14.7 %copy-start.3 = (f32[8,384]{1,0:T(8,128)S(1)}, f32[8,384]{1,0:T(8,128)}, u32[]{:S(2)}) copy-start(f32[8,384]{1,0:T(8,128)} %constant.14.clone.refs_5_.refs_6_) | copy-start | bytes 36868
  2.2 7.4 %collective-permute-start.1 = (f32[264,256]{1,0:T(8,128)S(1)}, f32[264,256]{1,0:T(8,128)S(1)}, u32[]{:S(2)}, u32[]{:S(2)}) collective-permute-start(f32[264,256]{1,0:T(8,128)S(1)} %get-tuple-element.37.refs_0_), channel_id=1, source_target_pairs={{0,2},{1,3},{2,0},{3,1},{4,6},{5,7},{6,4},{7,5},{8,10},{9,11},{10,... | collective-permute-start | bytes 811016 | tf_op jit(solution)/shard_map/ppermute | solution.py:442
  5.9 15.8 %copy-start.4 = (bf16[2,224,384]{2,1,0:T(8,128)(2,1)S(1)}, bf16[2,224,384]{2,1,0:T(8,128)(2,1)}, u32[]{:S(2)}) copy-start(bf16[2,224,384]{2,1,0:T(8,128)(2,1)} %constant.12.clone.refs_4_) | copy-start | bytes 1032196
  5.9 2.0 %collective-permute-start.5 = (f32[128,256]{1,0:T(8,128)S(1)}, f32[128,256]{1,0:T(8,128)S(1)}, u32[]{:S(2)}, u32[]{:S(2)}) collective-permute-start(f32[128,256]{1,0:T(8,128)S(1)} %get-tuple-element.50), channel_id=1, source_target_pairs={{0,1},{1,0},{2,3},{3,2},{4,5},{5,4},{6,7},{7,6},{8,9},{9,8},{10,11... | collective-permute-start | bytes 393224 | tf_op jit(solution)/shard_map/ppermute | solution.py:442
  6.9 1.3 %collective-permute-start.6 = (f32[128,256]{1,0:T(8,128)S(1)}, f32[128,256]{1,0:T(8,128)S(1)}, u32[]{:S(2)}, u32[]{:S(2)}) collective-permute-start(f32[128,256]{1,0:T(8,128)S(1)} %get-tuple-element.51), channel_id=1, source_target_pairs={{0,1},{1,0},{2,3},{3,2},{4,5},{5,4},{6,7},{7,6},{8,9},{9,8},{10,11... | collective-permute-start | bytes 393224 | tf_op jit(solution)/shard_map/ppermute | solution.py:442
  7.0 4.0 %collective-permute-start = (f32[264,256]{1,0:T(8,128)S(1)}, f32[264,256]{1,0:T(8,128)S(1)}, u32[]{:S(2)}, u32[]{:S(2)}) collective-permute-start(f32[264,256]{1,0:T(8,128)S(1)} %get-tuple-element.39), channel_id=1, source_target_pairs={{0,1},{1,0},{2,3},{3,2},{4,5},{5,4},{6,7},{7,6},{8,9},{9,8},{10,11... | collective-permute-start | bytes 811016 | tf_op jit(solution)/shard_map/ppermute | solution.py:442
  7.4 9.4 %collective-permute-start.2 = (f32[264,256]{1,0:T(8,128)S(1)}, f32[264,256]{1,0:T(8,128)S(1)}, u32[]{:S(2)}, u32[]{:S(2)}) collective-permute-start(f32[264,256]{1,0:T(8,128)S(1)} %get-tuple-element.40), channel_id=1, source_target_pairs={{0,3},{1,2},{2,1},{3,0},{4,7},{5,6},{6,5},{7,4},{8,11},{9,10},{10,... | collective-permute-start | bytes 811016 | tf_op jit(solution)/shard_map/ppermute | solution.py:442
  9.7 17.5 %collective-permute-start.7 = (f32[512,256]{1,0:T(8,128)S(1)}, f32[512,256]{1,0:T(8,128)S(1)}, u32[]{:S(2)}, u32[]{:S(2)}) collective-permute-start(f32[512,256]{1,0:T(8,128)S(1)} %shard_map.77.refs_0_), channel_id=1, source_target_pairs={{0,2},{1,3},{2,0},{3,1},{4,6},{5,7},{6,4},{7,5},{8,10},{9,11},{10,... | collective-permute-start | bytes 1572872 | tf_op jit(solution)/shard_map/ppermute | solution.py:442
  17.8 3.8 %collective-permute-start.4 = (f32[256,256]{1,0:T(8,128)S(1)}, f32[256,256]{1,0:T(8,128)S(1)}, u32[]{:S(2)}, u32[]{:S(2)}) collective-permute-start(f32[256,256]{1,0:T(8,128)S(1)} %get-tuple-element.48), channel_id=1, source_target_pairs={{0,1},{1,0},{2,3},{3,2},{4,5},{5,4},{6,7},{7,6},{8,9},{9,8},{10,11... | collective-permute-start | bytes 786440 | tf_op jit(solution)/shard_map/ppermute | solution.py:442
  18.2 6.3 %collective-permute-start.8 = (f32[264,256]{1,0:T(8,128)S(1)}, f32[264,256]{1,0:T(8,128)S(1)}, u32[]{:S(2)}, u32[]{:S(2)}) collective-permute-start(f32[264,256]{1,0:T(8,128)S(1)} %get-tuple-element.53), channel_id=1, source_target_pairs={{0,1},{1,0},{2,3},{3,2},{4,5},{5,4},{6,7},{7,6},{8,9},{9,8},{10,11... | collective-permute-start | bytes 811016 | tf_op jit(solution)/shard_map/ppermute | solution.py:442
  18.4 17.8 %collective-permute-start.11 = (f32[368,256]{1,0:T(8,128)S(1)}, f32[368,256]{1,0:T(8,128)S(1)}, u32[]{:S(2)}, u32[]{:S(2)}) collective-permute-start(f32[368,256]{1,0:T(8,128)S(1)} %get-tuple-element.57), channel_id=1, source_target_pairs={{0,4},{4,0},{8,12},{12,8},{16,20},{20,16},{24,28},{28,24},{1,5},{5... | collective-permute-start | bytes 1130504 | tf_op jit(solution)/shard_map/ppermute | solution.py:521
  19.6 12.3 %collective-permute-start.3 = (f32[352,256]{1,0:T(8,128)S(1)}, f32[352,256]{1,0:T(8,128)S(1)}, u32[]{:S(2)}, u32[]{:S(2)}) collective-permute-start(f32[352,256]{1,0:T(8,128)S(1)} %get-tuple-element.44), channel_id=1, source_target_pairs={{4,8},{8,4},{12,16},{16,12},{20,24},{24,20},{5,9},{9,5},{13,17},{1... | collective-permute-start | bytes 1081352 | tf_op jit(solution)/shard_map/ppermute | solution.py:521
  22.6 15.8 %collective-permute-start.14 = (f32[368,256]{1,0:T(8,128)S(1)}, f32[368,256]{1,0:T(8,128)S(1)}, u32[]{:S(2)}, u32[]{:S(2)}) collective-permute-start(f32[368,256]{1,0:T(8,128)S(1)} %shard_map.82), channel_id=1, source_target_pairs={{0,2},{1,3},{2,0},{3,1},{4,6},{5,7},{6,4},{7,5},{8,10},{9,11},{10,... | collective-permute-start | bytes 1130504 | tf_op jit(solution)/shard_map/ppermute | solution.py:442
  28.8 15.1 %collective-permute-start.15 = (f32[256,256]{1,0:T(8,128)S(1)}, f32[256,256]{1,0:T(8,128)S(1)}, u32[]{:S(2)}, u32[]{:S(2)}) collective-permute-start(f32[256,256]{1,0:T(8,128)S(1)} %get-tuple-element.61), channel_id=1, source_target_pairs={{0,1},{1,0},{2,3},{3,2},{4,5},{5,4},{6,7},{7,6},{8,9},{9,8},{10,11... | collective-permute-start | bytes 786440 | tf_op jit(solution)/shard_map/ppermute | solution.py:442
  33.0 11.0 %copy-start.5 = (bf16[2,128,576]{2,1,0:T(8,128)(2,1)S(1)}, bf16[2,128,576]{2,1,0:T(8,128)(2,1)}, u32[]{:S(2)}) copy-start(bf16[2,128,576]{2,1,0:T(8,128)(2,1)} %constant.13.clone.refs_2_) | copy-start | bytes 884740
  33.0 10.9 %collective-permute-start.10 = (f32[136,256]{1,0:T(8,128)S(1)}, f32[136,256]{1,0:T(8,128)S(1)}, u32[]{:S(2)}, u32[]{:S(2)}) collective-permute-start(f32[136,256]{1,0:T(8,128)S(1)} %get-tuple-element.56.refs_9_), channel_id=1, source_target_pairs={{0,3},{1,2},{2,1},{3,0},{4,7},{5,6},{6,5},{7,4},{8,11},{9,10},{10,... | collective-permute-start | bytes 417800 | tf_op jit(solution)/shard_map/ppermute | solution.py:442
  36.2 6.2 %collective-permute-start.9 = (f32[128,256]{1,0:T(8,128)S(1)}, f32[128,256]{1,0:T(8,128)S(1)}, u32[]{:S(2)}, u32[]{:S(2)}) collective-permute-start(f32[128,256]{1,0:T(8,128)S(1)} %get-tuple-element.55), channel_id=1, source_target_pairs={{0,2},{1,3},{2,0},{3,1},{4,6},{5,7},{6,4},{7,5},{8,10},{9,11},{10,... | collective-permute-start | bytes 393224 | tf_op jit(solution)/shard_map/ppermute | solution.py:442
  37.3 8.3 %collective-permute-start.18 = (f32[256,256]{1,0:T(8,128)S(1)}, f32[256,256]{1,0:T(8,128)S(1)}, u32[]{:S(2)}, u32[]{:S(2)}) collective-permute-start(f32[256,256]{1,0:T(8,128)S(1)} %get-tuple-element.68), channel_id=1, source_target_pairs={{0,1},{1,0},{2,3},{3,2},{4,5},{5,4},{6,7},{7,6},{8,9},{9,8},{10,11... | collective-permute-start | bytes 786440 | tf_op jit(solution)/shard_map/ppermute | solution.py:442
  38.4 8.2 %collective-permute-start.12 = (f32[128,256]{1,0:T(8,128)S(1)}, f32[128,256]{1,0:T(8,128)S(1)}, u32[]{:S(2)}, u32[]{:S(2)}) collective-permute-start(f32[128,256]{1,0:T(8,128)S(1)} %get-tuple-element.59), channel_id=1, source_target_pairs={{0,2},{1,3},{2,0},{3,1},{4,6},{5,7},{6,4},{7,5},{8,10},{9,11},{10,... | collective-permute-start | bytes 393224 | tf_op jit(solution)/shard_map/ppermute | solution.py:442
  42.4 5.4 %collective-permute-start.13 = (f32[128,256]{1,0:T(8,128)S(1)}, f32[128,256]{1,0:T(8,128)S(1)}, u32[]{:S(2)}, u32[]{:S(2)}) collective-permute-start(f32[128,256]{1,0:T(8,128)S(1)} %get-tuple-element.60.refs_3_), channel_id=1, source_target_pairs={{0,3},{1,2},{2,1},{3,0},{4,7},{5,6},{6,5},{7,4},{8,11},{9,10},{10,... | collective-permute-start | bytes 393224 | tf_op jit(solution)/shard_map/ppermute | solution.py:442
  44.3 3.5 %collective-permute-start.16 = (f32[128,256]{1,0:T(8,128)S(1)}, f32[128,256]{1,0:T(8,128)S(1)}, u32[]{:S(2)}, u32[]{:S(2)}) collective-permute-start(f32[128,256]{1,0:T(8,128)S(1)} %get-tuple-element.63), channel_id=1, source_target_pairs={{0,1},{1,0},{2,3},{3,2},{4,5},{5,4},{6,7},{7,6},{8,9},{9,8},{10,11... | collective-permute-start | bytes 393224 | tf_op jit(solution)/shard_map/ppermute | solution.py:442
  45.4 2.3 %collective-permute-start.17 = (f32[128,256]{1,0:T(8,128)S(1)}, f32[128,256]{1,0:T(8,128)S(1)}, u32[]{:S(2)}, u32[]{:S(2)}) collective-permute-start(f32[128,256]{1,0:T(8,128)S(1)} %get-tuple-element.64), channel_id=1, source_target_pairs={{0,1},{1,0},{2,3},{3,2},{4,5},{5,4},{6,7},{7,6},{8,9},{9,8},{10,11... | collective-permute-start | bytes 393224 | tf_op jit(solution)/shard_map/ppermute | solution.py:442
  (1 other events, 7.6 us)

commit v23 on v22

--- a/solution.py
+++ b/solution.py
@@ -16,7 +16,7 @@
 PARAMS = pltpu.CompilerParams(vmem_limit_bytes=24 * 1024 * 1024)
 LONG = pl.CostEstimate(flops=0, bytes_accessed=200_000_000, transcendentals=0)
 SHORT = pl.CostEstimate(flops=0, bytes_accessed=1024, transcendentals=0)
-SPLIT = 8
+SPLIT = 4
 
 
 def split(values):

time: 49.4 us -> 49.7 us (level)
  waiting for transfers between devices: 13.3 us -> 15.7 us
  starting transfers between devices: 20.6 us -> 19.4 us
  Pallas kernels: 14.7 us -> 14.2 us
    ppermute x17, waiting for transfers between devices: 11.8 us -> 13.5 us  [swap(): lax.ppermute(block, 'span', [(i, i ^ d) for i in range(lax.axis_size('spa...]
    ppermute x17, starting transfers between devices: 17.4 us -> 16.1 us  [swap(): lax.ppermute(block, 'span', [(i, i ^ d) for i in range(lax.axis_size('spa...]
    ppermute x2, waiting for transfers between devices: 1.44 us -> 2.16 us  [local(): lax.ppermute(row, 'plane', pair)]
    pallas_call x2, Pallas kernels: 4.53 us -> 4.01 us  [pack(): pl.pallas_call(functools.partial(pack_kernel, jobs, row_count, cells, len...]
  transfers between devices with their start and end apart: 19 -> 19, of which waited for: 8 -> 9; matrix products, arithmetic and copies ran while one was open for 0% -> 0% of each run, Pallas kernels for 24% -> 23%
where the time goes in v23:
time: 49.7 us; the launch traced here: 49.5 us
  starting transfers between devices  19.4 us (39%)
  waiting for transfers between devices  15.7 us (32%)
  Pallas kernels  14.2 us (29%)
    ppermute x17, starting transfers between devices, swap(): lax.ppermute(block, 'span', [(i, i ^ d) for i in range(lax.axis_size('spa...  16.1 us
    ppermute x17, waiting for transfers between devices, swap(): lax.ppermute(block, 'span', [(i, i ^ d) for i in range(lax.axis_size('spa...  13.5 us
    pallas_call x9, Pallas kernels, call(): pl.pallas_call(kernel, out_shape=shapes, in_specs=[VMEM] * len(args) + [A...  8.08 us
    pallas_call x2, Pallas kernels, pack(): pl.pallas_call(functools.partial(pack_kernel, jobs, row_count, cells, len...  4.01 us
    ppermute x2, starting transfers between devices, local(): lax.ppermute(row, 'plane', pair)  3.26 us
    ppermute x2, waiting for transfers between devices, local(): lax.ppermute(row, 'plane', pair)  2.16 us
    pallas_call x2, Pallas kernels, local(): pl.pallas_call(functools.partial(unpack_kernel, [piece[1:] for piece in c...  2.11 us
  transfers between devices with their start and end apart: 19, of which 9 were waited for; matrix products, arithmetic and copies ran while one was open for 0% of the time, Pallas kernels for 23%

profile of v23, /device:TPU:25, one launch (start us, length us, event | category | flops | bytes accessed | tf_op | source)
XLA Modules:
  0.0 49.5 jit_solution(520552739495272541)
XLA Ops:
  0.0 1.9 %shard_map.73 = (f32[264,256]{1,0:T(8,128)S(1)}, f32[264,256]{1,0:T(8,128)S(1)}, f32[264,256]{1,0:T(8,128)S(1)}) custom-call(f32[128,32,128]{2,1,0:T(8,128)} %bitcast.10), custom_call_target="tpu_custom_call" | custom-call | bytes 200000000 | tf_op jit(solution)/shard_map/pallas_call | solution.py:466
  2.0 1.3 %collective-permute-start.1 = (f32[264,256]{1,0:T(8,128)S(1)}, f32[264,256]{1,0:T(8,128)S(1)}, u32[]{:S(2)}, u32[]{:S(2)}) collective-permute-start(f32[264,256]{1,0:T(8,128)S(1)} %get-tuple-element.37.refs_0_), channel_id=1, source_target_pairs={{0,2},{1,3},{2,0},{3,1},{4,6},{5,7},{6,4},{7,5},{8,10},{9,11},{10,... | collective-permute-start | bytes 811016 | tf_op jit(solution)/shard_map/ppermute | solution.py:442
  3.3 2.1 %shard_map.74 = (f32[256,256]{1,0:T(8,128)S(1)}, f32[256,256]{1,0:T(8,128)S(1)}, f32[256,256]{1,0:T(8,128)S(1)}, f32[264,256]{1,0:T(8,128)S(1)}, f32[264,256]{1,...) custom-call(f32[128,32,128]{2,1,0:T(8,128)} %bitcast.11, ...), custom_call_target="tpu_custom_call" | custom-call | bytes 200000000 | tf_op jit(solution)/shard_map/pallas_call | solution.py:466
  5.4 1.0 %collective-permute-start.5 = (f32[128,256]{1,0:T(8,128)S(1)}, f32[128,256]{1,0:T(8,128)S(1)}, u32[]{:S(2)}, u32[]{:S(2)}) collective-permute-start(f32[128,256]{1,0:T(8,128)S(1)} %get-tuple-element.50), channel_id=1, source_target_pairs={{0,1},{1,0},{2,3},{3,2},{4,5},{5,4},{6,7},{7,6},{8,9},{9,8},{10,11... | collective-permute-start | bytes 393224 | tf_op jit(solution)/shard_map/ppermute | solution.py:442
  7.8 1.6 %collective-permute-done.1.refs_2_.refs_3_ = f32[264,256]{1,0:T(8,128)S(1)} collective-permute-done((f32[264,256]{1,0:T(8,128)S(1)}, f32[264,256]{1,0:T(8,128)S(1)}, u32[]{:S(2)}, u32[]{:S(2)}) %collective-permute-start.1) | collective-permute-done | bytes 270368 | tf_op jit(solution)/shard_map/ppermute | solution.py:442
  9.4 1.3 %collective-permute-start.7 = (f32[512,256]{1,0:T(8,128)S(1)}, f32[512,256]{1,0:T(8,128)S(1)}, u32[]{:S(2)}, u32[]{:S(2)}) collective-permute-start(f32[512,256]{1,0:T(8,128)S(1)} %shard_map.77.refs_0_), channel_id=1, source_target_pairs={{0,2},{1,3},{2,0},{3,1},{4,6},{5,7},{6,4},{7,5},{8,10},{9,11},{10,... | collective-permute-start | bytes 1572872 | tf_op jit(solution)/shard_map/ppermute | solution.py:442
  10.7 6.2 %collective-permute-done.2.refs_3_ = f32[264,256]{1,0:T(8,128)S(1)} collective-permute-done((f32[264,256]{1,0:T(8,128)S(1)}, f32[264,256]{1,0:T(8,128)S(1)}, u32[]{:S(2)}, u32[]{:S(2)}) %collective-permute-start.2) | collective-permute-done | bytes 270368 | tf_op jit(solution)/shard_map/ppermute | solution.py:442
  18.4 1.2 %collective-permute-start.11 = (f32[368,256]{1,0:T(8,128)S(1)}, f32[368,256]{1,0:T(8,128)S(1)}, u32[]{:S(2)}, u32[]{:S(2)}) collective-permute-start(f32[368,256]{1,0:T(8,128)S(1)} %get-tuple-element.57), channel_id=1, source_target_pairs={{0,4},{4,0},{8,12},{12,8},{16,20},{20,16},{24,28},{28,24},{1,5},{5... | collective-permute-start | bytes 1130504 | tf_op jit(solution)/shard_map/ppermute | solution.py:521
  19.6 2.0 %collective-permute-start.3 = (f32[352,256]{1,0:T(8,128)S(1)}, f32[352,256]{1,0:T(8,128)S(1)}, u32[]{:S(2)}, u32[]{:S(2)}) collective-permute-start(f32[352,256]{1,0:T(8,128)S(1)} %get-tuple-element.44), channel_id=1, source_target_pairs={{4,8},{8,4},{12,16},{16,12},{20,24},{24,20},{5,9},{9,5},{13,17},{1... | collective-permute-start | bytes 1081352 | tf_op jit(solution)/shard_map/ppermute | solution.py:521
  22.7 1.6 %collective-permute-start.14 = (f32[368,256]{1,0:T(8,128)S(1)}, f32[368,256]{1,0:T(8,128)S(1)}, u32[]{:S(2)}, u32[]{:S(2)}) collective-permute-start(f32[368,256]{1,0:T(8,128)S(1)} %shard_map.82), channel_id=1, source_target_pairs={{0,2},{1,3},{2,0},{3,1},{4,6},{5,7},{6,4},{7,5},{8,10},{9,11},{10,... | collective-permute-start | bytes 1130504 | tf_op jit(solution)/shard_map/ppermute | solution.py:442
  24.2 2.1 %shard_map.78.refs_9_.refs_1_ = f32[512,256]{1,0:T(8,128)S(1)} custom-call(f32[512,256]{1,0:T(8,128)S(1)} %shard_map.77.refs_0_, f32[264,256]{1,0:T(8,128)S(1)} %get-tuple-element.52.refs_1_, f32[264,256]{1,0:T(8,128)S(1)} %collective-permute-done.8.refs_2_, bf16[2,2,176,384]{3,2,1,0:T(8,128)(2,1)S(1)} %copy-done.1, bf16[2,2,128,528]{3,2,1,0:T(8,128)(2,1)S(1)} %copy-done, ...), custom_call_target="tpu_custom_call" | custom-call | bytes 1024 | tf_op jit(solution)/shard_map/pallas_call | solution.py:431
  26.7 1.6 %shard_map.79 = (f32[256,256]{1,0:T(8,128)S(1)}, f32[256,256]{1,0:T(8,128)S(1)}, f32[2,352,256]{2,1,0:T(8,128)S(1)}) custom-call(f32[256,256]{1,0:T(8,128)S(1)} %get-tuple-element.45.refs_0_, f32[256,256]{1,0:T(8,128)S(1)} %collective-permute-done.4.refs_1_, f32[512,256]{1,0:T(8,128)S(1)} %collective-permute-done.7.refs_2_, ...), custom_call_target="tpu_custom_call" | custom-call | bytes 1024 | tf_op jit(solution)/shard_map/pallas_call | solution.py:431
  28.3 2.2 %collective-permute-start.15 = (f32[256,256]{1,0:T(8,128)S(1)}, f32[256,256]{1,0:T(8,128)S(1)}, u32[]{:S(2)}, u32[]{:S(2)}) collective-permute-start(f32[256,256]{1,0:T(8,128)S(1)} %get-tuple-element.61), channel_id=1, source_target_pairs={{0,1},{1,0},{2,3},{3,2},{4,5},{5,4},{6,7},{7,6},{8,9},{9,8},{10,11... | collective-permute-start | bytes 786440 | tf_op jit(solution)/shard_map/ppermute | solution.py:442
  30.5 1.6 %collective-permute-done.3.refs_3_ = f32[352,256]{1,0:T(8,128)S(1)} collective-permute-done((f32[352,256]{1,0:T(8,128)S(1)}, f32[352,256]{1,0:T(8,128)S(1)}, u32[]{:S(2)}, u32[]{:S(2)}) %collective-permute-start.3) | collective-permute-done | bytes 360480 | tf_op jit(solution)/shard_map/ppermute | solution.py:521
  32.1 1.1 %shard_map.80 = (f32[128,256]{1,0:T(8,128)S(1)}, f32[128,256]{1,0:T(8,128)S(1)}, f32[128,256]{1,0:T(8,128)S(1)}, f32[136,256]{1,0:T(8,128)S(1)}) custom-call(f32[2,352,256]{2,1,0:T(8,128)S(1)} %get-tuple-element.41.refs_0_, f32[2,352,256]{2,1,0:T(8,128)S(1)} %get-tuple-element.42.refs_7_.refs_1_, f32[352,16]{1,0:T(8,128)S(1)} %get-tuple-element.43.refs_2_.refs_8_, ...), custom_call_target="tpu_custom_call" | custom-call | bytes 1024 | tf_op jit(solution)/shard_map/pallas_call | solution.py:431
  33.2 2.7 %collective-permute-start.10 = (f32[136,256]{1,0:T(8,128)S(1)}, f32[136,256]{1,0:T(8,128)S(1)}, u32[]{:S(2)}, u32[]{:S(2)}) collective-permute-start(f32[136,256]{1,0:T(8,128)S(1)} %get-tuple-element.56.refs_9_), channel_id=1, source_target_pairs={{0,3},{1,2},{2,1},{3,0},{4,7},{5,6},{6,5},{7,4},{8,11},{9,10},{10,... | collective-permute-start | bytes 417800 | tf_op jit(solution)/shard_map/ppermute | solution.py:442
  36.5 1.1 %shard_map.81 = (f32[128,256]{1,0:T(8,128)S(1)}, f32[256,256]{1,0:T(8,128)S(1)}, f32[128,256]{1,0:T(8,128)S(1)}, f32[128,256]{1,0:T(8,128)S(1)}) custom-call(f32[2,352,256]{2,1,0:T(8,128)S(1)} %get-tuple-element.41.refs_0_, f32[2,352,256]{2,1,0:T(8,128)S(1)} %get-tuple-element.42.refs_7_.refs_1_, f32[352,16]{1,0:T(8,128)S(1)} %get-tuple-element.43.refs_2_.refs_8_, ...), custom_call_target="tpu_custom_call" | custom-call | bytes 200000000 | tf_op jit(solution)/shard_map/pallas_call | solution.py:431
  38.5 1.5 %collective-permute-start.12 = (f32[128,256]{1,0:T(8,128)S(1)}, f32[128,256]{1,0:T(8,128)S(1)}, u32[]{:S(2)}, u32[]{:S(2)}) collective-permute-start(f32[128,256]{1,0:T(8,128)S(1)} %get-tuple-element.59), channel_id=1, source_target_pairs={{0,2},{1,3},{2,0},{3,1},{4,6},{5,7},{6,4},{7,5},{8,10},{9,11},{10,... | collective-permute-start | bytes 393224 | tf_op jit(solution)/shard_map/ppermute | solution.py:442
  40.0 2.6 %collective-permute-done.9.refs_4_.refs_0_ = f32[128,256]{1,0:T(8,128)S(1)} collective-permute-done((f32[128,256]{1,0:T(8,128)S(1)}, f32[128,256]{1,0:T(8,128)S(1)}, u32[]{:S(2)}, u32[]{:S(2)}) %collective-permute-start.9) | collective-permute-done | bytes 131104 | tf_op jit(solution)/shard_map/ppermute | solution.py:442
  42.6 1.0 %collective-permute-start.13 = (f32[128,256]{1,0:T(8,128)S(1)}, f32[128,256]{1,0:T(8,128)S(1)}, u32[]{:S(2)}, u32[]{:S(2)}) collective-permute-start(f32[128,256]{1,0:T(8,128)S(1)} %get-tuple-element.60.refs_3_), channel_id=1, source_target_pairs={{0,3},{1,2},{2,1},{3,0},{4,7},{5,6},{6,5},{7,4},{8,11},{9,10},{10,... | collective-permute-start | bytes 393224 | tf_op jit(solution)/shard_map/ppermute | solution.py:442
  44.0 1.2 %collective-permute-start.16 = (f32[128,256]{1,0:T(8,128)S(1)}, f32[128,256]{1,0:T(8,128)S(1)}, u32[]{:S(2)}, u32[]{:S(2)}) collective-permute-start(f32[128,256]{1,0:T(8,128)S(1)} %get-tuple-element.63), channel_id=1, source_target_pairs={{0,1},{1,0},{2,3},{3,2},{4,5},{5,4},{6,7},{7,6},{8,9},{9,8},{10,11... | collective-permute-start | bytes 393224 | tf_op jit(solution)/shard_map/ppermute | solution.py:442
  45.3 1.1 %shard_map.84.refs_7_ = f32[128,32,128]{2,1,0:T(8,128)} custom-call(f32[256,256]{1,0:T(8,128)S(1)} %get-tuple-element.65.refs_0_, f32[256,256]{1,0:T(8,128)S(1)} %collective-permute-done.15.refs_6_.refs_1_, f32[128,256]{1,0:T(8,128)S(1)} %get-tuple-element.66.refs_2_, f32[128,256]{1,0:T(8,128)S(1)} %get-tuple-element.67.refs_3_, ...), custom_call_target="tpu_custom_call" | custom-call | bytes 200000000 | tf_op jit(solution)/shard_map/pallas_call | solution.py:560
  46.4 2.1 %collective-permute-done.13.refs_3_ = f32[128,256]{1,0:T(8,128)S(1)} collective-permute-done((f32[128,256]{1,0:T(8,128)S(1)}, f32[128,256]{1,0:T(8,128)S(1)}, u32[]{:S(2)}, u32[]{:S(2)}) %collective-permute-start.13) | collective-permute-done | bytes 131104 | tf_op jit(solution)/shard_map/ppermute | solution.py:442
  48.5 1.1 %shard_map.85 = f32[128,32,128]{2,1,0:T(8,128)} custom-call(f32[128,256]{1,0:T(8,128)S(1)} %collective-permute-done.9.refs_4_.refs_0_, f32[136,256]{1,0:T(8,128)S(1)} %collective-permute-done.10.refs_5_.refs_1_, f32[128,256]{1,0:T(8,128)S(1)} %collective-permute-done.12.refs_2_, ...), custom_call_target="tpu_custom_call", output_to_operand_aliasing={{}: (7, {})} | custom-call | bytes 1024 | tf_op jit(solution)/shard_map/pallas_call | solution.py:560
  (39 shorter events, 6.1 us)
Async XLA Ops:
  1.9 15.0 %copy-start.1 = (bf16[2,2,176,384]{3,2,1,0:T(8,128)(2,1)S(1)}, bf16[2,2,176,384]{3,2,1,0:T(8,128)(2,1)}, u32[]{:S(2)}) copy-start(bf16[2,2,176,384]{3,2,1,0:T(8,128)(2,1)} %constant.10.clone.refs_4_.refs_3_) | copy-start | bytes 1622020
  1.9 15.0 %copy-start.2 = (s32[4,1024]{1,0:T(4,128)S(1)}, s32[4,1024]{1,0:T(4,128)}, u32[]{:S(2)}) copy-start(s32[4,1024]{1,0:T(4,128)} %refs_6_.9) | copy-start | bytes 49156
  2.0 15.0 %copy-start.3 = (f32[8,384]{1,0:T(8,128)S(1)}, f32[8,384]{1,0:T(8,128)}, u32[]{:S(2)}) copy-start(f32[8,384]{1,0:T(8,128)} %constant.14.clone.refs_5_.refs_6_) | copy-start | bytes 36868
  2.0 7.4 %collective-permute-start.1 = (f32[264,256]{1,0:T(8,128)S(1)}, f32[264,256]{1,0:T(8,128)S(1)}, u32[]{:S(2)}, u32[]{:S(2)}) collective-permute-start(f32[264,256]{1,0:T(8,128)S(1)} %get-tuple-element.37.refs_0_), channel_id=1, source_target_pairs={{0,2},{1,3},{2,0},{3,1},{4,6},{5,7},{6,4},{7,5},{8,10},{9,11},{10,... | collective-permute-start | bytes 811016 | tf_op jit(solution)/shard_map/ppermute | solution.py:442
  5.4 16.3 %copy-start.4 = (bf16[2,224,384]{2,1,0:T(8,128)(2,1)S(1)}, bf16[2,224,384]{2,1,0:T(8,128)(2,1)}, u32[]{:S(2)}) copy-start(bf16[2,224,384]{2,1,0:T(8,128)(2,1)} %constant.12.clone.refs_4_) | copy-start | bytes 1032196
  5.4 2.0 %collective-permute-start.5 = (f32[128,256]{1,0:T(8,128)S(1)}, f32[128,256]{1,0:T(8,128)S(1)}, u32[]{:S(2)}, u32[]{:S(2)}) collective-permute-start(f32[128,256]{1,0:T(8,128)S(1)} %get-tuple-element.50), channel_id=1, source_target_pairs={{0,1},{1,0},{2,3},{3,2},{4,5},{5,4},{6,7},{7,6},{8,9},{9,8},{10,11... | collective-permute-start | bytes 393224 | tf_op jit(solution)/shard_map/ppermute | solution.py:442
  6.4 1.3 %collective-permute-start.6 = (f32[128,256]{1,0:T(8,128)S(1)}, f32[128,256]{1,0:T(8,128)S(1)}, u32[]{:S(2)}, u32[]{:S(2)}) collective-permute-start(f32[128,256]{1,0:T(8,128)S(1)} %get-tuple-element.51), channel_id=1, source_target_pairs={{0,1},{1,0},{2,3},{3,2},{4,5},{5,4},{6,7},{7,6},{8,9},{9,8},{10,11... | collective-permute-start | bytes 393224 | tf_op jit(solution)/shard_map/ppermute | solution.py:442
  6.5 4.2 %collective-permute-start = (f32[264,256]{1,0:T(8,128)S(1)}, f32[264,256]{1,0:T(8,128)S(1)}, u32[]{:S(2)}, u32[]{:S(2)}) collective-permute-start(f32[264,256]{1,0:T(8,128)S(1)} %get-tuple-element.39), channel_id=1, source_target_pairs={{0,1},{1,0},{2,3},{3,2},{4,5},{5,4},{6,7},{7,6},{8,9},{9,8},{10,11... | collective-permute-start | bytes 811016 | tf_op jit(solution)/shard_map/ppermute | solution.py:442
  6.9 10.0 %collective-permute-start.2 = (f32[264,256]{1,0:T(8,128)S(1)}, f32[264,256]{1,0:T(8,128)S(1)}, u32[]{:S(2)}, u32[]{:S(2)}) collective-permute-start(f32[264,256]{1,0:T(8,128)S(1)} %get-tuple-element.40), channel_id=1, source_target_pairs={{0,3},{1,2},{2,1},{3,0},{4,7},{5,6},{6,5},{7,4},{8,11},{9,10},{10,... | collective-permute-start | bytes 811016 | tf_op jit(solution)/shard_map/ppermute | solution.py:442
  9.4 17.3 %collective-permute-start.7 = (f32[512,256]{1,0:T(8,128)S(1)}, f32[512,256]{1,0:T(8,128)S(1)}, u32[]{:S(2)}, u32[]{:S(2)}) collective-permute-start(f32[512,256]{1,0:T(8,128)S(1)} %shard_map.77.refs_0_), channel_id=1, source_target_pairs={{0,2},{1,3},{2,0},{3,1},{4,6},{5,7},{6,4},{7,5},{8,10},{9,11},{10,... | collective-permute-start | bytes 1572872 | tf_op jit(solution)/shard_map/ppermute | solution.py:442
  17.8 3.8 %collective-permute-start.4 = (f32[256,256]{1,0:T(8,128)S(1)}, f32[256,256]{1,0:T(8,128)S(1)}, u32[]{:S(2)}, u32[]{:S(2)}) collective-permute-start(f32[256,256]{1,0:T(8,128)S(1)} %get-tuple-element.48), channel_id=1, source_target_pairs={{0,1},{1,0},{2,3},{3,2},{4,5},{5,4},{6,7},{7,6},{8,9},{9,8},{10,11... | collective-permute-start | bytes 786440 | tf_op jit(solution)/shard_map/ppermute | solution.py:442
  17.9 6.3 %collective-permute-start.8 = (f32[264,256]{1,0:T(8,128)S(1)}, f32[264,256]{1,0:T(8,128)S(1)}, u32[]{:S(2)}, u32[]{:S(2)}) collective-permute-start(f32[264,256]{1,0:T(8,128)S(1)} %get-tuple-element.53), channel_id=1, source_target_pairs={{0,1},{1,0},{2,3},{3,2},{4,5},{5,4},{6,7},{7,6},{8,9},{9,8},{10,11... | collective-permute-start | bytes 811016 | tf_op jit(solution)/shard_map/ppermute | solution.py:442
  18.4 18.1 %collective-permute-start.11 = (f32[368,256]{1,0:T(8,128)S(1)}, f32[368,256]{1,0:T(8,128)S(1)}, u32[]{:S(2)}, u32[]{:S(2)}) collective-permute-start(f32[368,256]{1,0:T(8,128)S(1)} %get-tuple-element.57), channel_id=1, source_target_pairs={{0,4},{4,0},{8,12},{12,8},{16,20},{20,16},{24,28},{28,24},{1,5},{5... | collective-permute-start | bytes 1130504 | tf_op jit(solution)/shard_map/ppermute | solution.py:521
  19.6 12.5 %collective-permute-start.3 = (f32[352,256]{1,0:T(8,128)S(1)}, f32[352,256]{1,0:T(8,128)S(1)}, u32[]{:S(2)}, u32[]{:S(2)}) collective-permute-start(f32[352,256]{1,0:T(8,128)S(1)} %get-tuple-element.44), channel_id=1, source_target_pairs={{4,8},{8,4},{12,16},{16,12},{20,24},{24,20},{5,9},{9,5},{13,17},{1... | collective-permute-start | bytes 1081352 | tf_op jit(solution)/shard_map/ppermute | solution.py:521
  22.7 15.8 %collective-permute-start.14 = (f32[368,256]{1,0:T(8,128)S(1)}, f32[368,256]{1,0:T(8,128)S(1)}, u32[]{:S(2)}, u32[]{:S(2)}) collective-permute-start(f32[368,256]{1,0:T(8,128)S(1)} %shard_map.82), channel_id=1, source_target_pairs={{0,2},{1,3},{2,0},{3,1},{4,6},{5,7},{6,4},{7,5},{8,10},{9,11},{10,... | collective-permute-start | bytes 1130504 | tf_op jit(solution)/shard_map/ppermute | solution.py:442
  28.3 15.4 %collective-permute-start.15 = (f32[256,256]{1,0:T(8,128)S(1)}, f32[256,256]{1,0:T(8,128)S(1)}, u32[]{:S(2)}, u32[]{:S(2)}) collective-permute-start(f32[256,256]{1,0:T(8,128)S(1)} %get-tuple-element.61), channel_id=1, source_target_pairs={{0,1},{1,0},{2,3},{3,2},{4,5},{5,4},{6,7},{7,6},{8,9},{9,8},{10,11... | collective-permute-start | bytes 786440 | tf_op jit(solution)/shard_map/ppermute | solution.py:442
  33.2 10.5 %copy-start.5 = (bf16[2,128,576]{2,1,0:T(8,128)(2,1)S(1)}, bf16[2,128,576]{2,1,0:T(8,128)(2,1)}, u32[]{:S(2)}) copy-start(bf16[2,128,576]{2,1,0:T(8,128)(2,1)} %constant.13.clone.refs_2_) | copy-start | bytes 884740
  33.2 10.5 %collective-permute-start.10 = (f32[136,256]{1,0:T(8,128)S(1)}, f32[136,256]{1,0:T(8,128)S(1)}, u32[]{:S(2)}, u32[]{:S(2)}) collective-permute-start(f32[136,256]{1,0:T(8,128)S(1)} %get-tuple-element.56.refs_9_), channel_id=1, source_target_pairs={{0,3},{1,2},{2,1},{3,0},{4,7},{5,6},{6,5},{7,4},{8,11},{9,10},{10,... | collective-permute-start | bytes 417800 | tf_op jit(solution)/shard_map/ppermute | solution.py:442
  35.9 6.7 %collective-permute-start.9 = (f32[128,256]{1,0:T(8,128)S(1)}, f32[128,256]{1,0:T(8,128)S(1)}, u32[]{:S(2)}, u32[]{:S(2)}) collective-permute-start(f32[128,256]{1,0:T(8,128)S(1)} %get-tuple-element.55), channel_id=1, source_target_pairs={{0,2},{1,3},{2,0},{3,1},{4,6},{5,7},{6,4},{7,5},{8,10},{9,11},{10,... | collective-permute-start | bytes 393224 | tf_op jit(solution)/shard_map/ppermute | solution.py:442
  37.6 7.7 %collective-permute-start.18 = (f32[256,256]{1,0:T(8,128)S(1)}, f32[256,256]{1,0:T(8,128)S(1)}, u32[]{:S(2)}, u32[]{:S(2)}) collective-permute-start(f32[256,256]{1,0:T(8,128)S(1)} %get-tuple-element.68), channel_id=1, source_target_pairs={{0,1},{1,0},{2,3},{3,2},{4,5},{5,4},{6,7},{7,6},{8,9},{9,8},{10,11... | collective-permute-start | bytes 786440 | tf_op jit(solution)/shard_map/ppermute | solution.py:442
  38.5 7.9 %collective-permute-start.12 = (f32[128,256]{1,0:T(8,128)S(1)}, f32[128,256]{1,0:T(8,128)S(1)}, u32[]{:S(2)}, u32[]{:S(2)}) collective-permute-start(f32[128,256]{1,0:T(8,128)S(1)} %get-tuple-element.59), channel_id=1, source_target_pairs={{0,2},{1,3},{2,0},{3,1},{4,6},{5,7},{6,4},{7,5},{8,10},{9,11},{10,... | collective-permute-start | bytes 393224 | tf_op jit(solution)/shard_map/ppermute | solution.py:442
  42.6 5.9 %collective-permute-start.13 = (f32[128,256]{1,0:T(8,128)S(1)}, f32[128,256]{1,0:T(8,128)S(1)}, u32[]{:S(2)}, u32[]{:S(2)}) collective-permute-start(f32[128,256]{1,0:T(8,128)S(1)} %get-tuple-element.60.refs_3_), channel_id=1, source_target_pairs={{0,3},{1,2},{2,1},{3,0},{4,7},{5,6},{6,5},{7,4},{8,11},{9,10},{10,... | collective-permute-start | bytes 393224 | tf_op jit(solution)/shard_map/ppermute | solution.py:442
  44.0 4.4 %collective-permute-start.16 = (f32[128,256]{1,0:T(8,128)S(1)}, f32[128,256]{1,0:T(8,128)S(1)}, u32[]{:S(2)}, u32[]{:S(2)}) collective-permute-start(f32[128,256]{1,0:T(8,128)S(1)} %get-tuple-element.63), channel_id=1, source_target_pairs={{0,1},{1,0},{2,3},{3,2},{4,5},{5,4},{6,7},{7,6},{8,9},{9,8},{10,11... | collective-permute-start | bytes 393224 | tf_op jit(solution)/shard_map/ppermute | solution.py:442
  45.2 3.3 %collective-permute-start.17 = (f32[128,256]{1,0:T(8,128)S(1)}, f32[128,256]{1,0:T(8,128)S(1)}, u32[]{:S(2)}, u32[]{:S(2)}) collective-permute-start(f32[128,256]{1,0:T(8,128)S(1)} %get-tuple-element.64), channel_id=1, source_target_pairs={{0,1},{1,0},{2,3},{3,2},{4,5},{5,4},{6,7},{7,6},{8,9},{9,8},{10,11... | collective-permute-start | bytes 393224 | tf_op jit(solution)/shard_map/ppermute | solution.py:442
  (1 other events, 7.3 us)
